TPU v7x, 32 devices: a whole 2x2x4 slice. The times are simulated.
32 devices in a mesh: groups: 2 (over y), seq: 8 (over z, x), rep: 2 (over core).
Axes of the slice: x: 2, y: 2, z: 4, core: 2. Of those that a mesh axis runs over, the one named last changes fastest.
Arguments:
- stream: bfloat16 [4096, 1536], P(('groups', 'seq', 'rep')), parts along dimension 0, may hold values from -6 to 6
- queries: bfloat16 [4096, 2048], P(('groups', 'seq'), 'rep'), parts along dimension 0, may hold values from -10 to 10
- key_rows: bfloat16 [4096, 256], P(('groups', 'seq'), 'rep'), parts along dimension 0, may hold values from -10 to 10
- value_rows: bfloat16 [4096, 256], P(('groups', 'seq'), 'rep'), parts along dimension 0, may hold values from -6 to 6
- sink_logits: float32 [32], P('rep'), may hold values from 0 to 5
- out_weight: bfloat16 [2048, 1536], P('rep'), may hold values from -0.125 to 0.125
- norm_gain: float32 [1536], replicated, may hold values from 0.25 to 1.75
- expert_ids: int32 [4096, 4], P(('groups', 'seq', 'rep')), parts along dimension 0, may hold values from 0 to 7, all different within a row; in each aligned block of 128 rows (0 to 127, 128 to 255, ...) at most 96 rows name the same one
- route_weights: float32 [4096, 4], P(('groups', 'seq', 'rep')), parts along dimension 0, may hold values from 0.1 to 1
- gate_weight: bfloat16 [8, 1536, 1536], P('seq', None, 'rep'), may hold values from -0.15625 to 0.15625
- up_weight: bfloat16 [8, 1536, 1536], P('seq', None, 'rep'), may hold values from -0.15625 to 0.15625
- down_weight: bfloat16 [8, 1536, 1536], P('seq', 'rep'), may hold values from -0.15625 to 0.15625
Outputs:
- layer_out: bfloat16 [4096, 1536], P(('groups', 'seq', 'rep')), parts along dimension 0
There are 2 independent parts, one for each index of `groups`. A program takes and returns all parts, laid end to end along the dimension named above; an argument that names none is the same for every part. Nothing has to cross between parts.
Inputs may be any that keep to these rules, and one draw needn't show every extreme that they name: `expert_ids`: each token names 4 different experts; among the 128 tokens of one device no expert is named more than 96 times, a bound that some block reaches.
All inputs are finite; a program needn't handle non-finite values.
Results may differ from a plain program's by a relative error of at most 0.009.
Values may be sent and summed in bfloat16 or wider, within the bound.
No kernel may reach another device: no remote copies, remote signals or barrier semaphores. Data moves between devices by JAX's collectives and lax.ppermute only.
A program may use at most 128 MiB of HBM per device.

v0:
```python
import math

import jax
import jax.numpy as jnp
from jax import lax
from jax.sharding import PartitionSpec as P

HEAD_DIM = 64
WINDOW = 128
TOP = 4
EXP_DEV = 1


def shifted(value, axis, by):
    peers = lax.axis_size(axis)
    pairs = [(i, i + by) for i in range(peers) if 0 <= i + by < peers]
    return lax.ppermute(value, axis, pairs)


def per_device(
    stream,
    queries,
    key_rows,
    value_rows,
    sink_logits,
    out_weight,
    norm_gain,
    expert_ids,
    route_weights,
    gate_weight,
    up_weight,
    down_weight,
):
    block_len = queries.shape[0]
    kv_local = key_rows.shape[1] // HEAD_DIM
    group_size = queries.shape[1] // HEAD_DIM // kv_local
    kv_width = kv_local * HEAD_DIM
    joined = jnp.concatenate([key_rows, value_rows], axis=1)
    earlier = shifted(joined[block_len - WINDOW :], "seq", 1)
    extended = jnp.concatenate([earlier, joined], axis=0)
    key_part = extended[:, :kv_width].reshape(WINDOW + block_len, kv_local, HEAD_DIM)
    value_part = extended[:, kv_width:].reshape(WINDOW + block_len, kv_local, HEAD_DIM)
    offset = lax.axis_index("seq") * block_len
    query_pos = offset + jnp.arange(block_len, dtype=jnp.int32)
    key_pos = offset - WINDOW + jnp.arange(WINDOW + block_len, dtype=jnp.int32)
    distance = query_pos[:, None] - key_pos[None, :]
    allowed = (distance >= 0) & (distance < WINDOW) & (key_pos[None, :] >= 0)
    query_part = queries.reshape(block_len, kv_local, group_size, HEAD_DIM)
    scores = jnp.einsum(
        "igkd,jgd->gkij", query_part, key_part, preferred_element_type=jnp.float32
    ) * (1.0 / math.sqrt(HEAD_DIM))
    scores = jnp.where(allowed, scores, -jnp.inf)
    sink_grid = sink_logits.reshape(kv_local, group_size)[:, :, None, None]
    highest = jnp.maximum(jnp.max(scores, axis=-1, keepdims=True), sink_grid)
    weights = jnp.exp(scores - highest)
    summed = jnp.exp(sink_grid - highest) + jnp.sum(weights, axis=-1, keepdims=True)
    attn_probs = (weights / summed).astype(jnp.bfloat16)
    attended = jnp.einsum(
        "gkij,jgd->igkd", attn_probs, value_part, preferred_element_type=jnp.float32
    )
    attended = attended.astype(jnp.bfloat16).reshape(block_len, queries.shape[1])
    tokens_here = stream.shape[0]
    projected = lax.psum_scatter(
        jnp.dot(attended, out_weight, preferred_element_type=jnp.float32),
        "rep",
        scatter_dimension=0,
        tiled=True,
    )
    residual = (stream.astype(jnp.float32) + projected).astype(jnp.bfloat16)
    resid_f = residual.astype(jnp.float32)
    normed = (
        resid_f * lax.rsqrt(jnp.mean(resid_f * resid_f, axis=-1, keepdims=True) + 1e-05) * norm_gain
    ).astype(jnp.bfloat16)
    expert_count = EXP_DEV * lax.axis_size("seq")
    capacity = max(2, 3 * tokens_here * TOP // (2 * expert_count))
    flat_ids = expert_ids.reshape(-1)
    onehot = (flat_ids[:, None] == jnp.arange(expert_count, dtype=jnp.int32)[None, :]).astype(
        jnp.int32
    )
    earlier_count = jnp.cumsum(onehot, axis=0) - onehot
    slot_index = jnp.sum(earlier_count * onehot, axis=1)
    cell_index = (flat_ids * capacity + slot_index).reshape(tokens_here, TOP)
    chooser = jnp.any(
        cell_index[None, :, :]
        == jnp.arange(expert_count * capacity, dtype=jnp.int32)[:, None, None],
        axis=2,
    ).astype(jnp.bfloat16)
    outgoing = jnp.dot(chooser, normed, preferred_element_type=jnp.float32).astype(jnp.bfloat16)
    outgoing = outgoing.reshape(expert_count, capacity, normed.shape[1])
    paired = lax.all_gather(outgoing, "rep", axis=1, tiled=True)
    arrived = lax.all_to_all(paired, "seq", split_axis=0, concat_axis=1, tiled=True)
    gate_pre = jnp.einsum("erd,edf->erf", arrived, gate_weight, preferred_element_type=jnp.float32)
    up_pre = jnp.einsum("erd,edf->erf", arrived, up_weight, preferred_element_type=jnp.float32)
    activated = (gate_pre * jax.nn.sigmoid(1.702 * gate_pre) * (up_pre + 1.0)).astype(jnp.bfloat16)
    returned = lax.all_to_all(
        jnp.einsum(
            "erf,efd->erd", activated, down_weight, preferred_element_type=jnp.float32
        ).astype(jnp.bfloat16),
        "seq",
        split_axis=1,
        concat_axis=0,
        tiled=True,
    )
    expert_out = (
        lax.psum_scatter(returned, "rep", scatter_dimension=1, tiled=True)
        .astype(jnp.float32)
        .astype(jnp.bfloat16)
    )
    picked = expert_out.reshape(expert_count * capacity, -1)[cell_index.reshape(-1)]
    picked = picked.reshape(tokens_here, TOP, -1)
    expert_sum = jnp.sum(route_weights[:, :, None] * picked.astype(jnp.float32), axis=1)
    return (resid_f + expert_sum).astype(jnp.bfloat16)


def solution(mesh):
    return jax.shard_map(
        per_device,
        mesh=mesh,
        in_specs=(
            P(("groups", "seq", "rep"), None),
            P(("groups", "seq"), "rep"),
            P(("groups", "seq"), "rep"),
            P(("groups", "seq"), "rep"),
            P("rep"),
            P("rep", None),
            P(),
            P(("groups", "seq", "rep"), None),
            P(("groups", "seq", "rep"), None),
            P("seq", None, "rep"),
            P("seq", None, "rep"),
            P("seq", "rep", None),
        ),
        out_specs=P(("groups", "seq", "rep"), None),
        check_vma=False,
    )
```

profile of v0, /device:TPU:0, one launch (start us, length us, event | category | flops | bytes accessed | tf_op | source)
XLA Modules:
  0.0 402.9 jit_solution(9313064085084651106)
XLA Ops:
  6.5 1.0 constant_dynamic-update-slice_fusion.1
  7.5 0.9 constant_dynamic-update-slice_fusion
  8.4 4.8 %collective-permute-start = (bf16[128,256]{1,0:T(8,128)(2,1)S(1)}, bf16[128,256]{1,0:T(8,128)(2,1)S(1)}, u32[]{:S(2)}, u32[]{:S(2)}) collective-permute-start(bf16[128,256]{1,0:T(8,128)(2,1)S(1)} %slice.22), channel_id=1, source_target_pairs={{0,2},{2,4},{4,6},{6,8},{8,10},{10,12},{12,14},{1,3},{3,5},{5,7},{... | collective-permute-start | bytes 196616 | tf_op jit(solution)/shard_map/ppermute | solution.py:17
  13.3 0.2 fusion.20
  13.5 2.0 copy.47
  15.5 0.7 max.18
  16.3 0.7 pad_maximum_fusion
  16.9 1.0 copy.46
  17.9 2.1 fusion.2
  20.1 0.1 broadcast_maximum_fusion
  20.1 2.6 copy-done.2
  22.7 1.3 fusion.1
  24.0 0.1 exponential_add_fusion
  24.1 0.1 copy.45
  24.2 4.6 %fusion.11 = bf16[2,64,8,256]{3,1,2,0:T(8,128)(2,1)S(1)} fusion(bf16[384,2,64,1]{0,2,3,1:T(8,128)(2,1)S(1)} %bitcast.74, f32[2,384,256,8]{2,1,3,0:T(8,128)} %copy-done.2, f32[2,8,256]{2,1,0:T(8,128)S(1)} %exponential_add_fusion, f32[2,8,256]{2,1,0:T(8,128)S(1)} %broadcast_maximum_fusion, pred[256,384]{0,1:T(8,128)(4,1)S(1)} %fusion.20), kind=kOutput, calls=%fused_computation.18 | convolution fusion | flops 209453056 | bytes 7045120 | tf_op jit(solution)/shard_map/gkij,jgd->igkd/dot_general | solution.py:58
  28.8 2.2 fusion.30
  31.0 0.1 copy.50
  31.2 0.1 eq.42
  31.3 0.1 eq.38
  31.4 1.1 reduce-window.6
  32.5 0.2 slice_reduce_fusion
  32.8 0.1 fusion.23
  32.9 0.1 reduce_sum.42
  33.0 0.1 copy.53
  33.1 0.2 fusion.8
  33.3 7.9 %reduce-scatter.3.cloned.1.call-done = f32[128,1536]{1,0:T(8,128)} async-done(((f32[256,1536]{1,0:T(8,128)}), f32[128,1536]{1,0:T(8,128)}) %reduce-scatter.3.cloned.1.call-update) | async-done | bytes 786448 | tf_op jit(solution)/shard_map/reduce_scatter | solution.py:63
  41.2 1.4 fusion.12
  42.7 2.3 convolution_convert_fusion.1
  45.0 15.7 %all-gather.2.cloned.1.call-done = bf16[8,192,1536]{2,1,0:T(8,128)(2,1)} async-done(((bf16[8,96,1536]{2,1,0:T(8,128)(2,1)}), bf16[8,192,1536]{2,1,0:T(8,128)(2,1)}) %all-gather.2.cloned.1.call-update) | async-done | bytes 4718608 | tf_op jit(solution)/shard_map/all_gather | solution.py:90
  60.8 110.6 %all_to_all.21 = bf16[8,192,1536]{2,1,0:T(8,128)(2,1)S(1)} all-to-all(bf16[8,192,1536]{2,1,0:T(8,128)(2,1)} %all-gather.2.cloned.1.call-done), channel_id=1, replica_groups=mesh['groups'=2,'seq'=8,'rep'=2] {'seq'}, dimensions={0} | all-to-all | bytes 9437184 | tf_op jit(solution)/shard_map/all_to_all | solution.py:91
  171.4 2.2 copy-done.3
  173.6 5.4 %fusion.6 = f32[1536,768]{1,0:T(8,128)} fusion(bf16[1536,1536]{1,0:T(8,128)(2,1)S(1)} %bitcast.69, bf16[1,1536,768]{2,1,0:T(8,128)(2,1)S(1)} %copy-done.7), kind=kOutput, calls=%fused_computation.14 | convolution fusion | flops 3623878656 | bytes 11796480 | tf_op jit(solution)/shard_map/erd,edf->erf/dot_general | solution.py:92
  178.9 14.6 %fusion = bf16[1,1536,1536]{2,1,0:T(8,128)(2,1)} fusion(bf16[1,768,1536]{2,1,0:T(8,128)(2,1)} %param.23, f32[1536,768]{1,0:T(8,128)} %fusion.6, bf16[1536,1536]{1,0:T(8,128)(2,1)} %bitcast.70, bf16[1,1536,768]{2,1,0:T(8,128)(2,1)} %param.22), kind=kOutput, calls=%fused_computation.2 | convolution fusion | flops 7259553792 | bytes 18874368 | tf_op jit(solution)/shard_map/erf,efd->erd/dot_general | solution.py:96
  193.6 9.6 %copy.60 = bf16[1,1536,1536]{2,0,1:T(2,128)(2,1)} copy(bf16[1,1536,1536]{2,1,0:T(8,128)(2,1)} %fusion) | data formatting | bytes 9437184 | tf_op jit(solution)/shard_map/convert_element_type | solution.py:98
  203.1 0.5 broadcast.105
  203.6 32.0 %reduce.2 = bf16[1536,1536]{1,0:T(8,128)(2,1)} reduce(bf16[1536,1,1536]{2,1,0:T(2,128)(2,1)} %bitcast.65, bf16[]{:T(256)} %broadcast.105), dimensions={1}, to_apply=%bitcast.63.reduce_sub_computation | reduce | bytes 9437186
  235.6 8.2 %reshape.171 = bf16[8,2,147456]{2,1,0:T(2,128)(2,1)} reshape(bf16[1536,1536]{1,0:T(8,128)(2,1)} %reduce.2) | data formatting | bytes 9437184
  243.8 108.7 %all_to_all.22 = bf16[8,2,147456]{2,1,0:T(2,128)(2,1)} all-to-all(bf16[8,2,147456]{2,1,0:T(2,128)(2,1)} %reshape.171), channel_id=1, replica_groups=mesh['groups'=2,'seq'=8,'rep'=2] {'seq'}, dimensions={0} | all-to-all | bytes 9437184 | tf_op jit(solution)/shard_map/all_to_all | solution.py:95
  352.5 9.3 %reshape.172 = bf16[1536,1,1536]{2,1,0:T(2,128)(2,1)} reshape(bf16[8,2,147456]{2,1,0:T(2,128)(2,1)} %all_to_all.22) | data formatting | bytes 9437184
  361.9 7.2 %copy.58 = bf16[1,1536,1536]{2,1,0:T(8,128)(2,1)} copy(bf16[1,1536,1536]{2,0,1:T(2,128)(2,1)} %bitcast.66) | data formatting | bytes 9437184
  369.1 0.1 mul.92
  369.2 0.5 copy-done.6
  369.8 0.7 copy.49
  370.5 10.1 %reduce-scatter.5.cloned.1.call-done = bf16[8,96,1536]{2,1,0:T(8,128)(2,1)} async-done(((bf16[8,192,1536]{2,1,0:T(8,128)(2,1)}), bf16[8,96,1536]{2,1,0:T(8,128)(2,1)}) %reduce-scatter.5.cloned.1.call-update) | async-done | bytes 2359312 | tf_op jit(solution)/shard_map/reduce_scatter | solution.py:105
  380.7 6.5 %gather_fusion = bf16[512,1536]{1,0:T(8,128)(2,1)} fusion(bf16[768,1536]{1,0:T(8,128)(2,1)} %bitcast.64, s32[1024]{0:T(1024)S(1)} %pad_clamp_fusion), kind=kCustom, calls=%fused_computation | custom fusion | bytes 3147776 | tf_op jit(solution)/shard_map/gather | solution.py:109
  387.2 4.2 %reshape.159 = f32[128,4,1536]{2,1,0:T(4,128)} reshape(bf16[512,1536]{1,0:T(8,128)(2,1)} %gather_fusion) | data formatting | bytes 4718592 | tf_op jit(solution)/shard_map/convert_element_type | solution.py:111
  391.4 4.2 %multiply_reduce_fusion = f32[128,1536]{1,0:T(8,128)S(1)} fusion(f32[128,4,1536]{2,1,0:T(4,128)} %reshape.159, f32[128,4]{1,0:T(8,128)} %copy.49), kind=kLoop, calls=%fused_computation.10 | loop fusion | flops 1376256 | bytes 3934208 | tf_op jit(solution)/shard_map/reduce_sum | solution.py:111
  395.5 0.8 fusion.15
  (31 shorter events, 0.3 us)
Async XLA Ops:
  6.5 22.3 %copy-start = (bf16[1024,1536]{1,0:T(8,128)(2,1)S(1)}, bf16[1024,1536]{1,0:T(8,128)(2,1)}, u32[]{:S(2)}) copy-start(bf16[1024,1536]{1,0:T(8,128)(2,1)} %param.17) | copy-start | bytes 9437188
  6.5 34.7 %reduce-scatter.3.cloned.1.call-start = ((), (), s32[]{:S(2)}) async-start(), calls=%async_computation.4 | async-start | bytes 2359296 | tf_op jit(solution)/shard_map/reduce_scatter | solution.py:63
  8.4 7.9 %collective-permute-start = (bf16[128,256]{1,0:T(8,128)(2,1)S(1)}, bf16[128,256]{1,0:T(8,128)(2,1)S(1)}, u32[]{:S(2)}, u32[]{:S(2)}) collective-permute-start(bf16[128,256]{1,0:T(8,128)(2,1)S(1)} %slice.22), channel_id=1, source_target_pairs={{0,2},{2,4},{4,6},{6,8},{8,10},{10,12},{12,14},{1,3},{3,5},{5,7},{... | collective-permute-start | bytes 196616 | tf_op jit(solution)/shard_map/ppermute | solution.py:17
  20.1 2.7 copy-start.2
  28.8 2.3 copy-start.5
  28.8 13.9 %copy-start.4 = (f32[1536]{0:T(1024)S(1)}, f32[1536]{0:T(1024)}, u32[]{:S(2)}) copy-start(f32[1536]{0:T(1024)} %param.18) | copy-start | bytes 18436
  31.0 29.8 %all-gather.2.cloned.1.call-start = ((), (), s32[]{:S(2)}) async-start(), calls=%async_computation.5 | async-start | bytes 7077888 | tf_op jit(solution)/shard_map/all_gather | solution.py:90
  45.0 128.6 %copy-start.7 = (bf16[1,1536,768]{2,1,0:T(8,128)(2,1)S(1)}, bf16[1,1536,768]{2,1,0:T(8,128)(2,1)}, u32[]{:S(2)}) copy-start(bf16[1,1536,768]{2,1,0:T(8,128)(2,1)} %param.21) | copy-start | bytes 7077892
  45.0 335.7 %reduce-scatter.5.cloned.1.call-start = ((), (), s32[]{:S(2)}) async-start(), calls=%async_computation.6 | async-start | bytes 7077888 | tf_op jit(solution)/shard_map/reduce_scatter | solution.py:105
  171.4 2.2 copy-start.3
  369.1 0.7 copy-start.6
  380.7 15.7 %copy-start.1 = (bf16[1024,1536]{1,0:T(8,128)(2,1)S(1)}, bf16[1024,1536]{1,0:T(8,128)(2,1)}, u32[]{:S(2)}) copy-start(bf16[1024,1536]{1,0:T(8,128)(2,1)} %param.17) | copy-start | bytes 9437188
Sparse Core Ops, SparseCore 0:
  31.1 10.0 reduce-scatter.2
  45.1 15.6 all-gather.1
  369.2 11.3 reduce-scatter.4
where the time goes:
time: 404 us; the launch traced here: 403 us
  blocking collectives  219 us (54%)
  local copies, waits for them, and re-layouts  58.2 us (14%)
  other arithmetic  42.2 us (10%)
  waiting for transfers between devices  33.8 us (8%)
  matrix products  31.1 us (8%)
  between operations  13.3 us (3%)
  starting transfers between devices  4.93 us (1%)
    all_to_all x1, blocking collectives, per_device(): lax.all_to_all(paired, 'seq', split_axis=0, concat_axis=1, tiled=True)  111 us
    all_to_all x1, blocking collectives, per_device(): lax.all_to_all(jnp.einsum('erf,efd->erd', activated, down_weight, preferr...  109 us
    unnamed x24, local copies, waits for them, and re-layouts  34.5 us
    unnamed x1, other arithmetic  32 us
    all_gather x1, waiting for transfers between devices, per_device(): paired = lax.all_gather(outgoing, 'rep', axis=1, tiled=True)  15.7 us
    dot_general x1, matrix products, per_device(): jnp.einsum('erf,efd->erd', activated, down_weight, preferred_element_type...  14.6 us
    reduce_scatter x1, waiting for transfers between devices, per_device(): lax.psum_scatter(returned, 'rep', scatter_dimension=1, tiled=True)  10.1 us
    convert_element_type x1, local copies, waits for them, and re-layouts, per_device(): returned = lax.all_to_all(jnp.einsum('erf,efd->erd', activated, down_weig...  9.58 us
  transfers between devices with their start and end apart: 4, of which 3 were waited for; matrix products, arithmetic and copies ran while one was open for 2% of the time, Pallas kernels for 0%

commit v1 on v0

v1 whole, which is shorter than its diff:
```python
import functools
import math

import jax
import jax.numpy as jnp
from jax import lax
from jax.experimental import pallas as pl
from jax.experimental.pallas import tpu as pltpu
from jax.sharding import PartitionSpec as P

HEAD_DIM = 64
WINDOW = 128
TOP = 4
EXP_DEV = 1
LANES = 128
SNAKES = {8: (0, 2, 4, 6, 7, 5, 3, 1)}
MIB = 1 << 20


def shifted(value, axis, by):
    peers = lax.axis_size(axis)
    pairs = [(i, i + by) for i in range(peers) if 0 <= i + by < peers]
    return lax.ppermute(value, axis, pairs)


def swapped(value, axis, bit=1):
    peers = lax.axis_size(axis)
    return lax.ppermute(value, axis, [(i, i ^ bit) for i in range(peers)])


def mm(a, b):
    return jnp.dot(a, b, preferred_element_type=jnp.float32)


def attend_kernel(
    group_pairs, first_ref, sink_ref, q_ref, kp_ref, kc_ref, vp_ref, vc_ref, ow_ref, *rest
):
    mix = len(rest) > 2
    if mix:
        rank_ref, other_ref, send_ref, own_ref, total = rest
    else:
        out_ref, total = rest
    step = pl.program_id(0)
    rows = q_ref.shape[0]
    keys = kp_ref.shape[0] + kc_ref.shape[0]
    pairs_step = q_ref.shape[1] // LANES
    group = (step * pairs_step) // group_pairs

    lane_k = lax.broadcasted_iota(jnp.int32, (keys, LANES), 1)
    low = lane_k < HEAD_DIM
    k = jnp.concatenate([kp_ref[...], kc_ref[...]], axis=0).astype(jnp.float32)
    v = jnp.concatenate([vp_ref[...], vc_ref[...]], axis=0).astype(jnp.float32)
    k_low = jnp.where(low, jnp.where(group == 0, k, pltpu.roll(k, HEAD_DIM, 1)), 0.0)
    v_low = jnp.where(low, jnp.where(group == 0, v, pltpu.roll(v, HEAD_DIM, 1)), 0.0)
    k_high, v_high = pltpu.roll(k_low, HEAD_DIM, 1), pltpu.roll(v_low, HEAD_DIM, 1)
    kk = jnp.concatenate([k_low, k_high], axis=0).astype(jnp.bfloat16)
    one_low = jnp.where(low, 1.0, 0.0)
    vv = jnp.concatenate(
        [
            jnp.concatenate([v_low, one_low], axis=1),
            jnp.concatenate([v_high, 1.0 - one_low], axis=1),
        ],
        axis=0,
    ).astype(jnp.bfloat16)

    row = lax.broadcasted_iota(jnp.int32, (rows, keys), 0)
    column = lax.broadcasted_iota(jnp.int32, (rows, keys), 1)
    least = jnp.where(first_ref[0] == 1, WINDOW, 0)
    allowed = (column <= row + WINDOW) & (column > row) & (column >= least)
    low_out = lax.broadcasted_iota(jnp.int32, (rows, LANES), 1) < HEAD_DIM
    scale = 1.0 / math.sqrt(HEAD_DIM)

    done = []
    for pair in range(pairs_step):
        q = q_ref[:, pair * LANES : (pair + 1) * LANES]
        scores = lax.dot_general(
            q, kk, (((1,), (1,)), ((), ())), preferred_element_type=jnp.float32
        )
        weights, sinks = [], []
        for side in range(2):
            part = jnp.where(allowed, scores[:, side * keys : (side + 1) * keys] * scale, -jnp.inf)
            sink = sink_ref[(step * pairs_step + pair) * 2 + side]
            highest = jnp.maximum(jnp.max(part, axis=1, keepdims=True), sink)
            weights.append(jnp.exp(part - highest).astype(jnp.bfloat16))
            sinks.append(jnp.exp(sink - highest))
        both = mm(jnp.concatenate(weights, axis=1), vv)
        below = both[:, LANES:] + jnp.where(low_out, sinks[0], sinks[1])
        done.append((both[:, :LANES] / below).astype(jnp.bfloat16))
    part = mm(jnp.concatenate(done, axis=1), ow_ref[...])

    @pl.when(step == 0)
    def _():
        total[...] = part

    @pl.when(step > 0)
    def _():
        total[...] += part

    @pl.when(step == pl.num_programs(0) - 1)
    def _():
        if mix:
            mine = total[...]
            other = other_ref[...]
            own_first = rank_ref[0] == 0
            own_ref[...] = jnp.where(own_first, mine, other)
            send_ref[...] = jnp.where(own_first, other, mine).astype(jnp.bfloat16)
        else:
            out_ref[...] = total[...]


def attend(half, first, sinks, queries, keys, values, out_weight, rank=None, other=None):
    (k_prev, kp_index), (k_cur, kc_index) = keys
    (v_prev, vp_index), (v_cur, vc_index) = values
    rows, width, model = WINDOW, queries.shape[1], out_weight.shape[1]
    block = min(width, 256)
    group_pairs = width // LANES // (k_cur.shape[1] // HEAD_DIM)
    smem = pl.BlockSpec(memory_space=pltpu.SMEM)

    def fixed(index):
        return pl.BlockSpec((rows, LANES), lambda i: (index, 0))

    in_specs = [
        smem,
        smem,
        pl.BlockSpec((rows, block), lambda i: (half, i)),
        fixed(kp_index),
        fixed(kc_index),
        fixed(vp_index),
        fixed(vc_index),
        pl.BlockSpec((block, model), lambda i: (i, 0)),
    ]
    operands = [first, sinks, queries, k_prev, k_cur, v_prev, v_cur, out_weight]
    whole = pl.BlockSpec((rows, model), lambda i: (0, 0))
    wide = jax.ShapeDtypeStruct((rows, model), jnp.float32)
    narrow = jax.ShapeDtypeStruct((rows, model), jnp.bfloat16)
    if rank is None:
        out_shape, out_specs = wide, whole
    else:
        in_specs += [smem, whole]
        operands += [rank, other]
        out_shape, out_specs = (narrow, wide), (whole, whole)
    return pl.pallas_call(
        functools.partial(attend_kernel, group_pairs),
        grid=(width // block,),
        in_specs=in_specs,
        out_specs=out_specs,
        out_shape=out_shape,
        scratch_shapes=[pltpu.VMEM((rows, model), jnp.float32)],
        compiler_params=pltpu.CompilerParams(vmem_limit_bytes=32 * MIB),
        cost_estimate=pl.CostEstimate(
            flops=2 * rows * width * (model + 1024), bytes_accessed=6 * MIB, transcendentals=0
        ),
        name="attend",
    )(*operands)


def norm_kernel(stream_ref, own_ref, came_ref, gain_ref, residual_ref, *normed_refs):
    residual = (
        stream_ref[...].astype(jnp.float32) + own_ref[...] + came_ref[...].astype(jnp.float32)
    ).astype(jnp.bfloat16)
    residual_ref[...] = residual
    wide = residual.astype(jnp.float32)
    mean = jnp.mean(wide * wide, axis=-1, keepdims=True)
    normed = (wide * lax.rsqrt(mean + 1e-05) * gain_ref[...]).astype(jnp.bfloat16)
    rows = normed_refs[0].shape[0]
    for index, ref in enumerate(normed_refs):
        ref[...] = normed[index * rows : (index + 1) * rows]


def norm(stream, own, came, gain, pieces):
    rows, model = stream.shape
    return pl.pallas_call(
        norm_kernel,
        out_shape=[jax.ShapeDtypeStruct((rows, model), jnp.bfloat16)]
        + [jax.ShapeDtypeStruct((rows // pieces, model), jnp.bfloat16)] * pieces,
        compiler_params=pltpu.CompilerParams(vmem_limit_bytes=32 * MIB),
        cost_estimate=pl.CostEstimate(
            flops=8 * rows * model, bytes_accessed=14 * rows * model, transcendentals=rows
        ),
        name="norm",
    )(stream, own, came, gain.reshape(1, model))


def spread_kernel(ids_ref, weights_ref, out_ref):
    rows = ids_ref.shape[0]
    lane = lax.broadcasted_iota(jnp.int32, (rows, LANES), 1)
    dense = jnp.zeros((rows, LANES), jnp.float32)
    for k in range(TOP):
        dense += jnp.where(ids_ref[:, k : k + 1] == lane, weights_ref[:, k : k + 1], 0.0)
    out_ref[...] = dense.T[: out_ref.shape[0]]


def spread(expert_ids, route_weights, expert_count):
    return pl.pallas_call(
        spread_kernel,
        out_shape=jax.ShapeDtypeStruct((expert_count, expert_ids.shape[0]), jnp.float32),
        name="spread",
    )(expert_ids, route_weights)


def expert_kernel(places, *refs):
    count = len(places)
    x_refs, weight_ref, halves = refs[:count], refs[count], refs[count + 1 : count + 7]
    out_refs, (x, total) = refs[count + 7 : count + 7 + count], refs[count + 7 + count :]
    step, steps = pl.program_id(0), pl.num_programs(0)
    rows = x_refs[0].shape[0]

    @pl.when(step == 0)
    def _():
        for index, ref in enumerate(x_refs):
            x[index * rows : (index + 1) * rows] = ref[...]

    def tile(gate_ref, up_ref, down_ref):
        gate_pre = mm(x[...], gate_ref[...])
        up_pre = mm(x[...], up_ref[...])
        activated = gate_pre * jax.nn.sigmoid(1.702 * gate_pre) * (up_pre + 1.0)
        part = mm(activated.astype(jnp.bfloat16), down_ref[...])

        @pl.when(step == 0)
        def _():
            total[...] = part

        @pl.when(step > 0)
        def _():
            total[...] += part

    @pl.when(step < steps // 2)
    def _():
        tile(*halves[:3])

    @pl.when(step >= steps // 2)
    def _():
        tile(*halves[3:])

    @pl.when(step == steps - 1)
    def _():
        columns = weight_ref[...].T
        for index, ((source, start), ref) in enumerate(zip(places, out_refs)):
            scale = columns[start : start + rows, source : source + 1]
            ref[...] = (total[index * rows : (index + 1) * rows] * scale).astype(jnp.bfloat16)


def experts(blocks, places, weights, halves):
    rows, model = blocks[0].shape
    half = halves[0].shape[1]
    tile = min(256, half)
    tiles = half // tile
    block = pl.BlockSpec((rows, model), lambda i: (0, 0))

    def columns(low):
        return pl.BlockSpec((model, tile), lambda i: (0, jnp.clip(i - low, 0, tiles - 1)))

    def lines(low):
        return pl.BlockSpec((tile, model), lambda i: (jnp.clip(i - low, 0, tiles - 1), 0))

    total_rows = rows * len(blocks)
    return pl.pallas_call(
        functools.partial(expert_kernel, tuple(places)),
        grid=(2 * tiles,),
        in_specs=[block] * len(blocks)
        + [pl.BlockSpec(weights.shape, lambda i: (0, 0))]
        + [columns(0), columns(0), lines(0), columns(tiles), columns(tiles), lines(tiles)],
        out_specs=[block] * len(blocks),
        out_shape=[jax.ShapeDtypeStruct((rows, model), jnp.bfloat16)] * len(blocks),
        scratch_shapes=[
            pltpu.VMEM((total_rows, model), jnp.bfloat16),
            pltpu.VMEM((total_rows, model), jnp.float32),
        ],
        compiler_params=pltpu.CompilerParams(vmem_limit_bytes=40 * MIB),
        cost_estimate=pl.CostEstimate(
            flops=12 * total_rows * model * half,
            bytes_accessed=12 * model * half,
            transcendentals=2 * total_rows * half,
        ),
        name="experts",
    )(*blocks, weights, *halves)


def ring_experts(
    residual, pieces, expert_ids, route_weights, gate_weight, up_weight, down_weight, others
):
    chips = lax.axis_size("seq")
    ring = SNAKES.get(chips, tuple(range(chips)))
    far = chips // 2
    ahead = [(ring[i], ring[(i + 1) % chips]) for i in range(chips)]
    back = [(to, of) for of, to in ahead]
    me = lax.axis_index("seq")
    rows = pieces[0].shape[0]

    known = spread(expert_ids, route_weights, chips)
    bit = 1
    while bit < chips:
        known = jnp.concatenate([known, swapped(known, "seq", bit)], axis=0)
        bit *= 2
    known = known.reshape(chips, chips, -1)
    place_of = [ring.index(i) for i in range(chips)]
    mine = jnp.array(place_of, jnp.int32)[me]
    source = jnp.array(ring, jnp.int32)[(mine - jnp.arange(chips, dtype=jnp.int32)) % chips]
    wanted = (
        ((me ^ source)[:, None, None] == jnp.arange(chips, dtype=jnp.int32)[None, :, None])
        & (jnp.arange(chips, dtype=jnp.int32)[None, None, :] == me)
    )
    weights = jnp.sum(jnp.where(wanted[..., None], known[None], 0.0), axis=(1, 2))

    halves = (gate_weight, up_weight, down_weight) + tuple(others)
    lead, trail = 0, 1
    came = [{(0, 0): pieces[0], (0, 1): pieces[1]}, {(0, 0): pieces[0], (0, 1): pieces[1]}]
    hops = (ahead, back)
    leads = (0, 1)

    def bring(distance, kind):
        for side in range(2):
            piece = leads[side] if kind == lead else 1 - leads[side]
            came[side][distance, piece] = lax.ppermute(
                came[side][distance - 1, piece], "seq", hops[side]
            )

    given = {}

    def apply(keys):
        blocks, places = [], []
        for side, distance, piece in keys:
            blocks.append(came[side][distance, piece])
            places.append(((distance if side == 0 else -distance) % chips, piece * rows))
        outs = experts(blocks, places, weights, halves)
        for (at, start), out in zip(places, outs):
            given[at, start // rows] = out

    for distance in range(1, far):
        bring(distance, lead)
        bring(distance, trail)
    bring(far, lead)
    for distance in range(1, far):
        keys = [(side, distance, piece) for side in range(2) for piece in range(2)]
        if distance == 1:
            keys = [(0, 0, 0), (0, 0, 1)] + keys
        if distance < far - 1:
            apply(keys)
    apply(
        [(side, far - 1, leads[side]) for side in range(2)]
        + [(side, far, leads[side]) for side in range(2)]
    )
    apply([(side, far - 1, 1 - leads[side]) for side in range(2)])

    def own(side, distance, piece):
        return given[(-distance if side == 0 else distance) % chips, piece]

    def plus(a, b):
        return (a.astype(jnp.float32) + b.astype(jnp.float32)).astype(jnp.bfloat16)

    moving = {}
    for distance in range(far, 0, -1):
        for kind in (trail, lead):
            if distance == far and kind == trail:
                continue
            for side in range(2):
                piece = leads[side] if kind == lead else 1 - leads[side]
                value = own(side, distance, piece)
                if (side, piece) in moving:
                    value = plus(moving[side, piece], value)
                moving[side, piece] = lax.ppermute(value, "seq", hops[side])
    final = []
    for piece in range(2):
        total = given[0, piece].astype(jnp.float32)
        for side in range(2):
            total += moving[side, piece].astype(jnp.float32)
        final.append(total)
    return (residual.astype(jnp.float32) + jnp.concatenate(final, axis=0)).astype(jnp.bfloat16)


def dispatched_experts(
    residual, normed, expert_ids, route_weights, gate_weight, up_weight, down_weight
):
    tokens_here = normed.shape[0]
    resid_f = residual.astype(jnp.float32)
    expert_count = EXP_DEV * lax.axis_size("seq")
    capacity = max(2, 3 * tokens_here * TOP // (2 * expert_count))
    flat_ids = expert_ids.reshape(-1)
    onehot = (flat_ids[:, None] == jnp.arange(expert_count, dtype=jnp.int32)[None, :]).astype(
        jnp.int32
    )
    earlier_count = jnp.cumsum(onehot, axis=0) - onehot
    slot_index = jnp.sum(earlier_count * onehot, axis=1)
    cell_index = (flat_ids * capacity + slot_index).reshape(tokens_here, TOP)
    chooser = jnp.any(
        cell_index[None, :, :]
        == jnp.arange(expert_count * capacity, dtype=jnp.int32)[:, None, None],
        axis=2,
    ).astype(jnp.bfloat16)
    outgoing = mm(chooser, normed).astype(jnp.bfloat16)
    outgoing = outgoing.reshape(expert_count, capacity, normed.shape[1])
    paired = lax.all_gather(outgoing, "rep", axis=1, tiled=True)
    arrived = lax.all_to_all(paired, "seq", split_axis=0, concat_axis=1, tiled=True)[0]
    gate_pre = mm(arrived, gate_weight)
    up_pre = mm(arrived, up_weight)
    activated = (gate_pre * jax.nn.sigmoid(1.702 * gate_pre) * (up_pre + 1.0)).astype(jnp.bfloat16)
    returned = lax.all_to_all(
        mm(activated, down_weight).astype(jnp.bfloat16)[None],
        "seq",
        split_axis=1,
        concat_axis=0,
        tiled=True,
    )
    expert_out = lax.psum_scatter(returned, "rep", scatter_dimension=1, tiled=True)
    picked = expert_out.reshape(expert_count * capacity, -1)[cell_index.reshape(-1)]
    picked = picked.reshape(tokens_here, TOP, -1)
    expert_sum = jnp.sum(route_weights[:, :, None] * picked.astype(jnp.float32), axis=1)
    return (resid_f + expert_sum).astype(jnp.bfloat16)


def per_device(
    stream,
    queries,
    key_rows,
    value_rows,
    sink_logits,
    out_weight,
    norm_gain,
    expert_ids,
    route_weights,
    gate_weight,
    up_weight,
    down_weight,
):
    block_len = queries.shape[0]
    seq = lax.axis_index("seq")
    rank = lax.axis_index("rep").astype(jnp.int32).reshape(1)
    gate_weight, up_weight, down_weight = gate_weight[0], up_weight[0], down_weight[0]
    use_ring = EXP_DEV * lax.axis_size("seq") <= 2 * TOP

    tail = jnp.concatenate([key_rows[block_len - WINDOW :], value_rows[block_len - WINDOW :]], axis=1)
    earlier = shifted(tail, "seq", 1)
    if use_ring:
        others = [swapped(w, "rep") for w in (gate_weight, up_weight, down_weight)]
    never = jnp.zeros((1,), jnp.int32)
    first = (seq == 0).astype(jnp.int32).reshape(1)
    later_half = attend(
        1,
        never,
        sink_logits,
        queries,
        ((key_rows, 0), (key_rows, 1)),
        ((value_rows, 0), (value_rows, 1)),
        out_weight,
    )
    k_prev, v_prev = earlier[:, : key_rows.shape[1]], earlier[:, key_rows.shape[1] :]
    send, own = attend(
        0,
        first,
        sink_logits,
        queries,
        ((k_prev, 0), (key_rows, 0)),
        ((v_prev, 0), (value_rows, 0)),
        out_weight,
        rank,
        later_half,
    )
    came = swapped(send, "rep")
    residual, *pieces = norm(stream, own, came, norm_gain, 2)
    if use_ring:
        return ring_experts(
            residual,
            pieces,
            expert_ids,
            route_weights,
            gate_weight,
            up_weight,
            down_weight,
            others,
        )
    return dispatched_experts(
        residual,
        jnp.concatenate(pieces, axis=0),
        expert_ids,
        route_weights,
        gate_weight,
        up_weight,
        down_weight,
    )


def solution(mesh):
    return jax.shard_map(
        per_device,
        mesh=mesh,
        in_specs=(
            P(("groups", "seq", "rep"), None),
            P(("groups", "seq"), "rep"),
            P(("groups", "seq"), "rep"),
            P(("groups", "seq"), "rep"),
            P("rep"),
            P("rep", None),
            P(),
            P(("groups", "seq", "rep"), None),
            P(("groups", "seq", "rep"), None),
            P("seq", None, "rep"),
            P("seq", None, "rep"),
            P("seq", "rep", None),
        ),
        out_specs=P(("groups", "seq", "rep"), None),
        check_vma=False,
    )
```

time: 404 us -> 151 us (0.37)
  blocking collectives: 219 us -> 0 us
  Pallas kernels: 0 us -> 50.6 us
  local copies, waits for them, and re-layouts: 58.2 us -> 15 us
  other arithmetic: 42.2 us -> 4.49 us
  starting transfers between devices: 4.93 us -> 41.3 us
  matrix products: 31.1 us -> 0 us
  between operations: 13.3 us -> 0.3 us
  waiting for transfers between devices: 33.8 us -> 38.5 us
    all_to_all x2 -> x0, blocking collectives: 219 us -> none  [the longest x1 111 us: per_device(): lax.all_to_all(paired, 'seq', split_axis=0, concat_axis=1, tiled=True)]
    pallas_call x0 -> x8, Pallas kernels: none -> 50.6 us  [the longest x4 36.8 us: experts(): pl.pallas_call(functools.partial(expert_kernel, tuple(places)), grid=(2 *...]
    ppermute x0 -> x35, waiting for transfers between devices: none -> 38.5 us  [the longest x14 22.7 us: bring(): lax.ppermute(came[side][distance - 1, piece], 'seq', hops[side])]
    ppermute x0 -> x35, starting transfers between devices: none -> 36.9 us  [the longest x14 15 us: ring_experts(): moving[side, piece] = lax.ppermute(value, 'seq', hops[side])]
    unnamed x1 -> x0, other arithmetic: 32 us -> none
    dot_general x6 -> x0, matrix products: 31.1 us -> none  [the longest x1 14.6 us: per_device(): jnp.einsum('erf,efd->erd', activated, down_weight, preferred_element_type...]
    unnamed x24 -> x36, local copies, waits for them, and re-layouts: 34.5 us -> 10.8 us
    reduce_scatter x2 -> x0, waiting for transfers between devices: 18 us -> none  [the longest x1 10.1 us: per_device(): lax.psum_scatter(returned, 'rep', scatter_dimension=1, tiled=True)]
  transfers between devices with their start and end apart: 4 -> 36, of which waited for: 3 -> 13; matrix products, arithmetic and copies ran while one was open for 2% -> 6% of each run, Pallas kernels for 0% -> 34%
where the time goes in v1:
time: 151 us; the launch traced here: 150 us
  Pallas kernels  50.6 us (34%)
  starting transfers between devices  41.3 us (27%)
  waiting for transfers between devices  38.5 us (25%)
  local copies, waits for them, and re-layouts  15 us (10%)
  other arithmetic  4.49 us (3%)
    pallas_call x4, Pallas kernels, experts(): pl.pallas_call(functools.partial(expert_kernel, tuple(places)), grid=(2 *...  36.8 us
    ppermute x14, waiting for transfers between devices, bring(): lax.ppermute(came[side][distance - 1, piece], 'seq', hops[side])  22.7 us
    ppermute x14, starting transfers between devices, ring_experts(): moving[side, piece] = lax.ppermute(value, 'seq', hops[side])  15 us
    ppermute x14, starting transfers between devices, bring(): lax.ppermute(came[side][distance - 1, piece], 'seq', hops[side])  15 us
    ppermute x14, waiting for transfers between devices, ring_experts(): moving[side, piece] = lax.ppermute(value, 'seq', hops[side])  11.4 us
    unnamed x36, local copies, waits for them, and re-layouts  10.8 us
    pallas_call x2, Pallas kernels, attend(): pl.pallas_call(functools.partial(attend_kernel, group_pairs), grid=(width...  10 us
    ppermute x7, starting transfers between devices, swapped(): return lax.ppermute(value, axis, [(i, i ^ bit) for i in range(peers)])  6.9 us
  transfers between devices with their start and end apart: 36, of which 13 were waited for; matrix products, arithmetic and copies ran while one was open for 6% of the time, Pallas kernels for 34%

profile of v1, /device:TPU:0, one launch (start us, length us, event | category | flops | bytes accessed | tf_op | source)
XLA Modules:
  0.0 150.1 jit_solution(5920342722284502826)
XLA Ops:
  2.5 4.4 %collective-permute-start = (bf16[128,256]{1,0:T(8,128)(2,1)S(1)}, bf16[128,256]{1,0:T(8,128)(2,1)S(1)}, u32[]{:S(2)}, u32[]{:S(2)}) collective-permute-start(bf16[128,256]{1,0:T(8,128)(2,1)S(1)} %pad_maximum_fusion), channel_id=1, source_target_pairs={{0,2},{2,4},{4,6},{6,8},{8,10},{10,12},{12,14},{1,3},{3,5},{5,7},{... | collective-permute-start | bytes 196616 | tf_op jit(solution)/shard_map/ppermute | solution.py:23
  6.9 1.9 %copy-done.4 = bf16[1024,1536]{1,0:T(8,128)(2,1)S(1)} copy-done((bf16[1024,1536]{1,0:T(8,128)(2,1)S(1)}, bf16[1024,1536]{1,0:T(8,128)(2,1)}, u32[]{:S(2)}) %copy-start.4) | copy-done | bytes 3145752
  8.8 1.0 copy-done.6
  12.2 4.6 %attend.2.rest_1_ = f32[128,1536]{1,0:T(8,128)S(1)} custom-call(s32[1]{0:T(128)} %constant.30.clone.1.first_ref, f32[16]{0:T(128)S(1)} %copy-done.13, bf16[256,1024]{1,0:T(8,128)(2,1)S(1)} %copy-done.6, bf16[256,128]{1,0:T(8,128)(2,1)S(1)} %copy-done.9, bf16[256,128]{1,0:T(8,128)(2,1)S(1)} %copy-done.9, bf16[256,128]{1,0:T(8,128)(2,1)S(1)} %copy-done.8, ...), custom_call_target="tpu_custom_call" | custom-call | flops 671088640 | bytes 6291456 | tf_op jit(solution)/shard_map/attend/pallas_call | solution.py:142
  16.9 5.4 %attend.3 = (bf16[128,1536]{1,0:T(8,128)(2,1)}, f32[128,1536]{1,0:T(8,128)S(1)}) custom-call(s32[1]{0:T(128)} %bitcast.first_ref, f32[16]{0:T(128)S(1)} %copy-done.13, bf16[256,1024]{1,0:T(8,128)(2,1)S(1)} %copy-done.7, bf16[128,128]{1,0:T(8,128)(2,1)S(1)} %get-tuple-element.48.kp_ref, bf16[256,128]{1,0:T(8,128)(2,1)S(1)} %copy-done.9, ...), custom_call_target="tpu_custom_call" | custom-call | flops 671088640 | bytes 6291456 | tf_op jit(solution)/shard_map/attend/pallas_call | solution.py:142
  24.0 1.7 %spread.1 = f32[8,128]{1,0:T(8,128)} custom-call(s32[128,4]{1,0:T(8,128)} %copy.19.ids_ref, f32[128,4]{1,0:T(8,128)} %copy.20.weights_ref), custom_call_target="tpu_custom_call" | custom-call | tf_op jit(solution)/shard_map/spread/pallas_call | solution.py:194
  25.7 1.5 %collective-permute-start.6 = (f32[8,128]{1,0:T(8,128)}, f32[8,128]{1,0:T(8,128)S(1)}, u32[]{:S(2)}, u32[]{:S(2)}) collective-permute-start(f32[8,128]{1,0:T(8,128)} %spread.1), channel_id=1, source_target_pairs={{0,2},{2,0},{4,6},{6,4},{8,10},{10,8},{12,14},{14,12},{1,3},{3,1},... | collective-permute-start | bytes 12296 | tf_op jit(solution)/shard_map/ppermute | solution.py:28
  27.3 2.3 %collective-permute-done.6 = f32[8,128]{1,0:T(8,128)S(1)} collective-permute-done((f32[8,128]{1,0:T(8,128)}, f32[8,128]{1,0:T(8,128)S(1)}, u32[]{:S(2)}, u32[]{:S(2)}) %collective-permute-start.6) | collective-permute-done | bytes 4128 | tf_op jit(solution)/shard_map/ppermute | solution.py:28
  30.2 1.6 %collective-permute-start.7 = (f32[16,128]{1,0:T(8,128)S(1)}, f32[16,128]{1,0:T(8,128)S(1)}, u32[]{:S(2)}, u32[]{:S(2)}) collective-permute-start(f32[16,128]{1,0:T(8,128)S(1)} %pad_maximum_fusion.2), channel_id=1, source_target_pairs={{0,4},{2,6},{4,0},{6,2},{8,12},{10,14},{12,8},{14,10},{1,5},{3,7},... | collective-permute-start | bytes 24584 | tf_op jit(solution)/shard_map/ppermute | solution.py:28
  31.8 2.1 %collective-permute-done.7 = f32[16,128]{1,0:T(8,128)S(1)} collective-permute-done((f32[16,128]{1,0:T(8,128)S(1)}, f32[16,128]{1,0:T(8,128)S(1)}, u32[]{:S(2)}, u32[]{:S(2)}) %collective-permute-start.7) | collective-permute-done | bytes 8224 | tf_op jit(solution)/shard_map/ppermute | solution.py:28
  34.6 2.6 %collective-permute-start.8 = (f32[32,128]{1,0:T(8,128)S(1)}, f32[32,128]{1,0:T(8,128)}, u32[]{:S(2)}, u32[]{:S(2)}) collective-permute-start(f32[32,128]{1,0:T(8,128)S(1)} %pad_maximum_fusion.1), channel_id=1, source_target_pairs={{0,8},{2,10},{4,12},{6,14},{8,0},{10,2},{12,4},{14,6},{1,9},{3,11}... | collective-permute-start | bytes 49160 | tf_op jit(solution)/shard_map/ppermute | solution.py:28
  37.9 2.1 %norm.1 = (bf16[128,1536]{1,0:T(8,128)(2,1)S(1)}, bf16[64,1536]{1,0:T(8,128)(2,1)}, bf16[64,1536]{1,0:T(8,128)(2,1)}) custom-call(bf16[128,1536]{1,0:T(8,128)(2,1)S(1)} %copy-done.10, f32[128,1536]{1,0:T(8,128)S(1)} %get-tuple-element.26.own_ref, bf16[128,1536]{1,0:T(8,128)(2,1)} %collective-permute-done.1.came_ref, f32[1,1536]{1,0:T(1,128)S(1)} %reshape.97.gain_ref), custom_call_target="tpu_custom_call" | custom-call | flops 1572864 | bytes 2752512 | tf_op jit(solution)/shard_map/norm/pallas_call | solution.py:172
  40.7 1.6 %collective-permute-start.2 = (bf16[64,1536]{1,0:T(8,128)(2,1)}, bf16[64,1536]{1,0:T(8,128)(2,1)S(1)}, u32[]{:S(2)}, u32[]{:S(2)}) collective-permute-start(bf16[64,1536]{1,0:T(8,128)(2,1)} %get-tuple-element.29.refs_0_), channel_id=1, source_target_pairs={{0,4},{4,8},{8,12},{12,14},{14,10},{10,6},{6,2},{2,0},{1,5},{5,9},... | collective-permute-start | bytes 589832 | tf_op jit(solution)/shard_map/ppermute | solution.py:314
  42.7 1.3 dynamic_slice.3
  44.6 2.5 %collective-permute-done.2.refs_2_ = bf16[64,1536]{1,0:T(8,128)(2,1)S(1)} collective-permute-done((bf16[64,1536]{1,0:T(8,128)(2,1)}, bf16[64,1536]{1,0:T(8,128)(2,1)S(1)}, u32[]{:S(2)}, u32[]{:S(2)}) %collective-permute-start.2) | collective-permute-done | bytes 196640 | tf_op jit(solution)/shard_map/ppermute | solution.py:314
  47.1 1.6 %collective-permute-start.3 = (bf16[64,1536]{1,0:T(8,128)(2,1)}, bf16[64,1536]{1,0:T(8,128)(2,1)S(1)}, u32[]{:S(2)}, u32[]{:S(2)}) collective-permute-start(bf16[64,1536]{1,0:T(8,128)(2,1)} %get-tuple-element.30.refs_1_), channel_id=1, source_target_pairs={{0,4},{4,8},{8,12},{12,14},{14,10},{10,6},{6,2},{2,0},{1,5},{5,9},... | collective-permute-start | bytes 589832 | tf_op jit(solution)/shard_map/ppermute | solution.py:314
  50.0 4.8 %collective-permute-done.3.refs_3_ = bf16[64,1536]{1,0:T(8,128)(2,1)S(1)} collective-permute-done((bf16[64,1536]{1,0:T(8,128)(2,1)}, bf16[64,1536]{1,0:T(8,128)(2,1)S(1)}, u32[]{:S(2)}, u32[]{:S(2)}) %collective-permute-start.3) | collective-permute-done | bytes 196640 | tf_op jit(solution)/shard_map/ppermute | solution.py:314
  54.7 1.8 %collective-permute-start.12 = (bf16[64,1536]{1,0:T(8,128)(2,1)S(1)}, bf16[64,1536]{1,0:T(8,128)(2,1)S(1)}, u32[]{:S(2)}, u32[]{:S(2)}) collective-permute-start(bf16[64,1536]{1,0:T(8,128)(2,1)S(1)} %collective-permute-done.2.refs_2_), channel_id=1, source_target_pairs={{0,4},{4,8},{8,12},{12,14},{14,10},{10,6},{6,2},{2,0},{1,5},{5,9},... | collective-permute-start | bytes 589832 | tf_op jit(solution)/shard_map/ppermute | solution.py:314
  57.3 4.8 %collective-permute-done.12.refs_0_ = bf16[64,1536]{1,0:T(8,128)(2,1)S(1)} collective-permute-done((bf16[64,1536]{1,0:T(8,128)(2,1)S(1)}, bf16[64,1536]{1,0:T(8,128)(2,1)S(1)}, u32[]{:S(2)}, u32[]{:S(2)}) %collective-permute-start.12) | collective-permute-done | bytes 196640 | tf_op jit(solution)/shard_map/ppermute | solution.py:314
  62.1 1.4 collective-permute-start.19
  64.3 4.3 %collective-permute-done.19.refs_1_ = bf16[64,1536]{1,0:T(8,128)(2,1)S(1)} collective-permute-done((bf16[64,1536]{1,0:T(8,128)(2,1)S(1)}, bf16[64,1536]{1,0:T(8,128)(2,1)S(1)}, u32[]{:S(2)}, u32[]{:S(2)}) %collective-permute-start.19) | collective-permute-done | bytes 196640 | tf_op jit(solution)/shard_map/ppermute | solution.py:314
  68.6 1.0 collective-permute-start.13
  69.6 1.0 collective-permute-start.15
  70.7 3.6 %collective-permute-done.13.refs_0_ = bf16[64,1536]{1,0:T(8,128)(2,1)S(1)} collective-permute-done((bf16[64,1536]{1,0:T(8,128)(2,1)S(1)}, bf16[64,1536]{1,0:T(8,128)(2,1)S(1)}, u32[]{:S(2)}, u32[]{:S(2)}) %collective-permute-start.13) | collective-permute-done | bytes 196640 | tf_op jit(solution)/shard_map/ppermute | solution.py:314
  74.3 1.1 collective-permute-start.16
  77.2 2.8 %collective-permute-done.16.refs_2_ = bf16[64,1536]{1,0:T(8,128)(2,1)S(1)} collective-permute-done((bf16[64,1536]{1,0:T(8,128)(2,1)S(1)}, bf16[64,1536]{1,0:T(8,128)(2,1)S(1)}, u32[]{:S(2)}, u32[]{:S(2)}) %collective-permute-start.16) | collective-permute-done | bytes 196640 | tf_op jit(solution)/shard_map/ppermute | solution.py:314
  79.9 1.1 collective-permute-start.20
  82.0 1.7 %copy-done.1 = bf16[1,1536,768]{2,1,0:T(8,128)(2,1)S(1)} copy-done((bf16[1,1536,768]{2,1,0:T(8,128)(2,1)S(1)}, bf16[1,1536,768]{2,1,0:T(8,128)(2,1)}, u32[]{:S(2)}) %copy-start.1) | copy-done | bytes 2359320
  83.6 1.7 %copy-done.3 = bf16[1,768,1536]{2,1,0:T(8,128)(2,1)S(1)} copy-done((bf16[1,768,1536]{2,1,0:T(8,128)(2,1)S(1)}, bf16[1,768,1536]{2,1,0:T(8,128)(2,1)}, u32[]{:S(2)}) %copy-start.3) | copy-done | bytes 2359320
  85.3 9.3 %experts.5 = (bf16[64,1536]{1,0:T(8,128)(2,1)S(1)}, bf16[64,1536]{1,0:T(8,128)(2,1)S(1)}, bf16[64,1536]{1,0:T(8,128)(2,1)S(1)}, bf16[64,1536]{1,0:T(8,128)(2,1)S(1)}) custom-call(bf16[64,1536]{1,0:T(8,128)(2,1)S(1)} %collective-permute-done.13.refs_0_, bf16[64,1536]{1,0:T(8,128)(2,1)S(1)} %collective-permute-done.15.refs_1_, ...), custom_call_target="tpu_custom_call" | custom-call | flops 3623878656 | bytes 14155776 | tf_op jit(solution)/shard_map/experts/pallas_call | solution.py:257
  94.6 1.2 collective-permute-start.18
  96.7 1.1 collective-permute-start.29
  97.8 10.9 %experts.4 = (bf16[64,1536]{1,0:T(8,128)(2,1)S(1)}, bf16[64,1536]{1,0:T(8,128)(2,1)S(1)}, bf16[64,1536]{1,0:T(8,128)(2,1)S(1)}, bf16[64,1536]{1,0:T(8,128)(2,1)S...) custom-call(bf16[64,1536]{1,0:T(8,128)(2,1)} %get-tuple-element.29.refs_0_, ...), custom_call_target="tpu_custom_call" | custom-call | flops 5435817984 | bytes 14155776 | tf_op jit(solution)/shard_map/experts/pallas_call | solution.py:257
  108.7 9.2 %experts.7 = (bf16[64,1536]{1,0:T(8,128)(2,1)S(1)}, bf16[64,1536]{1,0:T(8,128)(2,1)S(1)}, bf16[64,1536]{1,0:T(8,128)(2,1)S(1)}, bf16[64,1536]{1,0:T(8,128)(2,1)S(1)}) custom-call(bf16[64,1536]{1,0:T(8,128)(2,1)S(1)} %collective-permute-done.12.refs_0_, bf16[64,1536]{1,0:T(8,128)(2,1)S(1)} %collective-permute-done.19.refs_1_, ...), custom_call_target="tpu_custom_call" | custom-call | flops 3623878656 | bytes 14155776 | tf_op jit(solution)/shard_map/experts/pallas_call | solution.py:257
  117.9 1.2 collective-permute-start.32
  119.0 7.4 %experts.6 = (bf16[64,1536]{1,0:T(8,128)(2,1)S(1)}, bf16[64,1536]{1,0:T(8,128)(2,1)S(1)}) custom-call(bf16[64,1536]{1,0:T(8,128)(2,1)S(1)} %collective-permute-done.20.refs_0_, bf16[64,1536]{1,0:T(8,128)(2,1)S(1)} %collective-permute-done.22.refs_1_, f32[8,128]{1,0:T(8,128)S(1)} %select_reduce_fusion.refs_6_.refs_4_.refs_2_, bf16[1536,768]{1,0:T(8,128)(2,1)S(1)} %bitcast.14, ...), custom_call_target="tpu_custom_call" | custom-call | flops 1811939328 | bytes 14155776 | tf_op jit(solution)/shard_map/experts/pallas_call | solution.py:257
  126.6 1.1 collective-permute-start.23
  128.8 1.1 collective-permute-start.30
  131.0 3.2 %collective-permute-done.23 = bf16[64,1536]{1,0:T(8,128)(2,1)S(1)} collective-permute-done((bf16[64,1536]{1,0:T(8,128)(2,1)S(1)}, bf16[64,1536]{1,0:T(8,128)(2,1)S(1)}, u32[]{:S(2)}, u32[]{:S(2)}) %collective-permute-start.23) | collective-permute-done | bytes 196640 | tf_op jit(solution)/shard_map/ppermute | solution.py:361
  134.3 1.2 collective-permute-start.24
  136.5 1.1 collective-permute-start.31
  137.7 1.0 collective-permute-start.34
  138.7 1.3 collective-permute-done.24
  140.0 1.2 collective-permute-start.25
  141.2 2.2 %collective-permute-done.34 = bf16[64,1536]{1,0:T(8,128)(2,1)S(1)} collective-permute-done((bf16[64,1536]{1,0:T(8,128)(2,1)S(1)}, bf16[64,1536]{1,0:T(8,128)(2,1)S(1)}, u32[]{:S(2)}, u32[]{:S(2)}) %collective-permute-start.34) | collective-permute-done | bytes 196640 | tf_op jit(solution)/shard_map/ppermute | solution.py:361
  143.5 1.0 collective-permute-start.35
  144.5 1.3 collective-permute-done.25
  145.9 3.4 %collective-permute-done.35 = bf16[64,1536]{1,0:T(8,128)(2,1)S(1)} collective-permute-done((bf16[64,1536]{1,0:T(8,128)(2,1)S(1)}, bf16[64,1536]{1,0:T(8,128)(2,1)S(1)}, u32[]{:S(2)}, u32[]{:S(2)}) %collective-permute-start.35) | collective-permute-done | bytes 196640 | tf_op jit(solution)/shard_map/ppermute | solution.py:361
  (98 shorter events, 21.5 us)
Async XLA Ops:
  0.0 82.0 %collective-permute-start.10 = (bf16[1536,768]{1,0:T(8,128)(2,1)}, bf16[1536,768]{1,0:T(8,128)(2,1)}, u32[]{:S(2)}, u32[]{:S(2)}) collective-permute-start(bf16[1536,768]{1,0:T(8,128)(2,1)} %bitcast.15), channel_id=1, source_target_pairs={{0,1},{1,0},{2,3},{3,2},{4,5},{5,4},{6,7},{7,6},{8,9},{9,8},{10,11... | collective-permute-start | bytes 7077896 | tf_op jit(solution)/shard_map/ppermute | solution.py:28
  0.5 81.5 %collective-permute-start.11 = (bf16[768,1536]{1,0:T(8,128)(2,1)}, bf16[768,1536]{1,0:T(8,128)(2,1)}, u32[]{:S(2)}, u32[]{:S(2)}) collective-permute-start(bf16[768,1536]{1,0:T(8,128)(2,1)} %bitcast.20), channel_id=1, source_target_pairs={{0,1},{1,0},{2,3},{3,2},{4,5},{5,4},{6,7},{7,6},{8,9},{9,8},{10,11... | collective-permute-start | bytes 7077896 | tf_op jit(solution)/shard_map/ppermute | solution.py:28
  0.5 81.5 %collective-permute-start.9 = (bf16[1536,768]{1,0:T(8,128)(2,1)}, bf16[1536,768]{1,0:T(8,128)(2,1)}, u32[]{:S(2)}, u32[]{:S(2)}) collective-permute-start(bf16[1536,768]{1,0:T(8,128)(2,1)} %bitcast.10), channel_id=1, source_target_pairs={{0,1},{1,0},{2,3},{3,2},{4,5},{5,4},{6,7},{7,6},{8,9},{9,8},{10,11... | collective-permute-start | bytes 7077896 | tf_op jit(solution)/shard_map/ppermute | solution.py:28
  2.5 14.3 %collective-permute-start = (bf16[128,256]{1,0:T(8,128)(2,1)S(1)}, bf16[128,256]{1,0:T(8,128)(2,1)S(1)}, u32[]{:S(2)}, u32[]{:S(2)}) collective-permute-start(bf16[128,256]{1,0:T(8,128)(2,1)S(1)} %pad_maximum_fusion), channel_id=1, source_target_pairs={{0,2},{2,4},{4,6},{6,8},{8,10},{10,12},{12,14},{1,3},{3,5},{5,7},{... | collective-permute-start | bytes 196616 | tf_op jit(solution)/shard_map/ppermute | solution.py:23
  6.9 1.9 %copy-start.4 = (bf16[1024,1536]{1,0:T(8,128)(2,1)S(1)}, bf16[1024,1536]{1,0:T(8,128)(2,1)}, u32[]{:S(2)}) copy-start(bf16[1024,1536]{1,0:T(8,128)(2,1)} %ow_ref.3) | copy-start | bytes 9437188
  12.2 4.7 %copy-start.5 = (bf16[1024,1536]{1,0:T(8,128)(2,1)S(1)}, bf16[1024,1536]{1,0:T(8,128)(2,1)}, u32[]{:S(2)}) copy-start(bf16[1024,1536]{1,0:T(8,128)(2,1)} %ow_ref.3) | copy-start | bytes 9437188
  12.2 4.7 %copy-start.7 = (bf16[256,1024]{1,0:T(8,128)(2,1)S(1)}, bf16[256,1024]{1,0:T(8,128)(2,1)}, u32[]{:S(2)}) copy-start(bf16[256,1024]{1,0:T(8,128)(2,1)} %q_ref.3) | copy-start | bytes 1572868
  16.8 5.7 %copy-start.15 = (s32[128,4]{0,1:T(4,128)S(1)}, s32[128,4]{0,1:T(4,128)}, u32[]{:S(2)}) copy-start(s32[128,4]{0,1:T(4,128)} %param.21) | copy-start | bytes 6148
  16.8 6.4 %copy-start.16 = (f32[128,4]{0,1:T(4,128)S(1)}, f32[128,4]{0,1:T(4,128)}, u32[]{:S(2)}) copy-start(f32[128,4]{0,1:T(4,128)} %param.22) | copy-start | bytes 6148
  16.9 21.0 %copy-start.10 = (bf16[128,1536]{1,0:T(8,128)(2,1)S(1)}, bf16[128,1536]{1,0:T(8,128)(2,1)}, u32[]{:S(2)}) copy-start(bf16[128,1536]{1,0:T(8,128)(2,1)} %stream_ref.1) | copy-start | bytes 1179652
  16.9 32.5 %copy-start.14 = (s32[8]{0:T(128)S(1)}, s32[8]{0:T(128)}, u32[]{:S(2)}) copy-start(s32[8]{0:T(128)} %constant.35.clone) | copy-start | bytes 100
  22.3 59.7 %copy-start = (bf16[1,1536,768]{2,1,0:T(8,128)(2,1)S(1)}, bf16[1,1536,768]{2,1,0:T(8,128)(2,1)}, u32[]{:S(2)}) copy-start(bf16[1,1536,768]{2,1,0:T(8,128)(2,1)} %param.23) | copy-start | bytes 7077892
  22.3 15.6 %collective-permute-start.1 = (bf16[128,1536]{1,0:T(8,128)(2,1)}, bf16[128,1536]{1,0:T(8,128)(2,1)}, u32[]{:S(2)}, u32[]{:S(2)}) collective-permute-start(bf16[128,1536]{1,0:T(8,128)(2,1)} %get-tuple-element.27), channel_id=1, source_target_pairs={{0,1},{1,0},{2,3},{3,2},{4,5},{5,4},{6,7},{7,6},{8,9},{9,8},{10,11... | collective-permute-start | bytes 1179656 | tf_op jit(solution)/shard_map/ppermute | solution.py:28
  25.7 3.8 %collective-permute-start.6 = (f32[8,128]{1,0:T(8,128)}, f32[8,128]{1,0:T(8,128)S(1)}, u32[]{:S(2)}, u32[]{:S(2)}) collective-permute-start(f32[8,128]{1,0:T(8,128)} %spread.1), channel_id=1, source_target_pairs={{0,2},{2,0},{4,6},{6,4},{8,10},{10,8},{12,14},{14,12},{1,3},{3,1},... | collective-permute-start | bytes 12296 | tf_op jit(solution)/shard_map/ppermute | solution.py:28
  30.2 3.7 %collective-permute-start.7 = (f32[16,128]{1,0:T(8,128)S(1)}, f32[16,128]{1,0:T(8,128)S(1)}, u32[]{:S(2)}, u32[]{:S(2)}) collective-permute-start(f32[16,128]{1,0:T(8,128)S(1)} %pad_maximum_fusion.2), channel_id=1, source_target_pairs={{0,4},{2,6},{4,0},{6,2},{8,12},{10,14},{12,8},{14,10},{1,5},{3,7},... | collective-permute-start | bytes 24584 | tf_op jit(solution)/shard_map/ppermute | solution.py:28
  34.6 7.7 %collective-permute-start.8 = (f32[32,128]{1,0:T(8,128)S(1)}, f32[32,128]{1,0:T(8,128)}, u32[]{:S(2)}, u32[]{:S(2)}) collective-permute-start(f32[32,128]{1,0:T(8,128)S(1)} %pad_maximum_fusion.1), channel_id=1, source_target_pairs={{0,8},{2,10},{4,12},{6,14},{8,0},{10,2},{12,4},{14,6},{1,9},{3,11}... | collective-permute-start | bytes 49160 | tf_op jit(solution)/shard_map/ppermute | solution.py:28
  40.7 6.5 %collective-permute-start.2 = (bf16[64,1536]{1,0:T(8,128)(2,1)}, bf16[64,1536]{1,0:T(8,128)(2,1)S(1)}, u32[]{:S(2)}, u32[]{:S(2)}) collective-permute-start(bf16[64,1536]{1,0:T(8,128)(2,1)} %get-tuple-element.29.refs_0_), channel_id=1, source_target_pairs={{0,4},{4,8},{8,12},{12,14},{14,10},{10,6},{6,2},{2,0},{1,5},{5,9},... | collective-permute-start | bytes 589832 | tf_op jit(solution)/shard_map/ppermute | solution.py:314
  42.3 6.5 %collective-permute-start.5 = (bf16[64,1536]{1,0:T(8,128)(2,1)}, bf16[64,1536]{1,0:T(8,128)(2,1)S(1)}, u32[]{:S(2)}, u32[]{:S(2)}) collective-permute-start(bf16[64,1536]{1,0:T(8,128)(2,1)} %get-tuple-element.30.refs_1_), channel_id=1, source_target_pairs={{4,0},{8,4},{12,8},{14,12},{10,14},{6,10},{2,6},{0,2},{5,1},{9,5},... | collective-permute-start | bytes 589832 | tf_op jit(solution)/shard_map/ppermute | solution.py:314
  47.1 7.6 %collective-permute-start.3 = (bf16[64,1536]{1,0:T(8,128)(2,1)}, bf16[64,1536]{1,0:T(8,128)(2,1)S(1)}, u32[]{:S(2)}, u32[]{:S(2)}) collective-permute-start(bf16[64,1536]{1,0:T(8,128)(2,1)} %get-tuple-element.30.refs_1_), channel_id=1, source_target_pairs={{0,4},{4,8},{8,12},{12,14},{14,10},{10,6},{6,2},{2,0},{1,5},{5,9},... | collective-permute-start | bytes 589832 | tf_op jit(solution)/shard_map/ppermute | solution.py:314
  48.7 7.8 %collective-permute-start.4 = (bf16[64,1536]{1,0:T(8,128)(2,1)}, bf16[64,1536]{1,0:T(8,128)(2,1)S(1)}, u32[]{:S(2)}, u32[]{:S(2)}) collective-permute-start(bf16[64,1536]{1,0:T(8,128)(2,1)} %get-tuple-element.29.refs_0_), channel_id=1, source_target_pairs={{4,0},{8,4},{12,8},{14,12},{10,14},{6,10},{2,6},{0,2},{5,1},{9,5},... | collective-permute-start | bytes 589832 | tf_op jit(solution)/shard_map/ppermute | solution.py:314
  54.7 7.3 %collective-permute-start.12 = (bf16[64,1536]{1,0:T(8,128)(2,1)S(1)}, bf16[64,1536]{1,0:T(8,128)(2,1)S(1)}, u32[]{:S(2)}, u32[]{:S(2)}) collective-permute-start(bf16[64,1536]{1,0:T(8,128)(2,1)S(1)} %collective-permute-done.2.refs_2_), channel_id=1, source_target_pairs={{0,4},{4,8},{8,12},{12,14},{14,10},{10,6},{6,2},{2,0},{1,5},{5,9},... | collective-permute-start | bytes 589832 | tf_op jit(solution)/shard_map/ppermute | solution.py:314
  56.6 6.9 %collective-permute-start.14 = (bf16[64,1536]{1,0:T(8,128)(2,1)S(1)}, bf16[64,1536]{1,0:T(8,128)(2,1)S(1)}, u32[]{:S(2)}, u32[]{:S(2)}) collective-permute-start(bf16[64,1536]{1,0:T(8,128)(2,1)S(1)} %collective-permute-done.5.refs_5_), channel_id=1, source_target_pairs={{4,0},{8,4},{12,8},{14,12},{10,14},{6,10},{2,6},{0,2},{5,1},{9,5},... | collective-permute-start | bytes 589832 | tf_op jit(solution)/shard_map/ppermute | solution.py:314
  62.1 6.5 %collective-permute-start.19 = (bf16[64,1536]{1,0:T(8,128)(2,1)S(1)}, bf16[64,1536]{1,0:T(8,128)(2,1)S(1)}, u32[]{:S(2)}, u32[]{:S(2)}) collective-permute-start(bf16[64,1536]{1,0:T(8,128)(2,1)S(1)} %collective-permute-done.3.refs_3_), channel_id=1, source_target_pairs={{0,4},{4,8},{8,12},{12,14},{14,10},{10,6},{6,2},{2,0},{1,5},{5,9},... | collective-permute-start | bytes 589832 | tf_op jit(solution)/shard_map/ppermute | solution.py:314
  63.5 6.1 %collective-permute-start.21 = (bf16[64,1536]{1,0:T(8,128)(2,1)S(1)}, bf16[64,1536]{1,0:T(8,128)(2,1)S(1)}, u32[]{:S(2)}, u32[]{:S(2)}) collective-permute-start(bf16[64,1536]{1,0:T(8,128)(2,1)S(1)} %collective-permute-done.4.refs_4_), channel_id=1, source_target_pairs={{4,0},{8,4},{12,8},{14,12},{10,14},{6,10},{2,6},{0,2},{5,1},{9,5},... | collective-permute-start | bytes 589832 | tf_op jit(solution)/shard_map/ppermute | solution.py:314
  68.6 5.7 %collective-permute-start.13 = (bf16[64,1536]{1,0:T(8,128)(2,1)S(1)}, bf16[64,1536]{1,0:T(8,128)(2,1)S(1)}, u32[]{:S(2)}, u32[]{:S(2)}) collective-permute-start(bf16[64,1536]{1,0:T(8,128)(2,1)S(1)} %collective-permute-done.12.refs_0_), channel_id=1, source_target_pairs={{0,4},{4,8},{8,12},{12,14},{14,10},{10,6},{6,2},{2,0},{1,5},{5,9},... | collective-permute-start | bytes 589832 | tf_op jit(solution)/shard_map/ppermute | solution.py:314
  69.6 5.8 %collective-permute-start.15 = (bf16[64,1536]{1,0:T(8,128)(2,1)S(1)}, bf16[64,1536]{1,0:T(8,128)(2,1)S(1)}, u32[]{:S(2)}, u32[]{:S(2)}) collective-permute-start(bf16[64,1536]{1,0:T(8,128)(2,1)S(1)} %collective-permute-done.14.refs_3_), channel_id=1, source_target_pairs={{4,0},{8,4},{12,8},{14,12},{10,14},{6,10},{2,6},{0,2},{5,1},{9,5},... | collective-permute-start | bytes 589832 | tf_op jit(solution)/shard_map/ppermute | solution.py:314
  74.3 5.7 %collective-permute-start.16 = (bf16[64,1536]{1,0:T(8,128)(2,1)S(1)}, bf16[64,1536]{1,0:T(8,128)(2,1)S(1)}, u32[]{:S(2)}, u32[]{:S(2)}) collective-permute-start(bf16[64,1536]{1,0:T(8,128)(2,1)S(1)} %collective-permute-done.13.refs_0_), channel_id=1, source_target_pairs={{0,4},{4,8},{8,12},{12,14},{14,10},{10,6},{6,2},{2,0},{1,5},{5,9},... | collective-permute-start | bytes 589832 | tf_op jit(solution)/shard_map/ppermute | solution.py:314
  75.4 5.7 %collective-permute-start.17 = (bf16[64,1536]{1,0:T(8,128)(2,1)S(1)}, bf16[64,1536]{1,0:T(8,128)(2,1)S(1)}, u32[]{:S(2)}, u32[]{:S(2)}) collective-permute-start(bf16[64,1536]{1,0:T(8,128)(2,1)S(1)} %collective-permute-done.15.refs_1_), channel_id=1, source_target_pairs={{4,0},{8,4},{12,8},{14,12},{10,14},{6,10},{2,6},{0,2},{5,1},{9,5},... | collective-permute-start | bytes 589832 | tf_op jit(solution)/shard_map/ppermute | solution.py:314
  79.9 38.0 %collective-permute-start.20 = (bf16[64,1536]{1,0:T(8,128)(2,1)S(1)}, bf16[64,1536]{1,0:T(8,128)(2,1)S(1)}, u32[]{:S(2)}, u32[]{:S(2)}) collective-permute-start(bf16[64,1536]{1,0:T(8,128)(2,1)S(1)} %collective-permute-done.19.refs_1_), channel_id=1, source_target_pairs={{0,4},{4,8},{8,12},{12,14},{14,10},{10,6},{6,2},{2,0},{1,5},{5,9},... | collective-permute-start | bytes 589832 | tf_op jit(solution)/shard_map/ppermute | solution.py:314
  81.0 38.0 %collective-permute-start.22 = (bf16[64,1536]{1,0:T(8,128)(2,1)S(1)}, bf16[64,1536]{1,0:T(8,128)(2,1)S(1)}, u32[]{:S(2)}, u32[]{:S(2)}) collective-permute-start(bf16[64,1536]{1,0:T(8,128)(2,1)S(1)} %collective-permute-done.21.refs_2_), channel_id=1, source_target_pairs={{4,0},{8,4},{12,8},{14,12},{10,14},{6,10},{2,6},{0,2},{5,1},{9,5},... | collective-permute-start | bytes 589832 | tf_op jit(solution)/shard_map/ppermute | solution.py:314
  82.0 1.7 %copy-start.1 = (bf16[1,1536,768]{2,1,0:T(8,128)(2,1)S(1)}, bf16[1,1536,768]{2,1,0:T(8,128)(2,1)}, u32[]{:S(2)}) copy-start(bf16[1,1536,768]{2,1,0:T(8,128)(2,1)} %param.24) | copy-start | bytes 7077892
  83.6 1.7 %copy-start.3 = (bf16[1,768,1536]{2,1,0:T(8,128)(2,1)S(1)}, bf16[1,768,1536]{2,1,0:T(8,128)(2,1)}, u32[]{:S(2)}) copy-start(bf16[1,768,1536]{2,1,0:T(8,128)(2,1)} %param.25) | copy-start | bytes 7077892
  85.3 12.5 %copy-start.2 = (bf16[1,1536,768]{2,1,0:T(8,128)(2,1)S(1)}, bf16[1,1536,768]{2,1,0:T(8,128)(2,1)}, u32[]{:S(2)}) copy-start(bf16[1,1536,768]{2,1,0:T(8,128)(2,1)} %param.24) | copy-start | bytes 7077892
  94.6 31.9 %collective-permute-start.18 = (bf16[64,1536]{1,0:T(8,128)(2,1)S(1)}, bf16[64,1536]{1,0:T(8,128)(2,1)S(1)}, u32[]{:S(2)}, u32[]{:S(2)}) collective-permute-start(bf16[64,1536]{1,0:T(8,128)(2,1)S(1)} %get-tuple-element.32), channel_id=1, source_target_pairs={{0,4},{4,8},{8,12},{12,14},{14,10},{10,6},{6,2},{2,0},{1,5},{5,9},... | collective-permute-start | bytes 589832 | tf_op jit(solution)/shard_map/ppermute | solution.py:361
  95.8 32.0 %collective-permute-start.26 = (bf16[64,1536]{1,0:T(8,128)(2,1)S(1)}, bf16[64,1536]{1,0:T(8,128)(2,1)S(1)}, u32[]{:S(2)}, u32[]{:S(2)}) collective-permute-start(bf16[64,1536]{1,0:T(8,128)(2,1)S(1)} %get-tuple-element.36), channel_id=1, source_target_pairs={{4,0},{8,4},{12,8},{14,12},{10,14},{6,10},{2,6},{0,2},{5,1},{9,5},... | collective-permute-start | bytes 589832 | tf_op jit(solution)/shard_map/ppermute | solution.py:361
  96.7 32.1 %collective-permute-start.29 = (bf16[64,1536]{1,0:T(8,128)(2,1)S(1)}, bf16[64,1536]{1,0:T(8,128)(2,1)S(1)}, u32[]{:S(2)}, u32[]{:S(2)}) collective-permute-start(bf16[64,1536]{1,0:T(8,128)(2,1)S(1)} %get-tuple-element.40), channel_id=1, source_target_pairs={{0,4},{4,8},{8,12},{12,14},{14,10},{10,6},{6,2},{2,0},{1,5},{5,9},... | collective-permute-start | bytes 589832 | tf_op jit(solution)/shard_map/ppermute | solution.py:361
  117.9 12.1 %collective-permute-start.32 = (bf16[64,1536]{1,0:T(8,128)(2,1)S(1)}, bf16[64,1536]{1,0:T(8,128)(2,1)S(1)}, u32[]{:S(2)}, u32[]{:S(2)}) collective-permute-start(bf16[64,1536]{1,0:T(8,128)(2,1)S(1)} %get-tuple-element.43), channel_id=1, source_target_pairs={{4,0},{8,4},{12,8},{14,12},{10,14},{6,10},{2,6},{0,2},{5,1},{9,5},... | collective-permute-start | bytes 589832 | tf_op jit(solution)/shard_map/ppermute | solution.py:361
  126.6 7.7 %collective-permute-start.23 = (bf16[64,1536]{1,0:T(8,128)(2,1)S(1)}, bf16[64,1536]{1,0:T(8,128)(2,1)S(1)}, u32[]{:S(2)}, u32[]{:S(2)}) collective-permute-start(bf16[64,1536]{1,0:T(8,128)(2,1)S(1)} %add_convert_fusion.9), channel_id=1, source_target_pairs={{0,4},{4,8},{8,12},{12,14},{14,10},{10,6},{6,2},{2,0},{1,5},{5,9},... | collective-permute-start | bytes 589832 | tf_op jit(solution)/shard_map/ppermute | solution.py:361
  127.8 7.7 %collective-permute-start.27 = (bf16[64,1536]{1,0:T(8,128)(2,1)S(1)}, bf16[64,1536]{1,0:T(8,128)(2,1)S(1)}, u32[]{:S(2)}, u32[]{:S(2)}) collective-permute-start(bf16[64,1536]{1,0:T(8,128)(2,1)S(1)} %add_convert_fusion.6), channel_id=1, source_target_pairs={{4,0},{8,4},{12,8},{14,12},{10,14},{6,10},{2,6},{0,2},{5,1},{9,5},... | collective-permute-start | bytes 589832 | tf_op jit(solution)/shard_map/ppermute | solution.py:361
  128.8 7.7 %collective-permute-start.30 = (bf16[64,1536]{1,0:T(8,128)(2,1)S(1)}, bf16[64,1536]{1,0:T(8,128)(2,1)S(1)}, u32[]{:S(2)}, u32[]{:S(2)}) collective-permute-start(bf16[64,1536]{1,0:T(8,128)(2,1)S(1)} %add_convert_fusion.4), channel_id=1, source_target_pairs={{0,4},{4,8},{8,12},{12,14},{14,10},{10,6},{6,2},{2,0},{1,5},{5,9},... | collective-permute-start | bytes 589832 | tf_op jit(solution)/shard_map/ppermute | solution.py:361
  130.0 7.7 %collective-permute-start.33 = (bf16[64,1536]{1,0:T(8,128)(2,1)S(1)}, bf16[64,1536]{1,0:T(8,128)(2,1)S(1)}, u32[]{:S(2)}, u32[]{:S(2)}) collective-permute-start(bf16[64,1536]{1,0:T(8,128)(2,1)S(1)} %add_convert_fusion.2), channel_id=1, source_target_pairs={{4,0},{8,4},{12,8},{14,12},{10,14},{6,10},{2,6},{0,2},{5,1},{9,5},... | collective-permute-start | bytes 589832 | tf_op jit(solution)/shard_map/ppermute | solution.py:361
  134.3 5.7 %collective-permute-start.24 = (bf16[64,1536]{1,0:T(8,128)(2,1)S(1)}, bf16[64,1536]{1,0:T(8,128)(2,1)S(1)}, u32[]{:S(2)}, u32[]{:S(2)}) collective-permute-start(bf16[64,1536]{1,0:T(8,128)(2,1)S(1)} %add_convert_fusion.8), channel_id=1, source_target_pairs={{0,4},{4,8},{8,12},{12,14},{14,10},{10,6},{6,2},{2,0},{1,5},{5,9},... | collective-permute-start | bytes 589832 | tf_op jit(solution)/shard_map/ppermute | solution.py:361
  135.4 13.9 %copy-start.12 = (bf16[128,1536]{1,0:T(8,128)(2,1)S(1)}, bf16[128,1536]{1,0:T(8,128)(2,1)}, u32[]{:S(2)}) copy-start(bf16[128,1536]{1,0:T(8,128)(2,1)} %copy-done.11) | copy-start | bytes 1179652
  135.5 9.0 %collective-permute-start.28 = (bf16[64,1536]{1,0:T(8,128)(2,1)S(1)}, bf16[64,1536]{1,0:T(8,128)(2,1)S(1)}, u32[]{:S(2)}, u32[]{:S(2)}) collective-permute-start(bf16[64,1536]{1,0:T(8,128)(2,1)S(1)} %add_convert_fusion.5), channel_id=1, source_target_pairs={{4,0},{8,4},{12,8},{14,12},{10,14},{6,10},{2,6},{0,2},{5,1},{9,5},... | collective-permute-start | bytes 589832 | tf_op jit(solution)/shard_map/ppermute | solution.py:361
  136.5 9.3 %collective-permute-start.31 = (bf16[64,1536]{1,0:T(8,128)(2,1)S(1)}, bf16[64,1536]{1,0:T(8,128)(2,1)S(1)}, u32[]{:S(2)}, u32[]{:S(2)}) collective-permute-start(bf16[64,1536]{1,0:T(8,128)(2,1)S(1)} %add_convert_fusion.3), channel_id=1, source_target_pairs={{0,4},{4,8},{8,12},{12,14},{14,10},{10,6},{6,2},{2,0},{1,5},{5,9},... | collective-permute-start | bytes 589832 | tf_op jit(solution)/shard_map/ppermute | solution.py:361
  137.7 5.7 %collective-permute-start.34 = (bf16[64,1536]{1,0:T(8,128)(2,1)S(1)}, bf16[64,1536]{1,0:T(8,128)(2,1)S(1)}, u32[]{:S(2)}, u32[]{:S(2)}) collective-permute-start(bf16[64,1536]{1,0:T(8,128)(2,1)S(1)} %add_convert_fusion.1), channel_id=1, source_target_pairs={{4,0},{8,4},{12,8},{14,12},{10,14},{6,10},{2,6},{0,2},{5,1},{9,5},... | collective-permute-start | bytes 589832 | tf_op jit(solution)/shard_map/ppermute | solution.py:361
  140.0 5.7 %collective-permute-start.25 = (bf16[64,1536]{1,0:T(8,128)(2,1)S(1)}, bf16[64,1536]{1,0:T(8,128)(2,1)S(1)}, u32[]{:S(2)}, u32[]{:S(2)}) collective-permute-start(bf16[64,1536]{1,0:T(8,128)(2,1)S(1)} %add_convert_fusion.7), channel_id=1, source_target_pairs={{0,4},{4,8},{8,12},{12,14},{14,10},{10,6},{6,2},{2,0},{1,5},{5,9},... | collective-permute-start | bytes 589832 | tf_op jit(solution)/shard_map/ppermute | solution.py:361
  143.5 5.7 %collective-permute-start.35 = (bf16[64,1536]{1,0:T(8,128)(2,1)S(1)}, bf16[64,1536]{1,0:T(8,128)(2,1)S(1)}, u32[]{:S(2)}, u32[]{:S(2)}) collective-permute-start(bf16[64,1536]{1,0:T(8,128)(2,1)S(1)} %add_convert_fusion), channel_id=1, source_target_pairs={{4,0},{8,4},{12,8},{14,12},{10,14},{6,10},{2,6},{0,2},{5,1},{9,5},... | collective-permute-start | bytes 589832 | tf_op jit(solution)/shard_map/ppermute | solution.py:361
  (5 other events, 4.1 us)

commit v2 on v1

v2 whole, which is shorter than its diff:
```python
import functools
import math

import jax
import jax.numpy as jnp
from jax import lax
from jax.experimental import pallas as pl
from jax.experimental.pallas import tpu as pltpu
from jax.sharding import PartitionSpec as P

HEAD_DIM = 64
WINDOW = 128
TOP = 4
EXP_DEV = 1
LANES = 128
SNAKES = {8: (0, 2, 4, 6, 7, 5, 3, 1)}
MIB = 1 << 20
EXPERT_VMEM = 16 * MIB


def shifted(value, axis, by):
    peers = lax.axis_size(axis)
    pairs = [(i, i + by) for i in range(peers) if 0 <= i + by < peers]
    return lax.ppermute(value, axis, pairs)


def swapped(value, axis, bit=1):
    peers = lax.axis_size(axis)
    return lax.ppermute(value, axis, [(i, i ^ bit) for i in range(peers)])


def mm(a, b):
    return jnp.dot(a, b, preferred_element_type=jnp.float32)


def attend_kernel(
    group_pairs, first_ref, sink_ref, q_ref, kp_ref, kc_ref, vp_ref, vc_ref, ow_ref, *rest
):
    mix = len(rest) > 2
    if mix:
        rank_ref, other_ref, send_ref, own_ref, total = rest
    else:
        out_ref, total = rest
    step = pl.program_id(0)
    rows = q_ref.shape[0]
    keys = kp_ref.shape[0] + kc_ref.shape[0]
    pairs_step = q_ref.shape[1] // LANES
    group = (step * pairs_step) // group_pairs

    lane_k = lax.broadcasted_iota(jnp.int32, (keys, LANES), 1)
    low = lane_k < HEAD_DIM
    k = jnp.concatenate([kp_ref[...], kc_ref[...]], axis=0).astype(jnp.float32)
    v = jnp.concatenate([vp_ref[...], vc_ref[...]], axis=0).astype(jnp.float32)
    k_low = jnp.where(low, jnp.where(group == 0, k, pltpu.roll(k, HEAD_DIM, 1)), 0.0)
    v_low = jnp.where(low, jnp.where(group == 0, v, pltpu.roll(v, HEAD_DIM, 1)), 0.0)
    k_high, v_high = pltpu.roll(k_low, HEAD_DIM, 1), pltpu.roll(v_low, HEAD_DIM, 1)
    kk = jnp.concatenate([k_low, k_high], axis=0).astype(jnp.bfloat16)
    one_low = jnp.where(low, 1.0, 0.0)
    vv = jnp.concatenate(
        [
            jnp.concatenate([v_low, one_low], axis=1),
            jnp.concatenate([v_high, 1.0 - one_low], axis=1),
        ],
        axis=0,
    ).astype(jnp.bfloat16)

    row = lax.broadcasted_iota(jnp.int32, (rows, keys), 0)
    column = lax.broadcasted_iota(jnp.int32, (rows, keys), 1)
    least = jnp.where(first_ref[0] == 1, WINDOW, 0)
    allowed = (column <= row + WINDOW) & (column > row) & (column >= least)
    low_out = lax.broadcasted_iota(jnp.int32, (rows, LANES), 1) < HEAD_DIM
    scale = 1.0 / math.sqrt(HEAD_DIM)

    done = []
    for pair in range(pairs_step):
        q = q_ref[:, pair * LANES : (pair + 1) * LANES]
        scores = lax.dot_general(
            q, kk, (((1,), (1,)), ((), ())), preferred_element_type=jnp.float32
        )
        weights, sinks = [], []
        for side in range(2):
            part = jnp.where(allowed, scores[:, side * keys : (side + 1) * keys] * scale, -jnp.inf)
            sink = sink_ref[(step * pairs_step + pair) * 2 + side]
            highest = jnp.maximum(jnp.max(part, axis=1, keepdims=True), sink)
            weights.append(jnp.exp(part - highest).astype(jnp.bfloat16))
            sinks.append(jnp.exp(sink - highest))
        both = mm(jnp.concatenate(weights, axis=1), vv)
        below = both[:, LANES:] + jnp.where(low_out, sinks[0], sinks[1])
        done.append((both[:, :LANES] / below).astype(jnp.bfloat16))
    part = mm(jnp.concatenate(done, axis=1), ow_ref[...])

    @pl.when(step == 0)
    def _():
        total[...] = part

    @pl.when(step > 0)
    def _():
        total[...] += part

    @pl.when(step == pl.num_programs(0) - 1)
    def _():
        if mix:
            mine = total[...]
            other = other_ref[...]
            own_first = rank_ref[0] == 0
            own_ref[...] = jnp.where(own_first, mine, other)
            send_ref[...] = jnp.where(own_first, other, mine).astype(jnp.bfloat16)
        else:
            out_ref[...] = total[...]


def attend(half, first, sinks, queries, keys, values, out_weight, rank=None, other=None):
    (k_prev, kp_index), (k_cur, kc_index) = keys
    (v_prev, vp_index), (v_cur, vc_index) = values
    rows, width, model = WINDOW, queries.shape[1], out_weight.shape[1]
    block = min(width, 256)
    group_pairs = width // LANES // (k_cur.shape[1] // HEAD_DIM)
    smem = pl.BlockSpec(memory_space=pltpu.SMEM)

    def fixed(index):
        return pl.BlockSpec((rows, LANES), lambda i: (index, 0))

    in_specs = [
        smem,
        smem,
        pl.BlockSpec((rows, block), lambda i: (half, i)),
        fixed(kp_index),
        fixed(kc_index),
        fixed(vp_index),
        fixed(vc_index),
        pl.BlockSpec((block, model), lambda i: (i, 0)),
    ]
    operands = [first, sinks, queries, k_prev, k_cur, v_prev, v_cur, out_weight]
    whole = pl.BlockSpec((rows, model), lambda i: (0, 0))
    wide = jax.ShapeDtypeStruct((rows, model), jnp.float32)
    narrow = jax.ShapeDtypeStruct((rows, model), jnp.bfloat16)
    if rank is None:
        out_shape, out_specs = wide, whole
    else:
        in_specs += [smem, whole]
        operands += [rank, other]
        out_shape, out_specs = (narrow, wide), (whole, whole)
    return pl.pallas_call(
        functools.partial(attend_kernel, group_pairs),
        grid=(width // block,),
        in_specs=in_specs,
        out_specs=out_specs,
        out_shape=out_shape,
        scratch_shapes=[pltpu.VMEM((rows, model), jnp.float32)],
        compiler_params=pltpu.CompilerParams(vmem_limit_bytes=48 * MIB),
        cost_estimate=pl.CostEstimate(
            flops=2 * rows * width * (model + 1024), bytes_accessed=6 * MIB, transcendentals=0
        ),
        name="attend",
    )(*operands)


def norm_kernel(
    expert_count, stream_ref, own_ref, came_ref, gain_ref, ids_ref, route_ref, *rest
):
    residual_ref, message_ref = rest[-2:]
    rows, model = stream_ref.shape
    residual = (
        stream_ref[...].astype(jnp.float32) + own_ref[...] + came_ref[...].astype(jnp.float32)
    ).astype(jnp.bfloat16)
    residual_ref[...] = residual
    wide = residual.astype(jnp.float32)
    mean = jnp.mean(wide * wide, axis=-1, keepdims=True)
    normed = (wide * lax.rsqrt(mean + 1e-05) * gain_ref[...]).astype(jnp.bfloat16)
    message_ref[:, :model] = normed
    if expert_count:
        expert = lax.broadcasted_iota(jnp.int32, (LANES, rows), 0)
        dense = jnp.zeros((LANES, rows), jnp.float32)
        for k in range(TOP):
            named = ids_ref[k : k + 1, :]
            hit = (expert == named) | (expert == named + expert_count)
            dense += jnp.where(hit, route_ref[k : k + 1, :], 0.0)
        lead = dense.astype(jnp.bfloat16).astype(jnp.float32)
        both = jnp.where(expert < expert_count, lead, dense - lead)
        message_ref[:, model:] = both.T.astype(jnp.bfloat16)


def norm(stream, own, came, gain, expert_ids, route_weights, expert_count, after):
    rows, model = stream.shape
    vmem = pl.BlockSpec(memory_space=pltpu.VMEM)
    extra = LANES if expert_count else 0
    return pl.pallas_call(
        functools.partial(norm_kernel, expert_count),
        in_specs=[vmem] * 6 + [pl.BlockSpec(memory_space=pl.ANY)] * len(after),
        out_shape=[
            jax.ShapeDtypeStruct((rows, model), jnp.bfloat16),
            jax.ShapeDtypeStruct((rows, model + extra), jnp.bfloat16),
        ],
        compiler_params=pltpu.CompilerParams(vmem_limit_bytes=16 * MIB),
        cost_estimate=pl.CostEstimate(
            flops=8 * rows * model, bytes_accessed=14 * rows * model, transcendentals=rows
        ),
        name="norm",
    )(stream, own, came, gain.reshape(1, model), expert_ids.T, route_weights.T, *after)


def expert_kernel(tile, expert_count, count, me_ref, *refs):
    x_refs, halves = refs[:count], refs[count : count + 6]
    out_refs, (x, total) = refs[count + 6 : 2 * count + 6], refs[2 * count + 6 :]
    model = halves[0].shape[0]
    starts = [0]
    for ref in x_refs:
        starts.append(starts[-1] + ref.shape[0])
    for start, ref in zip(starts, x_refs):
        x[start : start + ref.shape[0]] = ref[:, :model]
    total[...] = jnp.zeros_like(total)

    @pl.loop(0, halves[0].shape[1] // tile)
    def _(index):
        span = pl.ds(pl.multiple_of(index * tile, tile), tile)
        rows = x[...]
        parts = []
        for gate_ref, up_ref, down_ref in (halves[:3], halves[3:]):
            gate_pre = mm(rows, gate_ref[:, span])
            up_pre = mm(rows, up_ref[:, span])
            activated = gate_pre * jax.nn.sigmoid(1.702 * gate_pre) * (up_pre + 1.0)
            parts.append(mm(activated.astype(jnp.bfloat16), down_ref[span, :]))
        total[...] += parts[0] + parts[1]

    me = me_ref[0]
    for start, ref, out_ref in zip(starts, x_refs, out_refs):
        rows = ref.shape[0]
        sent = ref[:, model:].astype(jnp.float32)
        lane = lax.broadcasted_iota(jnp.int32, sent.shape, 1)
        mine = (lane == me) | (lane == me + expert_count)
        scale = jnp.sum(jnp.where(mine, sent, 0.0), axis=1, keepdims=True)
        out_ref[...] = (total[start : start + rows] * scale).astype(jnp.bfloat16)


def experts(blocks, me, halves, expert_count):
    model, half = halves[0].shape
    rows = sum(block.shape[0] for block in blocks)
    vmem = pl.BlockSpec(memory_space=pltpu.VMEM)
    return pl.pallas_call(
        functools.partial(expert_kernel, min(256, half), expert_count, len(blocks)),
        in_specs=[pl.BlockSpec(memory_space=pltpu.SMEM)] + [vmem] * (len(blocks) + 6),
        out_specs=[vmem] * len(blocks),
        out_shape=[jax.ShapeDtypeStruct((b.shape[0], model), jnp.bfloat16) for b in blocks],
        scratch_shapes=[
            pltpu.VMEM((rows, model), jnp.bfloat16),
            pltpu.VMEM((rows, model), jnp.float32),
        ],
        compiler_params=pltpu.CompilerParams(vmem_limit_bytes=EXPERT_VMEM),
        cost_estimate=pl.CostEstimate(
            flops=12 * rows * model * half, bytes_accessed=6 * rows * model, transcendentals=0
        ),
        name="experts",
    )(me, *blocks, *halves)


def ring_experts(residual, message, gate_weight, up_weight, down_weight, others):
    chips = lax.axis_size("seq")
    ring = SNAKES.get(chips, tuple(range(chips)))
    far = chips // 2
    ahead = [(ring[i], ring[(i + 1) % chips]) for i in range(chips)]
    hops = (ahead, [(to, of) for of, to in ahead])
    me = lax.axis_index("seq").astype(jnp.int32).reshape(1)
    half = message.shape[0] // 2
    spans = (slice(0, half), slice(half, 2 * half))
    halves = (gate_weight, up_weight, down_weight) + tuple(others)

    def apply(*blocks):
        return experts(blocks, me, halves, chips)

    came = [[message], [message]]
    given = [[None], [None]]
    for distance in range(1, far + 1):
        for side in range(2):
            block = came[side][distance - 1]
            if distance == far:
                block = block[spans[side]]
            came[side].append(lax.ppermute(block, "seq", hops[side]))
    (mine,) = apply(message)
    for distance in range(1, far + 1):
        outs = apply(came[0][distance], came[1][distance])
        given[0].append(outs[0])
        given[1].append(outs[1])

    wide = lambda value: value.astype(jnp.float32)
    total = wide(residual) + wide(mine)
    for side in range(2):
        moving = lax.ppermute(given[side][far], "seq", hops[side])
        for distance in range(far - 1, 0, -1):
            value = given[1 - side][distance]
            if distance == far - 1:
                parts = [value[spans[0]], value[spans[1]]]
                parts[side] = (wide(moving) + wide(parts[side])).astype(jnp.bfloat16)
                value = jnp.concatenate(parts, axis=0)
            else:
                value = (wide(moving) + wide(value)).astype(jnp.bfloat16)
            moving = lax.ppermute(value, "seq", hops[side])
        total += wide(moving)
    return total.astype(jnp.bfloat16)


def dispatched_experts(
    residual, normed, expert_ids, route_weights, gate_weight, up_weight, down_weight
):
    tokens_here = normed.shape[0]
    resid_f = residual.astype(jnp.float32)
    expert_count = EXP_DEV * lax.axis_size("seq")
    capacity = max(2, 3 * tokens_here * TOP // (2 * expert_count))
    flat_ids = expert_ids.reshape(-1)
    onehot = (flat_ids[:, None] == jnp.arange(expert_count, dtype=jnp.int32)[None, :]).astype(
        jnp.int32
    )
    earlier_count = jnp.cumsum(onehot, axis=0) - onehot
    slot_index = jnp.sum(earlier_count * onehot, axis=1)
    cell_index = (flat_ids * capacity + slot_index).reshape(tokens_here, TOP)
    chooser = jnp.any(
        cell_index[None, :, :]
        == jnp.arange(expert_count * capacity, dtype=jnp.int32)[:, None, None],
        axis=2,
    ).astype(jnp.bfloat16)
    outgoing = mm(chooser, normed).astype(jnp.bfloat16)
    outgoing = outgoing.reshape(expert_count, capacity, normed.shape[1])
    paired = lax.all_gather(outgoing, "rep", axis=1, tiled=True)
    arrived = lax.all_to_all(paired, "seq", split_axis=0, concat_axis=1, tiled=True)[0]
    gate_pre = mm(arrived, gate_weight)
    up_pre = mm(arrived, up_weight)
    activated = (gate_pre * jax.nn.sigmoid(1.702 * gate_pre) * (up_pre + 1.0)).astype(jnp.bfloat16)
    returned = lax.all_to_all(
        mm(activated, down_weight).astype(jnp.bfloat16)[None],
        "seq",
        split_axis=1,
        concat_axis=0,
        tiled=True,
    )
    expert_out = lax.psum_scatter(returned, "rep", scatter_dimension=1, tiled=True)
    picked = expert_out.reshape(expert_count * capacity, -1)[cell_index.reshape(-1)]
    picked = picked.reshape(tokens_here, TOP, -1)
    expert_sum = jnp.sum(route_weights[:, :, None] * picked.astype(jnp.float32), axis=1)
    return (resid_f + expert_sum).astype(jnp.bfloat16)


def per_device(
    stream,
    queries,
    key_rows,
    value_rows,
    sink_logits,
    out_weight,
    norm_gain,
    expert_ids,
    route_weights,
    gate_weight,
    up_weight,
    down_weight,
):
    block_len = queries.shape[0]
    seq = lax.axis_index("seq")
    rank = lax.axis_index("rep").astype(jnp.int32).reshape(1)
    gate_weight, up_weight, down_weight = gate_weight[0], up_weight[0], down_weight[0]
    use_ring = EXP_DEV * lax.axis_size("seq") <= 2 * TOP

    k_before, v_before = shifted(key_rows, "seq", 1), shifted(value_rows, "seq", 1)
    others = []
    if use_ring:
        others = [swapped(w, "rep") for w in (gate_weight, up_weight, down_weight)]
    never = jnp.zeros((1,), jnp.int32)
    first = (seq == 0).astype(jnp.int32).reshape(1)
    last = block_len // WINDOW - 1
    later_half = attend(
        1,
        never,
        sink_logits,
        queries,
        ((key_rows, 0), (key_rows, 1)),
        ((value_rows, 0), (value_rows, 1)),
        out_weight,
    )
    send, own = attend(
        0,
        first,
        sink_logits,
        queries,
        ((k_before, last), (key_rows, 0)),
        ((v_before, last), (value_rows, 0)),
        out_weight,
        rank,
        later_half,
    )
    came = swapped(send, "rep")
    expert_count = lax.axis_size("seq") * EXP_DEV if use_ring else 0
    residual, message = norm(
        stream, own, came, norm_gain, expert_ids, route_weights, expert_count, others
    )
    if use_ring:
        return ring_experts(residual, message, gate_weight, up_weight, down_weight, others)
    return dispatched_experts(
        residual, message, expert_ids, route_weights, gate_weight, up_weight, down_weight
    )


def solution(mesh):
    return jax.shard_map(
        per_device,
        mesh=mesh,
        in_specs=(
            P(("groups", "seq", "rep"), None),
            P(("groups", "seq"), "rep"),
            P(("groups", "seq"), "rep"),
            P(("groups", "seq"), "rep"),
            P("rep"),
            P("rep", None),
            P(),
            P(("groups", "seq", "rep"), None),
            P(("groups", "seq", "rep"), None),
            P("seq", None, "rep"),
            P("seq", None, "rep"),
            P("seq", "rep", None),
        ),
        out_specs=P(("groups", "seq", "rep"), None),
        check_vma=False,
    )
```

time: 151 us -> 121 us (0.80)
  starting transfers between devices: 41.3 us -> 25.6 us
  local copies, waits for them, and re-layouts: 15 us -> 5.38 us
  Pallas kernels: 50.6 us -> 41.6 us
  waiting for transfers between devices: 38.5 us -> 46 us
  other arithmetic: 4.49 us -> 1.47 us
    ppermute x28 -> x16, starting transfers between devices: 30 us -> 16.8 us  [the longest x8 8.26 us: ring_experts(): came[side].append(lax.ppermute(block, 'seq', hops[side]))]
    ppermute x28 -> x16, waiting for transfers between devices: 34.1 us -> 44.3 us  [the longest x8 19.8 us: ring_experts(): came[side].append(lax.ppermute(block, 'seq', hops[side]))]
    pallas_call x6, Pallas kernels: 40.6 us -> 32.3 us  [the longest x5 32 us: experts(): pl.pallas_call(functools.partial(expert_kernel, min(256, half), expert_co...]
    ppermute x7 -> x4, starting transfers between devices: 6.9 us -> 1.03 us  [swapped(): return lax.ppermute(value, axis, [(i, i ^ bit) for i in range(peers)])]
    unnamed x36 -> x32, local copies, waits for them, and re-layouts: 10.8 us -> 5.32 us
    ppermute x1 -> x2, starting transfers between devices: 4.4 us -> 7.84 us  [shifted(): return lax.ppermute(value, axis, pairs)]
    ppermute x7 -> x4, waiting for transfers between devices: 4.36 us -> 1.69 us  [swapped(): return lax.ppermute(value, axis, [(i, i ^ bit) for i in range(peers)])]
  transfers between devices with their start and end apart: 36 -> 22, of which waited for: 13 -> 10; matrix products, arithmetic and copies ran while one was open for 6% -> 0% of each run, Pallas kernels for 34% -> 30%
where the time goes in v2:
time: 121 us; the launch traced here: 120 us
  waiting for transfers between devices  46 us (38%)
  Pallas kernels  41.6 us (34%)
  starting transfers between devices  25.6 us (21%)
  local copies, waits for them, and re-layouts  5.38 us (4%)
  other arithmetic  1.47 us (1%)
    pallas_call x5, Pallas kernels, experts(): pl.pallas_call(functools.partial(expert_kernel, min(256, half), expert_co...  32 us
    ppermute x8, waiting for transfers between devices, ring_experts(): came[side].append(lax.ppermute(block, 'seq', hops[side]))  19.8 us
    ppermute x6, waiting for transfers between devices, ring_experts(): moving = lax.ppermute(value, 'seq', hops[side])  19.2 us
    pallas_call x2, Pallas kernels, attend(): pl.pallas_call(functools.partial(attend_kernel, group_pairs), grid=(width...  9.28 us
    ppermute x8, starting transfers between devices, ring_experts(): came[side].append(lax.ppermute(block, 'seq', hops[side]))  8.26 us
    ppermute x2, starting transfers between devices, shifted(): return lax.ppermute(value, axis, pairs)  7.84 us
    ppermute x6, starting transfers between devices, ring_experts(): moving = lax.ppermute(value, 'seq', hops[side])  6.37 us
    unnamed x32, local copies, waits for them, and re-layouts  5.32 us
  transfers between devices with their start and end apart: 22, of which 10 were waited for; matrix products, arithmetic and copies ran while one was open for 0% of the time, Pallas kernels for 30%

profile of v2, /device:TPU:0, one launch (start us, length us, event | category | flops | bytes accessed | tf_op | source)
XLA Modules:
  0.0 120.4 jit_solution(14671003898276095768)
XLA Ops:
  0.0 0.5 collective-permute-start.3
  0.5 0.5 collective-permute-start.5
  1.0 4.4 %collective-permute-start = (bf16[256,128]{1,0:T(8,128)(2,1)}, bf16[256,128]{1,0:T(8,128)(2,1)S(1)}, u32[]{:S(2)}, u32[]{:S(2)}) collective-permute-start(bf16[256,128]{1,0:T(8,128)(2,1)} %kc_ref.3), channel_id=1, source_target_pairs={{0,2},{2,4},{4,6},{6,8},{8,10},{10,12},{12,14},{1,3},{3,5},{5,7},{... | collective-permute-start | bytes 196616 | tf_op jit(solution)/shard_map/ppermute | solution.py:24
  5.4 3.5 %collective-permute-start.1 = (bf16[256,128]{1,0:T(8,128)(2,1)}, bf16[256,128]{1,0:T(8,128)(2,1)S(1)}, u32[]{:S(2)}, u32[]{:S(2)}) collective-permute-start(bf16[256,128]{1,0:T(8,128)(2,1)} %vc_ref.3), channel_id=1, source_target_pairs={{0,2},{2,4},{4,6},{6,8},{8,10},{10,12},{12,14},{1,3},{3,5},{5,7},{... | collective-permute-start | bytes 196616 | tf_op jit(solution)/shard_map/ppermute | solution.py:24
  8.8 1.9 %copy-done.3 = bf16[1024,1536]{1,0:T(8,128)(2,1)S(1)} copy-done((bf16[1024,1536]{1,0:T(8,128)(2,1)S(1)}, bf16[1024,1536]{1,0:T(8,128)(2,1)}, u32[]{:S(2)}) %copy-start.3) | copy-done | bytes 3145752
  10.7 1.0 copy-done.5
  11.8 0.8 copy-done.7
  12.6 0.8 copy-done.9
  13.4 0.7 copy-done.13
  14.1 4.6 %attend.2.rest_1_ = f32[128,1536]{1,0:T(8,128)S(1)} custom-call(s32[1]{0:T(128)} %constant.11.clone.1.first_ref, f32[16]{0:T(128)S(1)} %copy-done.13, bf16[256,1024]{1,0:T(8,128)(2,1)S(1)} %copy-done.5, bf16[256,128]{1,0:T(8,128)(2,1)S(1)} %copy-done.7, bf16[256,128]{1,0:T(8,128)(2,1)S(1)} %copy-done.7, bf16[256,128]{1,0:T(8,128)(2,1)S(1)} %copy-done.9, ...), custom_call_target="tpu_custom_call" | custom-call | flops 671088640 | bytes 6291456 | tf_op jit(solution)/shard_map/attend/pallas_call | solution.py:143
  18.8 4.7 %attend.3 = (bf16[128,1536]{1,0:T(8,128)(2,1)S(1)}, f32[128,1536]{1,0:T(8,128)S(1)}) custom-call(s32[1]{0:T(128)} %bitcast.first_ref, f32[16]{0:T(128)S(1)} %copy-done.14, bf16[256,1024]{1,0:T(8,128)(2,1)S(1)} %copy-done.6, bf16[256,128]{1,0:T(8,128)(2,1)S(1)} %collective-permute-done.kp_ref, bf16[256,128]{1,0:T(8,128)(2,1)S(1)} %copy-done.8, ...), custom_call_target="tpu_custom_call" | custom-call | flops 671088640 | bytes 6291456 | tf_op jit(solution)/shard_map/attend/pallas_call | solution.py:143
  23.6 1.7 %collective-permute-done.2.came_ref = bf16[128,1536]{1,0:T(8,128)(2,1)S(1)} collective-permute-done((bf16[128,1536]{1,0:T(8,128)(2,1)S(1)}, bf16[128,1536]{1,0:T(8,128)(2,1)S(1)}, u32[]{:S(2)}, u32[]{:S(2)}) %collective-permute-start.2) | collective-permute-done | bytes 393248 | tf_op jit(solution)/shard_map/ppermute | solution.py:29
  25.4 0.3 norm.1
  25.7 1.5 %collective-permute-start.10 = (bf16[128,1664]{1,0:T(8,128)(2,1)S(1)}, bf16[128,1664]{1,0:T(8,128)(2,1)S(1)}, u32[]{:S(2)}, u32[]{:S(2)}) collective-permute-start(bf16[128,1664]{1,0:T(8,128)(2,1)S(1)} %get-tuple-element.20.refs_0_), channel_id=1, source_target_pairs={{4,0},{8,4},{12,8},{14,12},{10,14},{6,10},{2,6},{0,2},{5,1},{9,5},... | collective-permute-start | bytes 1277960 | tf_op jit(solution)/shard_map/ppermute | solution.py:277
  27.3 0.5 collective-permute-start.6
  27.8 9.8 %collective-permute-done.10.refs_1_ = bf16[128,1664]{1,0:T(8,128)(2,1)S(1)} collective-permute-done((bf16[128,1664]{1,0:T(8,128)(2,1)S(1)}, bf16[128,1664]{1,0:T(8,128)(2,1)S(1)}, u32[]{:S(2)}, u32[]{:S(2)}) %collective-permute-start.10) | collective-permute-done | bytes 426016 | tf_op jit(solution)/shard_map/ppermute | solution.py:277
  37.6 1.5 %collective-permute-start.11 = (bf16[128,1664]{1,0:T(8,128)(2,1)S(1)}, bf16[128,1664]{1,0:T(8,128)(2,1)S(1)}, u32[]{:S(2)}, u32[]{:S(2)}) collective-permute-start(bf16[128,1664]{1,0:T(8,128)(2,1)S(1)} %collective-permute-done.10.refs_1_), channel_id=1, source_target_pairs={{4,0},{8,4},{12,8},{14,12},{10,14},{6,10},{2,6},{0,2},{5,1},{9,5},... | collective-permute-start | bytes 1277960 | tf_op jit(solution)/shard_map/ppermute | solution.py:277
  39.1 0.5 collective-permute-start.7
  39.7 9.0 %collective-permute-done.11.refs_1_ = bf16[128,1664]{1,0:T(8,128)(2,1)S(1)} collective-permute-done((bf16[128,1664]{1,0:T(8,128)(2,1)S(1)}, bf16[128,1664]{1,0:T(8,128)(2,1)S(1)}, u32[]{:S(2)}, u32[]{:S(2)}) %collective-permute-start.11) | collective-permute-done | bytes 426016 | tf_op jit(solution)/shard_map/ppermute | solution.py:277
  48.7 1.5 %collective-permute-start.12 = (bf16[128,1664]{1,0:T(8,128)(2,1)S(1)}, bf16[128,1664]{1,0:T(8,128)(2,1)S(1)}, u32[]{:S(2)}, u32[]{:S(2)}) collective-permute-start(bf16[128,1664]{1,0:T(8,128)(2,1)S(1)} %collective-permute-done.11.refs_1_), channel_id=1, source_target_pairs={{4,0},{8,4},{12,8},{14,12},{10,14},{6,10},{2,6},{0,2},{5,1},{9,5},... | collective-permute-start | bytes 1277960 | tf_op jit(solution)/shard_map/ppermute | solution.py:277
  50.2 0.5 collective-permute-start.8
  50.7 7.1 %experts.9 = (bf16[128,1536]{1,0:T(8,128)(2,1)S(1)}, bf16[128,1536]{1,0:T(8,128)(2,1)S(1)}) custom-call(s32[1]{0:T(128)} %bitcast.7.me_ref, bf16[128,1664]{1,0:T(8,128)(2,1)S(1)} %collective-permute-done.6.refs_0_, bf16[128,1664]{1,0:T(8,128)(2,1)S(1)} %collective-permute-done.10.refs_1_, bf16[1536,768]{1,0:T(8,128)(2,1)S(1)} %bitcast.9, ...), custom_call_target="tpu_custom_call" | custom-call | flops 3623878656 | bytes 2359296 | tf_op jit(solution)/shard_map/experts/pallas_call | solution.py:239
  57.8 0.9 collective-permute-done.12.refs_1_
  58.8 1.5 %collective-permute-start.13 = (bf16[64,1664]{1,0:T(8,128)(2,1)S(1)}, bf16[64,1664]{1,0:T(8,128)(2,1)S(1)}, u32[]{:S(2)}, u32[]{:S(2)}) collective-permute-start(bf16[64,1664]{1,0:T(8,128)(2,1)S(1)} %slice.25), channel_id=1, source_target_pairs={{4,0},{8,4},{12,8},{14,12},{10,14},{6,10},{2,6},{0,2},{5,1},{9,5},... | collective-permute-start | bytes 638984 | tf_op jit(solution)/shard_map/ppermute | solution.py:277
  60.4 0.6 collective-permute-start.9
  60.9 7.1 %experts.8 = (bf16[128,1536]{1,0:T(8,128)(2,1)S(1)}, bf16[128,1536]{1,0:T(8,128)(2,1)S(1)}) custom-call(s32[1]{0:T(128)} %bitcast.7.me_ref, bf16[128,1664]{1,0:T(8,128)(2,1)S(1)} %collective-permute-done.7.refs_0_, bf16[128,1664]{1,0:T(8,128)(2,1)S(1)} %collective-permute-done.11.refs_1_, bf16[1536,768]{1,0:T(8,128)(2,1)S(1)} %bitcast.10, ...), custom_call_target="tpu_custom_call" | custom-call | flops 3623878656 | bytes 2359296 | tf_op jit(solution)/shard_map/experts/pallas_call | solution.py:239
  68.1 5.3 %experts.6 = (bf16[64,1536]{1,0:T(8,128)(2,1)S(1)}, bf16[64,1536]{1,0:T(8,128)(2,1)S(1)}) custom-call(s32[1]{0:T(128)} %bitcast.7.me_ref, bf16[64,1664]{1,0:T(8,128)(2,1)S(1)} %collective-permute-done.9.refs_0_, bf16[64,1664]{1,0:T(8,128)(2,1)S(1)} %collective-permute-done.13.refs_1_, bf16[1536,768]{1,0:T(8,128)(2,1)S(1)} %bitcast.11, ...), custom_call_target="tpu_custom_call" | custom-call | flops 1811939328 | bytes 1179648 | tf_op jit(solution)/shard_map/experts/pallas_call | solution.py:239
  73.4 1.6 %collective-permute-start.14 = (bf16[64,1536]{1,0:T(8,128)(2,1)S(1)}, bf16[64,1536]{1,0:T(8,128)(2,1)S(1)}, u32[]{:S(2)}, u32[]{:S(2)}) collective-permute-start(bf16[64,1536]{1,0:T(8,128)(2,1)S(1)} %get-tuple-element.21), channel_id=1, source_target_pairs={{0,4},{4,8},{8,12},{12,14},{14,10},{10,6},{6,2},{2,0},{1,5},{5,9},... | collective-permute-start | bytes 589832 | tf_op jit(solution)/shard_map/ppermute | solution.py:287
  75.0 7.1 %experts.7 = (bf16[128,1536]{1,0:T(8,128)(2,1)S(1)}, bf16[128,1536]{1,0:T(8,128)(2,1)S(1)}) custom-call(s32[1]{0:T(128)} %bitcast.7.me_ref, bf16[128,1664]{1,0:T(8,128)(2,1)S(1)} %collective-permute-done.8.refs_0_, bf16[128,1664]{1,0:T(8,128)(2,1)S(1)} %collective-permute-done.12.refs_1_, bf16[1536,768]{1,0:T(8,128)(2,1)S(1)} %bitcast.12, ...), custom_call_target="tpu_custom_call" | custom-call | flops 3623878656 | bytes 2359296 | tf_op jit(solution)/shard_map/experts/pallas_call | solution.py:239
  82.2 0.5 collective-permute-start.18
  82.8 1.6 %collective-permute-start.15 = (bf16[128,1536]{1,0:T(8,128)(2,1)S(1)}, bf16[128,1536]{1,0:T(8,128)(2,1)S(1)}, u32[]{:S(2)}, u32[]{:S(2)}) collective-permute-start(bf16[128,1536]{1,0:T(8,128)(2,1)S(1)} %pad_maximum_fusion), channel_id=1, source_target_pairs={{0,4},{4,8},{8,12},{12,14},{14,10},{10,6},{6,2},{2,0},{1,5},{5,9},... | collective-permute-start | bytes 1179656 | tf_op jit(solution)/shard_map/ppermute | solution.py:296
  84.4 5.3 %collective-permute-done.18 = bf16[64,1536]{1,0:T(8,128)(2,1)S(1)} collective-permute-done((bf16[64,1536]{1,0:T(8,128)(2,1)S(1)}, bf16[64,1536]{1,0:T(8,128)(2,1)S(1)}, u32[]{:S(2)}, u32[]{:S(2)}) %collective-permute-start.18) | collective-permute-done | bytes 196640 | tf_op jit(solution)/shard_map/ppermute | solution.py:287
  89.8 0.5 collective-permute-start.19
  90.3 2.0 %collective-permute-done.15 = bf16[128,1536]{1,0:T(8,128)(2,1)S(1)} collective-permute-done((bf16[128,1536]{1,0:T(8,128)(2,1)S(1)}, bf16[128,1536]{1,0:T(8,128)(2,1)S(1)}, u32[]{:S(2)}, u32[]{:S(2)}) %collective-permute-start.15) | collective-permute-done | bytes 393248 | tf_op jit(solution)/shard_map/ppermute | solution.py:296
  92.3 0.1 add_convert_fusion.4
  92.4 1.6 %collective-permute-start.16 = (bf16[128,1536]{1,0:T(8,128)(2,1)S(1)}, bf16[128,1536]{1,0:T(8,128)(2,1)S(1)}, u32[]{:S(2)}, u32[]{:S(2)}) collective-permute-start(bf16[128,1536]{1,0:T(8,128)(2,1)S(1)} %add_convert_fusion.4), channel_id=1, source_target_pairs={{0,4},{4,8},{8,12},{12,14},{14,10},{10,6},{6,2},{2,0},{1,5},{5,9},... | collective-permute-start | bytes 1179656 | tf_op jit(solution)/shard_map/ppermute | solution.py:296
  94.0 6.1 %collective-permute-done.19 = bf16[128,1536]{1,0:T(8,128)(2,1)S(1)} collective-permute-done((bf16[128,1536]{1,0:T(8,128)(2,1)S(1)}, bf16[128,1536]{1,0:T(8,128)(2,1)S(1)}, u32[]{:S(2)}, u32[]{:S(2)}) %collective-permute-start.19) | collective-permute-done | bytes 393248 | tf_op jit(solution)/shard_map/ppermute | solution.py:296
  100.2 0.1 add_convert_fusion.2
  100.3 0.5 collective-permute-start.20
  100.8 2.0 %collective-permute-done.16 = bf16[128,1536]{1,0:T(8,128)(2,1)S(1)} collective-permute-done((bf16[128,1536]{1,0:T(8,128)(2,1)S(1)}, bf16[128,1536]{1,0:T(8,128)(2,1)S(1)}, u32[]{:S(2)}, u32[]{:S(2)}) %collective-permute-start.16) | collective-permute-done | bytes 393248 | tf_op jit(solution)/shard_map/ppermute | solution.py:296
  102.7 0.1 add_convert_fusion.3
  102.8 1.6 %collective-permute-start.17 = (bf16[128,1536]{1,0:T(8,128)(2,1)S(1)}, bf16[128,1536]{1,0:T(8,128)(2,1)S(1)}, u32[]{:S(2)}, u32[]{:S(2)}) collective-permute-start(bf16[128,1536]{1,0:T(8,128)(2,1)S(1)} %add_convert_fusion.3), channel_id=1, source_target_pairs={{0,4},{4,8},{8,12},{12,14},{14,10},{10,6},{6,2},{2,0},{1,5},{5,9},... | collective-permute-start | bytes 1179656 | tf_op jit(solution)/shard_map/ppermute | solution.py:296
  104.4 7.1 %collective-permute-done.20 = bf16[128,1536]{1,0:T(8,128)(2,1)S(1)} collective-permute-done((bf16[128,1536]{1,0:T(8,128)(2,1)S(1)}, bf16[128,1536]{1,0:T(8,128)(2,1)S(1)}, u32[]{:S(2)}, u32[]{:S(2)}) %collective-permute-start.20) | collective-permute-done | bytes 393248 | tf_op jit(solution)/shard_map/ppermute | solution.py:296
  111.5 0.1 add_convert_fusion.1
  111.6 0.5 collective-permute-start.21
  112.1 5.3 %experts.5 = bf16[128,1536]{1,0:T(8,128)(2,1)S(1)} custom-call(s32[1]{0:T(128)} %bitcast.7.me_ref, bf16[128,1664]{1,0:T(8,128)(2,1)S(1)} %get-tuple-element.20.refs_0_, bf16[1536,768]{1,0:T(8,128)(2,1)S(1)} %bitcast.13, bf16[1536,768]{1,0:T(8,128)(2,1)S(1)} %bitcast.19, bf16[768,1536]{1,0:T(8,128)(2,1)S(1)} %bitcast.25, ...), custom_call_target="tpu_custom_call" | custom-call | flops 1811939328 | bytes 1179648 | tf_op jit(solution)/shard_map/experts/pallas_call | solution.py:239
  117.4 2.0 %collective-permute-done.21 = bf16[128,1536]{1,0:T(8,128)(2,1)S(1)} collective-permute-done((bf16[128,1536]{1,0:T(8,128)(2,1)S(1)}, bf16[128,1536]{1,0:T(8,128)(2,1)S(1)}, u32[]{:S(2)}, u32[]{:S(2)}) %collective-permute-start.21) | collective-permute-done | bytes 393248 | tf_op jit(solution)/shard_map/ppermute | solution.py:296
  119.5 0.9 add_convert_fusion
  (50 shorter events, 0.5 us)
Async XLA Ops:
  0.0 25.3 %collective-permute-start.3 = (bf16[1536,768]{1,0:T(8,128)(2,1)}, bf16[1536,768]{1,0:T(8,128)(2,1)S(1)}, u32[]{:S(2)}, u32[]{:S(2)}) collective-permute-start(bf16[1536,768]{1,0:T(8,128)(2,1)} %bitcast.8), channel_id=1, source_target_pairs={{0,1},{1,0},{2,3},{3,2},{4,5},{5,4},{6,7},{7,6},{8,9},{9,8},{10,11... | collective-permute-start | bytes 7077896 | tf_op jit(solution)/shard_map/ppermute | solution.py:29
  0.5 24.9 %collective-permute-start.4 = (bf16[1536,768]{1,0:T(8,128)(2,1)}, bf16[1536,768]{1,0:T(8,128)(2,1)}, u32[]{:S(2)}, u32[]{:S(2)}) collective-permute-start(bf16[1536,768]{1,0:T(8,128)(2,1)} %bitcast.14), channel_id=1, source_target_pairs={{0,1},{1,0},{2,3},{3,2},{4,5},{5,4},{6,7},{7,6},{8,9},{9,8},{10,11... | collective-permute-start | bytes 7077896 | tf_op jit(solution)/shard_map/ppermute | solution.py:29
  0.5 24.8 %collective-permute-start.5 = (bf16[768,1536]{1,0:T(8,128)(2,1)}, bf16[768,1536]{1,0:T(8,128)(2,1)}, u32[]{:S(2)}, u32[]{:S(2)}) collective-permute-start(bf16[768,1536]{1,0:T(8,128)(2,1)} %bitcast.20), channel_id=1, source_target_pairs={{0,1},{1,0},{2,3},{3,2},{4,5},{5,4},{6,7},{7,6},{8,9},{9,8},{10,11... | collective-permute-start | bytes 7077896 | tf_op jit(solution)/shard_map/ppermute | solution.py:29
  1.0 17.8 %collective-permute-start = (bf16[256,128]{1,0:T(8,128)(2,1)}, bf16[256,128]{1,0:T(8,128)(2,1)S(1)}, u32[]{:S(2)}, u32[]{:S(2)}) collective-permute-start(bf16[256,128]{1,0:T(8,128)(2,1)} %kc_ref.3), channel_id=1, source_target_pairs={{0,2},{2,4},{4,6},{6,8},{8,10},{10,12},{12,14},{1,3},{3,5},{5,7},{... | collective-permute-start | bytes 196616 | tf_op jit(solution)/shard_map/ppermute | solution.py:24
  5.4 13.4 %collective-permute-start.1 = (bf16[256,128]{1,0:T(8,128)(2,1)}, bf16[256,128]{1,0:T(8,128)(2,1)S(1)}, u32[]{:S(2)}, u32[]{:S(2)}) collective-permute-start(bf16[256,128]{1,0:T(8,128)(2,1)} %vc_ref.3), channel_id=1, source_target_pairs={{0,2},{2,4},{4,6},{6,8},{8,10},{10,12},{12,14},{1,3},{3,5},{5,7},{... | collective-permute-start | bytes 196616 | tf_op jit(solution)/shard_map/ppermute | solution.py:24
  8.8 1.9 %copy-start.3 = (bf16[1024,1536]{1,0:T(8,128)(2,1)S(1)}, bf16[1024,1536]{1,0:T(8,128)(2,1)}, u32[]{:S(2)}) copy-start(bf16[1024,1536]{1,0:T(8,128)(2,1)} %ow_ref.3) | copy-start | bytes 9437188
  10.7 1.0 copy-start.5
  11.8 0.8 copy-start.7
  12.6 0.8 copy-start.9
  13.4 0.7 copy-start.13
  14.1 4.7 %copy-start.4 = (bf16[1024,1536]{1,0:T(8,128)(2,1)S(1)}, bf16[1024,1536]{1,0:T(8,128)(2,1)}, u32[]{:S(2)}) copy-start(bf16[1024,1536]{1,0:T(8,128)(2,1)} %ow_ref.3) | copy-start | bytes 9437188
  14.1 4.7 %copy-start.6 = (bf16[256,1024]{1,0:T(8,128)(2,1)S(1)}, bf16[256,1024]{1,0:T(8,128)(2,1)}, u32[]{:S(2)}) copy-start(bf16[256,1024]{1,0:T(8,128)(2,1)} %q_ref.3) | copy-start | bytes 1572868
  14.1 4.7 %copy-start.8 = (bf16[256,128]{1,0:T(8,128)(2,1)S(1)}, bf16[256,128]{1,0:T(8,128)(2,1)}, u32[]{:S(2)}) copy-start(bf16[256,128]{1,0:T(8,128)(2,1)} %kc_ref.3) | copy-start | bytes 196612
  14.1 4.7 %copy-start.14 = (f32[16]{0:T(128)S(1)}, f32[16]{0:T(128)}, u32[]{:S(2)}) copy-start(f32[16]{0:T(128)} %sink_ref.3) | copy-start | bytes 196
  18.8 4.8 %copy-start.15 = (f32[1536]{0:T(1024)S(1)}, f32[1536]{0:T(1024)}, u32[]{:S(2)}) copy-start(f32[1536]{0:T(1024)} %param.18) | copy-start | bytes 18436
  18.8 6.5 %copy-start.10 = (bf16[128,1536]{1,0:T(8,128)(2,1)S(1)}, bf16[128,1536]{1,0:T(8,128)(2,1)}, u32[]{:S(2)}) copy-start(bf16[128,1536]{1,0:T(8,128)(2,1)} %stream_ref.1) | copy-start | bytes 1179652
  18.8 6.5 %copy-start.11 = (s32[128,4]{0,1:T(4,128)S(1)}, s32[128,4]{0,1:T(4,128)}, u32[]{:S(2)}) copy-start(s32[128,4]{0,1:T(4,128)} %param.19) | copy-start | bytes 6148
  18.8 6.5 %copy-start.12 = (f32[128,4]{0,1:T(4,128)S(1)}, f32[128,4]{0,1:T(4,128)}, u32[]{:S(2)}) copy-start(f32[128,4]{0,1:T(4,128)} %param.20) | copy-start | bytes 6148
  23.5 1.8 %collective-permute-start.2 = (bf16[128,1536]{1,0:T(8,128)(2,1)S(1)}, bf16[128,1536]{1,0:T(8,128)(2,1)S(1)}, u32[]{:S(2)}, u32[]{:S(2)}) collective-permute-start(bf16[128,1536]{1,0:T(8,128)(2,1)S(1)} %get-tuple-element.18), channel_id=1, source_target_pairs={{0,1},{1,0},{2,3},{3,2},{4,5},{5,4},{6,7},{7,6},{8,9},{9,8},{10,11... | collective-permute-start | bytes 1179656 | tf_op jit(solution)/shard_map/ppermute | solution.py:29
  25.3 25.3 %copy-start = (bf16[1,1536,768]{2,1,0:T(8,128)(2,1)S(1)}, bf16[1,1536,768]{2,1,0:T(8,128)(2,1)}, u32[]{:S(2)}) copy-start(bf16[1,1536,768]{2,1,0:T(8,128)(2,1)} %param.21) | copy-start | bytes 7077892
  25.4 25.3 %copy-start.1 = (bf16[1,1536,768]{2,1,0:T(8,128)(2,1)S(1)}, bf16[1,1536,768]{2,1,0:T(8,128)(2,1)}, u32[]{:S(2)}) copy-start(bf16[1,1536,768]{2,1,0:T(8,128)(2,1)} %param.22) | copy-start | bytes 7077892
  25.4 25.3 %copy-start.2 = (bf16[1,768,1536]{2,1,0:T(8,128)(2,1)S(1)}, bf16[1,768,1536]{2,1,0:T(8,128)(2,1)}, u32[]{:S(2)}) copy-start(bf16[1,768,1536]{2,1,0:T(8,128)(2,1)} %param.23) | copy-start | bytes 7077892
  25.7 11.9 %collective-permute-start.10 = (bf16[128,1664]{1,0:T(8,128)(2,1)S(1)}, bf16[128,1664]{1,0:T(8,128)(2,1)S(1)}, u32[]{:S(2)}, u32[]{:S(2)}) collective-permute-start(bf16[128,1664]{1,0:T(8,128)(2,1)S(1)} %get-tuple-element.20.refs_0_), channel_id=1, source_target_pairs={{4,0},{8,4},{12,8},{14,12},{10,14},{6,10},{2,6},{0,2},{5,1},{9,5},... | collective-permute-start | bytes 1277960 | tf_op jit(solution)/shard_map/ppermute | solution.py:277
  27.3 11.9 %collective-permute-start.6 = (bf16[128,1664]{1,0:T(8,128)(2,1)S(1)}, bf16[128,1664]{1,0:T(8,128)(2,1)S(1)}, u32[]{:S(2)}, u32[]{:S(2)}) collective-permute-start(bf16[128,1664]{1,0:T(8,128)(2,1)S(1)} %get-tuple-element.20.refs_0_), channel_id=1, source_target_pairs={{0,4},{4,8},{8,12},{12,14},{14,10},{10,6},{6,2},{2,0},{1,5},{5,9},... | collective-permute-start | bytes 1277960 | tf_op jit(solution)/shard_map/ppermute | solution.py:277
  37.6 11.0 %collective-permute-start.11 = (bf16[128,1664]{1,0:T(8,128)(2,1)S(1)}, bf16[128,1664]{1,0:T(8,128)(2,1)S(1)}, u32[]{:S(2)}, u32[]{:S(2)}) collective-permute-start(bf16[128,1664]{1,0:T(8,128)(2,1)S(1)} %collective-permute-done.10.refs_1_), channel_id=1, source_target_pairs={{4,0},{8,4},{12,8},{14,12},{10,14},{6,10},{2,6},{0,2},{5,1},{9,5},... | collective-permute-start | bytes 1277960 | tf_op jit(solution)/shard_map/ppermute | solution.py:277
  39.1 11.0 %collective-permute-start.7 = (bf16[128,1664]{1,0:T(8,128)(2,1)S(1)}, bf16[128,1664]{1,0:T(8,128)(2,1)S(1)}, u32[]{:S(2)}, u32[]{:S(2)}) collective-permute-start(bf16[128,1664]{1,0:T(8,128)(2,1)S(1)} %collective-permute-done.6.refs_0_), channel_id=1, source_target_pairs={{0,4},{4,8},{8,12},{12,14},{14,10},{10,6},{6,2},{2,0},{1,5},{5,9},... | collective-permute-start | bytes 1277960 | tf_op jit(solution)/shard_map/ppermute | solution.py:277
  48.7 10.1 %collective-permute-start.12 = (bf16[128,1664]{1,0:T(8,128)(2,1)S(1)}, bf16[128,1664]{1,0:T(8,128)(2,1)S(1)}, u32[]{:S(2)}, u32[]{:S(2)}) collective-permute-start(bf16[128,1664]{1,0:T(8,128)(2,1)S(1)} %collective-permute-done.11.refs_1_), channel_id=1, source_target_pairs={{4,0},{8,4},{12,8},{14,12},{10,14},{6,10},{2,6},{0,2},{5,1},{9,5},... | collective-permute-start | bytes 1277960 | tf_op jit(solution)/shard_map/ppermute | solution.py:277
  50.2 10.2 %collective-permute-start.8 = (bf16[128,1664]{1,0:T(8,128)(2,1)S(1)}, bf16[128,1664]{1,0:T(8,128)(2,1)S(1)}, u32[]{:S(2)}, u32[]{:S(2)}) collective-permute-start(bf16[128,1664]{1,0:T(8,128)(2,1)S(1)} %collective-permute-done.7.refs_0_), channel_id=1, source_target_pairs={{0,4},{4,8},{8,12},{12,14},{14,10},{10,6},{6,2},{2,0},{1,5},{5,9},... | collective-permute-start | bytes 1277960 | tf_op jit(solution)/shard_map/ppermute | solution.py:277
  58.8 9.3 %collective-permute-start.13 = (bf16[64,1664]{1,0:T(8,128)(2,1)S(1)}, bf16[64,1664]{1,0:T(8,128)(2,1)S(1)}, u32[]{:S(2)}, u32[]{:S(2)}) collective-permute-start(bf16[64,1664]{1,0:T(8,128)(2,1)S(1)} %slice.25), channel_id=1, source_target_pairs={{4,0},{8,4},{12,8},{14,12},{10,14},{6,10},{2,6},{0,2},{5,1},{9,5},... | collective-permute-start | bytes 638984 | tf_op jit(solution)/shard_map/ppermute | solution.py:277
  60.4 7.7 %collective-permute-start.9 = (bf16[64,1664]{1,0:T(8,128)(2,1)S(1)}, bf16[64,1664]{1,0:T(8,128)(2,1)S(1)}, u32[]{:S(2)}, u32[]{:S(2)}) collective-permute-start(bf16[64,1664]{1,0:T(8,128)(2,1)S(1)} %slice.24), channel_id=1, source_target_pairs={{0,4},{4,8},{8,12},{12,14},{14,10},{10,6},{6,2},{2,0},{1,5},{5,9},... | collective-permute-start | bytes 638984 | tf_op jit(solution)/shard_map/ppermute | solution.py:277
  73.4 9.3 %collective-permute-start.14 = (bf16[64,1536]{1,0:T(8,128)(2,1)S(1)}, bf16[64,1536]{1,0:T(8,128)(2,1)S(1)}, u32[]{:S(2)}, u32[]{:S(2)}) collective-permute-start(bf16[64,1536]{1,0:T(8,128)(2,1)S(1)} %get-tuple-element.21), channel_id=1, source_target_pairs={{0,4},{4,8},{8,12},{12,14},{14,10},{10,6},{6,2},{2,0},{1,5},{5,9},... | collective-permute-start | bytes 589832 | tf_op jit(solution)/shard_map/ppermute | solution.py:287
  82.2 7.5 %collective-permute-start.18 = (bf16[64,1536]{1,0:T(8,128)(2,1)S(1)}, bf16[64,1536]{1,0:T(8,128)(2,1)S(1)}, u32[]{:S(2)}, u32[]{:S(2)}) collective-permute-start(bf16[64,1536]{1,0:T(8,128)(2,1)S(1)} %get-tuple-element.26), channel_id=1, source_target_pairs={{4,0},{8,4},{12,8},{14,12},{10,14},{6,10},{2,6},{0,2},{5,1},{9,5},... | collective-permute-start | bytes 589832 | tf_op jit(solution)/shard_map/ppermute | solution.py:287
  82.8 9.5 %collective-permute-start.15 = (bf16[128,1536]{1,0:T(8,128)(2,1)S(1)}, bf16[128,1536]{1,0:T(8,128)(2,1)S(1)}, u32[]{:S(2)}, u32[]{:S(2)}) collective-permute-start(bf16[128,1536]{1,0:T(8,128)(2,1)S(1)} %pad_maximum_fusion), channel_id=1, source_target_pairs={{0,4},{4,8},{8,12},{12,14},{14,10},{10,6},{6,2},{2,0},{1,5},{5,9},... | collective-permute-start | bytes 1179656 | tf_op jit(solution)/shard_map/ppermute | solution.py:296
  89.8 10.4 %collective-permute-start.19 = (bf16[128,1536]{1,0:T(8,128)(2,1)S(1)}, bf16[128,1536]{1,0:T(8,128)(2,1)S(1)}, u32[]{:S(2)}, u32[]{:S(2)}) collective-permute-start(bf16[128,1536]{1,0:T(8,128)(2,1)S(1)} %pad_maximum_fusion.1), channel_id=1, source_target_pairs={{4,0},{8,4},{12,8},{14,12},{10,14},{6,10},{2,6},{0,2},{5,1},{9,5},... | collective-permute-start | bytes 1179656 | tf_op jit(solution)/shard_map/ppermute | solution.py:296
  92.4 10.3 %collective-permute-start.16 = (bf16[128,1536]{1,0:T(8,128)(2,1)S(1)}, bf16[128,1536]{1,0:T(8,128)(2,1)S(1)}, u32[]{:S(2)}, u32[]{:S(2)}) collective-permute-start(bf16[128,1536]{1,0:T(8,128)(2,1)S(1)} %add_convert_fusion.4), channel_id=1, source_target_pairs={{0,4},{4,8},{8,12},{12,14},{14,10},{10,6},{6,2},{2,0},{1,5},{5,9},... | collective-permute-start | bytes 1179656 | tf_op jit(solution)/shard_map/ppermute | solution.py:296
  100.3 11.3 %collective-permute-start.20 = (bf16[128,1536]{1,0:T(8,128)(2,1)S(1)}, bf16[128,1536]{1,0:T(8,128)(2,1)S(1)}, u32[]{:S(2)}, u32[]{:S(2)}) collective-permute-start(bf16[128,1536]{1,0:T(8,128)(2,1)S(1)} %add_convert_fusion.2), channel_id=1, source_target_pairs={{4,0},{8,4},{12,8},{14,12},{10,14},{6,10},{2,6},{0,2},{5,1},{9,5},... | collective-permute-start | bytes 1179656 | tf_op jit(solution)/shard_map/ppermute | solution.py:296
  102.8 14.6 %collective-permute-start.17 = (bf16[128,1536]{1,0:T(8,128)(2,1)S(1)}, bf16[128,1536]{1,0:T(8,128)(2,1)S(1)}, u32[]{:S(2)}, u32[]{:S(2)}) collective-permute-start(bf16[128,1536]{1,0:T(8,128)(2,1)S(1)} %add_convert_fusion.3), channel_id=1, source_target_pairs={{0,4},{4,8},{8,12},{12,14},{14,10},{10,6},{6,2},{2,0},{1,5},{5,9},... | collective-permute-start | bytes 1179656 | tf_op jit(solution)/shard_map/ppermute | solution.py:296
  111.6 7.8 %collective-permute-start.21 = (bf16[128,1536]{1,0:T(8,128)(2,1)S(1)}, bf16[128,1536]{1,0:T(8,128)(2,1)S(1)}, u32[]{:S(2)}, u32[]{:S(2)}) collective-permute-start(bf16[128,1536]{1,0:T(8,128)(2,1)S(1)} %add_convert_fusion.1), channel_id=1, source_target_pairs={{4,0},{8,4},{12,8},{14,12},{10,14},{6,10},{2,6},{0,2},{5,1},{9,5},... | collective-permute-start | bytes 1179656 | tf_op jit(solution)/shard_map/ppermute | solution.py:296

commit v3 on v2

--- a/solution.py
+++ b/solution.py
@@ -15,13 +15,20 @@
 LANES = 128
 SNAKES = {8: (0, 2, 4, 6, 7, 5, 3, 1)}
 MIB = 1 << 20
-EXPERT_VMEM = 16 * MIB
+EXPERT_VMEM = 8 * MIB
 
 
 def shifted(value, axis, by):
     peers = lax.axis_size(axis)
-    pairs = [(i, i + by) for i in range(peers) if 0 <= i + by < peers]
-    return lax.ppermute(value, axis, pairs)
+    return lax.ppermute(value, axis, [(i, (i + by) % peers) for i in range(peers)])
+
+
+def pinned(values, space):
+    return [pltpu.with_memory_space_constraint(value, space) for value in values]
+
+
+def tied(value, *after):
+    return lax.optimization_barrier((value,) + after)[0]
 
 
 def swapped(value, axis, bit=1):
@@ -33,126 +40,123 @@
     return jnp.dot(a, b, preferred_element_type=jnp.float32)
 
 
-def attend_kernel(
-    group_pairs, first_ref, sink_ref, q_ref, kp_ref, kc_ref, vp_ref, vc_ref, ow_ref, *rest
-):
-    mix = len(rest) > 2
+def attend_kernel(half, mix, first_ref, sink_hbm, q_hbm, k_hbm, v_hbm, ow_hbm, *rest):
     if mix:
-        rank_ref, other_ref, send_ref, own_ref, total = rest
+        k_before, v_before, rank_ref, other_ref, send_ref, own_ref = rest[:6]
     else:
-        out_ref, total = rest
-    step = pl.program_id(0)
-    rows = q_ref.shape[0]
-    keys = kp_ref.shape[0] + kc_ref.shape[0]
-    pairs_step = q_ref.shape[1] // LANES
-    group = (step * pairs_step) // group_pairs
-
-    lane_k = lax.broadcasted_iota(jnp.int32, (keys, LANES), 1)
-    low = lane_k < HEAD_DIM
-    k = jnp.concatenate([kp_ref[...], kc_ref[...]], axis=0).astype(jnp.float32)
-    v = jnp.concatenate([vp_ref[...], vc_ref[...]], axis=0).astype(jnp.float32)
-    k_low = jnp.where(low, jnp.where(group == 0, k, pltpu.roll(k, HEAD_DIM, 1)), 0.0)
-    v_low = jnp.where(low, jnp.where(group == 0, v, pltpu.roll(v, HEAD_DIM, 1)), 0.0)
-    k_high, v_high = pltpu.roll(k_low, HEAD_DIM, 1), pltpu.roll(v_low, HEAD_DIM, 1)
-    kk = jnp.concatenate([k_low, k_high], axis=0).astype(jnp.bfloat16)
+        out_ref = rest[0]
+    sink_ref, q_ref, k_ref, v_ref, ow_ref, done_ref, sems = rest[-7:]
+    rows, keys = q_ref.shape[0], 2 * q_ref.shape[0]
+    pairs = q_ref.shape[1] // LANES
+    groups = k_ref.shape[1] // HEAD_DIM
+    spans = (pl.ds(half * rows, rows), pl.ds(0, k_ref.shape[0]))
+    copies = [
+        pltpu.make_async_copy(k_hbm.at[spans[1]], k_ref, sems.at[0]),
+        pltpu.make_async_copy(v_hbm.at[spans[1]], v_ref, sems.at[1]),
+        pltpu.make_async_copy(q_hbm.at[spans[0]], q_ref, sems.at[2]),
+        pltpu.make_async_copy(sink_hbm, sink_ref, sems.at[3]),
+        pltpu.make_async_copy(ow_hbm, ow_ref, sems.at[4]),
+    ]
+    for copy in copies:
+        copy.start()
+    for copy in copies[:4]:
+        copy.wait()
+
+    low = lax.broadcasted_iota(jnp.int32, (keys, LANES), 1) < HEAD_DIM
+    k, v = k_ref[...], v_ref[...]
+    if mix:
+        k = jnp.concatenate([k_before[rows:], k], axis=0)
+        v = jnp.concatenate([v_before[rows:], v], axis=0)
+    k = k.astype(jnp.float32) * (1.0 / math.sqrt(HEAD_DIM))
+    v = v.astype(jnp.float32)
+    k_turned, v_turned = pltpu.roll(k, HEAD_DIM, 1), pltpu.roll(v, HEAD_DIM, 1)
     one_low = jnp.where(low, 1.0, 0.0)
-    vv = jnp.concatenate(
-        [
-            jnp.concatenate([v_low, one_low], axis=1),
-            jnp.concatenate([v_high, 1.0 - one_low], axis=1),
-        ],
-        axis=0,
-    ).astype(jnp.bfloat16)
 
     row = lax.broadcasted_iota(jnp.int32, (rows, keys), 0)
     column = lax.broadcasted_iota(jnp.int32, (rows, keys), 1)
-    least = jnp.where(first_ref[0] == 1, WINDOW, 0)
-    allowed = (column <= row + WINDOW) & (column > row) & (column >= least)
+    allowed = (column <= row + rows) & (column > row)
+    if mix:
+        allowed = allowed & (column >= jnp.where(first_ref[0] == 1, rows, 0))
     low_out = lax.broadcasted_iota(jnp.int32, (rows, LANES), 1) < HEAD_DIM
-    scale = 1.0 / math.sqrt(HEAD_DIM)
-
-    done = []
-    for pair in range(pairs_step):
-        q = q_ref[:, pair * LANES : (pair + 1) * LANES]
-        scores = lax.dot_general(
-            q, kk, (((1,), (1,)), ((), ())), preferred_element_type=jnp.float32
-        )
-        weights, sinks = [], []
-        for side in range(2):
-            part = jnp.where(allowed, scores[:, side * keys : (side + 1) * keys] * scale, -jnp.inf)
-            sink = sink_ref[(step * pairs_step + pair) * 2 + side]
-            highest = jnp.maximum(jnp.max(part, axis=1, keepdims=True), sink)
-            weights.append(jnp.exp(part - highest).astype(jnp.bfloat16))
-            sinks.append(jnp.exp(sink - highest))
-        both = mm(jnp.concatenate(weights, axis=1), vv)
-        below = both[:, LANES:] + jnp.where(low_out, sinks[0], sinks[1])
-        done.append((both[:, :LANES] / below).astype(jnp.bfloat16))
-    part = mm(jnp.concatenate(done, axis=1), ow_ref[...])
-
-    @pl.when(step == 0)
-    def _():
-        total[...] = part
-
-    @pl.when(step > 0)
-    def _():
-        total[...] += part
-
-    @pl.when(step == pl.num_programs(0) - 1)
-    def _():
+
+    for group in range(groups):
+        here, there = (k, v), (k_turned, v_turned)
+        lows, highs = (here, there) if group == 0 else (there, here)
+        kk = jnp.concatenate(
+            [jnp.where(low, lows[0], 0.0), jnp.where(low, 0.0, highs[0])], axis=0
+        ).astype(jnp.bfloat16)
+        vv = jnp.concatenate(
+            [
+                jnp.concatenate([jnp.where(low, lows[1], 0.0), one_low], axis=1),
+                jnp.concatenate([jnp.where(low, 0.0, highs[1]), 1.0 - one_low], axis=1),
+            ],
+            axis=0,
+        ).astype(jnp.bfloat16)
+        for pair in range(group * pairs // groups, (group + 1) * pairs // groups):
+            lanes = slice(pair * LANES, (pair + 1) * LANES)
+            scores = lax.dot_general(
+                q_ref[:, lanes], kk, (((1,), (1,)), ((), ())), preferred_element_type=jnp.float32
+            )
+            weights, sinks = [], []
+            for side in range(2):
+                part = jnp.where(allowed, scores[:, side * keys : (side + 1) * keys], -jnp.inf)
+                sink = sink_ref[:, 2 * pair + side : 2 * pair + side + 1]
+                highest = jnp.maximum(jnp.max(part, axis=1, keepdims=True), sink)
+                weights.append(jnp.exp(part - highest).astype(jnp.bfloat16))
+                sinks.append(jnp.exp(sink - highest))
+            both = mm(jnp.concatenate(weights, axis=1), vv)
+            below = both[:, LANES:] + jnp.where(low_out, sinks[0], sinks[1])
+            done_ref[:, lanes] = (both[:, :LANES] / below).astype(jnp.bfloat16)
+
+    copies[4].wait()
+    model = ow_ref.shape[1]
+    width = 512 if model % 512 == 0 else model
+    if mix:
+        own_first = rank_ref[0] == 0
+    for start in range(0, model, width):
+        lanes = slice(start, start + width)
+        mine = mm(done_ref[...], ow_ref[:, lanes])
         if mix:
-            mine = total[...]
-            other = other_ref[...]
-            own_first = rank_ref[0] == 0
-            own_ref[...] = jnp.where(own_first, mine, other)
-            send_ref[...] = jnp.where(own_first, other, mine).astype(jnp.bfloat16)
+            other = other_ref[:, lanes]
+            own_ref[:, lanes] = jnp.where(own_first, mine, other)
+            send_ref[:, lanes] = jnp.where(own_first, other, mine).astype(jnp.bfloat16)
         else:
-            out_ref[...] = total[...]
-
-
-def attend(half, first, sinks, queries, keys, values, out_weight, rank=None, other=None):
-    (k_prev, kp_index), (k_cur, kc_index) = keys
-    (v_prev, vp_index), (v_cur, vc_index) = values
+            out_ref[:, lanes] = mine
+
+
+def attend(half, first, sinks, queries, keys, values, out_weight, before=(), rank=None, other=None):
+    mix = bool(before)
     rows, width, model = WINDOW, queries.shape[1], out_weight.shape[1]
-    block = min(width, 256)
-    group_pairs = width // LANES // (k_cur.shape[1] // HEAD_DIM)
+    local = rows if mix else 2 * rows
     smem = pl.BlockSpec(memory_space=pltpu.SMEM)
-
-    def fixed(index):
-        return pl.BlockSpec((rows, LANES), lambda i: (index, 0))
-
-    in_specs = [
-        smem,
-        smem,
-        pl.BlockSpec((rows, block), lambda i: (half, i)),
-        fixed(kp_index),
-        fixed(kc_index),
-        fixed(vp_index),
-        fixed(vc_index),
-        pl.BlockSpec((block, model), lambda i: (i, 0)),
-    ]
-    operands = [first, sinks, queries, k_prev, k_cur, v_prev, v_cur, out_weight]
-    whole = pl.BlockSpec((rows, model), lambda i: (0, 0))
+    vmem = pl.BlockSpec(memory_space=pltpu.VMEM)
+    hbm = pl.BlockSpec(memory_space=pltpu.HBM)
     wide = jax.ShapeDtypeStruct((rows, model), jnp.float32)
     narrow = jax.ShapeDtypeStruct((rows, model), jnp.bfloat16)
-    if rank is None:
-        out_shape, out_specs = wide, whole
-    else:
-        in_specs += [smem, whole]
-        operands += [rank, other]
-        out_shape, out_specs = (narrow, wide), (whole, whole)
     return pl.pallas_call(
-        functools.partial(attend_kernel, group_pairs),
-        grid=(width // block,),
-        in_specs=in_specs,
-        out_specs=out_specs,
-        out_shape=out_shape,
-        scratch_shapes=[pltpu.VMEM((rows, model), jnp.float32)],
-        compiler_params=pltpu.CompilerParams(vmem_limit_bytes=48 * MIB),
+        functools.partial(attend_kernel, half, mix),
+        in_specs=[smem] + [hbm] * 5 + ([vmem, vmem, smem, vmem] if mix else []),
+        out_specs=(vmem, vmem) if mix else vmem,
+        out_shape=(narrow, wide) if mix else wide,
+        scratch_shapes=[
+            pltpu.VMEM((1, sinks.shape[0]), jnp.float32),
+            pltpu.VMEM((rows, width), jnp.bfloat16),
+            pltpu.VMEM((local, LANES), jnp.bfloat16),
+            pltpu.VMEM((local, LANES), jnp.bfloat16),
+            pltpu.VMEM((width, model), jnp.bfloat16),
+            pltpu.VMEM((rows, width), jnp.bfloat16),
+            pltpu.SemaphoreType.DMA((5,)),
+        ],
+        compiler_params=pltpu.CompilerParams(vmem_limit_bytes=8 * MIB),
         cost_estimate=pl.CostEstimate(
             flops=2 * rows * width * (model + 1024), bytes_accessed=6 * MIB, transcendentals=0
         ),
         name="attend",
-    )(*operands)
+    )(
+        first,
+        *pinned((sinks.reshape(1, -1), queries, keys, values, out_weight), pltpu.HBM),
+        *((*before, rank, other) if mix else ()),
+    )
 
 
 def norm_kernel(
@@ -191,7 +195,7 @@
             jax.ShapeDtypeStruct((rows, model), jnp.bfloat16),
             jax.ShapeDtypeStruct((rows, model + extra), jnp.bfloat16),
         ],
-        compiler_params=pltpu.CompilerParams(vmem_limit_bytes=16 * MIB),
+        compiler_params=pltpu.CompilerParams(vmem_limit_bytes=8 * MIB),
         cost_estimate=pl.CostEstimate(
             flops=8 * rows * model, bytes_accessed=14 * rows * model, transcendentals=rows
         ),
@@ -201,35 +205,34 @@
 
 def expert_kernel(tile, expert_count, count, me_ref, *refs):
     x_refs, halves = refs[:count], refs[count : count + 6]
-    out_refs, (x, total) = refs[count + 6 : 2 * count + 6], refs[2 * count + 6 :]
-    model = halves[0].shape[0]
+    out_refs, (x, hidden) = refs[count + 6 : 2 * count + 6], refs[2 * count + 6 :]
+    model, half = halves[0].shape
     starts = [0]
     for ref in x_refs:
         starts.append(starts[-1] + ref.shape[0])
     for start, ref in zip(starts, x_refs):
         x[start : start + ref.shape[0]] = ref[:, :model]
-    total[...] = jnp.zeros_like(total)
-
-    @pl.loop(0, halves[0].shape[1] // tile)
-    def _(index):
-        span = pl.ds(pl.multiple_of(index * tile, tile), tile)
-        rows = x[...]
-        parts = []
-        for gate_ref, up_ref, down_ref in (halves[:3], halves[3:]):
-            gate_pre = mm(rows, gate_ref[:, span])
-            up_pre = mm(rows, up_ref[:, span])
+
+    for at in range(0, half, tile):
+        for side in range(2):
+            gate_ref, up_ref = halves[3 * side : 3 * side + 2]
+            gate_pre = mm(x[...], gate_ref[:, at : at + tile])
+            up_pre = mm(x[...], up_ref[:, at : at + tile])
             activated = gate_pre * jax.nn.sigmoid(1.702 * gate_pre) * (up_pre + 1.0)
-            parts.append(mm(activated.astype(jnp.bfloat16), down_ref[span, :]))
-        total[...] += parts[0] + parts[1]
+            hidden[:, side * half + at : side * half + at + tile] = activated.astype(jnp.bfloat16)
 
     me = me_ref[0]
-    for start, ref, out_ref in zip(starts, x_refs, out_refs):
-        rows = ref.shape[0]
+    scales = []
+    for ref in x_refs:
         sent = ref[:, model:].astype(jnp.float32)
         lane = lax.broadcasted_iota(jnp.int32, sent.shape, 1)
         mine = (lane == me) | (lane == me + expert_count)
-        scale = jnp.sum(jnp.where(mine, sent, 0.0), axis=1, keepdims=True)
-        out_ref[...] = (total[start : start + rows] * scale).astype(jnp.bfloat16)
+        scales.append(jnp.sum(jnp.where(mine, sent, 0.0), axis=1, keepdims=True))
+    for at in range(0, model, tile):
+        lanes = slice(at, at + tile)
+        total = mm(hidden[:, :half], halves[2][:, lanes]) + mm(hidden[:, half:], halves[5][:, lanes])
+        for start, ref, scale in zip(starts, out_refs, scales):
+            ref[:, lanes] = (total[start : start + ref.shape[0]] * scale).astype(jnp.bfloat16)
 
 
 def experts(blocks, me, halves, expert_count):
@@ -243,14 +246,14 @@
         out_shape=[jax.ShapeDtypeStruct((b.shape[0], model), jnp.bfloat16) for b in blocks],
         scratch_shapes=[
             pltpu.VMEM((rows, model), jnp.bfloat16),
-            pltpu.VMEM((rows, model), jnp.float32),
+            pltpu.VMEM((rows, 2 * half), jnp.bfloat16),
         ],
         compiler_params=pltpu.CompilerParams(vmem_limit_bytes=EXPERT_VMEM),
         cost_estimate=pl.CostEstimate(
             flops=12 * rows * model * half, bytes_accessed=6 * rows * model, transcendentals=0
         ),
         name="experts",
-    )(me, *blocks, *halves)
+    )(me, *blocks, *pinned(halves, pltpu.VMEM))
 
 
 def ring_experts(residual, message, gate_weight, up_weight, down_weight, others):
@@ -269,15 +272,21 @@
 
     came = [[message], [message]]
     given = [[None], [None]]
+    (mine,) = apply(message)
+    worked = [mine]
     for distance in range(1, far + 1):
         for side in range(2):
             block = came[side][distance - 1]
             if distance == far:
                 block = block[spans[side]]
+            if distance > 1:
+                block = tied(block, worked[distance - 2])
             came[side].append(lax.ppermute(block, "seq", hops[side]))
-    (mine,) = apply(message)
-    for distance in range(1, far + 1):
-        outs = apply(came[0][distance], came[1][distance])
+        if distance < far:
+            outs = apply(came[0][distance], came[1][distance])
+        else:
+            outs = apply(tied(came[0][far], worked[far - 1]), came[1][far])
+        worked.append(outs[0])
         given[0].append(outs[0])
         given[1].append(outs[1])
 
@@ -364,32 +373,15 @@
         others = [swapped(w, "rep") for w in (gate_weight, up_weight, down_weight)]
     never = jnp.zeros((1,), jnp.int32)
     first = (seq == 0).astype(jnp.int32).reshape(1)
-    last = block_len // WINDOW - 1
-    later_half = attend(
-        1,
-        never,
-        sink_logits,
-        queries,
-        ((key_rows, 0), (key_rows, 1)),
-        ((value_rows, 0), (value_rows, 1)),
-        out_weight,
-    )
-    send, own = attend(
-        0,
-        first,
-        sink_logits,
-        queries,
-        ((k_before, last), (key_rows, 0)),
-        ((v_before, last), (value_rows, 0)),
-        out_weight,
-        rank,
-        later_half,
-    )
+    shared = (sink_logits, queries, key_rows, value_rows, out_weight)
+    later_half = attend(1, never, *shared)
+    send, own = attend(0, first, *shared, (k_before, v_before), rank, later_half)
     came = swapped(send, "rep")
     expert_count = lax.axis_size("seq") * EXP_DEV if use_ring else 0
     residual, message = norm(
-        stream, own, came, norm_gain, expert_ids, route_weights, expert_count, others
-    )
+        stream, own, came, norm_gain, expert_ids, route_weights, expert_count, []
+    )
+    message, *others = lax.optimization_barrier((message, *others))
     if use_ring:
         return ring_experts(residual, message, gate_weight, up_weight, down_weight, others)
     return dispatched_experts(

time: 121 us -> 103 us (0.85)
  local copies, waits for them, and re-layouts: 5.38 us -> 0.09 us
  starting transfers between devices: 25.6 us -> 21.1 us
  Pallas kernels: 41.6 us -> 37.2 us
  waiting for transfers between devices: 46 us -> 43 us
    ppermute x8, waiting for transfers between devices: 19.8 us -> 9.93 us  [ring_experts(): came[side].append(lax.ppermute(block, 'seq', hops[side]))]
    ppermute x6, waiting for transfers between devices: 19.2 us -> 24.9 us  [ring_experts(): moving = lax.ppermute(value, 'seq', hops[side])]
    unnamed x32 -> x14, local copies, waits for them, and re-layouts: 5.32 us -> 0.03 us
    pallas_call x5, Pallas kernels: 32 us -> 27.7 us  [experts(): pl.pallas_call(functools.partial(expert_kernel, min(256, half), expert_co...]
    ppermute x2, starting transfers between devices: 7.84 us -> 4.04 us  [shifted(): lax.ppermute(value, axis, [(i, (i + by) % peers) for i in range(peers)])]
    ppermute x2, waiting for transfers between devices: 0.01 us -> 1.24 us  [shifted(): lax.ppermute(value, axis, [(i, (i + by) % peers) for i in range(peers)])]
  transfers between devices with their start and end apart: 22 -> 22, of which waited for: 10 -> 13; matrix products, arithmetic and copies ran while one was open for 0% -> 1% of each run, Pallas kernels for 30% -> 32%
where the time goes in v3:
time: 103 us
  waiting for transfers between devices  43 us (42%)
  Pallas kernels  37.2 us (36%)
  starting transfers between devices  21.1 us (20%)
  other arithmetic  1.46 us (1%)
    pallas_call x5, Pallas kernels, experts(): pl.pallas_call(functools.partial(expert_kernel, min(256, half), expert_co...  27.7 us
    ppermute x6, waiting for transfers between devices, ring_experts(): moving = lax.ppermute(value, 'seq', hops[side])  24.9 us
    ppermute x8, waiting for transfers between devices, ring_experts(): came[side].append(lax.ppermute(block, 'seq', hops[side]))  9.93 us
    pallas_call x2, Pallas kernels, attend(): pl.pallas_call(functools.partial(attend_kernel, half, mix), in_specs=[sme...  9.22 us
    ppermute x8, starting transfers between devices, ring_experts(): came[side].append(lax.ppermute(block, 'seq', hops[side]))  8.26 us
    ppermute x6, starting transfers between devices, ring_experts(): moving = lax.ppermute(value, 'seq', hops[side])  5.61 us
    ppermute x2, waiting for transfers between devices, ring_experts(): moving = lax.ppermute(given[side][far], 'seq', hops[side])  5.33 us
    ppermute x2, starting transfers between devices, shifted(): lax.ppermute(value, axis, [(i, (i + by) % peers) for i in range(peers)])  4.04 us
  transfers between devices with their start and end apart: 22, of which 13 were waited for; matrix products, arithmetic and copies ran while one was open for 1% of the time, Pallas kernels for 32%

profile of v3, /device:TPU:0, one launch (start us, length us, event | category | flops | bytes accessed | tf_op | source)
XLA Modules:
  0.0 103.1 jit_solution(895225048177796866)
XLA Ops:
  0.0 0.5 collective-permute-start.3
  0.5 0.1 collective-permute-start.4
  0.5 0.5 collective-permute-start.5
  1.0 2.5 %collective-permute-start = (bf16[256,128]{1,0:T(8,128)(2,1)}, bf16[256,128]{1,0:T(8,128)(2,1)S(1)}, u32[]{:S(2)}, u32[]{:S(2)}) collective-permute-start(bf16[256,128]{1,0:T(8,128)(2,1)} %k_hbm.3), channel_id=1, source_target_pairs={{0,2},{2,4},{4,6},{6,8},{8,10},{10,12},{12,14},{14,0},{1,3},{3,5},... | collective-permute-start | bytes 196616 | tf_op jit(solution)/shard_map/ppermute | solution.py:23
  3.5 1.5 %collective-permute-start.1 = (bf16[256,128]{1,0:T(8,128)(2,1)}, bf16[256,128]{1,0:T(8,128)(2,1)S(1)}, u32[]{:S(2)}, u32[]{:S(2)}) collective-permute-start(bf16[256,128]{1,0:T(8,128)(2,1)} %v_hbm.3), channel_id=1, source_target_pairs={{0,2},{2,4},{4,6},{6,8},{8,10},{10,12},{12,14},{14,0},{1,3},{3,5},... | collective-permute-start | bytes 196616 | tf_op jit(solution)/shard_map/ppermute | solution.py:23
  5.0 4.6 %attend.2.rest_3_ = f32[128,1536]{1,0:T(8,128)S(1)} custom-call(s32[1]{0:T(128)} %constant.11.clone.1.first_ref, f32[1,16]{1,0:T(1,128)} %bitcast.29, bf16[256,1024]{1,0:T(8,128)(2,1)} %q_hbm.3, bf16[256,128]{1,0:T(8,128)(2,1)} %k_hbm.3, bf16[256,128]{1,0:T(8,128)(2,1)} %v_hbm.3, bf16[1024,1536]{1,0:T(8,128)(2,1)} %ow_hbm.3), custom_call_target="tpu_custom_call" | custom-call | flops 671088640 | bytes 6291456 | tf_op jit(solution)/shard_map/attend/pallas_call | solution.py:136
  9.6 1.2 %collective-permute-done.1.rest_1_ = bf16[256,128]{1,0:T(8,128)(2,1)S(1)} collective-permute-done((bf16[256,128]{1,0:T(8,128)(2,1)}, bf16[256,128]{1,0:T(8,128)(2,1)S(1)}, u32[]{:S(2)}, u32[]{:S(2)}) %collective-permute-start.1) | collective-permute-done | bytes 65568 | tf_op jit(solution)/shard_map/ppermute | solution.py:23
  10.9 4.6 %attend.3 = (bf16[128,1536]{1,0:T(8,128)(2,1)S(1)}, f32[128,1536]{1,0:T(8,128)S(1)}) custom-call(s32[1]{0:T(128)} %bitcast.first_ref, f32[1,16]{1,0:T(1,128)} %bitcast.30, bf16[256,1024]{1,0:T(8,128)(2,1)} %q_hbm.3, bf16[256,128]{1,0:T(8,128)(2,1)} %k_hbm.3, bf16[256,128]{1,0:T(8,128)(2,1)} %v_hbm.3, bf16[1024,1536]{1,0:T(8,128)(2,1)} %ow_hbm.3, ...), custom_call_target="tpu_custom_call" | custom-call | flops 671088640 | bytes 6291456 | tf_op jit(solution)/shard_map/attend/pallas_call | solution.py:136
  15.5 0.1 collective-permute-start.2
  15.6 1.7 %collective-permute-done.2.came_ref = bf16[128,1536]{1,0:T(8,128)(2,1)S(1)} collective-permute-done((bf16[128,1536]{1,0:T(8,128)(2,1)S(1)}, bf16[128,1536]{1,0:T(8,128)(2,1)S(1)}, u32[]{:S(2)}, u32[]{:S(2)}) %collective-permute-start.2) | collective-permute-done | bytes 393248 | tf_op jit(solution)/shard_map/ppermute | solution.py:36
  17.3 0.3 norm.1
  17.6 0.4 collective-permute-start.8
  18.0 1.7 %collective-permute-start.6 = (bf16[128,1664]{1,0:T(8,128)(2,1)S(1)}, bf16[128,1664]{1,0:T(8,128)(2,1)S(1)}, u32[]{:S(2)}, u32[]{:S(2)}) collective-permute-start(bf16[128,1664]{1,0:T(8,128)(2,1)S(1)} %get-tuple-element.32.refs_0_), channel_id=1, source_target_pairs={{0,4},{4,8},{8,12},{12,14},{14,10},{10,6},{6,2},{2,0},{1,5},{5,9},... | collective-permute-start | bytes 1277960 | tf_op jit(solution)/shard_map/ppermute | solution.py:284
  19.7 4.5 %experts.5 = bf16[128,1536]{1,0:T(8,128)(2,1)S(1)} custom-call(s32[1]{0:T(128)} %bitcast.5.me_ref, bf16[128,1664]{1,0:T(8,128)(2,1)S(1)} %get-tuple-element.32.refs_0_, bf16[1536,768]{1,0:T(8,128)(2,1)S(1)} %bitcast.10, bf16[1536,768]{1,0:T(8,128)(2,1)S(1)} %bitcast.16, bf16[768,1536]{1,0:T(8,128)(2,1)S(1)} %bitcast.22, ...), custom_call_target="tpu_custom_call" | custom-call | flops 1811939328 | bytes 1179648 | tf_op jit(solution)/shard_map/experts/pallas_call | solution.py:242
  24.2 5.3 %collective-permute-done.8.refs_1_ = bf16[128,1664]{1,0:T(8,128)(2,1)S(1)} collective-permute-done((bf16[128,1664]{1,0:T(8,128)(2,1)S(1)}, bf16[128,1664]{1,0:T(8,128)(2,1)S(1)}, u32[]{:S(2)}, u32[]{:S(2)}) %collective-permute-start.8) | collective-permute-done | bytes 426016 | tf_op jit(solution)/shard_map/ppermute | solution.py:284
  29.5 0.3 collective-permute-start.10
  29.9 1.7 %collective-permute-start.7 = (bf16[128,1664]{1,0:T(8,128)(2,1)S(1)}, bf16[128,1664]{1,0:T(8,128)(2,1)S(1)}, u32[]{:S(2)}, u32[]{:S(2)}) collective-permute-start(bf16[128,1664]{1,0:T(8,128)(2,1)S(1)} %collective-permute-done.6.refs_0_), channel_id=1, source_target_pairs={{0,4},{4,8},{8,12},{12,14},{14,10},{10,6},{6,2},{2,0},{1,5},{5,9},... | collective-permute-start | bytes 1277960 | tf_op jit(solution)/shard_map/ppermute | solution.py:284
  31.6 6.2 %experts.6 = (bf16[128,1536]{1,0:T(8,128)(2,1)S(1)}, bf16[128,1536]{1,0:T(8,128)(2,1)S(1)}) custom-call(s32[1]{0:T(128)} %bitcast.5.me_ref, bf16[128,1664]{1,0:T(8,128)(2,1)S(1)} %collective-permute-done.6.refs_0_, bf16[128,1664]{1,0:T(8,128)(2,1)S(1)} %collective-permute-done.8.refs_1_, bf16[1536,768]{1,0:T(8,128)(2,1)S(1)} %bitcast.11, ...), custom_call_target="tpu_custom_call" | custom-call | flops 3623878656 | bytes 2359296 | tf_op jit(solution)/shard_map/experts/pallas_call | solution.py:242
  37.8 2.8 %collective-permute-done.10.refs_1_ = bf16[128,1664]{1,0:T(8,128)(2,1)S(1)} collective-permute-done((bf16[128,1664]{1,0:T(8,128)(2,1)S(1)}, bf16[128,1664]{1,0:T(8,128)(2,1)S(1)}, u32[]{:S(2)}, u32[]{:S(2)}) %collective-permute-start.10) | collective-permute-done | bytes 426016 | tf_op jit(solution)/shard_map/ppermute | solution.py:284
  40.6 0.3 collective-permute-start.12
  40.9 1.7 %collective-permute-start.9 = (bf16[128,1664]{1,0:T(8,128)(2,1)S(1)}, bf16[128,1664]{1,0:T(8,128)(2,1)S(1)}, u32[]{:S(2)}, u32[]{:S(2)}) collective-permute-start(bf16[128,1664]{1,0:T(8,128)(2,1)S(1)} %collective-permute-done.7.refs_0_), channel_id=1, source_target_pairs={{0,4},{4,8},{8,12},{12,14},{14,10},{10,6},{6,2},{2,0},{1,5},{5,9},... | collective-permute-start | bytes 1277960 | tf_op jit(solution)/shard_map/ppermute | solution.py:284
  42.6 6.2 %experts.7 = (bf16[128,1536]{1,0:T(8,128)(2,1)S(1)}, bf16[128,1536]{1,0:T(8,128)(2,1)S(1)}) custom-call(s32[1]{0:T(128)} %bitcast.5.me_ref, bf16[128,1664]{1,0:T(8,128)(2,1)S(1)} %collective-permute-done.7.refs_0_, bf16[128,1664]{1,0:T(8,128)(2,1)S(1)} %collective-permute-done.10.refs_1_, bf16[1536,768]{1,0:T(8,128)(2,1)S(1)} %bitcast.12, ...), custom_call_target="tpu_custom_call" | custom-call | flops 3623878656 | bytes 2359296 | tf_op jit(solution)/shard_map/experts/pallas_call | solution.py:242
  48.8 1.8 %collective-permute-done.12.refs_1_ = bf16[128,1664]{1,0:T(8,128)(2,1)S(1)} collective-permute-done((bf16[128,1664]{1,0:T(8,128)(2,1)S(1)}, bf16[128,1664]{1,0:T(8,128)(2,1)S(1)}, u32[]{:S(2)}, u32[]{:S(2)}) %collective-permute-start.12) | collective-permute-done | bytes 426016 | tf_op jit(solution)/shard_map/ppermute | solution.py:284
  50.7 0.4 collective-permute-start.13
  51.1 1.8 %collective-permute-start.11 = (bf16[64,1664]{1,0:T(8,128)(2,1)S(1)}, bf16[64,1664]{1,0:T(8,128)(2,1)S(1)}, u32[]{:S(2)}, u32[]{:S(2)}) collective-permute-start(bf16[64,1664]{1,0:T(8,128)(2,1)S(1)} %slice.24), channel_id=1, source_target_pairs={{0,4},{4,8},{8,12},{12,14},{14,10},{10,6},{6,2},{2,0},{1,5},{5,9},... | collective-permute-start | bytes 638984 | tf_op jit(solution)/shard_map/ppermute | solution.py:284
  52.8 6.2 %experts.8 = (bf16[128,1536]{1,0:T(8,128)(2,1)S(1)}, bf16[128,1536]{1,0:T(8,128)(2,1)S(1)}) custom-call(s32[1]{0:T(128)} %bitcast.5.me_ref, bf16[128,1664]{1,0:T(8,128)(2,1)S(1)} %collective-permute-done.9.refs_0_, bf16[128,1664]{1,0:T(8,128)(2,1)S(1)} %collective-permute-done.12.refs_1_, bf16[1536,768]{1,0:T(8,128)(2,1)S(1)} %bitcast.13, ...), custom_call_target="tpu_custom_call" | custom-call | flops 3623878656 | bytes 2359296 | tf_op jit(solution)/shard_map/experts/pallas_call | solution.py:242
  59.1 4.5 %experts.9 = (bf16[64,1536]{1,0:T(8,128)(2,1)S(1)}, bf16[64,1536]{1,0:T(8,128)(2,1)S(1)}) custom-call(s32[1]{0:T(128)} %bitcast.5.me_ref, bf16[64,1664]{1,0:T(8,128)(2,1)S(1)} %collective-permute-done.11.refs_0_, bf16[64,1664]{1,0:T(8,128)(2,1)S(1)} %collective-permute-done.13.refs_1_, bf16[1536,768]{1,0:T(8,128)(2,1)S(1)} %bitcast.14, ...), custom_call_target="tpu_custom_call" | custom-call | flops 1811939328 | bytes 1179648 | tf_op jit(solution)/shard_map/experts/pallas_call | solution.py:242
  63.6 0.4 collective-permute-start.14
  64.1 1.7 %collective-permute-start.18 = (bf16[64,1536]{1,0:T(8,128)(2,1)S(1)}, bf16[64,1536]{1,0:T(8,128)(2,1)S(1)}, u32[]{:S(2)}, u32[]{:S(2)}) collective-permute-start(bf16[64,1536]{1,0:T(8,128)(2,1)S(1)} %get-tuple-element.50), channel_id=1, source_target_pairs={{4,0},{8,4},{12,8},{14,12},{10,14},{6,10},{2,6},{0,2},{5,1},{9,5},... | collective-permute-start | bytes 589832 | tf_op jit(solution)/shard_map/ppermute | solution.py:296
  65.8 5.1 %collective-permute-done.14 = bf16[64,1536]{1,0:T(8,128)(2,1)S(1)} collective-permute-done((bf16[64,1536]{1,0:T(8,128)(2,1)S(1)}, bf16[64,1536]{1,0:T(8,128)(2,1)S(1)}, u32[]{:S(2)}, u32[]{:S(2)}) %collective-permute-start.14) | collective-permute-done | bytes 196640 | tf_op jit(solution)/shard_map/ppermute | solution.py:296
  71.0 0.4 collective-permute-start.15
  71.4 0.2 collective-permute-done.18
  71.7 1.7 %collective-permute-start.19 = (bf16[128,1536]{1,0:T(8,128)(2,1)S(1)}, bf16[128,1536]{1,0:T(8,128)(2,1)S(1)}, u32[]{:S(2)}, u32[]{:S(2)}) collective-permute-start(bf16[128,1536]{1,0:T(8,128)(2,1)S(1)} %pad_maximum_fusion.1), channel_id=1, source_target_pairs={{4,0},{8,4},{12,8},{14,12},{10,14},{6,10},{2,6},{0,2},{5,1},{9,5},... | collective-permute-start | bytes 1179656 | tf_op jit(solution)/shard_map/ppermute | solution.py:305
  73.4 8.1 %collective-permute-done.15 = bf16[128,1536]{1,0:T(8,128)(2,1)S(1)} collective-permute-done((bf16[128,1536]{1,0:T(8,128)(2,1)S(1)}, bf16[128,1536]{1,0:T(8,128)(2,1)S(1)}, u32[]{:S(2)}, u32[]{:S(2)}) %collective-permute-start.15) | collective-permute-done | bytes 393248 | tf_op jit(solution)/shard_map/ppermute | solution.py:305
  81.5 0.1 add_convert_fusion.4
  81.6 0.4 collective-permute-start.16
  82.0 0.3 collective-permute-done.19
  82.3 0.1 add_convert_fusion.2
  82.4 1.5 %collective-permute-start.20 = (bf16[128,1536]{1,0:T(8,128)(2,1)S(1)}, bf16[128,1536]{1,0:T(8,128)(2,1)S(1)}, u32[]{:S(2)}, u32[]{:S(2)}) collective-permute-start(bf16[128,1536]{1,0:T(8,128)(2,1)S(1)} %add_convert_fusion.2), channel_id=1, source_target_pairs={{4,0},{8,4},{12,8},{14,12},{10,14},{6,10},{2,6},{0,2},{5,1},{9,5},... | collective-permute-start | bytes 1179656 | tf_op jit(solution)/shard_map/ppermute | solution.py:305
  83.9 9.3 %collective-permute-done.16 = bf16[128,1536]{1,0:T(8,128)(2,1)S(1)} collective-permute-done((bf16[128,1536]{1,0:T(8,128)(2,1)S(1)}, bf16[128,1536]{1,0:T(8,128)(2,1)S(1)}, u32[]{:S(2)}, u32[]{:S(2)}) %collective-permute-start.16) | collective-permute-done | bytes 393248 | tf_op jit(solution)/shard_map/ppermute | solution.py:305
  93.3 0.1 add_convert_fusion.3
  93.4 0.1 collective-permute-start.17
  93.5 0.7 collective-permute-done.20
  94.2 0.1 add_convert_fusion.1
  94.3 1.4 %collective-permute-start.21 = (bf16[128,1536]{1,0:T(8,128)(2,1)S(1)}, bf16[128,1536]{1,0:T(8,128)(2,1)S(1)}, u32[]{:S(2)}, u32[]{:S(2)}) collective-permute-start(bf16[128,1536]{1,0:T(8,128)(2,1)S(1)} %add_convert_fusion.1), channel_id=1, source_target_pairs={{4,0},{8,4},{12,8},{14,12},{10,14},{6,10},{2,6},{0,2},{5,1},{9,5},... | collective-permute-start | bytes 1179656 | tf_op jit(solution)/shard_map/ppermute | solution.py:305
  95.7 5.5 %collective-permute-done.17 = bf16[128,1536]{1,0:T(8,128)(2,1)S(1)} collective-permute-done((bf16[128,1536]{1,0:T(8,128)(2,1)S(1)}, bf16[128,1536]{1,0:T(8,128)(2,1)S(1)}, u32[]{:S(2)}, u32[]{:S(2)}) %collective-permute-start.17) | collective-permute-done | bytes 393248 | tf_op jit(solution)/shard_map/ppermute | solution.py:305
  101.2 0.9 collective-permute-done.21
  102.1 0.9 add_convert_fusion
  (32 shorter events, 0.3 us)
Async XLA Ops:
  0.0 17.6 %collective-permute-start.3 = (bf16[1536,768]{1,0:T(8,128)(2,1)}, bf16[1536,768]{1,0:T(8,128)(2,1)S(1)}, u32[]{:S(2)}, u32[]{:S(2)}) collective-permute-start(bf16[1536,768]{1,0:T(8,128)(2,1)} %bitcast.9), channel_id=1, source_target_pairs={{0,1},{1,0},{2,3},{3,2},{4,5},{5,4},{6,7},{7,6},{8,9},{9,8},{10,11... | collective-permute-start | bytes 7077896 | tf_op jit(solution)/shard_map/ppermute | solution.py:36
  0.5 17.2 %collective-permute-start.4 = (bf16[1536,768]{1,0:T(8,128)(2,1)}, bf16[1536,768]{1,0:T(8,128)(2,1)}, u32[]{:S(2)}, u32[]{:S(2)}) collective-permute-start(bf16[1536,768]{1,0:T(8,128)(2,1)} %bitcast.15), channel_id=1, source_target_pairs={{0,1},{1,0},{2,3},{3,2},{4,5},{5,4},{6,7},{7,6},{8,9},{9,8},{10,11... | collective-permute-start | bytes 7077896 | tf_op jit(solution)/shard_map/ppermute | solution.py:36
  0.5 17.1 %collective-permute-start.5 = (bf16[768,1536]{1,0:T(8,128)(2,1)}, bf16[768,1536]{1,0:T(8,128)(2,1)}, u32[]{:S(2)}, u32[]{:S(2)}) collective-permute-start(bf16[768,1536]{1,0:T(8,128)(2,1)} %bitcast.21), channel_id=1, source_target_pairs={{0,1},{1,0},{2,3},{3,2},{4,5},{5,4},{6,7},{7,6},{8,9},{9,8},{10,11... | collective-permute-start | bytes 7077896 | tf_op jit(solution)/shard_map/ppermute | solution.py:36
  1.0 8.7 %collective-permute-start = (bf16[256,128]{1,0:T(8,128)(2,1)}, bf16[256,128]{1,0:T(8,128)(2,1)S(1)}, u32[]{:S(2)}, u32[]{:S(2)}) collective-permute-start(bf16[256,128]{1,0:T(8,128)(2,1)} %k_hbm.3), channel_id=1, source_target_pairs={{0,2},{2,4},{4,6},{6,8},{8,10},{10,12},{12,14},{14,0},{1,3},{3,5},... | collective-permute-start | bytes 196616 | tf_op jit(solution)/shard_map/ppermute | solution.py:23
  3.5 7.4 %collective-permute-start.1 = (bf16[256,128]{1,0:T(8,128)(2,1)}, bf16[256,128]{1,0:T(8,128)(2,1)S(1)}, u32[]{:S(2)}, u32[]{:S(2)}) collective-permute-start(bf16[256,128]{1,0:T(8,128)(2,1)} %v_hbm.3), channel_id=1, source_target_pairs={{0,2},{2,4},{4,6},{6,8},{8,10},{10,12},{12,14},{14,0},{1,3},{3,5},... | collective-permute-start | bytes 196616 | tf_op jit(solution)/shard_map/ppermute | solution.py:23
  5.0 10.6 %copy-start.6 = (f32[1536]{0:T(1024)S(1)}, f32[1536]{0:T(1024)}, u32[]{:S(2)}) copy-start(f32[1536]{0:T(1024)} %param.18) | copy-start | bytes 18436
  5.0 12.3 %copy-start.3 = (bf16[128,1536]{1,0:T(8,128)(2,1)S(1)}, bf16[128,1536]{1,0:T(8,128)(2,1)}, u32[]{:S(2)}) copy-start(bf16[128,1536]{1,0:T(8,128)(2,1)} %stream_ref.1) | copy-start | bytes 1179652
  5.0 14.7 %copy-start.2 = (bf16[1,768,1536]{2,1,0:T(8,128)(2,1)S(1)}, bf16[1,768,1536]{2,1,0:T(8,128)(2,1)}, u32[]{:S(2)}) copy-start(bf16[1,768,1536]{2,1,0:T(8,128)(2,1)} %param.23) | copy-start | bytes 7077892
  10.9 6.4 %copy-start.4 = (s32[128,4]{0,1:T(4,128)S(1)}, s32[128,4]{0,1:T(4,128)}, u32[]{:S(2)}) copy-start(s32[128,4]{0,1:T(4,128)} %param.19) | copy-start | bytes 6148
  10.9 6.4 %copy-start.5 = (f32[128,4]{0,1:T(4,128)S(1)}, f32[128,4]{0,1:T(4,128)}, u32[]{:S(2)}) copy-start(f32[128,4]{0,1:T(4,128)} %param.20) | copy-start | bytes 6148
  10.9 8.8 %copy-start = (bf16[1,1536,768]{2,1,0:T(8,128)(2,1)S(1)}, bf16[1,1536,768]{2,1,0:T(8,128)(2,1)}, u32[]{:S(2)}) copy-start(bf16[1,1536,768]{2,1,0:T(8,128)(2,1)} %param.21) | copy-start | bytes 7077892
  10.9 8.8 %copy-start.1 = (bf16[1,1536,768]{2,1,0:T(8,128)(2,1)S(1)}, bf16[1,1536,768]{2,1,0:T(8,128)(2,1)}, u32[]{:S(2)}) copy-start(bf16[1,1536,768]{2,1,0:T(8,128)(2,1)} %param.22) | copy-start | bytes 7077892
  15.5 1.8 %collective-permute-start.2 = (bf16[128,1536]{1,0:T(8,128)(2,1)S(1)}, bf16[128,1536]{1,0:T(8,128)(2,1)S(1)}, u32[]{:S(2)}, u32[]{:S(2)}) collective-permute-start(bf16[128,1536]{1,0:T(8,128)(2,1)S(1)} %get-tuple-element.29), channel_id=1, source_target_pairs={{0,1},{1,0},{2,3},{3,2},{4,5},{5,4},{6,7},{7,6},{8,9},{9,8},{10,11... | collective-permute-start | bytes 1179656 | tf_op jit(solution)/shard_map/ppermute | solution.py:36
  17.6 11.9 %collective-permute-start.8 = (bf16[128,1664]{1,0:T(8,128)(2,1)S(1)}, bf16[128,1664]{1,0:T(8,128)(2,1)S(1)}, u32[]{:S(2)}, u32[]{:S(2)}) collective-permute-start(bf16[128,1664]{1,0:T(8,128)(2,1)S(1)} %get-tuple-element.32.refs_0_), channel_id=1, source_target_pairs={{4,0},{8,4},{12,8},{14,12},{10,14},{6,10},{2,6},{0,2},{5,1},{9,5},... | collective-permute-start | bytes 1277960 | tf_op jit(solution)/shard_map/ppermute | solution.py:284
  18.0 11.9 %collective-permute-start.6 = (bf16[128,1664]{1,0:T(8,128)(2,1)S(1)}, bf16[128,1664]{1,0:T(8,128)(2,1)S(1)}, u32[]{:S(2)}, u32[]{:S(2)}) collective-permute-start(bf16[128,1664]{1,0:T(8,128)(2,1)S(1)} %get-tuple-element.32.refs_0_), channel_id=1, source_target_pairs={{0,4},{4,8},{8,12},{12,14},{14,10},{10,6},{6,2},{2,0},{1,5},{5,9},... | collective-permute-start | bytes 1277960 | tf_op jit(solution)/shard_map/ppermute | solution.py:284
  29.5 11.0 %collective-permute-start.10 = (bf16[128,1664]{1,0:T(8,128)(2,1)S(1)}, bf16[128,1664]{1,0:T(8,128)(2,1)S(1)}, u32[]{:S(2)}, u32[]{:S(2)}) collective-permute-start(bf16[128,1664]{1,0:T(8,128)(2,1)S(1)} %collective-permute-done.8.refs_1_), channel_id=1, source_target_pairs={{4,0},{8,4},{12,8},{14,12},{10,14},{6,10},{2,6},{0,2},{5,1},{9,5},... | collective-permute-start | bytes 1277960 | tf_op jit(solution)/shard_map/ppermute | solution.py:284
  29.9 11.0 %collective-permute-start.7 = (bf16[128,1664]{1,0:T(8,128)(2,1)S(1)}, bf16[128,1664]{1,0:T(8,128)(2,1)S(1)}, u32[]{:S(2)}, u32[]{:S(2)}) collective-permute-start(bf16[128,1664]{1,0:T(8,128)(2,1)S(1)} %collective-permute-done.6.refs_0_), channel_id=1, source_target_pairs={{0,4},{4,8},{8,12},{12,14},{14,10},{10,6},{6,2},{2,0},{1,5},{5,9},... | collective-permute-start | bytes 1277960 | tf_op jit(solution)/shard_map/ppermute | solution.py:284
  40.6 10.1 %collective-permute-start.12 = (bf16[128,1664]{1,0:T(8,128)(2,1)S(1)}, bf16[128,1664]{1,0:T(8,128)(2,1)S(1)}, u32[]{:S(2)}, u32[]{:S(2)}) collective-permute-start(bf16[128,1664]{1,0:T(8,128)(2,1)S(1)} %collective-permute-done.10.refs_1_), channel_id=1, source_target_pairs={{4,0},{8,4},{12,8},{14,12},{10,14},{6,10},{2,6},{0,2},{5,1},{9,5},... | collective-permute-start | bytes 1277960 | tf_op jit(solution)/shard_map/ppermute | solution.py:284
  40.9 10.2 %collective-permute-start.9 = (bf16[128,1664]{1,0:T(8,128)(2,1)S(1)}, bf16[128,1664]{1,0:T(8,128)(2,1)S(1)}, u32[]{:S(2)}, u32[]{:S(2)}) collective-permute-start(bf16[128,1664]{1,0:T(8,128)(2,1)S(1)} %collective-permute-done.7.refs_0_), channel_id=1, source_target_pairs={{0,4},{4,8},{8,12},{12,14},{14,10},{10,6},{6,2},{2,0},{1,5},{5,9},... | collective-permute-start | bytes 1277960 | tf_op jit(solution)/shard_map/ppermute | solution.py:284
  50.7 8.4 %collective-permute-start.13 = (bf16[64,1664]{1,0:T(8,128)(2,1)S(1)}, bf16[64,1664]{1,0:T(8,128)(2,1)S(1)}, u32[]{:S(2)}, u32[]{:S(2)}) collective-permute-start(bf16[64,1664]{1,0:T(8,128)(2,1)S(1)} %slice.25), channel_id=1, source_target_pairs={{4,0},{8,4},{12,8},{14,12},{10,14},{6,10},{2,6},{0,2},{5,1},{9,5},... | collective-permute-start | bytes 638984 | tf_op jit(solution)/shard_map/ppermute | solution.py:284
  51.1 8.0 %collective-permute-start.11 = (bf16[64,1664]{1,0:T(8,128)(2,1)S(1)}, bf16[64,1664]{1,0:T(8,128)(2,1)S(1)}, u32[]{:S(2)}, u32[]{:S(2)}) collective-permute-start(bf16[64,1664]{1,0:T(8,128)(2,1)S(1)} %slice.24), channel_id=1, source_target_pairs={{0,4},{4,8},{8,12},{12,14},{14,10},{10,6},{6,2},{2,0},{1,5},{5,9},... | collective-permute-start | bytes 638984 | tf_op jit(solution)/shard_map/ppermute | solution.py:284
  63.6 7.3 %collective-permute-start.14 = (bf16[64,1536]{1,0:T(8,128)(2,1)S(1)}, bf16[64,1536]{1,0:T(8,128)(2,1)S(1)}, u32[]{:S(2)}, u32[]{:S(2)}) collective-permute-start(bf16[64,1536]{1,0:T(8,128)(2,1)S(1)} %get-tuple-element.46), channel_id=1, source_target_pairs={{0,4},{4,8},{8,12},{12,14},{14,10},{10,6},{6,2},{2,0},{1,5},{5,9},... | collective-permute-start | bytes 589832 | tf_op jit(solution)/shard_map/ppermute | solution.py:296
  64.1 7.6 %collective-permute-start.18 = (bf16[64,1536]{1,0:T(8,128)(2,1)S(1)}, bf16[64,1536]{1,0:T(8,128)(2,1)S(1)}, u32[]{:S(2)}, u32[]{:S(2)}) collective-permute-start(bf16[64,1536]{1,0:T(8,128)(2,1)S(1)} %get-tuple-element.50), channel_id=1, source_target_pairs={{4,0},{8,4},{12,8},{14,12},{10,14},{6,10},{2,6},{0,2},{5,1},{9,5},... | collective-permute-start | bytes 589832 | tf_op jit(solution)/shard_map/ppermute | solution.py:296
  71.0 10.5 %collective-permute-start.15 = (bf16[128,1536]{1,0:T(8,128)(2,1)S(1)}, bf16[128,1536]{1,0:T(8,128)(2,1)S(1)}, u32[]{:S(2)}, u32[]{:S(2)}) collective-permute-start(bf16[128,1536]{1,0:T(8,128)(2,1)S(1)} %pad_maximum_fusion), channel_id=1, source_target_pairs={{0,4},{4,8},{8,12},{12,14},{14,10},{10,6},{6,2},{2,0},{1,5},{5,9},... | collective-permute-start | bytes 1179656 | tf_op jit(solution)/shard_map/ppermute | solution.py:305
  71.7 10.6 %collective-permute-start.19 = (bf16[128,1536]{1,0:T(8,128)(2,1)S(1)}, bf16[128,1536]{1,0:T(8,128)(2,1)S(1)}, u32[]{:S(2)}, u32[]{:S(2)}) collective-permute-start(bf16[128,1536]{1,0:T(8,128)(2,1)S(1)} %pad_maximum_fusion.1), channel_id=1, source_target_pairs={{4,0},{8,4},{12,8},{14,12},{10,14},{6,10},{2,6},{0,2},{5,1},{9,5},... | collective-permute-start | bytes 1179656 | tf_op jit(solution)/shard_map/ppermute | solution.py:305
  81.6 11.7 %collective-permute-start.16 = (bf16[128,1536]{1,0:T(8,128)(2,1)S(1)}, bf16[128,1536]{1,0:T(8,128)(2,1)S(1)}, u32[]{:S(2)}, u32[]{:S(2)}) collective-permute-start(bf16[128,1536]{1,0:T(8,128)(2,1)S(1)} %add_convert_fusion.4), channel_id=1, source_target_pairs={{0,4},{4,8},{8,12},{12,14},{14,10},{10,6},{6,2},{2,0},{1,5},{5,9},... | collective-permute-start | bytes 1179656 | tf_op jit(solution)/shard_map/ppermute | solution.py:305
  82.4 11.8 %collective-permute-start.20 = (bf16[128,1536]{1,0:T(8,128)(2,1)S(1)}, bf16[128,1536]{1,0:T(8,128)(2,1)S(1)}, u32[]{:S(2)}, u32[]{:S(2)}) collective-permute-start(bf16[128,1536]{1,0:T(8,128)(2,1)S(1)} %add_convert_fusion.2), channel_id=1, source_target_pairs={{4,0},{8,4},{12,8},{14,12},{10,14},{6,10},{2,6},{0,2},{5,1},{9,5},... | collective-permute-start | bytes 1179656 | tf_op jit(solution)/shard_map/ppermute | solution.py:305
  93.4 7.8 %collective-permute-start.17 = (bf16[128,1536]{1,0:T(8,128)(2,1)S(1)}, bf16[128,1536]{1,0:T(8,128)(2,1)S(1)}, u32[]{:S(2)}, u32[]{:S(2)}) collective-permute-start(bf16[128,1536]{1,0:T(8,128)(2,1)S(1)} %add_convert_fusion.3), channel_id=1, source_target_pairs={{0,4},{4,8},{8,12},{12,14},{14,10},{10,6},{6,2},{2,0},{1,5},{5,9},... | collective-permute-start | bytes 1179656 | tf_op jit(solution)/shard_map/ppermute | solution.py:305
  94.3 7.8 %collective-permute-start.21 = (bf16[128,1536]{1,0:T(8,128)(2,1)S(1)}, bf16[128,1536]{1,0:T(8,128)(2,1)S(1)}, u32[]{:S(2)}, u32[]{:S(2)}) collective-permute-start(bf16[128,1536]{1,0:T(8,128)(2,1)S(1)} %add_convert_fusion.1), channel_id=1, source_target_pairs={{4,0},{8,4},{12,8},{14,12},{10,14},{6,10},{2,6},{0,2},{5,1},{9,5},... | collective-permute-start | bytes 1179656 | tf_op jit(solution)/shard_map/ppermute | solution.py:305

commit v4 on v3

--- a/solution.py
+++ b/solution.py
@@ -162,8 +162,9 @@
 def norm_kernel(
     expert_count, stream_ref, own_ref, came_ref, gain_ref, ids_ref, route_ref, *rest
 ):
-    residual_ref, message_ref = rest[-2:]
+    residual_ref, *message_refs = rest
     rows, model = stream_ref.shape
+    size = message_refs[0].shape[0]
     residual = (
         stream_ref[...].astype(jnp.float32) + own_ref[...] + came_ref[...].astype(jnp.float32)
     ).astype(jnp.bfloat16)
@@ -171,7 +172,8 @@
     wide = residual.astype(jnp.float32)
     mean = jnp.mean(wide * wide, axis=-1, keepdims=True)
     normed = (wide * lax.rsqrt(mean + 1e-05) * gain_ref[...]).astype(jnp.bfloat16)
-    message_ref[:, :model] = normed
+    for index, ref in enumerate(message_refs):
+        ref[:, :model] = normed[index * size : (index + 1) * size]
     if expert_count:
         expert = lax.broadcasted_iota(jnp.int32, (LANES, rows), 0)
         dense = jnp.zeros((LANES, rows), jnp.float32)
@@ -181,31 +183,42 @@
             dense += jnp.where(hit, route_ref[k : k + 1, :], 0.0)
         lead = dense.astype(jnp.bfloat16).astype(jnp.float32)
         both = jnp.where(expert < expert_count, lead, dense - lead)
-        message_ref[:, model:] = both.T.astype(jnp.bfloat16)
-
-
-def norm(stream, own, came, gain, expert_ids, route_weights, expert_count, after):
+        tail = both.T.astype(jnp.bfloat16)
+        for index, ref in enumerate(message_refs):
+            ref[:, model:] = tail[index * size : (index + 1) * size]
+
+
+def norm(stream, own, came, gain, expert_ids, route_weights, expert_count, pieces):
     rows, model = stream.shape
     vmem = pl.BlockSpec(memory_space=pltpu.VMEM)
-    extra = LANES if expert_count else 0
+    width = model + (LANES if expert_count else 0)
     return pl.pallas_call(
         functools.partial(norm_kernel, expert_count),
-        in_specs=[vmem] * 6 + [pl.BlockSpec(memory_space=pl.ANY)] * len(after),
-        out_shape=[
-            jax.ShapeDtypeStruct((rows, model), jnp.bfloat16),
-            jax.ShapeDtypeStruct((rows, model + extra), jnp.bfloat16),
-        ],
+        in_specs=[vmem] * 6,
+        out_shape=[jax.ShapeDtypeStruct((rows, model), jnp.bfloat16)]
+        + [jax.ShapeDtypeStruct((rows // pieces, width), jnp.bfloat16)] * pieces,
         compiler_params=pltpu.CompilerParams(vmem_limit_bytes=8 * MIB),
         cost_estimate=pl.CostEstimate(
             flops=8 * rows * model, bytes_accessed=14 * rows * model, transcendentals=rows
         ),
         name="norm",
-    )(stream, own, came, gain.reshape(1, model), expert_ids.T, route_weights.T, *after)
-
-
-def expert_kernel(tile, expert_count, count, me_ref, *refs):
+    )(stream, own, came, gain.reshape(1, model), expert_ids.T, route_weights.T)
+
+
+def expert_kernel(tile, expert_count, count, load, me_ref, *refs):
     x_refs, halves = refs[:count], refs[count : count + 6]
-    out_refs, (x, hidden) = refs[count + 6 : 2 * count + 6], refs[2 * count + 6 :]
+    out_refs, rest = refs[count + 6 : 2 * count + 6], refs[2 * count + 6 :]
+    copies = []
+    if load:
+        kept, rest = rest[:6], rest[6:]
+        copies = [
+            pltpu.make_async_copy(here, there, rest[2].at[index])
+            for index, (here, there) in enumerate(zip(halves, kept))
+        ]
+        for index in (0, 1, 3, 4, 2, 5):
+            copies[index].start()
+        halves = kept
+    x, hidden = rest[:2]
     model, half = halves[0].shape
     starts = [0]
     for ref in x_refs:
@@ -213,13 +226,23 @@
     for start, ref in zip(starts, x_refs):
         x[start : start + ref.shape[0]] = ref[:, :model]
 
-    for at in range(0, half, tile):
-        for side in range(2):
-            gate_ref, up_ref = halves[3 * side : 3 * side + 2]
-            gate_pre = mm(x[...], gate_ref[:, at : at + tile])
-            up_pre = mm(x[...], up_ref[:, at : at + tile])
-            activated = gate_pre * jax.nn.sigmoid(1.702 * gate_pre) * (up_pre + 1.0)
-            hidden[:, side * half + at : side * half + at + tile] = activated.astype(jnp.bfloat16)
+    def arrived(*which):
+        for index in which:
+            if copies:
+                copies[index].wait()
+
+    def work(side, at):
+        gate_ref, up_ref = halves[3 * side : 3 * side + 2]
+        gate_pre = mm(x[...], gate_ref[:, at : at + tile])
+        up_pre = mm(x[...], up_ref[:, at : at + tile])
+        activated = gate_pre * jax.nn.sigmoid(1.702 * gate_pre) * (up_pre + 1.0)
+        hidden[:, side * half + at : side * half + at + tile] = activated.astype(jnp.bfloat16)
+
+    for side in range(2):
+        arrived(3 * side, 3 * side + 1)
+        for at in range(0, half, tile):
+            work(side, at)
+    arrived(2, 5)
 
     me = me_ref[0]
     scales = []
@@ -235,76 +258,106 @@
             ref[:, lanes] = (total[start : start + ref.shape[0]] * scale).astype(jnp.bfloat16)
 
 
-def experts(blocks, me, halves, expert_count):
+def experts(blocks, me, halves, expert_count, load=False):
     model, half = halves[0].shape
     rows = sum(block.shape[0] for block in blocks)
     vmem = pl.BlockSpec(memory_space=pltpu.VMEM)
+    hbm = pl.BlockSpec(memory_space=pltpu.HBM)
+    kept = [jax.ShapeDtypeStruct(w.shape, w.dtype) for w in halves] if load else []
+    scratch = [
+        pltpu.VMEM((rows, model), jnp.bfloat16),
+        pltpu.VMEM((rows, 2 * half), jnp.bfloat16),
+    ]
     return pl.pallas_call(
-        functools.partial(expert_kernel, min(256, half), expert_count, len(blocks)),
-        in_specs=[pl.BlockSpec(memory_space=pltpu.SMEM)] + [vmem] * (len(blocks) + 6),
-        out_specs=[vmem] * len(blocks),
-        out_shape=[jax.ShapeDtypeStruct((b.shape[0], model), jnp.bfloat16) for b in blocks],
-        scratch_shapes=[
-            pltpu.VMEM((rows, model), jnp.bfloat16),
-            pltpu.VMEM((rows, 2 * half), jnp.bfloat16),
-        ],
+        functools.partial(expert_kernel, min(256, half), expert_count, len(blocks), load),
+        in_specs=[pl.BlockSpec(memory_space=pltpu.SMEM)]
+        + [vmem] * len(blocks)
+        + [hbm if load else vmem] * 6,
+        out_specs=[vmem] * (len(blocks) + len(kept)),
+        out_shape=[jax.ShapeDtypeStruct((b.shape[0], model), jnp.bfloat16) for b in blocks] + kept,
+        scratch_shapes=scratch + ([pltpu.SemaphoreType.DMA((6,))] if load else []),
         compiler_params=pltpu.CompilerParams(vmem_limit_bytes=EXPERT_VMEM),
         cost_estimate=pl.CostEstimate(
             flops=12 * rows * model * half, bytes_accessed=6 * rows * model, transcendentals=0
         ),
         name="experts",
-    )(me, *blocks, *pinned(halves, pltpu.VMEM))
-
-
-def ring_experts(residual, message, gate_weight, up_weight, down_weight, others):
+    )(me, *blocks, *pinned(halves, pltpu.HBM if load else pltpu.VMEM))
+
+
+def ring_experts(residual, pieces, gate_weight, up_weight, down_weight, others):
     chips = lax.axis_size("seq")
     ring = SNAKES.get(chips, tuple(range(chips)))
     far = chips // 2
     ahead = [(ring[i], ring[(i + 1) % chips]) for i in range(chips)]
     hops = (ahead, [(to, of) for of, to in ahead])
+    sides = (0, 1)
     me = lax.axis_index("seq").astype(jnp.int32).reshape(1)
-    half = message.shape[0] // 2
-    spans = (slice(0, half), slice(half, 2 * half))
+    given = {}
+
+    def keep(keys, outs):
+        for (side, distance, piece), out in zip(keys, outs):
+            given[(distance if side == 0 else -distance) % chips, piece] = out
+
     halves = (gate_weight, up_weight, down_weight) + tuple(others)
-
-    def apply(*blocks):
-        return experts(blocks, me, halves, chips)
-
-    came = [[message], [message]]
-    given = [[None], [None]]
-    (mine,) = apply(message)
-    worked = [mine]
+    outs = experts(pieces, me, halves, chips, load=True)
+    halves = outs[2:]
+    keep([(0, 0, 0), (0, 0, 1)], outs)
+    worked = {0: outs[0]}
+    came = {(side, 0, piece): pieces[piece] for side in sides for piece in sides}
+
+    def bring(distance, lead, *after):
+        for side in sides:
+            piece = side if lead else 1 - side
+            block = tied(came[side, distance - 1, piece], *after)
+            came[side, distance, piece] = lax.ppermute(block, "seq", hops[side])
+
+    def apply(distance, *after):
+        kinds = (True, False) if distance < far else (True,)
+        keys = [(side, distance, side if lead else 1 - side) for lead in kinds for side in sides]
+        blocks = [came[key] for key in keys]
+        if after:
+            blocks[0] = tied(blocks[0], *after)
+        outs = experts(blocks, me, halves, chips)
+        worked[distance] = outs[0]
+        keep(keys, outs)
+
     for distance in range(1, far + 1):
-        for side in range(2):
-            block = came[side][distance - 1]
-            if distance == far:
-                block = block[spans[side]]
-            if distance > 1:
-                block = tied(block, worked[distance - 2])
-            came[side].append(lax.ppermute(block, "seq", hops[side]))
+        bring(distance, True, *([worked[distance - 2]] if distance > 1 else []))
         if distance < far:
-            outs = apply(came[0][distance], came[1][distance])
+            bring(
+                distance,
+                False,
+                *([came[side, distance - 1, side] for side in sides] if distance > 1 else []),
+            )
+            apply(distance)
         else:
-            outs = apply(tied(came[0][far], worked[far - 1]), came[1][far])
-        worked.append(outs[0])
-        given[0].append(outs[0])
-        given[1].append(outs[1])
-
-    wide = lambda value: value.astype(jnp.float32)
-    total = wide(residual) + wide(mine)
-    for side in range(2):
-        moving = lax.ppermute(given[side][far], "seq", hops[side])
-        for distance in range(far - 1, 0, -1):
-            value = given[1 - side][distance]
-            if distance == far - 1:
-                parts = [value[spans[0]], value[spans[1]]]
-                parts[side] = (wide(moving) + wide(parts[side])).astype(jnp.bfloat16)
-                value = jnp.concatenate(parts, axis=0)
-            else:
-                value = (wide(moving) + wide(value)).astype(jnp.bfloat16)
-            moving = lax.ppermute(value, "seq", hops[side])
-        total += wide(moving)
-    return total.astype(jnp.bfloat16)
+            apply(far, worked[far - 1])
+
+    moving = {}
+
+    def send(distance, lead, *after):
+        for side in sides:
+            piece = side if lead else 1 - side
+            value = given[(-distance if side == 0 else distance) % chips, piece]
+            if after:
+                value = tied(value, *after)
+            if (side, piece) in moving:
+                value = moving[side, piece].astype(jnp.float32) + value.astype(jnp.float32)
+                value = value.astype(jnp.bfloat16)
+            moving[side, piece] = lax.ppermute(value, "seq", hops[side])
+
+    for distance in range(far, 0, -1):
+        if distance > 1:
+            last = [came[side, far, side] for side in sides] if distance == far else []
+            send(distance - 1, False, *last)
+        send(distance, True)
+    final = []
+    for piece in sides:
+        total = given[0, piece].astype(jnp.float32)
+        for side in sides:
+            total += moving[side, piece].astype(jnp.float32)
+        final.append(total)
+    return (residual.astype(jnp.float32) + jnp.concatenate(final, axis=0)).astype(jnp.bfloat16)
 
 
 def dispatched_experts(
@@ -378,14 +431,20 @@
     send, own = attend(0, first, *shared, (k_before, v_before), rank, later_half)
     came = swapped(send, "rep")
     expert_count = lax.axis_size("seq") * EXP_DEV if use_ring else 0
-    residual, message = norm(
-        stream, own, came, norm_gain, expert_ids, route_weights, expert_count, []
-    )
-    message, *others = lax.optimization_barrier((message, *others))
+    residual, *pieces = norm(
+        stream, own, came, norm_gain, expert_ids, route_weights, expert_count, 2
+    )
     if use_ring:
-        return ring_experts(residual, message, gate_weight, up_weight, down_weight, others)
+        *pieces, _ = lax.optimization_barrier((*pieces, others))
+        return ring_experts(residual, pieces, gate_weight, up_weight, down_weight, others)
     return dispatched_experts(
-        residual, message, expert_ids, route_weights, gate_weight, up_weight, down_weight
+        residual,
+        jnp.concatenate(pieces, axis=0),
+        expert_ids,
+        route_weights,
+        gate_weight,
+        up_weight,
+        down_weight,
     )
 
 

time: 103 us -> 91.7 us (0.89)
  waiting for transfers between devices: 43 us -> 26.8 us
  starting transfers between devices: 21.1 us -> 34.2 us
  Pallas kernels: 37.2 us -> 28.9 us
    ppermute x16 -> x28, waiting for transfers between devices: 40.1 us -> 23.7 us  [the longest x14 19.9 us: send(): moving[side, piece] = lax.ppermute(value, 'seq', hops[side])]
    ppermute x16 -> x28, starting transfers between devices: 16 us -> 29.1 us  [the longest x14 14.8 us: send(): moving[side, piece] = lax.ppermute(value, 'seq', hops[side])]
    pallas_call x5, Pallas kernels: 27.7 us -> 19.6 us  [experts(): pl.pallas_call(functools.partial(expert_kernel, min(256, half), expert_co...]
  transfers between devices with their start and end apart: 22 -> 34, of which waited for: 13 -> 14; matrix products, arithmetic and copies ran while one was open for 1% -> 1% of each run, Pallas kernels for 32% -> 29%
where the time goes in v4:
time: 91.7 us; the launch traced here: 91.6 us
  starting transfers between devices  34.2 us (37%)
  Pallas kernels  28.9 us (32%)
  waiting for transfers between devices  26.8 us (29%)
  other arithmetic  1.43 us (2%)
    ppermute x14, waiting for transfers between devices, send(): moving[side, piece] = lax.ppermute(value, 'seq', hops[side])  19.9 us
    pallas_call x5, Pallas kernels, experts(): pl.pallas_call(functools.partial(expert_kernel, min(256, half), expert_co...  19.6 us
    ppermute x14, starting transfers between devices, send(): moving[side, piece] = lax.ppermute(value, 'seq', hops[side])  14.8 us
    ppermute x14, starting transfers between devices, bring(): came[side, distance, piece] = lax.ppermute(block, 'seq', hops[side])  14.3 us
    pallas_call x2, Pallas kernels, attend(): pl.pallas_call(functools.partial(attend_kernel, half, mix), in_specs=[sme...  8.99 us
    ppermute x2, starting transfers between devices, shifted(): lax.ppermute(value, axis, [(i, (i + by) % peers) for i in range(peers)])  4.04 us
    ppermute x14, waiting for transfers between devices, bring(): came[side, distance, piece] = lax.ppermute(block, 'seq', hops[side])  3.84 us
  transfers between devices with their start and end apart: 34, of which 14 were waited for; matrix products, arithmetic and copies ran while one was open for 1% of the time, Pallas kernels for 29%

profile of v4, /device:TPU:0, one launch (start us, length us, event | category | flops | bytes accessed | tf_op | source)
XLA Modules:
  0.0 91.6 jit_solution(3199422825826158630)
XLA Ops:
  0.0 0.5 collective-permute-start.3
  0.5 0.5 collective-permute-start.5
  1.0 2.5 %collective-permute-start = (bf16[256,128]{1,0:T(8,128)(2,1)}, bf16[256,128]{1,0:T(8,128)(2,1)S(1)}, u32[]{:S(2)}, u32[]{:S(2)}) collective-permute-start(bf16[256,128]{1,0:T(8,128)(2,1)} %k_hbm.3), channel_id=1, source_target_pairs={{0,2},{2,4},{4,6},{6,8},{8,10},{10,12},{12,14},{14,0},{1,3},{3,5},... | collective-permute-start | bytes 196616 | tf_op jit(solution)/shard_map/ppermute | solution.py:23
  3.5 1.5 %collective-permute-start.1 = (bf16[256,128]{1,0:T(8,128)(2,1)}, bf16[256,128]{1,0:T(8,128)(2,1)S(1)}, u32[]{:S(2)}, u32[]{:S(2)}) collective-permute-start(bf16[256,128]{1,0:T(8,128)(2,1)} %v_hbm.3), channel_id=1, source_target_pairs={{0,2},{2,4},{4,6},{6,8},{8,10},{10,12},{12,14},{14,0},{1,3},{3,5},... | collective-permute-start | bytes 196616 | tf_op jit(solution)/shard_map/ppermute | solution.py:23
  5.0 4.5 %attend.2.rest_3_ = f32[128,1536]{1,0:T(8,128)S(1)} custom-call(s32[1]{0:T(128)} %constant.11.clone.1.first_ref, f32[1,16]{1,0:T(1,128)} %bitcast.17, bf16[256,1024]{1,0:T(8,128)(2,1)} %q_hbm.3, bf16[256,128]{1,0:T(8,128)(2,1)} %k_hbm.3, bf16[256,128]{1,0:T(8,128)(2,1)} %v_hbm.3, bf16[1024,1536]{1,0:T(8,128)(2,1)} %ow_hbm.3), custom_call_target="tpu_custom_call" | custom-call | flops 671088640 | bytes 6291456 | tf_op jit(solution)/shard_map/attend/pallas_call | solution.py:136
  9.6 1.2 %collective-permute-done.1.rest_1_ = bf16[256,128]{1,0:T(8,128)(2,1)S(1)} collective-permute-done((bf16[256,128]{1,0:T(8,128)(2,1)}, bf16[256,128]{1,0:T(8,128)(2,1)S(1)}, u32[]{:S(2)}, u32[]{:S(2)}) %collective-permute-start.1) | collective-permute-done | bytes 65568 | tf_op jit(solution)/shard_map/ppermute | solution.py:23
  10.9 4.5 %attend.3 = (bf16[128,1536]{1,0:T(8,128)(2,1)S(1)}, f32[128,1536]{1,0:T(8,128)S(1)}) custom-call(s32[1]{0:T(128)} %bitcast.first_ref, f32[1,16]{1,0:T(1,128)} %bitcast.18, bf16[256,1024]{1,0:T(8,128)(2,1)} %q_hbm.3, bf16[256,128]{1,0:T(8,128)(2,1)} %k_hbm.3, bf16[256,128]{1,0:T(8,128)(2,1)} %v_hbm.3, bf16[1024,1536]{1,0:T(8,128)(2,1)} %ow_hbm.3, ...), custom_call_target="tpu_custom_call" | custom-call | flops 671088640 | bytes 6291456 | tf_op jit(solution)/shard_map/attend/pallas_call | solution.py:136
  15.5 1.7 %collective-permute-done.2.came_ref = bf16[128,1536]{1,0:T(8,128)(2,1)S(1)} collective-permute-done((bf16[128,1536]{1,0:T(8,128)(2,1)S(1)}, bf16[128,1536]{1,0:T(8,128)(2,1)S(1)}, u32[]{:S(2)}, u32[]{:S(2)}) %collective-permute-start.2) | collective-permute-done | bytes 393248 | tf_op jit(solution)/shard_map/ppermute | solution.py:36
  17.2 0.3 norm.1
  17.8 1.9 %collective-permute-start.6 = (bf16[64,1664]{1,0:T(8,128)(2,1)S(1)}, bf16[64,1664]{1,0:T(8,128)(2,1)S(1)}, u32[]{:S(2)}, u32[]{:S(2)}) collective-permute-start(bf16[64,1664]{1,0:T(8,128)(2,1)S(1)} %get-tuple-element.52.refs_0_), channel_id=1, source_target_pairs={{0,4},{4,8},{8,12},{12,14},{14,10},{10,6},{6,2},{2,0},{1,5},{5,9},... | collective-permute-start | bytes 638984 | tf_op jit(solution)/shard_map/ppermute | solution.py:312
  19.8 1.9 %collective-permute-start.9 = (bf16[64,1664]{1,0:T(8,128)(2,1)S(1)}, bf16[64,1664]{1,0:T(8,128)(2,1)S(1)}, u32[]{:S(2)}, u32[]{:S(2)}) collective-permute-start(bf16[64,1664]{1,0:T(8,128)(2,1)S(1)} %get-tuple-element.53.refs_1_), channel_id=1, source_target_pairs={{0,4},{4,8},{8,12},{12,14},{14,10},{10,6},{6,2},{2,0},{1,5},{5,9},... | collective-permute-start | bytes 638984 | tf_op jit(solution)/shard_map/ppermute | solution.py:312
  21.7 6.0 %experts.5 = (bf16[64,1536]{1,0:T(8,128)(2,1)S(1)}, bf16[64,1536]{1,0:T(8,128)(2,1)S(1)}, bf16[1536,768]{1,0:T(8,128)(2,1)S(1)}, bf16[1536,768]{1,0:T(8,128)(2,1...) custom-call(s32[1]{0:T(128)} %bitcast.5.me_ref, ...), custom_call_target="tpu_custom_call" | custom-call | flops 1811939328 | bytes 1179648 | tf_op jit(solution)/shard_map/experts/pallas_call | solution.py:271
  27.6 0.2 collective-permute-start.12
  27.9 1.9 %collective-permute-start.7 = (bf16[64,1664]{1,0:T(8,128)(2,1)S(1)}, bf16[64,1664]{1,0:T(8,128)(2,1)S(1)}, u32[]{:S(2)}, u32[]{:S(2)}) collective-permute-start(bf16[64,1664]{1,0:T(8,128)(2,1)S(1)} %collective-permute-done.6.refs_0_), channel_id=1, source_target_pairs={{0,4},{4,8},{8,12},{12,14},{14,10},{10,6},{6,2},{2,0},{1,5},{5,9},... | collective-permute-start | bytes 638984 | tf_op jit(solution)/shard_map/ppermute | solution.py:312
  29.9 1.9 %collective-permute-start.13 = (bf16[64,1664]{1,0:T(8,128)(2,1)S(1)}, bf16[64,1664]{1,0:T(8,128)(2,1)S(1)}, u32[]{:S(2)}, u32[]{:S(2)}) collective-permute-start(bf16[64,1664]{1,0:T(8,128)(2,1)S(1)} %collective-permute-done.9.refs_2_), channel_id=1, source_target_pairs={{0,4},{4,8},{8,12},{12,14},{14,10},{10,6},{6,2},{2,0},{1,5},{5,9},... | collective-permute-start | bytes 638984 | tf_op jit(solution)/shard_map/ppermute | solution.py:312
  31.8 3.9 %experts.6 = (bf16[64,1536]{1,0:T(8,128)(2,1)S(1)}, bf16[64,1536]{1,0:T(8,128)(2,1)S(1)}, bf16[64,1536]{1,0:T(8,128)(2,1)S(1)}, bf16[64,1536]{1,0:T(8,128)(2,1)S(1)}) custom-call(s32[1]{0:T(128)} %bitcast.5.me_ref, bf16[64,1664]{1,0:T(8,128)(2,1)S(1)} %collective-permute-done.6.refs_0_, bf16[64,1664]{1,0:T(8,128)(2,1)S(1)} %collective-permute-done.8.refs_1_, ...), custom_call_target="tpu_custom_call" | custom-call | flops 3623878656 | bytes 2359296 | tf_op jit(solution)/shard_map/experts/pallas_call | solution.py:271
  35.6 0.3 collective-permute-done.12.refs_1_
  36.1 1.9 %collective-permute-start.11 = (bf16[64,1664]{1,0:T(8,128)(2,1)S(1)}, bf16[64,1664]{1,0:T(8,128)(2,1)S(1)}, u32[]{:S(2)}, u32[]{:S(2)}) collective-permute-start(bf16[64,1664]{1,0:T(8,128)(2,1)S(1)} %collective-permute-done.7.refs_0_), channel_id=1, source_target_pairs={{0,4},{4,8},{8,12},{12,14},{14,10},{10,6},{6,2},{2,0},{1,5},{5,9},... | collective-permute-start | bytes 638984 | tf_op jit(solution)/shard_map/ppermute | solution.py:312
  37.9 2.4 %collective-permute-done.14.refs_3_ = bf16[64,1664]{1,0:T(8,128)(2,1)S(1)} collective-permute-done((bf16[64,1664]{1,0:T(8,128)(2,1)S(1)}, bf16[64,1664]{1,0:T(8,128)(2,1)S(1)}, u32[]{:S(2)}, u32[]{:S(2)}) %collective-permute-start.14) | collective-permute-done | bytes 213024 | tf_op jit(solution)/shard_map/ppermute | solution.py:312
  40.5 1.9 %collective-permute-start.17 = (bf16[64,1664]{1,0:T(8,128)(2,1)S(1)}, bf16[64,1664]{1,0:T(8,128)(2,1)S(1)}, u32[]{:S(2)}, u32[]{:S(2)}) collective-permute-start(bf16[64,1664]{1,0:T(8,128)(2,1)S(1)} %collective-permute-done.13.refs_2_), channel_id=1, source_target_pairs={{0,4},{4,8},{8,12},{12,14},{14,10},{10,6},{6,2},{2,0},{1,5},{5,9},... | collective-permute-start | bytes 638984 | tf_op jit(solution)/shard_map/ppermute | solution.py:312
  42.4 3.9 %experts.7 = (bf16[64,1536]{1,0:T(8,128)(2,1)S(1)}, bf16[64,1536]{1,0:T(8,128)(2,1)S(1)}, bf16[64,1536]{1,0:T(8,128)(2,1)S(1)}, bf16[64,1536]{1,0:T(8,128)(2,1)S(1)}) custom-call(s32[1]{0:T(128)} %bitcast.5.me_ref, bf16[64,1664]{1,0:T(8,128)(2,1)S(1)} %collective-permute-done.7.refs_0_, bf16[64,1664]{1,0:T(8,128)(2,1)S(1)} %collective-permute-done.12.refs_1_, ...), custom_call_target="tpu_custom_call" | custom-call | flops 3623878656 | bytes 2359296 | tf_op jit(solution)/shard_map/experts/pallas_call | solution.py:271
  46.5 1.9 %collective-permute-start.15 = (bf16[64,1664]{1,0:T(8,128)(2,1)S(1)}, bf16[64,1664]{1,0:T(8,128)(2,1)S(1)}, u32[]{:S(2)}, u32[]{:S(2)}) collective-permute-start(bf16[64,1664]{1,0:T(8,128)(2,1)S(1)} %collective-permute-done.11.refs_0_), channel_id=1, source_target_pairs={{0,4},{4,8},{8,12},{12,14},{14,10},{10,6},{6,2},{2,0},{1,5},{5,9},... | collective-permute-start | bytes 638984 | tf_op jit(solution)/shard_map/ppermute | solution.py:312
  48.3 1.1 %collective-permute-done.18.refs_3_ = bf16[64,1664]{1,0:T(8,128)(2,1)S(1)} collective-permute-done((bf16[64,1664]{1,0:T(8,128)(2,1)S(1)}, bf16[64,1664]{1,0:T(8,128)(2,1)S(1)}, u32[]{:S(2)}, u32[]{:S(2)}) %collective-permute-start.18) | collective-permute-done | bytes 213024 | tf_op jit(solution)/shard_map/ppermute | solution.py:312
  49.5 3.9 %experts.8 = (bf16[64,1536]{1,0:T(8,128)(2,1)S(1)}, bf16[64,1536]{1,0:T(8,128)(2,1)S(1)}, bf16[64,1536]{1,0:T(8,128)(2,1)S(1)}, bf16[64,1536]{1,0:T(8,128)(2,1)S(1)}) custom-call(s32[1]{0:T(128)} %bitcast.5.me_ref, bf16[64,1664]{1,0:T(8,128)(2,1)S(1)} %collective-permute-done.11.refs_0_, bf16[64,1664]{1,0:T(8,128)(2,1)S(1)} %collective-permute-done.16.refs_1_, ...), custom_call_target="tpu_custom_call" | custom-call | flops 3623878656 | bytes 2359296 | tf_op jit(solution)/shard_map/experts/pallas_call | solution.py:271
  53.4 2.1 %experts.9 = (bf16[64,1536]{1,0:T(8,128)(2,1)S(1)}, bf16[64,1536]{1,0:T(8,128)(2,1)S(1)}) custom-call(s32[1]{0:T(128)} %bitcast.5.me_ref, bf16[64,1664]{1,0:T(8,128)(2,1)S(1)} %collective-permute-done.15.refs_0_, bf16[64,1664]{1,0:T(8,128)(2,1)S(1)} %collective-permute-done.19.refs_1_, bf16[1536,768]{1,0:T(8,128)(2,1)S(1)} %get-tuple-element.56.refs_4_.refs_2_, ...), custom_call_target="tpu_custom_call" | custom-call | flops 1811939328 | bytes 1179648 | tf_op jit(solution)/shard_map/experts/pallas_call | solution.py:271
  55.4 1.8 %collective-permute-start.20 = (bf16[64,1536]{1,0:T(8,128)(2,1)S(1)}, bf16[64,1536]{1,0:T(8,128)(2,1)S(1)}, u32[]{:S(2)}, u32[]{:S(2)}) collective-permute-start(bf16[64,1536]{1,0:T(8,128)(2,1)S(1)} %get-tuple-element.75), channel_id=1, source_target_pairs={{0,4},{4,8},{8,12},{12,14},{14,10},{10,6},{6,2},{2,0},{1,5},{5,9},... | collective-permute-start | bytes 589832 | tf_op jit(solution)/shard_map/ppermute | solution.py:347
  57.2 0.3 collective-permute-start.24
  57.5 1.7 %collective-permute-start.27 = (bf16[64,1536]{1,0:T(8,128)(2,1)S(1)}, bf16[64,1536]{1,0:T(8,128)(2,1)S(1)}, u32[]{:S(2)}, u32[]{:S(2)}) collective-permute-start(bf16[64,1536]{1,0:T(8,128)(2,1)S(1)} %get-tuple-element.82), channel_id=1, source_target_pairs={{0,4},{4,8},{8,12},{12,14},{14,10},{10,6},{6,2},{2,0},{1,5},{5,9},... | collective-permute-start | bytes 589832 | tf_op jit(solution)/shard_map/ppermute | solution.py:347
  59.3 0.3 collective-permute-start.30
  59.6 3.4 %collective-permute-done.20 = bf16[64,1536]{1,0:T(8,128)(2,1)S(1)} collective-permute-done((bf16[64,1536]{1,0:T(8,128)(2,1)S(1)}, bf16[64,1536]{1,0:T(8,128)(2,1)S(1)}, u32[]{:S(2)}, u32[]{:S(2)}) %collective-permute-start.20) | collective-permute-done | bytes 196640 | tf_op jit(solution)/shard_map/ppermute | solution.py:347
  63.0 1.7 %collective-permute-start.21 = (bf16[64,1536]{1,0:T(8,128)(2,1)S(1)}, bf16[64,1536]{1,0:T(8,128)(2,1)S(1)}, u32[]{:S(2)}, u32[]{:S(2)}) collective-permute-start(bf16[64,1536]{1,0:T(8,128)(2,1)S(1)} %add_convert_fusion.9), channel_id=1, source_target_pairs={{0,4},{4,8},{8,12},{12,14},{14,10},{10,6},{6,2},{2,0},{1,5},{5,9},... | collective-permute-start | bytes 589832 | tf_op jit(solution)/shard_map/ppermute | solution.py:347
  64.8 0.4 collective-permute-start.25
  65.2 2.0 %collective-permute-done.27 = bf16[64,1536]{1,0:T(8,128)(2,1)S(1)} collective-permute-done((bf16[64,1536]{1,0:T(8,128)(2,1)S(1)}, bf16[64,1536]{1,0:T(8,128)(2,1)S(1)}, u32[]{:S(2)}, u32[]{:S(2)}) %collective-permute-start.27) | collective-permute-done | bytes 196640 | tf_op jit(solution)/shard_map/ppermute | solution.py:347
  67.3 1.7 %collective-permute-start.28 = (bf16[64,1536]{1,0:T(8,128)(2,1)S(1)}, bf16[64,1536]{1,0:T(8,128)(2,1)S(1)}, u32[]{:S(2)}, u32[]{:S(2)}) collective-permute-start(bf16[64,1536]{1,0:T(8,128)(2,1)S(1)} %add_convert_fusion.4), channel_id=1, source_target_pairs={{0,4},{4,8},{8,12},{12,14},{14,10},{10,6},{6,2},{2,0},{1,5},{5,9},... | collective-permute-start | bytes 589832 | tf_op jit(solution)/shard_map/ppermute | solution.py:347
  69.1 0.4 collective-permute-start.31
  69.4 2.0 %collective-permute-done.21 = bf16[64,1536]{1,0:T(8,128)(2,1)S(1)} collective-permute-done((bf16[64,1536]{1,0:T(8,128)(2,1)S(1)}, bf16[64,1536]{1,0:T(8,128)(2,1)S(1)}, u32[]{:S(2)}, u32[]{:S(2)}) %collective-permute-start.21) | collective-permute-done | bytes 196640 | tf_op jit(solution)/shard_map/ppermute | solution.py:347
  71.5 1.7 %collective-permute-start.22 = (bf16[64,1536]{1,0:T(8,128)(2,1)S(1)}, bf16[64,1536]{1,0:T(8,128)(2,1)S(1)}, u32[]{:S(2)}, u32[]{:S(2)}) collective-permute-start(bf16[64,1536]{1,0:T(8,128)(2,1)S(1)} %add_convert_fusion.8), channel_id=1, source_target_pairs={{0,4},{4,8},{8,12},{12,14},{14,10},{10,6},{6,2},{2,0},{1,5},{5,9},... | collective-permute-start | bytes 589832 | tf_op jit(solution)/shard_map/ppermute | solution.py:347
  73.3 0.4 collective-permute-start.26
  73.7 2.0 %collective-permute-done.28 = bf16[64,1536]{1,0:T(8,128)(2,1)S(1)} collective-permute-done((bf16[64,1536]{1,0:T(8,128)(2,1)S(1)}, bf16[64,1536]{1,0:T(8,128)(2,1)S(1)}, u32[]{:S(2)}, u32[]{:S(2)}) %collective-permute-start.28) | collective-permute-done | bytes 196640 | tf_op jit(solution)/shard_map/ppermute | solution.py:347
  75.7 1.7 %collective-permute-start.29 = (bf16[64,1536]{1,0:T(8,128)(2,1)S(1)}, bf16[64,1536]{1,0:T(8,128)(2,1)S(1)}, u32[]{:S(2)}, u32[]{:S(2)}) collective-permute-start(bf16[64,1536]{1,0:T(8,128)(2,1)S(1)} %add_convert_fusion.3), channel_id=1, source_target_pairs={{0,4},{4,8},{8,12},{12,14},{14,10},{10,6},{6,2},{2,0},{1,5},{5,9},... | collective-permute-start | bytes 589832 | tf_op jit(solution)/shard_map/ppermute | solution.py:347
  77.5 0.4 collective-permute-start.32
  77.9 2.0 %collective-permute-done.22 = bf16[64,1536]{1,0:T(8,128)(2,1)S(1)} collective-permute-done((bf16[64,1536]{1,0:T(8,128)(2,1)S(1)}, bf16[64,1536]{1,0:T(8,128)(2,1)S(1)}, u32[]{:S(2)}, u32[]{:S(2)}) %collective-permute-start.22) | collective-permute-done | bytes 196640 | tf_op jit(solution)/shard_map/ppermute | solution.py:347
  79.9 1.7 %collective-permute-start.23 = (bf16[64,1536]{1,0:T(8,128)(2,1)S(1)}, bf16[64,1536]{1,0:T(8,128)(2,1)S(1)}, u32[]{:S(2)}, u32[]{:S(2)}) collective-permute-start(bf16[64,1536]{1,0:T(8,128)(2,1)S(1)} %add_convert_fusion.7), channel_id=1, source_target_pairs={{0,4},{4,8},{8,12},{12,14},{14,10},{10,6},{6,2},{2,0},{1,5},{5,9},... | collective-permute-start | bytes 589832 | tf_op jit(solution)/shard_map/ppermute | solution.py:347
  81.6 3.3 %collective-permute-done.32 = bf16[64,1536]{1,0:T(8,128)(2,1)S(1)} collective-permute-done((bf16[64,1536]{1,0:T(8,128)(2,1)S(1)}, bf16[64,1536]{1,0:T(8,128)(2,1)S(1)}, u32[]{:S(2)}, u32[]{:S(2)}) %collective-permute-start.32) | collective-permute-done | bytes 196640 | tf_op jit(solution)/shard_map/ppermute | solution.py:347
  85.0 0.4 collective-permute-start.33
  85.4 0.3 collective-permute-done.23
  85.7 5.0 %collective-permute-done.33 = bf16[64,1536]{1,0:T(8,128)(2,1)S(1)} collective-permute-done((bf16[64,1536]{1,0:T(8,128)(2,1)S(1)}, bf16[64,1536]{1,0:T(8,128)(2,1)S(1)}, u32[]{:S(2)}, u32[]{:S(2)}) %collective-permute-start.33) | collective-permute-done | bytes 196640 | tf_op jit(solution)/shard_map/ppermute | solution.py:347
  90.8 0.8 fusion
  (52 shorter events, 2.1 us)
Async XLA Ops:
  0.0 17.5 %collective-permute-start.3 = (bf16[1536,768]{1,0:T(8,128)(2,1)}, bf16[1536,768]{1,0:T(8,128)(2,1)S(1)}, u32[]{:S(2)}, u32[]{:S(2)}) collective-permute-start(bf16[1536,768]{1,0:T(8,128)(2,1)} %bitcast.11), channel_id=1, source_target_pairs={{0,1},{1,0},{2,3},{3,2},{4,5},{5,4},{6,7},{7,6},{8,9},{9,8},{10,11... | collective-permute-start | bytes 7077896 | tf_op jit(solution)/shard_map/ppermute | solution.py:36
  0.5 17.1 %collective-permute-start.4 = (bf16[1536,768]{1,0:T(8,128)(2,1)}, bf16[1536,768]{1,0:T(8,128)(2,1)}, u32[]{:S(2)}, u32[]{:S(2)}) collective-permute-start(bf16[1536,768]{1,0:T(8,128)(2,1)} %bitcast.13), channel_id=1, source_target_pairs={{0,1},{1,0},{2,3},{3,2},{4,5},{5,4},{6,7},{7,6},{8,9},{9,8},{10,11... | collective-permute-start | bytes 7077896 | tf_op jit(solution)/shard_map/ppermute | solution.py:36
  0.5 17.0 %collective-permute-start.5 = (bf16[768,1536]{1,0:T(8,128)(2,1)}, bf16[768,1536]{1,0:T(8,128)(2,1)}, u32[]{:S(2)}, u32[]{:S(2)}) collective-permute-start(bf16[768,1536]{1,0:T(8,128)(2,1)} %bitcast.15), channel_id=1, source_target_pairs={{0,1},{1,0},{2,3},{3,2},{4,5},{5,4},{6,7},{7,6},{8,9},{9,8},{10,11... | collective-permute-start | bytes 7077896 | tf_op jit(solution)/shard_map/ppermute | solution.py:36
  1.0 8.7 %collective-permute-start = (bf16[256,128]{1,0:T(8,128)(2,1)}, bf16[256,128]{1,0:T(8,128)(2,1)S(1)}, u32[]{:S(2)}, u32[]{:S(2)}) collective-permute-start(bf16[256,128]{1,0:T(8,128)(2,1)} %k_hbm.3), channel_id=1, source_target_pairs={{0,2},{2,4},{4,6},{6,8},{8,10},{10,12},{12,14},{14,0},{1,3},{3,5},... | collective-permute-start | bytes 196616 | tf_op jit(solution)/shard_map/ppermute | solution.py:23
  3.5 7.4 %collective-permute-start.1 = (bf16[256,128]{1,0:T(8,128)(2,1)}, bf16[256,128]{1,0:T(8,128)(2,1)S(1)}, u32[]{:S(2)}, u32[]{:S(2)}) collective-permute-start(bf16[256,128]{1,0:T(8,128)(2,1)} %v_hbm.3), channel_id=1, source_target_pairs={{0,2},{2,4},{4,6},{6,8},{8,10},{10,12},{12,14},{14,0},{1,3},{3,5},... | collective-permute-start | bytes 196616 | tf_op jit(solution)/shard_map/ppermute | solution.py:23
  10.9 4.6 %copy-start.4 = (f32[1536]{0:T(1024)S(1)}, f32[1536]{0:T(1024)}, u32[]{:S(2)}) copy-start(f32[1536]{0:T(1024)} %param.18) | copy-start | bytes 18436
  10.9 6.3 %copy-start = (bf16[128,1536]{1,0:T(8,128)(2,1)S(1)}, bf16[128,1536]{1,0:T(8,128)(2,1)}, u32[]{:S(2)}) copy-start(bf16[128,1536]{1,0:T(8,128)(2,1)} %stream_ref.1) | copy-start | bytes 1179652
  10.9 6.3 %copy-start.1 = (s32[128,4]{0,1:T(4,128)S(1)}, s32[128,4]{0,1:T(4,128)}, u32[]{:S(2)}) copy-start(s32[128,4]{0,1:T(4,128)} %param.19) | copy-start | bytes 6148
  10.9 6.3 %copy-start.2 = (f32[128,4]{0,1:T(4,128)S(1)}, f32[128,4]{0,1:T(4,128)}, u32[]{:S(2)}) copy-start(f32[128,4]{0,1:T(4,128)} %param.20) | copy-start | bytes 6148
  15.4 1.8 %collective-permute-start.2 = (bf16[128,1536]{1,0:T(8,128)(2,1)S(1)}, bf16[128,1536]{1,0:T(8,128)(2,1)S(1)}, u32[]{:S(2)}, u32[]{:S(2)}) collective-permute-start(bf16[128,1536]{1,0:T(8,128)(2,1)S(1)} %get-tuple-element.48), channel_id=1, source_target_pairs={{0,1},{1,0},{2,3},{3,2},{4,5},{5,4},{6,7},{7,6},{8,9},{9,8},{10,11... | collective-permute-start | bytes 1179656 | tf_op jit(solution)/shard_map/ppermute | solution.py:36
  17.5 4.1 %copy-start.3 = (bf16[1536,768]{1,0:T(8,128)(2,1)}, bf16[1536,768]{1,0:T(8,128)(2,1)S(1)}, u32[]{:S(2)}) copy-start(bf16[1536,768]{1,0:T(8,128)(2,1)S(1)} %collective-permute-done.3.refs_5_) | copy-start | bytes 7077892
  17.5 10.1 %collective-permute-start.8 = (bf16[64,1664]{1,0:T(8,128)(2,1)S(1)}, bf16[64,1664]{1,0:T(8,128)(2,1)S(1)}, u32[]{:S(2)}, u32[]{:S(2)}) collective-permute-start(bf16[64,1664]{1,0:T(8,128)(2,1)S(1)} %get-tuple-element.53.refs_1_), channel_id=1, source_target_pairs={{4,0},{8,4},{12,8},{14,12},{10,14},{6,10},{2,6},{0,2},{5,1},{9,5},... | collective-permute-start | bytes 638984 | tf_op jit(solution)/shard_map/ppermute | solution.py:312
  17.8 10.1 %collective-permute-start.6 = (bf16[64,1664]{1,0:T(8,128)(2,1)S(1)}, bf16[64,1664]{1,0:T(8,128)(2,1)S(1)}, u32[]{:S(2)}, u32[]{:S(2)}) collective-permute-start(bf16[64,1664]{1,0:T(8,128)(2,1)S(1)} %get-tuple-element.52.refs_0_), channel_id=1, source_target_pairs={{0,4},{4,8},{8,12},{12,14},{14,10},{10,6},{6,2},{2,0},{1,5},{5,9},... | collective-permute-start | bytes 638984 | tf_op jit(solution)/shard_map/ppermute | solution.py:312
  19.6 10.1 %collective-permute-start.10 = (bf16[64,1664]{1,0:T(8,128)(2,1)S(1)}, bf16[64,1664]{1,0:T(8,128)(2,1)S(1)}, u32[]{:S(2)}, u32[]{:S(2)}) collective-permute-start(bf16[64,1664]{1,0:T(8,128)(2,1)S(1)} %get-tuple-element.52.refs_0_), channel_id=1, source_target_pairs={{4,0},{8,4},{12,8},{14,12},{10,14},{6,10},{2,6},{0,2},{5,1},{9,5},... | collective-permute-start | bytes 638984 | tf_op jit(solution)/shard_map/ppermute | solution.py:312
  19.8 10.1 %collective-permute-start.9 = (bf16[64,1664]{1,0:T(8,128)(2,1)S(1)}, bf16[64,1664]{1,0:T(8,128)(2,1)S(1)}, u32[]{:S(2)}, u32[]{:S(2)}) collective-permute-start(bf16[64,1664]{1,0:T(8,128)(2,1)S(1)} %get-tuple-element.53.refs_1_), channel_id=1, source_target_pairs={{0,4},{4,8},{8,12},{12,14},{14,10},{10,6},{6,2},{2,0},{1,5},{5,9},... | collective-permute-start | bytes 638984 | tf_op jit(solution)/shard_map/ppermute | solution.py:312
  27.6 8.2 %collective-permute-start.12 = (bf16[64,1664]{1,0:T(8,128)(2,1)S(1)}, bf16[64,1664]{1,0:T(8,128)(2,1)S(1)}, u32[]{:S(2)}, u32[]{:S(2)}) collective-permute-start(bf16[64,1664]{1,0:T(8,128)(2,1)S(1)} %collective-permute-done.8.refs_1_), channel_id=1, source_target_pairs={{4,0},{8,4},{12,8},{14,12},{10,14},{6,10},{2,6},{0,2},{5,1},{9,5},... | collective-permute-start | bytes 638984 | tf_op jit(solution)/shard_map/ppermute | solution.py:312
  27.9 8.2 %collective-permute-start.7 = (bf16[64,1664]{1,0:T(8,128)(2,1)S(1)}, bf16[64,1664]{1,0:T(8,128)(2,1)S(1)}, u32[]{:S(2)}, u32[]{:S(2)}) collective-permute-start(bf16[64,1664]{1,0:T(8,128)(2,1)S(1)} %collective-permute-done.6.refs_0_), channel_id=1, source_target_pairs={{0,4},{4,8},{8,12},{12,14},{14,10},{10,6},{6,2},{2,0},{1,5},{5,9},... | collective-permute-start | bytes 638984 | tf_op jit(solution)/shard_map/ppermute | solution.py:312
  29.7 10.6 %collective-permute-start.14 = (bf16[64,1664]{1,0:T(8,128)(2,1)S(1)}, bf16[64,1664]{1,0:T(8,128)(2,1)S(1)}, u32[]{:S(2)}, u32[]{:S(2)}) collective-permute-start(bf16[64,1664]{1,0:T(8,128)(2,1)S(1)} %collective-permute-done.10.refs_3_), channel_id=1, source_target_pairs={{4,0},{8,4},{12,8},{14,12},{10,14},{6,10},{2,6},{0,2},{5,1},{9,5},... | collective-permute-start | bytes 638984 | tf_op jit(solution)/shard_map/ppermute | solution.py:312
  29.9 10.6 %collective-permute-start.13 = (bf16[64,1664]{1,0:T(8,128)(2,1)S(1)}, bf16[64,1664]{1,0:T(8,128)(2,1)S(1)}, u32[]{:S(2)}, u32[]{:S(2)}) collective-permute-start(bf16[64,1664]{1,0:T(8,128)(2,1)S(1)} %collective-permute-done.9.refs_2_), channel_id=1, source_target_pairs={{0,4},{4,8},{8,12},{12,14},{14,10},{10,6},{6,2},{2,0},{1,5},{5,9},... | collective-permute-start | bytes 638984 | tf_op jit(solution)/shard_map/ppermute | solution.py:312
  35.9 10.4 %collective-permute-start.16 = (bf16[64,1664]{1,0:T(8,128)(2,1)S(1)}, bf16[64,1664]{1,0:T(8,128)(2,1)S(1)}, u32[]{:S(2)}, u32[]{:S(2)}) collective-permute-start(bf16[64,1664]{1,0:T(8,128)(2,1)S(1)} %collective-permute-done.12.refs_1_), channel_id=1, source_target_pairs={{4,0},{8,4},{12,8},{14,12},{10,14},{6,10},{2,6},{0,2},{5,1},{9,5},... | collective-permute-start | bytes 638984 | tf_op jit(solution)/shard_map/ppermute | solution.py:312
  36.1 10.4 %collective-permute-start.11 = (bf16[64,1664]{1,0:T(8,128)(2,1)S(1)}, bf16[64,1664]{1,0:T(8,128)(2,1)S(1)}, u32[]{:S(2)}, u32[]{:S(2)}) collective-permute-start(bf16[64,1664]{1,0:T(8,128)(2,1)S(1)} %collective-permute-done.7.refs_0_), channel_id=1, source_target_pairs={{0,4},{4,8},{8,12},{12,14},{14,10},{10,6},{6,2},{2,0},{1,5},{5,9},... | collective-permute-start | bytes 638984 | tf_op jit(solution)/shard_map/ppermute | solution.py:312
  40.3 9.1 %collective-permute-start.18 = (bf16[64,1664]{1,0:T(8,128)(2,1)S(1)}, bf16[64,1664]{1,0:T(8,128)(2,1)S(1)}, u32[]{:S(2)}, u32[]{:S(2)}) collective-permute-start(bf16[64,1664]{1,0:T(8,128)(2,1)S(1)} %collective-permute-done.14.refs_3_), channel_id=1, source_target_pairs={{4,0},{8,4},{12,8},{14,12},{10,14},{6,10},{2,6},{0,2},{5,1},{9,5},... | collective-permute-start | bytes 638984 | tf_op jit(solution)/shard_map/ppermute | solution.py:312
  40.5 9.0 %collective-permute-start.17 = (bf16[64,1664]{1,0:T(8,128)(2,1)S(1)}, bf16[64,1664]{1,0:T(8,128)(2,1)S(1)}, u32[]{:S(2)}, u32[]{:S(2)}) collective-permute-start(bf16[64,1664]{1,0:T(8,128)(2,1)S(1)} %collective-permute-done.13.refs_2_), channel_id=1, source_target_pairs={{0,4},{4,8},{8,12},{12,14},{14,10},{10,6},{6,2},{2,0},{1,5},{5,9},... | collective-permute-start | bytes 638984 | tf_op jit(solution)/shard_map/ppermute | solution.py:312
  46.3 7.1 %collective-permute-start.19 = (bf16[64,1664]{1,0:T(8,128)(2,1)S(1)}, bf16[64,1664]{1,0:T(8,128)(2,1)S(1)}, u32[]{:S(2)}, u32[]{:S(2)}) collective-permute-start(bf16[64,1664]{1,0:T(8,128)(2,1)S(1)} %collective-permute-done.16.refs_1_), channel_id=1, source_target_pairs={{4,0},{8,4},{12,8},{14,12},{10,14},{6,10},{2,6},{0,2},{5,1},{9,5},... | collective-permute-start | bytes 638984 | tf_op jit(solution)/shard_map/ppermute | solution.py:312
  46.5 6.9 %collective-permute-start.15 = (bf16[64,1664]{1,0:T(8,128)(2,1)S(1)}, bf16[64,1664]{1,0:T(8,128)(2,1)S(1)}, u32[]{:S(2)}, u32[]{:S(2)}) collective-permute-start(bf16[64,1664]{1,0:T(8,128)(2,1)S(1)} %collective-permute-done.11.refs_0_), channel_id=1, source_target_pairs={{0,4},{4,8},{8,12},{12,14},{14,10},{10,6},{6,2},{2,0},{1,5},{5,9},... | collective-permute-start | bytes 638984 | tf_op jit(solution)/shard_map/ppermute | solution.py:312
  55.4 7.6 %collective-permute-start.20 = (bf16[64,1536]{1,0:T(8,128)(2,1)S(1)}, bf16[64,1536]{1,0:T(8,128)(2,1)S(1)}, u32[]{:S(2)}, u32[]{:S(2)}) collective-permute-start(bf16[64,1536]{1,0:T(8,128)(2,1)S(1)} %get-tuple-element.75), channel_id=1, source_target_pairs={{0,4},{4,8},{8,12},{12,14},{14,10},{10,6},{6,2},{2,0},{1,5},{5,9},... | collective-permute-start | bytes 589832 | tf_op jit(solution)/shard_map/ppermute | solution.py:347
  57.2 7.6 %collective-permute-start.24 = (bf16[64,1536]{1,0:T(8,128)(2,1)S(1)}, bf16[64,1536]{1,0:T(8,128)(2,1)S(1)}, u32[]{:S(2)}, u32[]{:S(2)}) collective-permute-start(bf16[64,1536]{1,0:T(8,128)(2,1)S(1)} %get-tuple-element.79), channel_id=1, source_target_pairs={{4,0},{8,4},{12,8},{14,12},{10,14},{6,10},{2,6},{0,2},{5,1},{9,5},... | collective-permute-start | bytes 589832 | tf_op jit(solution)/shard_map/ppermute | solution.py:347
  57.5 9.7 %collective-permute-start.27 = (bf16[64,1536]{1,0:T(8,128)(2,1)S(1)}, bf16[64,1536]{1,0:T(8,128)(2,1)S(1)}, u32[]{:S(2)}, u32[]{:S(2)}) collective-permute-start(bf16[64,1536]{1,0:T(8,128)(2,1)S(1)} %get-tuple-element.82), channel_id=1, source_target_pairs={{0,4},{4,8},{8,12},{12,14},{14,10},{10,6},{6,2},{2,0},{1,5},{5,9},... | collective-permute-start | bytes 589832 | tf_op jit(solution)/shard_map/ppermute | solution.py:347
  59.3 9.7 %collective-permute-start.30 = (bf16[64,1536]{1,0:T(8,128)(2,1)S(1)}, bf16[64,1536]{1,0:T(8,128)(2,1)S(1)}, u32[]{:S(2)}, u32[]{:S(2)}) collective-permute-start(bf16[64,1536]{1,0:T(8,128)(2,1)S(1)} %get-tuple-element.85), channel_id=1, source_target_pairs={{4,0},{8,4},{12,8},{14,12},{10,14},{6,10},{2,6},{0,2},{5,1},{9,5},... | collective-permute-start | bytes 589832 | tf_op jit(solution)/shard_map/ppermute | solution.py:347
  63.0 8.4 %collective-permute-start.21 = (bf16[64,1536]{1,0:T(8,128)(2,1)S(1)}, bf16[64,1536]{1,0:T(8,128)(2,1)S(1)}, u32[]{:S(2)}, u32[]{:S(2)}) collective-permute-start(bf16[64,1536]{1,0:T(8,128)(2,1)S(1)} %add_convert_fusion.9), channel_id=1, source_target_pairs={{0,4},{4,8},{8,12},{12,14},{14,10},{10,6},{6,2},{2,0},{1,5},{5,9},... | collective-permute-start | bytes 589832 | tf_op jit(solution)/shard_map/ppermute | solution.py:347
  64.8 8.4 %collective-permute-start.25 = (bf16[64,1536]{1,0:T(8,128)(2,1)S(1)}, bf16[64,1536]{1,0:T(8,128)(2,1)S(1)}, u32[]{:S(2)}, u32[]{:S(2)}) collective-permute-start(bf16[64,1536]{1,0:T(8,128)(2,1)S(1)} %add_convert_fusion.6), channel_id=1, source_target_pairs={{4,0},{8,4},{12,8},{14,12},{10,14},{6,10},{2,6},{0,2},{5,1},{9,5},... | collective-permute-start | bytes 589832 | tf_op jit(solution)/shard_map/ppermute | solution.py:347
  67.3 8.4 %collective-permute-start.28 = (bf16[64,1536]{1,0:T(8,128)(2,1)S(1)}, bf16[64,1536]{1,0:T(8,128)(2,1)S(1)}, u32[]{:S(2)}, u32[]{:S(2)}) collective-permute-start(bf16[64,1536]{1,0:T(8,128)(2,1)S(1)} %add_convert_fusion.4), channel_id=1, source_target_pairs={{0,4},{4,8},{8,12},{12,14},{14,10},{10,6},{6,2},{2,0},{1,5},{5,9},... | collective-permute-start | bytes 589832 | tf_op jit(solution)/shard_map/ppermute | solution.py:347
  69.1 8.4 %collective-permute-start.31 = (bf16[64,1536]{1,0:T(8,128)(2,1)S(1)}, bf16[64,1536]{1,0:T(8,128)(2,1)S(1)}, u32[]{:S(2)}, u32[]{:S(2)}) collective-permute-start(bf16[64,1536]{1,0:T(8,128)(2,1)S(1)} %add_convert_fusion.2), channel_id=1, source_target_pairs={{4,0},{8,4},{12,8},{14,12},{10,14},{6,10},{2,6},{0,2},{5,1},{9,5},... | collective-permute-start | bytes 589832 | tf_op jit(solution)/shard_map/ppermute | solution.py:347
  71.5 8.4 %collective-permute-start.22 = (bf16[64,1536]{1,0:T(8,128)(2,1)S(1)}, bf16[64,1536]{1,0:T(8,128)(2,1)S(1)}, u32[]{:S(2)}, u32[]{:S(2)}) collective-permute-start(bf16[64,1536]{1,0:T(8,128)(2,1)S(1)} %add_convert_fusion.8), channel_id=1, source_target_pairs={{0,4},{4,8},{8,12},{12,14},{14,10},{10,6},{6,2},{2,0},{1,5},{5,9},... | collective-permute-start | bytes 589832 | tf_op jit(solution)/shard_map/ppermute | solution.py:347
  73.3 12.1 %collective-permute-start.26 = (bf16[64,1536]{1,0:T(8,128)(2,1)S(1)}, bf16[64,1536]{1,0:T(8,128)(2,1)S(1)}, u32[]{:S(2)}, u32[]{:S(2)}) collective-permute-start(bf16[64,1536]{1,0:T(8,128)(2,1)S(1)} %add_convert_fusion.5), channel_id=1, source_target_pairs={{4,0},{8,4},{12,8},{14,12},{10,14},{6,10},{2,6},{0,2},{5,1},{9,5},... | collective-permute-start | bytes 589832 | tf_op jit(solution)/shard_map/ppermute | solution.py:347
  75.7 10.0 %collective-permute-start.29 = (bf16[64,1536]{1,0:T(8,128)(2,1)S(1)}, bf16[64,1536]{1,0:T(8,128)(2,1)S(1)}, u32[]{:S(2)}, u32[]{:S(2)}) collective-permute-start(bf16[64,1536]{1,0:T(8,128)(2,1)S(1)} %add_convert_fusion.3), channel_id=1, source_target_pairs={{0,4},{4,8},{8,12},{12,14},{14,10},{10,6},{6,2},{2,0},{1,5},{5,9},... | collective-permute-start | bytes 589832 | tf_op jit(solution)/shard_map/ppermute | solution.py:347
  77.5 7.4 %collective-permute-start.32 = (bf16[64,1536]{1,0:T(8,128)(2,1)S(1)}, bf16[64,1536]{1,0:T(8,128)(2,1)S(1)}, u32[]{:S(2)}, u32[]{:S(2)}) collective-permute-start(bf16[64,1536]{1,0:T(8,128)(2,1)S(1)} %add_convert_fusion.1), channel_id=1, source_target_pairs={{4,0},{8,4},{12,8},{14,12},{10,14},{6,10},{2,6},{0,2},{5,1},{9,5},... | collective-permute-start | bytes 589832 | tf_op jit(solution)/shard_map/ppermute | solution.py:347
  79.9 5.7 %collective-permute-start.23 = (bf16[64,1536]{1,0:T(8,128)(2,1)S(1)}, bf16[64,1536]{1,0:T(8,128)(2,1)S(1)}, u32[]{:S(2)}, u32[]{:S(2)}) collective-permute-start(bf16[64,1536]{1,0:T(8,128)(2,1)S(1)} %add_convert_fusion.7), channel_id=1, source_target_pairs={{0,4},{4,8},{8,12},{12,14},{14,10},{10,6},{6,2},{2,0},{1,5},{5,9},... | collective-permute-start | bytes 589832 | tf_op jit(solution)/shard_map/ppermute | solution.py:347
  85.0 5.7 %collective-permute-start.33 = (bf16[64,1536]{1,0:T(8,128)(2,1)S(1)}, bf16[64,1536]{1,0:T(8,128)(2,1)S(1)}, u32[]{:S(2)}, u32[]{:S(2)}) collective-permute-start(bf16[64,1536]{1,0:T(8,128)(2,1)S(1)} %add_convert_fusion), channel_id=1, source_target_pairs={{4,0},{8,4},{12,8},{14,12},{10,14},{6,10},{2,6},{0,2},{5,1},{9,5},... | collective-permute-start | bytes 589832 | tf_op jit(solution)/shard_map/ppermute | solution.py:347

commit v5 on v4

--- a/solution.py
+++ b/solution.py
@@ -11,6 +11,7 @@
 HEAD_DIM = 64
 WINDOW = 128
 TOP = 4
+TAIL = 16
 EXP_DEV = 1
 LANES = 128
 SNAKES = {8: (0, 2, 4, 6, 7, 5, 3, 1)}
@@ -164,7 +165,6 @@
 ):
     residual_ref, *message_refs = rest
     rows, model = stream_ref.shape
-    size = message_refs[0].shape[0]
     residual = (
         stream_ref[...].astype(jnp.float32) + own_ref[...] + came_ref[...].astype(jnp.float32)
     ).astype(jnp.bfloat16)
@@ -172,31 +172,38 @@
     wide = residual.astype(jnp.float32)
     mean = jnp.mean(wide * wide, axis=-1, keepdims=True)
     normed = (wide * lax.rsqrt(mean + 1e-05) * gain_ref[...]).astype(jnp.bfloat16)
+    if not expert_count:
+        message_refs[0][...] = normed
+        return
+    size = rows // len(message_refs)
+    expert = lax.broadcasted_iota(jnp.int32, (TAIL, rows), 0)
+    dense = jnp.zeros((TAIL, rows), jnp.float32)
+    for k in range(TOP):
+        dense += jnp.where(expert == ids_ref[k : k + 1, :], route_ref[k : k + 1, :], 0.0)
+    lead = dense.astype(jnp.bfloat16).astype(jnp.float32)
+    rest = dense - lead
     for index, ref in enumerate(message_refs):
-        ref[:, :model] = normed[index * size : (index + 1) * size]
-    if expert_count:
-        expert = lax.broadcasted_iota(jnp.int32, (LANES, rows), 0)
-        dense = jnp.zeros((LANES, rows), jnp.float32)
-        for k in range(TOP):
-            named = ids_ref[k : k + 1, :]
-            hit = (expert == named) | (expert == named + expert_count)
-            dense += jnp.where(hit, route_ref[k : k + 1, :], 0.0)
-        lead = dense.astype(jnp.bfloat16).astype(jnp.float32)
-        both = jnp.where(expert < expert_count, lead, dense - lead)
-        tail = both.T.astype(jnp.bfloat16)
-        for index, ref in enumerate(message_refs):
-            ref[:, model:] = tail[index * size : (index + 1) * size]
-
-
-def norm(stream, own, came, gain, expert_ids, route_weights, expert_count, pieces):
+        for block in range(model // LANES):
+            ref[block * size : (block + 1) * size] = normed[
+                index * size : (index + 1) * size, block * LANES : (block + 1) * LANES
+            ]
+        span = slice(index * size, (index + 1) * size)
+        both = jnp.concatenate([lead[:, span], rest[:, span]], axis=1)
+        ref[model // LANES * size :] = both.astype(jnp.bfloat16)
+
+
+def norm(stream, own, came, gain, expert_ids, route_weights, expert_count):
     rows, model = stream.shape
     vmem = pl.BlockSpec(memory_space=pltpu.VMEM)
-    width = model + (LANES if expert_count else 0)
+    pieces, shape = 1, (rows, model)
+    if expert_count:
+        pieces = 2
+        shape = (rows // pieces * (model // LANES) + TAIL, LANES)
     return pl.pallas_call(
         functools.partial(norm_kernel, expert_count),
         in_specs=[vmem] * 6,
         out_shape=[jax.ShapeDtypeStruct((rows, model), jnp.bfloat16)]
-        + [jax.ShapeDtypeStruct((rows // pieces, width), jnp.bfloat16)] * pieces,
+        + [jax.ShapeDtypeStruct(shape, jnp.bfloat16)] * pieces,
         compiler_params=pltpu.CompilerParams(vmem_limit_bytes=8 * MIB),
         cost_estimate=pl.CostEstimate(
             flops=8 * rows * model, bytes_accessed=14 * rows * model, transcendentals=rows
@@ -205,7 +212,7 @@
     )(stream, own, came, gain.reshape(1, model), expert_ids.T, route_weights.T)
 
 
-def expert_kernel(tile, expert_count, count, load, me_ref, *refs):
+def expert_kernel(tile, count, load, me_ref, *refs):
     x_refs, halves = refs[:count], refs[count : count + 6]
     out_refs, rest = refs[count + 6 : 2 * count + 6], refs[2 * count + 6 :]
     copies = []
@@ -220,11 +227,13 @@
         halves = kept
     x, hidden = rest[:2]
     model, half = halves[0].shape
-    starts = [0]
-    for ref in x_refs:
-        starts.append(starts[-1] + ref.shape[0])
-    for start, ref in zip(starts, x_refs):
-        x[start : start + ref.shape[0]] = ref[:, :model]
+    rows = x.shape[0] // count
+    body = rows * (model // LANES)
+    for index, ref in enumerate(x_refs):
+        for block in range(model // LANES):
+            x[index * rows : (index + 1) * rows, block * LANES : (block + 1) * LANES] = ref[
+                block * rows : (block + 1) * rows
+            ]
 
     def arrived(*which):
         for index in which:
@@ -247,20 +256,22 @@
     me = me_ref[0]
     scales = []
     for ref in x_refs:
-        sent = ref[:, model:].astype(jnp.float32)
-        lane = lax.broadcasted_iota(jnp.int32, sent.shape, 1)
-        mine = (lane == me) | (lane == me + expert_count)
-        scales.append(jnp.sum(jnp.where(mine, sent, 0.0), axis=1, keepdims=True))
+        sent = ref[body:].astype(jnp.float32)
+        expert = lax.broadcasted_iota(jnp.int32, sent.shape, 0)
+        mine = jnp.sum(jnp.where(expert == me, sent, 0.0), axis=0, keepdims=True)
+        mine = jnp.broadcast_to(mine, (8, LANES))
+        scales.append((mine + pltpu.roll(mine, LANES - rows, 1)).T[:rows, :1])
     for at in range(0, model, tile):
         lanes = slice(at, at + tile)
         total = mm(hidden[:, :half], halves[2][:, lanes]) + mm(hidden[:, half:], halves[5][:, lanes])
-        for start, ref, scale in zip(starts, out_refs, scales):
-            ref[:, lanes] = (total[start : start + ref.shape[0]] * scale).astype(jnp.bfloat16)
-
-
-def experts(blocks, me, halves, expert_count, load=False):
+        for index, (ref, scale) in enumerate(zip(out_refs, scales)):
+            ref[:, lanes] = (total[index * rows : (index + 1) * rows] * scale).astype(jnp.bfloat16)
+
+
+def experts(blocks, me, halves, load=False):
     model, half = halves[0].shape
-    rows = sum(block.shape[0] for block in blocks)
+    size = (blocks[0].shape[0] - TAIL) // (model // LANES)
+    rows = size * len(blocks)
     vmem = pl.BlockSpec(memory_space=pltpu.VMEM)
     hbm = pl.BlockSpec(memory_space=pltpu.HBM)
     kept = [jax.ShapeDtypeStruct(w.shape, w.dtype) for w in halves] if load else []
@@ -269,12 +280,12 @@
         pltpu.VMEM((rows, 2 * half), jnp.bfloat16),
     ]
     return pl.pallas_call(
-        functools.partial(expert_kernel, min(256, half), expert_count, len(blocks), load),
+        functools.partial(expert_kernel, min(256, half), len(blocks), load),
         in_specs=[pl.BlockSpec(memory_space=pltpu.SMEM)]
         + [vmem] * len(blocks)
         + [hbm if load else vmem] * 6,
         out_specs=[vmem] * (len(blocks) + len(kept)),
-        out_shape=[jax.ShapeDtypeStruct((b.shape[0], model), jnp.bfloat16) for b in blocks] + kept,
+        out_shape=[jax.ShapeDtypeStruct((size, model), jnp.bfloat16)] * len(blocks) + kept,
         scratch_shapes=scratch + ([pltpu.SemaphoreType.DMA((6,))] if load else []),
         compiler_params=pltpu.CompilerParams(vmem_limit_bytes=EXPERT_VMEM),
         cost_estimate=pl.CostEstimate(
@@ -299,7 +310,7 @@
             given[(distance if side == 0 else -distance) % chips, piece] = out
 
     halves = (gate_weight, up_weight, down_weight) + tuple(others)
-    outs = experts(pieces, me, halves, chips, load=True)
+    outs = experts(pieces, me, halves, load=True)
     halves = outs[2:]
     keep([(0, 0, 0), (0, 0, 1)], outs)
     worked = {0: outs[0]}
@@ -309,15 +320,16 @@
         for side in sides:
             piece = side if lead else 1 - side
             block = tied(came[side, distance - 1, piece], *after)
-            came[side, distance, piece] = lax.ppermute(block, "seq", hops[side])
-
-    def apply(distance, *after):
-        kinds = (True, False) if distance < far else (True,)
+            with jax.named_scope(f"out_{'lead' if lead else 'trail'}{distance}"):
+                came[side, distance, piece] = lax.ppermute(block, "seq", hops[side])
+
+    def apply(distance, kinds, *after):
         keys = [(side, distance, side if lead else 1 - side) for lead in kinds for side in sides]
         blocks = [came[key] for key in keys]
         if after:
             blocks[0] = tied(blocks[0], *after)
-        outs = experts(blocks, me, halves, chips)
+        with jax.named_scope(f"hop{distance}"):
+            outs = experts(blocks, me, halves)
         worked[distance] = outs[0]
         keep(keys, outs)
 
@@ -329,9 +341,12 @@
                 False,
                 *([came[side, distance - 1, side] for side in sides] if distance > 1 else []),
             )
-            apply(distance)
-        else:
-            apply(far, worked[far - 1])
+        if distance < far - 1:
+            apply(distance, (True, False))
+        elif distance < far:
+            apply(distance, (True,), worked[distance - 1])
+    apply(far, (True,), worked[far - 1])
+    apply(far - 1, (False,), worked[far])
 
     moving = {}
 
@@ -344,12 +359,14 @@
             if (side, piece) in moving:
                 value = moving[side, piece].astype(jnp.float32) + value.astype(jnp.float32)
                 value = value.astype(jnp.bfloat16)
-            moving[side, piece] = lax.ppermute(value, "seq", hops[side])
+            with jax.named_scope(f"back_{'lead' if lead else 'trail'}{distance}"):
+                moving[side, piece] = lax.ppermute(value, "seq", hops[side])
 
     for distance in range(far, 0, -1):
-        if distance > 1:
-            last = [came[side, far, side] for side in sides] if distance == far else []
-            send(distance - 1, False, *last)
+        if distance == far:
+            send(far - 1, False, *[came[side, far, side] for side in sides])
+        elif distance > 1:
+            send(distance - 1, False, worked[far] if distance == far - 1 else moving[0, 0])
         send(distance, True)
     final = []
     for piece in sides:
@@ -432,14 +449,14 @@
     came = swapped(send, "rep")
     expert_count = lax.axis_size("seq") * EXP_DEV if use_ring else 0
     residual, *pieces = norm(
-        stream, own, came, norm_gain, expert_ids, route_weights, expert_count, 2
+        stream, own, came, norm_gain, expert_ids, route_weights, expert_count
     )
     if use_ring:
         *pieces, _ = lax.optimization_barrier((*pieces, others))
         return ring_experts(residual, pieces, gate_weight, up_weight, down_weight, others)
     return dispatched_experts(
         residual,
-        jnp.concatenate(pieces, axis=0),
+        pieces[0],
         expert_ids,
         route_weights,
         gate_weight,

time: 91.7 us -> 88.6 us (0.966)
  waiting for transfers between devices: 26.8 us -> 19 us
  starting transfers between devices: 34.2 us -> 38.3 us
    ppermute x14, waiting for transfers between devices: 19.9 us -> 12.3 us  [send(): moving[side, piece] = lax.ppermute(value, 'seq', hops[side])]
    ppermute x14, starting transfers between devices: 14.8 us -> 18.9 us  [send(): moving[side, piece] = lax.ppermute(value, 'seq', hops[side])]
    pallas_call x5 -> x6, Pallas kernels: 19.6 us -> 20.1 us  [experts(): pl.pallas_call(functools.partial(expert_kernel, min(256, half), len(block...]
  transfers between devices with their start and end apart: 34 -> 34, of which waited for: 14 -> 19; matrix products, arithmetic and copies ran while one was open for 1% -> 1% of each run, Pallas kernels for 29% -> 33%
where the time goes in v5:
time: 88.6 us; the launch traced here: 88.4 us
  starting transfers between devices  38.3 us (43%)
  Pallas kernels  29.4 us (33%)
  waiting for transfers between devices  19 us (21%)
  other arithmetic  1.44 us (2%)
    pallas_call x6, Pallas kernels, experts(): pl.pallas_call(functools.partial(expert_kernel, min(256, half), len(block...  20.1 us
    ppermute x14, starting transfers between devices, send(): moving[side, piece] = lax.ppermute(value, 'seq', hops[side])  18.9 us
    ppermute x14, starting transfers between devices, bring(): came[side, distance, piece] = lax.ppermute(block, 'seq', hops[side])  14.4 us
    ppermute x14, waiting for transfers between devices, send(): moving[side, piece] = lax.ppermute(value, 'seq', hops[side])  12.3 us
    pallas_call x2, Pallas kernels, attend(): pl.pallas_call(functools.partial(attend_kernel, half, mix), in_specs=[sme...  8.99 us
    ppermute x2, starting transfers between devices, shifted(): lax.ppermute(value, axis, [(i, (i + by) % peers) for i in range(peers)])  4.04 us
    ppermute x14, waiting for transfers between devices, bring(): came[side, distance, piece] = lax.ppermute(block, 'seq', hops[side])  3.66 us
  transfers between devices with their start and end apart: 34, of which 19 were waited for; matrix products, arithmetic and copies ran while one was open for 1% of the time, Pallas kernels for 33%

profile of v5, /device:TPU:0, one launch (start us, length us, event | category | flops | bytes accessed | tf_op | source)
XLA Modules:
  0.0 88.4 jit_solution(552937971676664384)
XLA Ops:
  0.0 0.5 collective-permute-start.3
  0.5 0.5 collective-permute-start.5
  1.0 2.5 %collective-permute-start = (bf16[256,128]{1,0:T(8,128)(2,1)}, bf16[256,128]{1,0:T(8,128)(2,1)S(1)}, u32[]{:S(2)}, u32[]{:S(2)}) collective-permute-start(bf16[256,128]{1,0:T(8,128)(2,1)} %k_hbm.3), channel_id=1, source_target_pairs={{0,2},{2,4},{4,6},{6,8},{8,10},{10,12},{12,14},{14,0},{1,3},{3,5},... | collective-permute-start | bytes 196616 | tf_op jit(solution)/shard_map/ppermute | solution.py:24
  3.5 1.5 %collective-permute-start.1 = (bf16[256,128]{1,0:T(8,128)(2,1)}, bf16[256,128]{1,0:T(8,128)(2,1)S(1)}, u32[]{:S(2)}, u32[]{:S(2)}) collective-permute-start(bf16[256,128]{1,0:T(8,128)(2,1)} %v_hbm.3), channel_id=1, source_target_pairs={{0,2},{2,4},{4,6},{6,8},{8,10},{10,12},{12,14},{14,0},{1,3},{3,5},... | collective-permute-start | bytes 196616 | tf_op jit(solution)/shard_map/ppermute | solution.py:24
  5.0 4.5 %attend.2.rest_3_ = f32[128,1536]{1,0:T(8,128)S(1)} custom-call(s32[1]{0:T(128)} %constant.11.clone.1.first_ref, f32[1,16]{1,0:T(1,128)} %bitcast.17, bf16[256,1024]{1,0:T(8,128)(2,1)} %q_hbm.3, bf16[256,128]{1,0:T(8,128)(2,1)} %k_hbm.3, bf16[256,128]{1,0:T(8,128)(2,1)} %v_hbm.3, bf16[1024,1536]{1,0:T(8,128)(2,1)} %ow_hbm.3), custom_call_target="tpu_custom_call" | custom-call | flops 671088640 | bytes 6291456 | tf_op jit(solution)/shard_map/attend/pallas_call | solution.py:137
  9.6 1.2 %collective-permute-done.1.rest_1_ = bf16[256,128]{1,0:T(8,128)(2,1)S(1)} collective-permute-done((bf16[256,128]{1,0:T(8,128)(2,1)}, bf16[256,128]{1,0:T(8,128)(2,1)S(1)}, u32[]{:S(2)}, u32[]{:S(2)}) %collective-permute-start.1) | collective-permute-done | bytes 65568 | tf_op jit(solution)/shard_map/ppermute | solution.py:24
  10.9 4.5 %attend.3 = (bf16[128,1536]{1,0:T(8,128)(2,1)S(1)}, f32[128,1536]{1,0:T(8,128)S(1)}) custom-call(s32[1]{0:T(128)} %bitcast.first_ref, f32[1,16]{1,0:T(1,128)} %bitcast.18, bf16[256,1024]{1,0:T(8,128)(2,1)} %q_hbm.3, bf16[256,128]{1,0:T(8,128)(2,1)} %k_hbm.3, bf16[256,128]{1,0:T(8,128)(2,1)} %v_hbm.3, bf16[1024,1536]{1,0:T(8,128)(2,1)} %ow_hbm.3, ...), custom_call_target="tpu_custom_call" | custom-call | flops 671088640 | bytes 6291456 | tf_op jit(solution)/shard_map/attend/pallas_call | solution.py:137
  15.5 1.7 %collective-permute-done.2.came_ref = bf16[128,1536]{1,0:T(8,128)(2,1)S(1)} collective-permute-done((bf16[128,1536]{1,0:T(8,128)(2,1)S(1)}, bf16[128,1536]{1,0:T(8,128)(2,1)S(1)}, u32[]{:S(2)}, u32[]{:S(2)}) %collective-permute-start.2) | collective-permute-done | bytes 393248 | tf_op jit(solution)/shard_map/ppermute | solution.py:37
  17.2 0.3 norm.1
  17.7 1.9 %collective-permute-start.6 = (bf16[784,128]{1,0:T(8,128)(2,1)S(1)}, bf16[784,128]{1,0:T(8,128)(2,1)S(1)}, u32[]{:S(2)}, u32[]{:S(2)}) collective-permute-start(bf16[784,128]{1,0:T(8,128)(2,1)S(1)} %get-tuple-element.57.refs_0_), channel_id=1, source_target_pairs={{0,4},{4,8},{8,12},{12,14},{14,10},{10,6},{6,2},{2,0},{1,5},{5,9},... | collective-permute-start | bytes 602120 | tf_op jit(solution)/shard_map/out_lead1/ppermute | solution.py:324
  19.8 1.9 %collective-permute-start.9 = (bf16[784,128]{1,0:T(8,128)(2,1)S(1)}, bf16[784,128]{1,0:T(8,128)(2,1)S(1)}, u32[]{:S(2)}, u32[]{:S(2)}) collective-permute-start(bf16[784,128]{1,0:T(8,128)(2,1)S(1)} %get-tuple-element.58.refs_1_), channel_id=1, source_target_pairs={{0,4},{4,8},{8,12},{12,14},{14,10},{10,6},{6,2},{2,0},{1,5},{5,9},... | collective-permute-start | bytes 602120 | tf_op jit(solution)/shard_map/out_trail1/ppermute | solution.py:324
  21.6 6.0 %experts.6 = (bf16[64,1536]{1,0:T(8,128)(2,1)S(1)}, bf16[64,1536]{1,0:T(8,128)(2,1)S(1)}, bf16[1536,768]{1,0:T(8,128)(2,1)S(1)}, bf16[1536,768]{1,0:T(8,128)(2,1...) custom-call(s32[1]{0:T(128)} %bitcast.5.me_ref, ...), custom_call_target="tpu_custom_call" | custom-call | flops 1811939328 | bytes 1179648 | tf_op jit(solution)/shard_map/experts/pallas_call | solution.py:282
  27.9 1.9 %collective-permute-start.7 = (bf16[784,128]{1,0:T(8,128)(2,1)S(1)}, bf16[784,128]{1,0:T(8,128)(2,1)S(1)}, u32[]{:S(2)}, u32[]{:S(2)}) collective-permute-start(bf16[784,128]{1,0:T(8,128)(2,1)S(1)} %collective-permute-done.6.refs_0_), channel_id=1, source_target_pairs={{0,4},{4,8},{8,12},{12,14},{14,10},{10,6},{6,2},{2,0},{1,5},{5,9},... | collective-permute-start | bytes 602120 | tf_op jit(solution)/shard_map/out_lead2/ppermute | solution.py:324
  29.9 1.9 %collective-permute-start.13 = (bf16[784,128]{1,0:T(8,128)(2,1)S(1)}, bf16[784,128]{1,0:T(8,128)(2,1)S(1)}, u32[]{:S(2)}, u32[]{:S(2)}) collective-permute-start(bf16[784,128]{1,0:T(8,128)(2,1)S(1)} %collective-permute-done.9.refs_2_), channel_id=1, source_target_pairs={{0,4},{4,8},{8,12},{12,14},{14,10},{10,6},{6,2},{2,0},{1,5},{5,9},... | collective-permute-start | bytes 602120 | tf_op jit(solution)/shard_map/out_trail2/ppermute | solution.py:324
  31.8 3.9 %experts.7 = (bf16[64,1536]{1,0:T(8,128)(2,1)S(1)}, bf16[64,1536]{1,0:T(8,128)(2,1)S(1)}, bf16[64,1536]{1,0:T(8,128)(2,1)S(1)}, bf16[64,1536]{1,0:T(8,128)(2,1)S(1)}) custom-call(s32[1]{0:T(128)} %bitcast.5.me_ref, bf16[784,128]{1,0:T(8,128)(2,1)S(1)} %collective-permute-done.6.refs_0_, bf16[784,128]{1,0:T(8,128)(2,1)S(1)} %collective-permute-done.8.refs_1_, ...), custom_call_target="tpu_custom_call" | custom-call | flops 3623878656 | bytes 2359296 | tf_op jit(solution)/shard_map/hop1/experts/pallas_call | solution.py:282
  35.9 1.9 %collective-permute-start.11 = (bf16[784,128]{1,0:T(8,128)(2,1)S(1)}, bf16[784,128]{1,0:T(8,128)(2,1)S(1)}, u32[]{:S(2)}, u32[]{:S(2)}) collective-permute-start(bf16[784,128]{1,0:T(8,128)(2,1)S(1)} %collective-permute-done.7.refs_0_), channel_id=1, source_target_pairs={{0,4},{4,8},{8,12},{12,14},{14,10},{10,6},{6,2},{2,0},{1,5},{5,9},... | collective-permute-start | bytes 602120 | tf_op jit(solution)/shard_map/out_lead3/ppermute | solution.py:324
  37.8 1.7 %collective-permute-done.14.refs_3_ = bf16[784,128]{1,0:T(8,128)(2,1)S(1)} collective-permute-done((bf16[784,128]{1,0:T(8,128)(2,1)S(1)}, bf16[784,128]{1,0:T(8,128)(2,1)S(1)}, u32[]{:S(2)}, u32[]{:S(2)}) %collective-permute-start.14) | collective-permute-done | bytes 200736 | tf_op jit(solution)/shard_map/out_trail2/ppermute | solution.py:324
  39.5 3.9 %experts.8 = (bf16[64,1536]{1,0:T(8,128)(2,1)S(1)}, bf16[64,1536]{1,0:T(8,128)(2,1)S(1)}, bf16[64,1536]{1,0:T(8,128)(2,1)S(1)}, bf16[64,1536]{1,0:T(8,128)(2,1)S(1)}) custom-call(s32[1]{0:T(128)} %bitcast.5.me_ref, bf16[784,128]{1,0:T(8,128)(2,1)S(1)} %collective-permute-done.7.refs_0_, bf16[784,128]{1,0:T(8,128)(2,1)S(1)} %collective-permute-done.12.refs_1_, ...), custom_call_target="tpu_custom_call" | custom-call | flops 3623878656 | bytes 2359296 | tf_op jit(solution)/shard_map/hop2/experts/pallas_call | solution.py:282
  43.5 1.8 %collective-permute-start.15 = (bf16[784,128]{1,0:T(8,128)(2,1)S(1)}, bf16[784,128]{1,0:T(8,128)(2,1)S(1)}, u32[]{:S(2)}, u32[]{:S(2)}) collective-permute-start(bf16[784,128]{1,0:T(8,128)(2,1)S(1)} %collective-permute-done.11.refs_0_), channel_id=1, source_target_pairs={{0,4},{4,8},{8,12},{12,14},{14,10},{10,6},{6,2},{2,0},{1,5},{5,9},... | collective-permute-start | bytes 602120 | tf_op jit(solution)/shard_map/out_lead4/ppermute | solution.py:324
  45.5 1.5 %collective-permute-start.20 = (bf16[784,128]{1,0:T(8,128)(2,1)S(1)}, bf16[784,128]{1,0:T(8,128)(2,1)S(1)}, u32[]{:S(2)}, u32[]{:S(2)}) collective-permute-start(bf16[784,128]{1,0:T(8,128)(2,1)S(1)} %collective-permute-done.14.refs_3_), channel_id=1, source_target_pairs={{4,0},{8,4},{12,8},{14,12},{10,14},{6,10},{2,6},{0,2},{5,1},{9,5},... | collective-permute-start | bytes 602120 | tf_op jit(solution)/shard_map/out_trail3/ppermute | solution.py:324
  47.0 0.6 collective-permute-start.19
  47.6 2.1 %experts.9 = (bf16[64,1536]{1,0:T(8,128)(2,1)S(1)}, bf16[64,1536]{1,0:T(8,128)(2,1)S(1)}) custom-call(s32[1]{0:T(128)} %bitcast.5.me_ref, bf16[784,128]{1,0:T(8,128)(2,1)S(1)} %collective-permute-done.11.refs_0_, bf16[784,128]{1,0:T(8,128)(2,1)S(1)} %collective-permute-done.16.refs_1_, bf16[1536,768]{1,0:T(8,128)(2,1)S(1)} %get-tuple-element.61.refs_4_.refs_2_, ...), custom_call_target="tpu_custom_call" | custom-call | flops 1811939328 | bytes 1179648 | tf_op jit(solution)/shard_map/hop3/experts/pallas_call | solution.py:282
  49.7 0.5 collective-permute-done.15.refs_0_
  50.1 1.0 %collective-permute-done.17.refs_1_ = bf16[784,128]{1,0:T(8,128)(2,1)S(1)} collective-permute-done((bf16[784,128]{1,0:T(8,128)(2,1)S(1)}, bf16[784,128]{1,0:T(8,128)(2,1)S(1)}, u32[]{:S(2)}, u32[]{:S(2)}) %collective-permute-start.17) | collective-permute-done | bytes 200736 | tf_op jit(solution)/shard_map/out_lead4/ppermute | solution.py:324
  51.1 2.1 %experts.10 = (bf16[64,1536]{1,0:T(8,128)(2,1)S(1)}, bf16[64,1536]{1,0:T(8,128)(2,1)S(1)}) custom-call(s32[1]{0:T(128)} %bitcast.5.me_ref, bf16[784,128]{1,0:T(8,128)(2,1)S(1)} %collective-permute-done.15.refs_0_, bf16[784,128]{1,0:T(8,128)(2,1)S(1)} %collective-permute-done.17.refs_1_, bf16[1536,768]{1,0:T(8,128)(2,1)S(1)} %get-tuple-element.61.refs_4_.refs_2_, ...), custom_call_target="tpu_custom_call" | custom-call | flops 1811939328 | bytes 1179648 | tf_op jit(solution)/shard_map/hop4/experts/pallas_call | solution.py:282
  53.2 0.4 collective-permute-start.18
  53.6 0.5 collective-permute-done.19.refs_0_
  54.1 2.4 %collective-permute-start.24 = (bf16[64,1536]{1,0:T(8,128)(2,1)S(1)}, bf16[64,1536]{1,0:T(8,128)(2,1)S(1)}, u32[]{:S(2)}, u32[]{:S(2)}) collective-permute-start(bf16[64,1536]{1,0:T(8,128)(2,1)S(1)} %get-tuple-element.85), channel_id=1, source_target_pairs={{4,0},{8,4},{12,8},{14,12},{10,14},{6,10},{2,6},{0,2},{5,1},{9,5},... | collective-permute-start | bytes 589832 | tf_op jit(solution)/shard_map/back_trail3/ppermute | solution.py:363
  56.4 2.0 %collective-permute-start.30 = (bf16[64,1536]{1,0:T(8,128)(2,1)S(1)}, bf16[64,1536]{1,0:T(8,128)(2,1)S(1)}, u32[]{:S(2)}, u32[]{:S(2)}) collective-permute-start(bf16[64,1536]{1,0:T(8,128)(2,1)S(1)} %get-tuple-element.95), channel_id=1, source_target_pairs={{4,0},{8,4},{12,8},{14,12},{10,14},{6,10},{2,6},{0,2},{5,1},{9,5},... | collective-permute-start | bytes 589832 | tf_op jit(solution)/shard_map/back_lead4/ppermute | solution.py:363
  58.5 2.1 %experts.11 = (bf16[64,1536]{1,0:T(8,128)(2,1)S(1)}, bf16[64,1536]{1,0:T(8,128)(2,1)S(1)}) custom-call(s32[1]{0:T(128)} %bitcast.5.me_ref, bf16[784,128]{1,0:T(8,128)(2,1)S(1)} %collective-permute-done.19.refs_0_, bf16[784,128]{1,0:T(8,128)(2,1)S(1)} %collective-permute-done.20.refs_1_, bf16[1536,768]{1,0:T(8,128)(2,1)S(1)} %get-tuple-element.61.refs_4_.refs_2_, ...), custom_call_target="tpu_custom_call" | custom-call | flops 1811939328 | bytes 1179648 | tf_op jit(solution)/shard_map/hop3/experts/pallas_call | solution.py:282
  60.8 0.7 collective-permute-start.21
  61.7 2.5 %collective-permute-start.25 = (bf16[64,1536]{1,0:T(8,128)(2,1)S(1)}, bf16[64,1536]{1,0:T(8,128)(2,1)S(1)}, u32[]{:S(2)}, u32[]{:S(2)}) collective-permute-start(bf16[64,1536]{1,0:T(8,128)(2,1)S(1)} %add_convert_fusion.6), channel_id=1, source_target_pairs={{4,0},{8,4},{12,8},{14,12},{10,14},{6,10},{2,6},{0,2},{5,1},{9,5},... | collective-permute-start | bytes 589832 | tf_op jit(solution)/shard_map/back_trail2/ppermute | solution.py:363
  64.3 0.7 collective-permute-done.27
  65.0 0.7 collective-permute-start.28
  66.0 2.5 %collective-permute-start.31 = (bf16[64,1536]{1,0:T(8,128)(2,1)S(1)}, bf16[64,1536]{1,0:T(8,128)(2,1)S(1)}, u32[]{:S(2)}, u32[]{:S(2)}) collective-permute-start(bf16[64,1536]{1,0:T(8,128)(2,1)S(1)} %add_convert_fusion.2), channel_id=1, source_target_pairs={{4,0},{8,4},{12,8},{14,12},{10,14},{6,10},{2,6},{0,2},{5,1},{9,5},... | collective-permute-start | bytes 589832 | tf_op jit(solution)/shard_map/back_lead3/ppermute | solution.py:363
  68.5 0.7 collective-permute-done.21
  69.2 0.7 collective-permute-start.22
  70.2 2.5 %collective-permute-start.26 = (bf16[64,1536]{1,0:T(8,128)(2,1)S(1)}, bf16[64,1536]{1,0:T(8,128)(2,1)S(1)}, u32[]{:S(2)}, u32[]{:S(2)}) collective-permute-start(bf16[64,1536]{1,0:T(8,128)(2,1)S(1)} %add_convert_fusion.5), channel_id=1, source_target_pairs={{4,0},{8,4},{12,8},{14,12},{10,14},{6,10},{2,6},{0,2},{5,1},{9,5},... | collective-permute-start | bytes 589832 | tf_op jit(solution)/shard_map/back_trail1/ppermute | solution.py:363
  72.7 0.7 collective-permute-done.28
  73.4 0.7 collective-permute-start.29
  74.3 1.9 %collective-permute-start.32 = (bf16[64,1536]{1,0:T(8,128)(2,1)S(1)}, bf16[64,1536]{1,0:T(8,128)(2,1)S(1)}, u32[]{:S(2)}, u32[]{:S(2)}) collective-permute-start(bf16[64,1536]{1,0:T(8,128)(2,1)S(1)} %add_convert_fusion.1), channel_id=1, source_target_pairs={{4,0},{8,4},{12,8},{14,12},{10,14},{6,10},{2,6},{0,2},{5,1},{9,5},... | collective-permute-start | bytes 589832 | tf_op jit(solution)/shard_map/back_lead2/ppermute | solution.py:363
  76.2 1.4 %collective-permute-done.22 = bf16[64,1536]{1,0:T(8,128)(2,1)S(1)} collective-permute-done((bf16[64,1536]{1,0:T(8,128)(2,1)S(1)}, bf16[64,1536]{1,0:T(8,128)(2,1)S(1)}, u32[]{:S(2)}, u32[]{:S(2)}) %collective-permute-start.22) | collective-permute-done | bytes 196640 | tf_op jit(solution)/shard_map/back_lead2/ppermute | solution.py:363
  77.7 0.7 collective-permute-start.23
  78.4 3.4 %collective-permute-done.32 = bf16[64,1536]{1,0:T(8,128)(2,1)S(1)} collective-permute-done((bf16[64,1536]{1,0:T(8,128)(2,1)S(1)}, bf16[64,1536]{1,0:T(8,128)(2,1)S(1)}, u32[]{:S(2)}, u32[]{:S(2)}) %collective-permute-start.32) | collective-permute-done | bytes 196640 | tf_op jit(solution)/shard_map/back_lead2/ppermute | solution.py:363
  81.8 0.9 collective-permute-start.33
  82.7 0.7 collective-permute-done.23
  83.5 4.1 %collective-permute-done.33 = bf16[64,1536]{1,0:T(8,128)(2,1)S(1)} collective-permute-done((bf16[64,1536]{1,0:T(8,128)(2,1)S(1)}, bf16[64,1536]{1,0:T(8,128)(2,1)S(1)}, u32[]{:S(2)}, u32[]{:S(2)}) %collective-permute-start.33) | collective-permute-done | bytes 196640 | tf_op jit(solution)/shard_map/back_lead1/ppermute | solution.py:363
  87.6 0.8 fusion
  (53 shorter events, 2.9 us)
Async XLA Ops:
  0.0 17.5 %collective-permute-start.3 = (bf16[1536,768]{1,0:T(8,128)(2,1)}, bf16[1536,768]{1,0:T(8,128)(2,1)S(1)}, u32[]{:S(2)}, u32[]{:S(2)}) collective-permute-start(bf16[1536,768]{1,0:T(8,128)(2,1)} %bitcast.11), channel_id=1, source_target_pairs={{0,1},{1,0},{2,3},{3,2},{4,5},{5,4},{6,7},{7,6},{8,9},{9,8},{10,11... | collective-permute-start | bytes 7077896 | tf_op jit(solution)/shard_map/ppermute | solution.py:37
  0.5 17.1 %collective-permute-start.4 = (bf16[1536,768]{1,0:T(8,128)(2,1)}, bf16[1536,768]{1,0:T(8,128)(2,1)}, u32[]{:S(2)}, u32[]{:S(2)}) collective-permute-start(bf16[1536,768]{1,0:T(8,128)(2,1)} %bitcast.13), channel_id=1, source_target_pairs={{0,1},{1,0},{2,3},{3,2},{4,5},{5,4},{6,7},{7,6},{8,9},{9,8},{10,11... | collective-permute-start | bytes 7077896 | tf_op jit(solution)/shard_map/ppermute | solution.py:37
  0.5 17.0 %collective-permute-start.5 = (bf16[768,1536]{1,0:T(8,128)(2,1)}, bf16[768,1536]{1,0:T(8,128)(2,1)}, u32[]{:S(2)}, u32[]{:S(2)}) collective-permute-start(bf16[768,1536]{1,0:T(8,128)(2,1)} %bitcast.15), channel_id=1, source_target_pairs={{0,1},{1,0},{2,3},{3,2},{4,5},{5,4},{6,7},{7,6},{8,9},{9,8},{10,11... | collective-permute-start | bytes 7077896 | tf_op jit(solution)/shard_map/ppermute | solution.py:37
  1.0 8.7 %collective-permute-start = (bf16[256,128]{1,0:T(8,128)(2,1)}, bf16[256,128]{1,0:T(8,128)(2,1)S(1)}, u32[]{:S(2)}, u32[]{:S(2)}) collective-permute-start(bf16[256,128]{1,0:T(8,128)(2,1)} %k_hbm.3), channel_id=1, source_target_pairs={{0,2},{2,4},{4,6},{6,8},{8,10},{10,12},{12,14},{14,0},{1,3},{3,5},... | collective-permute-start | bytes 196616 | tf_op jit(solution)/shard_map/ppermute | solution.py:24
  3.5 7.4 %collective-permute-start.1 = (bf16[256,128]{1,0:T(8,128)(2,1)}, bf16[256,128]{1,0:T(8,128)(2,1)S(1)}, u32[]{:S(2)}, u32[]{:S(2)}) collective-permute-start(bf16[256,128]{1,0:T(8,128)(2,1)} %v_hbm.3), channel_id=1, source_target_pairs={{0,2},{2,4},{4,6},{6,8},{8,10},{10,12},{12,14},{14,0},{1,3},{3,5},... | collective-permute-start | bytes 196616 | tf_op jit(solution)/shard_map/ppermute | solution.py:24
  10.9 4.6 %copy-start.4 = (f32[1536]{0:T(1024)S(1)}, f32[1536]{0:T(1024)}, u32[]{:S(2)}) copy-start(f32[1536]{0:T(1024)} %param.18) | copy-start | bytes 18436
  10.9 6.3 %copy-start = (bf16[128,1536]{1,0:T(8,128)(2,1)S(1)}, bf16[128,1536]{1,0:T(8,128)(2,1)}, u32[]{:S(2)}) copy-start(bf16[128,1536]{1,0:T(8,128)(2,1)} %stream_ref.1) | copy-start | bytes 1179652
  10.9 6.3 %copy-start.1 = (s32[128,4]{0,1:T(4,128)S(1)}, s32[128,4]{0,1:T(4,128)}, u32[]{:S(2)}) copy-start(s32[128,4]{0,1:T(4,128)} %param.19) | copy-start | bytes 6148
  10.9 6.3 %copy-start.2 = (f32[128,4]{0,1:T(4,128)S(1)}, f32[128,4]{0,1:T(4,128)}, u32[]{:S(2)}) copy-start(f32[128,4]{0,1:T(4,128)} %param.20) | copy-start | bytes 6148
  15.4 1.8 %collective-permute-start.2 = (bf16[128,1536]{1,0:T(8,128)(2,1)S(1)}, bf16[128,1536]{1,0:T(8,128)(2,1)S(1)}, u32[]{:S(2)}, u32[]{:S(2)}) collective-permute-start(bf16[128,1536]{1,0:T(8,128)(2,1)S(1)} %get-tuple-element.53), channel_id=1, source_target_pairs={{0,1},{1,0},{2,3},{3,2},{4,5},{5,4},{6,7},{7,6},{8,9},{9,8},{10,11... | collective-permute-start | bytes 1179656 | tf_op jit(solution)/shard_map/ppermute | solution.py:37
  17.5 4.1 %copy-start.3 = (bf16[1536,768]{1,0:T(8,128)(2,1)}, bf16[1536,768]{1,0:T(8,128)(2,1)S(1)}, u32[]{:S(2)}) copy-start(bf16[1536,768]{1,0:T(8,128)(2,1)S(1)} %collective-permute-done.3.refs_5_) | copy-start | bytes 7077892
  17.5 10.1 %collective-permute-start.8 = (bf16[784,128]{1,0:T(8,128)(2,1)S(1)}, bf16[784,128]{1,0:T(8,128)(2,1)S(1)}, u32[]{:S(2)}, u32[]{:S(2)}) collective-permute-start(bf16[784,128]{1,0:T(8,128)(2,1)S(1)} %get-tuple-element.58.refs_1_), channel_id=1, source_target_pairs={{4,0},{8,4},{12,8},{14,12},{10,14},{6,10},{2,6},{0,2},{5,1},{9,5},... | collective-permute-start | bytes 602120 | tf_op jit(solution)/shard_map/out_lead1/ppermute | solution.py:324
  17.7 10.1 %collective-permute-start.6 = (bf16[784,128]{1,0:T(8,128)(2,1)S(1)}, bf16[784,128]{1,0:T(8,128)(2,1)S(1)}, u32[]{:S(2)}, u32[]{:S(2)}) collective-permute-start(bf16[784,128]{1,0:T(8,128)(2,1)S(1)} %get-tuple-element.57.refs_0_), channel_id=1, source_target_pairs={{0,4},{4,8},{8,12},{12,14},{14,10},{10,6},{6,2},{2,0},{1,5},{5,9},... | collective-permute-start | bytes 602120 | tf_op jit(solution)/shard_map/out_lead1/ppermute | solution.py:324
  19.6 10.1 %collective-permute-start.10 = (bf16[784,128]{1,0:T(8,128)(2,1)S(1)}, bf16[784,128]{1,0:T(8,128)(2,1)S(1)}, u32[]{:S(2)}, u32[]{:S(2)}) collective-permute-start(bf16[784,128]{1,0:T(8,128)(2,1)S(1)} %get-tuple-element.57.refs_0_), channel_id=1, source_target_pairs={{4,0},{8,4},{12,8},{14,12},{10,14},{6,10},{2,6},{0,2},{5,1},{9,5},... | collective-permute-start | bytes 602120 | tf_op jit(solution)/shard_map/out_trail1/ppermute | solution.py:324
  19.8 10.1 %collective-permute-start.9 = (bf16[784,128]{1,0:T(8,128)(2,1)S(1)}, bf16[784,128]{1,0:T(8,128)(2,1)S(1)}, u32[]{:S(2)}, u32[]{:S(2)}) collective-permute-start(bf16[784,128]{1,0:T(8,128)(2,1)S(1)} %get-tuple-element.58.refs_1_), channel_id=1, source_target_pairs={{0,4},{4,8},{8,12},{12,14},{14,10},{10,6},{6,2},{2,0},{1,5},{5,9},... | collective-permute-start | bytes 602120 | tf_op jit(solution)/shard_map/out_trail1/ppermute | solution.py:324
  27.7 8.0 %collective-permute-start.12 = (bf16[784,128]{1,0:T(8,128)(2,1)S(1)}, bf16[784,128]{1,0:T(8,128)(2,1)S(1)}, u32[]{:S(2)}, u32[]{:S(2)}) collective-permute-start(bf16[784,128]{1,0:T(8,128)(2,1)S(1)} %collective-permute-done.8.refs_1_), channel_id=1, source_target_pairs={{4,0},{8,4},{12,8},{14,12},{10,14},{6,10},{2,6},{0,2},{5,1},{9,5},... | collective-permute-start | bytes 602120 | tf_op jit(solution)/shard_map/out_lead2/ppermute | solution.py:324
  27.9 8.0 %collective-permute-start.7 = (bf16[784,128]{1,0:T(8,128)(2,1)S(1)}, bf16[784,128]{1,0:T(8,128)(2,1)S(1)}, u32[]{:S(2)}, u32[]{:S(2)}) collective-permute-start(bf16[784,128]{1,0:T(8,128)(2,1)S(1)} %collective-permute-done.6.refs_0_), channel_id=1, source_target_pairs={{0,4},{4,8},{8,12},{12,14},{14,10},{10,6},{6,2},{2,0},{1,5},{5,9},... | collective-permute-start | bytes 602120 | tf_op jit(solution)/shard_map/out_lead2/ppermute | solution.py:324
  29.7 9.8 %collective-permute-start.14 = (bf16[784,128]{1,0:T(8,128)(2,1)S(1)}, bf16[784,128]{1,0:T(8,128)(2,1)S(1)}, u32[]{:S(2)}, u32[]{:S(2)}) collective-permute-start(bf16[784,128]{1,0:T(8,128)(2,1)S(1)} %collective-permute-done.10.refs_3_), channel_id=1, source_target_pairs={{4,0},{8,4},{12,8},{14,12},{10,14},{6,10},{2,6},{0,2},{5,1},{9,5},... | collective-permute-start | bytes 602120 | tf_op jit(solution)/shard_map/out_trail2/ppermute | solution.py:324
  29.9 9.6 %collective-permute-start.13 = (bf16[784,128]{1,0:T(8,128)(2,1)S(1)}, bf16[784,128]{1,0:T(8,128)(2,1)S(1)}, u32[]{:S(2)}, u32[]{:S(2)}) collective-permute-start(bf16[784,128]{1,0:T(8,128)(2,1)S(1)} %collective-permute-done.9.refs_2_), channel_id=1, source_target_pairs={{0,4},{4,8},{8,12},{12,14},{14,10},{10,6},{6,2},{2,0},{1,5},{5,9},... | collective-permute-start | bytes 602120 | tf_op jit(solution)/shard_map/out_trail2/ppermute | solution.py:324
  35.7 9.6 %collective-permute-start.16 = (bf16[784,128]{1,0:T(8,128)(2,1)S(1)}, bf16[784,128]{1,0:T(8,128)(2,1)S(1)}, u32[]{:S(2)}, u32[]{:S(2)}) collective-permute-start(bf16[784,128]{1,0:T(8,128)(2,1)S(1)} %collective-permute-done.12.refs_1_), channel_id=1, source_target_pairs={{4,0},{8,4},{12,8},{14,12},{10,14},{6,10},{2,6},{0,2},{5,1},{9,5},... | collective-permute-start | bytes 602120 | tf_op jit(solution)/shard_map/out_lead3/ppermute | solution.py:324
  35.9 7.5 %collective-permute-start.11 = (bf16[784,128]{1,0:T(8,128)(2,1)S(1)}, bf16[784,128]{1,0:T(8,128)(2,1)S(1)}, u32[]{:S(2)}, u32[]{:S(2)}) collective-permute-start(bf16[784,128]{1,0:T(8,128)(2,1)S(1)} %collective-permute-done.7.refs_0_), channel_id=1, source_target_pairs={{0,4},{4,8},{8,12},{12,14},{14,10},{10,6},{6,2},{2,0},{1,5},{5,9},... | collective-permute-start | bytes 602120 | tf_op jit(solution)/shard_map/out_lead3/ppermute | solution.py:324
  43.5 6.7 %collective-permute-start.15 = (bf16[784,128]{1,0:T(8,128)(2,1)S(1)}, bf16[784,128]{1,0:T(8,128)(2,1)S(1)}, u32[]{:S(2)}, u32[]{:S(2)}) collective-permute-start(bf16[784,128]{1,0:T(8,128)(2,1)S(1)} %collective-permute-done.11.refs_0_), channel_id=1, source_target_pairs={{0,4},{4,8},{8,12},{12,14},{14,10},{10,6},{6,2},{2,0},{1,5},{5,9},... | collective-permute-start | bytes 602120 | tf_op jit(solution)/shard_map/out_lead4/ppermute | solution.py:324
  45.3 5.9 %collective-permute-start.17 = (bf16[784,128]{1,0:T(8,128)(2,1)S(1)}, bf16[784,128]{1,0:T(8,128)(2,1)S(1)}, u32[]{:S(2)}, u32[]{:S(2)}) collective-permute-start(bf16[784,128]{1,0:T(8,128)(2,1)S(1)} %collective-permute-done.16.refs_1_), channel_id=1, source_target_pairs={{4,0},{8,4},{12,8},{14,12},{10,14},{6,10},{2,6},{0,2},{5,1},{9,5},... | collective-permute-start | bytes 602120 | tf_op jit(solution)/shard_map/out_lead4/ppermute | solution.py:324
  45.5 12.9 %collective-permute-start.20 = (bf16[784,128]{1,0:T(8,128)(2,1)S(1)}, bf16[784,128]{1,0:T(8,128)(2,1)S(1)}, u32[]{:S(2)}, u32[]{:S(2)}) collective-permute-start(bf16[784,128]{1,0:T(8,128)(2,1)S(1)} %collective-permute-done.14.refs_3_), channel_id=1, source_target_pairs={{4,0},{8,4},{12,8},{14,12},{10,14},{6,10},{2,6},{0,2},{5,1},{9,5},... | collective-permute-start | bytes 602120 | tf_op jit(solution)/shard_map/out_trail3/ppermute | solution.py:324
  47.0 7.1 %collective-permute-start.19 = (bf16[784,128]{1,0:T(8,128)(2,1)S(1)}, bf16[784,128]{1,0:T(8,128)(2,1)S(1)}, u32[]{:S(2)}, u32[]{:S(2)}) collective-permute-start(bf16[784,128]{1,0:T(8,128)(2,1)S(1)} %collective-permute-done.13.refs_2_), channel_id=1, source_target_pairs={{0,4},{4,8},{8,12},{12,14},{14,10},{10,6},{6,2},{2,0},{1,5},{5,9},... | collective-permute-start | bytes 602120 | tf_op jit(solution)/shard_map/out_trail3/ppermute | solution.py:324
  53.2 7.5 %collective-permute-start.18 = (bf16[64,1536]{1,0:T(8,128)(2,1)S(1)}, bf16[64,1536]{1,0:T(8,128)(2,1)S(1)}, u32[]{:S(2)}, u32[]{:S(2)}) collective-permute-start(bf16[64,1536]{1,0:T(8,128)(2,1)S(1)} %get-tuple-element.78), channel_id=1, source_target_pairs={{0,4},{4,8},{8,12},{12,14},{14,10},{10,6},{6,2},{2,0},{1,5},{5,9},... | collective-permute-start | bytes 589832 | tf_op jit(solution)/shard_map/back_lead4/ppermute | solution.py:363
  54.1 7.6 %collective-permute-start.24 = (bf16[64,1536]{1,0:T(8,128)(2,1)S(1)}, bf16[64,1536]{1,0:T(8,128)(2,1)S(1)}, u32[]{:S(2)}, u32[]{:S(2)}) collective-permute-start(bf16[64,1536]{1,0:T(8,128)(2,1)S(1)} %get-tuple-element.85), channel_id=1, source_target_pairs={{4,0},{8,4},{12,8},{14,12},{10,14},{6,10},{2,6},{0,2},{5,1},{9,5},... | collective-permute-start | bytes 589832 | tf_op jit(solution)/shard_map/back_trail3/ppermute | solution.py:363
  56.4 8.5 %collective-permute-start.27 = (bf16[64,1536]{1,0:T(8,128)(2,1)S(1)}, bf16[64,1536]{1,0:T(8,128)(2,1)S(1)}, u32[]{:S(2)}, u32[]{:S(2)}) collective-permute-start(bf16[64,1536]{1,0:T(8,128)(2,1)S(1)} %get-tuple-element.90), channel_id=1, source_target_pairs={{0,4},{4,8},{8,12},{12,14},{14,10},{10,6},{6,2},{2,0},{1,5},{5,9},... | collective-permute-start | bytes 589832 | tf_op jit(solution)/shard_map/back_trail3/ppermute | solution.py:363
  56.4 9.5 %collective-permute-start.30 = (bf16[64,1536]{1,0:T(8,128)(2,1)S(1)}, bf16[64,1536]{1,0:T(8,128)(2,1)S(1)}, u32[]{:S(2)}, u32[]{:S(2)}) collective-permute-start(bf16[64,1536]{1,0:T(8,128)(2,1)S(1)} %get-tuple-element.95), channel_id=1, source_target_pairs={{4,0},{8,4},{12,8},{14,12},{10,14},{6,10},{2,6},{0,2},{5,1},{9,5},... | collective-permute-start | bytes 589832 | tf_op jit(solution)/shard_map/back_lead4/ppermute | solution.py:363
  60.8 8.4 %collective-permute-start.21 = (bf16[64,1536]{1,0:T(8,128)(2,1)S(1)}, bf16[64,1536]{1,0:T(8,128)(2,1)S(1)}, u32[]{:S(2)}, u32[]{:S(2)}) collective-permute-start(bf16[64,1536]{1,0:T(8,128)(2,1)S(1)} %add_convert_fusion.9), channel_id=1, source_target_pairs={{0,4},{4,8},{8,12},{12,14},{14,10},{10,6},{6,2},{2,0},{1,5},{5,9},... | collective-permute-start | bytes 589832 | tf_op jit(solution)/shard_map/back_lead3/ppermute | solution.py:363
  61.7 8.4 %collective-permute-start.25 = (bf16[64,1536]{1,0:T(8,128)(2,1)S(1)}, bf16[64,1536]{1,0:T(8,128)(2,1)S(1)}, u32[]{:S(2)}, u32[]{:S(2)}) collective-permute-start(bf16[64,1536]{1,0:T(8,128)(2,1)S(1)} %add_convert_fusion.6), channel_id=1, source_target_pairs={{4,0},{8,4},{12,8},{14,12},{10,14},{6,10},{2,6},{0,2},{5,1},{9,5},... | collective-permute-start | bytes 589832 | tf_op jit(solution)/shard_map/back_trail2/ppermute | solution.py:363
  65.0 8.4 %collective-permute-start.28 = (bf16[64,1536]{1,0:T(8,128)(2,1)S(1)}, bf16[64,1536]{1,0:T(8,128)(2,1)S(1)}, u32[]{:S(2)}, u32[]{:S(2)}) collective-permute-start(bf16[64,1536]{1,0:T(8,128)(2,1)S(1)} %add_convert_fusion.4), channel_id=1, source_target_pairs={{0,4},{4,8},{8,12},{12,14},{14,10},{10,6},{6,2},{2,0},{1,5},{5,9},... | collective-permute-start | bytes 589832 | tf_op jit(solution)/shard_map/back_trail2/ppermute | solution.py:363
  66.0 8.3 %collective-permute-start.31 = (bf16[64,1536]{1,0:T(8,128)(2,1)S(1)}, bf16[64,1536]{1,0:T(8,128)(2,1)S(1)}, u32[]{:S(2)}, u32[]{:S(2)}) collective-permute-start(bf16[64,1536]{1,0:T(8,128)(2,1)S(1)} %add_convert_fusion.2), channel_id=1, source_target_pairs={{4,0},{8,4},{12,8},{14,12},{10,14},{6,10},{2,6},{0,2},{5,1},{9,5},... | collective-permute-start | bytes 589832 | tf_op jit(solution)/shard_map/back_lead3/ppermute | solution.py:363
  69.2 8.4 %collective-permute-start.22 = (bf16[64,1536]{1,0:T(8,128)(2,1)S(1)}, bf16[64,1536]{1,0:T(8,128)(2,1)S(1)}, u32[]{:S(2)}, u32[]{:S(2)}) collective-permute-start(bf16[64,1536]{1,0:T(8,128)(2,1)S(1)} %add_convert_fusion.8), channel_id=1, source_target_pairs={{0,4},{4,8},{8,12},{12,14},{14,10},{10,6},{6,2},{2,0},{1,5},{5,9},... | collective-permute-start | bytes 589832 | tf_op jit(solution)/shard_map/back_lead2/ppermute | solution.py:363
  70.2 12.5 %collective-permute-start.26 = (bf16[64,1536]{1,0:T(8,128)(2,1)S(1)}, bf16[64,1536]{1,0:T(8,128)(2,1)S(1)}, u32[]{:S(2)}, u32[]{:S(2)}) collective-permute-start(bf16[64,1536]{1,0:T(8,128)(2,1)S(1)} %add_convert_fusion.5), channel_id=1, source_target_pairs={{4,0},{8,4},{12,8},{14,12},{10,14},{6,10},{2,6},{0,2},{5,1},{9,5},... | collective-permute-start | bytes 589832 | tf_op jit(solution)/shard_map/back_trail1/ppermute | solution.py:363
  73.4 10.0 %collective-permute-start.29 = (bf16[64,1536]{1,0:T(8,128)(2,1)S(1)}, bf16[64,1536]{1,0:T(8,128)(2,1)S(1)}, u32[]{:S(2)}, u32[]{:S(2)}) collective-permute-start(bf16[64,1536]{1,0:T(8,128)(2,1)S(1)} %add_convert_fusion.3), channel_id=1, source_target_pairs={{0,4},{4,8},{8,12},{12,14},{14,10},{10,6},{6,2},{2,0},{1,5},{5,9},... | collective-permute-start | bytes 589832 | tf_op jit(solution)/shard_map/back_trail1/ppermute | solution.py:363
  74.3 7.5 %collective-permute-start.32 = (bf16[64,1536]{1,0:T(8,128)(2,1)S(1)}, bf16[64,1536]{1,0:T(8,128)(2,1)S(1)}, u32[]{:S(2)}, u32[]{:S(2)}) collective-permute-start(bf16[64,1536]{1,0:T(8,128)(2,1)S(1)} %add_convert_fusion.1), channel_id=1, source_target_pairs={{4,0},{8,4},{12,8},{14,12},{10,14},{6,10},{2,6},{0,2},{5,1},{9,5},... | collective-permute-start | bytes 589832 | tf_op jit(solution)/shard_map/back_lead2/ppermute | solution.py:363
  77.7 5.7 %collective-permute-start.23 = (bf16[64,1536]{1,0:T(8,128)(2,1)S(1)}, bf16[64,1536]{1,0:T(8,128)(2,1)S(1)}, u32[]{:S(2)}, u32[]{:S(2)}) collective-permute-start(bf16[64,1536]{1,0:T(8,128)(2,1)S(1)} %add_convert_fusion.7), channel_id=1, source_target_pairs={{0,4},{4,8},{8,12},{12,14},{14,10},{10,6},{6,2},{2,0},{1,5},{5,9},... | collective-permute-start | bytes 589832 | tf_op jit(solution)/shard_map/back_lead1/ppermute | solution.py:363
  81.8 5.7 %collective-permute-start.33 = (bf16[64,1536]{1,0:T(8,128)(2,1)S(1)}, bf16[64,1536]{1,0:T(8,128)(2,1)S(1)}, u32[]{:S(2)}, u32[]{:S(2)}) collective-permute-start(bf16[64,1536]{1,0:T(8,128)(2,1)S(1)} %add_convert_fusion), channel_id=1, source_target_pairs={{4,0},{8,4},{12,8},{14,12},{10,14},{6,10},{2,6},{0,2},{5,1},{9,5},... | collective-permute-start | bytes 589832 | tf_op jit(solution)/shard_map/back_lead1/ppermute | solution.py:363

commit v6 on v5

--- a/solution.py
+++ b/solution.py
@@ -313,7 +313,6 @@
     outs = experts(pieces, me, halves, load=True)
     halves = outs[2:]
     keep([(0, 0, 0), (0, 0, 1)], outs)
-    worked = {0: outs[0]}
     came = {(side, 0, piece): pieces[piece] for side in sides for piece in sides}
 
     def bring(distance, lead, *after):
@@ -326,27 +325,31 @@
     def apply(distance, kinds, *after):
         keys = [(side, distance, side if lead else 1 - side) for lead in kinds for side in sides]
         blocks = [came[key] for key in keys]
-        if after:
-            blocks[0] = tied(blocks[0], *after)
+        blocks[0] = tied(blocks[0], *after)
         with jax.named_scope(f"hop{distance}"):
             outs = experts(blocks, me, halves)
-        worked[distance] = outs[0]
         keep(keys, outs)
-
+        return outs[0]
+
+    worked = earlier = outs[0]
     for distance in range(1, far + 1):
-        bring(distance, True, *([worked[distance - 2]] if distance > 1 else []))
-        if distance < far:
+        bring(distance, True, *([earlier] if distance > 1 else []))
+        earlier = worked
+        if distance == far:
+            bring(far - 1, False, *[came[side, far - 1, side] for side in sides])
+            worked = apply(far - 1, (True,), worked)
+            worked = apply(far, (True,), worked)
+        elif distance < far - 1:
             bring(
                 distance,
                 False,
                 *([came[side, distance - 1, side] for side in sides] if distance > 1 else []),
             )
-        if distance < far - 1:
-            apply(distance, (True, False))
-        elif distance < far:
-            apply(distance, (True,), worked[distance - 1])
-    apply(far, (True,), worked[far - 1])
-    apply(far - 1, (False,), worked[far])
+            kinds = (True, False) if distance < far - 2 else (True,)
+            trail = [came[side, distance, 1 - side] for side in sides] if distance > 1 else []
+            worked = apply(distance, kinds, worked, *trail)
+    worked = apply(far - 1, (False,), worked)
+    worked = apply(far - 2, (False,), worked)
 
     moving = {}
 
@@ -364,10 +367,12 @@
 
     for distance in range(far, 0, -1):
         if distance == far:
-            send(far - 1, False, *[came[side, far, side] for side in sides])
-        elif distance > 1:
-            send(distance - 1, False, worked[far] if distance == far - 1 else moving[0, 0])
+            send(far, True)
+            send(far - 1, False, worked, *[moving[side, side] for side in sides])
+            continue
         send(distance, True)
+        if distance > 1:
+            send(distance - 1, False, moving[0, 0])
     final = []
     for piece in sides:
         total = given[0, piece].astype(jnp.float32)

time: 88.6 us -> 90.2 us (1.018)
  waiting for transfers between devices: 19 us -> 24.6 us
  starting transfers between devices: 38.3 us -> 34 us
    ppermute x14, waiting for transfers between devices: 12.3 us -> 16.9 us  [send(): moving[side, piece] = lax.ppermute(value, 'seq', hops[side])]
    ppermute x14, starting transfers between devices: 18.9 us -> 14.5 us  [send(): moving[side, piece] = lax.ppermute(value, 'seq', hops[side])]
    ppermute x14, waiting for transfers between devices: 3.66 us -> 4.63 us  [bring(): came[side, distance, piece] = lax.ppermute(block, 'seq', hops[side])]
    pallas_call x6 -> x7, Pallas kernels: 20.1 us -> 20.4 us  [experts(): pl.pallas_call(functools.partial(expert_kernel, min(256, half), len(block...]
  transfers between devices with their start and end apart: 34 -> 34, of which waited for: 19 -> 18; matrix products, arithmetic and copies ran while one was open for 1% -> 1% of each run, Pallas kernels for 33% -> 33%
where the time goes in v6:
time: 90.2 us; the launch traced here: 90.1 us
  starting transfers between devices  34 us (38%)
  Pallas kernels  29.7 us (33%)
  waiting for transfers between devices  24.6 us (27%)
  other arithmetic  1.46 us (2%)
    pallas_call x7, Pallas kernels, experts(): pl.pallas_call(functools.partial(expert_kernel, min(256, half), len(block...  20.4 us
    ppermute x14, waiting for transfers between devices, send(): moving[side, piece] = lax.ppermute(value, 'seq', hops[side])  16.9 us
    ppermute x14, starting transfers between devices, send(): moving[side, piece] = lax.ppermute(value, 'seq', hops[side])  14.5 us
    ppermute x14, starting transfers between devices, bring(): came[side, distance, piece] = lax.ppermute(block, 'seq', hops[side])  14.4 us
    pallas_call x2, Pallas kernels, attend(): pl.pallas_call(functools.partial(attend_kernel, half, mix), in_specs=[sme...  8.99 us
    ppermute x14, waiting for transfers between devices, bring(): came[side, distance, piece] = lax.ppermute(block, 'seq', hops[side])  4.63 us
    ppermute x2, starting transfers between devices, shifted(): lax.ppermute(value, axis, [(i, (i + by) % peers) for i in range(peers)])  4.04 us
  transfers between devices with their start and end apart: 34, of which 18 were waited for; matrix products, arithmetic and copies ran while one was open for 1% of the time, Pallas kernels for 33%

profile of v6, /device:TPU:0, one launch (start us, length us, event | category | flops | bytes accessed | tf_op | source)
XLA Modules:
  0.0 90.1 jit_solution(16000010215468864402)
XLA Ops:
  1.0 2.5 %collective-permute-start = (bf16[256,128]{1,0:T(8,128)(2,1)}, bf16[256,128]{1,0:T(8,128)(2,1)S(1)}, u32[]{:S(2)}, u32[]{:S(2)}) collective-permute-start(bf16[256,128]{1,0:T(8,128)(2,1)} %k_hbm.3), channel_id=1, source_target_pairs={{0,2},{2,4},{4,6},{6,8},{8,10},{10,12},{12,14},{14,0},{1,3},{3,5},... | collective-permute-start | bytes 196616 | tf_op jit(solution)/shard_map/ppermute | solution.py:24
  3.5 1.5 %collective-permute-start.1 = (bf16[256,128]{1,0:T(8,128)(2,1)}, bf16[256,128]{1,0:T(8,128)(2,1)S(1)}, u32[]{:S(2)}, u32[]{:S(2)}) collective-permute-start(bf16[256,128]{1,0:T(8,128)(2,1)} %v_hbm.3), channel_id=1, source_target_pairs={{0,2},{2,4},{4,6},{6,8},{8,10},{10,12},{12,14},{14,0},{1,3},{3,5},... | collective-permute-start | bytes 196616 | tf_op jit(solution)/shard_map/ppermute | solution.py:24
  5.0 4.5 %attend.2.rest_3_ = f32[128,1536]{1,0:T(8,128)S(1)} custom-call(s32[1]{0:T(128)} %constant.11.clone.1.first_ref, f32[1,16]{1,0:T(1,128)} %bitcast.17, bf16[256,1024]{1,0:T(8,128)(2,1)} %q_hbm.3, bf16[256,128]{1,0:T(8,128)(2,1)} %k_hbm.3, bf16[256,128]{1,0:T(8,128)(2,1)} %v_hbm.3, bf16[1024,1536]{1,0:T(8,128)(2,1)} %ow_hbm.3), custom_call_target="tpu_custom_call" | custom-call | flops 671088640 | bytes 6291456 | tf_op jit(solution)/shard_map/attend/pallas_call | solution.py:137
  9.6 1.2 %collective-permute-done.1.rest_1_ = bf16[256,128]{1,0:T(8,128)(2,1)S(1)} collective-permute-done((bf16[256,128]{1,0:T(8,128)(2,1)}, bf16[256,128]{1,0:T(8,128)(2,1)S(1)}, u32[]{:S(2)}, u32[]{:S(2)}) %collective-permute-start.1) | collective-permute-done | bytes 65568 | tf_op jit(solution)/shard_map/ppermute | solution.py:24
  10.9 4.5 %attend.3 = (bf16[128,1536]{1,0:T(8,128)(2,1)S(1)}, f32[128,1536]{1,0:T(8,128)S(1)}) custom-call(s32[1]{0:T(128)} %bitcast.first_ref, f32[1,16]{1,0:T(1,128)} %bitcast.18, bf16[256,1024]{1,0:T(8,128)(2,1)} %q_hbm.3, bf16[256,128]{1,0:T(8,128)(2,1)} %k_hbm.3, bf16[256,128]{1,0:T(8,128)(2,1)} %v_hbm.3, bf16[1024,1536]{1,0:T(8,128)(2,1)} %ow_hbm.3, ...), custom_call_target="tpu_custom_call" | custom-call | flops 671088640 | bytes 6291456 | tf_op jit(solution)/shard_map/attend/pallas_call | solution.py:137
  15.5 1.7 %collective-permute-done.2.came_ref = bf16[128,1536]{1,0:T(8,128)(2,1)S(1)} collective-permute-done((bf16[128,1536]{1,0:T(8,128)(2,1)S(1)}, bf16[128,1536]{1,0:T(8,128)(2,1)S(1)}, u32[]{:S(2)}, u32[]{:S(2)}) %collective-permute-start.2) | collective-permute-done | bytes 393248 | tf_op jit(solution)/shard_map/ppermute | solution.py:37
  17.8 1.8 %collective-permute-start.8 = (bf16[784,128]{1,0:T(8,128)(2,1)S(1)}, bf16[784,128]{1,0:T(8,128)(2,1)S(1)}, u32[]{:S(2)}, u32[]{:S(2)}) collective-permute-start(bf16[784,128]{1,0:T(8,128)(2,1)S(1)} %get-tuple-element.60.refs_1_), channel_id=1, source_target_pairs={{4,0},{8,4},{12,8},{14,12},{10,14},{6,10},{2,6},{0,2},{5,1},{9,5},... | collective-permute-start | bytes 602120 | tf_op jit(solution)/shard_map/out_lead1/ppermute | solution.py:323
  19.8 1.9 %collective-permute-start.9 = (bf16[784,128]{1,0:T(8,128)(2,1)S(1)}, bf16[784,128]{1,0:T(8,128)(2,1)S(1)}, u32[]{:S(2)}, u32[]{:S(2)}) collective-permute-start(bf16[784,128]{1,0:T(8,128)(2,1)S(1)} %get-tuple-element.60.refs_1_), channel_id=1, source_target_pairs={{0,4},{4,8},{8,12},{12,14},{14,10},{10,6},{6,2},{2,0},{1,5},{5,9},... | collective-permute-start | bytes 602120 | tf_op jit(solution)/shard_map/out_trail1/ppermute | solution.py:323
  21.6 6.0 %experts.7 = (bf16[64,1536]{1,0:T(8,128)(2,1)S(1)}, bf16[64,1536]{1,0:T(8,128)(2,1)S(1)}, bf16[1536,768]{1,0:T(8,128)(2,1)S(1)}, bf16[1536,768]{1,0:T(8,128)(2,1...) custom-call(s32[1]{0:T(128)} %bitcast.5.me_ref, ...), custom_call_target="tpu_custom_call" | custom-call | flops 1811939328 | bytes 1179648 | tf_op jit(solution)/shard_map/experts/pallas_call | solution.py:282
  27.9 1.9 %collective-permute-start.7 = (bf16[784,128]{1,0:T(8,128)(2,1)S(1)}, bf16[784,128]{1,0:T(8,128)(2,1)S(1)}, u32[]{:S(2)}, u32[]{:S(2)}) collective-permute-start(bf16[784,128]{1,0:T(8,128)(2,1)S(1)} %collective-permute-done.6.refs_0_), channel_id=1, source_target_pairs={{0,4},{4,8},{8,12},{12,14},{14,10},{10,6},{6,2},{2,0},{1,5},{5,9},... | collective-permute-start | bytes 602120 | tf_op jit(solution)/shard_map/out_lead2/ppermute | solution.py:323
  29.8 1.8 %collective-permute-start.13 = (bf16[784,128]{1,0:T(8,128)(2,1)S(1)}, bf16[784,128]{1,0:T(8,128)(2,1)S(1)}, u32[]{:S(2)}, u32[]{:S(2)}) collective-permute-start(bf16[784,128]{1,0:T(8,128)(2,1)S(1)} %collective-permute-done.10.refs_3_), channel_id=1, source_target_pairs={{4,0},{8,4},{12,8},{14,12},{10,14},{6,10},{2,6},{0,2},{5,1},{9,5},... | collective-permute-start | bytes 602120 | tf_op jit(solution)/shard_map/out_trail2/ppermute | solution.py:323
  31.8 3.9 %experts.8 = (bf16[64,1536]{1,0:T(8,128)(2,1)S(1)}, bf16[64,1536]{1,0:T(8,128)(2,1)S(1)}, bf16[64,1536]{1,0:T(8,128)(2,1)S(1)}, bf16[64,1536]{1,0:T(8,128)(2,1)S(1)}) custom-call(s32[1]{0:T(128)} %bitcast.5.me_ref, bf16[784,128]{1,0:T(8,128)(2,1)S(1)} %collective-permute-done.6.refs_0_, bf16[784,128]{1,0:T(8,128)(2,1)S(1)} %collective-permute-done.8.refs_1_, ...), custom_call_target="tpu_custom_call" | custom-call | flops 3623878656 | bytes 2359296 | tf_op jit(solution)/shard_map/hop1/experts/pallas_call | solution.py:282
  35.7 1.8 %collective-permute-start.11 = (bf16[784,128]{1,0:T(8,128)(2,1)S(1)}, bf16[784,128]{1,0:T(8,128)(2,1)S(1)}, u32[]{:S(2)}, u32[]{:S(2)}) collective-permute-start(bf16[784,128]{1,0:T(8,128)(2,1)S(1)} %collective-permute-done.7.refs_0_), channel_id=1, source_target_pairs={{0,4},{4,8},{8,12},{12,14},{14,10},{10,6},{6,2},{2,0},{1,5},{5,9},... | collective-permute-start | bytes 602120 | tf_op jit(solution)/shard_map/out_lead3/ppermute | solution.py:323
  37.9 0.7 collective-permute-done.13.refs_1_
  38.6 1.1 %collective-permute-done.12.refs_0_ = bf16[784,128]{1,0:T(8,128)(2,1)S(1)} collective-permute-done((bf16[784,128]{1,0:T(8,128)(2,1)S(1)}, bf16[784,128]{1,0:T(8,128)(2,1)S(1)}, u32[]{:S(2)}, u32[]{:S(2)}) %collective-permute-start.12) | collective-permute-done | bytes 200736 | tf_op jit(solution)/shard_map/out_trail2/ppermute | solution.py:323
  39.7 2.1 %experts.9 = (bf16[64,1536]{1,0:T(8,128)(2,1)S(1)}, bf16[64,1536]{1,0:T(8,128)(2,1)S(1)}) custom-call(s32[1]{0:T(128)} %bitcast.5.me_ref, bf16[784,128]{1,0:T(8,128)(2,1)S(1)} %collective-permute-done.7.refs_0_, bf16[784,128]{1,0:T(8,128)(2,1)S(1)} %collective-permute-done.14.refs_1_, bf16[1536,768]{1,0:T(8,128)(2,1)S(1)} %get-tuple-element.63.refs_4_.refs_2_, ...), custom_call_target="tpu_custom_call" | custom-call | flops 1811939328 | bytes 1179648 | tf_op jit(solution)/shard_map/hop2/experts/pallas_call | solution.py:282
  42.3 1.7 %collective-permute-start.15 = (bf16[784,128]{1,0:T(8,128)(2,1)S(1)}, bf16[784,128]{1,0:T(8,128)(2,1)S(1)}, u32[]{:S(2)}, u32[]{:S(2)}) collective-permute-start(bf16[784,128]{1,0:T(8,128)(2,1)S(1)} %collective-permute-done.11.refs_0_), channel_id=1, source_target_pairs={{0,4},{4,8},{8,12},{12,14},{14,10},{10,6},{6,2},{2,0},{1,5},{5,9},... | collective-permute-start | bytes 602120 | tf_op jit(solution)/shard_map/out_lead4/ppermute | solution.py:323
  44.3 1.4 %collective-permute-start.20 = (bf16[784,128]{1,0:T(8,128)(2,1)S(1)}, bf16[784,128]{1,0:T(8,128)(2,1)S(1)}, u32[]{:S(2)}, u32[]{:S(2)}) collective-permute-start(bf16[784,128]{1,0:T(8,128)(2,1)S(1)} %collective-permute-done.13.refs_1_), channel_id=1, source_target_pairs={{4,0},{8,4},{12,8},{14,12},{10,14},{6,10},{2,6},{0,2},{5,1},{9,5},... | collective-permute-start | bytes 602120 | tf_op jit(solution)/shard_map/out_trail3/ppermute | solution.py:323
  45.7 0.6 collective-permute-start.19
  46.4 2.1 %experts.10 = (bf16[64,1536]{1,0:T(8,128)(2,1)S(1)}, bf16[64,1536]{1,0:T(8,128)(2,1)S(1)}) custom-call(s32[1]{0:T(128)} %bitcast.5.me_ref, bf16[784,128]{1,0:T(8,128)(2,1)S(1)} %collective-permute-done.11.refs_0_, bf16[784,128]{1,0:T(8,128)(2,1)S(1)} %collective-permute-done.16.refs_1_, bf16[1536,768]{1,0:T(8,128)(2,1)S(1)} %get-tuple-element.63.refs_4_.refs_2_, ...), custom_call_target="tpu_custom_call" | custom-call | flops 1811939328 | bytes 1179648 | tf_op jit(solution)/shard_map/hop3/experts/pallas_call | solution.py:282
  48.5 1.6 %collective-permute-done.15.refs_0_ = bf16[784,128]{1,0:T(8,128)(2,1)S(1)} collective-permute-done((bf16[784,128]{1,0:T(8,128)(2,1)S(1)}, bf16[784,128]{1,0:T(8,128)(2,1)S(1)}, u32[]{:S(2)}, u32[]{:S(2)}) %collective-permute-start.15) | collective-permute-done | bytes 200736 | tf_op jit(solution)/shard_map/out_lead4/ppermute | solution.py:323
  50.0 0.7 collective-permute-done.17.refs_1_
  50.8 2.1 %experts.11 = (bf16[64,1536]{1,0:T(8,128)(2,1)S(1)}, bf16[64,1536]{1,0:T(8,128)(2,1)S(1)}) custom-call(s32[1]{0:T(128)} %bitcast.5.me_ref, bf16[784,128]{1,0:T(8,128)(2,1)S(1)} %collective-permute-done.15.refs_0_, bf16[784,128]{1,0:T(8,128)(2,1)S(1)} %collective-permute-done.17.refs_1_, bf16[1536,768]{1,0:T(8,128)(2,1)S(1)} %get-tuple-element.63.refs_4_.refs_2_, ...), custom_call_target="tpu_custom_call" | custom-call | flops 1811939328 | bytes 1179648 | tf_op jit(solution)/shard_map/hop4/experts/pallas_call | solution.py:282
  52.9 1.1 %collective-permute-start.18 = (bf16[64,1536]{1,0:T(8,128)(2,1)S(1)}, bf16[64,1536]{1,0:T(8,128)(2,1)S(1)}, u32[]{:S(2)}, u32[]{:S(2)}) collective-permute-start(bf16[64,1536]{1,0:T(8,128)(2,1)S(1)} %get-tuple-element.81), channel_id=1, source_target_pairs={{0,4},{4,8},{8,12},{12,14},{14,10},{10,6},{6,2},{2,0},{1,5},{5,9},... | collective-permute-start | bytes 589832 | tf_op jit(solution)/shard_map/back_lead4/ppermute | solution.py:366
  53.9 2.1 %experts.12 = (bf16[64,1536]{1,0:T(8,128)(2,1)S(1)}, bf16[64,1536]{1,0:T(8,128)(2,1)S(1)}) custom-call(s32[1]{0:T(128)} %bitcast.5.me_ref, bf16[784,128]{1,0:T(8,128)(2,1)S(1)} %collective-permute-done.19.refs_0_, bf16[784,128]{1,0:T(8,128)(2,1)S(1)} %collective-permute-done.20.refs_1_, bf16[1536,768]{1,0:T(8,128)(2,1)S(1)} %get-tuple-element.63.refs_4_.refs_2_, ...), custom_call_target="tpu_custom_call" | custom-call | flops 1811939328 | bytes 1179648 | tf_op jit(solution)/shard_map/hop3/experts/pallas_call | solution.py:282
  56.1 1.1 %collective-permute-start.24 = (bf16[64,1536]{1,0:T(8,128)(2,1)S(1)}, bf16[64,1536]{1,0:T(8,128)(2,1)S(1)}, u32[]{:S(2)}, u32[]{:S(2)}) collective-permute-start(bf16[64,1536]{1,0:T(8,128)(2,1)S(1)} %get-tuple-element.91), channel_id=1, source_target_pairs={{4,0},{8,4},{12,8},{14,12},{10,14},{6,10},{2,6},{0,2},{5,1},{9,5},... | collective-permute-start | bytes 589832 | tf_op jit(solution)/shard_map/back_lead4/ppermute | solution.py:366
  57.1 2.1 %experts.13 = (bf16[64,1536]{1,0:T(8,128)(2,1)S(1)}, bf16[64,1536]{1,0:T(8,128)(2,1)S(1)}) custom-call(s32[1]{0:T(128)} %bitcast.5.me_ref, bf16[784,128]{1,0:T(8,128)(2,1)S(1)} %collective-permute-done.12.refs_0_, bf16[784,128]{1,0:T(8,128)(2,1)S(1)} %collective-permute-done.13.refs_1_, bf16[1536,768]{1,0:T(8,128)(2,1)S(1)} %get-tuple-element.63.refs_4_.refs_2_, ...), custom_call_target="tpu_custom_call" | custom-call | flops 1811939328 | bytes 1179648 | tf_op jit(solution)/shard_map/hop2/experts/pallas_call | solution.py:282
  59.5 1.0 %collective-permute-start.21 = (bf16[64,1536]{1,0:T(8,128)(2,1)S(1)}, bf16[64,1536]{1,0:T(8,128)(2,1)S(1)}, u32[]{:S(2)}, u32[]{:S(2)}) collective-permute-start(bf16[64,1536]{1,0:T(8,128)(2,1)S(1)} %add_convert_fusion.9), channel_id=1, source_target_pairs={{0,4},{4,8},{8,12},{12,14},{14,10},{10,6},{6,2},{2,0},{1,5},{5,9},... | collective-permute-start | bytes 589832 | tf_op jit(solution)/shard_map/back_lead3/ppermute | solution.py:366
  60.5 3.4 %collective-permute-done.24 = bf16[64,1536]{1,0:T(8,128)(2,1)S(1)} collective-permute-done((bf16[64,1536]{1,0:T(8,128)(2,1)S(1)}, bf16[64,1536]{1,0:T(8,128)(2,1)S(1)}, u32[]{:S(2)}, u32[]{:S(2)}) %collective-permute-start.24) | collective-permute-done | bytes 196640 | tf_op jit(solution)/shard_map/back_lead4/ppermute | solution.py:366
  63.9 1.0 %collective-permute-start.25 = (bf16[64,1536]{1,0:T(8,128)(2,1)S(1)}, bf16[64,1536]{1,0:T(8,128)(2,1)S(1)}, u32[]{:S(2)}, u32[]{:S(2)}) collective-permute-start(bf16[64,1536]{1,0:T(8,128)(2,1)S(1)} %get-tuple-element.92), channel_id=1, source_target_pairs={{4,0},{8,4},{12,8},{14,12},{10,14},{6,10},{2,6},{0,2},{5,1},{9,5},... | collective-permute-start | bytes 589832 | tf_op jit(solution)/shard_map/back_trail3/ppermute | solution.py:366
  64.9 1.0 %collective-permute-start.28 = (bf16[64,1536]{1,0:T(8,128)(2,1)S(1)}, bf16[64,1536]{1,0:T(8,128)(2,1)S(1)}, u32[]{:S(2)}, u32[]{:S(2)}) collective-permute-start(bf16[64,1536]{1,0:T(8,128)(2,1)S(1)} %get-tuple-element.97), channel_id=1, source_target_pairs={{0,4},{4,8},{8,12},{12,14},{14,10},{10,6},{6,2},{2,0},{1,5},{5,9},... | collective-permute-start | bytes 589832 | tf_op jit(solution)/shard_map/back_trail3/ppermute | solution.py:366
  66.0 1.1 %collective-permute-start.31 = (bf16[64,1536]{1,0:T(8,128)(2,1)S(1)}, bf16[64,1536]{1,0:T(8,128)(2,1)S(1)}, u32[]{:S(2)}, u32[]{:S(2)}) collective-permute-start(bf16[64,1536]{1,0:T(8,128)(2,1)S(1)} %add_convert_fusion.2), channel_id=1, source_target_pairs={{4,0},{8,4},{12,8},{14,12},{10,14},{6,10},{2,6},{0,2},{5,1},{9,5},... | collective-permute-start | bytes 589832 | tf_op jit(solution)/shard_map/back_lead3/ppermute | solution.py:366
  67.2 1.0 %collective-permute-start.22 = (bf16[64,1536]{1,0:T(8,128)(2,1)S(1)}, bf16[64,1536]{1,0:T(8,128)(2,1)S(1)}, u32[]{:S(2)}, u32[]{:S(2)}) collective-permute-start(bf16[64,1536]{1,0:T(8,128)(2,1)S(1)} %add_convert_fusion.8), channel_id=1, source_target_pairs={{0,4},{4,8},{8,12},{12,14},{14,10},{10,6},{6,2},{2,0},{1,5},{5,9},... | collective-permute-start | bytes 589832 | tf_op jit(solution)/shard_map/back_lead2/ppermute | solution.py:366
  68.2 3.5 %collective-permute-done.25 = bf16[64,1536]{1,0:T(8,128)(2,1)S(1)} collective-permute-done((bf16[64,1536]{1,0:T(8,128)(2,1)S(1)}, bf16[64,1536]{1,0:T(8,128)(2,1)S(1)}, u32[]{:S(2)}, u32[]{:S(2)}) %collective-permute-start.25) | collective-permute-done | bytes 196640 | tf_op jit(solution)/shard_map/back_trail3/ppermute | solution.py:366
  71.7 1.1 %collective-permute-start.26 = (bf16[64,1536]{1,0:T(8,128)(2,1)S(1)}, bf16[64,1536]{1,0:T(8,128)(2,1)S(1)}, u32[]{:S(2)}, u32[]{:S(2)}) collective-permute-start(bf16[64,1536]{1,0:T(8,128)(2,1)S(1)} %add_convert_fusion.6), channel_id=1, source_target_pairs={{4,0},{8,4},{12,8},{14,12},{10,14},{6,10},{2,6},{0,2},{5,1},{9,5},... | collective-permute-start | bytes 589832 | tf_op jit(solution)/shard_map/back_trail2/ppermute | solution.py:366
  72.8 1.1 %collective-permute-start.29 = (bf16[64,1536]{1,0:T(8,128)(2,1)S(1)}, bf16[64,1536]{1,0:T(8,128)(2,1)S(1)}, u32[]{:S(2)}, u32[]{:S(2)}) collective-permute-start(bf16[64,1536]{1,0:T(8,128)(2,1)S(1)} %add_convert_fusion.4), channel_id=1, source_target_pairs={{0,4},{4,8},{8,12},{12,14},{14,10},{10,6},{6,2},{2,0},{1,5},{5,9},... | collective-permute-start | bytes 589832 | tf_op jit(solution)/shard_map/back_trail2/ppermute | solution.py:366
  73.9 2.0 %collective-permute-done.31 = bf16[64,1536]{1,0:T(8,128)(2,1)S(1)} collective-permute-done((bf16[64,1536]{1,0:T(8,128)(2,1)S(1)}, bf16[64,1536]{1,0:T(8,128)(2,1)S(1)}, u32[]{:S(2)}, u32[]{:S(2)}) %collective-permute-start.31) | collective-permute-done | bytes 196640 | tf_op jit(solution)/shard_map/back_lead3/ppermute | solution.py:366
  75.9 1.1 %collective-permute-start.32 = (bf16[64,1536]{1,0:T(8,128)(2,1)S(1)}, bf16[64,1536]{1,0:T(8,128)(2,1)S(1)}, u32[]{:S(2)}, u32[]{:S(2)}) collective-permute-start(bf16[64,1536]{1,0:T(8,128)(2,1)S(1)} %add_convert_fusion.1), channel_id=1, source_target_pairs={{4,0},{8,4},{12,8},{14,12},{10,14},{6,10},{2,6},{0,2},{5,1},{9,5},... | collective-permute-start | bytes 589832 | tf_op jit(solution)/shard_map/back_lead2/ppermute | solution.py:366
  77.0 1.1 %collective-permute-start.23 = (bf16[64,1536]{1,0:T(8,128)(2,1)S(1)}, bf16[64,1536]{1,0:T(8,128)(2,1)S(1)}, u32[]{:S(2)}, u32[]{:S(2)}) collective-permute-start(bf16[64,1536]{1,0:T(8,128)(2,1)S(1)} %add_convert_fusion.7), channel_id=1, source_target_pairs={{0,4},{4,8},{8,12},{12,14},{14,10},{10,6},{6,2},{2,0},{1,5},{5,9},... | collective-permute-start | bytes 589832 | tf_op jit(solution)/shard_map/back_lead1/ppermute | solution.py:366
  78.1 2.0 %collective-permute-done.26 = bf16[64,1536]{1,0:T(8,128)(2,1)S(1)} collective-permute-done((bf16[64,1536]{1,0:T(8,128)(2,1)S(1)}, bf16[64,1536]{1,0:T(8,128)(2,1)S(1)}, u32[]{:S(2)}, u32[]{:S(2)}) %collective-permute-start.26) | collective-permute-done | bytes 196640 | tf_op jit(solution)/shard_map/back_trail2/ppermute | solution.py:366
  80.1 1.1 %collective-permute-start.27 = (bf16[64,1536]{1,0:T(8,128)(2,1)S(1)}, bf16[64,1536]{1,0:T(8,128)(2,1)S(1)}, u32[]{:S(2)}, u32[]{:S(2)}) collective-permute-start(bf16[64,1536]{1,0:T(8,128)(2,1)S(1)} %add_convert_fusion.5), channel_id=1, source_target_pairs={{4,0},{8,4},{12,8},{14,12},{10,14},{6,10},{2,6},{0,2},{5,1},{9,5},... | collective-permute-start | bytes 589832 | tf_op jit(solution)/shard_map/back_trail1/ppermute | solution.py:366
  81.2 1.1 %collective-permute-start.30 = (bf16[64,1536]{1,0:T(8,128)(2,1)S(1)}, bf16[64,1536]{1,0:T(8,128)(2,1)S(1)}, u32[]{:S(2)}, u32[]{:S(2)}) collective-permute-start(bf16[64,1536]{1,0:T(8,128)(2,1)S(1)} %add_convert_fusion.3), channel_id=1, source_target_pairs={{0,4},{4,8},{8,12},{12,14},{14,10},{10,6},{6,2},{2,0},{1,5},{5,9},... | collective-permute-start | bytes 589832 | tf_op jit(solution)/shard_map/back_trail1/ppermute | solution.py:366
  82.3 1.1 %collective-permute-done.32 = bf16[64,1536]{1,0:T(8,128)(2,1)S(1)} collective-permute-done((bf16[64,1536]{1,0:T(8,128)(2,1)S(1)}, bf16[64,1536]{1,0:T(8,128)(2,1)S(1)}, u32[]{:S(2)}, u32[]{:S(2)}) %collective-permute-start.32) | collective-permute-done | bytes 196640 | tf_op jit(solution)/shard_map/back_lead2/ppermute | solution.py:366
  83.5 0.9 %collective-permute-start.33 = (bf16[64,1536]{1,0:T(8,128)(2,1)S(1)}, bf16[64,1536]{1,0:T(8,128)(2,1)S(1)}, u32[]{:S(2)}, u32[]{:S(2)}) collective-permute-start(bf16[64,1536]{1,0:T(8,128)(2,1)S(1)} %add_convert_fusion), channel_id=1, source_target_pairs={{4,0},{8,4},{12,8},{14,12},{10,14},{6,10},{2,6},{0,2},{5,1},{9,5},... | collective-permute-start | bytes 589832 | tf_op jit(solution)/shard_map/back_lead1/ppermute | solution.py:366
  84.4 1.5 %collective-permute-done.27 = bf16[64,1536]{1,0:T(8,128)(2,1)S(1)} collective-permute-done((bf16[64,1536]{1,0:T(8,128)(2,1)S(1)}, bf16[64,1536]{1,0:T(8,128)(2,1)S(1)}, u32[]{:S(2)}, u32[]{:S(2)}) %collective-permute-start.27) | collective-permute-done | bytes 196640 | tf_op jit(solution)/shard_map/back_trail1/ppermute | solution.py:366
  85.9 1.1 %collective-permute-done.30 = bf16[64,1536]{1,0:T(8,128)(2,1)S(1)} collective-permute-done((bf16[64,1536]{1,0:T(8,128)(2,1)S(1)}, bf16[64,1536]{1,0:T(8,128)(2,1)S(1)}, u32[]{:S(2)}, u32[]{:S(2)}) %collective-permute-start.30) | collective-permute-done | bytes 196640 | tf_op jit(solution)/shard_map/back_trail1/ppermute | solution.py:366
  87.0 2.2 %collective-permute-done.33 = bf16[64,1536]{1,0:T(8,128)(2,1)S(1)} collective-permute-done((bf16[64,1536]{1,0:T(8,128)(2,1)S(1)}, bf16[64,1536]{1,0:T(8,128)(2,1)S(1)}, u32[]{:S(2)}, u32[]{:S(2)}) %collective-permute-start.33) | collective-permute-done | bytes 196640 | tf_op jit(solution)/shard_map/back_lead1/ppermute | solution.py:366
  89.2 0.8 fusion
  (54 shorter events, 4.6 us)
Async XLA Ops:
  0.0 17.5 %collective-permute-start.3 = (bf16[1536,768]{1,0:T(8,128)(2,1)}, bf16[1536,768]{1,0:T(8,128)(2,1)S(1)}, u32[]{:S(2)}, u32[]{:S(2)}) collective-permute-start(bf16[1536,768]{1,0:T(8,128)(2,1)} %bitcast.11), channel_id=1, source_target_pairs={{0,1},{1,0},{2,3},{3,2},{4,5},{5,4},{6,7},{7,6},{8,9},{9,8},{10,11... | collective-permute-start | bytes 7077896 | tf_op jit(solution)/shard_map/ppermute | solution.py:37
  0.5 17.1 %collective-permute-start.4 = (bf16[1536,768]{1,0:T(8,128)(2,1)}, bf16[1536,768]{1,0:T(8,128)(2,1)}, u32[]{:S(2)}, u32[]{:S(2)}) collective-permute-start(bf16[1536,768]{1,0:T(8,128)(2,1)} %bitcast.13), channel_id=1, source_target_pairs={{0,1},{1,0},{2,3},{3,2},{4,5},{5,4},{6,7},{7,6},{8,9},{9,8},{10,11... | collective-permute-start | bytes 7077896 | tf_op jit(solution)/shard_map/ppermute | solution.py:37
  0.5 17.0 %collective-permute-start.5 = (bf16[768,1536]{1,0:T(8,128)(2,1)}, bf16[768,1536]{1,0:T(8,128)(2,1)}, u32[]{:S(2)}, u32[]{:S(2)}) collective-permute-start(bf16[768,1536]{1,0:T(8,128)(2,1)} %bitcast.15), channel_id=1, source_target_pairs={{0,1},{1,0},{2,3},{3,2},{4,5},{5,4},{6,7},{7,6},{8,9},{9,8},{10,11... | collective-permute-start | bytes 7077896 | tf_op jit(solution)/shard_map/ppermute | solution.py:37
  1.0 8.7 %collective-permute-start = (bf16[256,128]{1,0:T(8,128)(2,1)}, bf16[256,128]{1,0:T(8,128)(2,1)S(1)}, u32[]{:S(2)}, u32[]{:S(2)}) collective-permute-start(bf16[256,128]{1,0:T(8,128)(2,1)} %k_hbm.3), channel_id=1, source_target_pairs={{0,2},{2,4},{4,6},{6,8},{8,10},{10,12},{12,14},{14,0},{1,3},{3,5},... | collective-permute-start | bytes 196616 | tf_op jit(solution)/shard_map/ppermute | solution.py:24
  3.5 7.4 %collective-permute-start.1 = (bf16[256,128]{1,0:T(8,128)(2,1)}, bf16[256,128]{1,0:T(8,128)(2,1)S(1)}, u32[]{:S(2)}, u32[]{:S(2)}) collective-permute-start(bf16[256,128]{1,0:T(8,128)(2,1)} %v_hbm.3), channel_id=1, source_target_pairs={{0,2},{2,4},{4,6},{6,8},{8,10},{10,12},{12,14},{14,0},{1,3},{3,5},... | collective-permute-start | bytes 196616 | tf_op jit(solution)/shard_map/ppermute | solution.py:24
  10.9 4.6 %copy-start.4 = (f32[1536]{0:T(1024)S(1)}, f32[1536]{0:T(1024)}, u32[]{:S(2)}) copy-start(f32[1536]{0:T(1024)} %param.18) | copy-start | bytes 18436
  10.9 6.3 %copy-start = (bf16[128,1536]{1,0:T(8,128)(2,1)S(1)}, bf16[128,1536]{1,0:T(8,128)(2,1)}, u32[]{:S(2)}) copy-start(bf16[128,1536]{1,0:T(8,128)(2,1)} %stream_ref.1) | copy-start | bytes 1179652
  10.9 6.3 %copy-start.1 = (s32[128,4]{0,1:T(4,128)S(1)}, s32[128,4]{0,1:T(4,128)}, u32[]{:S(2)}) copy-start(s32[128,4]{0,1:T(4,128)} %param.19) | copy-start | bytes 6148
  10.9 6.3 %copy-start.2 = (f32[128,4]{0,1:T(4,128)S(1)}, f32[128,4]{0,1:T(4,128)}, u32[]{:S(2)}) copy-start(f32[128,4]{0,1:T(4,128)} %param.20) | copy-start | bytes 6148
  15.4 1.8 %collective-permute-start.2 = (bf16[128,1536]{1,0:T(8,128)(2,1)S(1)}, bf16[128,1536]{1,0:T(8,128)(2,1)S(1)}, u32[]{:S(2)}, u32[]{:S(2)}) collective-permute-start(bf16[128,1536]{1,0:T(8,128)(2,1)S(1)} %get-tuple-element.55), channel_id=1, source_target_pairs={{0,1},{1,0},{2,3},{3,2},{4,5},{5,4},{6,7},{7,6},{8,9},{9,8},{10,11... | collective-permute-start | bytes 1179656 | tf_op jit(solution)/shard_map/ppermute | solution.py:37
  17.5 4.1 %copy-start.3 = (bf16[1536,768]{1,0:T(8,128)(2,1)}, bf16[1536,768]{1,0:T(8,128)(2,1)S(1)}, u32[]{:S(2)}) copy-start(bf16[1536,768]{1,0:T(8,128)(2,1)S(1)} %collective-permute-done.3.refs_5_) | copy-start | bytes 7077892
  17.5 10.1 %collective-permute-start.6 = (bf16[784,128]{1,0:T(8,128)(2,1)S(1)}, bf16[784,128]{1,0:T(8,128)(2,1)S(1)}, u32[]{:S(2)}, u32[]{:S(2)}) collective-permute-start(bf16[784,128]{1,0:T(8,128)(2,1)S(1)} %get-tuple-element.59.refs_0_), channel_id=1, source_target_pairs={{0,4},{4,8},{8,12},{12,14},{14,10},{10,6},{6,2},{2,0},{1,5},{5,9},... | collective-permute-start | bytes 602120 | tf_op jit(solution)/shard_map/out_lead1/ppermute | solution.py:323
  17.8 9.8 %collective-permute-start.8 = (bf16[784,128]{1,0:T(8,128)(2,1)S(1)}, bf16[784,128]{1,0:T(8,128)(2,1)S(1)}, u32[]{:S(2)}, u32[]{:S(2)}) collective-permute-start(bf16[784,128]{1,0:T(8,128)(2,1)S(1)} %get-tuple-element.60.refs_1_), channel_id=1, source_target_pairs={{4,0},{8,4},{12,8},{14,12},{10,14},{6,10},{2,6},{0,2},{5,1},{9,5},... | collective-permute-start | bytes 602120 | tf_op jit(solution)/shard_map/out_lead1/ppermute | solution.py:323
  19.6 10.1 %collective-permute-start.10 = (bf16[784,128]{1,0:T(8,128)(2,1)S(1)}, bf16[784,128]{1,0:T(8,128)(2,1)S(1)}, u32[]{:S(2)}, u32[]{:S(2)}) collective-permute-start(bf16[784,128]{1,0:T(8,128)(2,1)S(1)} %get-tuple-element.59.refs_0_), channel_id=1, source_target_pairs={{4,0},{8,4},{12,8},{14,12},{10,14},{6,10},{2,6},{0,2},{5,1},{9,5},... | collective-permute-start | bytes 602120 | tf_op jit(solution)/shard_map/out_trail1/ppermute | solution.py:323
  19.8 11.8 %collective-permute-start.9 = (bf16[784,128]{1,0:T(8,128)(2,1)S(1)}, bf16[784,128]{1,0:T(8,128)(2,1)S(1)}, u32[]{:S(2)}, u32[]{:S(2)}) collective-permute-start(bf16[784,128]{1,0:T(8,128)(2,1)S(1)} %get-tuple-element.60.refs_1_), channel_id=1, source_target_pairs={{0,4},{4,8},{8,12},{12,14},{14,10},{10,6},{6,2},{2,0},{1,5},{5,9},... | collective-permute-start | bytes 602120 | tf_op jit(solution)/shard_map/out_trail1/ppermute | solution.py:323
  27.7 9.9 %collective-permute-start.14 = (bf16[784,128]{1,0:T(8,128)(2,1)S(1)}, bf16[784,128]{1,0:T(8,128)(2,1)S(1)}, u32[]{:S(2)}, u32[]{:S(2)}) collective-permute-start(bf16[784,128]{1,0:T(8,128)(2,1)S(1)} %collective-permute-done.8.refs_1_), channel_id=1, source_target_pairs={{4,0},{8,4},{12,8},{14,12},{10,14},{6,10},{2,6},{0,2},{5,1},{9,5},... | collective-permute-start | bytes 602120 | tf_op jit(solution)/shard_map/out_lead2/ppermute | solution.py:323
  27.9 7.8 %collective-permute-start.7 = (bf16[784,128]{1,0:T(8,128)(2,1)S(1)}, bf16[784,128]{1,0:T(8,128)(2,1)S(1)}, u32[]{:S(2)}, u32[]{:S(2)}) collective-permute-start(bf16[784,128]{1,0:T(8,128)(2,1)S(1)} %collective-permute-done.6.refs_0_), channel_id=1, source_target_pairs={{0,4},{4,8},{8,12},{12,14},{14,10},{10,6},{6,2},{2,0},{1,5},{5,9},... | collective-permute-start | bytes 602120 | tf_op jit(solution)/shard_map/out_lead2/ppermute | solution.py:323
  29.8 8.8 %collective-permute-start.13 = (bf16[784,128]{1,0:T(8,128)(2,1)S(1)}, bf16[784,128]{1,0:T(8,128)(2,1)S(1)}, u32[]{:S(2)}, u32[]{:S(2)}) collective-permute-start(bf16[784,128]{1,0:T(8,128)(2,1)S(1)} %collective-permute-done.10.refs_3_), channel_id=1, source_target_pairs={{4,0},{8,4},{12,8},{14,12},{10,14},{6,10},{2,6},{0,2},{5,1},{9,5},... | collective-permute-start | bytes 602120 | tf_op jit(solution)/shard_map/out_trail2/ppermute | solution.py:323
  31.6 8.1 %collective-permute-start.12 = (bf16[784,128]{1,0:T(8,128)(2,1)S(1)}, bf16[784,128]{1,0:T(8,128)(2,1)S(1)}, u32[]{:S(2)}, u32[]{:S(2)}) collective-permute-start(bf16[784,128]{1,0:T(8,128)(2,1)S(1)} %collective-permute-done.9.refs_2_), channel_id=1, source_target_pairs={{0,4},{4,8},{8,12},{12,14},{14,10},{10,6},{6,2},{2,0},{1,5},{5,9},... | collective-permute-start | bytes 602120 | tf_op jit(solution)/shard_map/out_trail2/ppermute | solution.py:323
  35.7 6.6 %collective-permute-start.11 = (bf16[784,128]{1,0:T(8,128)(2,1)S(1)}, bf16[784,128]{1,0:T(8,128)(2,1)S(1)}, u32[]{:S(2)}, u32[]{:S(2)}) collective-permute-start(bf16[784,128]{1,0:T(8,128)(2,1)S(1)} %collective-permute-done.7.refs_0_), channel_id=1, source_target_pairs={{0,4},{4,8},{8,12},{12,14},{14,10},{10,6},{6,2},{2,0},{1,5},{5,9},... | collective-permute-start | bytes 602120 | tf_op jit(solution)/shard_map/out_lead3/ppermute | solution.py:323
  37.5 6.5 %collective-permute-start.16 = (bf16[784,128]{1,0:T(8,128)(2,1)S(1)}, bf16[784,128]{1,0:T(8,128)(2,1)S(1)}, u32[]{:S(2)}, u32[]{:S(2)}) collective-permute-start(bf16[784,128]{1,0:T(8,128)(2,1)S(1)} %collective-permute-done.14.refs_1_), channel_id=1, source_target_pairs={{4,0},{8,4},{12,8},{14,12},{10,14},{6,10},{2,6},{0,2},{5,1},{9,5},... | collective-permute-start | bytes 602120 | tf_op jit(solution)/shard_map/out_lead3/ppermute | solution.py:323
  42.3 7.7 %collective-permute-start.15 = (bf16[784,128]{1,0:T(8,128)(2,1)S(1)}, bf16[784,128]{1,0:T(8,128)(2,1)S(1)}, u32[]{:S(2)}, u32[]{:S(2)}) collective-permute-start(bf16[784,128]{1,0:T(8,128)(2,1)S(1)} %collective-permute-done.11.refs_0_), channel_id=1, source_target_pairs={{0,4},{4,8},{8,12},{12,14},{14,10},{10,6},{6,2},{2,0},{1,5},{5,9},... | collective-permute-start | bytes 602120 | tf_op jit(solution)/shard_map/out_lead4/ppermute | solution.py:323
  44.0 6.8 %collective-permute-start.17 = (bf16[784,128]{1,0:T(8,128)(2,1)S(1)}, bf16[784,128]{1,0:T(8,128)(2,1)S(1)}, u32[]{:S(2)}, u32[]{:S(2)}) collective-permute-start(bf16[784,128]{1,0:T(8,128)(2,1)S(1)} %collective-permute-done.16.refs_1_), channel_id=1, source_target_pairs={{4,0},{8,4},{12,8},{14,12},{10,14},{6,10},{2,6},{0,2},{5,1},{9,5},... | collective-permute-start | bytes 602120 | tf_op jit(solution)/shard_map/out_lead4/ppermute | solution.py:323
  44.3 9.6 %collective-permute-start.20 = (bf16[784,128]{1,0:T(8,128)(2,1)S(1)}, bf16[784,128]{1,0:T(8,128)(2,1)S(1)}, u32[]{:S(2)}, u32[]{:S(2)}) collective-permute-start(bf16[784,128]{1,0:T(8,128)(2,1)S(1)} %collective-permute-done.13.refs_1_), channel_id=1, source_target_pairs={{4,0},{8,4},{12,8},{14,12},{10,14},{6,10},{2,6},{0,2},{5,1},{9,5},... | collective-permute-start | bytes 602120 | tf_op jit(solution)/shard_map/out_trail3/ppermute | solution.py:323
  45.7 8.2 %collective-permute-start.19 = (bf16[784,128]{1,0:T(8,128)(2,1)S(1)}, bf16[784,128]{1,0:T(8,128)(2,1)S(1)}, u32[]{:S(2)}, u32[]{:S(2)}) collective-permute-start(bf16[784,128]{1,0:T(8,128)(2,1)S(1)} %collective-permute-done.12.refs_0_), channel_id=1, source_target_pairs={{0,4},{4,8},{8,12},{12,14},{14,10},{10,6},{6,2},{2,0},{1,5},{5,9},... | collective-permute-start | bytes 602120 | tf_op jit(solution)/shard_map/out_trail3/ppermute | solution.py:323
  52.9 6.6 %collective-permute-start.18 = (bf16[64,1536]{1,0:T(8,128)(2,1)S(1)}, bf16[64,1536]{1,0:T(8,128)(2,1)S(1)}, u32[]{:S(2)}, u32[]{:S(2)}) collective-permute-start(bf16[64,1536]{1,0:T(8,128)(2,1)S(1)} %get-tuple-element.81), channel_id=1, source_target_pairs={{0,4},{4,8},{8,12},{12,14},{14,10},{10,6},{6,2},{2,0},{1,5},{5,9},... | collective-permute-start | bytes 589832 | tf_op jit(solution)/shard_map/back_lead4/ppermute | solution.py:366
  56.1 7.8 %collective-permute-start.24 = (bf16[64,1536]{1,0:T(8,128)(2,1)S(1)}, bf16[64,1536]{1,0:T(8,128)(2,1)S(1)}, u32[]{:S(2)}, u32[]{:S(2)}) collective-permute-start(bf16[64,1536]{1,0:T(8,128)(2,1)S(1)} %get-tuple-element.91), channel_id=1, source_target_pairs={{4,0},{8,4},{12,8},{14,12},{10,14},{6,10},{2,6},{0,2},{5,1},{9,5},... | collective-permute-start | bytes 589832 | tf_op jit(solution)/shard_map/back_lead4/ppermute | solution.py:366
  59.5 7.6 %collective-permute-start.21 = (bf16[64,1536]{1,0:T(8,128)(2,1)S(1)}, bf16[64,1536]{1,0:T(8,128)(2,1)S(1)}, u32[]{:S(2)}, u32[]{:S(2)}) collective-permute-start(bf16[64,1536]{1,0:T(8,128)(2,1)S(1)} %add_convert_fusion.9), channel_id=1, source_target_pairs={{0,4},{4,8},{8,12},{12,14},{14,10},{10,6},{6,2},{2,0},{1,5},{5,9},... | collective-permute-start | bytes 589832 | tf_op jit(solution)/shard_map/back_lead3/ppermute | solution.py:366
  63.9 7.8 %collective-permute-start.25 = (bf16[64,1536]{1,0:T(8,128)(2,1)S(1)}, bf16[64,1536]{1,0:T(8,128)(2,1)S(1)}, u32[]{:S(2)}, u32[]{:S(2)}) collective-permute-start(bf16[64,1536]{1,0:T(8,128)(2,1)S(1)} %get-tuple-element.92), channel_id=1, source_target_pairs={{4,0},{8,4},{12,8},{14,12},{10,14},{6,10},{2,6},{0,2},{5,1},{9,5},... | collective-permute-start | bytes 589832 | tf_op jit(solution)/shard_map/back_trail3/ppermute | solution.py:366
  64.9 7.9 %collective-permute-start.28 = (bf16[64,1536]{1,0:T(8,128)(2,1)S(1)}, bf16[64,1536]{1,0:T(8,128)(2,1)S(1)}, u32[]{:S(2)}, u32[]{:S(2)}) collective-permute-start(bf16[64,1536]{1,0:T(8,128)(2,1)S(1)} %get-tuple-element.97), channel_id=1, source_target_pairs={{0,4},{4,8},{8,12},{12,14},{14,10},{10,6},{6,2},{2,0},{1,5},{5,9},... | collective-permute-start | bytes 589832 | tf_op jit(solution)/shard_map/back_trail3/ppermute | solution.py:366
  66.0 9.9 %collective-permute-start.31 = (bf16[64,1536]{1,0:T(8,128)(2,1)S(1)}, bf16[64,1536]{1,0:T(8,128)(2,1)S(1)}, u32[]{:S(2)}, u32[]{:S(2)}) collective-permute-start(bf16[64,1536]{1,0:T(8,128)(2,1)S(1)} %add_convert_fusion.2), channel_id=1, source_target_pairs={{4,0},{8,4},{12,8},{14,12},{10,14},{6,10},{2,6},{0,2},{5,1},{9,5},... | collective-permute-start | bytes 589832 | tf_op jit(solution)/shard_map/back_lead3/ppermute | solution.py:366
  67.2 9.8 %collective-permute-start.22 = (bf16[64,1536]{1,0:T(8,128)(2,1)S(1)}, bf16[64,1536]{1,0:T(8,128)(2,1)S(1)}, u32[]{:S(2)}, u32[]{:S(2)}) collective-permute-start(bf16[64,1536]{1,0:T(8,128)(2,1)S(1)} %add_convert_fusion.8), channel_id=1, source_target_pairs={{0,4},{4,8},{8,12},{12,14},{14,10},{10,6},{6,2},{2,0},{1,5},{5,9},... | collective-permute-start | bytes 589832 | tf_op jit(solution)/shard_map/back_lead2/ppermute | solution.py:366
  71.7 8.4 %collective-permute-start.26 = (bf16[64,1536]{1,0:T(8,128)(2,1)S(1)}, bf16[64,1536]{1,0:T(8,128)(2,1)S(1)}, u32[]{:S(2)}, u32[]{:S(2)}) collective-permute-start(bf16[64,1536]{1,0:T(8,128)(2,1)S(1)} %add_convert_fusion.6), channel_id=1, source_target_pairs={{4,0},{8,4},{12,8},{14,12},{10,14},{6,10},{2,6},{0,2},{5,1},{9,5},... | collective-permute-start | bytes 589832 | tf_op jit(solution)/shard_map/back_trail2/ppermute | solution.py:366
  72.8 8.4 %collective-permute-start.29 = (bf16[64,1536]{1,0:T(8,128)(2,1)S(1)}, bf16[64,1536]{1,0:T(8,128)(2,1)S(1)}, u32[]{:S(2)}, u32[]{:S(2)}) collective-permute-start(bf16[64,1536]{1,0:T(8,128)(2,1)S(1)} %add_convert_fusion.4), channel_id=1, source_target_pairs={{0,4},{4,8},{8,12},{12,14},{14,10},{10,6},{6,2},{2,0},{1,5},{5,9},... | collective-permute-start | bytes 589832 | tf_op jit(solution)/shard_map/back_trail2/ppermute | solution.py:366
  75.9 7.5 %collective-permute-start.32 = (bf16[64,1536]{1,0:T(8,128)(2,1)S(1)}, bf16[64,1536]{1,0:T(8,128)(2,1)S(1)}, u32[]{:S(2)}, u32[]{:S(2)}) collective-permute-start(bf16[64,1536]{1,0:T(8,128)(2,1)S(1)} %add_convert_fusion.1), channel_id=1, source_target_pairs={{4,0},{8,4},{12,8},{14,12},{10,14},{6,10},{2,6},{0,2},{5,1},{9,5},... | collective-permute-start | bytes 589832 | tf_op jit(solution)/shard_map/back_lead2/ppermute | solution.py:366
  77.0 7.3 %collective-permute-start.23 = (bf16[64,1536]{1,0:T(8,128)(2,1)S(1)}, bf16[64,1536]{1,0:T(8,128)(2,1)S(1)}, u32[]{:S(2)}, u32[]{:S(2)}) collective-permute-start(bf16[64,1536]{1,0:T(8,128)(2,1)S(1)} %add_convert_fusion.7), channel_id=1, source_target_pairs={{0,4},{4,8},{8,12},{12,14},{14,10},{10,6},{6,2},{2,0},{1,5},{5,9},... | collective-permute-start | bytes 589832 | tf_op jit(solution)/shard_map/back_lead1/ppermute | solution.py:366
  80.1 5.7 %collective-permute-start.27 = (bf16[64,1536]{1,0:T(8,128)(2,1)S(1)}, bf16[64,1536]{1,0:T(8,128)(2,1)S(1)}, u32[]{:S(2)}, u32[]{:S(2)}) collective-permute-start(bf16[64,1536]{1,0:T(8,128)(2,1)S(1)} %add_convert_fusion.5), channel_id=1, source_target_pairs={{4,0},{8,4},{12,8},{14,12},{10,14},{6,10},{2,6},{0,2},{5,1},{9,5},... | collective-permute-start | bytes 589832 | tf_op jit(solution)/shard_map/back_trail1/ppermute | solution.py:366
  81.2 5.7 %collective-permute-start.30 = (bf16[64,1536]{1,0:T(8,128)(2,1)S(1)}, bf16[64,1536]{1,0:T(8,128)(2,1)S(1)}, u32[]{:S(2)}, u32[]{:S(2)}) collective-permute-start(bf16[64,1536]{1,0:T(8,128)(2,1)S(1)} %add_convert_fusion.3), channel_id=1, source_target_pairs={{0,4},{4,8},{8,12},{12,14},{14,10},{10,6},{6,2},{2,0},{1,5},{5,9},... | collective-permute-start | bytes 589832 | tf_op jit(solution)/shard_map/back_trail1/ppermute | solution.py:366
  83.5 5.7 %collective-permute-start.33 = (bf16[64,1536]{1,0:T(8,128)(2,1)S(1)}, bf16[64,1536]{1,0:T(8,128)(2,1)S(1)}, u32[]{:S(2)}, u32[]{:S(2)}) collective-permute-start(bf16[64,1536]{1,0:T(8,128)(2,1)S(1)} %add_convert_fusion), channel_id=1, source_target_pairs={{4,0},{8,4},{12,8},{14,12},{10,14},{6,10},{2,6},{0,2},{5,1},{9,5},... | collective-permute-start | bytes 589832 | tf_op jit(solution)/shard_map/back_lead1/ppermute | solution.py:366

commit v7 on v5

--- a/solution.py
+++ b/solution.py
@@ -351,13 +351,16 @@
     moving = {}
 
     def send(distance, lead, *after):
+        met = [moving.get((side, side if lead else 1 - side)) for side in sides]
+        if met[0] is not None:
+            met = list(lax.optimization_barrier(tuple(met)))
         for side in sides:
             piece = side if lead else 1 - side
             value = given[(-distance if side == 0 else distance) % chips, piece]
             if after:
                 value = tied(value, *after)
-            if (side, piece) in moving:
-                value = moving[side, piece].astype(jnp.float32) + value.astype(jnp.float32)
+            if met[0] is not None:
+                value = met[side].astype(jnp.float32) + value.astype(jnp.float32)
                 value = value.astype(jnp.bfloat16)
             with jax.named_scope(f"back_{'lead' if lead else 'trail'}{distance}"):
                 moving[side, piece] = lax.ppermute(value, "seq", hops[side])

time: 88.6 us -> 86.4 us (0.975)
  starting transfers between devices: 38.3 us -> 34.2 us
  waiting for transfers between devices: 19 us -> 20.9 us
    ppermute x14, starting transfers between devices: 18.9 us -> 14.8 us  [send(): moving[side, piece] = lax.ppermute(value, 'seq', hops[side])]
    ppermute x14, waiting for transfers between devices: 12.3 us -> 14.7 us  [send(): moving[side, piece] = lax.ppermute(value, 'seq', hops[side])]
  transfers between devices with their start and end apart: 34 -> 34, of which waited for: 19 -> 17; matrix products, arithmetic and copies ran while one was open for 1% -> 1% of each run, Pallas kernels for 33% -> 34%
where the time goes in v7:
time: 86.4 us; the launch traced here: 86.3 us
  starting transfers between devices  34.2 us (40%)
  Pallas kernels  29.4 us (34%)
  waiting for transfers between devices  20.9 us (24%)
  other arithmetic  1.45 us (2%)
    pallas_call x6, Pallas kernels, experts(): pl.pallas_call(functools.partial(expert_kernel, min(256, half), len(block...  20.1 us
    ppermute x14, starting transfers between devices, send(): moving[side, piece] = lax.ppermute(value, 'seq', hops[side])  14.8 us
    ppermute x14, waiting for transfers between devices, send(): moving[side, piece] = lax.ppermute(value, 'seq', hops[side])  14.7 us
    ppermute x14, starting transfers between devices, bring(): came[side, distance, piece] = lax.ppermute(block, 'seq', hops[side])  14.4 us
    pallas_call x2, Pallas kernels, attend(): pl.pallas_call(functools.partial(attend_kernel, half, mix), in_specs=[sme...  8.99 us
    ppermute x2, starting transfers between devices, shifted(): lax.ppermute(value, axis, [(i, (i + by) % peers) for i in range(peers)])  4.04 us
    ppermute x14, waiting for transfers between devices, bring(): came[side, distance, piece] = lax.ppermute(block, 'seq', hops[side])  3.19 us
  transfers between devices with their start and end apart: 34, of which 17 were waited for; matrix products, arithmetic and copies ran while one was open for 1% of the time, Pallas kernels for 34%

profile of v7, /device:TPU:0, one launch (start us, length us, event | category | flops | bytes accessed | tf_op | source)
XLA Modules:
  0.0 86.3 jit_solution(312187086431506978)
XLA Ops:
  0.0 0.5 collective-permute-start.3
  0.5 0.5 collective-permute-start.5
  1.0 2.5 %collective-permute-start = (bf16[256,128]{1,0:T(8,128)(2,1)}, bf16[256,128]{1,0:T(8,128)(2,1)S(1)}, u32[]{:S(2)}, u32[]{:S(2)}) collective-permute-start(bf16[256,128]{1,0:T(8,128)(2,1)} %k_hbm.3), channel_id=1, source_target_pairs={{0,2},{2,4},{4,6},{6,8},{8,10},{10,12},{12,14},{14,0},{1,3},{3,5},... | collective-permute-start | bytes 196616 | tf_op jit(solution)/shard_map/ppermute | solution.py:24
  3.5 1.5 %collective-permute-start.1 = (bf16[256,128]{1,0:T(8,128)(2,1)}, bf16[256,128]{1,0:T(8,128)(2,1)S(1)}, u32[]{:S(2)}, u32[]{:S(2)}) collective-permute-start(bf16[256,128]{1,0:T(8,128)(2,1)} %v_hbm.3), channel_id=1, source_target_pairs={{0,2},{2,4},{4,6},{6,8},{8,10},{10,12},{12,14},{14,0},{1,3},{3,5},... | collective-permute-start | bytes 196616 | tf_op jit(solution)/shard_map/ppermute | solution.py:24
  5.0 4.5 %attend.2.rest_3_ = f32[128,1536]{1,0:T(8,128)S(1)} custom-call(s32[1]{0:T(128)} %constant.11.clone.1.first_ref, f32[1,16]{1,0:T(1,128)} %bitcast.17, bf16[256,1024]{1,0:T(8,128)(2,1)} %q_hbm.3, bf16[256,128]{1,0:T(8,128)(2,1)} %k_hbm.3, bf16[256,128]{1,0:T(8,128)(2,1)} %v_hbm.3, bf16[1024,1536]{1,0:T(8,128)(2,1)} %ow_hbm.3), custom_call_target="tpu_custom_call" | custom-call | flops 671088640 | bytes 6291456 | tf_op jit(solution)/shard_map/attend/pallas_call | solution.py:137
  9.6 1.2 %collective-permute-done.1.rest_1_ = bf16[256,128]{1,0:T(8,128)(2,1)S(1)} collective-permute-done((bf16[256,128]{1,0:T(8,128)(2,1)}, bf16[256,128]{1,0:T(8,128)(2,1)S(1)}, u32[]{:S(2)}, u32[]{:S(2)}) %collective-permute-start.1) | collective-permute-done | bytes 65568 | tf_op jit(solution)/shard_map/ppermute | solution.py:24
  10.9 4.5 %attend.3 = (bf16[128,1536]{1,0:T(8,128)(2,1)S(1)}, f32[128,1536]{1,0:T(8,128)S(1)}) custom-call(s32[1]{0:T(128)} %bitcast.first_ref, f32[1,16]{1,0:T(1,128)} %bitcast.18, bf16[256,1024]{1,0:T(8,128)(2,1)} %q_hbm.3, bf16[256,128]{1,0:T(8,128)(2,1)} %k_hbm.3, bf16[256,128]{1,0:T(8,128)(2,1)} %v_hbm.3, bf16[1024,1536]{1,0:T(8,128)(2,1)} %ow_hbm.3, ...), custom_call_target="tpu_custom_call" | custom-call | flops 671088640 | bytes 6291456 | tf_op jit(solution)/shard_map/attend/pallas_call | solution.py:137
  15.5 1.7 %collective-permute-done.2.came_ref = bf16[128,1536]{1,0:T(8,128)(2,1)S(1)} collective-permute-done((bf16[128,1536]{1,0:T(8,128)(2,1)S(1)}, bf16[128,1536]{1,0:T(8,128)(2,1)S(1)}, u32[]{:S(2)}, u32[]{:S(2)}) %collective-permute-start.2) | collective-permute-done | bytes 393248 | tf_op jit(solution)/shard_map/ppermute | solution.py:37
  17.7 1.9 %collective-permute-start.6 = (bf16[784,128]{1,0:T(8,128)(2,1)S(1)}, bf16[784,128]{1,0:T(8,128)(2,1)S(1)}, u32[]{:S(2)}, u32[]{:S(2)}) collective-permute-start(bf16[784,128]{1,0:T(8,128)(2,1)S(1)} %get-tuple-element.67.refs_0_), channel_id=1, source_target_pairs={{0,4},{4,8},{8,12},{12,14},{14,10},{10,6},{6,2},{2,0},{1,5},{5,9},... | collective-permute-start | bytes 602120 | tf_op jit(solution)/shard_map/out_lead1/ppermute | solution.py:324
  19.8 1.9 %collective-permute-start.9 = (bf16[784,128]{1,0:T(8,128)(2,1)S(1)}, bf16[784,128]{1,0:T(8,128)(2,1)S(1)}, u32[]{:S(2)}, u32[]{:S(2)}) collective-permute-start(bf16[784,128]{1,0:T(8,128)(2,1)S(1)} %get-tuple-element.68.refs_1_), channel_id=1, source_target_pairs={{0,4},{4,8},{8,12},{12,14},{14,10},{10,6},{6,2},{2,0},{1,5},{5,9},... | collective-permute-start | bytes 602120 | tf_op jit(solution)/shard_map/out_trail1/ppermute | solution.py:324
  21.6 6.0 %experts.6 = (bf16[64,1536]{1,0:T(8,128)(2,1)S(1)}, bf16[64,1536]{1,0:T(8,128)(2,1)S(1)}, bf16[1536,768]{1,0:T(8,128)(2,1)S(1)}, bf16[1536,768]{1,0:T(8,128)(2,1...) custom-call(s32[1]{0:T(128)} %bitcast.5.me_ref, ...), custom_call_target="tpu_custom_call" | custom-call | flops 1811939328 | bytes 1179648 | tf_op jit(solution)/shard_map/experts/pallas_call | solution.py:282
  27.9 1.9 %collective-permute-start.7 = (bf16[784,128]{1,0:T(8,128)(2,1)S(1)}, bf16[784,128]{1,0:T(8,128)(2,1)S(1)}, u32[]{:S(2)}, u32[]{:S(2)}) collective-permute-start(bf16[784,128]{1,0:T(8,128)(2,1)S(1)} %collective-permute-done.6.refs_0_), channel_id=1, source_target_pairs={{0,4},{4,8},{8,12},{12,14},{14,10},{10,6},{6,2},{2,0},{1,5},{5,9},... | collective-permute-start | bytes 602120 | tf_op jit(solution)/shard_map/out_lead2/ppermute | solution.py:324
  29.9 1.9 %collective-permute-start.13 = (bf16[784,128]{1,0:T(8,128)(2,1)S(1)}, bf16[784,128]{1,0:T(8,128)(2,1)S(1)}, u32[]{:S(2)}, u32[]{:S(2)}) collective-permute-start(bf16[784,128]{1,0:T(8,128)(2,1)S(1)} %collective-permute-done.9.refs_2_), channel_id=1, source_target_pairs={{0,4},{4,8},{8,12},{12,14},{14,10},{10,6},{6,2},{2,0},{1,5},{5,9},... | collective-permute-start | bytes 602120 | tf_op jit(solution)/shard_map/out_trail2/ppermute | solution.py:324
  31.8 3.9 %experts.7 = (bf16[64,1536]{1,0:T(8,128)(2,1)S(1)}, bf16[64,1536]{1,0:T(8,128)(2,1)S(1)}, bf16[64,1536]{1,0:T(8,128)(2,1)S(1)}, bf16[64,1536]{1,0:T(8,128)(2,1)S(1)}) custom-call(s32[1]{0:T(128)} %bitcast.5.me_ref, bf16[784,128]{1,0:T(8,128)(2,1)S(1)} %collective-permute-done.6.refs_0_, bf16[784,128]{1,0:T(8,128)(2,1)S(1)} %collective-permute-done.8.refs_1_, ...), custom_call_target="tpu_custom_call" | custom-call | flops 3623878656 | bytes 2359296 | tf_op jit(solution)/shard_map/hop1/experts/pallas_call | solution.py:282
  35.9 1.9 %collective-permute-start.11 = (bf16[784,128]{1,0:T(8,128)(2,1)S(1)}, bf16[784,128]{1,0:T(8,128)(2,1)S(1)}, u32[]{:S(2)}, u32[]{:S(2)}) collective-permute-start(bf16[784,128]{1,0:T(8,128)(2,1)S(1)} %collective-permute-done.7.refs_0_), channel_id=1, source_target_pairs={{0,4},{4,8},{8,12},{12,14},{14,10},{10,6},{6,2},{2,0},{1,5},{5,9},... | collective-permute-start | bytes 602120 | tf_op jit(solution)/shard_map/out_lead3/ppermute | solution.py:324
  37.8 1.7 %collective-permute-done.14.refs_3_ = bf16[784,128]{1,0:T(8,128)(2,1)S(1)} collective-permute-done((bf16[784,128]{1,0:T(8,128)(2,1)S(1)}, bf16[784,128]{1,0:T(8,128)(2,1)S(1)}, u32[]{:S(2)}, u32[]{:S(2)}) %collective-permute-start.14) | collective-permute-done | bytes 200736 | tf_op jit(solution)/shard_map/out_trail2/ppermute | solution.py:324
  39.5 3.9 %experts.8 = (bf16[64,1536]{1,0:T(8,128)(2,1)S(1)}, bf16[64,1536]{1,0:T(8,128)(2,1)S(1)}, bf16[64,1536]{1,0:T(8,128)(2,1)S(1)}, bf16[64,1536]{1,0:T(8,128)(2,1)S(1)}) custom-call(s32[1]{0:T(128)} %bitcast.5.me_ref, bf16[784,128]{1,0:T(8,128)(2,1)S(1)} %collective-permute-done.7.refs_0_, bf16[784,128]{1,0:T(8,128)(2,1)S(1)} %collective-permute-done.12.refs_1_, ...), custom_call_target="tpu_custom_call" | custom-call | flops 3623878656 | bytes 2359296 | tf_op jit(solution)/shard_map/hop2/experts/pallas_call | solution.py:282
  43.5 1.8 %collective-permute-start.15 = (bf16[784,128]{1,0:T(8,128)(2,1)S(1)}, bf16[784,128]{1,0:T(8,128)(2,1)S(1)}, u32[]{:S(2)}, u32[]{:S(2)}) collective-permute-start(bf16[784,128]{1,0:T(8,128)(2,1)S(1)} %collective-permute-done.11.refs_0_), channel_id=1, source_target_pairs={{0,4},{4,8},{8,12},{12,14},{14,10},{10,6},{6,2},{2,0},{1,5},{5,9},... | collective-permute-start | bytes 602120 | tf_op jit(solution)/shard_map/out_lead4/ppermute | solution.py:324
  45.5 1.5 %collective-permute-start.21 = (bf16[784,128]{1,0:T(8,128)(2,1)S(1)}, bf16[784,128]{1,0:T(8,128)(2,1)S(1)}, u32[]{:S(2)}, u32[]{:S(2)}) collective-permute-start(bf16[784,128]{1,0:T(8,128)(2,1)S(1)} %collective-permute-done.14.refs_3_), channel_id=1, source_target_pairs={{4,0},{8,4},{12,8},{14,12},{10,14},{6,10},{2,6},{0,2},{5,1},{9,5},... | collective-permute-start | bytes 602120 | tf_op jit(solution)/shard_map/out_trail3/ppermute | solution.py:324
  47.0 0.6 collective-permute-start.20
  47.6 2.1 %experts.9 = (bf16[64,1536]{1,0:T(8,128)(2,1)S(1)}, bf16[64,1536]{1,0:T(8,128)(2,1)S(1)}) custom-call(s32[1]{0:T(128)} %bitcast.5.me_ref, bf16[784,128]{1,0:T(8,128)(2,1)S(1)} %collective-permute-done.11.refs_0_, bf16[784,128]{1,0:T(8,128)(2,1)S(1)} %collective-permute-done.16.refs_1_, bf16[1536,768]{1,0:T(8,128)(2,1)S(1)} %get-tuple-element.71.refs_4_.refs_2_, ...), custom_call_target="tpu_custom_call" | custom-call | flops 1811939328 | bytes 1179648 | tf_op jit(solution)/shard_map/hop3/experts/pallas_call | solution.py:282
  49.7 0.5 collective-permute-done.15.refs_0_
  50.1 1.0 %collective-permute-done.17.refs_1_ = bf16[784,128]{1,0:T(8,128)(2,1)S(1)} collective-permute-done((bf16[784,128]{1,0:T(8,128)(2,1)S(1)}, bf16[784,128]{1,0:T(8,128)(2,1)S(1)}, u32[]{:S(2)}, u32[]{:S(2)}) %collective-permute-start.17) | collective-permute-done | bytes 200736 | tf_op jit(solution)/shard_map/out_lead4/ppermute | solution.py:324
  51.1 2.1 %experts.10 = (bf16[64,1536]{1,0:T(8,128)(2,1)S(1)}, bf16[64,1536]{1,0:T(8,128)(2,1)S(1)}) custom-call(s32[1]{0:T(128)} %bitcast.5.me_ref, bf16[784,128]{1,0:T(8,128)(2,1)S(1)} %collective-permute-done.15.refs_0_, bf16[784,128]{1,0:T(8,128)(2,1)S(1)} %collective-permute-done.17.refs_1_, bf16[1536,768]{1,0:T(8,128)(2,1)S(1)} %get-tuple-element.71.refs_4_.refs_2_, ...), custom_call_target="tpu_custom_call" | custom-call | flops 1811939328 | bytes 1179648 | tf_op jit(solution)/shard_map/hop4/experts/pallas_call | solution.py:282
  53.2 0.4 collective-permute-start.18
  53.6 1.7 %collective-permute-start.19 = (bf16[64,1536]{1,0:T(8,128)(2,1)S(1)}, bf16[64,1536]{1,0:T(8,128)(2,1)S(1)}, u32[]{:S(2)}, u32[]{:S(2)}) collective-permute-start(bf16[64,1536]{1,0:T(8,128)(2,1)S(1)} %get-tuple-element.89), channel_id=1, source_target_pairs={{4,0},{8,4},{12,8},{14,12},{10,14},{6,10},{2,6},{0,2},{5,1},{9,5},... | collective-permute-start | bytes 589832 | tf_op jit(solution)/shard_map/back_lead4/ppermute | solution.py:366
  55.3 1.1 %collective-permute-start.28 = (bf16[64,1536]{1,0:T(8,128)(2,1)S(1)}, bf16[64,1536]{1,0:T(8,128)(2,1)S(1)}, u32[]{:S(2)}, u32[]{:S(2)}) collective-permute-start(bf16[64,1536]{1,0:T(8,128)(2,1)S(1)} %get-tuple-element.105), channel_id=1, source_target_pairs={{4,0},{8,4},{12,8},{14,12},{10,14},{6,10},{2,6},{0,2},{5,1},{9,5},... | collective-permute-start | bytes 589832 | tf_op jit(solution)/shard_map/back_trail3/ppermute | solution.py:366
  56.4 0.9 %collective-permute-start.27 = (bf16[64,1536]{1,0:T(8,128)(2,1)S(1)}, bf16[64,1536]{1,0:T(8,128)(2,1)S(1)}, u32[]{:S(2)}, u32[]{:S(2)}) collective-permute-start(bf16[64,1536]{1,0:T(8,128)(2,1)S(1)} %get-tuple-element.104), channel_id=1, source_target_pairs={{0,4},{4,8},{8,12},{12,14},{14,10},{10,6},{6,2},{2,0},{1,5},{5,9},... | collective-permute-start | bytes 589832 | tf_op jit(solution)/shard_map/back_trail3/ppermute | solution.py:366
  57.3 2.1 %experts.11 = (bf16[64,1536]{1,0:T(8,128)(2,1)S(1)}, bf16[64,1536]{1,0:T(8,128)(2,1)S(1)}) custom-call(s32[1]{0:T(128)} %bitcast.5.me_ref, bf16[784,128]{1,0:T(8,128)(2,1)S(1)} %collective-permute-done.20.refs_0_, bf16[784,128]{1,0:T(8,128)(2,1)S(1)} %collective-permute-done.21.refs_1_, bf16[1536,768]{1,0:T(8,128)(2,1)S(1)} %get-tuple-element.71.refs_4_.refs_2_, ...), custom_call_target="tpu_custom_call" | custom-call | flops 1811939328 | bytes 1179648 | tf_op jit(solution)/shard_map/hop3/experts/pallas_call | solution.py:282
  59.5 1.8 %collective-permute-done.19 = bf16[64,1536]{1,0:T(8,128)(2,1)S(1)} collective-permute-done((bf16[64,1536]{1,0:T(8,128)(2,1)S(1)}, bf16[64,1536]{1,0:T(8,128)(2,1)S(1)}, u32[]{:S(2)}, u32[]{:S(2)}) %collective-permute-start.19) | collective-permute-done | bytes 196640 | tf_op jit(solution)/shard_map/back_lead4/ppermute | solution.py:366
  61.4 1.8 %collective-permute-start.23 = (bf16[64,1536]{1,0:T(8,128)(2,1)S(1)}, bf16[64,1536]{1,0:T(8,128)(2,1)S(1)}, u32[]{:S(2)}, u32[]{:S(2)}) collective-permute-start(bf16[64,1536]{1,0:T(8,128)(2,1)S(1)} %add_convert_fusion.8), channel_id=1, source_target_pairs={{4,0},{8,4},{12,8},{14,12},{10,14},{6,10},{2,6},{0,2},{5,1},{9,5},... | collective-permute-start | bytes 589832 | tf_op jit(solution)/shard_map/back_lead3/ppermute | solution.py:366
  63.5 2.0 %collective-permute-done.28 = bf16[64,1536]{1,0:T(8,128)(2,1)S(1)} collective-permute-done((bf16[64,1536]{1,0:T(8,128)(2,1)S(1)}, bf16[64,1536]{1,0:T(8,128)(2,1)S(1)}, u32[]{:S(2)}, u32[]{:S(2)}) %collective-permute-start.28) | collective-permute-done | bytes 196640 | tf_op jit(solution)/shard_map/back_trail3/ppermute | solution.py:366
  65.6 1.8 %collective-permute-start.30 = (bf16[64,1536]{1,0:T(8,128)(2,1)S(1)}, bf16[64,1536]{1,0:T(8,128)(2,1)S(1)}, u32[]{:S(2)}, u32[]{:S(2)}) collective-permute-start(bf16[64,1536]{1,0:T(8,128)(2,1)S(1)} %add_convert_fusion.3), channel_id=1, source_target_pairs={{4,0},{8,4},{12,8},{14,12},{10,14},{6,10},{2,6},{0,2},{5,1},{9,5},... | collective-permute-start | bytes 589832 | tf_op jit(solution)/shard_map/back_trail2/ppermute | solution.py:366
  67.8 2.0 %collective-permute-done.23 = bf16[64,1536]{1,0:T(8,128)(2,1)S(1)} collective-permute-done((bf16[64,1536]{1,0:T(8,128)(2,1)S(1)}, bf16[64,1536]{1,0:T(8,128)(2,1)S(1)}, u32[]{:S(2)}, u32[]{:S(2)}) %collective-permute-start.23) | collective-permute-done | bytes 196640 | tf_op jit(solution)/shard_map/back_lead3/ppermute | solution.py:366
  69.7 1.2 %collective-permute-done.22 = bf16[64,1536]{1,0:T(8,128)(2,1)S(1)} collective-permute-done((bf16[64,1536]{1,0:T(8,128)(2,1)S(1)}, bf16[64,1536]{1,0:T(8,128)(2,1)S(1)}, u32[]{:S(2)}, u32[]{:S(2)}) %collective-permute-start.22) | collective-permute-done | bytes 196640 | tf_op jit(solution)/shard_map/back_lead3/ppermute | solution.py:366
  71.0 0.6 collective-permute-start.25
  71.7 1.6 %collective-permute-start.24 = (bf16[64,1536]{1,0:T(8,128)(2,1)S(1)}, bf16[64,1536]{1,0:T(8,128)(2,1)S(1)}, u32[]{:S(2)}, u32[]{:S(2)}) collective-permute-start(bf16[64,1536]{1,0:T(8,128)(2,1)S(1)} %add_convert_fusion.7), channel_id=1, source_target_pairs={{0,4},{4,8},{8,12},{12,14},{14,10},{10,6},{6,2},{2,0},{1,5},{5,9},... | collective-permute-start | bytes 589832 | tf_op jit(solution)/shard_map/back_lead2/ppermute | solution.py:366
  73.2 0.7 collective-permute-done.30
  73.9 1.4 %collective-permute-done.29 = bf16[64,1536]{1,0:T(8,128)(2,1)S(1)} collective-permute-done((bf16[64,1536]{1,0:T(8,128)(2,1)S(1)}, bf16[64,1536]{1,0:T(8,128)(2,1)S(1)}, u32[]{:S(2)}, u32[]{:S(2)}) %collective-permute-start.29) | collective-permute-done | bytes 196640 | tf_op jit(solution)/shard_map/back_trail2/ppermute | solution.py:366
  75.4 0.5 collective-permute-start.31
  76.0 1.6 %collective-permute-start.32 = (bf16[64,1536]{1,0:T(8,128)(2,1)S(1)}, bf16[64,1536]{1,0:T(8,128)(2,1)S(1)}, u32[]{:S(2)}, u32[]{:S(2)}) collective-permute-start(bf16[64,1536]{1,0:T(8,128)(2,1)S(1)} %add_convert_fusion.1), channel_id=1, source_target_pairs={{0,4},{4,8},{8,12},{12,14},{14,10},{10,6},{6,2},{2,0},{1,5},{5,9},... | collective-permute-start | bytes 589832 | tf_op jit(solution)/shard_map/back_trail1/ppermute | solution.py:366
  77.6 1.0 %collective-permute-done.25 = bf16[64,1536]{1,0:T(8,128)(2,1)S(1)} collective-permute-done((bf16[64,1536]{1,0:T(8,128)(2,1)S(1)}, bf16[64,1536]{1,0:T(8,128)(2,1)S(1)}, u32[]{:S(2)}, u32[]{:S(2)}) %collective-permute-start.25) | collective-permute-done | bytes 196640 | tf_op jit(solution)/shard_map/back_lead2/ppermute | solution.py:366
  78.5 0.5 collective-permute-done.24
  79.1 0.6 collective-permute-start.26
  79.7 1.6 %collective-permute-start.33 = (bf16[64,1536]{1,0:T(8,128)(2,1)S(1)}, bf16[64,1536]{1,0:T(8,128)(2,1)S(1)}, u32[]{:S(2)}, u32[]{:S(2)}) collective-permute-start(bf16[64,1536]{1,0:T(8,128)(2,1)S(1)} %add_convert_fusion), channel_id=1, source_target_pairs={{4,0},{8,4},{12,8},{14,12},{10,14},{6,10},{2,6},{0,2},{5,1},{9,5},... | collective-permute-start | bytes 589832 | tf_op jit(solution)/shard_map/back_lead1/ppermute | solution.py:366
  81.3 3.5 %collective-permute-done.26 = bf16[64,1536]{1,0:T(8,128)(2,1)S(1)} collective-permute-done((bf16[64,1536]{1,0:T(8,128)(2,1)S(1)}, bf16[64,1536]{1,0:T(8,128)(2,1)S(1)}, u32[]{:S(2)}, u32[]{:S(2)}) %collective-permute-start.26) | collective-permute-done | bytes 196640 | tf_op jit(solution)/shard_map/back_lead1/ppermute | solution.py:366
  84.9 0.5 collective-permute-done.33
  85.5 0.8 fusion
  (53 shorter events, 3.3 us)
Async XLA Ops:
  0.0 17.5 %collective-permute-start.3 = (bf16[1536,768]{1,0:T(8,128)(2,1)}, bf16[1536,768]{1,0:T(8,128)(2,1)S(1)}, u32[]{:S(2)}, u32[]{:S(2)}) collective-permute-start(bf16[1536,768]{1,0:T(8,128)(2,1)} %bitcast.11), channel_id=1, source_target_pairs={{0,1},{1,0},{2,3},{3,2},{4,5},{5,4},{6,7},{7,6},{8,9},{9,8},{10,11... | collective-permute-start | bytes 7077896 | tf_op jit(solution)/shard_map/ppermute | solution.py:37
  0.5 17.1 %collective-permute-start.4 = (bf16[1536,768]{1,0:T(8,128)(2,1)}, bf16[1536,768]{1,0:T(8,128)(2,1)}, u32[]{:S(2)}, u32[]{:S(2)}) collective-permute-start(bf16[1536,768]{1,0:T(8,128)(2,1)} %bitcast.13), channel_id=1, source_target_pairs={{0,1},{1,0},{2,3},{3,2},{4,5},{5,4},{6,7},{7,6},{8,9},{9,8},{10,11... | collective-permute-start | bytes 7077896 | tf_op jit(solution)/shard_map/ppermute | solution.py:37
  0.5 17.0 %collective-permute-start.5 = (bf16[768,1536]{1,0:T(8,128)(2,1)}, bf16[768,1536]{1,0:T(8,128)(2,1)}, u32[]{:S(2)}, u32[]{:S(2)}) collective-permute-start(bf16[768,1536]{1,0:T(8,128)(2,1)} %bitcast.15), channel_id=1, source_target_pairs={{0,1},{1,0},{2,3},{3,2},{4,5},{5,4},{6,7},{7,6},{8,9},{9,8},{10,11... | collective-permute-start | bytes 7077896 | tf_op jit(solution)/shard_map/ppermute | solution.py:37
  1.0 8.7 %collective-permute-start = (bf16[256,128]{1,0:T(8,128)(2,1)}, bf16[256,128]{1,0:T(8,128)(2,1)S(1)}, u32[]{:S(2)}, u32[]{:S(2)}) collective-permute-start(bf16[256,128]{1,0:T(8,128)(2,1)} %k_hbm.3), channel_id=1, source_target_pairs={{0,2},{2,4},{4,6},{6,8},{8,10},{10,12},{12,14},{14,0},{1,3},{3,5},... | collective-permute-start | bytes 196616 | tf_op jit(solution)/shard_map/ppermute | solution.py:24
  3.5 7.4 %collective-permute-start.1 = (bf16[256,128]{1,0:T(8,128)(2,1)}, bf16[256,128]{1,0:T(8,128)(2,1)S(1)}, u32[]{:S(2)}, u32[]{:S(2)}) collective-permute-start(bf16[256,128]{1,0:T(8,128)(2,1)} %v_hbm.3), channel_id=1, source_target_pairs={{0,2},{2,4},{4,6},{6,8},{8,10},{10,12},{12,14},{14,0},{1,3},{3,5},... | collective-permute-start | bytes 196616 | tf_op jit(solution)/shard_map/ppermute | solution.py:24
  10.9 4.6 %copy-start.4 = (f32[1536]{0:T(1024)S(1)}, f32[1536]{0:T(1024)}, u32[]{:S(2)}) copy-start(f32[1536]{0:T(1024)} %param.18) | copy-start | bytes 18436
  10.9 6.3 %copy-start = (bf16[128,1536]{1,0:T(8,128)(2,1)S(1)}, bf16[128,1536]{1,0:T(8,128)(2,1)}, u32[]{:S(2)}) copy-start(bf16[128,1536]{1,0:T(8,128)(2,1)} %stream_ref.1) | copy-start | bytes 1179652
  10.9 6.3 %copy-start.1 = (s32[128,4]{0,1:T(4,128)S(1)}, s32[128,4]{0,1:T(4,128)}, u32[]{:S(2)}) copy-start(s32[128,4]{0,1:T(4,128)} %param.19) | copy-start | bytes 6148
  10.9 6.3 %copy-start.2 = (f32[128,4]{0,1:T(4,128)S(1)}, f32[128,4]{0,1:T(4,128)}, u32[]{:S(2)}) copy-start(f32[128,4]{0,1:T(4,128)} %param.20) | copy-start | bytes 6148
  15.4 1.8 %collective-permute-start.2 = (bf16[128,1536]{1,0:T(8,128)(2,1)S(1)}, bf16[128,1536]{1,0:T(8,128)(2,1)S(1)}, u32[]{:S(2)}, u32[]{:S(2)}) collective-permute-start(bf16[128,1536]{1,0:T(8,128)(2,1)S(1)} %get-tuple-element.63), channel_id=1, source_target_pairs={{0,1},{1,0},{2,3},{3,2},{4,5},{5,4},{6,7},{7,6},{8,9},{9,8},{10,11... | collective-permute-start | bytes 1179656 | tf_op jit(solution)/shard_map/ppermute | solution.py:37
  17.5 4.1 %copy-start.3 = (bf16[1536,768]{1,0:T(8,128)(2,1)}, bf16[1536,768]{1,0:T(8,128)(2,1)S(1)}, u32[]{:S(2)}) copy-start(bf16[1536,768]{1,0:T(8,128)(2,1)S(1)} %collective-permute-done.3.refs_5_) | copy-start | bytes 7077892
  17.5 10.1 %collective-permute-start.8 = (bf16[784,128]{1,0:T(8,128)(2,1)S(1)}, bf16[784,128]{1,0:T(8,128)(2,1)S(1)}, u32[]{:S(2)}, u32[]{:S(2)}) collective-permute-start(bf16[784,128]{1,0:T(8,128)(2,1)S(1)} %get-tuple-element.68.refs_1_), channel_id=1, source_target_pairs={{4,0},{8,4},{12,8},{14,12},{10,14},{6,10},{2,6},{0,2},{5,1},{9,5},... | collective-permute-start | bytes 602120 | tf_op jit(solution)/shard_map/out_lead1/ppermute | solution.py:324
  17.7 10.1 %collective-permute-start.6 = (bf16[784,128]{1,0:T(8,128)(2,1)S(1)}, bf16[784,128]{1,0:T(8,128)(2,1)S(1)}, u32[]{:S(2)}, u32[]{:S(2)}) collective-permute-start(bf16[784,128]{1,0:T(8,128)(2,1)S(1)} %get-tuple-element.67.refs_0_), channel_id=1, source_target_pairs={{0,4},{4,8},{8,12},{12,14},{14,10},{10,6},{6,2},{2,0},{1,5},{5,9},... | collective-permute-start | bytes 602120 | tf_op jit(solution)/shard_map/out_lead1/ppermute | solution.py:324
  19.6 10.1 %collective-permute-start.10 = (bf16[784,128]{1,0:T(8,128)(2,1)S(1)}, bf16[784,128]{1,0:T(8,128)(2,1)S(1)}, u32[]{:S(2)}, u32[]{:S(2)}) collective-permute-start(bf16[784,128]{1,0:T(8,128)(2,1)S(1)} %get-tuple-element.67.refs_0_), channel_id=1, source_target_pairs={{4,0},{8,4},{12,8},{14,12},{10,14},{6,10},{2,6},{0,2},{5,1},{9,5},... | collective-permute-start | bytes 602120 | tf_op jit(solution)/shard_map/out_trail1/ppermute | solution.py:324
  19.8 10.1 %collective-permute-start.9 = (bf16[784,128]{1,0:T(8,128)(2,1)S(1)}, bf16[784,128]{1,0:T(8,128)(2,1)S(1)}, u32[]{:S(2)}, u32[]{:S(2)}) collective-permute-start(bf16[784,128]{1,0:T(8,128)(2,1)S(1)} %get-tuple-element.68.refs_1_), channel_id=1, source_target_pairs={{0,4},{4,8},{8,12},{12,14},{14,10},{10,6},{6,2},{2,0},{1,5},{5,9},... | collective-permute-start | bytes 602120 | tf_op jit(solution)/shard_map/out_trail1/ppermute | solution.py:324
  27.7 8.0 %collective-permute-start.12 = (bf16[784,128]{1,0:T(8,128)(2,1)S(1)}, bf16[784,128]{1,0:T(8,128)(2,1)S(1)}, u32[]{:S(2)}, u32[]{:S(2)}) collective-permute-start(bf16[784,128]{1,0:T(8,128)(2,1)S(1)} %collective-permute-done.8.refs_1_), channel_id=1, source_target_pairs={{4,0},{8,4},{12,8},{14,12},{10,14},{6,10},{2,6},{0,2},{5,1},{9,5},... | collective-permute-start | bytes 602120 | tf_op jit(solution)/shard_map/out_lead2/ppermute | solution.py:324
  27.9 8.0 %collective-permute-start.7 = (bf16[784,128]{1,0:T(8,128)(2,1)S(1)}, bf16[784,128]{1,0:T(8,128)(2,1)S(1)}, u32[]{:S(2)}, u32[]{:S(2)}) collective-permute-start(bf16[784,128]{1,0:T(8,128)(2,1)S(1)} %collective-permute-done.6.refs_0_), channel_id=1, source_target_pairs={{0,4},{4,8},{8,12},{12,14},{14,10},{10,6},{6,2},{2,0},{1,5},{5,9},... | collective-permute-start | bytes 602120 | tf_op jit(solution)/shard_map/out_lead2/ppermute | solution.py:324
  29.7 9.8 %collective-permute-start.14 = (bf16[784,128]{1,0:T(8,128)(2,1)S(1)}, bf16[784,128]{1,0:T(8,128)(2,1)S(1)}, u32[]{:S(2)}, u32[]{:S(2)}) collective-permute-start(bf16[784,128]{1,0:T(8,128)(2,1)S(1)} %collective-permute-done.10.refs_3_), channel_id=1, source_target_pairs={{4,0},{8,4},{12,8},{14,12},{10,14},{6,10},{2,6},{0,2},{5,1},{9,5},... | collective-permute-start | bytes 602120 | tf_op jit(solution)/shard_map/out_trail2/ppermute | solution.py:324
  29.9 9.6 %collective-permute-start.13 = (bf16[784,128]{1,0:T(8,128)(2,1)S(1)}, bf16[784,128]{1,0:T(8,128)(2,1)S(1)}, u32[]{:S(2)}, u32[]{:S(2)}) collective-permute-start(bf16[784,128]{1,0:T(8,128)(2,1)S(1)} %collective-permute-done.9.refs_2_), channel_id=1, source_target_pairs={{0,4},{4,8},{8,12},{12,14},{14,10},{10,6},{6,2},{2,0},{1,5},{5,9},... | collective-permute-start | bytes 602120 | tf_op jit(solution)/shard_map/out_trail2/ppermute | solution.py:324
  35.7 9.6 %collective-permute-start.16 = (bf16[784,128]{1,0:T(8,128)(2,1)S(1)}, bf16[784,128]{1,0:T(8,128)(2,1)S(1)}, u32[]{:S(2)}, u32[]{:S(2)}) collective-permute-start(bf16[784,128]{1,0:T(8,128)(2,1)S(1)} %collective-permute-done.12.refs_1_), channel_id=1, source_target_pairs={{4,0},{8,4},{12,8},{14,12},{10,14},{6,10},{2,6},{0,2},{5,1},{9,5},... | collective-permute-start | bytes 602120 | tf_op jit(solution)/shard_map/out_lead3/ppermute | solution.py:324
  35.9 7.5 %collective-permute-start.11 = (bf16[784,128]{1,0:T(8,128)(2,1)S(1)}, bf16[784,128]{1,0:T(8,128)(2,1)S(1)}, u32[]{:S(2)}, u32[]{:S(2)}) collective-permute-start(bf16[784,128]{1,0:T(8,128)(2,1)S(1)} %collective-permute-done.7.refs_0_), channel_id=1, source_target_pairs={{0,4},{4,8},{8,12},{12,14},{14,10},{10,6},{6,2},{2,0},{1,5},{5,9},... | collective-permute-start | bytes 602120 | tf_op jit(solution)/shard_map/out_lead3/ppermute | solution.py:324
  43.5 6.7 %collective-permute-start.15 = (bf16[784,128]{1,0:T(8,128)(2,1)S(1)}, bf16[784,128]{1,0:T(8,128)(2,1)S(1)}, u32[]{:S(2)}, u32[]{:S(2)}) collective-permute-start(bf16[784,128]{1,0:T(8,128)(2,1)S(1)} %collective-permute-done.11.refs_0_), channel_id=1, source_target_pairs={{0,4},{4,8},{8,12},{12,14},{14,10},{10,6},{6,2},{2,0},{1,5},{5,9},... | collective-permute-start | bytes 602120 | tf_op jit(solution)/shard_map/out_lead4/ppermute | solution.py:324
  45.3 5.9 %collective-permute-start.17 = (bf16[784,128]{1,0:T(8,128)(2,1)S(1)}, bf16[784,128]{1,0:T(8,128)(2,1)S(1)}, u32[]{:S(2)}, u32[]{:S(2)}) collective-permute-start(bf16[784,128]{1,0:T(8,128)(2,1)S(1)} %collective-permute-done.16.refs_1_), channel_id=1, source_target_pairs={{4,0},{8,4},{12,8},{14,12},{10,14},{6,10},{2,6},{0,2},{5,1},{9,5},... | collective-permute-start | bytes 602120 | tf_op jit(solution)/shard_map/out_lead4/ppermute | solution.py:324
  45.5 11.8 %collective-permute-start.21 = (bf16[784,128]{1,0:T(8,128)(2,1)S(1)}, bf16[784,128]{1,0:T(8,128)(2,1)S(1)}, u32[]{:S(2)}, u32[]{:S(2)}) collective-permute-start(bf16[784,128]{1,0:T(8,128)(2,1)S(1)} %collective-permute-done.14.refs_3_), channel_id=1, source_target_pairs={{4,0},{8,4},{12,8},{14,12},{10,14},{6,10},{2,6},{0,2},{5,1},{9,5},... | collective-permute-start | bytes 602120 | tf_op jit(solution)/shard_map/out_trail3/ppermute | solution.py:324
  47.0 8.3 %collective-permute-start.20 = (bf16[784,128]{1,0:T(8,128)(2,1)S(1)}, bf16[784,128]{1,0:T(8,128)(2,1)S(1)}, u32[]{:S(2)}, u32[]{:S(2)}) collective-permute-start(bf16[784,128]{1,0:T(8,128)(2,1)S(1)} %collective-permute-done.13.refs_2_), channel_id=1, source_target_pairs={{0,4},{4,8},{8,12},{12,14},{14,10},{10,6},{6,2},{2,0},{1,5},{5,9},... | collective-permute-start | bytes 602120 | tf_op jit(solution)/shard_map/out_trail3/ppermute | solution.py:324
  53.2 6.3 %collective-permute-start.18 = (bf16[64,1536]{1,0:T(8,128)(2,1)S(1)}, bf16[64,1536]{1,0:T(8,128)(2,1)S(1)}, u32[]{:S(2)}, u32[]{:S(2)}) collective-permute-start(bf16[64,1536]{1,0:T(8,128)(2,1)S(1)} %get-tuple-element.88), channel_id=1, source_target_pairs={{0,4},{4,8},{8,12},{12,14},{14,10},{10,6},{6,2},{2,0},{1,5},{5,9},... | collective-permute-start | bytes 589832 | tf_op jit(solution)/shard_map/back_lead4/ppermute | solution.py:366
  53.6 7.7 %collective-permute-start.19 = (bf16[64,1536]{1,0:T(8,128)(2,1)S(1)}, bf16[64,1536]{1,0:T(8,128)(2,1)S(1)}, u32[]{:S(2)}, u32[]{:S(2)}) collective-permute-start(bf16[64,1536]{1,0:T(8,128)(2,1)S(1)} %get-tuple-element.89), channel_id=1, source_target_pairs={{4,0},{8,4},{12,8},{14,12},{10,14},{6,10},{2,6},{0,2},{5,1},{9,5},... | collective-permute-start | bytes 589832 | tf_op jit(solution)/shard_map/back_lead4/ppermute | solution.py:366
  55.3 10.2 %collective-permute-start.28 = (bf16[64,1536]{1,0:T(8,128)(2,1)S(1)}, bf16[64,1536]{1,0:T(8,128)(2,1)S(1)}, u32[]{:S(2)}, u32[]{:S(2)}) collective-permute-start(bf16[64,1536]{1,0:T(8,128)(2,1)S(1)} %get-tuple-element.105), channel_id=1, source_target_pairs={{4,0},{8,4},{12,8},{14,12},{10,14},{6,10},{2,6},{0,2},{5,1},{9,5},... | collective-permute-start | bytes 589832 | tf_op jit(solution)/shard_map/back_trail3/ppermute | solution.py:366
  56.4 9.1 %collective-permute-start.27 = (bf16[64,1536]{1,0:T(8,128)(2,1)S(1)}, bf16[64,1536]{1,0:T(8,128)(2,1)S(1)}, u32[]{:S(2)}, u32[]{:S(2)}) collective-permute-start(bf16[64,1536]{1,0:T(8,128)(2,1)S(1)} %get-tuple-element.104), channel_id=1, source_target_pairs={{0,4},{4,8},{8,12},{12,14},{14,10},{10,6},{6,2},{2,0},{1,5},{5,9},... | collective-permute-start | bytes 589832 | tf_op jit(solution)/shard_map/back_trail3/ppermute | solution.py:366
  61.4 8.4 %collective-permute-start.23 = (bf16[64,1536]{1,0:T(8,128)(2,1)S(1)}, bf16[64,1536]{1,0:T(8,128)(2,1)S(1)}, u32[]{:S(2)}, u32[]{:S(2)}) collective-permute-start(bf16[64,1536]{1,0:T(8,128)(2,1)S(1)} %add_convert_fusion.8), channel_id=1, source_target_pairs={{4,0},{8,4},{12,8},{14,12},{10,14},{6,10},{2,6},{0,2},{5,1},{9,5},... | collective-permute-start | bytes 589832 | tf_op jit(solution)/shard_map/back_lead3/ppermute | solution.py:366
  63.2 7.7 %collective-permute-start.22 = (bf16[64,1536]{1,0:T(8,128)(2,1)S(1)}, bf16[64,1536]{1,0:T(8,128)(2,1)S(1)}, u32[]{:S(2)}, u32[]{:S(2)}) collective-permute-start(bf16[64,1536]{1,0:T(8,128)(2,1)S(1)} %add_convert_fusion.9), channel_id=1, source_target_pairs={{0,4},{4,8},{8,12},{12,14},{14,10},{10,6},{6,2},{2,0},{1,5},{5,9},... | collective-permute-start | bytes 589832 | tf_op jit(solution)/shard_map/back_lead3/ppermute | solution.py:366
  65.6 8.4 %collective-permute-start.30 = (bf16[64,1536]{1,0:T(8,128)(2,1)S(1)}, bf16[64,1536]{1,0:T(8,128)(2,1)S(1)}, u32[]{:S(2)}, u32[]{:S(2)}) collective-permute-start(bf16[64,1536]{1,0:T(8,128)(2,1)S(1)} %add_convert_fusion.3), channel_id=1, source_target_pairs={{4,0},{8,4},{12,8},{14,12},{10,14},{6,10},{2,6},{0,2},{5,1},{9,5},... | collective-permute-start | bytes 589832 | tf_op jit(solution)/shard_map/back_trail2/ppermute | solution.py:366
  67.4 7.9 %collective-permute-start.29 = (bf16[64,1536]{1,0:T(8,128)(2,1)S(1)}, bf16[64,1536]{1,0:T(8,128)(2,1)S(1)}, u32[]{:S(2)}, u32[]{:S(2)}) collective-permute-start(bf16[64,1536]{1,0:T(8,128)(2,1)S(1)} %add_convert_fusion.4), channel_id=1, source_target_pairs={{0,4},{4,8},{8,12},{12,14},{14,10},{10,6},{6,2},{2,0},{1,5},{5,9},... | collective-permute-start | bytes 589832 | tf_op jit(solution)/shard_map/back_trail2/ppermute | solution.py:366
  71.0 7.5 %collective-permute-start.25 = (bf16[64,1536]{1,0:T(8,128)(2,1)S(1)}, bf16[64,1536]{1,0:T(8,128)(2,1)S(1)}, u32[]{:S(2)}, u32[]{:S(2)}) collective-permute-start(bf16[64,1536]{1,0:T(8,128)(2,1)S(1)} %add_convert_fusion.6), channel_id=1, source_target_pairs={{4,0},{8,4},{12,8},{14,12},{10,14},{6,10},{2,6},{0,2},{5,1},{9,5},... | collective-permute-start | bytes 589832 | tf_op jit(solution)/shard_map/back_lead2/ppermute | solution.py:366
  71.7 7.4 %collective-permute-start.24 = (bf16[64,1536]{1,0:T(8,128)(2,1)S(1)}, bf16[64,1536]{1,0:T(8,128)(2,1)S(1)}, u32[]{:S(2)}, u32[]{:S(2)}) collective-permute-start(bf16[64,1536]{1,0:T(8,128)(2,1)S(1)} %add_convert_fusion.7), channel_id=1, source_target_pairs={{0,4},{4,8},{8,12},{12,14},{14,10},{10,6},{6,2},{2,0},{1,5},{5,9},... | collective-permute-start | bytes 589832 | tf_op jit(solution)/shard_map/back_lead2/ppermute | solution.py:366
  75.4 5.9 %collective-permute-start.31 = (bf16[64,1536]{1,0:T(8,128)(2,1)S(1)}, bf16[64,1536]{1,0:T(8,128)(2,1)S(1)}, u32[]{:S(2)}, u32[]{:S(2)}) collective-permute-start(bf16[64,1536]{1,0:T(8,128)(2,1)S(1)} %add_convert_fusion.2), channel_id=1, source_target_pairs={{4,0},{8,4},{12,8},{14,12},{10,14},{6,10},{2,6},{0,2},{5,1},{9,5},... | collective-permute-start | bytes 589832 | tf_op jit(solution)/shard_map/back_trail1/ppermute | solution.py:366
  76.0 8.9 %collective-permute-start.32 = (bf16[64,1536]{1,0:T(8,128)(2,1)S(1)}, bf16[64,1536]{1,0:T(8,128)(2,1)S(1)}, u32[]{:S(2)}, u32[]{:S(2)}) collective-permute-start(bf16[64,1536]{1,0:T(8,128)(2,1)S(1)} %add_convert_fusion.1), channel_id=1, source_target_pairs={{0,4},{4,8},{8,12},{12,14},{14,10},{10,6},{6,2},{2,0},{1,5},{5,9},... | collective-permute-start | bytes 589832 | tf_op jit(solution)/shard_map/back_trail1/ppermute | solution.py:366
  79.1 5.7 %collective-permute-start.26 = (bf16[64,1536]{1,0:T(8,128)(2,1)S(1)}, bf16[64,1536]{1,0:T(8,128)(2,1)S(1)}, u32[]{:S(2)}, u32[]{:S(2)}) collective-permute-start(bf16[64,1536]{1,0:T(8,128)(2,1)S(1)} %add_convert_fusion.5), channel_id=1, source_target_pairs={{0,4},{4,8},{8,12},{12,14},{14,10},{10,6},{6,2},{2,0},{1,5},{5,9},... | collective-permute-start | bytes 589832 | tf_op jit(solution)/shard_map/back_lead1/ppermute | solution.py:366
  79.7 5.7 %collective-permute-start.33 = (bf16[64,1536]{1,0:T(8,128)(2,1)S(1)}, bf16[64,1536]{1,0:T(8,128)(2,1)S(1)}, u32[]{:S(2)}, u32[]{:S(2)}) collective-permute-start(bf16[64,1536]{1,0:T(8,128)(2,1)S(1)} %add_convert_fusion), channel_id=1, source_target_pairs={{4,0},{8,4},{12,8},{14,12},{10,14},{6,10},{2,6},{0,2},{5,1},{9,5},... | collective-permute-start | bytes 589832 | tf_op jit(solution)/shard_map/back_lead1/ppermute | solution.py:366

commit v8 on v7

--- a/solution.py
+++ b/solution.py
@@ -41,44 +41,47 @@
     return jnp.dot(a, b, preferred_element_type=jnp.float32)
 
 
-def attend_kernel(half, mix, first_ref, sink_hbm, q_hbm, k_hbm, v_hbm, ow_hbm, *rest):
+def attend_kernel(mix, *refs):
+    done_ref = refs[-2]
+    rows = done_ref.shape[0]
+    keys = 2 * rows
     if mix:
-        k_before, v_before, rank_ref, other_ref, send_ref, own_ref = rest[:6]
+        sink_ref, q_ref, k_ref, v_ref, ow_ref = refs[:5]
+        first_ref, k_before, v_before, rank_ref, other_ref, send_ref, own_ref = refs[5:12]
+        queries = slice(0, rows)
+        k = jnp.concatenate([k_before[rows:], k_ref[:rows]], axis=0)
+        v = jnp.concatenate([v_before[rows:], v_ref[:rows]], axis=0)
+        copies = []
     else:
-        out_ref = rest[0]
-    sink_ref, q_ref, k_ref, v_ref, ow_ref, done_ref, sems = rest[-7:]
-    rows, keys = q_ref.shape[0], 2 * q_ref.shape[0]
+        sink_ref, q_ref, k_ref, v_ref, ow_ref, out_ref = refs[5:11]
+        queries = slice(rows, 2 * rows)
+        sems = refs[-1]
+        early, late = pl.ds(0, rows), pl.ds(rows, rows)
+        sources = [(refs[2], k_ref), (refs[3], v_ref), (refs[1].at[late], q_ref.at[late])]
+        sources += [(refs[0], sink_ref), (refs[4], ow_ref), (refs[1].at[early], q_ref.at[early])]
+        copies = [
+            pltpu.make_async_copy(here, there, sems.at[index])
+            for index, (here, there) in enumerate(sources)
+        ]
+        for copy in copies:
+            copy.start()
+        for copy in copies[:4]:
+            copy.wait()
+        k, v = k_ref[...], v_ref[...]
     pairs = q_ref.shape[1] // LANES
     groups = k_ref.shape[1] // HEAD_DIM
-    spans = (pl.ds(half * rows, rows), pl.ds(0, k_ref.shape[0]))
-    copies = [
-        pltpu.make_async_copy(k_hbm.at[spans[1]], k_ref, sems.at[0]),
-        pltpu.make_async_copy(v_hbm.at[spans[1]], v_ref, sems.at[1]),
-        pltpu.make_async_copy(q_hbm.at[spans[0]], q_ref, sems.at[2]),
-        pltpu.make_async_copy(sink_hbm, sink_ref, sems.at[3]),
-        pltpu.make_async_copy(ow_hbm, ow_ref, sems.at[4]),
-    ]
-    for copy in copies:
-        copy.start()
-    for copy in copies[:4]:
-        copy.wait()
 
     low = lax.broadcasted_iota(jnp.int32, (keys, LANES), 1) < HEAD_DIM
-    k, v = k_ref[...], v_ref[...]
-    if mix:
-        k = jnp.concatenate([k_before[rows:], k], axis=0)
-        v = jnp.concatenate([v_before[rows:], v], axis=0)
     k = k.astype(jnp.float32) * (1.0 / math.sqrt(HEAD_DIM))
     v = v.astype(jnp.float32)
     k_turned, v_turned = pltpu.roll(k, HEAD_DIM, 1), pltpu.roll(v, HEAD_DIM, 1)
-    one_low = jnp.where(low, 1.0, 0.0)
-
-    row = lax.broadcasted_iota(jnp.int32, (rows, keys), 0)
-    column = lax.broadcasted_iota(jnp.int32, (rows, keys), 1)
-    allowed = (column <= row + rows) & (column > row)
+    key = lax.broadcasted_iota(jnp.int32, (keys, rows), 0)
+    query = lax.broadcasted_iota(jnp.int32, (keys, rows), 1)
+    allowed = (key <= query + rows) & (key > query)
     if mix:
-        allowed = allowed & (column >= jnp.where(first_ref[0] == 1, rows, 0))
-    low_out = lax.broadcasted_iota(jnp.int32, (rows, LANES), 1) < HEAD_DIM
+        allowed = allowed & (key >= jnp.where(first_ref[0] == 1, rows, 0))
+    ones = jnp.ones((8, keys), jnp.float32)
+    zeros = jnp.zeros((8, keys), jnp.float32)
 
     for group in range(groups):
         here, there = (k, v), (k_turned, v_turned)
@@ -86,30 +89,38 @@
         kk = jnp.concatenate(
             [jnp.where(low, lows[0], 0.0), jnp.where(low, 0.0, highs[0])], axis=0
         ).astype(jnp.bfloat16)
+        v_low = jnp.where(low, lows[1], 0.0).T
+        v_high = jnp.where(low, 0.0, highs[1]).T
         vv = jnp.concatenate(
             [
-                jnp.concatenate([jnp.where(low, lows[1], 0.0), one_low], axis=1),
-                jnp.concatenate([jnp.where(low, 0.0, highs[1]), 1.0 - one_low], axis=1),
+                jnp.concatenate([v_low, v_high], axis=1),
+                jnp.concatenate([ones, zeros], axis=1),
+                jnp.concatenate([zeros, ones], axis=1),
             ],
             axis=0,
         ).astype(jnp.bfloat16)
         for pair in range(group * pairs // groups, (group + 1) * pairs // groups):
             lanes = slice(pair * LANES, (pair + 1) * LANES)
             scores = lax.dot_general(
-                q_ref[:, lanes], kk, (((1,), (1,)), ((), ())), preferred_element_type=jnp.float32
+                kk, q_ref[queries, lanes], (((1,), (1,)), ((), ())), preferred_element_type=jnp.float32
             )
             weights, sinks = [], []
             for side in range(2):
-                part = jnp.where(allowed, scores[:, side * keys : (side + 1) * keys], -jnp.inf)
+                part = jnp.where(allowed, scores[side * keys : (side + 1) * keys], -jnp.inf)
                 sink = sink_ref[:, 2 * pair + side : 2 * pair + side + 1]
-                highest = jnp.maximum(jnp.max(part, axis=1, keepdims=True), sink)
+                highest = jnp.maximum(jnp.max(part, axis=0, keepdims=True), sink)
                 weights.append(jnp.exp(part - highest).astype(jnp.bfloat16))
                 sinks.append(jnp.exp(sink - highest))
-            both = mm(jnp.concatenate(weights, axis=1), vv)
-            below = both[:, LANES:] + jnp.where(low_out, sinks[0], sinks[1])
-            done_ref[:, lanes] = (both[:, :LANES] / below).astype(jnp.bfloat16)
-
-    copies[4].wait()
+            both = mm(vv, jnp.concatenate(weights, axis=0))
+            parts = [
+                both[side * HEAD_DIM : (side + 1) * HEAD_DIM]
+                / (both[LANES + 8 * side : LANES + 8 * side + 1] + sinks[side])
+                for side in range(2)
+            ]
+            done_ref[:, lanes] = jnp.concatenate(parts, axis=0).T.astype(jnp.bfloat16)
+
+    for copy in copies[4:]:
+        copy.wait()
     model = ow_ref.shape[1]
     width = 512 if model % 512 == 0 else model
     if mix:
@@ -125,39 +136,33 @@
             out_ref[:, lanes] = mine
 
 
-def attend(half, first, sinks, queries, keys, values, out_weight, before=(), rank=None, other=None):
-    mix = bool(before)
+def attend(sinks, queries, keys, values, out_weight, mixed=()):
+    mix = bool(mixed)
     rows, width, model = WINDOW, queries.shape[1], out_weight.shape[1]
-    local = rows if mix else 2 * rows
     smem = pl.BlockSpec(memory_space=pltpu.SMEM)
     vmem = pl.BlockSpec(memory_space=pltpu.VMEM)
     hbm = pl.BlockSpec(memory_space=pltpu.HBM)
+    operands = (sinks, queries, keys, values, out_weight)
     wide = jax.ShapeDtypeStruct((rows, model), jnp.float32)
     narrow = jax.ShapeDtypeStruct((rows, model), jnp.bfloat16)
+    shapes = (narrow, wide)
+    if not mix:
+        shapes = tuple(jax.ShapeDtypeStruct(a.shape, a.dtype) for a in operands) + (wide,)
     return pl.pallas_call(
-        functools.partial(attend_kernel, half, mix),
-        in_specs=[smem] + [hbm] * 5 + ([vmem, vmem, smem, vmem] if mix else []),
-        out_specs=(vmem, vmem) if mix else vmem,
-        out_shape=(narrow, wide) if mix else wide,
+        functools.partial(attend_kernel, mix),
+        in_specs=[vmem if mix else hbm] * 5 + ([smem, vmem, vmem, smem, vmem] if mix else []),
+        out_specs=(vmem,) * len(shapes),
+        out_shape=shapes,
         scratch_shapes=[
-            pltpu.VMEM((1, sinks.shape[0]), jnp.float32),
             pltpu.VMEM((rows, width), jnp.bfloat16),
-            pltpu.VMEM((local, LANES), jnp.bfloat16),
-            pltpu.VMEM((local, LANES), jnp.bfloat16),
-            pltpu.VMEM((width, model), jnp.bfloat16),
-            pltpu.VMEM((rows, width), jnp.bfloat16),
-            pltpu.SemaphoreType.DMA((5,)),
+            pltpu.SemaphoreType.DMA((6,)),
         ],
         compiler_params=pltpu.CompilerParams(vmem_limit_bytes=8 * MIB),
         cost_estimate=pl.CostEstimate(
             flops=2 * rows * width * (model + 1024), bytes_accessed=6 * MIB, transcendentals=0
         ),
         name="attend",
-    )(
-        first,
-        *pinned((sinks.reshape(1, -1), queries, keys, values, out_weight), pltpu.HBM),
-        *((*before, rank, other) if mix else ()),
-    )
+    )(*pinned(operands, pltpu.VMEM if mix else pltpu.HBM), *mixed)
 
 
 def norm_kernel(
@@ -217,14 +222,14 @@
     out_refs, rest = refs[count + 6 : 2 * count + 6], refs[2 * count + 6 :]
     copies = []
     if load:
-        kept, rest = rest[:6], rest[6:]
+        kept, rest = rest[:3], rest[3:]
         copies = [
             pltpu.make_async_copy(here, there, rest[2].at[index])
-            for index, (here, there) in enumerate(zip(halves, kept))
+            for index, (here, there) in enumerate(zip(halves[3:], kept))
         ]
-        for index in (0, 1, 3, 4, 2, 5):
-            copies[index].start()
-        halves = kept
+        for copy in copies:
+            copy.start()
+        halves = halves[:3] + kept
     x, hidden = rest[:2]
     model, half = halves[0].shape
     rows = x.shape[0] // count
@@ -248,10 +253,11 @@
         hidden[:, side * half + at : side * half + at + tile] = activated.astype(jnp.bfloat16)
 
     for side in range(2):
-        arrived(3 * side, 3 * side + 1)
+        if side == 1:
+            arrived(0, 1)
         for at in range(0, half, tile):
             work(side, at)
-    arrived(2, 5)
+    arrived(2)
 
     me = me_ref[0]
     scales = []
@@ -274,7 +280,7 @@
     rows = size * len(blocks)
     vmem = pl.BlockSpec(memory_space=pltpu.VMEM)
     hbm = pl.BlockSpec(memory_space=pltpu.HBM)
-    kept = [jax.ShapeDtypeStruct(w.shape, w.dtype) for w in halves] if load else []
+    kept = [jax.ShapeDtypeStruct(w.shape, w.dtype) for w in halves[3:]] if load else []
     scratch = [
         pltpu.VMEM((rows, model), jnp.bfloat16),
         pltpu.VMEM((rows, 2 * half), jnp.bfloat16),
@@ -283,16 +289,22 @@
         functools.partial(expert_kernel, min(256, half), len(blocks), load),
         in_specs=[pl.BlockSpec(memory_space=pltpu.SMEM)]
         + [vmem] * len(blocks)
-        + [hbm if load else vmem] * 6,
+        + [vmem] * 3
+        + [hbm if load else vmem] * 3,
         out_specs=[vmem] * (len(blocks) + len(kept)),
         out_shape=[jax.ShapeDtypeStruct((size, model), jnp.bfloat16)] * len(blocks) + kept,
-        scratch_shapes=scratch + ([pltpu.SemaphoreType.DMA((6,))] if load else []),
+        scratch_shapes=scratch + ([pltpu.SemaphoreType.DMA((3,))] if load else []),
         compiler_params=pltpu.CompilerParams(vmem_limit_bytes=EXPERT_VMEM),
         cost_estimate=pl.CostEstimate(
             flops=12 * rows * model * half, bytes_accessed=6 * rows * model, transcendentals=0
         ),
         name="experts",
-    )(me, *blocks, *pinned(halves, pltpu.HBM if load else pltpu.VMEM))
+    )(
+        me,
+        *blocks,
+        *pinned(halves[:3], pltpu.VMEM),
+        *pinned(halves[3:], pltpu.HBM if load else pltpu.VMEM),
+    )
 
 
 def ring_experts(residual, pieces, gate_weight, up_weight, down_weight, others):
@@ -311,15 +323,15 @@
 
     halves = (gate_weight, up_weight, down_weight) + tuple(others)
     outs = experts(pieces, me, halves, load=True)
-    halves = outs[2:]
+    halves = halves[:3] + tuple(outs[2:])
     keep([(0, 0, 0), (0, 0, 1)], outs)
     worked = {0: outs[0]}
     came = {(side, 0, piece): pieces[piece] for side in sides for piece in sides}
 
     def bring(distance, lead, *after):
-        for side in sides:
-            piece = side if lead else 1 - side
-            block = tied(came[side, distance - 1, piece], *after)
+        keys = [(side, distance - 1, side if lead else 1 - side) for side in sides]
+        met = lax.optimization_barrier((*(came[key] for key in keys), *after))
+        for (side, _, piece), block in zip(keys, met):
             with jax.named_scope(f"out_{'lead' if lead else 'trail'}{distance}"):
                 came[side, distance, piece] = lax.ppermute(block, "seq", hops[side])
 
@@ -444,11 +456,11 @@
     others = []
     if use_ring:
         others = [swapped(w, "rep") for w in (gate_weight, up_weight, down_weight)]
-    never = jnp.zeros((1,), jnp.int32)
     first = (seq == 0).astype(jnp.int32).reshape(1)
-    shared = (sink_logits, queries, key_rows, value_rows, out_weight)
-    later_half = attend(1, never, *shared)
-    send, own = attend(0, first, *shared, (k_before, v_before), rank, later_half)
+    *operands, later_half = attend(
+        sink_logits.reshape(1, -1), queries, key_rows, value_rows, out_weight
+    )
+    send, own = attend(*operands, (first, k_before, v_before, rank, later_half))
     came = swapped(send, "rep")
     expert_count = lax.axis_size("seq") * EXP_DEV if use_ring else 0
     residual, *pieces = norm(

time: 86.4 us -> 84.4 us (0.977)
  Pallas kernels: 29.4 us -> 24.5 us
  waiting for transfers between devices: 20.9 us -> 23.7 us
    pallas_call x2, Pallas kernels: 8.99 us -> 5.96 us  [attend(): pl.pallas_call(functools.partial(attend_kernel, mix), in_specs=[vmem if m...]
    pallas_call x6, Pallas kernels: 20.1 us -> 18.2 us  [experts(): pl.pallas_call(functools.partial(expert_kernel, min(256, half), len(block...]
    ppermute x14, waiting for transfers between devices: 14.7 us -> 15.7 us  [send(): moving[side, piece] = lax.ppermute(value, 'seq', hops[side])]
  transfers between devices with their start and end apart: 34 -> 34, of which waited for: 17 -> 18; matrix products, arithmetic and copies ran while one was open for 1% -> 1% of each run, Pallas kernels for 34% -> 29%
where the time goes in v8:
time: 84.4 us; the launch traced here: 84.3 us
  starting transfers between devices  34.4 us (41%)
  Pallas kernels  24.5 us (29%)
  waiting for transfers between devices  23.7 us (28%)
  other arithmetic  1.46 us (2%)
    pallas_call x6, Pallas kernels, experts(): pl.pallas_call(functools.partial(expert_kernel, min(256, half), len(block...  18.2 us
    ppermute x14, waiting for transfers between devices, send(): moving[side, piece] = lax.ppermute(value, 'seq', hops[side])  15.7 us
    ppermute x14, starting transfers between devices, send(): moving[side, piece] = lax.ppermute(value, 'seq', hops[side])  14.8 us
    ppermute x14, starting transfers between devices, bring(): came[side, distance, piece] = lax.ppermute(block, 'seq', hops[side])  14.6 us
    pallas_call x2, Pallas kernels, attend(): pl.pallas_call(functools.partial(attend_kernel, mix), in_specs=[vmem if m...  5.96 us
    ppermute x2, starting transfers between devices, shifted(): lax.ppermute(value, axis, [(i, (i + by) % peers) for i in range(peers)])  4.04 us
    ppermute x14, waiting for transfers between devices, bring(): came[side, distance, piece] = lax.ppermute(block, 'seq', hops[side])  4.03 us
    ppermute x2, waiting for transfers between devices, shifted(): lax.ppermute(value, axis, [(i, (i + by) % peers) for i in range(peers)])  2.23 us
  transfers between devices with their start and end apart: 34, of which 18 were waited for; matrix products, arithmetic and copies ran while one was open for 1% of the time, Pallas kernels for 29%

profile of v8, /device:TPU:0, one launch (start us, length us, event | category | flops | bytes accessed | tf_op | source)
XLA Modules:
  0.0 84.3 jit_solution(1371790503788826060)
XLA Ops:
  0.0 0.5 collective-permute-start.3
  0.5 0.5 collective-permute-start.5
  1.0 2.5 %collective-permute-start = (bf16[256,128]{1,0:T(8,128)(2,1)}, bf16[256,128]{1,0:T(8,128)(2,1)S(1)}, u32[]{:S(2)}, u32[]{:S(2)}) collective-permute-start(bf16[256,128]{1,0:T(8,128)(2,1)} %refs_2_.1), channel_id=1, source_target_pairs={{0,2},{2,4},{4,6},{6,8},{8,10},{10,12},{12,14},{14,0},{1,3},{3,5},... | collective-permute-start | bytes 196616 | tf_op jit(solution)/shard_map/ppermute | solution.py:24
  3.5 1.5 %collective-permute-start.1 = (bf16[256,128]{1,0:T(8,128)(2,1)}, bf16[256,128]{1,0:T(8,128)(2,1)S(1)}, u32[]{:S(2)}, u32[]{:S(2)}) collective-permute-start(bf16[256,128]{1,0:T(8,128)(2,1)} %refs_3_.1), channel_id=1, source_target_pairs={{0,2},{2,4},{4,6},{6,8},{8,10},{10,12},{12,14},{14,0},{1,3},{3,5},... | collective-permute-start | bytes 196616 | tf_op jit(solution)/shard_map/ppermute | solution.py:24
  5.0 3.6 %attend.2 = (f32[1,16]{1,0:T(1,128)S(1)}, bf16[256,1024]{1,0:T(8,128)(2,1)S(1)}, bf16[256,128]{1,0:T(8,128)(2,1)S(1)}, bf16[256,128]{1,0:T(8,128)(2,1)S(1)}, bf1...) custom-call(f32[1,16]{1,0:T(1,128)} %bitcast.32, bf16[256,1024]{1,0:T(8,128)(2,1)} %refs_1_.1, ...), custom_call_target="tpu_custom_call" | custom-call | flops 671088640 | bytes 6291456 | tf_op jit(solution)/shard_map/attend/pallas_call | solution.py:151
  8.6 1.0 %collective-permute-done.refs_6_ = bf16[256,128]{1,0:T(8,128)(2,1)S(1)} collective-permute-done((bf16[256,128]{1,0:T(8,128)(2,1)}, bf16[256,128]{1,0:T(8,128)(2,1)S(1)}, u32[]{:S(2)}, u32[]{:S(2)}) %collective-permute-start) | collective-permute-done | bytes 65568 | tf_op jit(solution)/shard_map/ppermute | solution.py:24
  9.6 1.2 %collective-permute-done.1.refs_7_ = bf16[256,128]{1,0:T(8,128)(2,1)S(1)} collective-permute-done((bf16[256,128]{1,0:T(8,128)(2,1)}, bf16[256,128]{1,0:T(8,128)(2,1)S(1)}, u32[]{:S(2)}, u32[]{:S(2)}) %collective-permute-start.1) | collective-permute-done | bytes 65568 | tf_op jit(solution)/shard_map/ppermute | solution.py:24
  10.9 2.3 %attend.3 = (bf16[128,1536]{1,0:T(8,128)(2,1)S(1)}, f32[128,1536]{1,0:T(8,128)S(1)}) custom-call(f32[1,16]{1,0:T(1,128)S(1)} %get-tuple-element.70.refs_0_, bf16[256,1024]{1,0:T(8,128)(2,1)S(1)} %get-tuple-element.71.refs_1_, bf16[256,128]{1,0:T(8,128)(2,1)S(1)} %get-tuple-element.72.refs_2_, bf16[256,128]{1,0:T(8,128)(2,1)S(1)} %get-tuple-element.73.refs_3_, ...), custom_call_target="tpu_custom_call" | custom-call | flops 671088640 | bytes 6291456 | tf_op jit(solution)/shard_map/attend/pallas_call | solution.py:151
  13.3 1.7 %collective-permute-done.2.came_ref = bf16[128,1536]{1,0:T(8,128)(2,1)S(1)} collective-permute-done((bf16[128,1536]{1,0:T(8,128)(2,1)S(1)}, bf16[128,1536]{1,0:T(8,128)(2,1)S(1)}, u32[]{:S(2)}, u32[]{:S(2)}) %collective-permute-start.2) | collective-permute-done | bytes 393248 | tf_op jit(solution)/shard_map/ppermute | solution.py:37
  15.4 2.0 %collective-permute-start.7 = (bf16[784,128]{1,0:T(8,128)(2,1)S(1)}, bf16[784,128]{1,0:T(8,128)(2,1)S(1)}, u32[]{:S(2)}, u32[]{:S(2)}) collective-permute-start(bf16[784,128]{1,0:T(8,128)(2,1)S(1)} %get-tuple-element.88.refs_1_), channel_id=1, source_target_pairs={{4,0},{8,4},{12,8},{14,12},{10,14},{6,10},{2,6},{0,2},{5,1},{9,5},... | collective-permute-start | bytes 602120 | tf_op jit(solution)/shard_map/out_lead1/ppermute | solution.py:336
  17.5 2.0 %collective-permute-start.11 = (bf16[784,128]{1,0:T(8,128)(2,1)S(1)}, bf16[784,128]{1,0:T(8,128)(2,1)S(1)}, u32[]{:S(2)}, u32[]{:S(2)}) collective-permute-start(bf16[784,128]{1,0:T(8,128)(2,1)S(1)} %get-tuple-element.89.refs_0_), channel_id=1, source_target_pairs={{4,0},{8,4},{12,8},{14,12},{10,14},{6,10},{2,6},{0,2},{5,1},{9,5},... | collective-permute-start | bytes 602120 | tf_op jit(solution)/shard_map/out_trail1/ppermute | solution.py:336
  19.5 4.1 %experts.6 = (bf16[64,1536]{1,0:T(8,128)(2,1)S(1)}, bf16[64,1536]{1,0:T(8,128)(2,1)S(1)}, bf16[1536,768]{1,0:T(8,128)(2,1)S(1)}, bf16[1536,768]{1,0:T(8,128)(2,1)S(1)}, bf16[768,1536]{1,0:T(8,128)(2,1)S(1)}) custom-call(s32[1]{0:T(128)} %bitcast.5.me_ref, bf16[784,128]{1,0:T(8,128)(2,1)S(1)} %get-tuple-element.89.refs_0_, ...), custom_call_target="tpu_custom_call" | custom-call | flops 1811939328 | bytes 1179648 | tf_op jit(solution)/shard_map/experts/pallas_call | solution.py:288
  23.6 1.1 %collective-permute-start.8 = (bf16[784,128]{1,0:T(8,128)(2,1)S(1)}, bf16[784,128]{1,0:T(8,128)(2,1)S(1)}, u32[]{:S(2)}, u32[]{:S(2)}) collective-permute-start(bf16[784,128]{1,0:T(8,128)(2,1)S(1)} %collective-permute-done.6.refs_0_), channel_id=1, source_target_pairs={{0,4},{4,8},{8,12},{12,14},{14,10},{10,6},{6,2},{2,0},{1,5},{5,9},... | collective-permute-start | bytes 602120 | tf_op jit(solution)/shard_map/out_lead2/ppermute | solution.py:336
  24.7 0.9 %collective-permute-start.9 = (bf16[784,128]{1,0:T(8,128)(2,1)S(1)}, bf16[784,128]{1,0:T(8,128)(2,1)S(1)}, u32[]{:S(2)}, u32[]{:S(2)}) collective-permute-start(bf16[784,128]{1,0:T(8,128)(2,1)S(1)} %collective-permute-done.7.refs_1_), channel_id=1, source_target_pairs={{4,0},{8,4},{12,8},{14,12},{10,14},{6,10},{2,6},{0,2},{5,1},{9,5},... | collective-permute-start | bytes 602120 | tf_op jit(solution)/shard_map/out_lead2/ppermute | solution.py:336
  25.7 1.9 %collective-permute-done.10.refs_2_ = bf16[784,128]{1,0:T(8,128)(2,1)S(1)} collective-permute-done((bf16[784,128]{1,0:T(8,128)(2,1)S(1)}, bf16[784,128]{1,0:T(8,128)(2,1)S(1)}, u32[]{:S(2)}, u32[]{:S(2)}) %collective-permute-start.10) | collective-permute-done | bytes 200736 | tf_op jit(solution)/shard_map/out_trail1/ppermute | solution.py:336
  27.6 1.4 %collective-permute-start.14 = (bf16[784,128]{1,0:T(8,128)(2,1)S(1)}, bf16[784,128]{1,0:T(8,128)(2,1)S(1)}, u32[]{:S(2)}, u32[]{:S(2)}) collective-permute-start(bf16[784,128]{1,0:T(8,128)(2,1)S(1)} %collective-permute-done.10.refs_2_), channel_id=1, source_target_pairs={{0,4},{4,8},{8,12},{12,14},{14,10},{10,6},{6,2},{2,0},{1,5},{5,9},... | collective-permute-start | bytes 602120 | tf_op jit(solution)/shard_map/out_trail2/ppermute | solution.py:336
  29.0 0.6 collective-permute-start.15
  29.6 3.9 %experts.7 = (bf16[64,1536]{1,0:T(8,128)(2,1)S(1)}, bf16[64,1536]{1,0:T(8,128)(2,1)S(1)}, bf16[64,1536]{1,0:T(8,128)(2,1)S(1)}, bf16[64,1536]{1,0:T(8,128)(2,1)S(1)}) custom-call(s32[1]{0:T(128)} %bitcast.5.me_ref, bf16[784,128]{1,0:T(8,128)(2,1)S(1)} %collective-permute-done.6.refs_0_, bf16[784,128]{1,0:T(8,128)(2,1)S(1)} %collective-permute-done.7.refs_1_, ...), custom_call_target="tpu_custom_call" | custom-call | flops 3623878656 | bytes 2359296 | tf_op jit(solution)/shard_map/hop1/experts/pallas_call | solution.py:288
  33.6 1.5 %collective-permute-start.12 = (bf16[784,128]{1,0:T(8,128)(2,1)S(1)}, bf16[784,128]{1,0:T(8,128)(2,1)S(1)}, u32[]{:S(2)}, u32[]{:S(2)}) collective-permute-start(bf16[784,128]{1,0:T(8,128)(2,1)S(1)} %collective-permute-done.8.refs_0_), channel_id=1, source_target_pairs={{0,4},{4,8},{8,12},{12,14},{14,10},{10,6},{6,2},{2,0},{1,5},{5,9},... | collective-permute-start | bytes 602120 | tf_op jit(solution)/shard_map/out_lead3/ppermute | solution.py:336
  35.0 0.8 collective-permute-start.13
  36.1 3.9 %experts.8 = (bf16[64,1536]{1,0:T(8,128)(2,1)S(1)}, bf16[64,1536]{1,0:T(8,128)(2,1)S(1)}, bf16[64,1536]{1,0:T(8,128)(2,1)S(1)}, bf16[64,1536]{1,0:T(8,128)(2,1)S(1)}) custom-call(s32[1]{0:T(128)} %bitcast.5.me_ref, bf16[784,128]{1,0:T(8,128)(2,1)S(1)} %collective-permute-done.8.refs_0_, bf16[784,128]{1,0:T(8,128)(2,1)S(1)} %collective-permute-done.9.refs_1_, ...), custom_call_target="tpu_custom_call" | custom-call | flops 3623878656 | bytes 2359296 | tf_op jit(solution)/shard_map/hop2/experts/pallas_call | solution.py:288
  40.1 0.7 collective-permute-done.13.refs_1_
  40.8 1.6 %collective-permute-start.16 = (bf16[784,128]{1,0:T(8,128)(2,1)S(1)}, bf16[784,128]{1,0:T(8,128)(2,1)S(1)}, u32[]{:S(2)}, u32[]{:S(2)}) collective-permute-start(bf16[784,128]{1,0:T(8,128)(2,1)S(1)} %collective-permute-done.12.refs_0_), channel_id=1, source_target_pairs={{0,4},{4,8},{8,12},{12,14},{14,10},{10,6},{6,2},{2,0},{1,5},{5,9},... | collective-permute-start | bytes 602120 | tf_op jit(solution)/shard_map/out_lead4/ppermute | solution.py:336
  42.8 1.6 %collective-permute-start.20 = (bf16[784,128]{1,0:T(8,128)(2,1)S(1)}, bf16[784,128]{1,0:T(8,128)(2,1)S(1)}, u32[]{:S(2)}, u32[]{:S(2)}) collective-permute-start(bf16[784,128]{1,0:T(8,128)(2,1)S(1)} %collective-permute-done.14.refs_2_), channel_id=1, source_target_pairs={{0,4},{4,8},{8,12},{12,14},{14,10},{10,6},{6,2},{2,0},{1,5},{5,9},... | collective-permute-start | bytes 602120 | tf_op jit(solution)/shard_map/out_trail3/ppermute | solution.py:336
  44.8 2.1 %experts.9 = (bf16[64,1536]{1,0:T(8,128)(2,1)S(1)}, bf16[64,1536]{1,0:T(8,128)(2,1)S(1)}) custom-call(s32[1]{0:T(128)} %bitcast.5.me_ref, bf16[784,128]{1,0:T(8,128)(2,1)S(1)} %collective-permute-done.12.refs_0_, bf16[784,128]{1,0:T(8,128)(2,1)S(1)} %collective-permute-done.13.refs_1_, bf16[1536,768]{1,0:T(8,128)(2,1)S(1)} %bitcast.13, ...), custom_call_target="tpu_custom_call" | custom-call | flops 1811939328 | bytes 1179648 | tf_op jit(solution)/shard_map/hop3/experts/pallas_call | solution.py:288
  46.9 0.8 collective-permute-done.16.refs_0_
  48.1 2.1 %experts.10 = (bf16[64,1536]{1,0:T(8,128)(2,1)S(1)}, bf16[64,1536]{1,0:T(8,128)(2,1)S(1)}) custom-call(s32[1]{0:T(128)} %bitcast.5.me_ref, bf16[784,128]{1,0:T(8,128)(2,1)S(1)} %collective-permute-done.16.refs_0_, bf16[784,128]{1,0:T(8,128)(2,1)S(1)} %collective-permute-done.17.refs_1_, bf16[1536,768]{1,0:T(8,128)(2,1)S(1)} %bitcast.14, ...), custom_call_target="tpu_custom_call" | custom-call | flops 1811939328 | bytes 1179648 | tf_op jit(solution)/shard_map/hop4/experts/pallas_call | solution.py:288
  50.2 1.6 %collective-permute-start.18 = (bf16[64,1536]{1,0:T(8,128)(2,1)S(1)}, bf16[64,1536]{1,0:T(8,128)(2,1)S(1)}, u32[]{:S(2)}, u32[]{:S(2)}) collective-permute-start(bf16[64,1536]{1,0:T(8,128)(2,1)S(1)} %get-tuple-element.104), channel_id=1, source_target_pairs={{0,4},{4,8},{8,12},{12,14},{14,10},{10,6},{6,2},{2,0},{1,5},{5,9},... | collective-permute-start | bytes 589832 | tf_op jit(solution)/shard_map/back_lead4/ppermute | solution.py:378
  51.7 0.5 collective-permute-start.19
  52.2 1.4 %collective-permute-start.28 = (bf16[64,1536]{1,0:T(8,128)(2,1)S(1)}, bf16[64,1536]{1,0:T(8,128)(2,1)S(1)}, u32[]{:S(2)}, u32[]{:S(2)}) collective-permute-start(bf16[64,1536]{1,0:T(8,128)(2,1)S(1)} %get-tuple-element.121), channel_id=1, source_target_pairs={{4,0},{8,4},{12,8},{14,12},{10,14},{6,10},{2,6},{0,2},{5,1},{9,5},... | collective-permute-start | bytes 589832 | tf_op jit(solution)/shard_map/back_trail3/ppermute | solution.py:378
  53.6 0.6 collective-permute-start.27
  54.3 2.1 %experts.11 = (bf16[64,1536]{1,0:T(8,128)(2,1)S(1)}, bf16[64,1536]{1,0:T(8,128)(2,1)S(1)}) custom-call(s32[1]{0:T(128)} %bitcast.5.me_ref, bf16[784,128]{1,0:T(8,128)(2,1)S(1)} %collective-permute-done.20.refs_0_, bf16[784,128]{1,0:T(8,128)(2,1)S(1)} %collective-permute-done.21.refs_1_, bf16[1536,768]{1,0:T(8,128)(2,1)S(1)} %bitcast.15, ...), custom_call_target="tpu_custom_call" | custom-call | flops 1811939328 | bytes 1179648 | tf_op jit(solution)/shard_map/hop3/experts/pallas_call | solution.py:288
  56.4 3.0 %collective-permute-done.19 = bf16[64,1536]{1,0:T(8,128)(2,1)S(1)} collective-permute-done((bf16[64,1536]{1,0:T(8,128)(2,1)S(1)}, bf16[64,1536]{1,0:T(8,128)(2,1)S(1)}, u32[]{:S(2)}, u32[]{:S(2)}) %collective-permute-start.19) | collective-permute-done | bytes 196640 | tf_op jit(solution)/shard_map/back_lead4/ppermute | solution.py:378
  59.8 1.8 %collective-permute-start.22 = (bf16[64,1536]{1,0:T(8,128)(2,1)S(1)}, bf16[64,1536]{1,0:T(8,128)(2,1)S(1)}, u32[]{:S(2)}, u32[]{:S(2)}) collective-permute-start(bf16[64,1536]{1,0:T(8,128)(2,1)S(1)} %add_convert_fusion.9), channel_id=1, source_target_pairs={{0,4},{4,8},{8,12},{12,14},{14,10},{10,6},{6,2},{2,0},{1,5},{5,9},... | collective-permute-start | bytes 589832 | tf_op jit(solution)/shard_map/back_lead3/ppermute | solution.py:378
  61.7 2.0 %collective-permute-done.28 = bf16[64,1536]{1,0:T(8,128)(2,1)S(1)} collective-permute-done((bf16[64,1536]{1,0:T(8,128)(2,1)S(1)}, bf16[64,1536]{1,0:T(8,128)(2,1)S(1)}, u32[]{:S(2)}, u32[]{:S(2)}) %collective-permute-start.28) | collective-permute-done | bytes 196640 | tf_op jit(solution)/shard_map/back_trail3/ppermute | solution.py:378
  64.1 1.8 %collective-permute-start.29 = (bf16[64,1536]{1,0:T(8,128)(2,1)S(1)}, bf16[64,1536]{1,0:T(8,128)(2,1)S(1)}, u32[]{:S(2)}, u32[]{:S(2)}) collective-permute-start(bf16[64,1536]{1,0:T(8,128)(2,1)S(1)} %add_convert_fusion.4), channel_id=1, source_target_pairs={{0,4},{4,8},{8,12},{12,14},{14,10},{10,6},{6,2},{2,0},{1,5},{5,9},... | collective-permute-start | bytes 589832 | tf_op jit(solution)/shard_map/back_trail2/ppermute | solution.py:378
  65.9 2.0 %collective-permute-done.23 = bf16[64,1536]{1,0:T(8,128)(2,1)S(1)} collective-permute-done((bf16[64,1536]{1,0:T(8,128)(2,1)S(1)}, bf16[64,1536]{1,0:T(8,128)(2,1)S(1)}, u32[]{:S(2)}, u32[]{:S(2)}) %collective-permute-start.23) | collective-permute-done | bytes 196640 | tf_op jit(solution)/shard_map/back_lead3/ppermute | solution.py:378
  67.9 1.2 %collective-permute-start.25 = (bf16[64,1536]{1,0:T(8,128)(2,1)S(1)}, bf16[64,1536]{1,0:T(8,128)(2,1)S(1)}, u32[]{:S(2)}, u32[]{:S(2)}) collective-permute-start(bf16[64,1536]{1,0:T(8,128)(2,1)S(1)} %add_convert_fusion.6), channel_id=1, source_target_pairs={{4,0},{8,4},{12,8},{14,12},{10,14},{6,10},{2,6},{0,2},{5,1},{9,5},... | collective-permute-start | bytes 589832 | tf_op jit(solution)/shard_map/back_lead2/ppermute | solution.py:378
  69.2 0.9 %collective-permute-start.24 = (bf16[64,1536]{1,0:T(8,128)(2,1)S(1)}, bf16[64,1536]{1,0:T(8,128)(2,1)S(1)}, u32[]{:S(2)}, u32[]{:S(2)}) collective-permute-start(bf16[64,1536]{1,0:T(8,128)(2,1)S(1)} %add_convert_fusion.7), channel_id=1, source_target_pairs={{0,4},{4,8},{8,12},{12,14},{14,10},{10,6},{6,2},{2,0},{1,5},{5,9},... | collective-permute-start | bytes 589832 | tf_op jit(solution)/shard_map/back_lead2/ppermute | solution.py:378
  70.1 1.6 %collective-permute-done.30 = bf16[64,1536]{1,0:T(8,128)(2,1)S(1)} collective-permute-done((bf16[64,1536]{1,0:T(8,128)(2,1)S(1)}, bf16[64,1536]{1,0:T(8,128)(2,1)S(1)}, u32[]{:S(2)}, u32[]{:S(2)}) %collective-permute-start.30) | collective-permute-done | bytes 196640 | tf_op jit(solution)/shard_map/back_trail2/ppermute | solution.py:378
  72.0 1.4 %collective-permute-start.31 = (bf16[64,1536]{1,0:T(8,128)(2,1)S(1)}, bf16[64,1536]{1,0:T(8,128)(2,1)S(1)}, u32[]{:S(2)}, u32[]{:S(2)}) collective-permute-start(bf16[64,1536]{1,0:T(8,128)(2,1)S(1)} %add_convert_fusion.2), channel_id=1, source_target_pairs={{4,0},{8,4},{12,8},{14,12},{10,14},{6,10},{2,6},{0,2},{5,1},{9,5},... | collective-permute-start | bytes 589832 | tf_op jit(solution)/shard_map/back_trail1/ppermute | solution.py:378
  73.5 0.7 collective-permute-start.32
  74.2 1.7 %collective-permute-done.25 = bf16[64,1536]{1,0:T(8,128)(2,1)S(1)} collective-permute-done((bf16[64,1536]{1,0:T(8,128)(2,1)S(1)}, bf16[64,1536]{1,0:T(8,128)(2,1)S(1)}, u32[]{:S(2)}, u32[]{:S(2)}) %collective-permute-start.25) | collective-permute-done | bytes 196640 | tf_op jit(solution)/shard_map/back_lead2/ppermute | solution.py:378
  76.1 1.5 %collective-permute-start.26 = (bf16[64,1536]{1,0:T(8,128)(2,1)S(1)}, bf16[64,1536]{1,0:T(8,128)(2,1)S(1)}, u32[]{:S(2)}, u32[]{:S(2)}) collective-permute-start(bf16[64,1536]{1,0:T(8,128)(2,1)S(1)} %add_convert_fusion.5), channel_id=1, source_target_pairs={{0,4},{4,8},{8,12},{12,14},{14,10},{10,6},{6,2},{2,0},{1,5},{5,9},... | collective-permute-start | bytes 589832 | tf_op jit(solution)/shard_map/back_lead1/ppermute | solution.py:378
  77.7 0.6 collective-permute-start.33
  78.3 3.5 %collective-permute-done.26 = bf16[64,1536]{1,0:T(8,128)(2,1)S(1)} collective-permute-done((bf16[64,1536]{1,0:T(8,128)(2,1)S(1)}, bf16[64,1536]{1,0:T(8,128)(2,1)S(1)}, u32[]{:S(2)}, u32[]{:S(2)}) %collective-permute-start.26) | collective-permute-done | bytes 196640 | tf_op jit(solution)/shard_map/back_lead1/ppermute | solution.py:378
  81.9 1.5 %collective-permute-done.33 = bf16[64,1536]{1,0:T(8,128)(2,1)S(1)} collective-permute-done((bf16[64,1536]{1,0:T(8,128)(2,1)S(1)}, bf16[64,1536]{1,0:T(8,128)(2,1)S(1)}, u32[]{:S(2)}, u32[]{:S(2)}) %collective-permute-start.33) | collective-permute-done | bytes 196640 | tf_op jit(solution)/shard_map/back_lead1/ppermute | solution.py:378
  83.5 0.8 fusion
  (59 shorter events, 3.8 us)
Async XLA Ops:
  0.0 15.3 %collective-permute-start.3 = (bf16[1536,768]{1,0:T(8,128)(2,1)}, bf16[1536,768]{1,0:T(8,128)(2,1)S(1)}, u32[]{:S(2)}, u32[]{:S(2)}) collective-permute-start(bf16[1536,768]{1,0:T(8,128)(2,1)} %bitcast.9), channel_id=1, source_target_pairs={{0,1},{1,0},{2,3},{3,2},{4,5},{5,4},{6,7},{7,6},{8,9},{9,8},{10,11... | collective-permute-start | bytes 7077896 | tf_op jit(solution)/shard_map/ppermute | solution.py:37
  0.5 14.9 %collective-permute-start.4 = (bf16[1536,768]{1,0:T(8,128)(2,1)}, bf16[1536,768]{1,0:T(8,128)(2,1)}, u32[]{:S(2)}, u32[]{:S(2)}) collective-permute-start(bf16[1536,768]{1,0:T(8,128)(2,1)} %bitcast.16), channel_id=1, source_target_pairs={{0,1},{1,0},{2,3},{3,2},{4,5},{5,4},{6,7},{7,6},{8,9},{9,8},{10,11... | collective-permute-start | bytes 7077896 | tf_op jit(solution)/shard_map/ppermute | solution.py:37
  0.5 14.8 %collective-permute-start.5 = (bf16[768,1536]{1,0:T(8,128)(2,1)}, bf16[768,1536]{1,0:T(8,128)(2,1)}, u32[]{:S(2)}, u32[]{:S(2)}) collective-permute-start(bf16[768,1536]{1,0:T(8,128)(2,1)} %bitcast.23), channel_id=1, source_target_pairs={{0,1},{1,0},{2,3},{3,2},{4,5},{5,4},{6,7},{7,6},{8,9},{9,8},{10,11... | collective-permute-start | bytes 7077896 | tf_op jit(solution)/shard_map/ppermute | solution.py:37
  1.0 8.7 %collective-permute-start = (bf16[256,128]{1,0:T(8,128)(2,1)}, bf16[256,128]{1,0:T(8,128)(2,1)S(1)}, u32[]{:S(2)}, u32[]{:S(2)}) collective-permute-start(bf16[256,128]{1,0:T(8,128)(2,1)} %refs_2_.1), channel_id=1, source_target_pairs={{0,2},{2,4},{4,6},{6,8},{8,10},{10,12},{12,14},{14,0},{1,3},{3,5},... | collective-permute-start | bytes 196616 | tf_op jit(solution)/shard_map/ppermute | solution.py:24
  3.5 7.4 %collective-permute-start.1 = (bf16[256,128]{1,0:T(8,128)(2,1)}, bf16[256,128]{1,0:T(8,128)(2,1)S(1)}, u32[]{:S(2)}, u32[]{:S(2)}) collective-permute-start(bf16[256,128]{1,0:T(8,128)(2,1)} %refs_3_.1), channel_id=1, source_target_pairs={{0,2},{2,4},{4,6},{6,8},{8,10},{10,12},{12,14},{14,0},{1,3},{3,5},... | collective-permute-start | bytes 196616 | tf_op jit(solution)/shard_map/ppermute | solution.py:24
  5.0 8.3 %copy-start.7 = (f32[1536]{0:T(1024)S(1)}, f32[1536]{0:T(1024)}, u32[]{:S(2)}) copy-start(f32[1536]{0:T(1024)} %param.18) | copy-start | bytes 18436
  5.0 10.0 %copy-start.3 = (bf16[128,1536]{1,0:T(8,128)(2,1)S(1)}, bf16[128,1536]{1,0:T(8,128)(2,1)}, u32[]{:S(2)}) copy-start(bf16[128,1536]{1,0:T(8,128)(2,1)} %stream_ref.1) | copy-start | bytes 1179652
  5.0 14.5 %copy-start.2 = (bf16[1,768,1536]{2,1,0:T(8,128)(2,1)S(1)}, bf16[1,768,1536]{2,1,0:T(8,128)(2,1)}, u32[]{:S(2)}) copy-start(bf16[1,768,1536]{2,1,0:T(8,128)(2,1)} %param.23) | copy-start | bytes 7077892
  10.9 4.1 %copy-start.4 = (s32[128,4]{0,1:T(4,128)S(1)}, s32[128,4]{0,1:T(4,128)}, u32[]{:S(2)}) copy-start(s32[128,4]{0,1:T(4,128)} %param.19) | copy-start | bytes 6148
  10.9 4.1 %copy-start.5 = (f32[128,4]{0,1:T(4,128)S(1)}, f32[128,4]{0,1:T(4,128)}, u32[]{:S(2)}) copy-start(f32[128,4]{0,1:T(4,128)} %param.20) | copy-start | bytes 6148
  10.9 8.6 %copy-start = (bf16[1,1536,768]{2,1,0:T(8,128)(2,1)S(1)}, bf16[1,1536,768]{2,1,0:T(8,128)(2,1)}, u32[]{:S(2)}) copy-start(bf16[1,1536,768]{2,1,0:T(8,128)(2,1)} %param.21) | copy-start | bytes 7077892
  10.9 8.6 %copy-start.1 = (bf16[1,1536,768]{2,1,0:T(8,128)(2,1)S(1)}, bf16[1,1536,768]{2,1,0:T(8,128)(2,1)}, u32[]{:S(2)}) copy-start(bf16[1,1536,768]{2,1,0:T(8,128)(2,1)} %param.22) | copy-start | bytes 7077892
  13.2 1.8 %collective-permute-start.2 = (bf16[128,1536]{1,0:T(8,128)(2,1)S(1)}, bf16[128,1536]{1,0:T(8,128)(2,1)S(1)}, u32[]{:S(2)}, u32[]{:S(2)}) collective-permute-start(bf16[128,1536]{1,0:T(8,128)(2,1)S(1)} %get-tuple-element.77), channel_id=1, source_target_pairs={{0,1},{1,0},{2,3},{3,2},{4,5},{5,4},{6,7},{7,6},{8,9},{9,8},{10,11... | collective-permute-start | bytes 1179656 | tf_op jit(solution)/shard_map/ppermute | solution.py:37
  15.3 4.1 %copy-start.6 = (bf16[1536,768]{1,0:T(8,128)(2,1)}, bf16[1536,768]{1,0:T(8,128)(2,1)S(1)}, u32[]{:S(2)}) copy-start(bf16[1536,768]{1,0:T(8,128)(2,1)S(1)} %collective-permute-done.3.refs_5_) | copy-start | bytes 7077892
  15.4 8.2 %collective-permute-start.6 = (bf16[784,128]{1,0:T(8,128)(2,1)S(1)}, bf16[784,128]{1,0:T(8,128)(2,1)S(1)}, u32[]{:S(2)}, u32[]{:S(2)}) collective-permute-start(bf16[784,128]{1,0:T(8,128)(2,1)S(1)} %get-tuple-element.89.refs_0_), channel_id=1, source_target_pairs={{0,4},{4,8},{8,12},{12,14},{14,10},{10,6},{6,2},{2,0},{1,5},{5,9},... | collective-permute-start | bytes 602120 | tf_op jit(solution)/shard_map/out_lead1/ppermute | solution.py:336
  15.4 8.2 %collective-permute-start.7 = (bf16[784,128]{1,0:T(8,128)(2,1)S(1)}, bf16[784,128]{1,0:T(8,128)(2,1)S(1)}, u32[]{:S(2)}, u32[]{:S(2)}) collective-permute-start(bf16[784,128]{1,0:T(8,128)(2,1)S(1)} %get-tuple-element.88.refs_1_), channel_id=1, source_target_pairs={{4,0},{8,4},{12,8},{14,12},{10,14},{6,10},{2,6},{0,2},{5,1},{9,5},... | collective-permute-start | bytes 602120 | tf_op jit(solution)/shard_map/out_lead1/ppermute | solution.py:336
  17.4 10.1 %collective-permute-start.10 = (bf16[784,128]{1,0:T(8,128)(2,1)S(1)}, bf16[784,128]{1,0:T(8,128)(2,1)S(1)}, u32[]{:S(2)}, u32[]{:S(2)}) collective-permute-start(bf16[784,128]{1,0:T(8,128)(2,1)S(1)} %get-tuple-element.88.refs_1_), channel_id=1, source_target_pairs={{0,4},{4,8},{8,12},{12,14},{14,10},{10,6},{6,2},{2,0},{1,5},{5,9},... | collective-permute-start | bytes 602120 | tf_op jit(solution)/shard_map/out_trail1/ppermute | solution.py:336
  17.5 10.1 %collective-permute-start.11 = (bf16[784,128]{1,0:T(8,128)(2,1)S(1)}, bf16[784,128]{1,0:T(8,128)(2,1)S(1)}, u32[]{:S(2)}, u32[]{:S(2)}) collective-permute-start(bf16[784,128]{1,0:T(8,128)(2,1)S(1)} %get-tuple-element.89.refs_0_), channel_id=1, source_target_pairs={{4,0},{8,4},{12,8},{14,12},{10,14},{6,10},{2,6},{0,2},{5,1},{9,5},... | collective-permute-start | bytes 602120 | tf_op jit(solution)/shard_map/out_trail1/ppermute | solution.py:336
  23.6 10.0 %collective-permute-start.8 = (bf16[784,128]{1,0:T(8,128)(2,1)S(1)}, bf16[784,128]{1,0:T(8,128)(2,1)S(1)}, u32[]{:S(2)}, u32[]{:S(2)}) collective-permute-start(bf16[784,128]{1,0:T(8,128)(2,1)S(1)} %collective-permute-done.6.refs_0_), channel_id=1, source_target_pairs={{0,4},{4,8},{8,12},{12,14},{14,10},{10,6},{6,2},{2,0},{1,5},{5,9},... | collective-permute-start | bytes 602120 | tf_op jit(solution)/shard_map/out_lead2/ppermute | solution.py:336
  24.7 8.8 %collective-permute-start.9 = (bf16[784,128]{1,0:T(8,128)(2,1)S(1)}, bf16[784,128]{1,0:T(8,128)(2,1)S(1)}, u32[]{:S(2)}, u32[]{:S(2)}) collective-permute-start(bf16[784,128]{1,0:T(8,128)(2,1)S(1)} %collective-permute-done.7.refs_1_), channel_id=1, source_target_pairs={{4,0},{8,4},{12,8},{14,12},{10,14},{6,10},{2,6},{0,2},{5,1},{9,5},... | collective-permute-start | bytes 602120 | tf_op jit(solution)/shard_map/out_lead2/ppermute | solution.py:336
  27.6 8.5 %collective-permute-start.14 = (bf16[784,128]{1,0:T(8,128)(2,1)S(1)}, bf16[784,128]{1,0:T(8,128)(2,1)S(1)}, u32[]{:S(2)}, u32[]{:S(2)}) collective-permute-start(bf16[784,128]{1,0:T(8,128)(2,1)S(1)} %collective-permute-done.10.refs_2_), channel_id=1, source_target_pairs={{0,4},{4,8},{8,12},{12,14},{14,10},{10,6},{6,2},{2,0},{1,5},{5,9},... | collective-permute-start | bytes 602120 | tf_op jit(solution)/shard_map/out_trail2/ppermute | solution.py:336
  29.0 7.1 %collective-permute-start.15 = (bf16[784,128]{1,0:T(8,128)(2,1)S(1)}, bf16[784,128]{1,0:T(8,128)(2,1)S(1)}, u32[]{:S(2)}, u32[]{:S(2)}) collective-permute-start(bf16[784,128]{1,0:T(8,128)(2,1)S(1)} %collective-permute-done.11.refs_3_), channel_id=1, source_target_pairs={{4,0},{8,4},{12,8},{14,12},{10,14},{6,10},{2,6},{0,2},{5,1},{9,5},... | collective-permute-start | bytes 602120 | tf_op jit(solution)/shard_map/out_trail2/ppermute | solution.py:336
  33.6 6.5 %collective-permute-start.12 = (bf16[784,128]{1,0:T(8,128)(2,1)S(1)}, bf16[784,128]{1,0:T(8,128)(2,1)S(1)}, u32[]{:S(2)}, u32[]{:S(2)}) collective-permute-start(bf16[784,128]{1,0:T(8,128)(2,1)S(1)} %collective-permute-done.8.refs_0_), channel_id=1, source_target_pairs={{0,4},{4,8},{8,12},{12,14},{14,10},{10,6},{6,2},{2,0},{1,5},{5,9},... | collective-permute-start | bytes 602120 | tf_op jit(solution)/shard_map/out_lead3/ppermute | solution.py:336
  35.0 5.7 %collective-permute-start.13 = (bf16[784,128]{1,0:T(8,128)(2,1)S(1)}, bf16[784,128]{1,0:T(8,128)(2,1)S(1)}, u32[]{:S(2)}, u32[]{:S(2)}) collective-permute-start(bf16[784,128]{1,0:T(8,128)(2,1)S(1)} %collective-permute-done.9.refs_1_), channel_id=1, source_target_pairs={{4,0},{8,4},{12,8},{14,12},{10,14},{6,10},{2,6},{0,2},{5,1},{9,5},... | collective-permute-start | bytes 602120 | tf_op jit(solution)/shard_map/out_lead3/ppermute | solution.py:336
  40.8 6.9 %collective-permute-start.16 = (bf16[784,128]{1,0:T(8,128)(2,1)S(1)}, bf16[784,128]{1,0:T(8,128)(2,1)S(1)}, u32[]{:S(2)}, u32[]{:S(2)}) collective-permute-start(bf16[784,128]{1,0:T(8,128)(2,1)S(1)} %collective-permute-done.12.refs_0_), channel_id=1, source_target_pairs={{0,4},{4,8},{8,12},{12,14},{14,10},{10,6},{6,2},{2,0},{1,5},{5,9},... | collective-permute-start | bytes 602120 | tf_op jit(solution)/shard_map/out_lead4/ppermute | solution.py:336
  42.3 5.7 %collective-permute-start.17 = (bf16[784,128]{1,0:T(8,128)(2,1)S(1)}, bf16[784,128]{1,0:T(8,128)(2,1)S(1)}, u32[]{:S(2)}, u32[]{:S(2)}) collective-permute-start(bf16[784,128]{1,0:T(8,128)(2,1)S(1)} %collective-permute-done.13.refs_1_), channel_id=1, source_target_pairs={{4,0},{8,4},{12,8},{14,12},{10,14},{6,10},{2,6},{0,2},{5,1},{9,5},... | collective-permute-start | bytes 602120 | tf_op jit(solution)/shard_map/out_lead4/ppermute | solution.py:336
  42.8 9.5 %collective-permute-start.20 = (bf16[784,128]{1,0:T(8,128)(2,1)S(1)}, bf16[784,128]{1,0:T(8,128)(2,1)S(1)}, u32[]{:S(2)}, u32[]{:S(2)}) collective-permute-start(bf16[784,128]{1,0:T(8,128)(2,1)S(1)} %collective-permute-done.14.refs_2_), channel_id=1, source_target_pairs={{0,4},{4,8},{8,12},{12,14},{14,10},{10,6},{6,2},{2,0},{1,5},{5,9},... | collective-permute-start | bytes 602120 | tf_op jit(solution)/shard_map/out_trail3/ppermute | solution.py:336
  44.4 9.9 %collective-permute-start.21 = (bf16[784,128]{1,0:T(8,128)(2,1)S(1)}, bf16[784,128]{1,0:T(8,128)(2,1)S(1)}, u32[]{:S(2)}, u32[]{:S(2)}) collective-permute-start(bf16[784,128]{1,0:T(8,128)(2,1)S(1)} %collective-permute-done.15.refs_3_), channel_id=1, source_target_pairs={{4,0},{8,4},{12,8},{14,12},{10,14},{6,10},{2,6},{0,2},{5,1},{9,5},... | collective-permute-start | bytes 602120 | tf_op jit(solution)/shard_map/out_trail3/ppermute | solution.py:336
  50.2 6.2 %collective-permute-start.18 = (bf16[64,1536]{1,0:T(8,128)(2,1)S(1)}, bf16[64,1536]{1,0:T(8,128)(2,1)S(1)}, u32[]{:S(2)}, u32[]{:S(2)}) collective-permute-start(bf16[64,1536]{1,0:T(8,128)(2,1)S(1)} %get-tuple-element.104), channel_id=1, source_target_pairs={{0,4},{4,8},{8,12},{12,14},{14,10},{10,6},{6,2},{2,0},{1,5},{5,9},... | collective-permute-start | bytes 589832 | tf_op jit(solution)/shard_map/back_lead4/ppermute | solution.py:378
  51.7 7.7 %collective-permute-start.19 = (bf16[64,1536]{1,0:T(8,128)(2,1)S(1)}, bf16[64,1536]{1,0:T(8,128)(2,1)S(1)}, u32[]{:S(2)}, u32[]{:S(2)}) collective-permute-start(bf16[64,1536]{1,0:T(8,128)(2,1)S(1)} %get-tuple-element.105), channel_id=1, source_target_pairs={{4,0},{8,4},{12,8},{14,12},{10,14},{6,10},{2,6},{0,2},{5,1},{9,5},... | collective-permute-start | bytes 589832 | tf_op jit(solution)/shard_map/back_lead4/ppermute | solution.py:378
  52.2 11.4 %collective-permute-start.28 = (bf16[64,1536]{1,0:T(8,128)(2,1)S(1)}, bf16[64,1536]{1,0:T(8,128)(2,1)S(1)}, u32[]{:S(2)}, u32[]{:S(2)}) collective-permute-start(bf16[64,1536]{1,0:T(8,128)(2,1)S(1)} %get-tuple-element.121), channel_id=1, source_target_pairs={{4,0},{8,4},{12,8},{14,12},{10,14},{6,10},{2,6},{0,2},{5,1},{9,5},... | collective-permute-start | bytes 589832 | tf_op jit(solution)/shard_map/back_trail3/ppermute | solution.py:378
  53.6 10.0 %collective-permute-start.27 = (bf16[64,1536]{1,0:T(8,128)(2,1)S(1)}, bf16[64,1536]{1,0:T(8,128)(2,1)S(1)}, u32[]{:S(2)}, u32[]{:S(2)}) collective-permute-start(bf16[64,1536]{1,0:T(8,128)(2,1)S(1)} %get-tuple-element.120), channel_id=1, source_target_pairs={{0,4},{4,8},{8,12},{12,14},{14,10},{10,6},{6,2},{2,0},{1,5},{5,9},... | collective-permute-start | bytes 589832 | tf_op jit(solution)/shard_map/back_trail3/ppermute | solution.py:378
  59.5 8.4 %collective-permute-start.23 = (bf16[64,1536]{1,0:T(8,128)(2,1)S(1)}, bf16[64,1536]{1,0:T(8,128)(2,1)S(1)}, u32[]{:S(2)}, u32[]{:S(2)}) collective-permute-start(bf16[64,1536]{1,0:T(8,128)(2,1)S(1)} %add_convert_fusion.8), channel_id=1, source_target_pairs={{4,0},{8,4},{12,8},{14,12},{10,14},{6,10},{2,6},{0,2},{5,1},{9,5},... | collective-permute-start | bytes 589832 | tf_op jit(solution)/shard_map/back_lead3/ppermute | solution.py:378
  59.8 8.0 %collective-permute-start.22 = (bf16[64,1536]{1,0:T(8,128)(2,1)S(1)}, bf16[64,1536]{1,0:T(8,128)(2,1)S(1)}, u32[]{:S(2)}, u32[]{:S(2)}) collective-permute-start(bf16[64,1536]{1,0:T(8,128)(2,1)S(1)} %add_convert_fusion.9), channel_id=1, source_target_pairs={{0,4},{4,8},{8,12},{12,14},{14,10},{10,6},{6,2},{2,0},{1,5},{5,9},... | collective-permute-start | bytes 589832 | tf_op jit(solution)/shard_map/back_lead3/ppermute | solution.py:378
  63.7 8.0 %collective-permute-start.30 = (bf16[64,1536]{1,0:T(8,128)(2,1)S(1)}, bf16[64,1536]{1,0:T(8,128)(2,1)S(1)}, u32[]{:S(2)}, u32[]{:S(2)}) collective-permute-start(bf16[64,1536]{1,0:T(8,128)(2,1)S(1)} %add_convert_fusion.3), channel_id=1, source_target_pairs={{4,0},{8,4},{12,8},{14,12},{10,14},{6,10},{2,6},{0,2},{5,1},{9,5},... | collective-permute-start | bytes 589832 | tf_op jit(solution)/shard_map/back_trail2/ppermute | solution.py:378
  64.1 7.9 %collective-permute-start.29 = (bf16[64,1536]{1,0:T(8,128)(2,1)S(1)}, bf16[64,1536]{1,0:T(8,128)(2,1)S(1)}, u32[]{:S(2)}, u32[]{:S(2)}) collective-permute-start(bf16[64,1536]{1,0:T(8,128)(2,1)S(1)} %add_convert_fusion.4), channel_id=1, source_target_pairs={{0,4},{4,8},{8,12},{12,14},{14,10},{10,6},{6,2},{2,0},{1,5},{5,9},... | collective-permute-start | bytes 589832 | tf_op jit(solution)/shard_map/back_trail2/ppermute | solution.py:378
  67.9 8.0 %collective-permute-start.25 = (bf16[64,1536]{1,0:T(8,128)(2,1)S(1)}, bf16[64,1536]{1,0:T(8,128)(2,1)S(1)}, u32[]{:S(2)}, u32[]{:S(2)}) collective-permute-start(bf16[64,1536]{1,0:T(8,128)(2,1)S(1)} %add_convert_fusion.6), channel_id=1, source_target_pairs={{4,0},{8,4},{12,8},{14,12},{10,14},{6,10},{2,6},{0,2},{5,1},{9,5},... | collective-permute-start | bytes 589832 | tf_op jit(solution)/shard_map/back_lead2/ppermute | solution.py:378
  69.2 6.9 %collective-permute-start.24 = (bf16[64,1536]{1,0:T(8,128)(2,1)S(1)}, bf16[64,1536]{1,0:T(8,128)(2,1)S(1)}, u32[]{:S(2)}, u32[]{:S(2)}) collective-permute-start(bf16[64,1536]{1,0:T(8,128)(2,1)S(1)} %add_convert_fusion.7), channel_id=1, source_target_pairs={{0,4},{4,8},{8,12},{12,14},{14,10},{10,6},{6,2},{2,0},{1,5},{5,9},... | collective-permute-start | bytes 589832 | tf_op jit(solution)/shard_map/back_lead2/ppermute | solution.py:378
  72.0 6.3 %collective-permute-start.31 = (bf16[64,1536]{1,0:T(8,128)(2,1)S(1)}, bf16[64,1536]{1,0:T(8,128)(2,1)S(1)}, u32[]{:S(2)}, u32[]{:S(2)}) collective-permute-start(bf16[64,1536]{1,0:T(8,128)(2,1)S(1)} %add_convert_fusion.2), channel_id=1, source_target_pairs={{4,0},{8,4},{12,8},{14,12},{10,14},{6,10},{2,6},{0,2},{5,1},{9,5},... | collective-permute-start | bytes 589832 | tf_op jit(solution)/shard_map/back_trail1/ppermute | solution.py:378
  73.5 8.4 %collective-permute-start.32 = (bf16[64,1536]{1,0:T(8,128)(2,1)S(1)}, bf16[64,1536]{1,0:T(8,128)(2,1)S(1)}, u32[]{:S(2)}, u32[]{:S(2)}) collective-permute-start(bf16[64,1536]{1,0:T(8,128)(2,1)S(1)} %add_convert_fusion.1), channel_id=1, source_target_pairs={{0,4},{4,8},{8,12},{12,14},{14,10},{10,6},{6,2},{2,0},{1,5},{5,9},... | collective-permute-start | bytes 589832 | tf_op jit(solution)/shard_map/back_trail1/ppermute | solution.py:378
  76.1 5.7 %collective-permute-start.26 = (bf16[64,1536]{1,0:T(8,128)(2,1)S(1)}, bf16[64,1536]{1,0:T(8,128)(2,1)S(1)}, u32[]{:S(2)}, u32[]{:S(2)}) collective-permute-start(bf16[64,1536]{1,0:T(8,128)(2,1)S(1)} %add_convert_fusion.5), channel_id=1, source_target_pairs={{0,4},{4,8},{8,12},{12,14},{14,10},{10,6},{6,2},{2,0},{1,5},{5,9},... | collective-permute-start | bytes 589832 | tf_op jit(solution)/shard_map/back_lead1/ppermute | solution.py:378
  77.7 5.7 %collective-permute-start.33 = (bf16[64,1536]{1,0:T(8,128)(2,1)S(1)}, bf16[64,1536]{1,0:T(8,128)(2,1)S(1)}, u32[]{:S(2)}, u32[]{:S(2)}) collective-permute-start(bf16[64,1536]{1,0:T(8,128)(2,1)S(1)} %add_convert_fusion), channel_id=1, source_target_pairs={{4,0},{8,4},{12,8},{14,12},{10,14},{6,10},{2,6},{0,2},{5,1},{9,5},... | collective-permute-start | bytes 589832 | tf_op jit(solution)/shard_map/back_lead1/ppermute | solution.py:378

commit v9 on v8

--- a/solution.py
+++ b/solution.py
@@ -21,7 +21,8 @@
 
 def shifted(value, axis, by):
     peers = lax.axis_size(axis)
-    return lax.ppermute(value, axis, [(i, (i + by) % peers) for i in range(peers)])
+    pairs = [(i, i + by) for i in range(peers) if 0 <= i + by < peers]
+    return lax.ppermute(value, axis, pairs)
 
 
 def pinned(values, space):
@@ -41,19 +42,45 @@
     return jnp.dot(a, b, preferred_element_type=jnp.float32)
 
 
+def tail_kernel(keys_hbm, values_hbm, out_ref, sems):
+    rows, width = out_ref.shape
+    last = pl.ds(keys_hbm.shape[0] - rows, rows)
+    copies = [
+        pltpu.make_async_copy(
+            ref.at[last], out_ref.at[:, pl.ds(index * width // 2, width // 2)], sems.at[index]
+        )
+        for index, ref in enumerate((keys_hbm, values_hbm))
+    ]
+    for copy in copies:
+        copy.start()
+    for copy in copies:
+        copy.wait()
+
+
+def tail(keys, values):
+    return pl.pallas_call(
+        tail_kernel,
+        in_specs=[pl.BlockSpec(memory_space=pltpu.HBM)] * 2,
+        out_specs=pl.BlockSpec(memory_space=pltpu.VMEM),
+        out_shape=jax.ShapeDtypeStruct((WINDOW, 2 * keys.shape[1]), keys.dtype),
+        scratch_shapes=[pltpu.SemaphoreType.DMA((2,))],
+        name="tail",
+    )(*pinned((keys, values), pltpu.HBM))
+
+
 def attend_kernel(mix, *refs):
-    done_ref = refs[-2]
-    rows = done_ref.shape[0]
-    keys = 2 * rows
     if mix:
         sink_ref, q_ref, k_ref, v_ref, ow_ref = refs[:5]
-        first_ref, k_before, v_before, rank_ref, other_ref, send_ref, own_ref = refs[5:12]
+        first_ref, before_ref, rank_ref, later_ref, send_ref, own_ref, done_ref = refs[5:]
+        rows, width = before_ref.shape[0], k_ref.shape[1]
         queries = slice(0, rows)
-        k = jnp.concatenate([k_before[rows:], k_ref[:rows]], axis=0)
-        v = jnp.concatenate([v_before[rows:], v_ref[:rows]], axis=0)
+        k = jnp.concatenate([before_ref[:, :width], k_ref[:rows]], axis=0)
+        v = jnp.concatenate([before_ref[:, width:], v_ref[:rows]], axis=0)
+        done_ref[rows:] = later_ref[...]
         copies = []
     else:
-        sink_ref, q_ref, k_ref, v_ref, ow_ref, out_ref = refs[5:11]
+        sink_ref, q_ref, k_ref, v_ref, ow_ref, done_ref = refs[5:11]
+        rows = done_ref.shape[0]
         queries = slice(rows, 2 * rows)
         sems = refs[-1]
         early, late = pl.ds(0, rows), pl.ds(rows, rows)
@@ -68,6 +95,7 @@
         for copy in copies[:4]:
             copy.wait()
         k, v = k_ref[...], v_ref[...]
+    keys = 2 * rows
     pairs = q_ref.shape[1] // LANES
     groups = k_ref.shape[1] // HEAD_DIM
 
@@ -117,23 +145,21 @@
                 / (both[LANES + 8 * side : LANES + 8 * side + 1] + sinks[side])
                 for side in range(2)
             ]
-            done_ref[:, lanes] = jnp.concatenate(parts, axis=0).T.astype(jnp.bfloat16)
+            done_ref[:rows, lanes] = jnp.concatenate(parts, axis=0).T.astype(jnp.bfloat16)
 
     for copy in copies[4:]:
         copy.wait()
+    if not mix:
+        return
     model = ow_ref.shape[1]
     width = 512 if model % 512 == 0 else model
-    if mix:
-        own_first = rank_ref[0] == 0
+    own_first = rank_ref[0] == 0
     for start in range(0, model, width):
         lanes = slice(start, start + width)
-        mine = mm(done_ref[...], ow_ref[:, lanes])
-        if mix:
-            other = other_ref[:, lanes]
-            own_ref[:, lanes] = jnp.where(own_first, mine, other)
-            send_ref[:, lanes] = jnp.where(own_first, other, mine).astype(jnp.bfloat16)
-        else:
-            out_ref[:, lanes] = mine
+        both = mm(done_ref[...], ow_ref[:, lanes])
+        early, late = both[:rows], both[rows:]
+        own_ref[:, lanes] = jnp.where(own_first, early, late)
+        send_ref[:, lanes] = jnp.where(own_first, late, early).astype(jnp.bfloat16)
 
 
 def attend(sinks, queries, keys, values, out_weight, mixed=()):
@@ -147,15 +173,15 @@
     narrow = jax.ShapeDtypeStruct((rows, model), jnp.bfloat16)
     shapes = (narrow, wide)
     if not mix:
-        shapes = tuple(jax.ShapeDtypeStruct(a.shape, a.dtype) for a in operands) + (wide,)
+        shapes = tuple(jax.ShapeDtypeStruct(a.shape, a.dtype) for a in operands)
+        shapes += (jax.ShapeDtypeStruct((rows, width), jnp.bfloat16),)
     return pl.pallas_call(
         functools.partial(attend_kernel, mix),
-        in_specs=[vmem if mix else hbm] * 5 + ([smem, vmem, vmem, smem, vmem] if mix else []),
+        in_specs=[vmem if mix else hbm] * 5 + ([smem, vmem, smem, vmem] if mix else []),
         out_specs=(vmem,) * len(shapes),
         out_shape=shapes,
         scratch_shapes=[
-            pltpu.VMEM((rows, width), jnp.bfloat16),
-            pltpu.SemaphoreType.DMA((6,)),
+            pltpu.VMEM((2 * rows, width), jnp.bfloat16) if mix else pltpu.SemaphoreType.DMA((6,))
         ],
         compiler_params=pltpu.CompilerParams(vmem_limit_bytes=8 * MIB),
         cost_estimate=pl.CostEstimate(
@@ -342,23 +368,20 @@
             blocks[0] = tied(blocks[0], *after)
         with jax.named_scope(f"hop{distance}"):
             outs = experts(blocks, me, halves)
-        worked[distance] = outs[0]
+        worked.setdefault(distance, outs[0])
         keep(keys, outs)
+        return outs[0]
 
     for distance in range(1, far + 1):
         bring(distance, True, *([worked[distance - 2]] if distance > 1 else []))
+        trails = []
         if distance < far:
-            bring(
-                distance,
-                False,
-                *([came[side, distance - 1, side] for side in sides] if distance > 1 else []),
-            )
-        if distance < far - 1:
-            apply(distance, (True, False))
-        elif distance < far:
-            apply(distance, (True,), worked[distance - 1])
-    apply(far, (True,), worked[far - 1])
-    apply(far - 1, (False,), worked[far])
+            before = [came[side, distance - 1, side] for side in sides] if distance > 1 else []
+            bring(distance, False, *before)
+            if 1 < distance < far - 1:
+                trails = [came[side, distance, 1 - side] for side in sides]
+        latest = apply(distance, (True,), worked[distance - 1], *trails)
+    latest = apply(far - 1, (False,), latest)
 
     moving = {}
 
@@ -377,12 +400,14 @@
             with jax.named_scope(f"back_{'lead' if lead else 'trail'}{distance}"):
                 moving[side, piece] = lax.ppermute(value, "seq", hops[side])
 
-    for distance in range(far, 0, -1):
-        if distance == far:
-            send(far - 1, False, *[came[side, far, side] for side in sides])
-        elif distance > 1:
-            send(distance - 1, False, worked[far] if distance == far - 1 else moving[0, 0])
+    send(far, True)
+    send(far - 1, False, *[came[side, far, side] for side in sides])
+    for distance in range(far - 1, 0, -1):
+        leads = [moving[side, side] for side in sides]
         send(distance, True)
+        if distance > 1:
+            latest = apply(distance - 1, (False,), latest, *leads)
+            send(distance - 1, False, leads[0])
     final = []
     for piece in sides:
         total = given[0, piece].astype(jnp.float32)
@@ -452,7 +477,7 @@
     gate_weight, up_weight, down_weight = gate_weight[0], up_weight[0], down_weight[0]
     use_ring = EXP_DEV * lax.axis_size("seq") <= 2 * TOP
 
-    k_before, v_before = shifted(key_rows, "seq", 1), shifted(value_rows, "seq", 1)
+    before = shifted(tail(key_rows, value_rows), "seq", 1)
     others = []
     if use_ring:
         others = [swapped(w, "rep") for w in (gate_weight, up_weight, down_weight)]
@@ -460,7 +485,7 @@
     *operands, later_half = attend(
         sink_logits.reshape(1, -1), queries, key_rows, value_rows, out_weight
     )
-    send, own = attend(*operands, (first, k_before, v_before, rank, later_half))
+    send, own = attend(*operands, (first, before, rank, later_half))
     came = swapped(send, "rep")
     expert_count = lax.axis_size("seq") * EXP_DEV if use_ring else 0
     residual, *pieces = norm(

time: 84.4 us -> 86.3 us (1.023)
  Pallas kernels: 24.5 us -> 26 us
    ppermute x14, waiting for transfers between devices: 4.03 us -> 10.5 us  [bring(): came[side, distance, piece] = lax.ppermute(block, 'seq', hops[side])]
    ppermute x14, waiting for transfers between devices: 15.7 us -> 11.1 us  [send(): moving[side, piece] = lax.ppermute(value, 'seq', hops[side])]
    ppermute x2 -> x1, waiting for transfers between devices: 2.23 us -> 0.01 us  [shifted(): return lax.ppermute(value, axis, pairs)]
    pallas_call x0 -> x1, Pallas kernels: none -> 1.42 us  [tail(): pl.pallas_call(tail_kernel, in_specs=[pl.BlockSpec(memory_space=pltpu.HBM...]
    pallas_call x6 -> x8, Pallas kernels: 18.2 us -> 18.8 us  [experts(): pl.pallas_call(functools.partial(expert_kernel, min(256, half), len(block...]
    ppermute x2 -> x1, starting transfers between devices: 4.04 us -> 4.4 us  [shifted(): return lax.ppermute(value, axis, pairs)]
  transfers between devices with their start and end apart: 34 -> 33, of which waited for: 18 -> 15; matrix products, arithmetic and copies ran while one was open for 1% -> 1% of each run, Pallas kernels for 29% -> 30%
where the time goes in v9:
time: 86.3 us; the launch traced here: 86.2 us
  starting transfers between devices  35.2 us (41%)
  Pallas kernels  26 us (30%)
  waiting for transfers between devices  23.1 us (27%)
  other arithmetic  1.44 us (2%)
    pallas_call x8, Pallas kernels, experts(): pl.pallas_call(functools.partial(expert_kernel, min(256, half), len(block...  18.8 us
    ppermute x14, starting transfers between devices, bring(): came[side, distance, piece] = lax.ppermute(block, 'seq', hops[side])  14.8 us
    ppermute x14, starting transfers between devices, send(): moving[side, piece] = lax.ppermute(value, 'seq', hops[side])  14.8 us
    ppermute x14, waiting for transfers between devices, send(): moving[side, piece] = lax.ppermute(value, 'seq', hops[side])  11.1 us
    ppermute x14, waiting for transfers between devices, bring(): came[side, distance, piece] = lax.ppermute(block, 'seq', hops[side])  10.5 us
    pallas_call x2, Pallas kernels, attend(): pl.pallas_call(functools.partial(attend_kernel, mix), in_specs=[vmem if m...  5.56 us
    ppermute x1, starting transfers between devices, shifted(): return lax.ppermute(value, axis, pairs)  4.4 us
  transfers between devices with their start and end apart: 33, of which 15 were waited for; matrix products, arithmetic and copies ran while one was open for 1% of the time, Pallas kernels for 30%

profile of v9, /device:TPU:0, one launch (start us, length us, event | category | flops | bytes accessed | tf_op | source)
XLA Modules:
  0.0 86.2 jit_solution(14474811829732064728)
XLA Ops:
  0.0 0.5 collective-permute-start.2
  0.5 0.5 collective-permute-start.4
  1.0 1.4 %tail.1 = bf16[128,256]{1,0:T(8,128)(2,1)} custom-call(bf16[256,128]{1,0:T(8,128)(2,1)} %keys_hbm.1, bf16[256,128]{1,0:T(8,128)(2,1)} %values_hbm.1), custom_call_target="tpu_custom_call" | custom-call | tf_op jit(solution)/shard_map/tail/pallas_call | solution.py:61
  2.4 4.4 %collective-permute-start = (bf16[128,256]{1,0:T(8,128)(2,1)}, bf16[128,256]{1,0:T(8,128)(2,1)S(1)}, u32[]{:S(2)}, u32[]{:S(2)}) collective-permute-start(bf16[128,256]{1,0:T(8,128)(2,1)} %tail.1), channel_id=1, source_target_pairs={{0,2},{2,4},{4,6},{6,8},{8,10},{10,12},{12,14},{1,3},{3,5},{5,7},{... | collective-permute-start | bytes 196616 | tf_op jit(solution)/shard_map/ppermute | solution.py:25
  6.8 3.0 %attend.2 = (f32[1,16]{1,0:T(1,128)S(1)}, bf16[256,1024]{1,0:T(8,128)(2,1)S(1)}, bf16[256,128]{1,0:T(8,128)(2,1)S(1)}, bf16[256,128]{1,0:T(8,128)(2,1)S(1)}, bf1...) custom-call(f32[1,16]{1,0:T(1,128)} %bitcast.38, bf16[256,1024]{1,0:T(8,128)(2,1)} %refs_1_.1, ...), custom_call_target="tpu_custom_call" | custom-call | flops 671088640 | bytes 6291456 | tf_op jit(solution)/shard_map/attend/pallas_call | solution.py:178
  9.9 2.6 %attend.3 = (bf16[128,1536]{1,0:T(8,128)(2,1)S(1)}, f32[128,1536]{1,0:T(8,128)S(1)}) custom-call(f32[1,16]{1,0:T(1,128)S(1)} %get-tuple-element.74.refs_0_, bf16[256,1024]{1,0:T(8,128)(2,1)S(1)} %get-tuple-element.75.refs_1_, bf16[256,128]{1,0:T(8,128)(2,1)S(1)} %get-tuple-element.76.refs_2_, bf16[256,128]{1,0:T(8,128)(2,1)S(1)} %get-tuple-element.77.refs_3_, ...), custom_call_target="tpu_custom_call" | custom-call | flops 671088640 | bytes 6291456 | tf_op jit(solution)/shard_map/attend/pallas_call | solution.py:178
  12.8 1.5 %collective-permute-done.1.came_ref = bf16[128,1536]{1,0:T(8,128)(2,1)S(1)} collective-permute-done((bf16[128,1536]{1,0:T(8,128)(2,1)S(1)}, bf16[128,1536]{1,0:T(8,128)(2,1)S(1)}, u32[]{:S(2)}, u32[]{:S(2)}) %collective-permute-start.1) | collective-permute-done | bytes 393248 | tf_op jit(solution)/shard_map/ppermute | solution.py:38
  14.6 2.6 %collective-permute-start.5 = (bf16[784,128]{1,0:T(8,128)(2,1)S(1)}, bf16[784,128]{1,0:T(8,128)(2,1)S(1)}, u32[]{:S(2)}, u32[]{:S(2)}) collective-permute-start(bf16[784,128]{1,0:T(8,128)(2,1)S(1)} %get-tuple-element.88.refs_0_), channel_id=1, source_target_pairs={{0,4},{4,8},{8,12},{12,14},{14,10},{10,6},{6,2},{2,0},{1,5},{5,9},... | collective-permute-start | bytes 602120 | tf_op jit(solution)/shard_map/out_lead1/ppermute | solution.py:362
  17.2 2.0 %collective-permute-start.11 = (bf16[784,128]{1,0:T(8,128)(2,1)S(1)}, bf16[784,128]{1,0:T(8,128)(2,1)S(1)}, u32[]{:S(2)}, u32[]{:S(2)}) collective-permute-start(bf16[784,128]{1,0:T(8,128)(2,1)S(1)} %get-tuple-element.89.refs_1_), channel_id=1, source_target_pairs={{0,4},{4,8},{8,12},{12,14},{14,10},{10,6},{6,2},{2,0},{1,5},{5,9},... | collective-permute-start | bytes 602120 | tf_op jit(solution)/shard_map/out_trail1/ppermute | solution.py:362
  19.3 4.1 %experts.8 = (bf16[64,1536]{1,0:T(8,128)(2,1)S(1)}, bf16[64,1536]{1,0:T(8,128)(2,1)S(1)}, bf16[1536,768]{1,0:T(8,128)(2,1)S(1)}, bf16[1536,768]{1,0:T(8,128)(2,1)S(1)}, bf16[768,1536]{1,0:T(8,128)(2,1)S(1)}) custom-call(s32[1]{0:T(128)} %bitcast.5.me_ref, bf16[784,128]{1,0:T(8,128)(2,1)S(1)} %get-tuple-element.88.refs_0_, ...), custom_call_target="tpu_custom_call" | custom-call | flops 1811939328 | bytes 1179648 | tf_op jit(solution)/shard_map/experts/pallas_call | solution.py:314
  23.4 1.7 %collective-permute-done.6.refs_1_ = bf16[784,128]{1,0:T(8,128)(2,1)S(1)} collective-permute-done((bf16[784,128]{1,0:T(8,128)(2,1)S(1)}, bf16[784,128]{1,0:T(8,128)(2,1)S(1)}, u32[]{:S(2)}, u32[]{:S(2)}) %collective-permute-start.6) | collective-permute-done | bytes 200736 | tf_op jit(solution)/shard_map/out_lead1/ppermute | solution.py:362
  25.1 1.6 %collective-permute-start.7 = (bf16[784,128]{1,0:T(8,128)(2,1)S(1)}, bf16[784,128]{1,0:T(8,128)(2,1)S(1)}, u32[]{:S(2)}, u32[]{:S(2)}) collective-permute-start(bf16[784,128]{1,0:T(8,128)(2,1)S(1)} %collective-permute-done.5.refs_0_), channel_id=1, source_target_pairs={{0,4},{4,8},{8,12},{12,14},{14,10},{10,6},{6,2},{2,0},{1,5},{5,9},... | collective-permute-start | bytes 602120 | tf_op jit(solution)/shard_map/out_lead2/ppermute | solution.py:362
  26.7 0.4 collective-permute-start.8
  27.1 2.3 %collective-permute-done.12.refs_1_ = bf16[784,128]{1,0:T(8,128)(2,1)S(1)} collective-permute-done((bf16[784,128]{1,0:T(8,128)(2,1)S(1)}, bf16[784,128]{1,0:T(8,128)(2,1)S(1)}, u32[]{:S(2)}, u32[]{:S(2)}) %collective-permute-start.12) | collective-permute-done | bytes 200736 | tf_op jit(solution)/shard_map/out_trail1/ppermute | solution.py:362
  29.4 1.6 %collective-permute-start.13 = (bf16[784,128]{1,0:T(8,128)(2,1)S(1)}, bf16[784,128]{1,0:T(8,128)(2,1)S(1)}, u32[]{:S(2)}, u32[]{:S(2)}) collective-permute-start(bf16[784,128]{1,0:T(8,128)(2,1)S(1)} %collective-permute-done.11.refs_0_), channel_id=1, source_target_pairs={{0,4},{4,8},{8,12},{12,14},{14,10},{10,6},{6,2},{2,0},{1,5},{5,9},... | collective-permute-start | bytes 602120 | tf_op jit(solution)/shard_map/out_trail2/ppermute | solution.py:362
  31.4 2.1 %experts.9 = (bf16[64,1536]{1,0:T(8,128)(2,1)S(1)}, bf16[64,1536]{1,0:T(8,128)(2,1)S(1)}) custom-call(s32[1]{0:T(128)} %bitcast.5.me_ref, bf16[784,128]{1,0:T(8,128)(2,1)S(1)} %collective-permute-done.5.refs_0_, bf16[784,128]{1,0:T(8,128)(2,1)S(1)} %collective-permute-done.6.refs_1_, bf16[1536,768]{1,0:T(8,128)(2,1)S(1)} %bitcast.11, ...), custom_call_target="tpu_custom_call" | custom-call | flops 1811939328 | bytes 1179648 | tf_op jit(solution)/shard_map/hop1/experts/pallas_call | solution.py:314
  33.6 0.5 collective-permute-done.8.refs_1_
  34.0 1.6 %collective-permute-start.9 = (bf16[784,128]{1,0:T(8,128)(2,1)S(1)}, bf16[784,128]{1,0:T(8,128)(2,1)S(1)}, u32[]{:S(2)}, u32[]{:S(2)}) collective-permute-start(bf16[784,128]{1,0:T(8,128)(2,1)S(1)} %collective-permute-done.7.refs_0_), channel_id=1, source_target_pairs={{0,4},{4,8},{8,12},{12,14},{14,10},{10,6},{6,2},{2,0},{1,5},{5,9},... | collective-permute-start | bytes 602120 | tf_op jit(solution)/shard_map/out_lead3/ppermute | solution.py:362
  36.1 0.8 collective-permute-done.13.refs_0_
  36.8 1.7 %collective-permute-done.14.refs_1_ = bf16[784,128]{1,0:T(8,128)(2,1)S(1)} collective-permute-done((bf16[784,128]{1,0:T(8,128)(2,1)S(1)}, bf16[784,128]{1,0:T(8,128)(2,1)S(1)}, u32[]{:S(2)}, u32[]{:S(2)}) %collective-permute-start.14) | collective-permute-done | bytes 200736 | tf_op jit(solution)/shard_map/out_trail2/ppermute | solution.py:362
  38.5 2.1 %experts.10 = (bf16[64,1536]{1,0:T(8,128)(2,1)S(1)}, bf16[64,1536]{1,0:T(8,128)(2,1)S(1)}) custom-call(s32[1]{0:T(128)} %bitcast.5.me_ref, bf16[784,128]{1,0:T(8,128)(2,1)S(1)} %collective-permute-done.7.refs_0_, bf16[784,128]{1,0:T(8,128)(2,1)S(1)} %collective-permute-done.8.refs_1_, bf16[1536,768]{1,0:T(8,128)(2,1)S(1)} %bitcast.12, ...), custom_call_target="tpu_custom_call" | custom-call | flops 1811939328 | bytes 1179648 | tf_op jit(solution)/shard_map/hop2/experts/pallas_call | solution.py:314
  40.7 0.7 collective-permute-done.10.refs_1_
  41.3 1.4 %collective-permute-start.15 = (bf16[784,128]{1,0:T(8,128)(2,1)S(1)}, bf16[784,128]{1,0:T(8,128)(2,1)S(1)}, u32[]{:S(2)}, u32[]{:S(2)}) collective-permute-start(bf16[784,128]{1,0:T(8,128)(2,1)S(1)} %collective-permute-done.9.refs_0_), channel_id=1, source_target_pairs={{0,4},{4,8},{8,12},{12,14},{14,10},{10,6},{6,2},{2,0},{1,5},{5,9},... | collective-permute-start | bytes 602120 | tf_op jit(solution)/shard_map/out_lead4/ppermute | solution.py:362
  42.8 0.6 collective-permute-start.16
  43.4 1.4 %collective-permute-start.19 = (bf16[784,128]{1,0:T(8,128)(2,1)S(1)}, bf16[784,128]{1,0:T(8,128)(2,1)S(1)}, u32[]{:S(2)}, u32[]{:S(2)}) collective-permute-start(bf16[784,128]{1,0:T(8,128)(2,1)S(1)} %collective-permute-done.13.refs_0_), channel_id=1, source_target_pairs={{0,4},{4,8},{8,12},{12,14},{14,10},{10,6},{6,2},{2,0},{1,5},{5,9},... | collective-permute-start | bytes 602120 | tf_op jit(solution)/shard_map/out_trail3/ppermute | solution.py:362
  44.8 0.6 collective-permute-start.20
  45.4 2.1 %experts.11 = (bf16[64,1536]{1,0:T(8,128)(2,1)S(1)}, bf16[64,1536]{1,0:T(8,128)(2,1)S(1)}) custom-call(s32[1]{0:T(128)} %bitcast.5.me_ref, bf16[784,128]{1,0:T(8,128)(2,1)S(1)} %collective-permute-done.9.refs_0_, bf16[784,128]{1,0:T(8,128)(2,1)S(1)} %collective-permute-done.10.refs_1_, bf16[1536,768]{1,0:T(8,128)(2,1)S(1)} %bitcast.13, ...), custom_call_target="tpu_custom_call" | custom-call | flops 1811939328 | bytes 1179648 | tf_op jit(solution)/shard_map/hop3/experts/pallas_call | solution.py:314
  47.5 0.7 collective-permute-done.15.refs_0_
  48.2 2.1 %collective-permute-done.16.refs_1_ = bf16[784,128]{1,0:T(8,128)(2,1)S(1)} collective-permute-done((bf16[784,128]{1,0:T(8,128)(2,1)S(1)}, bf16[784,128]{1,0:T(8,128)(2,1)S(1)}, u32[]{:S(2)}, u32[]{:S(2)}) %collective-permute-start.16) | collective-permute-done | bytes 200736 | tf_op jit(solution)/shard_map/out_lead4/ppermute | solution.py:362
  50.3 2.1 %experts.12 = (bf16[64,1536]{1,0:T(8,128)(2,1)S(1)}, bf16[64,1536]{1,0:T(8,128)(2,1)S(1)}) custom-call(s32[1]{0:T(128)} %bitcast.5.me_ref, bf16[784,128]{1,0:T(8,128)(2,1)S(1)} %collective-permute-done.15.refs_0_, bf16[784,128]{1,0:T(8,128)(2,1)S(1)} %collective-permute-done.16.refs_1_, bf16[1536,768]{1,0:T(8,128)(2,1)S(1)} %bitcast.14, ...), custom_call_target="tpu_custom_call" | custom-call | flops 1811939328 | bytes 1179648 | tf_op jit(solution)/shard_map/hop4/experts/pallas_call | solution.py:314
  52.5 1.8 %collective-permute-start.17 = (bf16[64,1536]{1,0:T(8,128)(2,1)S(1)}, bf16[64,1536]{1,0:T(8,128)(2,1)S(1)}, u32[]{:S(2)}, u32[]{:S(2)}) collective-permute-start(bf16[64,1536]{1,0:T(8,128)(2,1)S(1)} %get-tuple-element.110), channel_id=1, source_target_pairs={{0,4},{4,8},{8,12},{12,14},{14,10},{10,6},{6,2},{2,0},{1,5},{5,9},... | collective-permute-start | bytes 589832 | tf_op jit(solution)/shard_map/back_lead4/ppermute | solution.py:401
  54.6 2.0 %collective-permute-start.26 = (bf16[64,1536]{1,0:T(8,128)(2,1)S(1)}, bf16[64,1536]{1,0:T(8,128)(2,1)S(1)}, u32[]{:S(2)}, u32[]{:S(2)}) collective-permute-start(bf16[64,1536]{1,0:T(8,128)(2,1)S(1)} %get-tuple-element.128), channel_id=1, source_target_pairs={{0,4},{4,8},{8,12},{12,14},{14,10},{10,6},{6,2},{2,0},{1,5},{5,9},... | collective-permute-start | bytes 589832 | tf_op jit(solution)/shard_map/back_trail3/ppermute | solution.py:401
  56.6 2.1 %experts.13 = (bf16[64,1536]{1,0:T(8,128)(2,1)S(1)}, bf16[64,1536]{1,0:T(8,128)(2,1)S(1)}) custom-call(s32[1]{0:T(128)} %bitcast.5.me_ref, bf16[784,128]{1,0:T(8,128)(2,1)S(1)} %collective-permute-done.19.refs_0_, bf16[784,128]{1,0:T(8,128)(2,1)S(1)} %collective-permute-done.20.refs_1_, bf16[1536,768]{1,0:T(8,128)(2,1)S(1)} %bitcast.15, ...), custom_call_target="tpu_custom_call" | custom-call | flops 1811939328 | bytes 1179648 | tf_op jit(solution)/shard_map/hop3/experts/pallas_call | solution.py:314
  59.1 2.9 %collective-permute-done.18 = bf16[64,1536]{1,0:T(8,128)(2,1)S(1)} collective-permute-done((bf16[64,1536]{1,0:T(8,128)(2,1)S(1)}, bf16[64,1536]{1,0:T(8,128)(2,1)S(1)}, u32[]{:S(2)}, u32[]{:S(2)}) %collective-permute-start.18) | collective-permute-done | bytes 196640 | tf_op jit(solution)/shard_map/back_lead4/ppermute | solution.py:401
  62.4 1.8 %collective-permute-start.21 = (bf16[64,1536]{1,0:T(8,128)(2,1)S(1)}, bf16[64,1536]{1,0:T(8,128)(2,1)S(1)}, u32[]{:S(2)}, u32[]{:S(2)}) collective-permute-start(bf16[64,1536]{1,0:T(8,128)(2,1)S(1)} %add_convert_fusion.9), channel_id=1, source_target_pairs={{0,4},{4,8},{8,12},{12,14},{14,10},{10,6},{6,2},{2,0},{1,5},{5,9},... | collective-permute-start | bytes 589832 | tf_op jit(solution)/shard_map/back_lead3/ppermute | solution.py:401
  64.2 2.0 %collective-permute-done.27 = bf16[64,1536]{1,0:T(8,128)(2,1)S(1)} collective-permute-done((bf16[64,1536]{1,0:T(8,128)(2,1)S(1)}, bf16[64,1536]{1,0:T(8,128)(2,1)S(1)}, u32[]{:S(2)}, u32[]{:S(2)}) %collective-permute-start.27) | collective-permute-done | bytes 196640 | tf_op jit(solution)/shard_map/back_trail3/ppermute | solution.py:401
  66.6 1.8 %collective-permute-start.28 = (bf16[64,1536]{1,0:T(8,128)(2,1)S(1)}, bf16[64,1536]{1,0:T(8,128)(2,1)S(1)}, u32[]{:S(2)}, u32[]{:S(2)}) collective-permute-start(bf16[64,1536]{1,0:T(8,128)(2,1)S(1)} %add_convert_fusion.4), channel_id=1, source_target_pairs={{0,4},{4,8},{8,12},{12,14},{14,10},{10,6},{6,2},{2,0},{1,5},{5,9},... | collective-permute-start | bytes 589832 | tf_op jit(solution)/shard_map/back_trail2/ppermute | solution.py:401
  68.4 2.1 %experts.14 = (bf16[64,1536]{1,0:T(8,128)(2,1)S(1)}, bf16[64,1536]{1,0:T(8,128)(2,1)S(1)}) custom-call(s32[1]{0:T(128)} %bitcast.5.me_ref, bf16[784,128]{1,0:T(8,128)(2,1)S(1)} %collective-permute-done.13.refs_0_, bf16[784,128]{1,0:T(8,128)(2,1)S(1)} %collective-permute-done.14.refs_1_, bf16[1536,768]{1,0:T(8,128)(2,1)S(1)} %bitcast.16, ...), custom_call_target="tpu_custom_call" | custom-call | flops 1811939328 | bytes 1179648 | tf_op jit(solution)/shard_map/hop2/experts/pallas_call | solution.py:314
  71.0 1.8 %collective-permute-start.23 = (bf16[64,1536]{1,0:T(8,128)(2,1)S(1)}, bf16[64,1536]{1,0:T(8,128)(2,1)S(1)}, u32[]{:S(2)}, u32[]{:S(2)}) collective-permute-start(bf16[64,1536]{1,0:T(8,128)(2,1)S(1)} %add_convert_fusion.7), channel_id=1, source_target_pairs={{0,4},{4,8},{8,12},{12,14},{14,10},{10,6},{6,2},{2,0},{1,5},{5,9},... | collective-permute-start | bytes 589832 | tf_op jit(solution)/shard_map/back_lead2/ppermute | solution.py:401
  72.8 1.2 %collective-permute-done.29 = bf16[64,1536]{1,0:T(8,128)(2,1)S(1)} collective-permute-done((bf16[64,1536]{1,0:T(8,128)(2,1)S(1)}, bf16[64,1536]{1,0:T(8,128)(2,1)S(1)}, u32[]{:S(2)}, u32[]{:S(2)}) %collective-permute-start.29) | collective-permute-done | bytes 196640 | tf_op jit(solution)/shard_map/back_trail2/ppermute | solution.py:401
  74.0 0.6 collective-permute-start.30
  74.7 1.5 %collective-permute-start.31 = (bf16[64,1536]{1,0:T(8,128)(2,1)S(1)}, bf16[64,1536]{1,0:T(8,128)(2,1)S(1)}, u32[]{:S(2)}, u32[]{:S(2)}) collective-permute-start(bf16[64,1536]{1,0:T(8,128)(2,1)S(1)} %add_convert_fusion.1), channel_id=1, source_target_pairs={{0,4},{4,8},{8,12},{12,14},{14,10},{10,6},{6,2},{2,0},{1,5},{5,9},... | collective-permute-start | bytes 589832 | tf_op jit(solution)/shard_map/back_trail1/ppermute | solution.py:401
  76.2 2.1 %experts.15 = (bf16[64,1536]{1,0:T(8,128)(2,1)S(1)}, bf16[64,1536]{1,0:T(8,128)(2,1)S(1)}) custom-call(s32[1]{0:T(128)} %bitcast.5.me_ref, bf16[784,128]{1,0:T(8,128)(2,1)S(1)} %collective-permute-done.11.refs_0_, bf16[784,128]{1,0:T(8,128)(2,1)S(1)} %collective-permute-done.12.refs_1_, bf16[1536,768]{1,0:T(8,128)(2,1)S(1)} %bitcast.17, ...), custom_call_target="tpu_custom_call" | custom-call | flops 1811939328 | bytes 1179648 | tf_op jit(solution)/shard_map/hop1/experts/pallas_call | solution.py:314
  78.4 1.1 %collective-permute-start.25 = (bf16[64,1536]{1,0:T(8,128)(2,1)S(1)}, bf16[64,1536]{1,0:T(8,128)(2,1)S(1)}, u32[]{:S(2)}, u32[]{:S(2)}) collective-permute-start(bf16[64,1536]{1,0:T(8,128)(2,1)S(1)} %add_convert_fusion.5), channel_id=1, source_target_pairs={{0,4},{4,8},{8,12},{12,14},{14,10},{10,6},{6,2},{2,0},{1,5},{5,9},... | collective-permute-start | bytes 589832 | tf_op jit(solution)/shard_map/back_lead1/ppermute | solution.py:401
  79.5 1.0 %collective-permute-start.32 = (bf16[64,1536]{1,0:T(8,128)(2,1)S(1)}, bf16[64,1536]{1,0:T(8,128)(2,1)S(1)}, u32[]{:S(2)}, u32[]{:S(2)}) collective-permute-start(bf16[64,1536]{1,0:T(8,128)(2,1)S(1)} %add_convert_fusion), channel_id=1, source_target_pairs={{4,0},{8,4},{12,8},{14,12},{10,14},{6,10},{2,6},{0,2},{5,1},{9,5},... | collective-permute-start | bytes 589832 | tf_op jit(solution)/shard_map/back_lead1/ppermute | solution.py:401
  80.6 3.5 %collective-permute-done.25 = bf16[64,1536]{1,0:T(8,128)(2,1)S(1)} collective-permute-done((bf16[64,1536]{1,0:T(8,128)(2,1)S(1)}, bf16[64,1536]{1,0:T(8,128)(2,1)S(1)}, u32[]{:S(2)}, u32[]{:S(2)}) %collective-permute-start.25) | collective-permute-done | bytes 196640 | tf_op jit(solution)/shard_map/back_lead1/ppermute | solution.py:401
  84.2 1.1 %collective-permute-done.32 = bf16[64,1536]{1,0:T(8,128)(2,1)S(1)} collective-permute-done((bf16[64,1536]{1,0:T(8,128)(2,1)S(1)}, bf16[64,1536]{1,0:T(8,128)(2,1)S(1)}, u32[]{:S(2)}, u32[]{:S(2)}) %collective-permute-start.32) | collective-permute-done | bytes 196640 | tf_op jit(solution)/shard_map/back_lead1/ppermute | solution.py:401
  85.3 0.8 fusion
  (60 shorter events, 4.0 us)
Async XLA Ops:
  0.0 14.6 %collective-permute-start.2 = (bf16[1536,768]{1,0:T(8,128)(2,1)}, bf16[1536,768]{1,0:T(8,128)(2,1)S(1)}, u32[]{:S(2)}, u32[]{:S(2)}) collective-permute-start(bf16[1536,768]{1,0:T(8,128)(2,1)} %bitcast.9), channel_id=1, source_target_pairs={{0,1},{1,0},{2,3},{3,2},{4,5},{5,4},{6,7},{7,6},{8,9},{9,8},{10,11... | collective-permute-start | bytes 7077896 | tf_op jit(solution)/shard_map/ppermute | solution.py:38
  0.5 14.2 %collective-permute-start.3 = (bf16[1536,768]{1,0:T(8,128)(2,1)}, bf16[1536,768]{1,0:T(8,128)(2,1)}, u32[]{:S(2)}, u32[]{:S(2)}) collective-permute-start(bf16[1536,768]{1,0:T(8,128)(2,1)} %bitcast.18), channel_id=1, source_target_pairs={{0,1},{1,0},{2,3},{3,2},{4,5},{5,4},{6,7},{7,6},{8,9},{9,8},{10,11... | collective-permute-start | bytes 7077896 | tf_op jit(solution)/shard_map/ppermute | solution.py:38
  0.5 14.1 %collective-permute-start.4 = (bf16[768,1536]{1,0:T(8,128)(2,1)}, bf16[768,1536]{1,0:T(8,128)(2,1)}, u32[]{:S(2)}, u32[]{:S(2)}) collective-permute-start(bf16[768,1536]{1,0:T(8,128)(2,1)} %bitcast.27), channel_id=1, source_target_pairs={{0,1},{1,0},{2,3},{3,2},{4,5},{5,4},{6,7},{7,6},{8,9},{9,8},{10,11... | collective-permute-start | bytes 7077896 | tf_op jit(solution)/shard_map/ppermute | solution.py:38
  2.4 7.5 %collective-permute-start = (bf16[128,256]{1,0:T(8,128)(2,1)}, bf16[128,256]{1,0:T(8,128)(2,1)S(1)}, u32[]{:S(2)}, u32[]{:S(2)}) collective-permute-start(bf16[128,256]{1,0:T(8,128)(2,1)} %tail.1), channel_id=1, source_target_pairs={{0,2},{2,4},{4,6},{6,8},{8,10},{10,12},{12,14},{1,3},{3,5},{5,7},{... | collective-permute-start | bytes 196616 | tf_op jit(solution)/shard_map/ppermute | solution.py:25
  6.8 12.5 %copy-start.2 = (bf16[1,768,1536]{2,1,0:T(8,128)(2,1)S(1)}, bf16[1,768,1536]{2,1,0:T(8,128)(2,1)}, u32[]{:S(2)}) copy-start(bf16[1,768,1536]{2,1,0:T(8,128)(2,1)} %param.23) | copy-start | bytes 7077892
  9.8 2.9 %copy-start.7 = (f32[1536]{0:T(1024)S(1)}, f32[1536]{0:T(1024)}, u32[]{:S(2)}) copy-start(f32[1536]{0:T(1024)} %param.18) | copy-start | bytes 18436
  9.8 4.4 %copy-start.3 = (bf16[128,1536]{1,0:T(8,128)(2,1)S(1)}, bf16[128,1536]{1,0:T(8,128)(2,1)}, u32[]{:S(2)}) copy-start(bf16[128,1536]{1,0:T(8,128)(2,1)} %stream_ref.1) | copy-start | bytes 1179652
  9.9 4.4 %copy-start.4 = (s32[128,4]{0,1:T(4,128)S(1)}, s32[128,4]{0,1:T(4,128)}, u32[]{:S(2)}) copy-start(s32[128,4]{0,1:T(4,128)} %param.19) | copy-start | bytes 6148
  9.9 4.4 %copy-start.5 = (f32[128,4]{0,1:T(4,128)S(1)}, f32[128,4]{0,1:T(4,128)}, u32[]{:S(2)}) copy-start(f32[128,4]{0,1:T(4,128)} %param.20) | copy-start | bytes 6148
  9.9 9.4 %copy-start = (bf16[1,1536,768]{2,1,0:T(8,128)(2,1)S(1)}, bf16[1,1536,768]{2,1,0:T(8,128)(2,1)}, u32[]{:S(2)}) copy-start(bf16[1,1536,768]{2,1,0:T(8,128)(2,1)} %param.21) | copy-start | bytes 7077892
  9.9 9.4 %copy-start.1 = (bf16[1,1536,768]{2,1,0:T(8,128)(2,1)S(1)}, bf16[1,1536,768]{2,1,0:T(8,128)(2,1)}, u32[]{:S(2)}) copy-start(bf16[1,1536,768]{2,1,0:T(8,128)(2,1)} %param.22) | copy-start | bytes 7077892
  12.5 1.8 %collective-permute-start.1 = (bf16[128,1536]{1,0:T(8,128)(2,1)S(1)}, bf16[128,1536]{1,0:T(8,128)(2,1)S(1)}, u32[]{:S(2)}, u32[]{:S(2)}) collective-permute-start(bf16[128,1536]{1,0:T(8,128)(2,1)S(1)} %get-tuple-element.81), channel_id=1, source_target_pairs={{0,1},{1,0},{2,3},{3,2},{4,5},{5,4},{6,7},{7,6},{8,9},{9,8},{10,11... | collective-permute-start | bytes 1179656 | tf_op jit(solution)/shard_map/ppermute | solution.py:38
  14.6 4.7 %copy-start.6 = (bf16[1536,768]{1,0:T(8,128)(2,1)}, bf16[1536,768]{1,0:T(8,128)(2,1)S(1)}, u32[]{:S(2)}) copy-start(bf16[1536,768]{1,0:T(8,128)(2,1)S(1)} %collective-permute-done.2.refs_5_) | copy-start | bytes 7077892
  14.6 8.8 %collective-permute-start.5 = (bf16[784,128]{1,0:T(8,128)(2,1)S(1)}, bf16[784,128]{1,0:T(8,128)(2,1)S(1)}, u32[]{:S(2)}, u32[]{:S(2)}) collective-permute-start(bf16[784,128]{1,0:T(8,128)(2,1)S(1)} %get-tuple-element.88.refs_0_), channel_id=1, source_target_pairs={{0,4},{4,8},{8,12},{12,14},{14,10},{10,6},{6,2},{2,0},{1,5},{5,9},... | collective-permute-start | bytes 602120 | tf_op jit(solution)/shard_map/out_lead1/ppermute | solution.py:362
  17.2 7.9 %collective-permute-start.6 = (bf16[784,128]{1,0:T(8,128)(2,1)S(1)}, bf16[784,128]{1,0:T(8,128)(2,1)S(1)}, u32[]{:S(2)}, u32[]{:S(2)}) collective-permute-start(bf16[784,128]{1,0:T(8,128)(2,1)S(1)} %get-tuple-element.89.refs_1_), channel_id=1, source_target_pairs={{4,0},{8,4},{12,8},{14,12},{10,14},{6,10},{2,6},{0,2},{5,1},{9,5},... | collective-permute-start | bytes 602120 | tf_op jit(solution)/shard_map/out_lead1/ppermute | solution.py:362
  17.2 9.9 %collective-permute-start.11 = (bf16[784,128]{1,0:T(8,128)(2,1)S(1)}, bf16[784,128]{1,0:T(8,128)(2,1)S(1)}, u32[]{:S(2)}, u32[]{:S(2)}) collective-permute-start(bf16[784,128]{1,0:T(8,128)(2,1)S(1)} %get-tuple-element.89.refs_1_), channel_id=1, source_target_pairs={{0,4},{4,8},{8,12},{12,14},{14,10},{10,6},{6,2},{2,0},{1,5},{5,9},... | collective-permute-start | bytes 602120 | tf_op jit(solution)/shard_map/out_trail1/ppermute | solution.py:362
  19.3 10.2 %collective-permute-start.12 = (bf16[784,128]{1,0:T(8,128)(2,1)S(1)}, bf16[784,128]{1,0:T(8,128)(2,1)S(1)}, u32[]{:S(2)}, u32[]{:S(2)}) collective-permute-start(bf16[784,128]{1,0:T(8,128)(2,1)S(1)} %get-tuple-element.88.refs_0_), channel_id=1, source_target_pairs={{4,0},{8,4},{12,8},{14,12},{10,14},{6,10},{2,6},{0,2},{5,1},{9,5},... | collective-permute-start | bytes 602120 | tf_op jit(solution)/shard_map/out_trail1/ppermute | solution.py:362
  25.1 8.4 %collective-permute-start.7 = (bf16[784,128]{1,0:T(8,128)(2,1)S(1)}, bf16[784,128]{1,0:T(8,128)(2,1)S(1)}, u32[]{:S(2)}, u32[]{:S(2)}) collective-permute-start(bf16[784,128]{1,0:T(8,128)(2,1)S(1)} %collective-permute-done.5.refs_0_), channel_id=1, source_target_pairs={{0,4},{4,8},{8,12},{12,14},{14,10},{10,6},{6,2},{2,0},{1,5},{5,9},... | collective-permute-start | bytes 602120 | tf_op jit(solution)/shard_map/out_lead2/ppermute | solution.py:362
  26.7 7.3 %collective-permute-start.8 = (bf16[784,128]{1,0:T(8,128)(2,1)S(1)}, bf16[784,128]{1,0:T(8,128)(2,1)S(1)}, u32[]{:S(2)}, u32[]{:S(2)}) collective-permute-start(bf16[784,128]{1,0:T(8,128)(2,1)S(1)} %collective-permute-done.6.refs_1_), channel_id=1, source_target_pairs={{4,0},{8,4},{12,8},{14,12},{10,14},{6,10},{2,6},{0,2},{5,1},{9,5},... | collective-permute-start | bytes 602120 | tf_op jit(solution)/shard_map/out_lead2/ppermute | solution.py:362
  29.4 7.4 %collective-permute-start.13 = (bf16[784,128]{1,0:T(8,128)(2,1)S(1)}, bf16[784,128]{1,0:T(8,128)(2,1)S(1)}, u32[]{:S(2)}, u32[]{:S(2)}) collective-permute-start(bf16[784,128]{1,0:T(8,128)(2,1)S(1)} %collective-permute-done.11.refs_0_), channel_id=1, source_target_pairs={{0,4},{4,8},{8,12},{12,14},{14,10},{10,6},{6,2},{2,0},{1,5},{5,9},... | collective-permute-start | bytes 602120 | tf_op jit(solution)/shard_map/out_trail2/ppermute | solution.py:362
  31.0 7.5 %collective-permute-start.14 = (bf16[784,128]{1,0:T(8,128)(2,1)S(1)}, bf16[784,128]{1,0:T(8,128)(2,1)S(1)}, u32[]{:S(2)}, u32[]{:S(2)}) collective-permute-start(bf16[784,128]{1,0:T(8,128)(2,1)S(1)} %collective-permute-done.12.refs_1_), channel_id=1, source_target_pairs={{4,0},{8,4},{12,8},{14,12},{10,14},{6,10},{2,6},{0,2},{5,1},{9,5},... | collective-permute-start | bytes 602120 | tf_op jit(solution)/shard_map/out_trail2/ppermute | solution.py:362
  34.0 6.6 %collective-permute-start.9 = (bf16[784,128]{1,0:T(8,128)(2,1)S(1)}, bf16[784,128]{1,0:T(8,128)(2,1)S(1)}, u32[]{:S(2)}, u32[]{:S(2)}) collective-permute-start(bf16[784,128]{1,0:T(8,128)(2,1)S(1)} %collective-permute-done.7.refs_0_), channel_id=1, source_target_pairs={{0,4},{4,8},{8,12},{12,14},{14,10},{10,6},{6,2},{2,0},{1,5},{5,9},... | collective-permute-start | bytes 602120 | tf_op jit(solution)/shard_map/out_lead3/ppermute | solution.py:362
  35.6 5.7 %collective-permute-start.10 = (bf16[784,128]{1,0:T(8,128)(2,1)S(1)}, bf16[784,128]{1,0:T(8,128)(2,1)S(1)}, u32[]{:S(2)}, u32[]{:S(2)}) collective-permute-start(bf16[784,128]{1,0:T(8,128)(2,1)S(1)} %collective-permute-done.8.refs_1_), channel_id=1, source_target_pairs={{4,0},{8,4},{12,8},{14,12},{10,14},{6,10},{2,6},{0,2},{5,1},{9,5},... | collective-permute-start | bytes 602120 | tf_op jit(solution)/shard_map/out_lead3/ppermute | solution.py:362
  41.3 6.9 %collective-permute-start.15 = (bf16[784,128]{1,0:T(8,128)(2,1)S(1)}, bf16[784,128]{1,0:T(8,128)(2,1)S(1)}, u32[]{:S(2)}, u32[]{:S(2)}) collective-permute-start(bf16[784,128]{1,0:T(8,128)(2,1)S(1)} %collective-permute-done.9.refs_0_), channel_id=1, source_target_pairs={{0,4},{4,8},{8,12},{12,14},{14,10},{10,6},{6,2},{2,0},{1,5},{5,9},... | collective-permute-start | bytes 602120 | tf_op jit(solution)/shard_map/out_lead4/ppermute | solution.py:362
  42.8 7.6 %collective-permute-start.16 = (bf16[784,128]{1,0:T(8,128)(2,1)S(1)}, bf16[784,128]{1,0:T(8,128)(2,1)S(1)}, u32[]{:S(2)}, u32[]{:S(2)}) collective-permute-start(bf16[784,128]{1,0:T(8,128)(2,1)S(1)} %collective-permute-done.10.refs_1_), channel_id=1, source_target_pairs={{4,0},{8,4},{12,8},{14,12},{10,14},{6,10},{2,6},{0,2},{5,1},{9,5},... | collective-permute-start | bytes 602120 | tf_op jit(solution)/shard_map/out_lead4/ppermute | solution.py:362
  43.4 11.2 %collective-permute-start.19 = (bf16[784,128]{1,0:T(8,128)(2,1)S(1)}, bf16[784,128]{1,0:T(8,128)(2,1)S(1)}, u32[]{:S(2)}, u32[]{:S(2)}) collective-permute-start(bf16[784,128]{1,0:T(8,128)(2,1)S(1)} %collective-permute-done.13.refs_0_), channel_id=1, source_target_pairs={{0,4},{4,8},{8,12},{12,14},{14,10},{10,6},{6,2},{2,0},{1,5},{5,9},... | collective-permute-start | bytes 602120 | tf_op jit(solution)/shard_map/out_trail3/ppermute | solution.py:362
  44.8 11.8 %collective-permute-start.20 = (bf16[784,128]{1,0:T(8,128)(2,1)S(1)}, bf16[784,128]{1,0:T(8,128)(2,1)S(1)}, u32[]{:S(2)}, u32[]{:S(2)}) collective-permute-start(bf16[784,128]{1,0:T(8,128)(2,1)S(1)} %collective-permute-done.14.refs_1_), channel_id=1, source_target_pairs={{4,0},{8,4},{12,8},{14,12},{10,14},{6,10},{2,6},{0,2},{5,1},{9,5},... | collective-permute-start | bytes 602120 | tf_op jit(solution)/shard_map/out_trail3/ppermute | solution.py:362
  52.5 6.6 %collective-permute-start.17 = (bf16[64,1536]{1,0:T(8,128)(2,1)S(1)}, bf16[64,1536]{1,0:T(8,128)(2,1)S(1)}, u32[]{:S(2)}, u32[]{:S(2)}) collective-permute-start(bf16[64,1536]{1,0:T(8,128)(2,1)S(1)} %get-tuple-element.110), channel_id=1, source_target_pairs={{0,4},{4,8},{8,12},{12,14},{14,10},{10,6},{6,2},{2,0},{1,5},{5,9},... | collective-permute-start | bytes 589832 | tf_op jit(solution)/shard_map/back_lead4/ppermute | solution.py:401
  54.2 7.7 %collective-permute-start.18 = (bf16[64,1536]{1,0:T(8,128)(2,1)S(1)}, bf16[64,1536]{1,0:T(8,128)(2,1)S(1)}, u32[]{:S(2)}, u32[]{:S(2)}) collective-permute-start(bf16[64,1536]{1,0:T(8,128)(2,1)S(1)} %get-tuple-element.111), channel_id=1, source_target_pairs={{4,0},{8,4},{12,8},{14,12},{10,14},{6,10},{2,6},{0,2},{5,1},{9,5},... | collective-permute-start | bytes 589832 | tf_op jit(solution)/shard_map/back_lead4/ppermute | solution.py:401
  54.5 11.7 %collective-permute-start.27 = (bf16[64,1536]{1,0:T(8,128)(2,1)S(1)}, bf16[64,1536]{1,0:T(8,128)(2,1)S(1)}, u32[]{:S(2)}, u32[]{:S(2)}) collective-permute-start(bf16[64,1536]{1,0:T(8,128)(2,1)S(1)} %get-tuple-element.129), channel_id=1, source_target_pairs={{4,0},{8,4},{12,8},{14,12},{10,14},{6,10},{2,6},{0,2},{5,1},{9,5},... | collective-permute-start | bytes 589832 | tf_op jit(solution)/shard_map/back_trail3/ppermute | solution.py:401
  54.6 11.6 %collective-permute-start.26 = (bf16[64,1536]{1,0:T(8,128)(2,1)S(1)}, bf16[64,1536]{1,0:T(8,128)(2,1)S(1)}, u32[]{:S(2)}, u32[]{:S(2)}) collective-permute-start(bf16[64,1536]{1,0:T(8,128)(2,1)S(1)} %get-tuple-element.128), channel_id=1, source_target_pairs={{0,4},{4,8},{8,12},{12,14},{14,10},{10,6},{6,2},{2,0},{1,5},{5,9},... | collective-permute-start | bytes 589832 | tf_op jit(solution)/shard_map/back_trail3/ppermute | solution.py:401
  62.0 8.5 %collective-permute-start.22 = (bf16[64,1536]{1,0:T(8,128)(2,1)S(1)}, bf16[64,1536]{1,0:T(8,128)(2,1)S(1)}, u32[]{:S(2)}, u32[]{:S(2)}) collective-permute-start(bf16[64,1536]{1,0:T(8,128)(2,1)S(1)} %add_convert_fusion.8), channel_id=1, source_target_pairs={{4,0},{8,4},{12,8},{14,12},{10,14},{6,10},{2,6},{0,2},{5,1},{9,5},... | collective-permute-start | bytes 589832 | tf_op jit(solution)/shard_map/back_lead3/ppermute | solution.py:401
  62.4 8.1 %collective-permute-start.21 = (bf16[64,1536]{1,0:T(8,128)(2,1)S(1)}, bf16[64,1536]{1,0:T(8,128)(2,1)S(1)}, u32[]{:S(2)}, u32[]{:S(2)}) collective-permute-start(bf16[64,1536]{1,0:T(8,128)(2,1)S(1)} %add_convert_fusion.9), channel_id=1, source_target_pairs={{0,4},{4,8},{8,12},{12,14},{14,10},{10,6},{6,2},{2,0},{1,5},{5,9},... | collective-permute-start | bytes 589832 | tf_op jit(solution)/shard_map/back_lead3/ppermute | solution.py:401
  66.3 7.7 %collective-permute-start.29 = (bf16[64,1536]{1,0:T(8,128)(2,1)S(1)}, bf16[64,1536]{1,0:T(8,128)(2,1)S(1)}, u32[]{:S(2)}, u32[]{:S(2)}) collective-permute-start(bf16[64,1536]{1,0:T(8,128)(2,1)S(1)} %add_convert_fusion.3), channel_id=1, source_target_pairs={{4,0},{8,4},{12,8},{14,12},{10,14},{6,10},{2,6},{0,2},{5,1},{9,5},... | collective-permute-start | bytes 589832 | tf_op jit(solution)/shard_map/back_trail2/ppermute | solution.py:401
  66.6 7.3 %collective-permute-start.28 = (bf16[64,1536]{1,0:T(8,128)(2,1)S(1)}, bf16[64,1536]{1,0:T(8,128)(2,1)S(1)}, u32[]{:S(2)}, u32[]{:S(2)}) collective-permute-start(bf16[64,1536]{1,0:T(8,128)(2,1)S(1)} %add_convert_fusion.4), channel_id=1, source_target_pairs={{0,4},{4,8},{8,12},{12,14},{14,10},{10,6},{6,2},{2,0},{1,5},{5,9},... | collective-permute-start | bytes 589832 | tf_op jit(solution)/shard_map/back_trail2/ppermute | solution.py:401
  70.6 7.7 %collective-permute-start.24 = (bf16[64,1536]{1,0:T(8,128)(2,1)S(1)}, bf16[64,1536]{1,0:T(8,128)(2,1)S(1)}, u32[]{:S(2)}, u32[]{:S(2)}) collective-permute-start(bf16[64,1536]{1,0:T(8,128)(2,1)S(1)} %add_convert_fusion.6), channel_id=1, source_target_pairs={{4,0},{8,4},{12,8},{14,12},{10,14},{6,10},{2,6},{0,2},{5,1},{9,5},... | collective-permute-start | bytes 589832 | tf_op jit(solution)/shard_map/back_lead2/ppermute | solution.py:401
  71.0 7.3 %collective-permute-start.23 = (bf16[64,1536]{1,0:T(8,128)(2,1)S(1)}, bf16[64,1536]{1,0:T(8,128)(2,1)S(1)}, u32[]{:S(2)}, u32[]{:S(2)}) collective-permute-start(bf16[64,1536]{1,0:T(8,128)(2,1)S(1)} %add_convert_fusion.7), channel_id=1, source_target_pairs={{0,4},{4,8},{8,12},{12,14},{14,10},{10,6},{6,2},{2,0},{1,5},{5,9},... | collective-permute-start | bytes 589832 | tf_op jit(solution)/shard_map/back_lead2/ppermute | solution.py:401
  74.0 6.5 %collective-permute-start.30 = (bf16[64,1536]{1,0:T(8,128)(2,1)S(1)}, bf16[64,1536]{1,0:T(8,128)(2,1)S(1)}, u32[]{:S(2)}, u32[]{:S(2)}) collective-permute-start(bf16[64,1536]{1,0:T(8,128)(2,1)S(1)} %add_convert_fusion.2), channel_id=1, source_target_pairs={{4,0},{8,4},{12,8},{14,12},{10,14},{6,10},{2,6},{0,2},{5,1},{9,5},... | collective-permute-start | bytes 589832 | tf_op jit(solution)/shard_map/back_trail1/ppermute | solution.py:401
  74.7 9.5 %collective-permute-start.31 = (bf16[64,1536]{1,0:T(8,128)(2,1)S(1)}, bf16[64,1536]{1,0:T(8,128)(2,1)S(1)}, u32[]{:S(2)}, u32[]{:S(2)}) collective-permute-start(bf16[64,1536]{1,0:T(8,128)(2,1)S(1)} %add_convert_fusion.1), channel_id=1, source_target_pairs={{0,4},{4,8},{8,12},{12,14},{14,10},{10,6},{6,2},{2,0},{1,5},{5,9},... | collective-permute-start | bytes 589832 | tf_op jit(solution)/shard_map/back_trail1/ppermute | solution.py:401
  78.4 5.7 %collective-permute-start.25 = (bf16[64,1536]{1,0:T(8,128)(2,1)S(1)}, bf16[64,1536]{1,0:T(8,128)(2,1)S(1)}, u32[]{:S(2)}, u32[]{:S(2)}) collective-permute-start(bf16[64,1536]{1,0:T(8,128)(2,1)S(1)} %add_convert_fusion.5), channel_id=1, source_target_pairs={{0,4},{4,8},{8,12},{12,14},{14,10},{10,6},{6,2},{2,0},{1,5},{5,9},... | collective-permute-start | bytes 589832 | tf_op jit(solution)/shard_map/back_lead1/ppermute | solution.py:401
  79.5 5.7 %collective-permute-start.32 = (bf16[64,1536]{1,0:T(8,128)(2,1)S(1)}, bf16[64,1536]{1,0:T(8,128)(2,1)S(1)}, u32[]{:S(2)}, u32[]{:S(2)}) collective-permute-start(bf16[64,1536]{1,0:T(8,128)(2,1)S(1)} %add_convert_fusion), channel_id=1, source_target_pairs={{4,0},{8,4},{12,8},{14,12},{10,14},{6,10},{2,6},{0,2},{5,1},{9,5},... | collective-permute-start | bytes 589832 | tf_op jit(solution)/shard_map/back_lead1/ppermute | solution.py:401

commit v10 on v9

--- a/solution.py
+++ b/solution.py
@@ -21,8 +21,7 @@
 
 def shifted(value, axis, by):
     peers = lax.axis_size(axis)
-    pairs = [(i, i + by) for i in range(peers) if 0 <= i + by < peers]
-    return lax.ppermute(value, axis, pairs)
+    return lax.ppermute(value, axis, [(i, (i + by) % peers) for i in range(peers)])
 
 
 def pinned(values, space):
@@ -42,40 +41,14 @@
     return jnp.dot(a, b, preferred_element_type=jnp.float32)
 
 
-def tail_kernel(keys_hbm, values_hbm, out_ref, sems):
-    rows, width = out_ref.shape
-    last = pl.ds(keys_hbm.shape[0] - rows, rows)
-    copies = [
-        pltpu.make_async_copy(
-            ref.at[last], out_ref.at[:, pl.ds(index * width // 2, width // 2)], sems.at[index]
-        )
-        for index, ref in enumerate((keys_hbm, values_hbm))
-    ]
-    for copy in copies:
-        copy.start()
-    for copy in copies:
-        copy.wait()
-
-
-def tail(keys, values):
-    return pl.pallas_call(
-        tail_kernel,
-        in_specs=[pl.BlockSpec(memory_space=pltpu.HBM)] * 2,
-        out_specs=pl.BlockSpec(memory_space=pltpu.VMEM),
-        out_shape=jax.ShapeDtypeStruct((WINDOW, 2 * keys.shape[1]), keys.dtype),
-        scratch_shapes=[pltpu.SemaphoreType.DMA((2,))],
-        name="tail",
-    )(*pinned((keys, values), pltpu.HBM))
-
-
 def attend_kernel(mix, *refs):
     if mix:
         sink_ref, q_ref, k_ref, v_ref, ow_ref = refs[:5]
-        first_ref, before_ref, rank_ref, later_ref, send_ref, own_ref, done_ref = refs[5:]
-        rows, width = before_ref.shape[0], k_ref.shape[1]
+        first_ref, k_before, v_before, rank_ref, later_ref, send_ref, own_ref, done_ref = refs[5:]
+        rows = later_ref.shape[0]
         queries = slice(0, rows)
-        k = jnp.concatenate([before_ref[:, :width], k_ref[:rows]], axis=0)
-        v = jnp.concatenate([before_ref[:, width:], v_ref[:rows]], axis=0)
+        k = jnp.concatenate([k_before[rows:], k_ref[:rows]], axis=0)
+        v = jnp.concatenate([v_before[rows:], v_ref[:rows]], axis=0)
         done_ref[rows:] = later_ref[...]
         copies = []
     else:
@@ -177,7 +150,7 @@
         shapes += (jax.ShapeDtypeStruct((rows, width), jnp.bfloat16),)
     return pl.pallas_call(
         functools.partial(attend_kernel, mix),
-        in_specs=[vmem if mix else hbm] * 5 + ([smem, vmem, smem, vmem] if mix else []),
+        in_specs=[vmem if mix else hbm] * 5 + ([smem, vmem, vmem, smem, vmem] if mix else []),
         out_specs=(vmem,) * len(shapes),
         out_shape=shapes,
         scratch_shapes=[
@@ -356,10 +329,14 @@
 
     def bring(distance, lead, *after):
         keys = [(side, distance - 1, side if lead else 1 - side) for side in sides]
-        met = lax.optimization_barrier((*(came[key] for key in keys), *after))
+        met = lax.optimization_barrier(tuple(came[key] for key in keys))
         for (side, _, piece), block in zip(keys, met):
+            block = tied(block, *after)
             with jax.named_scope(f"out_{'lead' if lead else 'trail'}{distance}"):
                 came[side, distance, piece] = lax.ppermute(block, "seq", hops[side])
+
+    def both(value):
+        return swapped(value[:16, :LANES], "rep")
 
     def apply(distance, kinds, *after):
         keys = [(side, distance, side if lead else 1 - side) for lead in kinds for side in sides]
@@ -373,7 +350,10 @@
         return outs[0]
 
     for distance in range(1, far + 1):
-        bring(distance, True, *([worked[distance - 2]] if distance > 1 else []))
+        hold = [worked[distance - 2]] if distance > 1 else []
+        if distance == far:
+            hold.append(both(hold[0]))
+        bring(distance, True, *hold)
         trails = []
         if distance < far:
             before = [came[side, distance - 1, side] for side in sides] if distance > 1 else []
@@ -400,7 +380,7 @@
             with jax.named_scope(f"back_{'lead' if lead else 'trail'}{distance}"):
                 moving[side, piece] = lax.ppermute(value, "seq", hops[side])
 
-    send(far, True)
+    send(far, True, both(worked[far - 1]))
     send(far - 1, False, *[came[side, far, side] for side in sides])
     for distance in range(far - 1, 0, -1):
         leads = [moving[side, side] for side in sides]
@@ -477,7 +457,7 @@
     gate_weight, up_weight, down_weight = gate_weight[0], up_weight[0], down_weight[0]
     use_ring = EXP_DEV * lax.axis_size("seq") <= 2 * TOP
 
-    before = shifted(tail(key_rows, value_rows), "seq", 1)
+    before = shifted(key_rows, "seq", 1), shifted(value_rows, "seq", 1)
     others = []
     if use_ring:
         others = [swapped(w, "rep") for w in (gate_weight, up_weight, down_weight)]
@@ -485,7 +465,7 @@
     *operands, later_half = attend(
         sink_logits.reshape(1, -1), queries, key_rows, value_rows, out_weight
     )
-    send, own = attend(*operands, (first, before, rank, later_half))
+    send, own = attend(*operands, (first, *before, rank, later_half))
     came = swapped(send, "rep")
     expert_count = lax.axis_size("seq") * EXP_DEV if use_ring else 0
     residual, *pieces = norm(

time: 86.3 us -> 85.5 us (level)
  waiting for transfers between devices: 23.1 us -> 24.6 us
  Pallas kernels: 26 us -> 24.6 us
  starting transfers between devices: 35.2 us -> 34.3 us
    ppermute x1 -> x2, waiting for transfers between devices: 0.01 us -> 2.81 us  [shifted(): lax.ppermute(value, axis, [(i, (i + by) % peers) for i in range(peers)])]
    ppermute x14, waiting for transfers between devices: 10.5 us -> 8.91 us  [bring(): came[side, distance, piece] = lax.ppermute(block, 'seq', hops[side])]
    pallas_call x1 -> x0, Pallas kernels: 1.42 us -> none  [tail(): pl.pallas_call(tail_kernel, in_specs=[pl.BlockSpec(memory_space=pltpu.HBM...]
    ppermute x4 -> x6, waiting for transfers between devices: 1.5 us -> 2.12 us  [swapped(): return lax.ppermute(value, axis, [(i, i ^ bit) for i in range(peers)])]
    ppermute x1 -> x2, starting transfers between devices: 4.4 us -> 4.04 us  [shifted(): lax.ppermute(value, axis, [(i, (i + by) % peers) for i in range(peers)])]
  transfers between devices with their start and end apart: 33 -> 36, of which waited for: 15 -> 19; matrix products, arithmetic and copies ran while one was open for 1% -> 1% of each run, Pallas kernels for 30% -> 29%
where the time goes in v10:
time: 85.5 us; the launch traced here: 85.3 us
  starting transfers between devices  34.3 us (40%)
  Pallas kernels  24.6 us (29%)
  waiting for transfers between devices  24.6 us (29%)
  other arithmetic  1.46 us (2%)
    pallas_call x8, Pallas kernels, experts(): pl.pallas_call(functools.partial(expert_kernel, min(256, half), len(block...  18.8 us
    ppermute x14, starting transfers between devices, send(): moving[side, piece] = lax.ppermute(value, 'seq', hops[side])  14.8 us
    ppermute x14, starting transfers between devices, bring(): came[side, distance, piece] = lax.ppermute(block, 'seq', hops[side])  14.3 us
    ppermute x14, waiting for transfers between devices, send(): moving[side, piece] = lax.ppermute(value, 'seq', hops[side])  10.7 us
    ppermute x14, waiting for transfers between devices, bring(): came[side, distance, piece] = lax.ppermute(block, 'seq', hops[side])  8.91 us
    pallas_call x2, Pallas kernels, attend(): pl.pallas_call(functools.partial(attend_kernel, mix), in_specs=[vmem if m...  5.54 us
    ppermute x2, starting transfers between devices, shifted(): lax.ppermute(value, axis, [(i, (i + by) % peers) for i in range(peers)])  4.04 us
    ppermute x2, waiting for transfers between devices, shifted(): lax.ppermute(value, axis, [(i, (i + by) % peers) for i in range(peers)])  2.81 us
  transfers between devices with their start and end apart: 36, of which 19 were waited for; matrix products, arithmetic and copies ran while one was open for 1% of the time, Pallas kernels for 29%

profile of v10, /device:TPU:0, one launch (start us, length us, event | category | flops | bytes accessed | tf_op | source)
XLA Modules:
  0.0 85.3 jit_solution(14166201979349769256)
XLA Ops:
  1.0 2.5 %collective-permute-start = (bf16[256,128]{1,0:T(8,128)(2,1)}, bf16[256,128]{1,0:T(8,128)(2,1)S(1)}, u32[]{:S(2)}, u32[]{:S(2)}) collective-permute-start(bf16[256,128]{1,0:T(8,128)(2,1)} %refs_2_.1), channel_id=1, source_target_pairs={{0,2},{2,4},{4,6},{6,8},{8,10},{10,12},{12,14},{14,0},{1,3},{3,5},... | collective-permute-start | bytes 196616 | tf_op jit(solution)/shard_map/ppermute | solution.py:24
  3.5 1.5 %collective-permute-start.1 = (bf16[256,128]{1,0:T(8,128)(2,1)}, bf16[256,128]{1,0:T(8,128)(2,1)S(1)}, u32[]{:S(2)}, u32[]{:S(2)}) collective-permute-start(bf16[256,128]{1,0:T(8,128)(2,1)} %refs_3_.1), channel_id=1, source_target_pairs={{0,2},{2,4},{4,6},{6,8},{8,10},{10,12},{12,14},{14,0},{1,3},{3,5},... | collective-permute-start | bytes 196616 | tf_op jit(solution)/shard_map/ppermute | solution.py:24
  5.0 3.0 %attend.2 = (f32[1,16]{1,0:T(1,128)S(1)}, bf16[256,1024]{1,0:T(8,128)(2,1)S(1)}, bf16[256,128]{1,0:T(8,128)(2,1)S(1)}, bf16[256,128]{1,0:T(8,128)(2,1)S(1)}, bf1...) custom-call(f32[1,16]{1,0:T(1,128)} %bitcast.38, bf16[256,1024]{1,0:T(8,128)(2,1)} %refs_1_.1, ...), custom_call_target="tpu_custom_call" | custom-call | flops 671088640 | bytes 6291456 | tf_op jit(solution)/shard_map/attend/pallas_call | solution.py:151
  8.1 1.6 %collective-permute-done.refs_6_ = bf16[256,128]{1,0:T(8,128)(2,1)S(1)} collective-permute-done((bf16[256,128]{1,0:T(8,128)(2,1)}, bf16[256,128]{1,0:T(8,128)(2,1)S(1)}, u32[]{:S(2)}, u32[]{:S(2)}) %collective-permute-start) | collective-permute-done | bytes 65568 | tf_op jit(solution)/shard_map/ppermute | solution.py:24
  9.6 1.2 %collective-permute-done.1.refs_7_ = bf16[256,128]{1,0:T(8,128)(2,1)S(1)} collective-permute-done((bf16[256,128]{1,0:T(8,128)(2,1)}, bf16[256,128]{1,0:T(8,128)(2,1)S(1)}, u32[]{:S(2)}, u32[]{:S(2)}) %collective-permute-start.1) | collective-permute-done | bytes 65568 | tf_op jit(solution)/shard_map/ppermute | solution.py:24
  10.9 2.5 %attend.3 = (bf16[128,1536]{1,0:T(8,128)(2,1)S(1)}, f32[128,1536]{1,0:T(8,128)S(1)}) custom-call(f32[1,16]{1,0:T(1,128)S(1)} %get-tuple-element.86.refs_0_, bf16[256,1024]{1,0:T(8,128)(2,1)S(1)} %get-tuple-element.87.refs_1_, bf16[256,128]{1,0:T(8,128)(2,1)S(1)} %get-tuple-element.88.refs_2_, bf16[256,128]{1,0:T(8,128)(2,1)S(1)} %get-tuple-element.89.refs_3_, ...), custom_call_target="tpu_custom_call" | custom-call | flops 671088640 | bytes 6291456 | tf_op jit(solution)/shard_map/attend/pallas_call | solution.py:151
  13.5 1.7 %collective-permute-done.2.came_ref = bf16[128,1536]{1,0:T(8,128)(2,1)S(1)} collective-permute-done((bf16[128,1536]{1,0:T(8,128)(2,1)S(1)}, bf16[128,1536]{1,0:T(8,128)(2,1)S(1)}, u32[]{:S(2)}, u32[]{:S(2)}) %collective-permute-start.2) | collective-permute-done | bytes 393248 | tf_op jit(solution)/shard_map/ppermute | solution.py:37
  15.6 2.0 %collective-permute-start.7 = (bf16[784,128]{1,0:T(8,128)(2,1)S(1)}, bf16[784,128]{1,0:T(8,128)(2,1)S(1)}, u32[]{:S(2)}, u32[]{:S(2)}) collective-permute-start(bf16[784,128]{1,0:T(8,128)(2,1)S(1)} %get-tuple-element.101.refs_1_), channel_id=1, source_target_pairs={{4,0},{8,4},{12,8},{14,12},{10,14},{6,10},{2,6},{0,2},{5,1},{9,5},... | collective-permute-start | bytes 602120 | tf_op jit(solution)/shard_map/out_lead1/ppermute | solution.py:336
  17.7 2.0 %collective-permute-start.13 = (bf16[784,128]{1,0:T(8,128)(2,1)S(1)}, bf16[784,128]{1,0:T(8,128)(2,1)S(1)}, u32[]{:S(2)}, u32[]{:S(2)}) collective-permute-start(bf16[784,128]{1,0:T(8,128)(2,1)S(1)} %get-tuple-element.100.refs_0_), channel_id=1, source_target_pairs={{4,0},{8,4},{12,8},{14,12},{10,14},{6,10},{2,6},{0,2},{5,1},{9,5},... | collective-permute-start | bytes 602120 | tf_op jit(solution)/shard_map/out_trail1/ppermute | solution.py:336
  19.7 4.1 %experts.8 = (bf16[64,1536]{1,0:T(8,128)(2,1)S(1)}, bf16[64,1536]{1,0:T(8,128)(2,1)S(1)}, bf16[1536,768]{1,0:T(8,128)(2,1)S(1)}, bf16[1536,768]{1,0:T(8,128)(2,1)S(1)}, bf16[768,1536]{1,0:T(8,128)(2,1)S(1)}) custom-call(s32[1]{0:T(128)} %bitcast.5.me_ref, bf16[784,128]{1,0:T(8,128)(2,1)S(1)} %get-tuple-element.100.refs_0_, ...), custom_call_target="tpu_custom_call" | custom-call | flops 1811939328 | bytes 1179648 | tf_op jit(solution)/shard_map/experts/pallas_call | solution.py:287
  23.8 1.0 %collective-permute-start.8 = (bf16[784,128]{1,0:T(8,128)(2,1)S(1)}, bf16[784,128]{1,0:T(8,128)(2,1)S(1)}, u32[]{:S(2)}, u32[]{:S(2)}) collective-permute-start(bf16[784,128]{1,0:T(8,128)(2,1)S(1)} %collective-permute-done.6.refs_0_), channel_id=1, source_target_pairs={{0,4},{4,8},{8,12},{12,14},{14,10},{10,6},{6,2},{2,0},{1,5},{5,9},... | collective-permute-start | bytes 602120 | tf_op jit(solution)/shard_map/out_lead2/ppermute | solution.py:336
  24.8 1.1 %collective-permute-start.9 = (bf16[784,128]{1,0:T(8,128)(2,1)S(1)}, bf16[784,128]{1,0:T(8,128)(2,1)S(1)}, u32[]{:S(2)}, u32[]{:S(2)}) collective-permute-start(bf16[784,128]{1,0:T(8,128)(2,1)S(1)} %collective-permute-done.7.refs_1_), channel_id=1, source_target_pairs={{4,0},{8,4},{12,8},{14,12},{10,14},{6,10},{2,6},{0,2},{5,1},{9,5},... | collective-permute-start | bytes 602120 | tf_op jit(solution)/shard_map/out_lead2/ppermute | solution.py:336
  25.9 1.9 %collective-permute-done.12.refs_0_ = bf16[784,128]{1,0:T(8,128)(2,1)S(1)} collective-permute-done((bf16[784,128]{1,0:T(8,128)(2,1)S(1)}, bf16[784,128]{1,0:T(8,128)(2,1)S(1)}, u32[]{:S(2)}, u32[]{:S(2)}) %collective-permute-start.12) | collective-permute-done | bytes 200736 | tf_op jit(solution)/shard_map/out_trail1/ppermute | solution.py:336
  27.8 2.0 %collective-permute-start.15 = (bf16[784,128]{1,0:T(8,128)(2,1)S(1)}, bf16[784,128]{1,0:T(8,128)(2,1)S(1)}, u32[]{:S(2)}, u32[]{:S(2)}) collective-permute-start(bf16[784,128]{1,0:T(8,128)(2,1)S(1)} %collective-permute-done.13.refs_1_), channel_id=1, source_target_pairs={{4,0},{8,4},{12,8},{14,12},{10,14},{6,10},{2,6},{0,2},{5,1},{9,5},... | collective-permute-start | bytes 602120 | tf_op jit(solution)/shard_map/out_trail2/ppermute | solution.py:336
  29.9 2.1 %experts.9 = (bf16[64,1536]{1,0:T(8,128)(2,1)S(1)}, bf16[64,1536]{1,0:T(8,128)(2,1)S(1)}) custom-call(s32[1]{0:T(128)} %bitcast.5.me_ref, bf16[784,128]{1,0:T(8,128)(2,1)S(1)} %collective-permute-done.6.refs_0_, bf16[784,128]{1,0:T(8,128)(2,1)S(1)} %collective-permute-done.7.refs_1_, bf16[1536,768]{1,0:T(8,128)(2,1)S(1)} %bitcast.11, ...), custom_call_target="tpu_custom_call" | custom-call | flops 1811939328 | bytes 1179648 | tf_op jit(solution)/shard_map/hop1/experts/pallas_call | solution.py:287
  32.1 0.6 collective-permute-done.9.refs_1_
  32.7 1.4 %collective-permute-start.11 = (bf16[784,128]{1,0:T(8,128)(2,1)S(1)}, bf16[784,128]{1,0:T(8,128)(2,1)S(1)}, u32[]{:S(2)}, u32[]{:S(2)}) collective-permute-start(bf16[784,128]{1,0:T(8,128)(2,1)S(1)} %collective-permute-done.9.refs_1_), channel_id=1, source_target_pairs={{4,0},{8,4},{12,8},{14,12},{10,14},{6,10},{2,6},{0,2},{5,1},{9,5},... | collective-permute-start | bytes 602120 | tf_op jit(solution)/shard_map/out_lead3/ppermute | solution.py:336
  34.1 0.6 collective-permute-start.10
  34.7 2.3 %collective-permute-done.15.refs_1_ = bf16[784,128]{1,0:T(8,128)(2,1)S(1)} collective-permute-done((bf16[784,128]{1,0:T(8,128)(2,1)S(1)}, bf16[784,128]{1,0:T(8,128)(2,1)S(1)}, u32[]{:S(2)}, u32[]{:S(2)}) %collective-permute-start.15) | collective-permute-done | bytes 200736 | tf_op jit(solution)/shard_map/out_trail2/ppermute | solution.py:336
  37.0 2.1 %experts.10 = (bf16[64,1536]{1,0:T(8,128)(2,1)S(1)}, bf16[64,1536]{1,0:T(8,128)(2,1)S(1)}) custom-call(s32[1]{0:T(128)} %bitcast.5.me_ref, bf16[784,128]{1,0:T(8,128)(2,1)S(1)} %collective-permute-done.8.refs_0_, bf16[784,128]{1,0:T(8,128)(2,1)S(1)} %collective-permute-done.9.refs_1_, bf16[1536,768]{1,0:T(8,128)(2,1)S(1)} %bitcast.12, ...), custom_call_target="tpu_custom_call" | custom-call | flops 1811939328 | bytes 1179648 | tf_op jit(solution)/shard_map/hop2/experts/pallas_call | solution.py:287
  39.2 0.7 collective-permute-done.11.refs_1_
  40.4 1.6 %collective-permute-start.17 = (bf16[784,128]{1,0:T(8,128)(2,1)S(1)}, bf16[784,128]{1,0:T(8,128)(2,1)S(1)}, u32[]{:S(2)}, u32[]{:S(2)}) collective-permute-start(bf16[784,128]{1,0:T(8,128)(2,1)S(1)} %collective-permute-done.10.refs_0_), channel_id=1, source_target_pairs={{0,4},{4,8},{8,12},{12,14},{14,10},{10,6},{6,2},{2,0},{1,5},{5,9},... | collective-permute-start | bytes 602120 | tf_op jit(solution)/shard_map/out_lead4/ppermute | solution.py:336
  42.4 1.4 %collective-permute-start.23 = (bf16[784,128]{1,0:T(8,128)(2,1)S(1)}, bf16[784,128]{1,0:T(8,128)(2,1)S(1)}, u32[]{:S(2)}, u32[]{:S(2)}) collective-permute-start(bf16[784,128]{1,0:T(8,128)(2,1)S(1)} %collective-permute-done.15.refs_1_), channel_id=1, source_target_pairs={{4,0},{8,4},{12,8},{14,12},{10,14},{6,10},{2,6},{0,2},{5,1},{9,5},... | collective-permute-start | bytes 602120 | tf_op jit(solution)/shard_map/out_trail3/ppermute | solution.py:336
  43.8 0.6 collective-permute-start.22
  44.4 2.1 %experts.11 = (bf16[64,1536]{1,0:T(8,128)(2,1)S(1)}, bf16[64,1536]{1,0:T(8,128)(2,1)S(1)}) custom-call(s32[1]{0:T(128)} %bitcast.5.me_ref, bf16[784,128]{1,0:T(8,128)(2,1)S(1)} %collective-permute-done.10.refs_0_, bf16[784,128]{1,0:T(8,128)(2,1)S(1)} %collective-permute-done.11.refs_1_, bf16[1536,768]{1,0:T(8,128)(2,1)S(1)} %bitcast.13, ...), custom_call_target="tpu_custom_call" | custom-call | flops 1811939328 | bytes 1179648 | tf_op jit(solution)/shard_map/hop3/experts/pallas_call | solution.py:287
  46.6 1.6 %collective-permute-done.17.refs_0_ = bf16[784,128]{1,0:T(8,128)(2,1)S(1)} collective-permute-done((bf16[784,128]{1,0:T(8,128)(2,1)S(1)}, bf16[784,128]{1,0:T(8,128)(2,1)S(1)}, u32[]{:S(2)}, u32[]{:S(2)}) %collective-permute-start.17) | collective-permute-done | bytes 200736 | tf_op jit(solution)/shard_map/out_lead4/ppermute | solution.py:336
  48.2 1.6 %collective-permute-done.18.refs_1_ = bf16[784,128]{1,0:T(8,128)(2,1)S(1)} collective-permute-done((bf16[784,128]{1,0:T(8,128)(2,1)S(1)}, bf16[784,128]{1,0:T(8,128)(2,1)S(1)}, u32[]{:S(2)}, u32[]{:S(2)}) %collective-permute-start.18) | collective-permute-done | bytes 200736 | tf_op jit(solution)/shard_map/out_lead4/ppermute | solution.py:336
  49.8 2.1 %experts.12 = (bf16[64,1536]{1,0:T(8,128)(2,1)S(1)}, bf16[64,1536]{1,0:T(8,128)(2,1)S(1)}) custom-call(s32[1]{0:T(128)} %bitcast.5.me_ref, bf16[784,128]{1,0:T(8,128)(2,1)S(1)} %collective-permute-done.17.refs_0_, bf16[784,128]{1,0:T(8,128)(2,1)S(1)} %collective-permute-done.18.refs_1_, bf16[1536,768]{1,0:T(8,128)(2,1)S(1)} %bitcast.14, ...), custom_call_target="tpu_custom_call" | custom-call | flops 1811939328 | bytes 1179648 | tf_op jit(solution)/shard_map/hop4/experts/pallas_call | solution.py:287
  52.4 1.6 %collective-permute-start.20 = (bf16[64,1536]{1,0:T(8,128)(2,1)S(1)}, bf16[64,1536]{1,0:T(8,128)(2,1)S(1)}, u32[]{:S(2)}, u32[]{:S(2)}) collective-permute-start(bf16[64,1536]{1,0:T(8,128)(2,1)S(1)} %get-tuple-element.131), channel_id=1, source_target_pairs={{0,4},{4,8},{8,12},{12,14},{14,10},{10,6},{6,2},{2,0},{1,5},{5,9},... | collective-permute-start | bytes 589832 | tf_op jit(solution)/shard_map/back_lead4/ppermute | solution.py:381
  54.5 1.6 %collective-permute-start.29 = (bf16[64,1536]{1,0:T(8,128)(2,1)S(1)}, bf16[64,1536]{1,0:T(8,128)(2,1)S(1)}, u32[]{:S(2)}, u32[]{:S(2)}) collective-permute-start(bf16[64,1536]{1,0:T(8,128)(2,1)S(1)} %get-tuple-element.152), channel_id=1, source_target_pairs={{0,4},{4,8},{8,12},{12,14},{14,10},{10,6},{6,2},{2,0},{1,5},{5,9},... | collective-permute-start | bytes 589832 | tf_op jit(solution)/shard_map/back_trail3/ppermute | solution.py:381
  56.0 2.1 %experts.13 = (bf16[64,1536]{1,0:T(8,128)(2,1)S(1)}, bf16[64,1536]{1,0:T(8,128)(2,1)S(1)}) custom-call(s32[1]{0:T(128)} %bitcast.5.me_ref, bf16[784,128]{1,0:T(8,128)(2,1)S(1)} %collective-permute-done.22.refs_0_, bf16[784,128]{1,0:T(8,128)(2,1)S(1)} %collective-permute-done.23.refs_1_, bf16[1536,768]{1,0:T(8,128)(2,1)S(1)} %bitcast.15, ...), custom_call_target="tpu_custom_call" | custom-call | flops 1811939328 | bytes 1179648 | tf_op jit(solution)/shard_map/hop3/experts/pallas_call | solution.py:287
  58.1 1.7 %collective-permute-done.21 = bf16[64,1536]{1,0:T(8,128)(2,1)S(1)} collective-permute-done((bf16[64,1536]{1,0:T(8,128)(2,1)S(1)}, bf16[64,1536]{1,0:T(8,128)(2,1)S(1)}, u32[]{:S(2)}, u32[]{:S(2)}) %collective-permute-start.21) | collective-permute-done | bytes 196640 | tf_op jit(solution)/shard_map/back_lead4/ppermute | solution.py:381
  59.9 1.3 %collective-permute-start.25 = (bf16[64,1536]{1,0:T(8,128)(2,1)S(1)}, bf16[64,1536]{1,0:T(8,128)(2,1)S(1)}, u32[]{:S(2)}, u32[]{:S(2)}) collective-permute-start(bf16[64,1536]{1,0:T(8,128)(2,1)S(1)} %add_convert_fusion.8), channel_id=1, source_target_pairs={{4,0},{8,4},{12,8},{14,12},{10,14},{6,10},{2,6},{0,2},{5,1},{9,5},... | collective-permute-start | bytes 589832 | tf_op jit(solution)/shard_map/back_lead3/ppermute | solution.py:381
  61.2 0.8 collective-permute-start.24
  62.1 2.0 %collective-permute-done.30 = bf16[64,1536]{1,0:T(8,128)(2,1)S(1)} collective-permute-done((bf16[64,1536]{1,0:T(8,128)(2,1)S(1)}, bf16[64,1536]{1,0:T(8,128)(2,1)S(1)}, u32[]{:S(2)}, u32[]{:S(2)}) %collective-permute-start.30) | collective-permute-done | bytes 196640 | tf_op jit(solution)/shard_map/back_trail3/ppermute | solution.py:381
  64.1 1.3 %collective-permute-start.32 = (bf16[64,1536]{1,0:T(8,128)(2,1)S(1)}, bf16[64,1536]{1,0:T(8,128)(2,1)S(1)}, u32[]{:S(2)}, u32[]{:S(2)}) collective-permute-start(bf16[64,1536]{1,0:T(8,128)(2,1)S(1)} %add_convert_fusion.3), channel_id=1, source_target_pairs={{4,0},{8,4},{12,8},{14,12},{10,14},{6,10},{2,6},{0,2},{5,1},{9,5},... | collective-permute-start | bytes 589832 | tf_op jit(solution)/shard_map/back_trail2/ppermute | solution.py:381
  65.4 0.8 collective-permute-start.31
  66.3 2.1 %experts.14 = (bf16[64,1536]{1,0:T(8,128)(2,1)S(1)}, bf16[64,1536]{1,0:T(8,128)(2,1)S(1)}) custom-call(s32[1]{0:T(128)} %bitcast.5.me_ref, bf16[784,128]{1,0:T(8,128)(2,1)S(1)} %collective-permute-done.14.refs_0_, bf16[784,128]{1,0:T(8,128)(2,1)S(1)} %collective-permute-done.15.refs_1_, bf16[1536,768]{1,0:T(8,128)(2,1)S(1)} %bitcast.16, ...), custom_call_target="tpu_custom_call" | custom-call | flops 1811939328 | bytes 1179648 | tf_op jit(solution)/shard_map/hop2/experts/pallas_call | solution.py:287
  68.5 2.1 %collective-permute-start.27 = (bf16[64,1536]{1,0:T(8,128)(2,1)S(1)}, bf16[64,1536]{1,0:T(8,128)(2,1)S(1)}, u32[]{:S(2)}, u32[]{:S(2)}) collective-permute-start(bf16[64,1536]{1,0:T(8,128)(2,1)S(1)} %add_convert_fusion.6), channel_id=1, source_target_pairs={{4,0},{8,4},{12,8},{14,12},{10,14},{6,10},{2,6},{0,2},{5,1},{9,5},... | collective-permute-start | bytes 589832 | tf_op jit(solution)/shard_map/back_lead2/ppermute | solution.py:381
  70.7 1.7 %collective-permute-done.32 = bf16[64,1536]{1,0:T(8,128)(2,1)S(1)} collective-permute-done((bf16[64,1536]{1,0:T(8,128)(2,1)S(1)}, bf16[64,1536]{1,0:T(8,128)(2,1)S(1)}, u32[]{:S(2)}, u32[]{:S(2)}) %collective-permute-start.32) | collective-permute-done | bytes 196640 | tf_op jit(solution)/shard_map/back_trail2/ppermute | solution.py:381
  72.5 0.9 %collective-permute-done.31 = bf16[64,1536]{1,0:T(8,128)(2,1)S(1)} collective-permute-done((bf16[64,1536]{1,0:T(8,128)(2,1)S(1)}, bf16[64,1536]{1,0:T(8,128)(2,1)S(1)}, u32[]{:S(2)}, u32[]{:S(2)}) %collective-permute-start.31) | collective-permute-done | bytes 196640 | tf_op jit(solution)/shard_map/back_trail2/ppermute | solution.py:381
  73.4 1.5 %collective-permute-start.33 = (bf16[64,1536]{1,0:T(8,128)(2,1)S(1)}, bf16[64,1536]{1,0:T(8,128)(2,1)S(1)}, u32[]{:S(2)}, u32[]{:S(2)}) collective-permute-start(bf16[64,1536]{1,0:T(8,128)(2,1)S(1)} %add_convert_fusion.2), channel_id=1, source_target_pairs={{4,0},{8,4},{12,8},{14,12},{10,14},{6,10},{2,6},{0,2},{5,1},{9,5},... | collective-permute-start | bytes 589832 | tf_op jit(solution)/shard_map/back_trail1/ppermute | solution.py:381
  74.9 0.7 collective-permute-start.34
  75.6 2.1 %experts.15 = (bf16[64,1536]{1,0:T(8,128)(2,1)S(1)}, bf16[64,1536]{1,0:T(8,128)(2,1)S(1)}) custom-call(s32[1]{0:T(128)} %bitcast.5.me_ref, bf16[784,128]{1,0:T(8,128)(2,1)S(1)} %collective-permute-done.12.refs_0_, bf16[784,128]{1,0:T(8,128)(2,1)S(1)} %collective-permute-done.13.refs_1_, bf16[1536,768]{1,0:T(8,128)(2,1)S(1)} %bitcast.17, ...), custom_call_target="tpu_custom_call" | custom-call | flops 1811939328 | bytes 1179648 | tf_op jit(solution)/shard_map/hop1/experts/pallas_call | solution.py:287
  77.7 0.8 collective-permute-done.26
  78.7 2.0 %collective-permute-start.35 = (bf16[64,1536]{1,0:T(8,128)(2,1)S(1)}, bf16[64,1536]{1,0:T(8,128)(2,1)S(1)}, u32[]{:S(2)}, u32[]{:S(2)}) collective-permute-start(bf16[64,1536]{1,0:T(8,128)(2,1)S(1)} %add_convert_fusion), channel_id=1, source_target_pairs={{4,0},{8,4},{12,8},{14,12},{10,14},{6,10},{2,6},{0,2},{5,1},{9,5},... | collective-permute-start | bytes 589832 | tf_op jit(solution)/shard_map/back_lead1/ppermute | solution.py:381
  80.7 3.5 %collective-permute-done.28 = bf16[64,1536]{1,0:T(8,128)(2,1)S(1)} collective-permute-done((bf16[64,1536]{1,0:T(8,128)(2,1)S(1)}, bf16[64,1536]{1,0:T(8,128)(2,1)S(1)}, u32[]{:S(2)}, u32[]{:S(2)}) %collective-permute-start.28) | collective-permute-done | bytes 196640 | tf_op jit(solution)/shard_map/back_lead1/ppermute | solution.py:381
  84.5 0.8 fusion
  (67 shorter events, 4.7 us)
Async XLA Ops:
  0.0 15.5 %collective-permute-start.3 = (bf16[1536,768]{1,0:T(8,128)(2,1)}, bf16[1536,768]{1,0:T(8,128)(2,1)S(1)}, u32[]{:S(2)}, u32[]{:S(2)}) collective-permute-start(bf16[1536,768]{1,0:T(8,128)(2,1)} %bitcast.9), channel_id=1, source_target_pairs={{0,1},{1,0},{2,3},{3,2},{4,5},{5,4},{6,7},{7,6},{8,9},{9,8},{10,11... | collective-permute-start | bytes 7077896 | tf_op jit(solution)/shard_map/ppermute | solution.py:37
  0.5 15.1 %collective-permute-start.4 = (bf16[1536,768]{1,0:T(8,128)(2,1)}, bf16[1536,768]{1,0:T(8,128)(2,1)}, u32[]{:S(2)}, u32[]{:S(2)}) collective-permute-start(bf16[1536,768]{1,0:T(8,128)(2,1)} %bitcast.18), channel_id=1, source_target_pairs={{0,1},{1,0},{2,3},{3,2},{4,5},{5,4},{6,7},{7,6},{8,9},{9,8},{10,11... | collective-permute-start | bytes 7077896 | tf_op jit(solution)/shard_map/ppermute | solution.py:37
  0.5 15.1 %collective-permute-start.5 = (bf16[768,1536]{1,0:T(8,128)(2,1)}, bf16[768,1536]{1,0:T(8,128)(2,1)}, u32[]{:S(2)}, u32[]{:S(2)}) collective-permute-start(bf16[768,1536]{1,0:T(8,128)(2,1)} %bitcast.27), channel_id=1, source_target_pairs={{0,1},{1,0},{2,3},{3,2},{4,5},{5,4},{6,7},{7,6},{8,9},{9,8},{10,11... | collective-permute-start | bytes 7077896 | tf_op jit(solution)/shard_map/ppermute | solution.py:37
  1.0 8.7 %collective-permute-start = (bf16[256,128]{1,0:T(8,128)(2,1)}, bf16[256,128]{1,0:T(8,128)(2,1)S(1)}, u32[]{:S(2)}, u32[]{:S(2)}) collective-permute-start(bf16[256,128]{1,0:T(8,128)(2,1)} %refs_2_.1), channel_id=1, source_target_pairs={{0,2},{2,4},{4,6},{6,8},{8,10},{10,12},{12,14},{14,0},{1,3},{3,5},... | collective-permute-start | bytes 196616 | tf_op jit(solution)/shard_map/ppermute | solution.py:24
  3.5 7.4 %collective-permute-start.1 = (bf16[256,128]{1,0:T(8,128)(2,1)}, bf16[256,128]{1,0:T(8,128)(2,1)S(1)}, u32[]{:S(2)}, u32[]{:S(2)}) collective-permute-start(bf16[256,128]{1,0:T(8,128)(2,1)} %refs_3_.1), channel_id=1, source_target_pairs={{0,2},{2,4},{4,6},{6,8},{8,10},{10,12},{12,14},{14,0},{1,3},{3,5},... | collective-permute-start | bytes 196616 | tf_op jit(solution)/shard_map/ppermute | solution.py:24
  5.0 14.7 %copy-start.2 = (bf16[1,768,1536]{2,1,0:T(8,128)(2,1)S(1)}, bf16[1,768,1536]{2,1,0:T(8,128)(2,1)}, u32[]{:S(2)}) copy-start(bf16[1,768,1536]{2,1,0:T(8,128)(2,1)} %param.23) | copy-start | bytes 7077892
  8.0 5.5 %copy-start.7 = (f32[1536]{0:T(1024)S(1)}, f32[1536]{0:T(1024)}, u32[]{:S(2)}) copy-start(f32[1536]{0:T(1024)} %param.18) | copy-start | bytes 18436
  8.0 7.2 %copy-start.3 = (bf16[128,1536]{1,0:T(8,128)(2,1)S(1)}, bf16[128,1536]{1,0:T(8,128)(2,1)}, u32[]{:S(2)}) copy-start(bf16[128,1536]{1,0:T(8,128)(2,1)} %stream_ref.1) | copy-start | bytes 1179652
  8.0 7.2 %copy-start.4 = (s32[128,4]{0,1:T(4,128)S(1)}, s32[128,4]{0,1:T(4,128)}, u32[]{:S(2)}) copy-start(s32[128,4]{0,1:T(4,128)} %param.19) | copy-start | bytes 6148
  8.0 7.2 %copy-start.5 = (f32[128,4]{0,1:T(4,128)S(1)}, f32[128,4]{0,1:T(4,128)}, u32[]{:S(2)}) copy-start(f32[128,4]{0,1:T(4,128)} %param.20) | copy-start | bytes 6148
  10.9 8.8 %copy-start = (bf16[1,1536,768]{2,1,0:T(8,128)(2,1)S(1)}, bf16[1,1536,768]{2,1,0:T(8,128)(2,1)}, u32[]{:S(2)}) copy-start(bf16[1,1536,768]{2,1,0:T(8,128)(2,1)} %param.21) | copy-start | bytes 7077892
  10.9 8.8 %copy-start.1 = (bf16[1,1536,768]{2,1,0:T(8,128)(2,1)S(1)}, bf16[1,1536,768]{2,1,0:T(8,128)(2,1)}, u32[]{:S(2)}) copy-start(bf16[1,1536,768]{2,1,0:T(8,128)(2,1)} %param.22) | copy-start | bytes 7077892
  13.4 1.8 %collective-permute-start.2 = (bf16[128,1536]{1,0:T(8,128)(2,1)S(1)}, bf16[128,1536]{1,0:T(8,128)(2,1)S(1)}, u32[]{:S(2)}, u32[]{:S(2)}) collective-permute-start(bf16[128,1536]{1,0:T(8,128)(2,1)S(1)} %get-tuple-element.93), channel_id=1, source_target_pairs={{0,1},{1,0},{2,3},{3,2},{4,5},{5,4},{6,7},{7,6},{8,9},{9,8},{10,11... | collective-permute-start | bytes 1179656 | tf_op jit(solution)/shard_map/ppermute | solution.py:37
  15.5 4.1 %copy-start.6 = (bf16[1536,768]{1,0:T(8,128)(2,1)}, bf16[1536,768]{1,0:T(8,128)(2,1)S(1)}, u32[]{:S(2)}) copy-start(bf16[1536,768]{1,0:T(8,128)(2,1)S(1)} %collective-permute-done.3.refs_5_) | copy-start | bytes 7077892
  15.6 8.2 %collective-permute-start.6 = (bf16[784,128]{1,0:T(8,128)(2,1)S(1)}, bf16[784,128]{1,0:T(8,128)(2,1)S(1)}, u32[]{:S(2)}, u32[]{:S(2)}) collective-permute-start(bf16[784,128]{1,0:T(8,128)(2,1)S(1)} %get-tuple-element.100.refs_0_), channel_id=1, source_target_pairs={{0,4},{4,8},{8,12},{12,14},{14,10},{10,6},{6,2},{2,0},{1,5},{5,9},... | collective-permute-start | bytes 602120 | tf_op jit(solution)/shard_map/out_lead1/ppermute | solution.py:336
  15.6 8.2 %collective-permute-start.7 = (bf16[784,128]{1,0:T(8,128)(2,1)S(1)}, bf16[784,128]{1,0:T(8,128)(2,1)S(1)}, u32[]{:S(2)}, u32[]{:S(2)}) collective-permute-start(bf16[784,128]{1,0:T(8,128)(2,1)S(1)} %get-tuple-element.101.refs_1_), channel_id=1, source_target_pairs={{4,0},{8,4},{12,8},{14,12},{10,14},{6,10},{2,6},{0,2},{5,1},{9,5},... | collective-permute-start | bytes 602120 | tf_op jit(solution)/shard_map/out_lead1/ppermute | solution.py:336
  17.7 10.1 %collective-permute-start.12 = (bf16[784,128]{1,0:T(8,128)(2,1)S(1)}, bf16[784,128]{1,0:T(8,128)(2,1)S(1)}, u32[]{:S(2)}, u32[]{:S(2)}) collective-permute-start(bf16[784,128]{1,0:T(8,128)(2,1)S(1)} %get-tuple-element.101.refs_1_), channel_id=1, source_target_pairs={{0,4},{4,8},{8,12},{12,14},{14,10},{10,6},{6,2},{2,0},{1,5},{5,9},... | collective-permute-start | bytes 602120 | tf_op jit(solution)/shard_map/out_trail1/ppermute | solution.py:336
  17.7 10.1 %collective-permute-start.13 = (bf16[784,128]{1,0:T(8,128)(2,1)S(1)}, bf16[784,128]{1,0:T(8,128)(2,1)S(1)}, u32[]{:S(2)}, u32[]{:S(2)}) collective-permute-start(bf16[784,128]{1,0:T(8,128)(2,1)S(1)} %get-tuple-element.100.refs_0_), channel_id=1, source_target_pairs={{4,0},{8,4},{12,8},{14,12},{10,14},{6,10},{2,6},{0,2},{5,1},{9,5},... | collective-permute-start | bytes 602120 | tf_op jit(solution)/shard_map/out_trail1/ppermute | solution.py:336
  23.8 8.3 %collective-permute-start.8 = (bf16[784,128]{1,0:T(8,128)(2,1)S(1)}, bf16[784,128]{1,0:T(8,128)(2,1)S(1)}, u32[]{:S(2)}, u32[]{:S(2)}) collective-permute-start(bf16[784,128]{1,0:T(8,128)(2,1)S(1)} %collective-permute-done.6.refs_0_), channel_id=1, source_target_pairs={{0,4},{4,8},{8,12},{12,14},{14,10},{10,6},{6,2},{2,0},{1,5},{5,9},... | collective-permute-start | bytes 602120 | tf_op jit(solution)/shard_map/out_lead2/ppermute | solution.py:336
  24.8 7.9 %collective-permute-start.9 = (bf16[784,128]{1,0:T(8,128)(2,1)S(1)}, bf16[784,128]{1,0:T(8,128)(2,1)S(1)}, u32[]{:S(2)}, u32[]{:S(2)}) collective-permute-start(bf16[784,128]{1,0:T(8,128)(2,1)S(1)} %collective-permute-done.7.refs_1_), channel_id=1, source_target_pairs={{4,0},{8,4},{12,8},{14,12},{10,14},{6,10},{2,6},{0,2},{5,1},{9,5},... | collective-permute-start | bytes 602120 | tf_op jit(solution)/shard_map/out_lead2/ppermute | solution.py:336
  27.8 9.2 %collective-permute-start.15 = (bf16[784,128]{1,0:T(8,128)(2,1)S(1)}, bf16[784,128]{1,0:T(8,128)(2,1)S(1)}, u32[]{:S(2)}, u32[]{:S(2)}) collective-permute-start(bf16[784,128]{1,0:T(8,128)(2,1)S(1)} %collective-permute-done.13.refs_1_), channel_id=1, source_target_pairs={{4,0},{8,4},{12,8},{14,12},{10,14},{6,10},{2,6},{0,2},{5,1},{9,5},... | collective-permute-start | bytes 602120 | tf_op jit(solution)/shard_map/out_trail2/ppermute | solution.py:336
  29.8 7.2 %collective-permute-start.14 = (bf16[784,128]{1,0:T(8,128)(2,1)S(1)}, bf16[784,128]{1,0:T(8,128)(2,1)S(1)}, u32[]{:S(2)}, u32[]{:S(2)}) collective-permute-start(bf16[784,128]{1,0:T(8,128)(2,1)S(1)} %collective-permute-done.12.refs_0_), channel_id=1, source_target_pairs={{0,4},{4,8},{8,12},{12,14},{14,10},{10,6},{6,2},{2,0},{1,5},{5,9},... | collective-permute-start | bytes 602120 | tf_op jit(solution)/shard_map/out_trail2/ppermute | solution.py:336
  32.7 7.2 %collective-permute-start.11 = (bf16[784,128]{1,0:T(8,128)(2,1)S(1)}, bf16[784,128]{1,0:T(8,128)(2,1)S(1)}, u32[]{:S(2)}, u32[]{:S(2)}) collective-permute-start(bf16[784,128]{1,0:T(8,128)(2,1)S(1)} %collective-permute-done.9.refs_1_), channel_id=1, source_target_pairs={{4,0},{8,4},{12,8},{14,12},{10,14},{6,10},{2,6},{0,2},{5,1},{9,5},... | collective-permute-start | bytes 602120 | tf_op jit(solution)/shard_map/out_lead3/ppermute | solution.py:336
  34.1 5.8 %collective-permute-start.10 = (bf16[784,128]{1,0:T(8,128)(2,1)S(1)}, bf16[784,128]{1,0:T(8,128)(2,1)S(1)}, u32[]{:S(2)}, u32[]{:S(2)}) collective-permute-start(bf16[784,128]{1,0:T(8,128)(2,1)S(1)} %collective-permute-done.8.refs_0_), channel_id=1, source_target_pairs={{0,4},{4,8},{8,12},{12,14},{14,10},{10,6},{6,2},{2,0},{1,5},{5,9},... | collective-permute-start | bytes 602120 | tf_op jit(solution)/shard_map/out_lead3/ppermute | solution.py:336
  39.1 1.2 %collective-permute-start.16 = (bf16[16,128]{1,0:T(8,128)(2,1)S(1)}, bf16[16,128]{1,0:T(8,128)(2,1)S(1)}, u32[]{:S(2)}, u32[]{:S(2)}) collective-permute-start(bf16[16,128]{1,0:T(8,128)(2,1)S(1)} %slice.6), channel_id=1, source_target_pairs={{0,1},{1,0},{2,3},{3,2},{4,5},{5,4},{6,7},{7,6},{8,9},{9,8},{10,11... | collective-permute-start | bytes 12296 | tf_op jit(solution)/shard_map/ppermute | solution.py:37
  40.4 7.8 %collective-permute-start.17 = (bf16[784,128]{1,0:T(8,128)(2,1)S(1)}, bf16[784,128]{1,0:T(8,128)(2,1)S(1)}, u32[]{:S(2)}, u32[]{:S(2)}) collective-permute-start(bf16[784,128]{1,0:T(8,128)(2,1)S(1)} %collective-permute-done.10.refs_0_), channel_id=1, source_target_pairs={{0,4},{4,8},{8,12},{12,14},{14,10},{10,6},{6,2},{2,0},{1,5},{5,9},... | collective-permute-start | bytes 602120 | tf_op jit(solution)/shard_map/out_lead4/ppermute | solution.py:336
  41.9 7.9 %collective-permute-start.18 = (bf16[784,128]{1,0:T(8,128)(2,1)S(1)}, bf16[784,128]{1,0:T(8,128)(2,1)S(1)}, u32[]{:S(2)}, u32[]{:S(2)}) collective-permute-start(bf16[784,128]{1,0:T(8,128)(2,1)S(1)} %collective-permute-done.11.refs_1_), channel_id=1, source_target_pairs={{4,0},{8,4},{12,8},{14,12},{10,14},{6,10},{2,6},{0,2},{5,1},{9,5},... | collective-permute-start | bytes 602120 | tf_op jit(solution)/shard_map/out_lead4/ppermute | solution.py:336
  42.4 13.7 %collective-permute-start.23 = (bf16[784,128]{1,0:T(8,128)(2,1)S(1)}, bf16[784,128]{1,0:T(8,128)(2,1)S(1)}, u32[]{:S(2)}, u32[]{:S(2)}) collective-permute-start(bf16[784,128]{1,0:T(8,128)(2,1)S(1)} %collective-permute-done.15.refs_1_), channel_id=1, source_target_pairs={{4,0},{8,4},{12,8},{14,12},{10,14},{6,10},{2,6},{0,2},{5,1},{9,5},... | collective-permute-start | bytes 602120 | tf_op jit(solution)/shard_map/out_trail3/ppermute | solution.py:336
  43.8 10.2 %collective-permute-start.22 = (bf16[784,128]{1,0:T(8,128)(2,1)S(1)}, bf16[784,128]{1,0:T(8,128)(2,1)S(1)}, u32[]{:S(2)}, u32[]{:S(2)}) collective-permute-start(bf16[784,128]{1,0:T(8,128)(2,1)S(1)} %collective-permute-done.14.refs_0_), channel_id=1, source_target_pairs={{0,4},{4,8},{8,12},{12,14},{14,10},{10,6},{6,2},{2,0},{1,5},{5,9},... | collective-permute-start | bytes 602120 | tf_op jit(solution)/shard_map/out_trail3/ppermute | solution.py:336
  46.5 5.4 %collective-permute-start.19 = (bf16[16,128]{1,0:T(8,128)(2,1)S(1)}, bf16[16,128]{1,0:T(8,128)(2,1)S(1)}, u32[]{:S(2)}, u32[]{:S(2)}) collective-permute-start(bf16[16,128]{1,0:T(8,128)(2,1)S(1)} %slice.7), channel_id=1, source_target_pairs={{0,1},{1,0},{2,3},{3,2},{4,5},{5,4},{6,7},{7,6},{8,9},{9,8},{10,11... | collective-permute-start | bytes 12296 | tf_op jit(solution)/shard_map/ppermute | solution.py:37
  51.9 7.9 %collective-permute-start.21 = (bf16[64,1536]{1,0:T(8,128)(2,1)S(1)}, bf16[64,1536]{1,0:T(8,128)(2,1)S(1)}, u32[]{:S(2)}, u32[]{:S(2)}) collective-permute-start(bf16[64,1536]{1,0:T(8,128)(2,1)S(1)} %get-tuple-element.133), channel_id=1, source_target_pairs={{4,0},{8,4},{12,8},{14,12},{10,14},{6,10},{2,6},{0,2},{5,1},{9,5},... | collective-permute-start | bytes 589832 | tf_op jit(solution)/shard_map/back_lead4/ppermute | solution.py:381
  52.4 7.4 %collective-permute-start.20 = (bf16[64,1536]{1,0:T(8,128)(2,1)S(1)}, bf16[64,1536]{1,0:T(8,128)(2,1)S(1)}, u32[]{:S(2)}, u32[]{:S(2)}) collective-permute-start(bf16[64,1536]{1,0:T(8,128)(2,1)S(1)} %get-tuple-element.131), channel_id=1, source_target_pairs={{0,4},{4,8},{8,12},{12,14},{14,10},{10,6},{6,2},{2,0},{1,5},{5,9},... | collective-permute-start | bytes 589832 | tf_op jit(solution)/shard_map/back_lead4/ppermute | solution.py:381
  54.0 10.0 %collective-permute-start.30 = (bf16[64,1536]{1,0:T(8,128)(2,1)S(1)}, bf16[64,1536]{1,0:T(8,128)(2,1)S(1)}, u32[]{:S(2)}, u32[]{:S(2)}) collective-permute-start(bf16[64,1536]{1,0:T(8,128)(2,1)S(1)} %get-tuple-element.153), channel_id=1, source_target_pairs={{4,0},{8,4},{12,8},{14,12},{10,14},{6,10},{2,6},{0,2},{5,1},{9,5},... | collective-permute-start | bytes 589832 | tf_op jit(solution)/shard_map/back_trail3/ppermute | solution.py:381
  54.5 9.6 %collective-permute-start.29 = (bf16[64,1536]{1,0:T(8,128)(2,1)S(1)}, bf16[64,1536]{1,0:T(8,128)(2,1)S(1)}, u32[]{:S(2)}, u32[]{:S(2)}) collective-permute-start(bf16[64,1536]{1,0:T(8,128)(2,1)S(1)} %get-tuple-element.152), channel_id=1, source_target_pairs={{0,4},{4,8},{8,12},{12,14},{14,10},{10,6},{6,2},{2,0},{1,5},{5,9},... | collective-permute-start | bytes 589832 | tf_op jit(solution)/shard_map/back_trail3/ppermute | solution.py:381
  59.9 8.5 %collective-permute-start.25 = (bf16[64,1536]{1,0:T(8,128)(2,1)S(1)}, bf16[64,1536]{1,0:T(8,128)(2,1)S(1)}, u32[]{:S(2)}, u32[]{:S(2)}) collective-permute-start(bf16[64,1536]{1,0:T(8,128)(2,1)S(1)} %add_convert_fusion.8), channel_id=1, source_target_pairs={{4,0},{8,4},{12,8},{14,12},{10,14},{6,10},{2,6},{0,2},{5,1},{9,5},... | collective-permute-start | bytes 589832 | tf_op jit(solution)/shard_map/back_lead3/ppermute | solution.py:381
  61.2 7.2 %collective-permute-start.24 = (bf16[64,1536]{1,0:T(8,128)(2,1)S(1)}, bf16[64,1536]{1,0:T(8,128)(2,1)S(1)}, u32[]{:S(2)}, u32[]{:S(2)}) collective-permute-start(bf16[64,1536]{1,0:T(8,128)(2,1)S(1)} %add_convert_fusion.9), channel_id=1, source_target_pairs={{0,4},{4,8},{8,12},{12,14},{14,10},{10,6},{6,2},{2,0},{1,5},{5,9},... | collective-permute-start | bytes 589832 | tf_op jit(solution)/shard_map/back_lead3/ppermute | solution.py:381
  64.1 8.4 %collective-permute-start.32 = (bf16[64,1536]{1,0:T(8,128)(2,1)S(1)}, bf16[64,1536]{1,0:T(8,128)(2,1)S(1)}, u32[]{:S(2)}, u32[]{:S(2)}) collective-permute-start(bf16[64,1536]{1,0:T(8,128)(2,1)S(1)} %add_convert_fusion.3), channel_id=1, source_target_pairs={{4,0},{8,4},{12,8},{14,12},{10,14},{6,10},{2,6},{0,2},{5,1},{9,5},... | collective-permute-start | bytes 589832 | tf_op jit(solution)/shard_map/back_trail2/ppermute | solution.py:381
  65.4 7.9 %collective-permute-start.31 = (bf16[64,1536]{1,0:T(8,128)(2,1)S(1)}, bf16[64,1536]{1,0:T(8,128)(2,1)S(1)}, u32[]{:S(2)}, u32[]{:S(2)}) collective-permute-start(bf16[64,1536]{1,0:T(8,128)(2,1)S(1)} %add_convert_fusion.4), channel_id=1, source_target_pairs={{0,4},{4,8},{8,12},{12,14},{14,10},{10,6},{6,2},{2,0},{1,5},{5,9},... | collective-permute-start | bytes 589832 | tf_op jit(solution)/shard_map/back_trail2/ppermute | solution.py:381
  68.5 9.2 %collective-permute-start.27 = (bf16[64,1536]{1,0:T(8,128)(2,1)S(1)}, bf16[64,1536]{1,0:T(8,128)(2,1)S(1)}, u32[]{:S(2)}, u32[]{:S(2)}) collective-permute-start(bf16[64,1536]{1,0:T(8,128)(2,1)S(1)} %add_convert_fusion.6), channel_id=1, source_target_pairs={{4,0},{8,4},{12,8},{14,12},{10,14},{6,10},{2,6},{0,2},{5,1},{9,5},... | collective-permute-start | bytes 589832 | tf_op jit(solution)/shard_map/back_lead2/ppermute | solution.py:381
  70.7 7.8 %collective-permute-start.26 = (bf16[64,1536]{1,0:T(8,128)(2,1)S(1)}, bf16[64,1536]{1,0:T(8,128)(2,1)S(1)}, u32[]{:S(2)}, u32[]{:S(2)}) collective-permute-start(bf16[64,1536]{1,0:T(8,128)(2,1)S(1)} %add_convert_fusion.7), channel_id=1, source_target_pairs={{0,4},{4,8},{8,12},{12,14},{14,10},{10,6},{6,2},{2,0},{1,5},{5,9},... | collective-permute-start | bytes 589832 | tf_op jit(solution)/shard_map/back_lead2/ppermute | solution.py:381
  73.4 7.3 %collective-permute-start.33 = (bf16[64,1536]{1,0:T(8,128)(2,1)S(1)}, bf16[64,1536]{1,0:T(8,128)(2,1)S(1)}, u32[]{:S(2)}, u32[]{:S(2)}) collective-permute-start(bf16[64,1536]{1,0:T(8,128)(2,1)S(1)} %add_convert_fusion.2), channel_id=1, source_target_pairs={{4,0},{8,4},{12,8},{14,12},{10,14},{6,10},{2,6},{0,2},{5,1},{9,5},... | collective-permute-start | bytes 589832 | tf_op jit(solution)/shard_map/back_trail1/ppermute | solution.py:381
  74.9 9.4 %collective-permute-start.34 = (bf16[64,1536]{1,0:T(8,128)(2,1)S(1)}, bf16[64,1536]{1,0:T(8,128)(2,1)S(1)}, u32[]{:S(2)}, u32[]{:S(2)}) collective-permute-start(bf16[64,1536]{1,0:T(8,128)(2,1)S(1)} %add_convert_fusion.1), channel_id=1, source_target_pairs={{0,4},{4,8},{8,12},{12,14},{14,10},{10,6},{6,2},{2,0},{1,5},{5,9},... | collective-permute-start | bytes 589832 | tf_op jit(solution)/shard_map/back_trail1/ppermute | solution.py:381
  78.5 5.7 %collective-permute-start.28 = (bf16[64,1536]{1,0:T(8,128)(2,1)S(1)}, bf16[64,1536]{1,0:T(8,128)(2,1)S(1)}, u32[]{:S(2)}, u32[]{:S(2)}) collective-permute-start(bf16[64,1536]{1,0:T(8,128)(2,1)S(1)} %add_convert_fusion.5), channel_id=1, source_target_pairs={{0,4},{4,8},{8,12},{12,14},{14,10},{10,6},{6,2},{2,0},{1,5},{5,9},... | collective-permute-start | bytes 589832 | tf_op jit(solution)/shard_map/back_lead1/ppermute | solution.py:381
  78.7 5.7 %collective-permute-start.35 = (bf16[64,1536]{1,0:T(8,128)(2,1)S(1)}, bf16[64,1536]{1,0:T(8,128)(2,1)S(1)}, u32[]{:S(2)}, u32[]{:S(2)}) collective-permute-start(bf16[64,1536]{1,0:T(8,128)(2,1)S(1)} %add_convert_fusion), channel_id=1, source_target_pairs={{4,0},{8,4},{12,8},{14,12},{10,14},{6,10},{2,6},{0,2},{5,1},{9,5},... | collective-permute-start | bytes 589832 | tf_op jit(solution)/shard_map/back_lead1/ppermute | solution.py:381

commit v11 on v10

--- a/solution.py
+++ b/solution.py
@@ -335,9 +335,6 @@
             with jax.named_scope(f"out_{'lead' if lead else 'trail'}{distance}"):
                 came[side, distance, piece] = lax.ppermute(block, "seq", hops[side])
 
-    def both(value):
-        return swapped(value[:16, :LANES], "rep")
-
     def apply(distance, kinds, *after):
         keys = [(side, distance, side if lead else 1 - side) for lead in kinds for side in sides]
         blocks = [came[key] for key in keys]
@@ -350,10 +347,7 @@
         return outs[0]
 
     for distance in range(1, far + 1):
-        hold = [worked[distance - 2]] if distance > 1 else []
-        if distance == far:
-            hold.append(both(hold[0]))
-        bring(distance, True, *hold)
+        bring(distance, True, *([worked[distance - 2]] if distance > 1 else []))
         trails = []
         if distance < far:
             before = [came[side, distance - 1, side] for side in sides] if distance > 1 else []
@@ -380,7 +374,7 @@
             with jax.named_scope(f"back_{'lead' if lead else 'trail'}{distance}"):
                 moving[side, piece] = lax.ppermute(value, "seq", hops[side])
 
-    send(far, True, both(worked[far - 1]))
+    send(far, True)
     send(far - 1, False, *[came[side, far, side] for side in sides])
     for distance in range(far - 1, 0, -1):
         leads = [moving[side, side] for side in sides]

time: 85.5 us -> 84.8 us (level)
    ppermute x14, waiting for transfers between devices: 8.91 us -> 7.4 us  [bring(): came[side, distance, piece] = lax.ppermute(block, 'seq', hops[side])]
    ppermute x14, waiting for transfers between devices: 10.7 us -> 12 us  [send(): moving[side, piece] = lax.ppermute(value, 'seq', hops[side])]
    ppermute x6 -> x4, waiting for transfers between devices: 2.12 us -> 1.69 us  [swapped(): return lax.ppermute(value, axis, [(i, i ^ bit) for i in range(peers)])]
  transfers between devices with their start and end apart: 36 -> 34, of which waited for: 19 -> 18; matrix products, arithmetic and copies ran while one was open for 1% -> 1% of each run, Pallas kernels for 29% -> 29%
where the time goes in v11:
time: 84.8 us; the launch traced here: 84.7 us
  starting transfers between devices  34.3 us (40%)
  Pallas kernels  24.6 us (29%)
  waiting for transfers between devices  24 us (28%)
  other arithmetic  1.44 us (2%)
    pallas_call x8, Pallas kernels, experts(): pl.pallas_call(functools.partial(expert_kernel, min(256, half), len(block...  18.8 us
    ppermute x14, starting transfers between devices, send(): moving[side, piece] = lax.ppermute(value, 'seq', hops[side])  14.9 us
    ppermute x14, starting transfers between devices, bring(): came[side, distance, piece] = lax.ppermute(block, 'seq', hops[side])  14.3 us
    ppermute x14, waiting for transfers between devices, send(): moving[side, piece] = lax.ppermute(value, 'seq', hops[side])  12 us
    ppermute x14, waiting for transfers between devices, bring(): came[side, distance, piece] = lax.ppermute(block, 'seq', hops[side])  7.4 us
    pallas_call x2, Pallas kernels, attend(): pl.pallas_call(functools.partial(attend_kernel, mix), in_specs=[vmem if m...  5.54 us
    ppermute x2, starting transfers between devices, shifted(): lax.ppermute(value, axis, [(i, (i + by) % peers) for i in range(peers)])  4.04 us
    ppermute x2, waiting for transfers between devices, shifted(): lax.ppermute(value, axis, [(i, (i + by) % peers) for i in range(peers)])  2.81 us
  transfers between devices with their start and end apart: 34, of which 18 were waited for; matrix products, arithmetic and copies ran while one was open for 1% of the time, Pallas kernels for 29%

profile of v11, /device:TPU:0, one launch (start us, length us, event | category | flops | bytes accessed | tf_op | source)
XLA Modules:
  0.0 84.7 jit_solution(7572394836517830252)
XLA Ops:
  0.0 0.5 collective-permute-start.3
  0.5 0.5 collective-permute-start.5
  1.0 2.5 %collective-permute-start = (bf16[256,128]{1,0:T(8,128)(2,1)}, bf16[256,128]{1,0:T(8,128)(2,1)S(1)}, u32[]{:S(2)}, u32[]{:S(2)}) collective-permute-start(bf16[256,128]{1,0:T(8,128)(2,1)} %refs_2_.1), channel_id=1, source_target_pairs={{0,2},{2,4},{4,6},{6,8},{8,10},{10,12},{12,14},{14,0},{1,3},{3,5},... | collective-permute-start | bytes 196616 | tf_op jit(solution)/shard_map/ppermute | solution.py:24
  3.5 1.5 %collective-permute-start.1 = (bf16[256,128]{1,0:T(8,128)(2,1)}, bf16[256,128]{1,0:T(8,128)(2,1)S(1)}, u32[]{:S(2)}, u32[]{:S(2)}) collective-permute-start(bf16[256,128]{1,0:T(8,128)(2,1)} %refs_3_.1), channel_id=1, source_target_pairs={{0,2},{2,4},{4,6},{6,8},{8,10},{10,12},{12,14},{14,0},{1,3},{3,5},... | collective-permute-start | bytes 196616 | tf_op jit(solution)/shard_map/ppermute | solution.py:24
  5.0 3.0 %attend.2 = (f32[1,16]{1,0:T(1,128)S(1)}, bf16[256,1024]{1,0:T(8,128)(2,1)S(1)}, bf16[256,128]{1,0:T(8,128)(2,1)S(1)}, bf16[256,128]{1,0:T(8,128)(2,1)S(1)}, bf1...) custom-call(f32[1,16]{1,0:T(1,128)} %bitcast.38, bf16[256,1024]{1,0:T(8,128)(2,1)} %refs_1_.1, ...), custom_call_target="tpu_custom_call" | custom-call | flops 671088640 | bytes 6291456 | tf_op jit(solution)/shard_map/attend/pallas_call | solution.py:151
  8.1 1.6 %collective-permute-done.refs_6_ = bf16[256,128]{1,0:T(8,128)(2,1)S(1)} collective-permute-done((bf16[256,128]{1,0:T(8,128)(2,1)}, bf16[256,128]{1,0:T(8,128)(2,1)S(1)}, u32[]{:S(2)}, u32[]{:S(2)}) %collective-permute-start) | collective-permute-done | bytes 65568 | tf_op jit(solution)/shard_map/ppermute | solution.py:24
  9.6 1.2 %collective-permute-done.1.refs_7_ = bf16[256,128]{1,0:T(8,128)(2,1)S(1)} collective-permute-done((bf16[256,128]{1,0:T(8,128)(2,1)}, bf16[256,128]{1,0:T(8,128)(2,1)S(1)}, u32[]{:S(2)}, u32[]{:S(2)}) %collective-permute-start.1) | collective-permute-done | bytes 65568 | tf_op jit(solution)/shard_map/ppermute | solution.py:24
  10.9 2.5 %attend.3 = (bf16[128,1536]{1,0:T(8,128)(2,1)S(1)}, f32[128,1536]{1,0:T(8,128)S(1)}) custom-call(f32[1,16]{1,0:T(1,128)S(1)} %get-tuple-element.84.refs_0_, bf16[256,1024]{1,0:T(8,128)(2,1)S(1)} %get-tuple-element.85.refs_1_, bf16[256,128]{1,0:T(8,128)(2,1)S(1)} %get-tuple-element.86.refs_2_, bf16[256,128]{1,0:T(8,128)(2,1)S(1)} %get-tuple-element.87.refs_3_, ...), custom_call_target="tpu_custom_call" | custom-call | flops 671088640 | bytes 6291456 | tf_op jit(solution)/shard_map/attend/pallas_call | solution.py:151
  13.5 1.7 %collective-permute-done.2.came_ref = bf16[128,1536]{1,0:T(8,128)(2,1)S(1)} collective-permute-done((bf16[128,1536]{1,0:T(8,128)(2,1)S(1)}, bf16[128,1536]{1,0:T(8,128)(2,1)S(1)}, u32[]{:S(2)}, u32[]{:S(2)}) %collective-permute-start.2) | collective-permute-done | bytes 393248 | tf_op jit(solution)/shard_map/ppermute | solution.py:37
  15.6 2.0 %collective-permute-start.7 = (bf16[784,128]{1,0:T(8,128)(2,1)S(1)}, bf16[784,128]{1,0:T(8,128)(2,1)S(1)}, u32[]{:S(2)}, u32[]{:S(2)}) collective-permute-start(bf16[784,128]{1,0:T(8,128)(2,1)S(1)} %get-tuple-element.99.refs_1_), channel_id=1, source_target_pairs={{4,0},{8,4},{12,8},{14,12},{10,14},{6,10},{2,6},{0,2},{5,1},{9,5},... | collective-permute-start | bytes 602120 | tf_op jit(solution)/shard_map/out_lead1/ppermute | solution.py:336
  17.7 2.0 %collective-permute-start.13 = (bf16[784,128]{1,0:T(8,128)(2,1)S(1)}, bf16[784,128]{1,0:T(8,128)(2,1)S(1)}, u32[]{:S(2)}, u32[]{:S(2)}) collective-permute-start(bf16[784,128]{1,0:T(8,128)(2,1)S(1)} %get-tuple-element.98.refs_0_), channel_id=1, source_target_pairs={{4,0},{8,4},{12,8},{14,12},{10,14},{6,10},{2,6},{0,2},{5,1},{9,5},... | collective-permute-start | bytes 602120 | tf_op jit(solution)/shard_map/out_trail1/ppermute | solution.py:336
  19.7 4.1 %experts.8 = (bf16[64,1536]{1,0:T(8,128)(2,1)S(1)}, bf16[64,1536]{1,0:T(8,128)(2,1)S(1)}, bf16[1536,768]{1,0:T(8,128)(2,1)S(1)}, bf16[1536,768]{1,0:T(8,128)(2,1)S(1)}, bf16[768,1536]{1,0:T(8,128)(2,1)S(1)}) custom-call(s32[1]{0:T(128)} %bitcast.5.me_ref, bf16[784,128]{1,0:T(8,128)(2,1)S(1)} %get-tuple-element.98.refs_0_, ...), custom_call_target="tpu_custom_call" | custom-call | flops 1811939328 | bytes 1179648 | tf_op jit(solution)/shard_map/experts/pallas_call | solution.py:287
  23.8 1.0 %collective-permute-start.8 = (bf16[784,128]{1,0:T(8,128)(2,1)S(1)}, bf16[784,128]{1,0:T(8,128)(2,1)S(1)}, u32[]{:S(2)}, u32[]{:S(2)}) collective-permute-start(bf16[784,128]{1,0:T(8,128)(2,1)S(1)} %collective-permute-done.6.refs_0_), channel_id=1, source_target_pairs={{0,4},{4,8},{8,12},{12,14},{14,10},{10,6},{6,2},{2,0},{1,5},{5,9},... | collective-permute-start | bytes 602120 | tf_op jit(solution)/shard_map/out_lead2/ppermute | solution.py:336
  24.8 1.1 %collective-permute-start.9 = (bf16[784,128]{1,0:T(8,128)(2,1)S(1)}, bf16[784,128]{1,0:T(8,128)(2,1)S(1)}, u32[]{:S(2)}, u32[]{:S(2)}) collective-permute-start(bf16[784,128]{1,0:T(8,128)(2,1)S(1)} %collective-permute-done.7.refs_1_), channel_id=1, source_target_pairs={{4,0},{8,4},{12,8},{14,12},{10,14},{6,10},{2,6},{0,2},{5,1},{9,5},... | collective-permute-start | bytes 602120 | tf_op jit(solution)/shard_map/out_lead2/ppermute | solution.py:336
  25.9 1.9 %collective-permute-done.12.refs_0_ = bf16[784,128]{1,0:T(8,128)(2,1)S(1)} collective-permute-done((bf16[784,128]{1,0:T(8,128)(2,1)S(1)}, bf16[784,128]{1,0:T(8,128)(2,1)S(1)}, u32[]{:S(2)}, u32[]{:S(2)}) %collective-permute-start.12) | collective-permute-done | bytes 200736 | tf_op jit(solution)/shard_map/out_trail1/ppermute | solution.py:336
  27.8 2.0 %collective-permute-start.15 = (bf16[784,128]{1,0:T(8,128)(2,1)S(1)}, bf16[784,128]{1,0:T(8,128)(2,1)S(1)}, u32[]{:S(2)}, u32[]{:S(2)}) collective-permute-start(bf16[784,128]{1,0:T(8,128)(2,1)S(1)} %collective-permute-done.13.refs_1_), channel_id=1, source_target_pairs={{4,0},{8,4},{12,8},{14,12},{10,14},{6,10},{2,6},{0,2},{5,1},{9,5},... | collective-permute-start | bytes 602120 | tf_op jit(solution)/shard_map/out_trail2/ppermute | solution.py:336
  29.9 2.1 %experts.9 = (bf16[64,1536]{1,0:T(8,128)(2,1)S(1)}, bf16[64,1536]{1,0:T(8,128)(2,1)S(1)}) custom-call(s32[1]{0:T(128)} %bitcast.5.me_ref, bf16[784,128]{1,0:T(8,128)(2,1)S(1)} %collective-permute-done.6.refs_0_, bf16[784,128]{1,0:T(8,128)(2,1)S(1)} %collective-permute-done.7.refs_1_, bf16[1536,768]{1,0:T(8,128)(2,1)S(1)} %bitcast.11, ...), custom_call_target="tpu_custom_call" | custom-call | flops 1811939328 | bytes 1179648 | tf_op jit(solution)/shard_map/hop1/experts/pallas_call | solution.py:287
  32.1 0.6 collective-permute-done.9.refs_1_
  32.7 1.4 %collective-permute-start.11 = (bf16[784,128]{1,0:T(8,128)(2,1)S(1)}, bf16[784,128]{1,0:T(8,128)(2,1)S(1)}, u32[]{:S(2)}, u32[]{:S(2)}) collective-permute-start(bf16[784,128]{1,0:T(8,128)(2,1)S(1)} %collective-permute-done.9.refs_1_), channel_id=1, source_target_pairs={{4,0},{8,4},{12,8},{14,12},{10,14},{6,10},{2,6},{0,2},{5,1},{9,5},... | collective-permute-start | bytes 602120 | tf_op jit(solution)/shard_map/out_lead3/ppermute | solution.py:336
  34.1 0.6 collective-permute-start.10
  34.7 2.3 %collective-permute-done.15.refs_1_ = bf16[784,128]{1,0:T(8,128)(2,1)S(1)} collective-permute-done((bf16[784,128]{1,0:T(8,128)(2,1)S(1)}, bf16[784,128]{1,0:T(8,128)(2,1)S(1)}, u32[]{:S(2)}, u32[]{:S(2)}) %collective-permute-start.15) | collective-permute-done | bytes 200736 | tf_op jit(solution)/shard_map/out_trail2/ppermute | solution.py:336
  37.0 2.1 %experts.10 = (bf16[64,1536]{1,0:T(8,128)(2,1)S(1)}, bf16[64,1536]{1,0:T(8,128)(2,1)S(1)}) custom-call(s32[1]{0:T(128)} %bitcast.5.me_ref, bf16[784,128]{1,0:T(8,128)(2,1)S(1)} %collective-permute-done.8.refs_0_, bf16[784,128]{1,0:T(8,128)(2,1)S(1)} %collective-permute-done.9.refs_1_, bf16[1536,768]{1,0:T(8,128)(2,1)S(1)} %bitcast.12, ...), custom_call_target="tpu_custom_call" | custom-call | flops 1811939328 | bytes 1179648 | tf_op jit(solution)/shard_map/hop2/experts/pallas_call | solution.py:287
  39.1 0.8 collective-permute-done.11.refs_1_
  39.9 0.9 %collective-permute-start.16 = (bf16[784,128]{1,0:T(8,128)(2,1)S(1)}, bf16[784,128]{1,0:T(8,128)(2,1)S(1)}, u32[]{:S(2)}, u32[]{:S(2)}) collective-permute-start(bf16[784,128]{1,0:T(8,128)(2,1)S(1)} %collective-permute-done.10.refs_0_), channel_id=1, source_target_pairs={{0,4},{4,8},{8,12},{12,14},{14,10},{10,6},{6,2},{2,0},{1,5},{5,9},... | collective-permute-start | bytes 602120 | tf_op jit(solution)/shard_map/out_lead4/ppermute | solution.py:336
  40.9 1.1 %collective-permute-start.17 = (bf16[784,128]{1,0:T(8,128)(2,1)S(1)}, bf16[784,128]{1,0:T(8,128)(2,1)S(1)}, u32[]{:S(2)}, u32[]{:S(2)}) collective-permute-start(bf16[784,128]{1,0:T(8,128)(2,1)S(1)} %collective-permute-done.11.refs_1_), channel_id=1, source_target_pairs={{4,0},{8,4},{12,8},{14,12},{10,14},{6,10},{2,6},{0,2},{5,1},{9,5},... | collective-permute-start | bytes 602120 | tf_op jit(solution)/shard_map/out_lead4/ppermute | solution.py:336
  42.0 1.7 %collective-permute-start.21 = (bf16[784,128]{1,0:T(8,128)(2,1)S(1)}, bf16[784,128]{1,0:T(8,128)(2,1)S(1)}, u32[]{:S(2)}, u32[]{:S(2)}) collective-permute-start(bf16[784,128]{1,0:T(8,128)(2,1)S(1)} %collective-permute-done.15.refs_1_), channel_id=1, source_target_pairs={{4,0},{8,4},{12,8},{14,12},{10,14},{6,10},{2,6},{0,2},{5,1},{9,5},... | collective-permute-start | bytes 602120 | tf_op jit(solution)/shard_map/out_trail3/ppermute | solution.py:336
  44.0 2.1 %experts.11 = (bf16[64,1536]{1,0:T(8,128)(2,1)S(1)}, bf16[64,1536]{1,0:T(8,128)(2,1)S(1)}) custom-call(s32[1]{0:T(128)} %bitcast.5.me_ref, bf16[784,128]{1,0:T(8,128)(2,1)S(1)} %collective-permute-done.10.refs_0_, bf16[784,128]{1,0:T(8,128)(2,1)S(1)} %collective-permute-done.11.refs_1_, bf16[1536,768]{1,0:T(8,128)(2,1)S(1)} %bitcast.13, ...), custom_call_target="tpu_custom_call" | custom-call | flops 1811939328 | bytes 1179648 | tf_op jit(solution)/shard_map/hop3/experts/pallas_call | solution.py:287
  46.1 1.0 %collective-permute-done.16.refs_0_ = bf16[784,128]{1,0:T(8,128)(2,1)S(1)} collective-permute-done((bf16[784,128]{1,0:T(8,128)(2,1)S(1)}, bf16[784,128]{1,0:T(8,128)(2,1)S(1)}, u32[]{:S(2)}, u32[]{:S(2)}) %collective-permute-start.16) | collective-permute-done | bytes 200736 | tf_op jit(solution)/shard_map/out_lead4/ppermute | solution.py:336
  47.1 0.6 collective-permute-done.17.refs_1_
  47.7 2.1 %experts.12 = (bf16[64,1536]{1,0:T(8,128)(2,1)S(1)}, bf16[64,1536]{1,0:T(8,128)(2,1)S(1)}) custom-call(s32[1]{0:T(128)} %bitcast.5.me_ref, bf16[784,128]{1,0:T(8,128)(2,1)S(1)} %collective-permute-done.16.refs_0_, bf16[784,128]{1,0:T(8,128)(2,1)S(1)} %collective-permute-done.17.refs_1_, bf16[1536,768]{1,0:T(8,128)(2,1)S(1)} %bitcast.14, ...), custom_call_target="tpu_custom_call" | custom-call | flops 1811939328 | bytes 1179648 | tf_op jit(solution)/shard_map/hop4/experts/pallas_call | solution.py:287
  49.8 2.2 %collective-permute-start.18 = (bf16[64,1536]{1,0:T(8,128)(2,1)S(1)}, bf16[64,1536]{1,0:T(8,128)(2,1)S(1)}, u32[]{:S(2)}, u32[]{:S(2)}) collective-permute-start(bf16[64,1536]{1,0:T(8,128)(2,1)S(1)} %get-tuple-element.128), channel_id=1, source_target_pairs={{0,4},{4,8},{8,12},{12,14},{14,10},{10,6},{6,2},{2,0},{1,5},{5,9},... | collective-permute-start | bytes 589832 | tf_op jit(solution)/shard_map/back_lead4/ppermute | solution.py:375
  52.1 1.8 %collective-permute-start.28 = (bf16[64,1536]{1,0:T(8,128)(2,1)S(1)}, bf16[64,1536]{1,0:T(8,128)(2,1)S(1)}, u32[]{:S(2)}, u32[]{:S(2)}) collective-permute-start(bf16[64,1536]{1,0:T(8,128)(2,1)S(1)} %get-tuple-element.149), channel_id=1, source_target_pairs={{4,0},{8,4},{12,8},{14,12},{10,14},{6,10},{2,6},{0,2},{5,1},{9,5},... | collective-permute-start | bytes 589832 | tf_op jit(solution)/shard_map/back_trail3/ppermute | solution.py:375
  54.1 2.1 %experts.13 = (bf16[64,1536]{1,0:T(8,128)(2,1)S(1)}, bf16[64,1536]{1,0:T(8,128)(2,1)S(1)}) custom-call(s32[1]{0:T(128)} %bitcast.5.me_ref, bf16[784,128]{1,0:T(8,128)(2,1)S(1)} %collective-permute-done.20.refs_0_, bf16[784,128]{1,0:T(8,128)(2,1)S(1)} %collective-permute-done.21.refs_1_, bf16[1536,768]{1,0:T(8,128)(2,1)S(1)} %bitcast.15, ...), custom_call_target="tpu_custom_call" | custom-call | flops 1811939328 | bytes 1179648 | tf_op jit(solution)/shard_map/hop3/experts/pallas_call | solution.py:287
  56.4 3.3 %collective-permute-done.19 = bf16[64,1536]{1,0:T(8,128)(2,1)S(1)} collective-permute-done((bf16[64,1536]{1,0:T(8,128)(2,1)S(1)}, bf16[64,1536]{1,0:T(8,128)(2,1)S(1)}, u32[]{:S(2)}, u32[]{:S(2)}) %collective-permute-start.19) | collective-permute-done | bytes 196640 | tf_op jit(solution)/shard_map/back_lead4/ppermute | solution.py:375
  60.0 2.0 %collective-permute-start.22 = (bf16[64,1536]{1,0:T(8,128)(2,1)S(1)}, bf16[64,1536]{1,0:T(8,128)(2,1)S(1)}, u32[]{:S(2)}, u32[]{:S(2)}) collective-permute-start(bf16[64,1536]{1,0:T(8,128)(2,1)S(1)} %add_convert_fusion.9), channel_id=1, source_target_pairs={{0,4},{4,8},{8,12},{12,14},{14,10},{10,6},{6,2},{2,0},{1,5},{5,9},... | collective-permute-start | bytes 589832 | tf_op jit(solution)/shard_map/back_lead3/ppermute | solution.py:375
  62.0 2.0 %collective-permute-done.28 = bf16[64,1536]{1,0:T(8,128)(2,1)S(1)} collective-permute-done((bf16[64,1536]{1,0:T(8,128)(2,1)S(1)}, bf16[64,1536]{1,0:T(8,128)(2,1)S(1)}, u32[]{:S(2)}, u32[]{:S(2)}) %collective-permute-start.28) | collective-permute-done | bytes 196640 | tf_op jit(solution)/shard_map/back_trail3/ppermute | solution.py:375
  64.2 2.0 %collective-permute-start.29 = (bf16[64,1536]{1,0:T(8,128)(2,1)S(1)}, bf16[64,1536]{1,0:T(8,128)(2,1)S(1)}, u32[]{:S(2)}, u32[]{:S(2)}) collective-permute-start(bf16[64,1536]{1,0:T(8,128)(2,1)S(1)} %add_convert_fusion.4), channel_id=1, source_target_pairs={{0,4},{4,8},{8,12},{12,14},{14,10},{10,6},{6,2},{2,0},{1,5},{5,9},... | collective-permute-start | bytes 589832 | tf_op jit(solution)/shard_map/back_trail2/ppermute | solution.py:375
  66.2 2.1 %experts.14 = (bf16[64,1536]{1,0:T(8,128)(2,1)S(1)}, bf16[64,1536]{1,0:T(8,128)(2,1)S(1)}) custom-call(s32[1]{0:T(128)} %bitcast.5.me_ref, bf16[784,128]{1,0:T(8,128)(2,1)S(1)} %collective-permute-done.14.refs_0_, bf16[784,128]{1,0:T(8,128)(2,1)S(1)} %collective-permute-done.15.refs_1_, bf16[1536,768]{1,0:T(8,128)(2,1)S(1)} %bitcast.16, ...), custom_call_target="tpu_custom_call" | custom-call | flops 1811939328 | bytes 1179648 | tf_op jit(solution)/shard_map/hop2/experts/pallas_call | solution.py:287
  68.4 1.2 %collective-permute-start.25 = (bf16[64,1536]{1,0:T(8,128)(2,1)S(1)}, bf16[64,1536]{1,0:T(8,128)(2,1)S(1)}, u32[]{:S(2)}, u32[]{:S(2)}) collective-permute-start(bf16[64,1536]{1,0:T(8,128)(2,1)S(1)} %add_convert_fusion.6), channel_id=1, source_target_pairs={{4,0},{8,4},{12,8},{14,12},{10,14},{6,10},{2,6},{0,2},{5,1},{9,5},... | collective-permute-start | bytes 589832 | tf_op jit(solution)/shard_map/back_lead2/ppermute | solution.py:375
  69.6 1.0 %collective-permute-start.24 = (bf16[64,1536]{1,0:T(8,128)(2,1)S(1)}, bf16[64,1536]{1,0:T(8,128)(2,1)S(1)}, u32[]{:S(2)}, u32[]{:S(2)}) collective-permute-start(bf16[64,1536]{1,0:T(8,128)(2,1)S(1)} %add_convert_fusion.7), channel_id=1, source_target_pairs={{0,4},{4,8},{8,12},{12,14},{14,10},{10,6},{6,2},{2,0},{1,5},{5,9},... | collective-permute-start | bytes 589832 | tf_op jit(solution)/shard_map/back_lead2/ppermute | solution.py:375
  70.6 1.2 %collective-permute-done.30 = bf16[64,1536]{1,0:T(8,128)(2,1)S(1)} collective-permute-done((bf16[64,1536]{1,0:T(8,128)(2,1)S(1)}, bf16[64,1536]{1,0:T(8,128)(2,1)S(1)}, u32[]{:S(2)}, u32[]{:S(2)}) %collective-permute-start.30) | collective-permute-done | bytes 196640 | tf_op jit(solution)/shard_map/back_trail2/ppermute | solution.py:375
  72.2 1.7 %collective-permute-start.31 = (bf16[64,1536]{1,0:T(8,128)(2,1)S(1)}, bf16[64,1536]{1,0:T(8,128)(2,1)S(1)}, u32[]{:S(2)}, u32[]{:S(2)}) collective-permute-start(bf16[64,1536]{1,0:T(8,128)(2,1)S(1)} %add_convert_fusion.2), channel_id=1, source_target_pairs={{4,0},{8,4},{12,8},{14,12},{10,14},{6,10},{2,6},{0,2},{5,1},{9,5},... | collective-permute-start | bytes 589832 | tf_op jit(solution)/shard_map/back_trail1/ppermute | solution.py:375
  74.3 2.1 %experts.15 = (bf16[64,1536]{1,0:T(8,128)(2,1)S(1)}, bf16[64,1536]{1,0:T(8,128)(2,1)S(1)}) custom-call(s32[1]{0:T(128)} %bitcast.5.me_ref, bf16[784,128]{1,0:T(8,128)(2,1)S(1)} %collective-permute-done.12.refs_0_, bf16[784,128]{1,0:T(8,128)(2,1)S(1)} %collective-permute-done.13.refs_1_, bf16[1536,768]{1,0:T(8,128)(2,1)S(1)} %bitcast.17, ...), custom_call_target="tpu_custom_call" | custom-call | flops 1811939328 | bytes 1179648 | tf_op jit(solution)/shard_map/hop1/experts/pallas_call | solution.py:287
  76.5 1.5 %collective-permute-start.26 = (bf16[64,1536]{1,0:T(8,128)(2,1)S(1)}, bf16[64,1536]{1,0:T(8,128)(2,1)S(1)}, u32[]{:S(2)}, u32[]{:S(2)}) collective-permute-start(bf16[64,1536]{1,0:T(8,128)(2,1)S(1)} %add_convert_fusion.5), channel_id=1, source_target_pairs={{0,4},{4,8},{8,12},{12,14},{14,10},{10,6},{6,2},{2,0},{1,5},{5,9},... | collective-permute-start | bytes 589832 | tf_op jit(solution)/shard_map/back_lead1/ppermute | solution.py:375
  78.1 0.6 collective-permute-start.33
  78.7 3.5 %collective-permute-done.26 = bf16[64,1536]{1,0:T(8,128)(2,1)S(1)} collective-permute-done((bf16[64,1536]{1,0:T(8,128)(2,1)S(1)}, bf16[64,1536]{1,0:T(8,128)(2,1)S(1)}, u32[]{:S(2)}, u32[]{:S(2)}) %collective-permute-start.26) | collective-permute-done | bytes 196640 | tf_op jit(solution)/shard_map/back_lead1/ppermute | solution.py:375
  82.3 1.5 %collective-permute-done.33 = bf16[64,1536]{1,0:T(8,128)(2,1)S(1)} collective-permute-done((bf16[64,1536]{1,0:T(8,128)(2,1)S(1)}, bf16[64,1536]{1,0:T(8,128)(2,1)S(1)}, u32[]{:S(2)}, u32[]{:S(2)}) %collective-permute-start.33) | collective-permute-done | bytes 196640 | tf_op jit(solution)/shard_map/back_lead1/ppermute | solution.py:375
  83.9 0.8 fusion
  (61 shorter events, 3.2 us)
Async XLA Ops:
  0.0 15.5 %collective-permute-start.3 = (bf16[1536,768]{1,0:T(8,128)(2,1)}, bf16[1536,768]{1,0:T(8,128)(2,1)S(1)}, u32[]{:S(2)}, u32[]{:S(2)}) collective-permute-start(bf16[1536,768]{1,0:T(8,128)(2,1)} %bitcast.9), channel_id=1, source_target_pairs={{0,1},{1,0},{2,3},{3,2},{4,5},{5,4},{6,7},{7,6},{8,9},{9,8},{10,11... | collective-permute-start | bytes 7077896 | tf_op jit(solution)/shard_map/ppermute | solution.py:37
  0.5 15.1 %collective-permute-start.4 = (bf16[1536,768]{1,0:T(8,128)(2,1)}, bf16[1536,768]{1,0:T(8,128)(2,1)}, u32[]{:S(2)}, u32[]{:S(2)}) collective-permute-start(bf16[1536,768]{1,0:T(8,128)(2,1)} %bitcast.18), channel_id=1, source_target_pairs={{0,1},{1,0},{2,3},{3,2},{4,5},{5,4},{6,7},{7,6},{8,9},{9,8},{10,11... | collective-permute-start | bytes 7077896 | tf_op jit(solution)/shard_map/ppermute | solution.py:37
  0.5 15.1 %collective-permute-start.5 = (bf16[768,1536]{1,0:T(8,128)(2,1)}, bf16[768,1536]{1,0:T(8,128)(2,1)}, u32[]{:S(2)}, u32[]{:S(2)}) collective-permute-start(bf16[768,1536]{1,0:T(8,128)(2,1)} %bitcast.27), channel_id=1, source_target_pairs={{0,1},{1,0},{2,3},{3,2},{4,5},{5,4},{6,7},{7,6},{8,9},{9,8},{10,11... | collective-permute-start | bytes 7077896 | tf_op jit(solution)/shard_map/ppermute | solution.py:37
  1.0 8.7 %collective-permute-start = (bf16[256,128]{1,0:T(8,128)(2,1)}, bf16[256,128]{1,0:T(8,128)(2,1)S(1)}, u32[]{:S(2)}, u32[]{:S(2)}) collective-permute-start(bf16[256,128]{1,0:T(8,128)(2,1)} %refs_2_.1), channel_id=1, source_target_pairs={{0,2},{2,4},{4,6},{6,8},{8,10},{10,12},{12,14},{14,0},{1,3},{3,5},... | collective-permute-start | bytes 196616 | tf_op jit(solution)/shard_map/ppermute | solution.py:24
  3.5 7.4 %collective-permute-start.1 = (bf16[256,128]{1,0:T(8,128)(2,1)}, bf16[256,128]{1,0:T(8,128)(2,1)S(1)}, u32[]{:S(2)}, u32[]{:S(2)}) collective-permute-start(bf16[256,128]{1,0:T(8,128)(2,1)} %refs_3_.1), channel_id=1, source_target_pairs={{0,2},{2,4},{4,6},{6,8},{8,10},{10,12},{12,14},{14,0},{1,3},{3,5},... | collective-permute-start | bytes 196616 | tf_op jit(solution)/shard_map/ppermute | solution.py:24
  5.0 14.7 %copy-start.2 = (bf16[1,768,1536]{2,1,0:T(8,128)(2,1)S(1)}, bf16[1,768,1536]{2,1,0:T(8,128)(2,1)}, u32[]{:S(2)}) copy-start(bf16[1,768,1536]{2,1,0:T(8,128)(2,1)} %param.23) | copy-start | bytes 7077892
  8.0 5.5 %copy-start.7 = (f32[1536]{0:T(1024)S(1)}, f32[1536]{0:T(1024)}, u32[]{:S(2)}) copy-start(f32[1536]{0:T(1024)} %param.18) | copy-start | bytes 18436
  8.0 7.2 %copy-start.3 = (bf16[128,1536]{1,0:T(8,128)(2,1)S(1)}, bf16[128,1536]{1,0:T(8,128)(2,1)}, u32[]{:S(2)}) copy-start(bf16[128,1536]{1,0:T(8,128)(2,1)} %stream_ref.1) | copy-start | bytes 1179652
  8.0 7.2 %copy-start.4 = (s32[128,4]{0,1:T(4,128)S(1)}, s32[128,4]{0,1:T(4,128)}, u32[]{:S(2)}) copy-start(s32[128,4]{0,1:T(4,128)} %param.19) | copy-start | bytes 6148
  8.0 7.2 %copy-start.5 = (f32[128,4]{0,1:T(4,128)S(1)}, f32[128,4]{0,1:T(4,128)}, u32[]{:S(2)}) copy-start(f32[128,4]{0,1:T(4,128)} %param.20) | copy-start | bytes 6148
  10.9 8.8 %copy-start = (bf16[1,1536,768]{2,1,0:T(8,128)(2,1)S(1)}, bf16[1,1536,768]{2,1,0:T(8,128)(2,1)}, u32[]{:S(2)}) copy-start(bf16[1,1536,768]{2,1,0:T(8,128)(2,1)} %param.21) | copy-start | bytes 7077892
  10.9 8.8 %copy-start.1 = (bf16[1,1536,768]{2,1,0:T(8,128)(2,1)S(1)}, bf16[1,1536,768]{2,1,0:T(8,128)(2,1)}, u32[]{:S(2)}) copy-start(bf16[1,1536,768]{2,1,0:T(8,128)(2,1)} %param.22) | copy-start | bytes 7077892
  13.4 1.8 %collective-permute-start.2 = (bf16[128,1536]{1,0:T(8,128)(2,1)S(1)}, bf16[128,1536]{1,0:T(8,128)(2,1)S(1)}, u32[]{:S(2)}, u32[]{:S(2)}) collective-permute-start(bf16[128,1536]{1,0:T(8,128)(2,1)S(1)} %get-tuple-element.91), channel_id=1, source_target_pairs={{0,1},{1,0},{2,3},{3,2},{4,5},{5,4},{6,7},{7,6},{8,9},{9,8},{10,11... | collective-permute-start | bytes 1179656 | tf_op jit(solution)/shard_map/ppermute | solution.py:37
  15.5 4.1 %copy-start.6 = (bf16[1536,768]{1,0:T(8,128)(2,1)}, bf16[1536,768]{1,0:T(8,128)(2,1)S(1)}, u32[]{:S(2)}) copy-start(bf16[1536,768]{1,0:T(8,128)(2,1)S(1)} %collective-permute-done.3.refs_5_) | copy-start | bytes 7077892
  15.6 8.2 %collective-permute-start.6 = (bf16[784,128]{1,0:T(8,128)(2,1)S(1)}, bf16[784,128]{1,0:T(8,128)(2,1)S(1)}, u32[]{:S(2)}, u32[]{:S(2)}) collective-permute-start(bf16[784,128]{1,0:T(8,128)(2,1)S(1)} %get-tuple-element.98.refs_0_), channel_id=1, source_target_pairs={{0,4},{4,8},{8,12},{12,14},{14,10},{10,6},{6,2},{2,0},{1,5},{5,9},... | collective-permute-start | bytes 602120 | tf_op jit(solution)/shard_map/out_lead1/ppermute | solution.py:336
  15.6 8.2 %collective-permute-start.7 = (bf16[784,128]{1,0:T(8,128)(2,1)S(1)}, bf16[784,128]{1,0:T(8,128)(2,1)S(1)}, u32[]{:S(2)}, u32[]{:S(2)}) collective-permute-start(bf16[784,128]{1,0:T(8,128)(2,1)S(1)} %get-tuple-element.99.refs_1_), channel_id=1, source_target_pairs={{4,0},{8,4},{12,8},{14,12},{10,14},{6,10},{2,6},{0,2},{5,1},{9,5},... | collective-permute-start | bytes 602120 | tf_op jit(solution)/shard_map/out_lead1/ppermute | solution.py:336
  17.7 10.1 %collective-permute-start.12 = (bf16[784,128]{1,0:T(8,128)(2,1)S(1)}, bf16[784,128]{1,0:T(8,128)(2,1)S(1)}, u32[]{:S(2)}, u32[]{:S(2)}) collective-permute-start(bf16[784,128]{1,0:T(8,128)(2,1)S(1)} %get-tuple-element.99.refs_1_), channel_id=1, source_target_pairs={{0,4},{4,8},{8,12},{12,14},{14,10},{10,6},{6,2},{2,0},{1,5},{5,9},... | collective-permute-start | bytes 602120 | tf_op jit(solution)/shard_map/out_trail1/ppermute | solution.py:336
  17.7 10.1 %collective-permute-start.13 = (bf16[784,128]{1,0:T(8,128)(2,1)S(1)}, bf16[784,128]{1,0:T(8,128)(2,1)S(1)}, u32[]{:S(2)}, u32[]{:S(2)}) collective-permute-start(bf16[784,128]{1,0:T(8,128)(2,1)S(1)} %get-tuple-element.98.refs_0_), channel_id=1, source_target_pairs={{4,0},{8,4},{12,8},{14,12},{10,14},{6,10},{2,6},{0,2},{5,1},{9,5},... | collective-permute-start | bytes 602120 | tf_op jit(solution)/shard_map/out_trail1/ppermute | solution.py:336
  23.8 8.3 %collective-permute-start.8 = (bf16[784,128]{1,0:T(8,128)(2,1)S(1)}, bf16[784,128]{1,0:T(8,128)(2,1)S(1)}, u32[]{:S(2)}, u32[]{:S(2)}) collective-permute-start(bf16[784,128]{1,0:T(8,128)(2,1)S(1)} %collective-permute-done.6.refs_0_), channel_id=1, source_target_pairs={{0,4},{4,8},{8,12},{12,14},{14,10},{10,6},{6,2},{2,0},{1,5},{5,9},... | collective-permute-start | bytes 602120 | tf_op jit(solution)/shard_map/out_lead2/ppermute | solution.py:336
  24.8 7.9 %collective-permute-start.9 = (bf16[784,128]{1,0:T(8,128)(2,1)S(1)}, bf16[784,128]{1,0:T(8,128)(2,1)S(1)}, u32[]{:S(2)}, u32[]{:S(2)}) collective-permute-start(bf16[784,128]{1,0:T(8,128)(2,1)S(1)} %collective-permute-done.7.refs_1_), channel_id=1, source_target_pairs={{4,0},{8,4},{12,8},{14,12},{10,14},{6,10},{2,6},{0,2},{5,1},{9,5},... | collective-permute-start | bytes 602120 | tf_op jit(solution)/shard_map/out_lead2/ppermute | solution.py:336
  27.8 9.2 %collective-permute-start.15 = (bf16[784,128]{1,0:T(8,128)(2,1)S(1)}, bf16[784,128]{1,0:T(8,128)(2,1)S(1)}, u32[]{:S(2)}, u32[]{:S(2)}) collective-permute-start(bf16[784,128]{1,0:T(8,128)(2,1)S(1)} %collective-permute-done.13.refs_1_), channel_id=1, source_target_pairs={{4,0},{8,4},{12,8},{14,12},{10,14},{6,10},{2,6},{0,2},{5,1},{9,5},... | collective-permute-start | bytes 602120 | tf_op jit(solution)/shard_map/out_trail2/ppermute | solution.py:336
  29.8 7.2 %collective-permute-start.14 = (bf16[784,128]{1,0:T(8,128)(2,1)S(1)}, bf16[784,128]{1,0:T(8,128)(2,1)S(1)}, u32[]{:S(2)}, u32[]{:S(2)}) collective-permute-start(bf16[784,128]{1,0:T(8,128)(2,1)S(1)} %collective-permute-done.12.refs_0_), channel_id=1, source_target_pairs={{0,4},{4,8},{8,12},{12,14},{14,10},{10,6},{6,2},{2,0},{1,5},{5,9},... | collective-permute-start | bytes 602120 | tf_op jit(solution)/shard_map/out_trail2/ppermute | solution.py:336
  32.7 7.2 %collective-permute-start.11 = (bf16[784,128]{1,0:T(8,128)(2,1)S(1)}, bf16[784,128]{1,0:T(8,128)(2,1)S(1)}, u32[]{:S(2)}, u32[]{:S(2)}) collective-permute-start(bf16[784,128]{1,0:T(8,128)(2,1)S(1)} %collective-permute-done.9.refs_1_), channel_id=1, source_target_pairs={{4,0},{8,4},{12,8},{14,12},{10,14},{6,10},{2,6},{0,2},{5,1},{9,5},... | collective-permute-start | bytes 602120 | tf_op jit(solution)/shard_map/out_lead3/ppermute | solution.py:336
  34.1 5.8 %collective-permute-start.10 = (bf16[784,128]{1,0:T(8,128)(2,1)S(1)}, bf16[784,128]{1,0:T(8,128)(2,1)S(1)}, u32[]{:S(2)}, u32[]{:S(2)}) collective-permute-start(bf16[784,128]{1,0:T(8,128)(2,1)S(1)} %collective-permute-done.8.refs_0_), channel_id=1, source_target_pairs={{0,4},{4,8},{8,12},{12,14},{14,10},{10,6},{6,2},{2,0},{1,5},{5,9},... | collective-permute-start | bytes 602120 | tf_op jit(solution)/shard_map/out_lead3/ppermute | solution.py:336
  39.9 7.2 %collective-permute-start.16 = (bf16[784,128]{1,0:T(8,128)(2,1)S(1)}, bf16[784,128]{1,0:T(8,128)(2,1)S(1)}, u32[]{:S(2)}, u32[]{:S(2)}) collective-permute-start(bf16[784,128]{1,0:T(8,128)(2,1)S(1)} %collective-permute-done.10.refs_0_), channel_id=1, source_target_pairs={{0,4},{4,8},{8,12},{12,14},{14,10},{10,6},{6,2},{2,0},{1,5},{5,9},... | collective-permute-start | bytes 602120 | tf_op jit(solution)/shard_map/out_lead4/ppermute | solution.py:336
  40.9 6.8 %collective-permute-start.17 = (bf16[784,128]{1,0:T(8,128)(2,1)S(1)}, bf16[784,128]{1,0:T(8,128)(2,1)S(1)}, u32[]{:S(2)}, u32[]{:S(2)}) collective-permute-start(bf16[784,128]{1,0:T(8,128)(2,1)S(1)} %collective-permute-done.11.refs_1_), channel_id=1, source_target_pairs={{4,0},{8,4},{12,8},{14,12},{10,14},{6,10},{2,6},{0,2},{5,1},{9,5},... | collective-permute-start | bytes 602120 | tf_op jit(solution)/shard_map/out_lead4/ppermute | solution.py:336
  42.0 12.2 %collective-permute-start.21 = (bf16[784,128]{1,0:T(8,128)(2,1)S(1)}, bf16[784,128]{1,0:T(8,128)(2,1)S(1)}, u32[]{:S(2)}, u32[]{:S(2)}) collective-permute-start(bf16[784,128]{1,0:T(8,128)(2,1)S(1)} %collective-permute-done.15.refs_1_), channel_id=1, source_target_pairs={{4,0},{8,4},{12,8},{14,12},{10,14},{6,10},{2,6},{0,2},{5,1},{9,5},... | collective-permute-start | bytes 602120 | tf_op jit(solution)/shard_map/out_trail3/ppermute | solution.py:336
  43.6 8.4 %collective-permute-start.20 = (bf16[784,128]{1,0:T(8,128)(2,1)S(1)}, bf16[784,128]{1,0:T(8,128)(2,1)S(1)}, u32[]{:S(2)}, u32[]{:S(2)}) collective-permute-start(bf16[784,128]{1,0:T(8,128)(2,1)S(1)} %collective-permute-done.14.refs_0_), channel_id=1, source_target_pairs={{0,4},{4,8},{8,12},{12,14},{14,10},{10,6},{6,2},{2,0},{1,5},{5,9},... | collective-permute-start | bytes 602120 | tf_op jit(solution)/shard_map/out_trail3/ppermute | solution.py:336
  49.8 6.6 %collective-permute-start.18 = (bf16[64,1536]{1,0:T(8,128)(2,1)S(1)}, bf16[64,1536]{1,0:T(8,128)(2,1)S(1)}, u32[]{:S(2)}, u32[]{:S(2)}) collective-permute-start(bf16[64,1536]{1,0:T(8,128)(2,1)S(1)} %get-tuple-element.128), channel_id=1, source_target_pairs={{0,4},{4,8},{8,12},{12,14},{14,10},{10,6},{6,2},{2,0},{1,5},{5,9},... | collective-permute-start | bytes 589832 | tf_op jit(solution)/shard_map/back_lead4/ppermute | solution.py:375
  52.1 7.7 %collective-permute-start.19 = (bf16[64,1536]{1,0:T(8,128)(2,1)S(1)}, bf16[64,1536]{1,0:T(8,128)(2,1)S(1)}, u32[]{:S(2)}, u32[]{:S(2)}) collective-permute-start(bf16[64,1536]{1,0:T(8,128)(2,1)S(1)} %get-tuple-element.129), channel_id=1, source_target_pairs={{4,0},{8,4},{12,8},{14,12},{10,14},{6,10},{2,6},{0,2},{5,1},{9,5},... | collective-permute-start | bytes 589832 | tf_op jit(solution)/shard_map/back_lead4/ppermute | solution.py:375
  52.1 11.9 %collective-permute-start.28 = (bf16[64,1536]{1,0:T(8,128)(2,1)S(1)}, bf16[64,1536]{1,0:T(8,128)(2,1)S(1)}, u32[]{:S(2)}, u32[]{:S(2)}) collective-permute-start(bf16[64,1536]{1,0:T(8,128)(2,1)S(1)} %get-tuple-element.149), channel_id=1, source_target_pairs={{4,0},{8,4},{12,8},{14,12},{10,14},{6,10},{2,6},{0,2},{5,1},{9,5},... | collective-permute-start | bytes 589832 | tf_op jit(solution)/shard_map/back_trail3/ppermute | solution.py:375
  53.8 10.2 %collective-permute-start.27 = (bf16[64,1536]{1,0:T(8,128)(2,1)S(1)}, bf16[64,1536]{1,0:T(8,128)(2,1)S(1)}, u32[]{:S(2)}, u32[]{:S(2)}) collective-permute-start(bf16[64,1536]{1,0:T(8,128)(2,1)S(1)} %get-tuple-element.148), channel_id=1, source_target_pairs={{0,4},{4,8},{8,12},{12,14},{14,10},{10,6},{6,2},{2,0},{1,5},{5,9},... | collective-permute-start | bytes 589832 | tf_op jit(solution)/shard_map/back_trail3/ppermute | solution.py:375
  59.8 8.5 %collective-permute-start.23 = (bf16[64,1536]{1,0:T(8,128)(2,1)S(1)}, bf16[64,1536]{1,0:T(8,128)(2,1)S(1)}, u32[]{:S(2)}, u32[]{:S(2)}) collective-permute-start(bf16[64,1536]{1,0:T(8,128)(2,1)S(1)} %add_convert_fusion.8), channel_id=1, source_target_pairs={{4,0},{8,4},{12,8},{14,12},{10,14},{6,10},{2,6},{0,2},{5,1},{9,5},... | collective-permute-start | bytes 589832 | tf_op jit(solution)/shard_map/back_lead3/ppermute | solution.py:375
  60.0 8.4 %collective-permute-start.22 = (bf16[64,1536]{1,0:T(8,128)(2,1)S(1)}, bf16[64,1536]{1,0:T(8,128)(2,1)S(1)}, u32[]{:S(2)}, u32[]{:S(2)}) collective-permute-start(bf16[64,1536]{1,0:T(8,128)(2,1)S(1)} %add_convert_fusion.9), channel_id=1, source_target_pairs={{0,4},{4,8},{8,12},{12,14},{14,10},{10,6},{6,2},{2,0},{1,5},{5,9},... | collective-permute-start | bytes 589832 | tf_op jit(solution)/shard_map/back_lead3/ppermute | solution.py:375
  64.0 7.7 %collective-permute-start.30 = (bf16[64,1536]{1,0:T(8,128)(2,1)S(1)}, bf16[64,1536]{1,0:T(8,128)(2,1)S(1)}, u32[]{:S(2)}, u32[]{:S(2)}) collective-permute-start(bf16[64,1536]{1,0:T(8,128)(2,1)S(1)} %add_convert_fusion.3), channel_id=1, source_target_pairs={{4,0},{8,4},{12,8},{14,12},{10,14},{6,10},{2,6},{0,2},{5,1},{9,5},... | collective-permute-start | bytes 589832 | tf_op jit(solution)/shard_map/back_trail2/ppermute | solution.py:375
  64.2 7.9 %collective-permute-start.29 = (bf16[64,1536]{1,0:T(8,128)(2,1)S(1)}, bf16[64,1536]{1,0:T(8,128)(2,1)S(1)}, u32[]{:S(2)}, u32[]{:S(2)}) collective-permute-start(bf16[64,1536]{1,0:T(8,128)(2,1)S(1)} %add_convert_fusion.4), channel_id=1, source_target_pairs={{0,4},{4,8},{8,12},{12,14},{14,10},{10,6},{6,2},{2,0},{1,5},{5,9},... | collective-permute-start | bytes 589832 | tf_op jit(solution)/shard_map/back_trail2/ppermute | solution.py:375
  68.4 8.0 %collective-permute-start.25 = (bf16[64,1536]{1,0:T(8,128)(2,1)S(1)}, bf16[64,1536]{1,0:T(8,128)(2,1)S(1)}, u32[]{:S(2)}, u32[]{:S(2)}) collective-permute-start(bf16[64,1536]{1,0:T(8,128)(2,1)S(1)} %add_convert_fusion.6), channel_id=1, source_target_pairs={{4,0},{8,4},{12,8},{14,12},{10,14},{6,10},{2,6},{0,2},{5,1},{9,5},... | collective-permute-start | bytes 589832 | tf_op jit(solution)/shard_map/back_lead2/ppermute | solution.py:375
  69.6 6.8 %collective-permute-start.24 = (bf16[64,1536]{1,0:T(8,128)(2,1)S(1)}, bf16[64,1536]{1,0:T(8,128)(2,1)S(1)}, u32[]{:S(2)}, u32[]{:S(2)}) collective-permute-start(bf16[64,1536]{1,0:T(8,128)(2,1)S(1)} %add_convert_fusion.7), channel_id=1, source_target_pairs={{0,4},{4,8},{8,12},{12,14},{14,10},{10,6},{6,2},{2,0},{1,5},{5,9},... | collective-permute-start | bytes 589832 | tf_op jit(solution)/shard_map/back_lead2/ppermute | solution.py:375
  72.2 6.5 %collective-permute-start.31 = (bf16[64,1536]{1,0:T(8,128)(2,1)S(1)}, bf16[64,1536]{1,0:T(8,128)(2,1)S(1)}, u32[]{:S(2)}, u32[]{:S(2)}) collective-permute-start(bf16[64,1536]{1,0:T(8,128)(2,1)S(1)} %add_convert_fusion.2), channel_id=1, source_target_pairs={{4,0},{8,4},{12,8},{14,12},{10,14},{6,10},{2,6},{0,2},{5,1},{9,5},... | collective-permute-start | bytes 589832 | tf_op jit(solution)/shard_map/back_trail1/ppermute | solution.py:375
  73.9 8.4 %collective-permute-start.32 = (bf16[64,1536]{1,0:T(8,128)(2,1)S(1)}, bf16[64,1536]{1,0:T(8,128)(2,1)S(1)}, u32[]{:S(2)}, u32[]{:S(2)}) collective-permute-start(bf16[64,1536]{1,0:T(8,128)(2,1)S(1)} %add_convert_fusion.1), channel_id=1, source_target_pairs={{0,4},{4,8},{8,12},{12,14},{14,10},{10,6},{6,2},{2,0},{1,5},{5,9},... | collective-permute-start | bytes 589832 | tf_op jit(solution)/shard_map/back_trail1/ppermute | solution.py:375
  76.5 5.7 %collective-permute-start.26 = (bf16[64,1536]{1,0:T(8,128)(2,1)S(1)}, bf16[64,1536]{1,0:T(8,128)(2,1)S(1)}, u32[]{:S(2)}, u32[]{:S(2)}) collective-permute-start(bf16[64,1536]{1,0:T(8,128)(2,1)S(1)} %add_convert_fusion.5), channel_id=1, source_target_pairs={{0,4},{4,8},{8,12},{12,14},{14,10},{10,6},{6,2},{2,0},{1,5},{5,9},... | collective-permute-start | bytes 589832 | tf_op jit(solution)/shard_map/back_lead1/ppermute | solution.py:375
  78.1 5.7 %collective-permute-start.33 = (bf16[64,1536]{1,0:T(8,128)(2,1)S(1)}, bf16[64,1536]{1,0:T(8,128)(2,1)S(1)}, u32[]{:S(2)}, u32[]{:S(2)}) collective-permute-start(bf16[64,1536]{1,0:T(8,128)(2,1)S(1)} %add_convert_fusion), channel_id=1, source_target_pairs={{4,0},{8,4},{12,8},{14,12},{10,14},{6,10},{2,6},{0,2},{5,1},{9,5},... | collective-permute-start | bytes 589832 | tf_op jit(solution)/shard_map/back_lead1/ppermute | solution.py:375

commit v12 on v11

--- a/solution.py
+++ b/solution.py
@@ -352,7 +352,7 @@
         if distance < far:
             before = [came[side, distance - 1, side] for side in sides] if distance > 1 else []
             bring(distance, False, *before)
-            if 1 < distance < far - 1:
+            if distance > 1:
                 trails = [came[side, distance, 1 - side] for side in sides]
         latest = apply(distance, (True,), worked[distance - 1], *trails)
     latest = apply(far - 1, (False,), latest)
@@ -374,8 +374,8 @@
             with jax.named_scope(f"back_{'lead' if lead else 'trail'}{distance}"):
                 moving[side, piece] = lax.ppermute(value, "seq", hops[side])
 
+    send(far - 1, False)
     send(far, True)
-    send(far - 1, False, *[came[side, far, side] for side in sides])
     for distance in range(far - 1, 0, -1):
         leads = [moving[side, side] for side in sides]
         send(distance, True)

time: 84.8 us -> 84.1 us (level)
    ppermute x14, waiting for transfers between devices: 12 us -> 10.8 us  [send(): moving[side, piece] = lax.ppermute(value, 'seq', hops[side])]
where the time goes in v12:
time: 84.1 us; the launch traced here: 84 us
  starting transfers between devices  34.1 us (41%)
  Pallas kernels  24.6 us (29%)
  waiting for transfers between devices  23.4 us (28%)
  other arithmetic  1.45 us (2%)
    pallas_call x8, Pallas kernels, experts(): pl.pallas_call(functools.partial(expert_kernel, min(256, half), len(block...  18.8 us
    ppermute x14, starting transfers between devices, send(): moving[side, piece] = lax.ppermute(value, 'seq', hops[side])  14.8 us
    ppermute x14, starting transfers between devices, bring(): came[side, distance, piece] = lax.ppermute(block, 'seq', hops[side])  14.3 us
    ppermute x14, waiting for transfers between devices, send(): moving[side, piece] = lax.ppermute(value, 'seq', hops[side])  10.8 us
    ppermute x14, waiting for transfers between devices, bring(): came[side, distance, piece] = lax.ppermute(block, 'seq', hops[side])  8.11 us
    pallas_call x2, Pallas kernels, attend(): pl.pallas_call(functools.partial(attend_kernel, mix), in_specs=[vmem if m...  5.54 us
    ppermute x2, starting transfers between devices, shifted(): lax.ppermute(value, axis, [(i, (i + by) % peers) for i in range(peers)])  4.04 us
    ppermute x2, waiting for transfers between devices, shifted(): lax.ppermute(value, axis, [(i, (i + by) % peers) for i in range(peers)])  2.81 us
  transfers between devices with their start and end apart: 34, of which 18 were waited for; matrix products, arithmetic and copies ran while one was open for 1% of the time, Pallas kernels for 29%

profile of v12, /device:TPU:0, one launch (start us, length us, event | category | flops | bytes accessed | tf_op | source)
XLA Modules:
  0.0 84.0 jit_solution(6760432585640446813)
XLA Ops:
  1.0 2.5 %collective-permute-start = (bf16[256,128]{1,0:T(8,128)(2,1)}, bf16[256,128]{1,0:T(8,128)(2,1)S(1)}, u32[]{:S(2)}, u32[]{:S(2)}) collective-permute-start(bf16[256,128]{1,0:T(8,128)(2,1)} %refs_2_.1), channel_id=1, source_target_pairs={{0,2},{2,4},{4,6},{6,8},{8,10},{10,12},{12,14},{14,0},{1,3},{3,5},... | collective-permute-start | bytes 196616 | tf_op jit(solution)/shard_map/ppermute | solution.py:24
  3.5 1.5 %collective-permute-start.1 = (bf16[256,128]{1,0:T(8,128)(2,1)}, bf16[256,128]{1,0:T(8,128)(2,1)S(1)}, u32[]{:S(2)}, u32[]{:S(2)}) collective-permute-start(bf16[256,128]{1,0:T(8,128)(2,1)} %refs_3_.1), channel_id=1, source_target_pairs={{0,2},{2,4},{4,6},{6,8},{8,10},{10,12},{12,14},{14,0},{1,3},{3,5},... | collective-permute-start | bytes 196616 | tf_op jit(solution)/shard_map/ppermute | solution.py:24
  5.0 3.0 %attend.2 = (f32[1,16]{1,0:T(1,128)S(1)}, bf16[256,1024]{1,0:T(8,128)(2,1)S(1)}, bf16[256,128]{1,0:T(8,128)(2,1)S(1)}, bf16[256,128]{1,0:T(8,128)(2,1)S(1)}, bf1...) custom-call(f32[1,16]{1,0:T(1,128)} %bitcast.38, bf16[256,1024]{1,0:T(8,128)(2,1)} %refs_1_.1, ...), custom_call_target="tpu_custom_call" | custom-call | flops 671088640 | bytes 6291456 | tf_op jit(solution)/shard_map/attend/pallas_call | solution.py:151
  8.1 1.6 %collective-permute-done.refs_6_ = bf16[256,128]{1,0:T(8,128)(2,1)S(1)} collective-permute-done((bf16[256,128]{1,0:T(8,128)(2,1)}, bf16[256,128]{1,0:T(8,128)(2,1)S(1)}, u32[]{:S(2)}, u32[]{:S(2)}) %collective-permute-start) | collective-permute-done | bytes 65568 | tf_op jit(solution)/shard_map/ppermute | solution.py:24
  9.6 1.2 %collective-permute-done.1.refs_7_ = bf16[256,128]{1,0:T(8,128)(2,1)S(1)} collective-permute-done((bf16[256,128]{1,0:T(8,128)(2,1)}, bf16[256,128]{1,0:T(8,128)(2,1)S(1)}, u32[]{:S(2)}, u32[]{:S(2)}) %collective-permute-start.1) | collective-permute-done | bytes 65568 | tf_op jit(solution)/shard_map/ppermute | solution.py:24
  10.9 2.5 %attend.3 = (bf16[128,1536]{1,0:T(8,128)(2,1)S(1)}, f32[128,1536]{1,0:T(8,128)S(1)}) custom-call(f32[1,16]{1,0:T(1,128)S(1)} %get-tuple-element.82.refs_0_, bf16[256,1024]{1,0:T(8,128)(2,1)S(1)} %get-tuple-element.83.refs_1_, bf16[256,128]{1,0:T(8,128)(2,1)S(1)} %get-tuple-element.84.refs_2_, bf16[256,128]{1,0:T(8,128)(2,1)S(1)} %get-tuple-element.85.refs_3_, ...), custom_call_target="tpu_custom_call" | custom-call | flops 671088640 | bytes 6291456 | tf_op jit(solution)/shard_map/attend/pallas_call | solution.py:151
  13.5 1.7 %collective-permute-done.2.came_ref = bf16[128,1536]{1,0:T(8,128)(2,1)S(1)} collective-permute-done((bf16[128,1536]{1,0:T(8,128)(2,1)S(1)}, bf16[128,1536]{1,0:T(8,128)(2,1)S(1)}, u32[]{:S(2)}, u32[]{:S(2)}) %collective-permute-start.2) | collective-permute-done | bytes 393248 | tf_op jit(solution)/shard_map/ppermute | solution.py:37
  15.6 2.0 %collective-permute-start.7 = (bf16[784,128]{1,0:T(8,128)(2,1)S(1)}, bf16[784,128]{1,0:T(8,128)(2,1)S(1)}, u32[]{:S(2)}, u32[]{:S(2)}) collective-permute-start(bf16[784,128]{1,0:T(8,128)(2,1)S(1)} %get-tuple-element.97.refs_1_), channel_id=1, source_target_pairs={{4,0},{8,4},{12,8},{14,12},{10,14},{6,10},{2,6},{0,2},{5,1},{9,5},... | collective-permute-start | bytes 602120 | tf_op jit(solution)/shard_map/out_lead1/ppermute | solution.py:336
  17.7 2.0 %collective-permute-start.13 = (bf16[784,128]{1,0:T(8,128)(2,1)S(1)}, bf16[784,128]{1,0:T(8,128)(2,1)S(1)}, u32[]{:S(2)}, u32[]{:S(2)}) collective-permute-start(bf16[784,128]{1,0:T(8,128)(2,1)S(1)} %get-tuple-element.96.refs_0_), channel_id=1, source_target_pairs={{4,0},{8,4},{12,8},{14,12},{10,14},{6,10},{2,6},{0,2},{5,1},{9,5},... | collective-permute-start | bytes 602120 | tf_op jit(solution)/shard_map/out_trail1/ppermute | solution.py:336
  19.7 4.1 %experts.8 = (bf16[64,1536]{1,0:T(8,128)(2,1)S(1)}, bf16[64,1536]{1,0:T(8,128)(2,1)S(1)}, bf16[1536,768]{1,0:T(8,128)(2,1)S(1)}, bf16[1536,768]{1,0:T(8,128)(2,1)S(1)}, bf16[768,1536]{1,0:T(8,128)(2,1)S(1)}) custom-call(s32[1]{0:T(128)} %bitcast.5.me_ref, bf16[784,128]{1,0:T(8,128)(2,1)S(1)} %get-tuple-element.96.refs_0_, ...), custom_call_target="tpu_custom_call" | custom-call | flops 1811939328 | bytes 1179648 | tf_op jit(solution)/shard_map/experts/pallas_call | solution.py:287
  23.8 1.0 %collective-permute-start.8 = (bf16[784,128]{1,0:T(8,128)(2,1)S(1)}, bf16[784,128]{1,0:T(8,128)(2,1)S(1)}, u32[]{:S(2)}, u32[]{:S(2)}) collective-permute-start(bf16[784,128]{1,0:T(8,128)(2,1)S(1)} %collective-permute-done.6.refs_0_), channel_id=1, source_target_pairs={{0,4},{4,8},{8,12},{12,14},{14,10},{10,6},{6,2},{2,0},{1,5},{5,9},... | collective-permute-start | bytes 602120 | tf_op jit(solution)/shard_map/out_lead2/ppermute | solution.py:336
  24.8 1.1 %collective-permute-start.9 = (bf16[784,128]{1,0:T(8,128)(2,1)S(1)}, bf16[784,128]{1,0:T(8,128)(2,1)S(1)}, u32[]{:S(2)}, u32[]{:S(2)}) collective-permute-start(bf16[784,128]{1,0:T(8,128)(2,1)S(1)} %collective-permute-done.7.refs_1_), channel_id=1, source_target_pairs={{4,0},{8,4},{12,8},{14,12},{10,14},{6,10},{2,6},{0,2},{5,1},{9,5},... | collective-permute-start | bytes 602120 | tf_op jit(solution)/shard_map/out_lead2/ppermute | solution.py:336
  25.9 1.9 %collective-permute-done.12.refs_0_ = bf16[784,128]{1,0:T(8,128)(2,1)S(1)} collective-permute-done((bf16[784,128]{1,0:T(8,128)(2,1)S(1)}, bf16[784,128]{1,0:T(8,128)(2,1)S(1)}, u32[]{:S(2)}, u32[]{:S(2)}) %collective-permute-start.12) | collective-permute-done | bytes 200736 | tf_op jit(solution)/shard_map/out_trail1/ppermute | solution.py:336
  27.8 2.0 %collective-permute-start.15 = (bf16[784,128]{1,0:T(8,128)(2,1)S(1)}, bf16[784,128]{1,0:T(8,128)(2,1)S(1)}, u32[]{:S(2)}, u32[]{:S(2)}) collective-permute-start(bf16[784,128]{1,0:T(8,128)(2,1)S(1)} %collective-permute-done.13.refs_1_), channel_id=1, source_target_pairs={{4,0},{8,4},{12,8},{14,12},{10,14},{6,10},{2,6},{0,2},{5,1},{9,5},... | collective-permute-start | bytes 602120 | tf_op jit(solution)/shard_map/out_trail2/ppermute | solution.py:336
  29.9 2.1 %experts.9 = (bf16[64,1536]{1,0:T(8,128)(2,1)S(1)}, bf16[64,1536]{1,0:T(8,128)(2,1)S(1)}) custom-call(s32[1]{0:T(128)} %bitcast.5.me_ref, bf16[784,128]{1,0:T(8,128)(2,1)S(1)} %collective-permute-done.6.refs_0_, bf16[784,128]{1,0:T(8,128)(2,1)S(1)} %collective-permute-done.7.refs_1_, bf16[1536,768]{1,0:T(8,128)(2,1)S(1)} %bitcast.11, ...), custom_call_target="tpu_custom_call" | custom-call | flops 1811939328 | bytes 1179648 | tf_op jit(solution)/shard_map/hop1/experts/pallas_call | solution.py:287
  32.1 0.6 collective-permute-done.9.refs_1_
  32.7 1.4 %collective-permute-start.11 = (bf16[784,128]{1,0:T(8,128)(2,1)S(1)}, bf16[784,128]{1,0:T(8,128)(2,1)S(1)}, u32[]{:S(2)}, u32[]{:S(2)}) collective-permute-start(bf16[784,128]{1,0:T(8,128)(2,1)S(1)} %collective-permute-done.9.refs_1_), channel_id=1, source_target_pairs={{4,0},{8,4},{12,8},{14,12},{10,14},{6,10},{2,6},{0,2},{5,1},{9,5},... | collective-permute-start | bytes 602120 | tf_op jit(solution)/shard_map/out_lead3/ppermute | solution.py:336
  34.1 0.6 collective-permute-start.10
  34.7 2.3 %collective-permute-done.15.refs_1_ = bf16[784,128]{1,0:T(8,128)(2,1)S(1)} collective-permute-done((bf16[784,128]{1,0:T(8,128)(2,1)S(1)}, bf16[784,128]{1,0:T(8,128)(2,1)S(1)}, u32[]{:S(2)}, u32[]{:S(2)}) %collective-permute-start.15) | collective-permute-done | bytes 200736 | tf_op jit(solution)/shard_map/out_trail2/ppermute | solution.py:336
  37.0 1.4 %collective-permute-start.18 = (bf16[784,128]{1,0:T(8,128)(2,1)S(1)}, bf16[784,128]{1,0:T(8,128)(2,1)S(1)}, u32[]{:S(2)}, u32[]{:S(2)}) collective-permute-start(bf16[784,128]{1,0:T(8,128)(2,1)S(1)} %collective-permute-done.15.refs_1_), channel_id=1, source_target_pairs={{4,0},{8,4},{12,8},{14,12},{10,14},{6,10},{2,6},{0,2},{5,1},{9,5},... | collective-permute-start | bytes 602120 | tf_op jit(solution)/shard_map/out_trail3/ppermute | solution.py:336
  38.4 0.6 collective-permute-start.17
  39.0 2.1 %experts.10 = (bf16[64,1536]{1,0:T(8,128)(2,1)S(1)}, bf16[64,1536]{1,0:T(8,128)(2,1)S(1)}) custom-call(s32[1]{0:T(128)} %bitcast.5.me_ref, bf16[784,128]{1,0:T(8,128)(2,1)S(1)} %collective-permute-done.8.refs_0_, bf16[784,128]{1,0:T(8,128)(2,1)S(1)} %collective-permute-done.9.refs_1_, bf16[1536,768]{1,0:T(8,128)(2,1)S(1)} %bitcast.12, ...), custom_call_target="tpu_custom_call" | custom-call | flops 1811939328 | bytes 1179648 | tf_op jit(solution)/shard_map/hop2/experts/pallas_call | solution.py:287
  41.3 1.6 %collective-permute-start.16 = (bf16[784,128]{1,0:T(8,128)(2,1)S(1)}, bf16[784,128]{1,0:T(8,128)(2,1)S(1)}, u32[]{:S(2)}, u32[]{:S(2)}) collective-permute-start(bf16[784,128]{1,0:T(8,128)(2,1)S(1)} %collective-permute-done.10.refs_0_), channel_id=1, source_target_pairs={{0,4},{4,8},{8,12},{12,14},{14,10},{10,6},{6,2},{2,0},{1,5},{5,9},... | collective-permute-start | bytes 602120 | tf_op jit(solution)/shard_map/out_lead4/ppermute | solution.py:336
  43.3 2.3 %collective-permute-done.18.refs_1_ = bf16[784,128]{1,0:T(8,128)(2,1)S(1)} collective-permute-done((bf16[784,128]{1,0:T(8,128)(2,1)S(1)}, bf16[784,128]{1,0:T(8,128)(2,1)S(1)}, u32[]{:S(2)}, u32[]{:S(2)}) %collective-permute-start.18) | collective-permute-done | bytes 200736 | tf_op jit(solution)/shard_map/out_trail3/ppermute | solution.py:336
  45.6 0.7 collective-permute-done.17.refs_0_
  46.3 2.1 %experts.11 = (bf16[64,1536]{1,0:T(8,128)(2,1)S(1)}, bf16[64,1536]{1,0:T(8,128)(2,1)S(1)}) custom-call(s32[1]{0:T(128)} %bitcast.5.me_ref, bf16[784,128]{1,0:T(8,128)(2,1)S(1)} %collective-permute-done.10.refs_0_, bf16[784,128]{1,0:T(8,128)(2,1)S(1)} %collective-permute-done.11.refs_1_, bf16[1536,768]{1,0:T(8,128)(2,1)S(1)} %bitcast.13, ...), custom_call_target="tpu_custom_call" | custom-call | flops 1811939328 | bytes 1179648 | tf_op jit(solution)/shard_map/hop3/experts/pallas_call | solution.py:287
  48.4 0.6 collective-permute-start.27
  49.1 1.4 %collective-permute-start.28 = (bf16[64,1536]{1,0:T(8,128)(2,1)S(1)}, bf16[64,1536]{1,0:T(8,128)(2,1)S(1)}, u32[]{:S(2)}, u32[]{:S(2)}) collective-permute-start(bf16[64,1536]{1,0:T(8,128)(2,1)S(1)} %get-tuple-element.126), channel_id=1, source_target_pairs={{4,0},{8,4},{12,8},{14,12},{10,14},{6,10},{2,6},{0,2},{5,1},{9,5},... | collective-permute-start | bytes 589832 | tf_op jit(solution)/shard_map/back_trail3/ppermute | solution.py:375
  50.5 2.1 %experts.12 = (bf16[64,1536]{1,0:T(8,128)(2,1)S(1)}, bf16[64,1536]{1,0:T(8,128)(2,1)S(1)}) custom-call(s32[1]{0:T(128)} %bitcast.5.me_ref, bf16[784,128]{1,0:T(8,128)(2,1)S(1)} %collective-permute-done.16.refs_0_, bf16[784,128]{1,0:T(8,128)(2,1)S(1)} %collective-permute-done.19.refs_1_, bf16[1536,768]{1,0:T(8,128)(2,1)S(1)} %bitcast.14, ...), custom_call_target="tpu_custom_call" | custom-call | flops 1811939328 | bytes 1179648 | tf_op jit(solution)/shard_map/hop4/experts/pallas_call | solution.py:287
  52.6 0.6 collective-permute-start.20
  53.3 1.4 %collective-permute-start.21 = (bf16[64,1536]{1,0:T(8,128)(2,1)S(1)}, bf16[64,1536]{1,0:T(8,128)(2,1)S(1)}, u32[]{:S(2)}, u32[]{:S(2)}) collective-permute-start(bf16[64,1536]{1,0:T(8,128)(2,1)S(1)} %get-tuple-element.131), channel_id=1, source_target_pairs={{4,0},{8,4},{12,8},{14,12},{10,14},{6,10},{2,6},{0,2},{5,1},{9,5},... | collective-permute-start | bytes 589832 | tf_op jit(solution)/shard_map/back_lead4/ppermute | solution.py:375
  54.7 1.4 %collective-permute-done.27 = bf16[64,1536]{1,0:T(8,128)(2,1)S(1)} collective-permute-done((bf16[64,1536]{1,0:T(8,128)(2,1)S(1)}, bf16[64,1536]{1,0:T(8,128)(2,1)S(1)}, u32[]{:S(2)}, u32[]{:S(2)}) %collective-permute-start.27) | collective-permute-done | bytes 196640 | tf_op jit(solution)/shard_map/back_trail3/ppermute | solution.py:375
  56.1 2.1 %experts.13 = (bf16[64,1536]{1,0:T(8,128)(2,1)S(1)}, bf16[64,1536]{1,0:T(8,128)(2,1)S(1)}) custom-call(s32[1]{0:T(128)} %bitcast.5.me_ref, bf16[784,128]{1,0:T(8,128)(2,1)S(1)} %collective-permute-done.17.refs_0_, bf16[784,128]{1,0:T(8,128)(2,1)S(1)} %collective-permute-done.18.refs_1_, bf16[1536,768]{1,0:T(8,128)(2,1)S(1)} %bitcast.15, ...), custom_call_target="tpu_custom_call" | custom-call | flops 1811939328 | bytes 1179648 | tf_op jit(solution)/shard_map/hop3/experts/pallas_call | solution.py:287
  58.4 0.6 collective-permute-done.21
  59.0 1.5 %collective-permute-start.23 = (bf16[64,1536]{1,0:T(8,128)(2,1)S(1)}, bf16[64,1536]{1,0:T(8,128)(2,1)S(1)}, u32[]{:S(2)}, u32[]{:S(2)}) collective-permute-start(bf16[64,1536]{1,0:T(8,128)(2,1)S(1)} %add_convert_fusion.8), channel_id=1, source_target_pairs={{4,0},{8,4},{12,8},{14,12},{10,14},{6,10},{2,6},{0,2},{5,1},{9,5},... | collective-permute-start | bytes 589832 | tf_op jit(solution)/shard_map/back_lead3/ppermute | solution.py:375
  60.5 0.6 collective-permute-start.22
  61.2 1.5 %collective-permute-start.30 = (bf16[64,1536]{1,0:T(8,128)(2,1)S(1)}, bf16[64,1536]{1,0:T(8,128)(2,1)S(1)}, u32[]{:S(2)}, u32[]{:S(2)}) collective-permute-start(bf16[64,1536]{1,0:T(8,128)(2,1)S(1)} %add_convert_fusion.3), channel_id=1, source_target_pairs={{4,0},{8,4},{12,8},{14,12},{10,14},{6,10},{2,6},{0,2},{5,1},{9,5},... | collective-permute-start | bytes 589832 | tf_op jit(solution)/shard_map/back_trail2/ppermute | solution.py:375
  62.8 0.6 collective-permute-start.29
  63.4 2.1 %experts.14 = (bf16[64,1536]{1,0:T(8,128)(2,1)S(1)}, bf16[64,1536]{1,0:T(8,128)(2,1)S(1)}) custom-call(s32[1]{0:T(128)} %bitcast.5.me_ref, bf16[784,128]{1,0:T(8,128)(2,1)S(1)} %collective-permute-done.14.refs_0_, bf16[784,128]{1,0:T(8,128)(2,1)S(1)} %collective-permute-done.15.refs_1_, bf16[1536,768]{1,0:T(8,128)(2,1)S(1)} %bitcast.16, ...), custom_call_target="tpu_custom_call" | custom-call | flops 1811939328 | bytes 1179648 | tf_op jit(solution)/shard_map/hop2/experts/pallas_call | solution.py:287
  65.5 1.8 %collective-permute-done.22 = bf16[64,1536]{1,0:T(8,128)(2,1)S(1)} collective-permute-done((bf16[64,1536]{1,0:T(8,128)(2,1)S(1)}, bf16[64,1536]{1,0:T(8,128)(2,1)S(1)}, u32[]{:S(2)}, u32[]{:S(2)}) %collective-permute-start.22) | collective-permute-done | bytes 196640 | tf_op jit(solution)/shard_map/back_lead3/ppermute | solution.py:375
  67.4 1.9 %collective-permute-start.25 = (bf16[64,1536]{1,0:T(8,128)(2,1)S(1)}, bf16[64,1536]{1,0:T(8,128)(2,1)S(1)}, u32[]{:S(2)}, u32[]{:S(2)}) collective-permute-start(bf16[64,1536]{1,0:T(8,128)(2,1)S(1)} %add_convert_fusion.6), channel_id=1, source_target_pairs={{4,0},{8,4},{12,8},{14,12},{10,14},{6,10},{2,6},{0,2},{5,1},{9,5},... | collective-permute-start | bytes 589832 | tf_op jit(solution)/shard_map/back_lead2/ppermute | solution.py:375
  69.6 2.0 %collective-permute-done.29 = bf16[64,1536]{1,0:T(8,128)(2,1)S(1)} collective-permute-done((bf16[64,1536]{1,0:T(8,128)(2,1)S(1)}, bf16[64,1536]{1,0:T(8,128)(2,1)S(1)}, u32[]{:S(2)}, u32[]{:S(2)}) %collective-permute-start.29) | collective-permute-done | bytes 196640 | tf_op jit(solution)/shard_map/back_trail2/ppermute | solution.py:375
  71.6 1.9 %collective-permute-start.31 = (bf16[64,1536]{1,0:T(8,128)(2,1)S(1)}, bf16[64,1536]{1,0:T(8,128)(2,1)S(1)}, u32[]{:S(2)}, u32[]{:S(2)}) collective-permute-start(bf16[64,1536]{1,0:T(8,128)(2,1)S(1)} %add_convert_fusion.2), channel_id=1, source_target_pairs={{4,0},{8,4},{12,8},{14,12},{10,14},{6,10},{2,6},{0,2},{5,1},{9,5},... | collective-permute-start | bytes 589832 | tf_op jit(solution)/shard_map/back_trail1/ppermute | solution.py:375
  73.8 2.1 %experts.15 = (bf16[64,1536]{1,0:T(8,128)(2,1)S(1)}, bf16[64,1536]{1,0:T(8,128)(2,1)S(1)}) custom-call(s32[1]{0:T(128)} %bitcast.5.me_ref, bf16[784,128]{1,0:T(8,128)(2,1)S(1)} %collective-permute-done.12.refs_0_, bf16[784,128]{1,0:T(8,128)(2,1)S(1)} %collective-permute-done.13.refs_1_, bf16[1536,768]{1,0:T(8,128)(2,1)S(1)} %bitcast.17, ...), custom_call_target="tpu_custom_call" | custom-call | flops 1811939328 | bytes 1179648 | tf_op jit(solution)/shard_map/hop1/experts/pallas_call | solution.py:287
  75.9 1.3 %collective-permute-done.24 = bf16[64,1536]{1,0:T(8,128)(2,1)S(1)} collective-permute-done((bf16[64,1536]{1,0:T(8,128)(2,1)S(1)}, bf16[64,1536]{1,0:T(8,128)(2,1)S(1)}, u32[]{:S(2)}, u32[]{:S(2)}) %collective-permute-start.24) | collective-permute-done | bytes 196640 | tf_op jit(solution)/shard_map/back_lead2/ppermute | solution.py:375
  77.4 2.1 %collective-permute-start.33 = (bf16[64,1536]{1,0:T(8,128)(2,1)S(1)}, bf16[64,1536]{1,0:T(8,128)(2,1)S(1)}, u32[]{:S(2)}, u32[]{:S(2)}) collective-permute-start(bf16[64,1536]{1,0:T(8,128)(2,1)S(1)} %add_convert_fusion), channel_id=1, source_target_pairs={{4,0},{8,4},{12,8},{14,12},{10,14},{6,10},{2,6},{0,2},{5,1},{9,5},... | collective-permute-start | bytes 589832 | tf_op jit(solution)/shard_map/back_lead1/ppermute | solution.py:375
  79.4 3.5 %collective-permute-done.26 = bf16[64,1536]{1,0:T(8,128)(2,1)S(1)} collective-permute-done((bf16[64,1536]{1,0:T(8,128)(2,1)S(1)}, bf16[64,1536]{1,0:T(8,128)(2,1)S(1)}, u32[]{:S(2)}, u32[]{:S(2)}) %collective-permute-start.26) | collective-permute-done | bytes 196640 | tf_op jit(solution)/shard_map/back_lead1/ppermute | solution.py:375
  83.2 0.8 fusion
  (61 shorter events, 3.8 us)
Async XLA Ops:
  0.0 15.5 %collective-permute-start.3 = (bf16[1536,768]{1,0:T(8,128)(2,1)}, bf16[1536,768]{1,0:T(8,128)(2,1)S(1)}, u32[]{:S(2)}, u32[]{:S(2)}) collective-permute-start(bf16[1536,768]{1,0:T(8,128)(2,1)} %bitcast.9), channel_id=1, source_target_pairs={{0,1},{1,0},{2,3},{3,2},{4,5},{5,4},{6,7},{7,6},{8,9},{9,8},{10,11... | collective-permute-start | bytes 7077896 | tf_op jit(solution)/shard_map/ppermute | solution.py:37
  0.5 15.1 %collective-permute-start.4 = (bf16[1536,768]{1,0:T(8,128)(2,1)}, bf16[1536,768]{1,0:T(8,128)(2,1)}, u32[]{:S(2)}, u32[]{:S(2)}) collective-permute-start(bf16[1536,768]{1,0:T(8,128)(2,1)} %bitcast.18), channel_id=1, source_target_pairs={{0,1},{1,0},{2,3},{3,2},{4,5},{5,4},{6,7},{7,6},{8,9},{9,8},{10,11... | collective-permute-start | bytes 7077896 | tf_op jit(solution)/shard_map/ppermute | solution.py:37
  0.5 15.1 %collective-permute-start.5 = (bf16[768,1536]{1,0:T(8,128)(2,1)}, bf16[768,1536]{1,0:T(8,128)(2,1)}, u32[]{:S(2)}, u32[]{:S(2)}) collective-permute-start(bf16[768,1536]{1,0:T(8,128)(2,1)} %bitcast.27), channel_id=1, source_target_pairs={{0,1},{1,0},{2,3},{3,2},{4,5},{5,4},{6,7},{7,6},{8,9},{9,8},{10,11... | collective-permute-start | bytes 7077896 | tf_op jit(solution)/shard_map/ppermute | solution.py:37
  1.0 8.7 %collective-permute-start = (bf16[256,128]{1,0:T(8,128)(2,1)}, bf16[256,128]{1,0:T(8,128)(2,1)S(1)}, u32[]{:S(2)}, u32[]{:S(2)}) collective-permute-start(bf16[256,128]{1,0:T(8,128)(2,1)} %refs_2_.1), channel_id=1, source_target_pairs={{0,2},{2,4},{4,6},{6,8},{8,10},{10,12},{12,14},{14,0},{1,3},{3,5},... | collective-permute-start | bytes 196616 | tf_op jit(solution)/shard_map/ppermute | solution.py:24
  3.5 7.4 %collective-permute-start.1 = (bf16[256,128]{1,0:T(8,128)(2,1)}, bf16[256,128]{1,0:T(8,128)(2,1)S(1)}, u32[]{:S(2)}, u32[]{:S(2)}) collective-permute-start(bf16[256,128]{1,0:T(8,128)(2,1)} %refs_3_.1), channel_id=1, source_target_pairs={{0,2},{2,4},{4,6},{6,8},{8,10},{10,12},{12,14},{14,0},{1,3},{3,5},... | collective-permute-start | bytes 196616 | tf_op jit(solution)/shard_map/ppermute | solution.py:24
  5.0 14.7 %copy-start.2 = (bf16[1,768,1536]{2,1,0:T(8,128)(2,1)S(1)}, bf16[1,768,1536]{2,1,0:T(8,128)(2,1)}, u32[]{:S(2)}) copy-start(bf16[1,768,1536]{2,1,0:T(8,128)(2,1)} %param.23) | copy-start | bytes 7077892
  8.0 5.5 %copy-start.7 = (f32[1536]{0:T(1024)S(1)}, f32[1536]{0:T(1024)}, u32[]{:S(2)}) copy-start(f32[1536]{0:T(1024)} %param.18) | copy-start | bytes 18436
  8.0 7.2 %copy-start.3 = (bf16[128,1536]{1,0:T(8,128)(2,1)S(1)}, bf16[128,1536]{1,0:T(8,128)(2,1)}, u32[]{:S(2)}) copy-start(bf16[128,1536]{1,0:T(8,128)(2,1)} %stream_ref.1) | copy-start | bytes 1179652
  8.0 7.2 %copy-start.4 = (s32[128,4]{0,1:T(4,128)S(1)}, s32[128,4]{0,1:T(4,128)}, u32[]{:S(2)}) copy-start(s32[128,4]{0,1:T(4,128)} %param.19) | copy-start | bytes 6148
  8.0 7.2 %copy-start.5 = (f32[128,4]{0,1:T(4,128)S(1)}, f32[128,4]{0,1:T(4,128)}, u32[]{:S(2)}) copy-start(f32[128,4]{0,1:T(4,128)} %param.20) | copy-start | bytes 6148
  10.9 8.8 %copy-start = (bf16[1,1536,768]{2,1,0:T(8,128)(2,1)S(1)}, bf16[1,1536,768]{2,1,0:T(8,128)(2,1)}, u32[]{:S(2)}) copy-start(bf16[1,1536,768]{2,1,0:T(8,128)(2,1)} %param.21) | copy-start | bytes 7077892
  10.9 8.8 %copy-start.1 = (bf16[1,1536,768]{2,1,0:T(8,128)(2,1)S(1)}, bf16[1,1536,768]{2,1,0:T(8,128)(2,1)}, u32[]{:S(2)}) copy-start(bf16[1,1536,768]{2,1,0:T(8,128)(2,1)} %param.22) | copy-start | bytes 7077892
  13.4 1.8 %collective-permute-start.2 = (bf16[128,1536]{1,0:T(8,128)(2,1)S(1)}, bf16[128,1536]{1,0:T(8,128)(2,1)S(1)}, u32[]{:S(2)}, u32[]{:S(2)}) collective-permute-start(bf16[128,1536]{1,0:T(8,128)(2,1)S(1)} %get-tuple-element.89), channel_id=1, source_target_pairs={{0,1},{1,0},{2,3},{3,2},{4,5},{5,4},{6,7},{7,6},{8,9},{9,8},{10,11... | collective-permute-start | bytes 1179656 | tf_op jit(solution)/shard_map/ppermute | solution.py:37
  15.5 4.1 %copy-start.6 = (bf16[1536,768]{1,0:T(8,128)(2,1)}, bf16[1536,768]{1,0:T(8,128)(2,1)S(1)}, u32[]{:S(2)}) copy-start(bf16[1536,768]{1,0:T(8,128)(2,1)S(1)} %collective-permute-done.3.refs_5_) | copy-start | bytes 7077892
  15.6 8.2 %collective-permute-start.6 = (bf16[784,128]{1,0:T(8,128)(2,1)S(1)}, bf16[784,128]{1,0:T(8,128)(2,1)S(1)}, u32[]{:S(2)}, u32[]{:S(2)}) collective-permute-start(bf16[784,128]{1,0:T(8,128)(2,1)S(1)} %get-tuple-element.96.refs_0_), channel_id=1, source_target_pairs={{0,4},{4,8},{8,12},{12,14},{14,10},{10,6},{6,2},{2,0},{1,5},{5,9},... | collective-permute-start | bytes 602120 | tf_op jit(solution)/shard_map/out_lead1/ppermute | solution.py:336
  15.6 8.2 %collective-permute-start.7 = (bf16[784,128]{1,0:T(8,128)(2,1)S(1)}, bf16[784,128]{1,0:T(8,128)(2,1)S(1)}, u32[]{:S(2)}, u32[]{:S(2)}) collective-permute-start(bf16[784,128]{1,0:T(8,128)(2,1)S(1)} %get-tuple-element.97.refs_1_), channel_id=1, source_target_pairs={{4,0},{8,4},{12,8},{14,12},{10,14},{6,10},{2,6},{0,2},{5,1},{9,5},... | collective-permute-start | bytes 602120 | tf_op jit(solution)/shard_map/out_lead1/ppermute | solution.py:336
  17.7 10.1 %collective-permute-start.12 = (bf16[784,128]{1,0:T(8,128)(2,1)S(1)}, bf16[784,128]{1,0:T(8,128)(2,1)S(1)}, u32[]{:S(2)}, u32[]{:S(2)}) collective-permute-start(bf16[784,128]{1,0:T(8,128)(2,1)S(1)} %get-tuple-element.97.refs_1_), channel_id=1, source_target_pairs={{0,4},{4,8},{8,12},{12,14},{14,10},{10,6},{6,2},{2,0},{1,5},{5,9},... | collective-permute-start | bytes 602120 | tf_op jit(solution)/shard_map/out_trail1/ppermute | solution.py:336
  17.7 10.1 %collective-permute-start.13 = (bf16[784,128]{1,0:T(8,128)(2,1)S(1)}, bf16[784,128]{1,0:T(8,128)(2,1)S(1)}, u32[]{:S(2)}, u32[]{:S(2)}) collective-permute-start(bf16[784,128]{1,0:T(8,128)(2,1)S(1)} %get-tuple-element.96.refs_0_), channel_id=1, source_target_pairs={{4,0},{8,4},{12,8},{14,12},{10,14},{6,10},{2,6},{0,2},{5,1},{9,5},... | collective-permute-start | bytes 602120 | tf_op jit(solution)/shard_map/out_trail1/ppermute | solution.py:336
  23.8 8.3 %collective-permute-start.8 = (bf16[784,128]{1,0:T(8,128)(2,1)S(1)}, bf16[784,128]{1,0:T(8,128)(2,1)S(1)}, u32[]{:S(2)}, u32[]{:S(2)}) collective-permute-start(bf16[784,128]{1,0:T(8,128)(2,1)S(1)} %collective-permute-done.6.refs_0_), channel_id=1, source_target_pairs={{0,4},{4,8},{8,12},{12,14},{14,10},{10,6},{6,2},{2,0},{1,5},{5,9},... | collective-permute-start | bytes 602120 | tf_op jit(solution)/shard_map/out_lead2/ppermute | solution.py:336
  24.8 7.9 %collective-permute-start.9 = (bf16[784,128]{1,0:T(8,128)(2,1)S(1)}, bf16[784,128]{1,0:T(8,128)(2,1)S(1)}, u32[]{:S(2)}, u32[]{:S(2)}) collective-permute-start(bf16[784,128]{1,0:T(8,128)(2,1)S(1)} %collective-permute-done.7.refs_1_), channel_id=1, source_target_pairs={{4,0},{8,4},{12,8},{14,12},{10,14},{6,10},{2,6},{0,2},{5,1},{9,5},... | collective-permute-start | bytes 602120 | tf_op jit(solution)/shard_map/out_lead2/ppermute | solution.py:336
  27.8 9.2 %collective-permute-start.15 = (bf16[784,128]{1,0:T(8,128)(2,1)S(1)}, bf16[784,128]{1,0:T(8,128)(2,1)S(1)}, u32[]{:S(2)}, u32[]{:S(2)}) collective-permute-start(bf16[784,128]{1,0:T(8,128)(2,1)S(1)} %collective-permute-done.13.refs_1_), channel_id=1, source_target_pairs={{4,0},{8,4},{12,8},{14,12},{10,14},{6,10},{2,6},{0,2},{5,1},{9,5},... | collective-permute-start | bytes 602120 | tf_op jit(solution)/shard_map/out_trail2/ppermute | solution.py:336
  29.8 7.2 %collective-permute-start.14 = (bf16[784,128]{1,0:T(8,128)(2,1)S(1)}, bf16[784,128]{1,0:T(8,128)(2,1)S(1)}, u32[]{:S(2)}, u32[]{:S(2)}) collective-permute-start(bf16[784,128]{1,0:T(8,128)(2,1)S(1)} %collective-permute-done.12.refs_0_), channel_id=1, source_target_pairs={{0,4},{4,8},{8,12},{12,14},{14,10},{10,6},{6,2},{2,0},{1,5},{5,9},... | collective-permute-start | bytes 602120 | tf_op jit(solution)/shard_map/out_trail2/ppermute | solution.py:336
  32.7 8.6 %collective-permute-start.11 = (bf16[784,128]{1,0:T(8,128)(2,1)S(1)}, bf16[784,128]{1,0:T(8,128)(2,1)S(1)}, u32[]{:S(2)}, u32[]{:S(2)}) collective-permute-start(bf16[784,128]{1,0:T(8,128)(2,1)S(1)} %collective-permute-done.9.refs_1_), channel_id=1, source_target_pairs={{4,0},{8,4},{12,8},{14,12},{10,14},{6,10},{2,6},{0,2},{5,1},{9,5},... | collective-permute-start | bytes 602120 | tf_op jit(solution)/shard_map/out_lead3/ppermute | solution.py:336
  34.1 7.2 %collective-permute-start.10 = (bf16[784,128]{1,0:T(8,128)(2,1)S(1)}, bf16[784,128]{1,0:T(8,128)(2,1)S(1)}, u32[]{:S(2)}, u32[]{:S(2)}) collective-permute-start(bf16[784,128]{1,0:T(8,128)(2,1)S(1)} %collective-permute-done.8.refs_0_), channel_id=1, source_target_pairs={{0,4},{4,8},{8,12},{12,14},{14,10},{10,6},{6,2},{2,0},{1,5},{5,9},... | collective-permute-start | bytes 602120 | tf_op jit(solution)/shard_map/out_lead3/ppermute | solution.py:336
  37.0 8.6 %collective-permute-start.18 = (bf16[784,128]{1,0:T(8,128)(2,1)S(1)}, bf16[784,128]{1,0:T(8,128)(2,1)S(1)}, u32[]{:S(2)}, u32[]{:S(2)}) collective-permute-start(bf16[784,128]{1,0:T(8,128)(2,1)S(1)} %collective-permute-done.15.refs_1_), channel_id=1, source_target_pairs={{4,0},{8,4},{12,8},{14,12},{10,14},{6,10},{2,6},{0,2},{5,1},{9,5},... | collective-permute-start | bytes 602120 | tf_op jit(solution)/shard_map/out_trail3/ppermute | solution.py:336
  38.4 7.9 %collective-permute-start.17 = (bf16[784,128]{1,0:T(8,128)(2,1)S(1)}, bf16[784,128]{1,0:T(8,128)(2,1)S(1)}, u32[]{:S(2)}, u32[]{:S(2)}) collective-permute-start(bf16[784,128]{1,0:T(8,128)(2,1)S(1)} %collective-permute-done.14.refs_0_), channel_id=1, source_target_pairs={{0,4},{4,8},{8,12},{12,14},{14,10},{10,6},{6,2},{2,0},{1,5},{5,9},... | collective-permute-start | bytes 602120 | tf_op jit(solution)/shard_map/out_trail3/ppermute | solution.py:336
  41.3 9.2 %collective-permute-start.16 = (bf16[784,128]{1,0:T(8,128)(2,1)S(1)}, bf16[784,128]{1,0:T(8,128)(2,1)S(1)}, u32[]{:S(2)}, u32[]{:S(2)}) collective-permute-start(bf16[784,128]{1,0:T(8,128)(2,1)S(1)} %collective-permute-done.10.refs_0_), channel_id=1, source_target_pairs={{0,4},{4,8},{8,12},{12,14},{14,10},{10,6},{6,2},{2,0},{1,5},{5,9},... | collective-permute-start | bytes 602120 | tf_op jit(solution)/shard_map/out_lead4/ppermute | solution.py:336
  42.9 7.6 %collective-permute-start.19 = (bf16[784,128]{1,0:T(8,128)(2,1)S(1)}, bf16[784,128]{1,0:T(8,128)(2,1)S(1)}, u32[]{:S(2)}, u32[]{:S(2)}) collective-permute-start(bf16[784,128]{1,0:T(8,128)(2,1)S(1)} %collective-permute-done.11.refs_1_), channel_id=1, source_target_pairs={{4,0},{8,4},{12,8},{14,12},{10,14},{6,10},{2,6},{0,2},{5,1},{9,5},... | collective-permute-start | bytes 602120 | tf_op jit(solution)/shard_map/out_lead4/ppermute | solution.py:336
  48.4 7.7 %collective-permute-start.27 = (bf16[64,1536]{1,0:T(8,128)(2,1)S(1)}, bf16[64,1536]{1,0:T(8,128)(2,1)S(1)}, u32[]{:S(2)}, u32[]{:S(2)}) collective-permute-start(bf16[64,1536]{1,0:T(8,128)(2,1)S(1)} %get-tuple-element.145), channel_id=1, source_target_pairs={{0,4},{4,8},{8,12},{12,14},{14,10},{10,6},{6,2},{2,0},{1,5},{5,9},... | collective-permute-start | bytes 589832 | tf_op jit(solution)/shard_map/back_trail3/ppermute | solution.py:375
  49.1 7.1 %collective-permute-start.28 = (bf16[64,1536]{1,0:T(8,128)(2,1)S(1)}, bf16[64,1536]{1,0:T(8,128)(2,1)S(1)}, u32[]{:S(2)}, u32[]{:S(2)}) collective-permute-start(bf16[64,1536]{1,0:T(8,128)(2,1)S(1)} %get-tuple-element.126), channel_id=1, source_target_pairs={{4,0},{8,4},{12,8},{14,12},{10,14},{6,10},{2,6},{0,2},{5,1},{9,5},... | collective-permute-start | bytes 589832 | tf_op jit(solution)/shard_map/back_trail3/ppermute | solution.py:375
  52.6 5.7 %collective-permute-start.20 = (bf16[64,1536]{1,0:T(8,128)(2,1)S(1)}, bf16[64,1536]{1,0:T(8,128)(2,1)S(1)}, u32[]{:S(2)}, u32[]{:S(2)}) collective-permute-start(bf16[64,1536]{1,0:T(8,128)(2,1)S(1)} %get-tuple-element.130), channel_id=1, source_target_pairs={{0,4},{4,8},{8,12},{12,14},{14,10},{10,6},{6,2},{2,0},{1,5},{5,9},... | collective-permute-start | bytes 589832 | tf_op jit(solution)/shard_map/back_lead4/ppermute | solution.py:375
  53.3 5.7 %collective-permute-start.21 = (bf16[64,1536]{1,0:T(8,128)(2,1)S(1)}, bf16[64,1536]{1,0:T(8,128)(2,1)S(1)}, u32[]{:S(2)}, u32[]{:S(2)}) collective-permute-start(bf16[64,1536]{1,0:T(8,128)(2,1)S(1)} %get-tuple-element.131), channel_id=1, source_target_pairs={{4,0},{8,4},{12,8},{14,12},{10,14},{6,10},{2,6},{0,2},{5,1},{9,5},... | collective-permute-start | bytes 589832 | tf_op jit(solution)/shard_map/back_lead4/ppermute | solution.py:375
  59.0 6.6 %collective-permute-start.23 = (bf16[64,1536]{1,0:T(8,128)(2,1)S(1)}, bf16[64,1536]{1,0:T(8,128)(2,1)S(1)}, u32[]{:S(2)}, u32[]{:S(2)}) collective-permute-start(bf16[64,1536]{1,0:T(8,128)(2,1)S(1)} %add_convert_fusion.8), channel_id=1, source_target_pairs={{4,0},{8,4},{12,8},{14,12},{10,14},{6,10},{2,6},{0,2},{5,1},{9,5},... | collective-permute-start | bytes 589832 | tf_op jit(solution)/shard_map/back_lead3/ppermute | solution.py:375
  60.5 6.8 %collective-permute-start.22 = (bf16[64,1536]{1,0:T(8,128)(2,1)S(1)}, bf16[64,1536]{1,0:T(8,128)(2,1)S(1)}, u32[]{:S(2)}, u32[]{:S(2)}) collective-permute-start(bf16[64,1536]{1,0:T(8,128)(2,1)S(1)} %add_convert_fusion.9), channel_id=1, source_target_pairs={{0,4},{4,8},{8,12},{12,14},{14,10},{10,6},{6,2},{2,0},{1,5},{5,9},... | collective-permute-start | bytes 589832 | tf_op jit(solution)/shard_map/back_lead3/ppermute | solution.py:375
  61.2 8.4 %collective-permute-start.30 = (bf16[64,1536]{1,0:T(8,128)(2,1)S(1)}, bf16[64,1536]{1,0:T(8,128)(2,1)S(1)}, u32[]{:S(2)}, u32[]{:S(2)}) collective-permute-start(bf16[64,1536]{1,0:T(8,128)(2,1)S(1)} %add_convert_fusion.3), channel_id=1, source_target_pairs={{4,0},{8,4},{12,8},{14,12},{10,14},{6,10},{2,6},{0,2},{5,1},{9,5},... | collective-permute-start | bytes 589832 | tf_op jit(solution)/shard_map/back_trail2/ppermute | solution.py:375
  62.8 8.8 %collective-permute-start.29 = (bf16[64,1536]{1,0:T(8,128)(2,1)S(1)}, bf16[64,1536]{1,0:T(8,128)(2,1)S(1)}, u32[]{:S(2)}, u32[]{:S(2)}) collective-permute-start(bf16[64,1536]{1,0:T(8,128)(2,1)S(1)} %add_convert_fusion.4), channel_id=1, source_target_pairs={{0,4},{4,8},{8,12},{12,14},{14,10},{10,6},{6,2},{2,0},{1,5},{5,9},... | collective-permute-start | bytes 589832 | tf_op jit(solution)/shard_map/back_trail2/ppermute | solution.py:375
  67.4 8.5 %collective-permute-start.25 = (bf16[64,1536]{1,0:T(8,128)(2,1)S(1)}, bf16[64,1536]{1,0:T(8,128)(2,1)S(1)}, u32[]{:S(2)}, u32[]{:S(2)}) collective-permute-start(bf16[64,1536]{1,0:T(8,128)(2,1)S(1)} %add_convert_fusion.6), channel_id=1, source_target_pairs={{4,0},{8,4},{12,8},{14,12},{10,14},{6,10},{2,6},{0,2},{5,1},{9,5},... | collective-permute-start | bytes 589832 | tf_op jit(solution)/shard_map/back_lead2/ppermute | solution.py:375
  69.3 7.9 %collective-permute-start.24 = (bf16[64,1536]{1,0:T(8,128)(2,1)S(1)}, bf16[64,1536]{1,0:T(8,128)(2,1)S(1)}, u32[]{:S(2)}, u32[]{:S(2)}) collective-permute-start(bf16[64,1536]{1,0:T(8,128)(2,1)S(1)} %add_convert_fusion.7), channel_id=1, source_target_pairs={{0,4},{4,8},{8,12},{12,14},{14,10},{10,6},{6,2},{2,0},{1,5},{5,9},... | collective-permute-start | bytes 589832 | tf_op jit(solution)/shard_map/back_lead2/ppermute | solution.py:375
  71.6 7.8 %collective-permute-start.31 = (bf16[64,1536]{1,0:T(8,128)(2,1)S(1)}, bf16[64,1536]{1,0:T(8,128)(2,1)S(1)}, u32[]{:S(2)}, u32[]{:S(2)}) collective-permute-start(bf16[64,1536]{1,0:T(8,128)(2,1)S(1)} %add_convert_fusion.2), channel_id=1, source_target_pairs={{4,0},{8,4},{12,8},{14,12},{10,14},{6,10},{2,6},{0,2},{5,1},{9,5},... | collective-permute-start | bytes 589832 | tf_op jit(solution)/shard_map/back_trail1/ppermute | solution.py:375
  73.5 9.5 %collective-permute-start.32 = (bf16[64,1536]{1,0:T(8,128)(2,1)S(1)}, bf16[64,1536]{1,0:T(8,128)(2,1)S(1)}, u32[]{:S(2)}, u32[]{:S(2)}) collective-permute-start(bf16[64,1536]{1,0:T(8,128)(2,1)S(1)} %add_convert_fusion.1), channel_id=1, source_target_pairs={{0,4},{4,8},{8,12},{12,14},{14,10},{10,6},{6,2},{2,0},{1,5},{5,9},... | collective-permute-start | bytes 589832 | tf_op jit(solution)/shard_map/back_trail1/ppermute | solution.py:375
  77.2 5.7 %collective-permute-start.26 = (bf16[64,1536]{1,0:T(8,128)(2,1)S(1)}, bf16[64,1536]{1,0:T(8,128)(2,1)S(1)}, u32[]{:S(2)}, u32[]{:S(2)}) collective-permute-start(bf16[64,1536]{1,0:T(8,128)(2,1)S(1)} %add_convert_fusion.5), channel_id=1, source_target_pairs={{0,4},{4,8},{8,12},{12,14},{14,10},{10,6},{6,2},{2,0},{1,5},{5,9},... | collective-permute-start | bytes 589832 | tf_op jit(solution)/shard_map/back_lead1/ppermute | solution.py:375
  77.4 5.7 %collective-permute-start.33 = (bf16[64,1536]{1,0:T(8,128)(2,1)S(1)}, bf16[64,1536]{1,0:T(8,128)(2,1)S(1)}, u32[]{:S(2)}, u32[]{:S(2)}) collective-permute-start(bf16[64,1536]{1,0:T(8,128)(2,1)S(1)} %add_convert_fusion), channel_id=1, source_target_pairs={{4,0},{8,4},{12,8},{14,12},{10,14},{6,10},{2,6},{0,2},{5,1},{9,5},... | collective-permute-start | bytes 589832 | tf_op jit(solution)/shard_map/back_lead1/ppermute | solution.py:375

commit v13 on v9

--- a/solution.py
+++ b/solution.py
@@ -21,8 +21,7 @@
 
 def shifted(value, axis, by):
     peers = lax.axis_size(axis)
-    pairs = [(i, i + by) for i in range(peers) if 0 <= i + by < peers]
-    return lax.ppermute(value, axis, pairs)
+    return lax.ppermute(value, axis, [(i, (i + by) % peers) for i in range(peers)])
 
 
 def pinned(values, space):
@@ -43,12 +42,10 @@
 
 
 def tail_kernel(keys_hbm, values_hbm, out_ref, sems):
-    rows, width = out_ref.shape
+    rows = out_ref.shape[0] // 2
     last = pl.ds(keys_hbm.shape[0] - rows, rows)
     copies = [
-        pltpu.make_async_copy(
-            ref.at[last], out_ref.at[:, pl.ds(index * width // 2, width // 2)], sems.at[index]
-        )
+        pltpu.make_async_copy(ref.at[last], out_ref.at[pl.ds(index * rows, rows)], sems.at[index])
         for index, ref in enumerate((keys_hbm, values_hbm))
     ]
     for copy in copies:
@@ -62,7 +59,7 @@
         tail_kernel,
         in_specs=[pl.BlockSpec(memory_space=pltpu.HBM)] * 2,
         out_specs=pl.BlockSpec(memory_space=pltpu.VMEM),
-        out_shape=jax.ShapeDtypeStruct((WINDOW, 2 * keys.shape[1]), keys.dtype),
+        out_shape=jax.ShapeDtypeStruct((2 * WINDOW, keys.shape[1]), keys.dtype),
         scratch_shapes=[pltpu.SemaphoreType.DMA((2,))],
         name="tail",
     )(*pinned((keys, values), pltpu.HBM))
@@ -72,10 +69,10 @@
     if mix:
         sink_ref, q_ref, k_ref, v_ref, ow_ref = refs[:5]
         first_ref, before_ref, rank_ref, later_ref, send_ref, own_ref, done_ref = refs[5:]
-        rows, width = before_ref.shape[0], k_ref.shape[1]
+        rows = later_ref.shape[0]
         queries = slice(0, rows)
-        k = jnp.concatenate([before_ref[:, :width], k_ref[:rows]], axis=0)
-        v = jnp.concatenate([before_ref[:, width:], v_ref[:rows]], axis=0)
+        k = jnp.concatenate([before_ref[:rows], k_ref[:rows]], axis=0)
+        v = jnp.concatenate([before_ref[rows:], v_ref[:rows]], axis=0)
         done_ref[rows:] = later_ref[...]
         copies = []
     else:
@@ -356,8 +353,9 @@
 
     def bring(distance, lead, *after):
         keys = [(side, distance - 1, side if lead else 1 - side) for side in sides]
-        met = lax.optimization_barrier((*(came[key] for key in keys), *after))
+        met = lax.optimization_barrier(tuple(came[key] for key in keys))
         for (side, _, piece), block in zip(keys, met):
+            block = tied(block, *after)
             with jax.named_scope(f"out_{'lead' if lead else 'trail'}{distance}"):
                 came[side, distance, piece] = lax.ppermute(block, "seq", hops[side])
 
@@ -380,6 +378,8 @@
             bring(distance, False, *before)
             if 1 < distance < far - 1:
                 trails = [came[side, distance, 1 - side] for side in sides]
+        else:
+            trails = [came[side, far - 1, 1 - side] for side in sides]
         latest = apply(distance, (True,), worked[distance - 1], *trails)
     latest = apply(far - 1, (False,), latest)
 
@@ -400,8 +400,8 @@
             with jax.named_scope(f"back_{'lead' if lead else 'trail'}{distance}"):
                 moving[side, piece] = lax.ppermute(value, "seq", hops[side])
 
+    send(far - 1, False)
     send(far, True)
-    send(far - 1, False, *[came[side, far, side] for side in sides])
     for distance in range(far - 1, 0, -1):
         leads = [moving[side, side] for side in sides]
         send(distance, True)

time: 86.3 us -> 87 us (level)
  waiting for transfers between devices: 23.1 us -> 26.3 us
  starting transfers between devices: 35.2 us -> 32.7 us
    ppermute x1, waiting for transfers between devices: 0.01 us -> 2.96 us  [shifted(): lax.ppermute(value, axis, [(i, (i + by) % peers) for i in range(peers)])]
    ppermute x14, waiting for transfers between devices: 11.1 us -> 13.5 us  [send(): moving[side, piece] = lax.ppermute(value, 'seq', hops[side])]
    ppermute x14, waiting for transfers between devices: 10.5 us -> 8.23 us  [bring(): came[side, distance, piece] = lax.ppermute(block, 'seq', hops[side])]
    ppermute x1, starting transfers between devices: 4.4 us -> 2.54 us  [shifted(): lax.ppermute(value, axis, [(i, (i + by) % peers) for i in range(peers)])]
  transfers between devices with their start and end apart: 33 -> 33, of which waited for: 15 -> 18; matrix products, arithmetic and copies ran while one was open for 1% -> 1% of each run, Pallas kernels for 30% -> 30%
where the time goes in v13:
time: 87 us; the launch traced here: 86.9 us
  starting transfers between devices  32.7 us (38%)
  waiting for transfers between devices  26.3 us (30%)
  Pallas kernels  26 us (30%)
  other arithmetic  1.45 us (2%)
    pallas_call x8, Pallas kernels, experts(): pl.pallas_call(functools.partial(expert_kernel, min(256, half), len(block...  18.8 us
    ppermute x14, starting transfers between devices, send(): moving[side, piece] = lax.ppermute(value, 'seq', hops[side])  14.8 us
    ppermute x14, starting transfers between devices, bring(): came[side, distance, piece] = lax.ppermute(block, 'seq', hops[side])  14.3 us
    ppermute x14, waiting for transfers between devices, send(): moving[side, piece] = lax.ppermute(value, 'seq', hops[side])  13.5 us
    ppermute x14, waiting for transfers between devices, bring(): came[side, distance, piece] = lax.ppermute(block, 'seq', hops[side])  8.23 us
    pallas_call x2, Pallas kernels, attend(): pl.pallas_call(functools.partial(attend_kernel, mix), in_specs=[vmem if m...  5.55 us
    ppermute x1, waiting for transfers between devices, shifted(): lax.ppermute(value, axis, [(i, (i + by) % peers) for i in range(peers)])  2.96 us
    ppermute x1, starting transfers between devices, shifted(): lax.ppermute(value, axis, [(i, (i + by) % peers) for i in range(peers)])  2.54 us
  transfers between devices with their start and end apart: 33, of which 18 were waited for; matrix products, arithmetic and copies ran while one was open for 1% of the time, Pallas kernels for 30%

profile of v13, /device:TPU:0, one launch (start us, length us, event | category | flops | bytes accessed | tf_op | source)
XLA Modules:
  0.0 86.9 jit_solution(7673790138463550561)
XLA Ops:
  1.0 1.4 %tail.1 = bf16[256,128]{1,0:T(8,128)(2,1)} custom-call(bf16[256,128]{1,0:T(8,128)(2,1)} %keys_hbm.1, bf16[256,128]{1,0:T(8,128)(2,1)} %values_hbm.1), custom_call_target="tpu_custom_call" | custom-call | tf_op jit(solution)/shard_map/tail/pallas_call | solution.py:58
  2.4 2.5 %collective-permute-start = (bf16[256,128]{1,0:T(8,128)(2,1)}, bf16[256,128]{1,0:T(8,128)(2,1)S(1)}, u32[]{:S(2)}, u32[]{:S(2)}) collective-permute-start(bf16[256,128]{1,0:T(8,128)(2,1)} %tail.1), channel_id=1, source_target_pairs={{0,2},{2,4},{4,6},{6,8},{8,10},{10,12},{12,14},{14,0},{1,3},{3,5},... | collective-permute-start | bytes 196616 | tf_op jit(solution)/shard_map/ppermute | solution.py:24
  4.9 3.0 %attend.2 = (f32[1,16]{1,0:T(1,128)S(1)}, bf16[256,1024]{1,0:T(8,128)(2,1)S(1)}, bf16[256,128]{1,0:T(8,128)(2,1)S(1)}, bf16[256,128]{1,0:T(8,128)(2,1)S(1)}, bf1...) custom-call(f32[1,16]{1,0:T(1,128)} %bitcast.38, bf16[256,1024]{1,0:T(8,128)(2,1)} %refs_1_.1, ...), custom_call_target="tpu_custom_call" | custom-call | flops 671088640 | bytes 6291456 | tf_op jit(solution)/shard_map/attend/pallas_call | solution.py:175
  8.0 3.0 %collective-permute-done.refs_6_ = bf16[256,128]{1,0:T(8,128)(2,1)S(1)} collective-permute-done((bf16[256,128]{1,0:T(8,128)(2,1)}, bf16[256,128]{1,0:T(8,128)(2,1)S(1)}, u32[]{:S(2)}, u32[]{:S(2)}) %collective-permute-start) | collective-permute-done | bytes 65568 | tf_op jit(solution)/shard_map/ppermute | solution.py:24
  10.9 2.6 %attend.3 = (bf16[128,1536]{1,0:T(8,128)(2,1)S(1)}, f32[128,1536]{1,0:T(8,128)S(1)}) custom-call(f32[1,16]{1,0:T(1,128)S(1)} %get-tuple-element.82.refs_0_, bf16[256,1024]{1,0:T(8,128)(2,1)S(1)} %get-tuple-element.83.refs_1_, bf16[256,128]{1,0:T(8,128)(2,1)S(1)} %get-tuple-element.84.refs_2_, bf16[256,128]{1,0:T(8,128)(2,1)S(1)} %get-tuple-element.85.refs_3_, ...), custom_call_target="tpu_custom_call" | custom-call | flops 671088640 | bytes 6291456 | tf_op jit(solution)/shard_map/attend/pallas_call | solution.py:175
  13.6 1.7 %collective-permute-done.1.came_ref = bf16[128,1536]{1,0:T(8,128)(2,1)S(1)} collective-permute-done((bf16[128,1536]{1,0:T(8,128)(2,1)S(1)}, bf16[128,1536]{1,0:T(8,128)(2,1)S(1)}, u32[]{:S(2)}, u32[]{:S(2)}) %collective-permute-start.1) | collective-permute-done | bytes 393248 | tf_op jit(solution)/shard_map/ppermute | solution.py:37
  15.7 2.0 %collective-permute-start.6 = (bf16[784,128]{1,0:T(8,128)(2,1)S(1)}, bf16[784,128]{1,0:T(8,128)(2,1)S(1)}, u32[]{:S(2)}, u32[]{:S(2)}) collective-permute-start(bf16[784,128]{1,0:T(8,128)(2,1)S(1)} %get-tuple-element.97.refs_1_), channel_id=1, source_target_pairs={{4,0},{8,4},{12,8},{14,12},{10,14},{6,10},{2,6},{0,2},{5,1},{9,5},... | collective-permute-start | bytes 602120 | tf_op jit(solution)/shard_map/out_lead1/ppermute | solution.py:360
  17.8 2.0 %collective-permute-start.12 = (bf16[784,128]{1,0:T(8,128)(2,1)S(1)}, bf16[784,128]{1,0:T(8,128)(2,1)S(1)}, u32[]{:S(2)}, u32[]{:S(2)}) collective-permute-start(bf16[784,128]{1,0:T(8,128)(2,1)S(1)} %get-tuple-element.96.refs_0_), channel_id=1, source_target_pairs={{4,0},{8,4},{12,8},{14,12},{10,14},{6,10},{2,6},{0,2},{5,1},{9,5},... | collective-permute-start | bytes 602120 | tf_op jit(solution)/shard_map/out_trail1/ppermute | solution.py:360
  19.8 4.1 %experts.8 = (bf16[64,1536]{1,0:T(8,128)(2,1)S(1)}, bf16[64,1536]{1,0:T(8,128)(2,1)S(1)}, bf16[1536,768]{1,0:T(8,128)(2,1)S(1)}, bf16[1536,768]{1,0:T(8,128)(2,1)S(1)}, bf16[768,1536]{1,0:T(8,128)(2,1)S(1)}) custom-call(s32[1]{0:T(128)} %bitcast.5.me_ref, bf16[784,128]{1,0:T(8,128)(2,1)S(1)} %get-tuple-element.96.refs_0_, ...), custom_call_target="tpu_custom_call" | custom-call | flops 1811939328 | bytes 1179648 | tf_op jit(solution)/shard_map/experts/pallas_call | solution.py:311
  23.9 1.0 %collective-permute-start.7 = (bf16[784,128]{1,0:T(8,128)(2,1)S(1)}, bf16[784,128]{1,0:T(8,128)(2,1)S(1)}, u32[]{:S(2)}, u32[]{:S(2)}) collective-permute-start(bf16[784,128]{1,0:T(8,128)(2,1)S(1)} %collective-permute-done.5.refs_0_), channel_id=1, source_target_pairs={{0,4},{4,8},{8,12},{12,14},{14,10},{10,6},{6,2},{2,0},{1,5},{5,9},... | collective-permute-start | bytes 602120 | tf_op jit(solution)/shard_map/out_lead2/ppermute | solution.py:360
  24.9 1.1 %collective-permute-start.8 = (bf16[784,128]{1,0:T(8,128)(2,1)S(1)}, bf16[784,128]{1,0:T(8,128)(2,1)S(1)}, u32[]{:S(2)}, u32[]{:S(2)}) collective-permute-start(bf16[784,128]{1,0:T(8,128)(2,1)S(1)} %collective-permute-done.6.refs_1_), channel_id=1, source_target_pairs={{4,0},{8,4},{12,8},{14,12},{10,14},{6,10},{2,6},{0,2},{5,1},{9,5},... | collective-permute-start | bytes 602120 | tf_op jit(solution)/shard_map/out_lead2/ppermute | solution.py:360
  26.0 1.9 %collective-permute-done.11.refs_0_ = bf16[784,128]{1,0:T(8,128)(2,1)S(1)} collective-permute-done((bf16[784,128]{1,0:T(8,128)(2,1)S(1)}, bf16[784,128]{1,0:T(8,128)(2,1)S(1)}, u32[]{:S(2)}, u32[]{:S(2)}) %collective-permute-start.11) | collective-permute-done | bytes 200736 | tf_op jit(solution)/shard_map/out_trail1/ppermute | solution.py:360
  27.9 2.0 %collective-permute-start.14 = (bf16[784,128]{1,0:T(8,128)(2,1)S(1)}, bf16[784,128]{1,0:T(8,128)(2,1)S(1)}, u32[]{:S(2)}, u32[]{:S(2)}) collective-permute-start(bf16[784,128]{1,0:T(8,128)(2,1)S(1)} %collective-permute-done.12.refs_1_), channel_id=1, source_target_pairs={{4,0},{8,4},{12,8},{14,12},{10,14},{6,10},{2,6},{0,2},{5,1},{9,5},... | collective-permute-start | bytes 602120 | tf_op jit(solution)/shard_map/out_trail2/ppermute | solution.py:360
  29.9 2.1 %experts.9 = (bf16[64,1536]{1,0:T(8,128)(2,1)S(1)}, bf16[64,1536]{1,0:T(8,128)(2,1)S(1)}) custom-call(s32[1]{0:T(128)} %bitcast.5.me_ref, bf16[784,128]{1,0:T(8,128)(2,1)S(1)} %collective-permute-done.5.refs_0_, bf16[784,128]{1,0:T(8,128)(2,1)S(1)} %collective-permute-done.6.refs_1_, bf16[1536,768]{1,0:T(8,128)(2,1)S(1)} %bitcast.11, ...), custom_call_target="tpu_custom_call" | custom-call | flops 1811939328 | bytes 1179648 | tf_op jit(solution)/shard_map/hop1/experts/pallas_call | solution.py:311
  32.2 0.6 collective-permute-done.8.refs_1_
  32.8 1.4 %collective-permute-start.10 = (bf16[784,128]{1,0:T(8,128)(2,1)S(1)}, bf16[784,128]{1,0:T(8,128)(2,1)S(1)}, u32[]{:S(2)}, u32[]{:S(2)}) collective-permute-start(bf16[784,128]{1,0:T(8,128)(2,1)S(1)} %collective-permute-done.8.refs_1_), channel_id=1, source_target_pairs={{4,0},{8,4},{12,8},{14,12},{10,14},{6,10},{2,6},{0,2},{5,1},{9,5},... | collective-permute-start | bytes 602120 | tf_op jit(solution)/shard_map/out_lead3/ppermute | solution.py:360
  34.2 0.6 collective-permute-start.9
  34.8 2.3 %collective-permute-done.14.refs_1_ = bf16[784,128]{1,0:T(8,128)(2,1)S(1)} collective-permute-done((bf16[784,128]{1,0:T(8,128)(2,1)S(1)}, bf16[784,128]{1,0:T(8,128)(2,1)S(1)}, u32[]{:S(2)}, u32[]{:S(2)}) %collective-permute-start.14) | collective-permute-done | bytes 200736 | tf_op jit(solution)/shard_map/out_trail2/ppermute | solution.py:360
  37.1 1.4 %collective-permute-start.17 = (bf16[784,128]{1,0:T(8,128)(2,1)S(1)}, bf16[784,128]{1,0:T(8,128)(2,1)S(1)}, u32[]{:S(2)}, u32[]{:S(2)}) collective-permute-start(bf16[784,128]{1,0:T(8,128)(2,1)S(1)} %collective-permute-done.14.refs_1_), channel_id=1, source_target_pairs={{4,0},{8,4},{12,8},{14,12},{10,14},{6,10},{2,6},{0,2},{5,1},{9,5},... | collective-permute-start | bytes 602120 | tf_op jit(solution)/shard_map/out_trail3/ppermute | solution.py:360
  39.1 2.1 %experts.10 = (bf16[64,1536]{1,0:T(8,128)(2,1)S(1)}, bf16[64,1536]{1,0:T(8,128)(2,1)S(1)}) custom-call(s32[1]{0:T(128)} %bitcast.5.me_ref, bf16[784,128]{1,0:T(8,128)(2,1)S(1)} %collective-permute-done.7.refs_0_, bf16[784,128]{1,0:T(8,128)(2,1)S(1)} %collective-permute-done.8.refs_1_, bf16[1536,768]{1,0:T(8,128)(2,1)S(1)} %bitcast.12, ...), custom_call_target="tpu_custom_call" | custom-call | flops 1811939328 | bytes 1179648 | tf_op jit(solution)/shard_map/hop2/experts/pallas_call | solution.py:311
  41.4 1.6 %collective-permute-start.15 = (bf16[784,128]{1,0:T(8,128)(2,1)S(1)}, bf16[784,128]{1,0:T(8,128)(2,1)S(1)}, u32[]{:S(2)}, u32[]{:S(2)}) collective-permute-start(bf16[784,128]{1,0:T(8,128)(2,1)S(1)} %collective-permute-done.9.refs_0_), channel_id=1, source_target_pairs={{0,4},{4,8},{8,12},{12,14},{14,10},{10,6},{6,2},{2,0},{1,5},{5,9},... | collective-permute-start | bytes 602120 | tf_op jit(solution)/shard_map/out_lead4/ppermute | solution.py:360
  43.4 2.1 %experts.11 = (bf16[64,1536]{1,0:T(8,128)(2,1)S(1)}, bf16[64,1536]{1,0:T(8,128)(2,1)S(1)}) custom-call(s32[1]{0:T(128)} %bitcast.5.me_ref, bf16[784,128]{1,0:T(8,128)(2,1)S(1)} %collective-permute-done.9.refs_0_, bf16[784,128]{1,0:T(8,128)(2,1)S(1)} %collective-permute-done.10.refs_1_, bf16[1536,768]{1,0:T(8,128)(2,1)S(1)} %bitcast.13, ...), custom_call_target="tpu_custom_call" | custom-call | flops 1811939328 | bytes 1179648 | tf_op jit(solution)/shard_map/hop3/experts/pallas_call | solution.py:311
  45.5 1.6 %collective-permute-start.26 = (bf16[64,1536]{1,0:T(8,128)(2,1)S(1)}, bf16[64,1536]{1,0:T(8,128)(2,1)S(1)}, u32[]{:S(2)}, u32[]{:S(2)}) collective-permute-start(bf16[64,1536]{1,0:T(8,128)(2,1)S(1)} %get-tuple-element.145), channel_id=1, source_target_pairs={{0,4},{4,8},{8,12},{12,14},{14,10},{10,6},{6,2},{2,0},{1,5},{5,9},... | collective-permute-start | bytes 589832 | tf_op jit(solution)/shard_map/back_trail3/ppermute | solution.py:401
  47.6 3.0 %collective-permute-done.15.refs_0_ = bf16[784,128]{1,0:T(8,128)(2,1)S(1)} collective-permute-done((bf16[784,128]{1,0:T(8,128)(2,1)S(1)}, bf16[784,128]{1,0:T(8,128)(2,1)S(1)}, u32[]{:S(2)}, u32[]{:S(2)}) %collective-permute-start.15) | collective-permute-done | bytes 200736 | tf_op jit(solution)/shard_map/out_lead4/ppermute | solution.py:360
  50.7 2.1 %experts.12 = (bf16[64,1536]{1,0:T(8,128)(2,1)S(1)}, bf16[64,1536]{1,0:T(8,128)(2,1)S(1)}) custom-call(s32[1]{0:T(128)} %bitcast.5.me_ref, bf16[784,128]{1,0:T(8,128)(2,1)S(1)} %collective-permute-done.15.refs_0_, bf16[784,128]{1,0:T(8,128)(2,1)S(1)} %collective-permute-done.18.refs_1_, bf16[1536,768]{1,0:T(8,128)(2,1)S(1)} %bitcast.14, ...), custom_call_target="tpu_custom_call" | custom-call | flops 1811939328 | bytes 1179648 | tf_op jit(solution)/shard_map/hop4/experts/pallas_call | solution.py:311
  52.8 1.0 %collective-permute-start.19 = (bf16[64,1536]{1,0:T(8,128)(2,1)S(1)}, bf16[64,1536]{1,0:T(8,128)(2,1)S(1)}, u32[]{:S(2)}, u32[]{:S(2)}) collective-permute-start(bf16[64,1536]{1,0:T(8,128)(2,1)S(1)} %get-tuple-element.130), channel_id=1, source_target_pairs={{0,4},{4,8},{8,12},{12,14},{14,10},{10,6},{6,2},{2,0},{1,5},{5,9},... | collective-permute-start | bytes 589832 | tf_op jit(solution)/shard_map/back_lead4/ppermute | solution.py:401
  53.8 1.1 %collective-permute-start.20 = (bf16[64,1536]{1,0:T(8,128)(2,1)S(1)}, bf16[64,1536]{1,0:T(8,128)(2,1)S(1)}, u32[]{:S(2)}, u32[]{:S(2)}) collective-permute-start(bf16[64,1536]{1,0:T(8,128)(2,1)S(1)} %get-tuple-element.131), channel_id=1, source_target_pairs={{4,0},{8,4},{12,8},{14,12},{10,14},{6,10},{2,6},{0,2},{5,1},{9,5},... | collective-permute-start | bytes 589832 | tf_op jit(solution)/shard_map/back_lead4/ppermute | solution.py:401
  54.9 2.1 %experts.13 = (bf16[64,1536]{1,0:T(8,128)(2,1)S(1)}, bf16[64,1536]{1,0:T(8,128)(2,1)S(1)}) custom-call(s32[1]{0:T(128)} %bitcast.5.me_ref, bf16[784,128]{1,0:T(8,128)(2,1)S(1)} %collective-permute-done.16.refs_0_, bf16[784,128]{1,0:T(8,128)(2,1)S(1)} %collective-permute-done.17.refs_1_, bf16[1536,768]{1,0:T(8,128)(2,1)S(1)} %bitcast.15, ...), custom_call_target="tpu_custom_call" | custom-call | flops 1811939328 | bytes 1179648 | tf_op jit(solution)/shard_map/hop3/experts/pallas_call | solution.py:311
  57.0 1.5 %collective-permute-done.19 = bf16[64,1536]{1,0:T(8,128)(2,1)S(1)} collective-permute-done((bf16[64,1536]{1,0:T(8,128)(2,1)S(1)}, bf16[64,1536]{1,0:T(8,128)(2,1)S(1)}, u32[]{:S(2)}, u32[]{:S(2)}) %collective-permute-start.19) | collective-permute-done | bytes 196640 | tf_op jit(solution)/shard_map/back_lead4/ppermute | solution.py:401
  58.5 2.9 %collective-permute-done.20 = bf16[64,1536]{1,0:T(8,128)(2,1)S(1)} collective-permute-done((bf16[64,1536]{1,0:T(8,128)(2,1)S(1)}, bf16[64,1536]{1,0:T(8,128)(2,1)S(1)}, u32[]{:S(2)}, u32[]{:S(2)}) %collective-permute-start.20) | collective-permute-done | bytes 196640 | tf_op jit(solution)/shard_map/back_lead4/ppermute | solution.py:401
  61.5 0.6 collective-permute-start.22
  62.2 1.5 %collective-permute-start.21 = (bf16[64,1536]{1,0:T(8,128)(2,1)S(1)}, bf16[64,1536]{1,0:T(8,128)(2,1)S(1)}, u32[]{:S(2)}, u32[]{:S(2)}) collective-permute-start(bf16[64,1536]{1,0:T(8,128)(2,1)S(1)} %add_convert_fusion.9), channel_id=1, source_target_pairs={{0,4},{4,8},{8,12},{12,14},{14,10},{10,6},{6,2},{2,0},{1,5},{5,9},... | collective-permute-start | bytes 589832 | tf_op jit(solution)/shard_map/back_lead3/ppermute | solution.py:401
  63.8 0.6 collective-permute-start.29
  64.5 1.5 %collective-permute-start.28 = (bf16[64,1536]{1,0:T(8,128)(2,1)S(1)}, bf16[64,1536]{1,0:T(8,128)(2,1)S(1)}, u32[]{:S(2)}, u32[]{:S(2)}) collective-permute-start(bf16[64,1536]{1,0:T(8,128)(2,1)S(1)} %add_convert_fusion.4), channel_id=1, source_target_pairs={{0,4},{4,8},{8,12},{12,14},{14,10},{10,6},{6,2},{2,0},{1,5},{5,9},... | collective-permute-start | bytes 589832 | tf_op jit(solution)/shard_map/back_trail2/ppermute | solution.py:401
  66.0 2.1 %experts.14 = (bf16[64,1536]{1,0:T(8,128)(2,1)S(1)}, bf16[64,1536]{1,0:T(8,128)(2,1)S(1)}) custom-call(s32[1]{0:T(128)} %bitcast.5.me_ref, bf16[784,128]{1,0:T(8,128)(2,1)S(1)} %collective-permute-done.13.refs_0_, bf16[784,128]{1,0:T(8,128)(2,1)S(1)} %collective-permute-done.14.refs_1_, bf16[1536,768]{1,0:T(8,128)(2,1)S(1)} %bitcast.16, ...), custom_call_target="tpu_custom_call" | custom-call | flops 1811939328 | bytes 1179648 | tf_op jit(solution)/shard_map/hop2/experts/pallas_call | solution.py:311
  68.1 1.3 %collective-permute-done.22 = bf16[64,1536]{1,0:T(8,128)(2,1)S(1)} collective-permute-done((bf16[64,1536]{1,0:T(8,128)(2,1)S(1)}, bf16[64,1536]{1,0:T(8,128)(2,1)S(1)}, u32[]{:S(2)}, u32[]{:S(2)}) %collective-permute-start.22) | collective-permute-done | bytes 196640 | tf_op jit(solution)/shard_map/back_lead3/ppermute | solution.py:401
  69.3 0.7 collective-permute-done.21
  70.1 1.0 %collective-permute-start.24 = (bf16[64,1536]{1,0:T(8,128)(2,1)S(1)}, bf16[64,1536]{1,0:T(8,128)(2,1)S(1)}, u32[]{:S(2)}, u32[]{:S(2)}) collective-permute-start(bf16[64,1536]{1,0:T(8,128)(2,1)S(1)} %add_convert_fusion.6), channel_id=1, source_target_pairs={{4,0},{8,4},{12,8},{14,12},{10,14},{6,10},{2,6},{0,2},{5,1},{9,5},... | collective-permute-start | bytes 589832 | tf_op jit(solution)/shard_map/back_lead2/ppermute | solution.py:401
  71.1 1.1 %collective-permute-start.23 = (bf16[64,1536]{1,0:T(8,128)(2,1)S(1)}, bf16[64,1536]{1,0:T(8,128)(2,1)S(1)}, u32[]{:S(2)}, u32[]{:S(2)}) collective-permute-start(bf16[64,1536]{1,0:T(8,128)(2,1)S(1)} %add_convert_fusion.7), channel_id=1, source_target_pairs={{0,4},{4,8},{8,12},{12,14},{14,10},{10,6},{6,2},{2,0},{1,5},{5,9},... | collective-permute-start | bytes 589832 | tf_op jit(solution)/shard_map/back_lead2/ppermute | solution.py:401
  72.3 1.3 %collective-permute-done.29 = bf16[64,1536]{1,0:T(8,128)(2,1)S(1)} collective-permute-done((bf16[64,1536]{1,0:T(8,128)(2,1)S(1)}, bf16[64,1536]{1,0:T(8,128)(2,1)S(1)}, u32[]{:S(2)}, u32[]{:S(2)}) %collective-permute-start.29) | collective-permute-done | bytes 196640 | tf_op jit(solution)/shard_map/back_trail2/ppermute | solution.py:401
  73.6 0.7 collective-permute-done.28
  74.3 1.0 %collective-permute-start.30 = (bf16[64,1536]{1,0:T(8,128)(2,1)S(1)}, bf16[64,1536]{1,0:T(8,128)(2,1)S(1)}, u32[]{:S(2)}, u32[]{:S(2)}) collective-permute-start(bf16[64,1536]{1,0:T(8,128)(2,1)S(1)} %add_convert_fusion.2), channel_id=1, source_target_pairs={{4,0},{8,4},{12,8},{14,12},{10,14},{6,10},{2,6},{0,2},{5,1},{9,5},... | collective-permute-start | bytes 589832 | tf_op jit(solution)/shard_map/back_trail1/ppermute | solution.py:401
  75.3 1.1 %collective-permute-start.31 = (bf16[64,1536]{1,0:T(8,128)(2,1)S(1)}, bf16[64,1536]{1,0:T(8,128)(2,1)S(1)}, u32[]{:S(2)}, u32[]{:S(2)}) collective-permute-start(bf16[64,1536]{1,0:T(8,128)(2,1)S(1)} %add_convert_fusion.1), channel_id=1, source_target_pairs={{0,4},{4,8},{8,12},{12,14},{14,10},{10,6},{6,2},{2,0},{1,5},{5,9},... | collective-permute-start | bytes 589832 | tf_op jit(solution)/shard_map/back_trail1/ppermute | solution.py:401
  76.5 2.1 %experts.15 = (bf16[64,1536]{1,0:T(8,128)(2,1)S(1)}, bf16[64,1536]{1,0:T(8,128)(2,1)S(1)}) custom-call(s32[1]{0:T(128)} %bitcast.5.me_ref, bf16[784,128]{1,0:T(8,128)(2,1)S(1)} %collective-permute-done.11.refs_0_, bf16[784,128]{1,0:T(8,128)(2,1)S(1)} %collective-permute-done.12.refs_1_, bf16[1536,768]{1,0:T(8,128)(2,1)S(1)} %bitcast.17, ...), custom_call_target="tpu_custom_call" | custom-call | flops 1811939328 | bytes 1179648 | tf_op jit(solution)/shard_map/hop1/experts/pallas_call | solution.py:311
  78.6 1.5 %collective-permute-start.25 = (bf16[64,1536]{1,0:T(8,128)(2,1)S(1)}, bf16[64,1536]{1,0:T(8,128)(2,1)S(1)}, u32[]{:S(2)}, u32[]{:S(2)}) collective-permute-start(bf16[64,1536]{1,0:T(8,128)(2,1)S(1)} %add_convert_fusion.5), channel_id=1, source_target_pairs={{0,4},{4,8},{8,12},{12,14},{14,10},{10,6},{6,2},{2,0},{1,5},{5,9},... | collective-permute-start | bytes 589832 | tf_op jit(solution)/shard_map/back_lead1/ppermute | solution.py:401
  80.8 3.5 %collective-permute-done.25 = bf16[64,1536]{1,0:T(8,128)(2,1)S(1)} collective-permute-done((bf16[64,1536]{1,0:T(8,128)(2,1)S(1)}, bf16[64,1536]{1,0:T(8,128)(2,1)S(1)}, u32[]{:S(2)}, u32[]{:S(2)}) %collective-permute-start.25) | collective-permute-done | bytes 196640 | tf_op jit(solution)/shard_map/back_lead1/ppermute | solution.py:401
  84.4 1.5 %collective-permute-done.32 = bf16[64,1536]{1,0:T(8,128)(2,1)S(1)} collective-permute-done((bf16[64,1536]{1,0:T(8,128)(2,1)S(1)}, bf16[64,1536]{1,0:T(8,128)(2,1)S(1)}, u32[]{:S(2)}, u32[]{:S(2)}) %collective-permute-start.32) | collective-permute-done | bytes 196640 | tf_op jit(solution)/shard_map/back_lead1/ppermute | solution.py:401
  86.0 0.8 fusion
  (60 shorter events, 4.7 us)
Async XLA Ops:
  0.0 15.6 %collective-permute-start.2 = (bf16[1536,768]{1,0:T(8,128)(2,1)}, bf16[1536,768]{1,0:T(8,128)(2,1)S(1)}, u32[]{:S(2)}, u32[]{:S(2)}) collective-permute-start(bf16[1536,768]{1,0:T(8,128)(2,1)} %bitcast.9), channel_id=1, source_target_pairs={{0,1},{1,0},{2,3},{3,2},{4,5},{5,4},{6,7},{7,6},{8,9},{9,8},{10,11... | collective-permute-start | bytes 7077896 | tf_op jit(solution)/shard_map/ppermute | solution.py:37
  0.5 15.2 %collective-permute-start.3 = (bf16[1536,768]{1,0:T(8,128)(2,1)}, bf16[1536,768]{1,0:T(8,128)(2,1)}, u32[]{:S(2)}, u32[]{:S(2)}) collective-permute-start(bf16[1536,768]{1,0:T(8,128)(2,1)} %bitcast.18), channel_id=1, source_target_pairs={{0,1},{1,0},{2,3},{3,2},{4,5},{5,4},{6,7},{7,6},{8,9},{9,8},{10,11... | collective-permute-start | bytes 7077896 | tf_op jit(solution)/shard_map/ppermute | solution.py:37
  0.5 15.1 %collective-permute-start.4 = (bf16[768,1536]{1,0:T(8,128)(2,1)}, bf16[768,1536]{1,0:T(8,128)(2,1)}, u32[]{:S(2)}, u32[]{:S(2)}) collective-permute-start(bf16[768,1536]{1,0:T(8,128)(2,1)} %bitcast.27), channel_id=1, source_target_pairs={{0,1},{1,0},{2,3},{3,2},{4,5},{5,4},{6,7},{7,6},{8,9},{9,8},{10,11... | collective-permute-start | bytes 7077896 | tf_op jit(solution)/shard_map/ppermute | solution.py:37
  2.4 8.6 %collective-permute-start = (bf16[256,128]{1,0:T(8,128)(2,1)}, bf16[256,128]{1,0:T(8,128)(2,1)S(1)}, u32[]{:S(2)}, u32[]{:S(2)}) collective-permute-start(bf16[256,128]{1,0:T(8,128)(2,1)} %tail.1), channel_id=1, source_target_pairs={{0,2},{2,4},{4,6},{6,8},{8,10},{10,12},{12,14},{14,0},{1,3},{3,5},... | collective-permute-start | bytes 196616 | tf_op jit(solution)/shard_map/ppermute | solution.py:24
  4.9 14.8 %copy-start.2 = (bf16[1,768,1536]{2,1,0:T(8,128)(2,1)S(1)}, bf16[1,768,1536]{2,1,0:T(8,128)(2,1)}, u32[]{:S(2)}) copy-start(bf16[1,768,1536]{2,1,0:T(8,128)(2,1)} %param.23) | copy-start | bytes 7077892
  7.9 5.7 %copy-start.7 = (f32[1536]{0:T(1024)S(1)}, f32[1536]{0:T(1024)}, u32[]{:S(2)}) copy-start(f32[1536]{0:T(1024)} %param.18) | copy-start | bytes 18436
  8.0 7.4 %copy-start.3 = (bf16[128,1536]{1,0:T(8,128)(2,1)S(1)}, bf16[128,1536]{1,0:T(8,128)(2,1)}, u32[]{:S(2)}) copy-start(bf16[128,1536]{1,0:T(8,128)(2,1)} %stream_ref.1) | copy-start | bytes 1179652
  8.0 7.3 %copy-start.4 = (s32[128,4]{0,1:T(4,128)S(1)}, s32[128,4]{0,1:T(4,128)}, u32[]{:S(2)}) copy-start(s32[128,4]{0,1:T(4,128)} %param.19) | copy-start | bytes 6148
  8.0 7.3 %copy-start.5 = (f32[128,4]{0,1:T(4,128)S(1)}, f32[128,4]{0,1:T(4,128)}, u32[]{:S(2)}) copy-start(f32[128,4]{0,1:T(4,128)} %param.20) | copy-start | bytes 6148
  10.9 8.8 %copy-start = (bf16[1,1536,768]{2,1,0:T(8,128)(2,1)S(1)}, bf16[1,1536,768]{2,1,0:T(8,128)(2,1)}, u32[]{:S(2)}) copy-start(bf16[1,1536,768]{2,1,0:T(8,128)(2,1)} %param.21) | copy-start | bytes 7077892
  10.9 8.8 %copy-start.1 = (bf16[1,1536,768]{2,1,0:T(8,128)(2,1)S(1)}, bf16[1,1536,768]{2,1,0:T(8,128)(2,1)}, u32[]{:S(2)}) copy-start(bf16[1,1536,768]{2,1,0:T(8,128)(2,1)} %param.22) | copy-start | bytes 7077892
  13.5 1.8 %collective-permute-start.1 = (bf16[128,1536]{1,0:T(8,128)(2,1)S(1)}, bf16[128,1536]{1,0:T(8,128)(2,1)S(1)}, u32[]{:S(2)}, u32[]{:S(2)}) collective-permute-start(bf16[128,1536]{1,0:T(8,128)(2,1)S(1)} %get-tuple-element.89), channel_id=1, source_target_pairs={{0,1},{1,0},{2,3},{3,2},{4,5},{5,4},{6,7},{7,6},{8,9},{9,8},{10,11... | collective-permute-start | bytes 1179656 | tf_op jit(solution)/shard_map/ppermute | solution.py:37
  15.6 4.1 %copy-start.6 = (bf16[1536,768]{1,0:T(8,128)(2,1)}, bf16[1536,768]{1,0:T(8,128)(2,1)S(1)}, u32[]{:S(2)}) copy-start(bf16[1536,768]{1,0:T(8,128)(2,1)S(1)} %collective-permute-done.2.refs_5_) | copy-start | bytes 7077892
  15.7 8.2 %collective-permute-start.5 = (bf16[784,128]{1,0:T(8,128)(2,1)S(1)}, bf16[784,128]{1,0:T(8,128)(2,1)S(1)}, u32[]{:S(2)}, u32[]{:S(2)}) collective-permute-start(bf16[784,128]{1,0:T(8,128)(2,1)S(1)} %get-tuple-element.96.refs_0_), channel_id=1, source_target_pairs={{0,4},{4,8},{8,12},{12,14},{14,10},{10,6},{6,2},{2,0},{1,5},{5,9},... | collective-permute-start | bytes 602120 | tf_op jit(solution)/shard_map/out_lead1/ppermute | solution.py:360
  15.7 8.2 %collective-permute-start.6 = (bf16[784,128]{1,0:T(8,128)(2,1)S(1)}, bf16[784,128]{1,0:T(8,128)(2,1)S(1)}, u32[]{:S(2)}, u32[]{:S(2)}) collective-permute-start(bf16[784,128]{1,0:T(8,128)(2,1)S(1)} %get-tuple-element.97.refs_1_), channel_id=1, source_target_pairs={{4,0},{8,4},{12,8},{14,12},{10,14},{6,10},{2,6},{0,2},{5,1},{9,5},... | collective-permute-start | bytes 602120 | tf_op jit(solution)/shard_map/out_lead1/ppermute | solution.py:360
  17.7 10.1 %collective-permute-start.11 = (bf16[784,128]{1,0:T(8,128)(2,1)S(1)}, bf16[784,128]{1,0:T(8,128)(2,1)S(1)}, u32[]{:S(2)}, u32[]{:S(2)}) collective-permute-start(bf16[784,128]{1,0:T(8,128)(2,1)S(1)} %get-tuple-element.97.refs_1_), channel_id=1, source_target_pairs={{0,4},{4,8},{8,12},{12,14},{14,10},{10,6},{6,2},{2,0},{1,5},{5,9},... | collective-permute-start | bytes 602120 | tf_op jit(solution)/shard_map/out_trail1/ppermute | solution.py:360
  17.8 10.1 %collective-permute-start.12 = (bf16[784,128]{1,0:T(8,128)(2,1)S(1)}, bf16[784,128]{1,0:T(8,128)(2,1)S(1)}, u32[]{:S(2)}, u32[]{:S(2)}) collective-permute-start(bf16[784,128]{1,0:T(8,128)(2,1)S(1)} %get-tuple-element.96.refs_0_), channel_id=1, source_target_pairs={{4,0},{8,4},{12,8},{14,12},{10,14},{6,10},{2,6},{0,2},{5,1},{9,5},... | collective-permute-start | bytes 602120 | tf_op jit(solution)/shard_map/out_trail1/ppermute | solution.py:360
  23.9 8.3 %collective-permute-start.7 = (bf16[784,128]{1,0:T(8,128)(2,1)S(1)}, bf16[784,128]{1,0:T(8,128)(2,1)S(1)}, u32[]{:S(2)}, u32[]{:S(2)}) collective-permute-start(bf16[784,128]{1,0:T(8,128)(2,1)S(1)} %collective-permute-done.5.refs_0_), channel_id=1, source_target_pairs={{0,4},{4,8},{8,12},{12,14},{14,10},{10,6},{6,2},{2,0},{1,5},{5,9},... | collective-permute-start | bytes 602120 | tf_op jit(solution)/shard_map/out_lead2/ppermute | solution.py:360
  24.9 7.9 %collective-permute-start.8 = (bf16[784,128]{1,0:T(8,128)(2,1)S(1)}, bf16[784,128]{1,0:T(8,128)(2,1)S(1)}, u32[]{:S(2)}, u32[]{:S(2)}) collective-permute-start(bf16[784,128]{1,0:T(8,128)(2,1)S(1)} %collective-permute-done.6.refs_1_), channel_id=1, source_target_pairs={{4,0},{8,4},{12,8},{14,12},{10,14},{6,10},{2,6},{0,2},{5,1},{9,5},... | collective-permute-start | bytes 602120 | tf_op jit(solution)/shard_map/out_lead2/ppermute | solution.py:360
  27.9 9.2 %collective-permute-start.14 = (bf16[784,128]{1,0:T(8,128)(2,1)S(1)}, bf16[784,128]{1,0:T(8,128)(2,1)S(1)}, u32[]{:S(2)}, u32[]{:S(2)}) collective-permute-start(bf16[784,128]{1,0:T(8,128)(2,1)S(1)} %collective-permute-done.12.refs_1_), channel_id=1, source_target_pairs={{4,0},{8,4},{12,8},{14,12},{10,14},{6,10},{2,6},{0,2},{5,1},{9,5},... | collective-permute-start | bytes 602120 | tf_op jit(solution)/shard_map/out_trail2/ppermute | solution.py:360
  29.9 7.2 %collective-permute-start.13 = (bf16[784,128]{1,0:T(8,128)(2,1)S(1)}, bf16[784,128]{1,0:T(8,128)(2,1)S(1)}, u32[]{:S(2)}, u32[]{:S(2)}) collective-permute-start(bf16[784,128]{1,0:T(8,128)(2,1)S(1)} %collective-permute-done.11.refs_0_), channel_id=1, source_target_pairs={{0,4},{4,8},{8,12},{12,14},{14,10},{10,6},{6,2},{2,0},{1,5},{5,9},... | collective-permute-start | bytes 602120 | tf_op jit(solution)/shard_map/out_trail2/ppermute | solution.py:360
  32.8 8.6 %collective-permute-start.10 = (bf16[784,128]{1,0:T(8,128)(2,1)S(1)}, bf16[784,128]{1,0:T(8,128)(2,1)S(1)}, u32[]{:S(2)}, u32[]{:S(2)}) collective-permute-start(bf16[784,128]{1,0:T(8,128)(2,1)S(1)} %collective-permute-done.8.refs_1_), channel_id=1, source_target_pairs={{4,0},{8,4},{12,8},{14,12},{10,14},{6,10},{2,6},{0,2},{5,1},{9,5},... | collective-permute-start | bytes 602120 | tf_op jit(solution)/shard_map/out_lead3/ppermute | solution.py:360
  34.2 7.2 %collective-permute-start.9 = (bf16[784,128]{1,0:T(8,128)(2,1)S(1)}, bf16[784,128]{1,0:T(8,128)(2,1)S(1)}, u32[]{:S(2)}, u32[]{:S(2)}) collective-permute-start(bf16[784,128]{1,0:T(8,128)(2,1)S(1)} %collective-permute-done.7.refs_0_), channel_id=1, source_target_pairs={{0,4},{4,8},{8,12},{12,14},{14,10},{10,6},{6,2},{2,0},{1,5},{5,9},... | collective-permute-start | bytes 602120 | tf_op jit(solution)/shard_map/out_lead3/ppermute | solution.py:360
  37.1 10.1 %collective-permute-start.17 = (bf16[784,128]{1,0:T(8,128)(2,1)S(1)}, bf16[784,128]{1,0:T(8,128)(2,1)S(1)}, u32[]{:S(2)}, u32[]{:S(2)}) collective-permute-start(bf16[784,128]{1,0:T(8,128)(2,1)S(1)} %collective-permute-done.14.refs_1_), channel_id=1, source_target_pairs={{4,0},{8,4},{12,8},{14,12},{10,14},{6,10},{2,6},{0,2},{5,1},{9,5},... | collective-permute-start | bytes 602120 | tf_op jit(solution)/shard_map/out_trail3/ppermute | solution.py:360
  38.5 9.1 %collective-permute-start.16 = (bf16[784,128]{1,0:T(8,128)(2,1)S(1)}, bf16[784,128]{1,0:T(8,128)(2,1)S(1)}, u32[]{:S(2)}, u32[]{:S(2)}) collective-permute-start(bf16[784,128]{1,0:T(8,128)(2,1)S(1)} %collective-permute-done.13.refs_0_), channel_id=1, source_target_pairs={{0,4},{4,8},{8,12},{12,14},{14,10},{10,6},{6,2},{2,0},{1,5},{5,9},... | collective-permute-start | bytes 602120 | tf_op jit(solution)/shard_map/out_trail3/ppermute | solution.py:360
  41.4 9.3 %collective-permute-start.15 = (bf16[784,128]{1,0:T(8,128)(2,1)S(1)}, bf16[784,128]{1,0:T(8,128)(2,1)S(1)}, u32[]{:S(2)}, u32[]{:S(2)}) collective-permute-start(bf16[784,128]{1,0:T(8,128)(2,1)S(1)} %collective-permute-done.9.refs_0_), channel_id=1, source_target_pairs={{0,4},{4,8},{8,12},{12,14},{14,10},{10,6},{6,2},{2,0},{1,5},{5,9},... | collective-permute-start | bytes 602120 | tf_op jit(solution)/shard_map/out_lead4/ppermute | solution.py:360
  43.0 7.8 %collective-permute-start.18 = (bf16[784,128]{1,0:T(8,128)(2,1)S(1)}, bf16[784,128]{1,0:T(8,128)(2,1)S(1)}, u32[]{:S(2)}, u32[]{:S(2)}) collective-permute-start(bf16[784,128]{1,0:T(8,128)(2,1)S(1)} %collective-permute-done.10.refs_1_), channel_id=1, source_target_pairs={{4,0},{8,4},{12,8},{14,12},{10,14},{6,10},{2,6},{0,2},{5,1},{9,5},... | collective-permute-start | bytes 602120 | tf_op jit(solution)/shard_map/out_lead4/ppermute | solution.py:360
  45.5 9.4 %collective-permute-start.26 = (bf16[64,1536]{1,0:T(8,128)(2,1)S(1)}, bf16[64,1536]{1,0:T(8,128)(2,1)S(1)}, u32[]{:S(2)}, u32[]{:S(2)}) collective-permute-start(bf16[64,1536]{1,0:T(8,128)(2,1)S(1)} %get-tuple-element.145), channel_id=1, source_target_pairs={{0,4},{4,8},{8,12},{12,14},{14,10},{10,6},{6,2},{2,0},{1,5},{5,9},... | collective-permute-start | bytes 589832 | tf_op jit(solution)/shard_map/back_trail3/ppermute | solution.py:401
  47.1 7.8 %collective-permute-start.27 = (bf16[64,1536]{1,0:T(8,128)(2,1)S(1)}, bf16[64,1536]{1,0:T(8,128)(2,1)S(1)}, u32[]{:S(2)}, u32[]{:S(2)}) collective-permute-start(bf16[64,1536]{1,0:T(8,128)(2,1)S(1)} %get-tuple-element.122), channel_id=1, source_target_pairs={{4,0},{8,4},{12,8},{14,12},{10,14},{6,10},{2,6},{0,2},{5,1},{9,5},... | collective-permute-start | bytes 589832 | tf_op jit(solution)/shard_map/back_trail3/ppermute | solution.py:401
  52.8 5.7 %collective-permute-start.19 = (bf16[64,1536]{1,0:T(8,128)(2,1)S(1)}, bf16[64,1536]{1,0:T(8,128)(2,1)S(1)}, u32[]{:S(2)}, u32[]{:S(2)}) collective-permute-start(bf16[64,1536]{1,0:T(8,128)(2,1)S(1)} %get-tuple-element.130), channel_id=1, source_target_pairs={{0,4},{4,8},{8,12},{12,14},{14,10},{10,6},{6,2},{2,0},{1,5},{5,9},... | collective-permute-start | bytes 589832 | tf_op jit(solution)/shard_map/back_lead4/ppermute | solution.py:401
  53.8 7.7 %collective-permute-start.20 = (bf16[64,1536]{1,0:T(8,128)(2,1)S(1)}, bf16[64,1536]{1,0:T(8,128)(2,1)S(1)}, u32[]{:S(2)}, u32[]{:S(2)}) collective-permute-start(bf16[64,1536]{1,0:T(8,128)(2,1)S(1)} %get-tuple-element.131), channel_id=1, source_target_pairs={{4,0},{8,4},{12,8},{14,12},{10,14},{6,10},{2,6},{0,2},{5,1},{9,5},... | collective-permute-start | bytes 589832 | tf_op jit(solution)/shard_map/back_lead4/ppermute | solution.py:401
  61.5 7.8 %collective-permute-start.22 = (bf16[64,1536]{1,0:T(8,128)(2,1)S(1)}, bf16[64,1536]{1,0:T(8,128)(2,1)S(1)}, u32[]{:S(2)}, u32[]{:S(2)}) collective-permute-start(bf16[64,1536]{1,0:T(8,128)(2,1)S(1)} %add_convert_fusion.8), channel_id=1, source_target_pairs={{4,0},{8,4},{12,8},{14,12},{10,14},{6,10},{2,6},{0,2},{5,1},{9,5},... | collective-permute-start | bytes 589832 | tf_op jit(solution)/shard_map/back_lead3/ppermute | solution.py:401
  62.2 7.8 %collective-permute-start.21 = (bf16[64,1536]{1,0:T(8,128)(2,1)S(1)}, bf16[64,1536]{1,0:T(8,128)(2,1)S(1)}, u32[]{:S(2)}, u32[]{:S(2)}) collective-permute-start(bf16[64,1536]{1,0:T(8,128)(2,1)S(1)} %add_convert_fusion.9), channel_id=1, source_target_pairs={{0,4},{4,8},{8,12},{12,14},{14,10},{10,6},{6,2},{2,0},{1,5},{5,9},... | collective-permute-start | bytes 589832 | tf_op jit(solution)/shard_map/back_lead3/ppermute | solution.py:401
  63.8 9.8 %collective-permute-start.29 = (bf16[64,1536]{1,0:T(8,128)(2,1)S(1)}, bf16[64,1536]{1,0:T(8,128)(2,1)S(1)}, u32[]{:S(2)}, u32[]{:S(2)}) collective-permute-start(bf16[64,1536]{1,0:T(8,128)(2,1)S(1)} %add_convert_fusion.3), channel_id=1, source_target_pairs={{4,0},{8,4},{12,8},{14,12},{10,14},{6,10},{2,6},{0,2},{5,1},{9,5},... | collective-permute-start | bytes 589832 | tf_op jit(solution)/shard_map/back_trail2/ppermute | solution.py:401
  64.5 9.8 %collective-permute-start.28 = (bf16[64,1536]{1,0:T(8,128)(2,1)S(1)}, bf16[64,1536]{1,0:T(8,128)(2,1)S(1)}, u32[]{:S(2)}, u32[]{:S(2)}) collective-permute-start(bf16[64,1536]{1,0:T(8,128)(2,1)S(1)} %add_convert_fusion.4), channel_id=1, source_target_pairs={{0,4},{4,8},{8,12},{12,14},{14,10},{10,6},{6,2},{2,0},{1,5},{5,9},... | collective-permute-start | bytes 589832 | tf_op jit(solution)/shard_map/back_trail2/ppermute | solution.py:401
  70.1 8.5 %collective-permute-start.24 = (bf16[64,1536]{1,0:T(8,128)(2,1)S(1)}, bf16[64,1536]{1,0:T(8,128)(2,1)S(1)}, u32[]{:S(2)}, u32[]{:S(2)}) collective-permute-start(bf16[64,1536]{1,0:T(8,128)(2,1)S(1)} %add_convert_fusion.6), channel_id=1, source_target_pairs={{4,0},{8,4},{12,8},{14,12},{10,14},{6,10},{2,6},{0,2},{5,1},{9,5},... | collective-permute-start | bytes 589832 | tf_op jit(solution)/shard_map/back_lead2/ppermute | solution.py:401
  71.1 7.5 %collective-permute-start.23 = (bf16[64,1536]{1,0:T(8,128)(2,1)S(1)}, bf16[64,1536]{1,0:T(8,128)(2,1)S(1)}, u32[]{:S(2)}, u32[]{:S(2)}) collective-permute-start(bf16[64,1536]{1,0:T(8,128)(2,1)S(1)} %add_convert_fusion.7), channel_id=1, source_target_pairs={{0,4},{4,8},{8,12},{12,14},{14,10},{10,6},{6,2},{2,0},{1,5},{5,9},... | collective-permute-start | bytes 589832 | tf_op jit(solution)/shard_map/back_lead2/ppermute | solution.py:401
  74.3 6.5 %collective-permute-start.30 = (bf16[64,1536]{1,0:T(8,128)(2,1)S(1)}, bf16[64,1536]{1,0:T(8,128)(2,1)S(1)}, u32[]{:S(2)}, u32[]{:S(2)}) collective-permute-start(bf16[64,1536]{1,0:T(8,128)(2,1)S(1)} %add_convert_fusion.2), channel_id=1, source_target_pairs={{4,0},{8,4},{12,8},{14,12},{10,14},{6,10},{2,6},{0,2},{5,1},{9,5},... | collective-permute-start | bytes 589832 | tf_op jit(solution)/shard_map/back_trail1/ppermute | solution.py:401
  75.3 9.1 %collective-permute-start.31 = (bf16[64,1536]{1,0:T(8,128)(2,1)S(1)}, bf16[64,1536]{1,0:T(8,128)(2,1)S(1)}, u32[]{:S(2)}, u32[]{:S(2)}) collective-permute-start(bf16[64,1536]{1,0:T(8,128)(2,1)S(1)} %add_convert_fusion.1), channel_id=1, source_target_pairs={{0,4},{4,8},{8,12},{12,14},{14,10},{10,6},{6,2},{2,0},{1,5},{5,9},... | collective-permute-start | bytes 589832 | tf_op jit(solution)/shard_map/back_trail1/ppermute | solution.py:401
  78.6 5.7 %collective-permute-start.25 = (bf16[64,1536]{1,0:T(8,128)(2,1)S(1)}, bf16[64,1536]{1,0:T(8,128)(2,1)S(1)}, u32[]{:S(2)}, u32[]{:S(2)}) collective-permute-start(bf16[64,1536]{1,0:T(8,128)(2,1)S(1)} %add_convert_fusion.5), channel_id=1, source_target_pairs={{0,4},{4,8},{8,12},{12,14},{14,10},{10,6},{6,2},{2,0},{1,5},{5,9},... | collective-permute-start | bytes 589832 | tf_op jit(solution)/shard_map/back_lead1/ppermute | solution.py:401
  80.2 5.7 %collective-permute-start.32 = (bf16[64,1536]{1,0:T(8,128)(2,1)S(1)}, bf16[64,1536]{1,0:T(8,128)(2,1)S(1)}, u32[]{:S(2)}, u32[]{:S(2)}) collective-permute-start(bf16[64,1536]{1,0:T(8,128)(2,1)S(1)} %add_convert_fusion), channel_id=1, source_target_pairs={{4,0},{8,4},{12,8},{14,12},{10,14},{6,10},{2,6},{0,2},{5,1},{9,5},... | collective-permute-start | bytes 589832 | tf_op jit(solution)/shard_map/back_lead1/ppermute | solution.py:401

commit v14 on v13

--- a/solution.py
+++ b/solution.py
@@ -19,9 +19,11 @@
 EXPERT_VMEM = 8 * MIB
 
 
-def shifted(value, axis, by):
+def neighbours(value, axis):
     peers = lax.axis_size(axis)
-    return lax.ppermute(value, axis, [(i, (i + by) % peers) for i in range(peers)])
+    within = [(i, i ^ 1) for i in range(peers)]
+    across = [(i, i if i in (0, peers - 1) else ((i + 1) ^ 1) - 1) for i in range(peers)]
+    return lax.ppermute(value, axis, within), lax.ppermute(value, axis, across)
 
 
 def pinned(values, space):
@@ -68,11 +70,12 @@
 def attend_kernel(mix, *refs):
     if mix:
         sink_ref, q_ref, k_ref, v_ref, ow_ref = refs[:5]
-        first_ref, before_ref, rank_ref, later_ref, send_ref, own_ref, done_ref = refs[5:]
+        place_ref, one_ref, two_ref, rank_ref, later_ref, send_ref, own_ref, done_ref = refs[5:]
         rows = later_ref.shape[0]
         queries = slice(0, rows)
-        k = jnp.concatenate([before_ref[:rows], k_ref[:rows]], axis=0)
-        v = jnp.concatenate([before_ref[rows:], v_ref[:rows]], axis=0)
+        before = jnp.where(place_ref[1] == 1, one_ref[...], two_ref[...])
+        k = jnp.concatenate([before[:rows], k_ref[:rows]], axis=0)
+        v = jnp.concatenate([before[rows:], v_ref[:rows]], axis=0)
         done_ref[rows:] = later_ref[...]
         copies = []
     else:
@@ -104,7 +107,7 @@
     query = lax.broadcasted_iota(jnp.int32, (keys, rows), 1)
     allowed = (key <= query + rows) & (key > query)
     if mix:
-        allowed = allowed & (key >= jnp.where(first_ref[0] == 1, rows, 0))
+        allowed = allowed & (key >= jnp.where(place_ref[0] == 1, rows, 0))
     ones = jnp.ones((8, keys), jnp.float32)
     zeros = jnp.zeros((8, keys), jnp.float32)
 
@@ -174,7 +177,7 @@
         shapes += (jax.ShapeDtypeStruct((rows, width), jnp.bfloat16),)
     return pl.pallas_call(
         functools.partial(attend_kernel, mix),
-        in_specs=[vmem if mix else hbm] * 5 + ([smem, vmem, smem, vmem] if mix else []),
+        in_specs=[vmem if mix else hbm] * 5 + ([smem, vmem, vmem, smem, vmem] if mix else []),
         out_specs=(vmem,) * len(shapes),
         out_shape=shapes,
         scratch_shapes=[
@@ -376,10 +379,8 @@
         if distance < far:
             before = [came[side, distance - 1, side] for side in sides] if distance > 1 else []
             bring(distance, False, *before)
-            if 1 < distance < far - 1:
+            if distance > 1:
                 trails = [came[side, distance, 1 - side] for side in sides]
-        else:
-            trails = [came[side, far - 1, 1 - side] for side in sides]
         latest = apply(distance, (True,), worked[distance - 1], *trails)
     latest = apply(far - 1, (False,), latest)
 
@@ -477,15 +478,15 @@
     gate_weight, up_weight, down_weight = gate_weight[0], up_weight[0], down_weight[0]
     use_ring = EXP_DEV * lax.axis_size("seq") <= 2 * TOP
 
-    before = shifted(tail(key_rows, value_rows), "seq", 1)
+    before = neighbours(tail(key_rows, value_rows), "seq")
     others = []
     if use_ring:
         others = [swapped(w, "rep") for w in (gate_weight, up_weight, down_weight)]
-    first = (seq == 0).astype(jnp.int32).reshape(1)
+    place = jnp.stack([seq == 0, seq % 2 == 1]).astype(jnp.int32)
     *operands, later_half = attend(
         sink_logits.reshape(1, -1), queries, key_rows, value_rows, out_weight
     )
-    send, own = attend(*operands, (first, before, rank, later_half))
+    send, own = attend(*operands, (place, *before, rank, later_half))
     came = swapped(send, "rep")
     expert_count = lax.axis_size("seq") * EXP_DEV if use_ring else 0
     residual, *pieces = norm(

time: 87 us -> 87.6 us (level)
  waiting for transfers between devices: 26.3 us -> 22.4 us
  starting transfers between devices: 32.7 us -> 36.5 us
    ppermute x1 -> x2, waiting for transfers between devices: 2.96 us -> 0.01 us  [the longest x1 0.01 us: neighbours(): lax.ppermute(value, axis, within)]
    ppermute x14, starting transfers between devices: 14.3 us -> 16.4 us  [bring(): came[side, distance, piece] = lax.ppermute(block, 'seq', hops[side])]
    ppermute x14, waiting for transfers between devices: 13.5 us -> 11.6 us  [send(): moving[side, piece] = lax.ppermute(value, 'seq', hops[side])]
    ppermute x1 -> x2, starting transfers between devices: 2.54 us -> 4.04 us  [the longest x1 2.55 us: neighbours(): lax.ppermute(value, axis, within)]
    ppermute x14, waiting for transfers between devices: 8.23 us -> 9.26 us  [bring(): came[side, distance, piece] = lax.ppermute(block, 'seq', hops[side])]
  transfers between devices with their start and end apart: 33 -> 34, of which waited for: 18 -> 15; matrix products, arithmetic and copies ran while one was open for 1% -> 1% of each run, Pallas kernels for 30% -> 30%
where the time goes in v14:
time: 87.6 us; the launch traced here: 87.4 us
  starting transfers between devices  36.5 us (42%)
  Pallas kernels  26.6 us (30%)
  waiting for transfers between devices  22.4 us (26%)
  other arithmetic  1.52 us (2%)
    pallas_call x8, Pallas kernels, experts(): pl.pallas_call(functools.partial(expert_kernel, min(256, half), len(block...  18.8 us
    ppermute x14, starting transfers between devices, bring(): came[side, distance, piece] = lax.ppermute(block, 'seq', hops[side])  16.4 us
    ppermute x14, starting transfers between devices, send(): moving[side, piece] = lax.ppermute(value, 'seq', hops[side])  14.8 us
    ppermute x14, waiting for transfers between devices, send(): moving[side, piece] = lax.ppermute(value, 'seq', hops[side])  11.6 us
    ppermute x14, waiting for transfers between devices, bring(): came[side, distance, piece] = lax.ppermute(block, 'seq', hops[side])  9.26 us
    pallas_call x2, Pallas kernels, attend(): pl.pallas_call(functools.partial(attend_kernel, mix), in_specs=[vmem if m...  6.11 us
    ppermute x1, starting transfers between devices, neighbours(): lax.ppermute(value, axis, within)  2.55 us
  transfers between devices with their start and end apart: 34, of which 15 were waited for; matrix products, arithmetic and copies ran while one was open for 1% of the time, Pallas kernels for 30%

profile of v14, /device:TPU:0, one launch (start us, length us, event | category | flops | bytes accessed | tf_op | source)
XLA Modules:
  0.0 87.4 jit_solution(1154754588866163498)
XLA Ops:
  0.0 0.5 collective-permute-start.3
  0.5 0.5 collective-permute-start.5
  1.0 1.4 %tail.1 = bf16[256,128]{1,0:T(8,128)(2,1)} custom-call(bf16[256,128]{1,0:T(8,128)(2,1)} %keys_hbm.1, bf16[256,128]{1,0:T(8,128)(2,1)} %values_hbm.1), custom_call_target="tpu_custom_call" | custom-call | tf_op jit(solution)/shard_map/tail/pallas_call | solution.py:60
  2.4 2.6 %collective-permute-start = (bf16[256,128]{1,0:T(8,128)(2,1)}, bf16[256,128]{1,0:T(8,128)(2,1)S(1)}, u32[]{:S(2)}, u32[]{:S(2)}) collective-permute-start(bf16[256,128]{1,0:T(8,128)(2,1)} %tail.1), channel_id=1, source_target_pairs={{0,2},{2,0},{4,6},{6,4},{8,10},{10,8},{12,14},{14,12},{1,3},{3,1},... | collective-permute-start | bytes 196616 | tf_op jit(solution)/shard_map/ppermute | solution.py:26
  4.9 1.5 %collective-permute-start.1 = (bf16[256,128]{1,0:T(8,128)(2,1)}, bf16[256,128]{1,0:T(8,128)(2,1)S(1)}, u32[]{:S(2)}, u32[]{:S(2)}) collective-permute-start(bf16[256,128]{1,0:T(8,128)(2,1)} %tail.1), channel_id=1, source_target_pairs={{0,0},{2,4},{4,2},{6,8},{8,6},{10,12},{12,10},{14,14},{1,1},{3,5},... | collective-permute-start | bytes 196616 | tf_op jit(solution)/shard_map/ppermute | solution.py:26
  6.5 3.0 %attend.2 = (f32[1,16]{1,0:T(1,128)S(1)}, bf16[256,1024]{1,0:T(8,128)(2,1)S(1)}, bf16[256,128]{1,0:T(8,128)(2,1)S(1)}, bf16[256,128]{1,0:T(8,128)(2,1)S(1)}, bf1...) custom-call(f32[1,16]{1,0:T(1,128)} %bitcast.39, bf16[256,1024]{1,0:T(8,128)(2,1)} %refs_1_.1, ...), custom_call_target="tpu_custom_call" | custom-call | flops 671088640 | bytes 6291456 | tf_op jit(solution)/shard_map/attend/pallas_call | solution.py:178
  9.6 3.1 %attend.3 = (bf16[128,1536]{1,0:T(8,128)(2,1)S(1)}, f32[128,1536]{1,0:T(8,128)S(1)}) custom-call(f32[1,16]{1,0:T(1,128)S(1)} %get-tuple-element.82.refs_0_, bf16[256,1024]{1,0:T(8,128)(2,1)S(1)} %get-tuple-element.83.refs_1_, bf16[256,128]{1,0:T(8,128)(2,1)S(1)} %get-tuple-element.84.refs_2_, bf16[256,128]{1,0:T(8,128)(2,1)S(1)} %get-tuple-element.85.refs_3_, ...), custom_call_target="tpu_custom_call" | custom-call | flops 671088640 | bytes 6291456 | tf_op jit(solution)/shard_map/attend/pallas_call | solution.py:178
  13.0 1.5 %collective-permute-done.2.came_ref = bf16[128,1536]{1,0:T(8,128)(2,1)S(1)} collective-permute-done((bf16[128,1536]{1,0:T(8,128)(2,1)S(1)}, bf16[128,1536]{1,0:T(8,128)(2,1)S(1)}, u32[]{:S(2)}, u32[]{:S(2)}) %collective-permute-start.2) | collective-permute-done | bytes 393248 | tf_op jit(solution)/shard_map/ppermute | solution.py:39
  14.9 4.2 %collective-permute-start.6 = (bf16[784,128]{1,0:T(8,128)(2,1)S(1)}, bf16[784,128]{1,0:T(8,128)(2,1)S(1)}, u32[]{:S(2)}, u32[]{:S(2)}) collective-permute-start(bf16[784,128]{1,0:T(8,128)(2,1)S(1)} %get-tuple-element.96.refs_0_), channel_id=1, source_target_pairs={{0,4},{4,8},{8,12},{12,14},{14,10},{10,6},{6,2},{2,0},{1,5},{5,9},... | collective-permute-start | bytes 602120 | tf_op jit(solution)/shard_map/out_lead1/ppermute | solution.py:363
  19.1 2.0 %collective-permute-start.12 = (bf16[784,128]{1,0:T(8,128)(2,1)S(1)}, bf16[784,128]{1,0:T(8,128)(2,1)S(1)}, u32[]{:S(2)}, u32[]{:S(2)}) collective-permute-start(bf16[784,128]{1,0:T(8,128)(2,1)S(1)} %get-tuple-element.97.refs_1_), channel_id=1, source_target_pairs={{0,4},{4,8},{8,12},{12,14},{14,10},{10,6},{6,2},{2,0},{1,5},{5,9},... | collective-permute-start | bytes 602120 | tf_op jit(solution)/shard_map/out_trail1/ppermute | solution.py:363
  21.2 4.1 %experts.8 = (bf16[64,1536]{1,0:T(8,128)(2,1)S(1)}, bf16[64,1536]{1,0:T(8,128)(2,1)S(1)}, bf16[1536,768]{1,0:T(8,128)(2,1)S(1)}, bf16[1536,768]{1,0:T(8,128)(2,1)S(1)}, bf16[768,1536]{1,0:T(8,128)(2,1)S(1)}) custom-call(s32[1]{0:T(128)} %bitcast.6.me_ref, bf16[784,128]{1,0:T(8,128)(2,1)S(1)} %get-tuple-element.96.refs_0_, ...), custom_call_target="tpu_custom_call" | custom-call | flops 1811939328 | bytes 1179648 | tf_op jit(solution)/shard_map/experts/pallas_call | solution.py:314
  25.3 1.7 %collective-permute-done.7.refs_1_ = bf16[784,128]{1,0:T(8,128)(2,1)S(1)} collective-permute-done((bf16[784,128]{1,0:T(8,128)(2,1)S(1)}, bf16[784,128]{1,0:T(8,128)(2,1)S(1)}, u32[]{:S(2)}, u32[]{:S(2)}) %collective-permute-start.7) | collective-permute-done | bytes 200736 | tf_op jit(solution)/shard_map/out_lead1/ppermute | solution.py:363
  27.0 1.6 %collective-permute-start.8 = (bf16[784,128]{1,0:T(8,128)(2,1)S(1)}, bf16[784,128]{1,0:T(8,128)(2,1)S(1)}, u32[]{:S(2)}, u32[]{:S(2)}) collective-permute-start(bf16[784,128]{1,0:T(8,128)(2,1)S(1)} %collective-permute-done.6.refs_0_), channel_id=1, source_target_pairs={{0,4},{4,8},{8,12},{12,14},{14,10},{10,6},{6,2},{2,0},{1,5},{5,9},... | collective-permute-start | bytes 602120 | tf_op jit(solution)/shard_map/out_lead2/ppermute | solution.py:363
  29.0 2.3 %collective-permute-done.13.refs_1_ = bf16[784,128]{1,0:T(8,128)(2,1)S(1)} collective-permute-done((bf16[784,128]{1,0:T(8,128)(2,1)S(1)}, bf16[784,128]{1,0:T(8,128)(2,1)S(1)}, u32[]{:S(2)}, u32[]{:S(2)}) %collective-permute-start.13) | collective-permute-done | bytes 200736 | tf_op jit(solution)/shard_map/out_trail1/ppermute | solution.py:363
  31.3 2.0 %collective-permute-start.14 = (bf16[784,128]{1,0:T(8,128)(2,1)S(1)}, bf16[784,128]{1,0:T(8,128)(2,1)S(1)}, u32[]{:S(2)}, u32[]{:S(2)}) collective-permute-start(bf16[784,128]{1,0:T(8,128)(2,1)S(1)} %collective-permute-done.12.refs_0_), channel_id=1, source_target_pairs={{0,4},{4,8},{8,12},{12,14},{14,10},{10,6},{6,2},{2,0},{1,5},{5,9},... | collective-permute-start | bytes 602120 | tf_op jit(solution)/shard_map/out_trail2/ppermute | solution.py:363
  33.3 2.1 %experts.9 = (bf16[64,1536]{1,0:T(8,128)(2,1)S(1)}, bf16[64,1536]{1,0:T(8,128)(2,1)S(1)}) custom-call(s32[1]{0:T(128)} %bitcast.6.me_ref, bf16[784,128]{1,0:T(8,128)(2,1)S(1)} %collective-permute-done.6.refs_0_, bf16[784,128]{1,0:T(8,128)(2,1)S(1)} %collective-permute-done.7.refs_1_, bf16[1536,768]{1,0:T(8,128)(2,1)S(1)} %bitcast.12, ...), custom_call_target="tpu_custom_call" | custom-call | flops 1811939328 | bytes 1179648 | tf_op jit(solution)/shard_map/hop1/experts/pallas_call | solution.py:314
  35.4 1.1 %collective-permute-done.9.refs_1_ = bf16[784,128]{1,0:T(8,128)(2,1)S(1)} collective-permute-done((bf16[784,128]{1,0:T(8,128)(2,1)S(1)}, bf16[784,128]{1,0:T(8,128)(2,1)S(1)}, u32[]{:S(2)}, u32[]{:S(2)}) %collective-permute-start.9) | collective-permute-done | bytes 200736 | tf_op jit(solution)/shard_map/out_lead2/ppermute | solution.py:363
  36.9 1.6 %collective-permute-start.10 = (bf16[784,128]{1,0:T(8,128)(2,1)S(1)}, bf16[784,128]{1,0:T(8,128)(2,1)S(1)}, u32[]{:S(2)}, u32[]{:S(2)}) collective-permute-start(bf16[784,128]{1,0:T(8,128)(2,1)S(1)} %collective-permute-done.8.refs_0_), channel_id=1, source_target_pairs={{0,4},{4,8},{8,12},{12,14},{14,10},{10,6},{6,2},{2,0},{1,5},{5,9},... | collective-permute-start | bytes 602120 | tf_op jit(solution)/shard_map/out_lead3/ppermute | solution.py:363
  38.5 2.3 %collective-permute-done.15.refs_1_ = bf16[784,128]{1,0:T(8,128)(2,1)S(1)} collective-permute-done((bf16[784,128]{1,0:T(8,128)(2,1)S(1)}, bf16[784,128]{1,0:T(8,128)(2,1)S(1)}, u32[]{:S(2)}, u32[]{:S(2)}) %collective-permute-start.15) | collective-permute-done | bytes 200736 | tf_op jit(solution)/shard_map/out_trail2/ppermute | solution.py:363
  41.2 1.6 %collective-permute-start.17 = (bf16[784,128]{1,0:T(8,128)(2,1)S(1)}, bf16[784,128]{1,0:T(8,128)(2,1)S(1)}, u32[]{:S(2)}, u32[]{:S(2)}) collective-permute-start(bf16[784,128]{1,0:T(8,128)(2,1)S(1)} %collective-permute-done.14.refs_0_), channel_id=1, source_target_pairs={{0,4},{4,8},{8,12},{12,14},{14,10},{10,6},{6,2},{2,0},{1,5},{5,9},... | collective-permute-start | bytes 602120 | tf_op jit(solution)/shard_map/out_trail3/ppermute | solution.py:363
  42.8 2.1 %experts.10 = (bf16[64,1536]{1,0:T(8,128)(2,1)S(1)}, bf16[64,1536]{1,0:T(8,128)(2,1)S(1)}) custom-call(s32[1]{0:T(128)} %bitcast.6.me_ref, bf16[784,128]{1,0:T(8,128)(2,1)S(1)} %collective-permute-done.8.refs_0_, bf16[784,128]{1,0:T(8,128)(2,1)S(1)} %collective-permute-done.9.refs_1_, bf16[1536,768]{1,0:T(8,128)(2,1)S(1)} %bitcast.13, ...), custom_call_target="tpu_custom_call" | custom-call | flops 1811939328 | bytes 1179648 | tf_op jit(solution)/shard_map/hop2/experts/pallas_call | solution.py:314
  45.1 1.6 %collective-permute-start.16 = (bf16[784,128]{1,0:T(8,128)(2,1)S(1)}, bf16[784,128]{1,0:T(8,128)(2,1)S(1)}, u32[]{:S(2)}, u32[]{:S(2)}) collective-permute-start(bf16[784,128]{1,0:T(8,128)(2,1)S(1)} %collective-permute-done.10.refs_0_), channel_id=1, source_target_pairs={{0,4},{4,8},{8,12},{12,14},{14,10},{10,6},{6,2},{2,0},{1,5},{5,9},... | collective-permute-start | bytes 602120 | tf_op jit(solution)/shard_map/out_lead4/ppermute | solution.py:363
  46.7 0.4 collective-permute-start.19
  47.1 1.8 %collective-permute-done.18.refs_1_ = bf16[784,128]{1,0:T(8,128)(2,1)S(1)} collective-permute-done((bf16[784,128]{1,0:T(8,128)(2,1)S(1)}, bf16[784,128]{1,0:T(8,128)(2,1)S(1)}, u32[]{:S(2)}, u32[]{:S(2)}) %collective-permute-start.18) | collective-permute-done | bytes 200736 | tf_op jit(solution)/shard_map/out_trail3/ppermute | solution.py:363
  48.9 2.1 %experts.11 = (bf16[64,1536]{1,0:T(8,128)(2,1)S(1)}, bf16[64,1536]{1,0:T(8,128)(2,1)S(1)}) custom-call(s32[1]{0:T(128)} %bitcast.6.me_ref, bf16[784,128]{1,0:T(8,128)(2,1)S(1)} %collective-permute-done.10.refs_0_, bf16[784,128]{1,0:T(8,128)(2,1)S(1)} %collective-permute-done.11.refs_1_, bf16[1536,768]{1,0:T(8,128)(2,1)S(1)} %bitcast.14, ...), custom_call_target="tpu_custom_call" | custom-call | flops 1811939328 | bytes 1179648 | tf_op jit(solution)/shard_map/hop3/experts/pallas_call | solution.py:314
  51.0 1.5 %collective-permute-start.27 = (bf16[64,1536]{1,0:T(8,128)(2,1)S(1)}, bf16[64,1536]{1,0:T(8,128)(2,1)S(1)}, u32[]{:S(2)}, u32[]{:S(2)}) collective-permute-start(bf16[64,1536]{1,0:T(8,128)(2,1)S(1)} %get-tuple-element.145), channel_id=1, source_target_pairs={{0,4},{4,8},{8,12},{12,14},{14,10},{10,6},{6,2},{2,0},{1,5},{5,9},... | collective-permute-start | bytes 589832 | tf_op jit(solution)/shard_map/back_trail3/ppermute | solution.py:402
  52.4 0.6 collective-permute-start.28
  53.1 2.1 %experts.12 = (bf16[64,1536]{1,0:T(8,128)(2,1)S(1)}, bf16[64,1536]{1,0:T(8,128)(2,1)S(1)}) custom-call(s32[1]{0:T(128)} %bitcast.6.me_ref, bf16[784,128]{1,0:T(8,128)(2,1)S(1)} %collective-permute-done.16.refs_0_, bf16[784,128]{1,0:T(8,128)(2,1)S(1)} %collective-permute-done.19.refs_1_, bf16[1536,768]{1,0:T(8,128)(2,1)S(1)} %bitcast.15, ...), custom_call_target="tpu_custom_call" | custom-call | flops 1811939328 | bytes 1179648 | tf_op jit(solution)/shard_map/hop4/experts/pallas_call | solution.py:314
  55.2 1.5 %collective-permute-start.20 = (bf16[64,1536]{1,0:T(8,128)(2,1)S(1)}, bf16[64,1536]{1,0:T(8,128)(2,1)S(1)}, u32[]{:S(2)}, u32[]{:S(2)}) collective-permute-start(bf16[64,1536]{1,0:T(8,128)(2,1)S(1)} %get-tuple-element.130), channel_id=1, source_target_pairs={{0,4},{4,8},{8,12},{12,14},{14,10},{10,6},{6,2},{2,0},{1,5},{5,9},... | collective-permute-start | bytes 589832 | tf_op jit(solution)/shard_map/back_lead4/ppermute | solution.py:402
  56.6 0.6 collective-permute-start.21
  57.3 1.3 %collective-permute-done.27 = bf16[64,1536]{1,0:T(8,128)(2,1)S(1)} collective-permute-done((bf16[64,1536]{1,0:T(8,128)(2,1)S(1)}, bf16[64,1536]{1,0:T(8,128)(2,1)S(1)}, u32[]{:S(2)}, u32[]{:S(2)}) %collective-permute-start.27) | collective-permute-done | bytes 196640 | tf_op jit(solution)/shard_map/back_trail3/ppermute | solution.py:402
  58.6 1.2 %collective-permute-done.28 = bf16[64,1536]{1,0:T(8,128)(2,1)S(1)} collective-permute-done((bf16[64,1536]{1,0:T(8,128)(2,1)S(1)}, bf16[64,1536]{1,0:T(8,128)(2,1)S(1)}, u32[]{:S(2)}, u32[]{:S(2)}) %collective-permute-start.28) | collective-permute-done | bytes 196640 | tf_op jit(solution)/shard_map/back_trail3/ppermute | solution.py:402
  59.8 2.1 %experts.13 = (bf16[64,1536]{1,0:T(8,128)(2,1)S(1)}, bf16[64,1536]{1,0:T(8,128)(2,1)S(1)}) custom-call(s32[1]{0:T(128)} %bitcast.6.me_ref, bf16[784,128]{1,0:T(8,128)(2,1)S(1)} %collective-permute-done.17.refs_0_, bf16[784,128]{1,0:T(8,128)(2,1)S(1)} %collective-permute-done.18.refs_1_, bf16[1536,768]{1,0:T(8,128)(2,1)S(1)} %bitcast.16, ...), custom_call_target="tpu_custom_call" | custom-call | flops 1811939328 | bytes 1179648 | tf_op jit(solution)/shard_map/hop3/experts/pallas_call | solution.py:314
  62.4 0.6 collective-permute-start.23
  63.1 1.5 %collective-permute-start.22 = (bf16[64,1536]{1,0:T(8,128)(2,1)S(1)}, bf16[64,1536]{1,0:T(8,128)(2,1)S(1)}, u32[]{:S(2)}, u32[]{:S(2)}) collective-permute-start(bf16[64,1536]{1,0:T(8,128)(2,1)S(1)} %add_convert_fusion.9), channel_id=1, source_target_pairs={{0,4},{4,8},{8,12},{12,14},{14,10},{10,6},{6,2},{2,0},{1,5},{5,9},... | collective-permute-start | bytes 589832 | tf_op jit(solution)/shard_map/back_lead3/ppermute | solution.py:402
  64.6 0.6 collective-permute-start.30
  65.3 1.5 %collective-permute-start.29 = (bf16[64,1536]{1,0:T(8,128)(2,1)S(1)}, bf16[64,1536]{1,0:T(8,128)(2,1)S(1)}, u32[]{:S(2)}, u32[]{:S(2)}) collective-permute-start(bf16[64,1536]{1,0:T(8,128)(2,1)S(1)} %add_convert_fusion.4), channel_id=1, source_target_pairs={{0,4},{4,8},{8,12},{12,14},{14,10},{10,6},{6,2},{2,0},{1,5},{5,9},... | collective-permute-start | bytes 589832 | tf_op jit(solution)/shard_map/back_trail2/ppermute | solution.py:402
  66.8 2.1 %experts.14 = (bf16[64,1536]{1,0:T(8,128)(2,1)S(1)}, bf16[64,1536]{1,0:T(8,128)(2,1)S(1)}) custom-call(s32[1]{0:T(128)} %bitcast.6.me_ref, bf16[784,128]{1,0:T(8,128)(2,1)S(1)} %collective-permute-done.14.refs_0_, bf16[784,128]{1,0:T(8,128)(2,1)S(1)} %collective-permute-done.15.refs_1_, bf16[1536,768]{1,0:T(8,128)(2,1)S(1)} %bitcast.17, ...), custom_call_target="tpu_custom_call" | custom-call | flops 1811939328 | bytes 1179648 | tf_op jit(solution)/shard_map/hop2/experts/pallas_call | solution.py:314
  68.9 1.2 %collective-permute-done.23 = bf16[64,1536]{1,0:T(8,128)(2,1)S(1)} collective-permute-done((bf16[64,1536]{1,0:T(8,128)(2,1)S(1)}, bf16[64,1536]{1,0:T(8,128)(2,1)S(1)}, u32[]{:S(2)}, u32[]{:S(2)}) %collective-permute-start.23) | collective-permute-done | bytes 196640 | tf_op jit(solution)/shard_map/back_lead3/ppermute | solution.py:402
  70.5 1.9 %collective-permute-start.24 = (bf16[64,1536]{1,0:T(8,128)(2,1)S(1)}, bf16[64,1536]{1,0:T(8,128)(2,1)S(1)}, u32[]{:S(2)}, u32[]{:S(2)}) collective-permute-start(bf16[64,1536]{1,0:T(8,128)(2,1)S(1)} %add_convert_fusion.7), channel_id=1, source_target_pairs={{0,4},{4,8},{8,12},{12,14},{14,10},{10,6},{6,2},{2,0},{1,5},{5,9},... | collective-permute-start | bytes 589832 | tf_op jit(solution)/shard_map/back_lead2/ppermute | solution.py:402
  72.4 2.0 %collective-permute-done.30 = bf16[64,1536]{1,0:T(8,128)(2,1)S(1)} collective-permute-done((bf16[64,1536]{1,0:T(8,128)(2,1)S(1)}, bf16[64,1536]{1,0:T(8,128)(2,1)S(1)}, u32[]{:S(2)}, u32[]{:S(2)}) %collective-permute-start.30) | collective-permute-done | bytes 196640 | tf_op jit(solution)/shard_map/back_trail2/ppermute | solution.py:402
  74.7 1.9 %collective-permute-start.32 = (bf16[64,1536]{1,0:T(8,128)(2,1)S(1)}, bf16[64,1536]{1,0:T(8,128)(2,1)S(1)}, u32[]{:S(2)}, u32[]{:S(2)}) collective-permute-start(bf16[64,1536]{1,0:T(8,128)(2,1)S(1)} %add_convert_fusion.1), channel_id=1, source_target_pairs={{0,4},{4,8},{8,12},{12,14},{14,10},{10,6},{6,2},{2,0},{1,5},{5,9},... | collective-permute-start | bytes 589832 | tf_op jit(solution)/shard_map/back_trail1/ppermute | solution.py:402
  76.6 2.1 %experts.15 = (bf16[64,1536]{1,0:T(8,128)(2,1)S(1)}, bf16[64,1536]{1,0:T(8,128)(2,1)S(1)}) custom-call(s32[1]{0:T(128)} %bitcast.6.me_ref, bf16[784,128]{1,0:T(8,128)(2,1)S(1)} %collective-permute-done.12.refs_0_, bf16[784,128]{1,0:T(8,128)(2,1)S(1)} %collective-permute-done.13.refs_1_, bf16[1536,768]{1,0:T(8,128)(2,1)S(1)} %bitcast.18, ...), custom_call_target="tpu_custom_call" | custom-call | flops 1811939328 | bytes 1179648 | tf_op jit(solution)/shard_map/hop1/experts/pallas_call | solution.py:314
  78.8 1.9 %collective-permute-start.26 = (bf16[64,1536]{1,0:T(8,128)(2,1)S(1)}, bf16[64,1536]{1,0:T(8,128)(2,1)S(1)}, u32[]{:S(2)}, u32[]{:S(2)}) collective-permute-start(bf16[64,1536]{1,0:T(8,128)(2,1)S(1)} %add_convert_fusion.5), channel_id=1, source_target_pairs={{0,4},{4,8},{8,12},{12,14},{14,10},{10,6},{6,2},{2,0},{1,5},{5,9},... | collective-permute-start | bytes 589832 | tf_op jit(solution)/shard_map/back_lead1/ppermute | solution.py:402
  81.0 1.1 %collective-permute-done.31 = bf16[64,1536]{1,0:T(8,128)(2,1)S(1)} collective-permute-done((bf16[64,1536]{1,0:T(8,128)(2,1)S(1)}, bf16[64,1536]{1,0:T(8,128)(2,1)S(1)}, u32[]{:S(2)}, u32[]{:S(2)}) %collective-permute-start.31) | collective-permute-done | bytes 196640 | tf_op jit(solution)/shard_map/back_trail1/ppermute | solution.py:402
  82.1 2.5 %collective-permute-done.26 = bf16[64,1536]{1,0:T(8,128)(2,1)S(1)} collective-permute-done((bf16[64,1536]{1,0:T(8,128)(2,1)S(1)}, bf16[64,1536]{1,0:T(8,128)(2,1)S(1)}, u32[]{:S(2)}, u32[]{:S(2)}) %collective-permute-start.26) | collective-permute-done | bytes 196640 | tf_op jit(solution)/shard_map/back_lead1/ppermute | solution.py:402
  84.6 1.9 %collective-permute-done.33 = bf16[64,1536]{1,0:T(8,128)(2,1)S(1)} collective-permute-done((bf16[64,1536]{1,0:T(8,128)(2,1)S(1)}, bf16[64,1536]{1,0:T(8,128)(2,1)S(1)}, u32[]{:S(2)}, u32[]{:S(2)}) %collective-permute-start.33) | collective-permute-done | bytes 196640 | tf_op jit(solution)/shard_map/back_lead1/ppermute | solution.py:402
  86.6 0.8 fusion
  (63 shorter events, 4.0 us)
Async XLA Ops:
  0.0 14.8 %collective-permute-start.3 = (bf16[1536,768]{1,0:T(8,128)(2,1)}, bf16[1536,768]{1,0:T(8,128)(2,1)S(1)}, u32[]{:S(2)}, u32[]{:S(2)}) collective-permute-start(bf16[1536,768]{1,0:T(8,128)(2,1)} %bitcast.10), channel_id=1, source_target_pairs={{0,1},{1,0},{2,3},{3,2},{4,5},{5,4},{6,7},{7,6},{8,9},{9,8},{10,11... | collective-permute-start | bytes 7077896 | tf_op jit(solution)/shard_map/ppermute | solution.py:39
  0.5 14.4 %collective-permute-start.4 = (bf16[1536,768]{1,0:T(8,128)(2,1)}, bf16[1536,768]{1,0:T(8,128)(2,1)}, u32[]{:S(2)}, u32[]{:S(2)}) collective-permute-start(bf16[1536,768]{1,0:T(8,128)(2,1)} %bitcast.19), channel_id=1, source_target_pairs={{0,1},{1,0},{2,3},{3,2},{4,5},{5,4},{6,7},{7,6},{8,9},{9,8},{10,11... | collective-permute-start | bytes 7077896 | tf_op jit(solution)/shard_map/ppermute | solution.py:39
  0.5 14.4 %collective-permute-start.5 = (bf16[768,1536]{1,0:T(8,128)(2,1)}, bf16[768,1536]{1,0:T(8,128)(2,1)}, u32[]{:S(2)}, u32[]{:S(2)}) collective-permute-start(bf16[768,1536]{1,0:T(8,128)(2,1)} %bitcast.28), channel_id=1, source_target_pairs={{0,1},{1,0},{2,3},{3,2},{4,5},{5,4},{6,7},{7,6},{8,9},{9,8},{10,11... | collective-permute-start | bytes 7077896 | tf_op jit(solution)/shard_map/ppermute | solution.py:39
  2.4 7.2 %collective-permute-start = (bf16[256,128]{1,0:T(8,128)(2,1)}, bf16[256,128]{1,0:T(8,128)(2,1)S(1)}, u32[]{:S(2)}, u32[]{:S(2)}) collective-permute-start(bf16[256,128]{1,0:T(8,128)(2,1)} %tail.1), channel_id=1, source_target_pairs={{0,2},{2,0},{4,6},{6,4},{8,10},{10,8},{12,14},{14,12},{1,3},{3,1},... | collective-permute-start | bytes 196616 | tf_op jit(solution)/shard_map/ppermute | solution.py:26
  4.9 4.6 %collective-permute-start.1 = (bf16[256,128]{1,0:T(8,128)(2,1)}, bf16[256,128]{1,0:T(8,128)(2,1)S(1)}, u32[]{:S(2)}, u32[]{:S(2)}) collective-permute-start(bf16[256,128]{1,0:T(8,128)(2,1)} %tail.1), channel_id=1, source_target_pairs={{0,0},{2,4},{4,2},{6,8},{8,6},{10,12},{12,10},{14,14},{1,1},{3,5},... | collective-permute-start | bytes 196616 | tf_op jit(solution)/shard_map/ppermute | solution.py:26
  6.5 14.6 %copy-start.2 = (bf16[1,768,1536]{2,1,0:T(8,128)(2,1)S(1)}, bf16[1,768,1536]{2,1,0:T(8,128)(2,1)}, u32[]{:S(2)}) copy-start(bf16[1,768,1536]{2,1,0:T(8,128)(2,1)} %param.23) | copy-start | bytes 7077892
  9.5 3.5 %copy-start.7 = (f32[1536]{0:T(1024)S(1)}, f32[1536]{0:T(1024)}, u32[]{:S(2)}) copy-start(f32[1536]{0:T(1024)} %param.18) | copy-start | bytes 18436
  9.5 5.0 %copy-start.3 = (bf16[128,1536]{1,0:T(8,128)(2,1)S(1)}, bf16[128,1536]{1,0:T(8,128)(2,1)}, u32[]{:S(2)}) copy-start(bf16[128,1536]{1,0:T(8,128)(2,1)} %stream_ref.1) | copy-start | bytes 1179652
  9.5 5.0 %copy-start.4 = (s32[128,4]{0,1:T(4,128)S(1)}, s32[128,4]{0,1:T(4,128)}, u32[]{:S(2)}) copy-start(s32[128,4]{0,1:T(4,128)} %param.19) | copy-start | bytes 6148
  9.6 5.0 %copy-start.5 = (f32[128,4]{0,1:T(4,128)S(1)}, f32[128,4]{0,1:T(4,128)}, u32[]{:S(2)}) copy-start(f32[128,4]{0,1:T(4,128)} %param.20) | copy-start | bytes 6148
  9.6 11.6 %copy-start = (bf16[1,1536,768]{2,1,0:T(8,128)(2,1)S(1)}, bf16[1,1536,768]{2,1,0:T(8,128)(2,1)}, u32[]{:S(2)}) copy-start(bf16[1,1536,768]{2,1,0:T(8,128)(2,1)} %param.21) | copy-start | bytes 7077892
  9.6 11.6 %copy-start.1 = (bf16[1,1536,768]{2,1,0:T(8,128)(2,1)S(1)}, bf16[1,1536,768]{2,1,0:T(8,128)(2,1)}, u32[]{:S(2)}) copy-start(bf16[1,1536,768]{2,1,0:T(8,128)(2,1)} %param.22) | copy-start | bytes 7077892
  12.7 1.8 %collective-permute-start.2 = (bf16[128,1536]{1,0:T(8,128)(2,1)S(1)}, bf16[128,1536]{1,0:T(8,128)(2,1)S(1)}, u32[]{:S(2)}, u32[]{:S(2)}) collective-permute-start(bf16[128,1536]{1,0:T(8,128)(2,1)S(1)} %get-tuple-element.89), channel_id=1, source_target_pairs={{0,1},{1,0},{2,3},{3,2},{4,5},{5,4},{6,7},{7,6},{8,9},{9,8},{10,11... | collective-permute-start | bytes 1179656 | tf_op jit(solution)/shard_map/ppermute | solution.py:39
  14.8 6.3 %copy-start.6 = (bf16[1536,768]{1,0:T(8,128)(2,1)}, bf16[1536,768]{1,0:T(8,128)(2,1)S(1)}, u32[]{:S(2)}) copy-start(bf16[1536,768]{1,0:T(8,128)(2,1)S(1)} %collective-permute-done.3.refs_5_) | copy-start | bytes 7077892
  14.9 10.4 %collective-permute-start.6 = (bf16[784,128]{1,0:T(8,128)(2,1)S(1)}, bf16[784,128]{1,0:T(8,128)(2,1)S(1)}, u32[]{:S(2)}, u32[]{:S(2)}) collective-permute-start(bf16[784,128]{1,0:T(8,128)(2,1)S(1)} %get-tuple-element.96.refs_0_), channel_id=1, source_target_pairs={{0,4},{4,8},{8,12},{12,14},{14,10},{10,6},{6,2},{2,0},{1,5},{5,9},... | collective-permute-start | bytes 602120 | tf_op jit(solution)/shard_map/out_lead1/ppermute | solution.py:363
  19.1 7.9 %collective-permute-start.7 = (bf16[784,128]{1,0:T(8,128)(2,1)S(1)}, bf16[784,128]{1,0:T(8,128)(2,1)S(1)}, u32[]{:S(2)}, u32[]{:S(2)}) collective-permute-start(bf16[784,128]{1,0:T(8,128)(2,1)S(1)} %get-tuple-element.97.refs_1_), channel_id=1, source_target_pairs={{4,0},{8,4},{12,8},{14,12},{10,14},{6,10},{2,6},{0,2},{5,1},{9,5},... | collective-permute-start | bytes 602120 | tf_op jit(solution)/shard_map/out_lead1/ppermute | solution.py:363
  19.1 9.9 %collective-permute-start.12 = (bf16[784,128]{1,0:T(8,128)(2,1)S(1)}, bf16[784,128]{1,0:T(8,128)(2,1)S(1)}, u32[]{:S(2)}, u32[]{:S(2)}) collective-permute-start(bf16[784,128]{1,0:T(8,128)(2,1)S(1)} %get-tuple-element.97.refs_1_), channel_id=1, source_target_pairs={{0,4},{4,8},{8,12},{12,14},{14,10},{10,6},{6,2},{2,0},{1,5},{5,9},... | collective-permute-start | bytes 602120 | tf_op jit(solution)/shard_map/out_trail1/ppermute | solution.py:363
  21.1 10.2 %collective-permute-start.13 = (bf16[784,128]{1,0:T(8,128)(2,1)S(1)}, bf16[784,128]{1,0:T(8,128)(2,1)S(1)}, u32[]{:S(2)}, u32[]{:S(2)}) collective-permute-start(bf16[784,128]{1,0:T(8,128)(2,1)S(1)} %get-tuple-element.96.refs_0_), channel_id=1, source_target_pairs={{4,0},{8,4},{12,8},{14,12},{10,14},{6,10},{2,6},{0,2},{5,1},{9,5},... | collective-permute-start | bytes 602120 | tf_op jit(solution)/shard_map/out_trail1/ppermute | solution.py:363
  27.0 8.4 %collective-permute-start.8 = (bf16[784,128]{1,0:T(8,128)(2,1)S(1)}, bf16[784,128]{1,0:T(8,128)(2,1)S(1)}, u32[]{:S(2)}, u32[]{:S(2)}) collective-permute-start(bf16[784,128]{1,0:T(8,128)(2,1)S(1)} %collective-permute-done.6.refs_0_), channel_id=1, source_target_pairs={{0,4},{4,8},{8,12},{12,14},{14,10},{10,6},{6,2},{2,0},{1,5},{5,9},... | collective-permute-start | bytes 602120 | tf_op jit(solution)/shard_map/out_lead2/ppermute | solution.py:363
  28.6 7.9 %collective-permute-start.9 = (bf16[784,128]{1,0:T(8,128)(2,1)S(1)}, bf16[784,128]{1,0:T(8,128)(2,1)S(1)}, u32[]{:S(2)}, u32[]{:S(2)}) collective-permute-start(bf16[784,128]{1,0:T(8,128)(2,1)S(1)} %collective-permute-done.7.refs_1_), channel_id=1, source_target_pairs={{4,0},{8,4},{12,8},{14,12},{10,14},{6,10},{2,6},{0,2},{5,1},{9,5},... | collective-permute-start | bytes 602120 | tf_op jit(solution)/shard_map/out_lead2/ppermute | solution.py:363
  31.3 9.5 %collective-permute-start.15 = (bf16[784,128]{1,0:T(8,128)(2,1)S(1)}, bf16[784,128]{1,0:T(8,128)(2,1)S(1)}, u32[]{:S(2)}, u32[]{:S(2)}) collective-permute-start(bf16[784,128]{1,0:T(8,128)(2,1)S(1)} %collective-permute-done.13.refs_1_), channel_id=1, source_target_pairs={{4,0},{8,4},{12,8},{14,12},{10,14},{6,10},{2,6},{0,2},{5,1},{9,5},... | collective-permute-start | bytes 602120 | tf_op jit(solution)/shard_map/out_trail2/ppermute | solution.py:363
  31.3 9.5 %collective-permute-start.14 = (bf16[784,128]{1,0:T(8,128)(2,1)S(1)}, bf16[784,128]{1,0:T(8,128)(2,1)S(1)}, u32[]{:S(2)}, u32[]{:S(2)}) collective-permute-start(bf16[784,128]{1,0:T(8,128)(2,1)S(1)} %collective-permute-done.12.refs_0_), channel_id=1, source_target_pairs={{0,4},{4,8},{8,12},{12,14},{14,10},{10,6},{6,2},{2,0},{1,5},{5,9},... | collective-permute-start | bytes 602120 | tf_op jit(solution)/shard_map/out_trail2/ppermute | solution.py:363
  36.5 8.6 %collective-permute-start.11 = (bf16[784,128]{1,0:T(8,128)(2,1)S(1)}, bf16[784,128]{1,0:T(8,128)(2,1)S(1)}, u32[]{:S(2)}, u32[]{:S(2)}) collective-permute-start(bf16[784,128]{1,0:T(8,128)(2,1)S(1)} %collective-permute-done.9.refs_1_), channel_id=1, source_target_pairs={{4,0},{8,4},{12,8},{14,12},{10,14},{6,10},{2,6},{0,2},{5,1},{9,5},... | collective-permute-start | bytes 602120 | tf_op jit(solution)/shard_map/out_lead3/ppermute | solution.py:363
  36.9 8.2 %collective-permute-start.10 = (bf16[784,128]{1,0:T(8,128)(2,1)S(1)}, bf16[784,128]{1,0:T(8,128)(2,1)S(1)}, u32[]{:S(2)}, u32[]{:S(2)}) collective-permute-start(bf16[784,128]{1,0:T(8,128)(2,1)S(1)} %collective-permute-done.8.refs_0_), channel_id=1, source_target_pairs={{0,4},{4,8},{8,12},{12,14},{14,10},{10,6},{6,2},{2,0},{1,5},{5,9},... | collective-permute-start | bytes 602120 | tf_op jit(solution)/shard_map/out_lead3/ppermute | solution.py:363
  40.8 8.1 %collective-permute-start.18 = (bf16[784,128]{1,0:T(8,128)(2,1)S(1)}, bf16[784,128]{1,0:T(8,128)(2,1)S(1)}, u32[]{:S(2)}, u32[]{:S(2)}) collective-permute-start(bf16[784,128]{1,0:T(8,128)(2,1)S(1)} %collective-permute-done.15.refs_1_), channel_id=1, source_target_pairs={{4,0},{8,4},{12,8},{14,12},{10,14},{6,10},{2,6},{0,2},{5,1},{9,5},... | collective-permute-start | bytes 602120 | tf_op jit(solution)/shard_map/out_trail3/ppermute | solution.py:363
  41.2 7.6 %collective-permute-start.17 = (bf16[784,128]{1,0:T(8,128)(2,1)S(1)}, bf16[784,128]{1,0:T(8,128)(2,1)S(1)}, u32[]{:S(2)}, u32[]{:S(2)}) collective-permute-start(bf16[784,128]{1,0:T(8,128)(2,1)S(1)} %collective-permute-done.14.refs_0_), channel_id=1, source_target_pairs={{0,4},{4,8},{8,12},{12,14},{14,10},{10,6},{6,2},{2,0},{1,5},{5,9},... | collective-permute-start | bytes 602120 | tf_op jit(solution)/shard_map/out_trail3/ppermute | solution.py:363
  45.1 8.0 %collective-permute-start.16 = (bf16[784,128]{1,0:T(8,128)(2,1)S(1)}, bf16[784,128]{1,0:T(8,128)(2,1)S(1)}, u32[]{:S(2)}, u32[]{:S(2)}) collective-permute-start(bf16[784,128]{1,0:T(8,128)(2,1)S(1)} %collective-permute-done.10.refs_0_), channel_id=1, source_target_pairs={{0,4},{4,8},{8,12},{12,14},{14,10},{10,6},{6,2},{2,0},{1,5},{5,9},... | collective-permute-start | bytes 602120 | tf_op jit(solution)/shard_map/out_lead4/ppermute | solution.py:363
  46.7 6.4 %collective-permute-start.19 = (bf16[784,128]{1,0:T(8,128)(2,1)S(1)}, bf16[784,128]{1,0:T(8,128)(2,1)S(1)}, u32[]{:S(2)}, u32[]{:S(2)}) collective-permute-start(bf16[784,128]{1,0:T(8,128)(2,1)S(1)} %collective-permute-done.11.refs_1_), channel_id=1, source_target_pairs={{4,0},{8,4},{12,8},{14,12},{10,14},{6,10},{2,6},{0,2},{5,1},{9,5},... | collective-permute-start | bytes 602120 | tf_op jit(solution)/shard_map/out_lead4/ppermute | solution.py:363
  51.0 7.6 %collective-permute-start.27 = (bf16[64,1536]{1,0:T(8,128)(2,1)S(1)}, bf16[64,1536]{1,0:T(8,128)(2,1)S(1)}, u32[]{:S(2)}, u32[]{:S(2)}) collective-permute-start(bf16[64,1536]{1,0:T(8,128)(2,1)S(1)} %get-tuple-element.145), channel_id=1, source_target_pairs={{0,4},{4,8},{8,12},{12,14},{14,10},{10,6},{6,2},{2,0},{1,5},{5,9},... | collective-permute-start | bytes 589832 | tf_op jit(solution)/shard_map/back_trail3/ppermute | solution.py:402
  52.4 7.3 %collective-permute-start.28 = (bf16[64,1536]{1,0:T(8,128)(2,1)S(1)}, bf16[64,1536]{1,0:T(8,128)(2,1)S(1)}, u32[]{:S(2)}, u32[]{:S(2)}) collective-permute-start(bf16[64,1536]{1,0:T(8,128)(2,1)S(1)} %get-tuple-element.126), channel_id=1, source_target_pairs={{4,0},{8,4},{12,8},{14,12},{10,14},{6,10},{2,6},{0,2},{5,1},{9,5},... | collective-permute-start | bytes 589832 | tf_op jit(solution)/shard_map/back_trail3/ppermute | solution.py:402
  55.2 6.7 %collective-permute-start.20 = (bf16[64,1536]{1,0:T(8,128)(2,1)S(1)}, bf16[64,1536]{1,0:T(8,128)(2,1)S(1)}, u32[]{:S(2)}, u32[]{:S(2)}) collective-permute-start(bf16[64,1536]{1,0:T(8,128)(2,1)S(1)} %get-tuple-element.130), channel_id=1, source_target_pairs={{0,4},{4,8},{8,12},{12,14},{14,10},{10,6},{6,2},{2,0},{1,5},{5,9},... | collective-permute-start | bytes 589832 | tf_op jit(solution)/shard_map/back_lead4/ppermute | solution.py:402
  56.6 5.7 %collective-permute-start.21 = (bf16[64,1536]{1,0:T(8,128)(2,1)S(1)}, bf16[64,1536]{1,0:T(8,128)(2,1)S(1)}, u32[]{:S(2)}, u32[]{:S(2)}) collective-permute-start(bf16[64,1536]{1,0:T(8,128)(2,1)S(1)} %get-tuple-element.131), channel_id=1, source_target_pairs={{4,0},{8,4},{12,8},{14,12},{10,14},{6,10},{2,6},{0,2},{5,1},{9,5},... | collective-permute-start | bytes 589832 | tf_op jit(solution)/shard_map/back_lead4/ppermute | solution.py:402
  62.4 7.8 %collective-permute-start.23 = (bf16[64,1536]{1,0:T(8,128)(2,1)S(1)}, bf16[64,1536]{1,0:T(8,128)(2,1)S(1)}, u32[]{:S(2)}, u32[]{:S(2)}) collective-permute-start(bf16[64,1536]{1,0:T(8,128)(2,1)S(1)} %add_convert_fusion.8), channel_id=1, source_target_pairs={{4,0},{8,4},{12,8},{14,12},{10,14},{6,10},{2,6},{0,2},{5,1},{9,5},... | collective-permute-start | bytes 589832 | tf_op jit(solution)/shard_map/back_lead3/ppermute | solution.py:402
  63.1 7.1 %collective-permute-start.22 = (bf16[64,1536]{1,0:T(8,128)(2,1)S(1)}, bf16[64,1536]{1,0:T(8,128)(2,1)S(1)}, u32[]{:S(2)}, u32[]{:S(2)}) collective-permute-start(bf16[64,1536]{1,0:T(8,128)(2,1)S(1)} %add_convert_fusion.9), channel_id=1, source_target_pairs={{0,4},{4,8},{8,12},{12,14},{14,10},{10,6},{6,2},{2,0},{1,5},{5,9},... | collective-permute-start | bytes 589832 | tf_op jit(solution)/shard_map/back_lead3/ppermute | solution.py:402
  64.6 9.8 %collective-permute-start.30 = (bf16[64,1536]{1,0:T(8,128)(2,1)S(1)}, bf16[64,1536]{1,0:T(8,128)(2,1)S(1)}, u32[]{:S(2)}, u32[]{:S(2)}) collective-permute-start(bf16[64,1536]{1,0:T(8,128)(2,1)S(1)} %add_convert_fusion.3), channel_id=1, source_target_pairs={{4,0},{8,4},{12,8},{14,12},{10,14},{6,10},{2,6},{0,2},{5,1},{9,5},... | collective-permute-start | bytes 589832 | tf_op jit(solution)/shard_map/back_trail2/ppermute | solution.py:402
  65.3 9.1 %collective-permute-start.29 = (bf16[64,1536]{1,0:T(8,128)(2,1)S(1)}, bf16[64,1536]{1,0:T(8,128)(2,1)S(1)}, u32[]{:S(2)}, u32[]{:S(2)}) collective-permute-start(bf16[64,1536]{1,0:T(8,128)(2,1)S(1)} %add_convert_fusion.4), channel_id=1, source_target_pairs={{0,4},{4,8},{8,12},{12,14},{14,10},{10,6},{6,2},{2,0},{1,5},{5,9},... | collective-permute-start | bytes 589832 | tf_op jit(solution)/shard_map/back_trail2/ppermute | solution.py:402
  70.2 8.5 %collective-permute-start.25 = (bf16[64,1536]{1,0:T(8,128)(2,1)S(1)}, bf16[64,1536]{1,0:T(8,128)(2,1)S(1)}, u32[]{:S(2)}, u32[]{:S(2)}) collective-permute-start(bf16[64,1536]{1,0:T(8,128)(2,1)S(1)} %add_convert_fusion.6), channel_id=1, source_target_pairs={{4,0},{8,4},{12,8},{14,12},{10,14},{6,10},{2,6},{0,2},{5,1},{9,5},... | collective-permute-start | bytes 589832 | tf_op jit(solution)/shard_map/back_lead2/ppermute | solution.py:402
  70.5 8.2 %collective-permute-start.24 = (bf16[64,1536]{1,0:T(8,128)(2,1)S(1)}, bf16[64,1536]{1,0:T(8,128)(2,1)S(1)}, u32[]{:S(2)}, u32[]{:S(2)}) collective-permute-start(bf16[64,1536]{1,0:T(8,128)(2,1)S(1)} %add_convert_fusion.7), channel_id=1, source_target_pairs={{0,4},{4,8},{8,12},{12,14},{14,10},{10,6},{6,2},{2,0},{1,5},{5,9},... | collective-permute-start | bytes 589832 | tf_op jit(solution)/shard_map/back_lead2/ppermute | solution.py:402
  74.4 7.6 %collective-permute-start.31 = (bf16[64,1536]{1,0:T(8,128)(2,1)S(1)}, bf16[64,1536]{1,0:T(8,128)(2,1)S(1)}, u32[]{:S(2)}, u32[]{:S(2)}) collective-permute-start(bf16[64,1536]{1,0:T(8,128)(2,1)S(1)} %add_convert_fusion.2), channel_id=1, source_target_pairs={{4,0},{8,4},{12,8},{14,12},{10,14},{6,10},{2,6},{0,2},{5,1},{9,5},... | collective-permute-start | bytes 589832 | tf_op jit(solution)/shard_map/back_trail1/ppermute | solution.py:402
  74.7 9.9 %collective-permute-start.32 = (bf16[64,1536]{1,0:T(8,128)(2,1)S(1)}, bf16[64,1536]{1,0:T(8,128)(2,1)S(1)}, u32[]{:S(2)}, u32[]{:S(2)}) collective-permute-start(bf16[64,1536]{1,0:T(8,128)(2,1)S(1)} %add_convert_fusion.1), channel_id=1, source_target_pairs={{0,4},{4,8},{8,12},{12,14},{14,10},{10,6},{6,2},{2,0},{1,5},{5,9},... | collective-permute-start | bytes 589832 | tf_op jit(solution)/shard_map/back_trail1/ppermute | solution.py:402
  78.8 5.7 %collective-permute-start.26 = (bf16[64,1536]{1,0:T(8,128)(2,1)S(1)}, bf16[64,1536]{1,0:T(8,128)(2,1)S(1)}, u32[]{:S(2)}, u32[]{:S(2)}) collective-permute-start(bf16[64,1536]{1,0:T(8,128)(2,1)S(1)} %add_convert_fusion.5), channel_id=1, source_target_pairs={{0,4},{4,8},{8,12},{12,14},{14,10},{10,6},{6,2},{2,0},{1,5},{5,9},... | collective-permute-start | bytes 589832 | tf_op jit(solution)/shard_map/back_lead1/ppermute | solution.py:402
  80.8 5.7 %collective-permute-start.33 = (bf16[64,1536]{1,0:T(8,128)(2,1)S(1)}, bf16[64,1536]{1,0:T(8,128)(2,1)S(1)}, u32[]{:S(2)}, u32[]{:S(2)}) collective-permute-start(bf16[64,1536]{1,0:T(8,128)(2,1)S(1)} %add_convert_fusion), channel_id=1, source_target_pairs={{4,0},{8,4},{12,8},{14,12},{10,14},{6,10},{2,6},{0,2},{5,1},{9,5},... | collective-permute-start | bytes 589832 | tf_op jit(solution)/shard_map/back_lead1/ppermute | solution.py:402

commit v15 on v12

--- a/solution.py
+++ b/solution.py
@@ -374,8 +374,8 @@
             with jax.named_scope(f"back_{'lead' if lead else 'trail'}{distance}"):
                 moving[side, piece] = lax.ppermute(value, "seq", hops[side])
 
-    send(far - 1, False)
     send(far, True)
+    send(far - 1, False, *[came[side, far, side] for side in sides])
     for distance in range(far - 1, 0, -1):
         leads = [moving[side, side] for side in sides]
         send(distance, True)

time: 84.1 us -> 85.1 us (1.012)
  starting transfers between devices: 34.1 us -> 35 us
    ppermute x14, starting transfers between devices: 14.8 us -> 15.7 us  [send(): moving[side, piece] = lax.ppermute(value, 'seq', hops[side])]
  transfers between devices with their start and end apart: 34 -> 34, of which waited for: 18 -> 21; matrix products, arithmetic and copies ran while one was open for 1% -> 1% of each run, Pallas kernels for 29% -> 26%
where the time goes in v15:
time: 85.1 us; the launch traced here: 85 us
  starting transfers between devices  35 us (41%)
  Pallas kernels  24.6 us (29%)
  waiting for transfers between devices  23.5 us (28%)
  other arithmetic  1.44 us (2%)
    pallas_call x8, Pallas kernels, experts(): pl.pallas_call(functools.partial(expert_kernel, min(256, half), len(block...  18.8 us
    ppermute x14, starting transfers between devices, send(): moving[side, piece] = lax.ppermute(value, 'seq', hops[side])  15.7 us
    ppermute x14, starting transfers between devices, bring(): came[side, distance, piece] = lax.ppermute(block, 'seq', hops[side])  14.3 us
    ppermute x14, waiting for transfers between devices, send(): moving[side, piece] = lax.ppermute(value, 'seq', hops[side])  10.7 us
    ppermute x14, waiting for transfers between devices, bring(): came[side, distance, piece] = lax.ppermute(block, 'seq', hops[side])  8.29 us
    pallas_call x2, Pallas kernels, attend(): pl.pallas_call(functools.partial(attend_kernel, mix), in_specs=[vmem if m...  5.54 us
    ppermute x2, starting transfers between devices, shifted(): lax.ppermute(value, axis, [(i, (i + by) % peers) for i in range(peers)])  4.04 us
    ppermute x2, waiting for transfers between devices, shifted(): lax.ppermute(value, axis, [(i, (i + by) % peers) for i in range(peers)])  2.81 us
  transfers between devices with their start and end apart: 34, of which 21 were waited for; matrix products, arithmetic and copies ran while one was open for 1% of the time, Pallas kernels for 26%

profile of v15, /device:TPU:0, one launch (start us, length us, event | category | flops | bytes accessed | tf_op | source)
XLA Modules:
  0.0 85.0 jit_solution(4488615193509520570)
XLA Ops:
  1.0 2.5 %collective-permute-start = (bf16[256,128]{1,0:T(8,128)(2,1)}, bf16[256,128]{1,0:T(8,128)(2,1)S(1)}, u32[]{:S(2)}, u32[]{:S(2)}) collective-permute-start(bf16[256,128]{1,0:T(8,128)(2,1)} %refs_2_.1), channel_id=1, source_target_pairs={{0,2},{2,4},{4,6},{6,8},{8,10},{10,12},{12,14},{14,0},{1,3},{3,5},... | collective-permute-start | bytes 196616 | tf_op jit(solution)/shard_map/ppermute | solution.py:24
  3.5 1.5 %collective-permute-start.1 = (bf16[256,128]{1,0:T(8,128)(2,1)}, bf16[256,128]{1,0:T(8,128)(2,1)S(1)}, u32[]{:S(2)}, u32[]{:S(2)}) collective-permute-start(bf16[256,128]{1,0:T(8,128)(2,1)} %refs_3_.1), channel_id=1, source_target_pairs={{0,2},{2,4},{4,6},{6,8},{8,10},{10,12},{12,14},{14,0},{1,3},{3,5},... | collective-permute-start | bytes 196616 | tf_op jit(solution)/shard_map/ppermute | solution.py:24
  5.0 3.0 %attend.2 = (f32[1,16]{1,0:T(1,128)S(1)}, bf16[256,1024]{1,0:T(8,128)(2,1)S(1)}, bf16[256,128]{1,0:T(8,128)(2,1)S(1)}, bf16[256,128]{1,0:T(8,128)(2,1)S(1)}, bf1...) custom-call(f32[1,16]{1,0:T(1,128)} %bitcast.38, bf16[256,1024]{1,0:T(8,128)(2,1)} %refs_1_.1, ...), custom_call_target="tpu_custom_call" | custom-call | flops 671088640 | bytes 6291456 | tf_op jit(solution)/shard_map/attend/pallas_call | solution.py:151
  8.1 1.6 %collective-permute-done.refs_6_ = bf16[256,128]{1,0:T(8,128)(2,1)S(1)} collective-permute-done((bf16[256,128]{1,0:T(8,128)(2,1)}, bf16[256,128]{1,0:T(8,128)(2,1)S(1)}, u32[]{:S(2)}, u32[]{:S(2)}) %collective-permute-start) | collective-permute-done | bytes 65568 | tf_op jit(solution)/shard_map/ppermute | solution.py:24
  9.6 1.2 %collective-permute-done.1.refs_7_ = bf16[256,128]{1,0:T(8,128)(2,1)S(1)} collective-permute-done((bf16[256,128]{1,0:T(8,128)(2,1)}, bf16[256,128]{1,0:T(8,128)(2,1)S(1)}, u32[]{:S(2)}, u32[]{:S(2)}) %collective-permute-start.1) | collective-permute-done | bytes 65568 | tf_op jit(solution)/shard_map/ppermute | solution.py:24
  10.9 2.5 %attend.3 = (bf16[128,1536]{1,0:T(8,128)(2,1)S(1)}, f32[128,1536]{1,0:T(8,128)S(1)}) custom-call(f32[1,16]{1,0:T(1,128)S(1)} %get-tuple-element.84.refs_0_, bf16[256,1024]{1,0:T(8,128)(2,1)S(1)} %get-tuple-element.85.refs_1_, bf16[256,128]{1,0:T(8,128)(2,1)S(1)} %get-tuple-element.86.refs_2_, bf16[256,128]{1,0:T(8,128)(2,1)S(1)} %get-tuple-element.87.refs_3_, ...), custom_call_target="tpu_custom_call" | custom-call | flops 671088640 | bytes 6291456 | tf_op jit(solution)/shard_map/attend/pallas_call | solution.py:151
  13.5 1.7 %collective-permute-done.2.came_ref = bf16[128,1536]{1,0:T(8,128)(2,1)S(1)} collective-permute-done((bf16[128,1536]{1,0:T(8,128)(2,1)S(1)}, bf16[128,1536]{1,0:T(8,128)(2,1)S(1)}, u32[]{:S(2)}, u32[]{:S(2)}) %collective-permute-start.2) | collective-permute-done | bytes 393248 | tf_op jit(solution)/shard_map/ppermute | solution.py:37
  15.6 2.0 %collective-permute-start.7 = (bf16[784,128]{1,0:T(8,128)(2,1)S(1)}, bf16[784,128]{1,0:T(8,128)(2,1)S(1)}, u32[]{:S(2)}, u32[]{:S(2)}) collective-permute-start(bf16[784,128]{1,0:T(8,128)(2,1)S(1)} %get-tuple-element.99.refs_1_), channel_id=1, source_target_pairs={{4,0},{8,4},{12,8},{14,12},{10,14},{6,10},{2,6},{0,2},{5,1},{9,5},... | collective-permute-start | bytes 602120 | tf_op jit(solution)/shard_map/out_lead1/ppermute | solution.py:336
  17.7 2.0 %collective-permute-start.13 = (bf16[784,128]{1,0:T(8,128)(2,1)S(1)}, bf16[784,128]{1,0:T(8,128)(2,1)S(1)}, u32[]{:S(2)}, u32[]{:S(2)}) collective-permute-start(bf16[784,128]{1,0:T(8,128)(2,1)S(1)} %get-tuple-element.98.refs_0_), channel_id=1, source_target_pairs={{4,0},{8,4},{12,8},{14,12},{10,14},{6,10},{2,6},{0,2},{5,1},{9,5},... | collective-permute-start | bytes 602120 | tf_op jit(solution)/shard_map/out_trail1/ppermute | solution.py:336
  19.7 4.1 %experts.8 = (bf16[64,1536]{1,0:T(8,128)(2,1)S(1)}, bf16[64,1536]{1,0:T(8,128)(2,1)S(1)}, bf16[1536,768]{1,0:T(8,128)(2,1)S(1)}, bf16[1536,768]{1,0:T(8,128)(2,1)S(1)}, bf16[768,1536]{1,0:T(8,128)(2,1)S(1)}) custom-call(s32[1]{0:T(128)} %bitcast.5.me_ref, bf16[784,128]{1,0:T(8,128)(2,1)S(1)} %get-tuple-element.98.refs_0_, ...), custom_call_target="tpu_custom_call" | custom-call | flops 1811939328 | bytes 1179648 | tf_op jit(solution)/shard_map/experts/pallas_call | solution.py:287
  23.8 1.0 %collective-permute-start.8 = (bf16[784,128]{1,0:T(8,128)(2,1)S(1)}, bf16[784,128]{1,0:T(8,128)(2,1)S(1)}, u32[]{:S(2)}, u32[]{:S(2)}) collective-permute-start(bf16[784,128]{1,0:T(8,128)(2,1)S(1)} %collective-permute-done.6.refs_0_), channel_id=1, source_target_pairs={{0,4},{4,8},{8,12},{12,14},{14,10},{10,6},{6,2},{2,0},{1,5},{5,9},... | collective-permute-start | bytes 602120 | tf_op jit(solution)/shard_map/out_lead2/ppermute | solution.py:336
  24.8 1.1 %collective-permute-start.9 = (bf16[784,128]{1,0:T(8,128)(2,1)S(1)}, bf16[784,128]{1,0:T(8,128)(2,1)S(1)}, u32[]{:S(2)}, u32[]{:S(2)}) collective-permute-start(bf16[784,128]{1,0:T(8,128)(2,1)S(1)} %collective-permute-done.7.refs_1_), channel_id=1, source_target_pairs={{4,0},{8,4},{12,8},{14,12},{10,14},{6,10},{2,6},{0,2},{5,1},{9,5},... | collective-permute-start | bytes 602120 | tf_op jit(solution)/shard_map/out_lead2/ppermute | solution.py:336
  25.9 1.9 %collective-permute-done.12.refs_0_ = bf16[784,128]{1,0:T(8,128)(2,1)S(1)} collective-permute-done((bf16[784,128]{1,0:T(8,128)(2,1)S(1)}, bf16[784,128]{1,0:T(8,128)(2,1)S(1)}, u32[]{:S(2)}, u32[]{:S(2)}) %collective-permute-start.12) | collective-permute-done | bytes 200736 | tf_op jit(solution)/shard_map/out_trail1/ppermute | solution.py:336
  27.8 2.0 %collective-permute-start.15 = (bf16[784,128]{1,0:T(8,128)(2,1)S(1)}, bf16[784,128]{1,0:T(8,128)(2,1)S(1)}, u32[]{:S(2)}, u32[]{:S(2)}) collective-permute-start(bf16[784,128]{1,0:T(8,128)(2,1)S(1)} %collective-permute-done.13.refs_1_), channel_id=1, source_target_pairs={{4,0},{8,4},{12,8},{14,12},{10,14},{6,10},{2,6},{0,2},{5,1},{9,5},... | collective-permute-start | bytes 602120 | tf_op jit(solution)/shard_map/out_trail2/ppermute | solution.py:336
  29.9 2.1 %experts.9 = (bf16[64,1536]{1,0:T(8,128)(2,1)S(1)}, bf16[64,1536]{1,0:T(8,128)(2,1)S(1)}) custom-call(s32[1]{0:T(128)} %bitcast.5.me_ref, bf16[784,128]{1,0:T(8,128)(2,1)S(1)} %collective-permute-done.6.refs_0_, bf16[784,128]{1,0:T(8,128)(2,1)S(1)} %collective-permute-done.7.refs_1_, bf16[1536,768]{1,0:T(8,128)(2,1)S(1)} %bitcast.11, ...), custom_call_target="tpu_custom_call" | custom-call | flops 1811939328 | bytes 1179648 | tf_op jit(solution)/shard_map/hop1/experts/pallas_call | solution.py:287
  32.1 0.6 collective-permute-done.9.refs_1_
  32.7 1.4 %collective-permute-start.11 = (bf16[784,128]{1,0:T(8,128)(2,1)S(1)}, bf16[784,128]{1,0:T(8,128)(2,1)S(1)}, u32[]{:S(2)}, u32[]{:S(2)}) collective-permute-start(bf16[784,128]{1,0:T(8,128)(2,1)S(1)} %collective-permute-done.9.refs_1_), channel_id=1, source_target_pairs={{4,0},{8,4},{12,8},{14,12},{10,14},{6,10},{2,6},{0,2},{5,1},{9,5},... | collective-permute-start | bytes 602120 | tf_op jit(solution)/shard_map/out_lead3/ppermute | solution.py:336
  34.7 2.3 %collective-permute-done.15.refs_1_ = bf16[784,128]{1,0:T(8,128)(2,1)S(1)} collective-permute-done((bf16[784,128]{1,0:T(8,128)(2,1)S(1)}, bf16[784,128]{1,0:T(8,128)(2,1)S(1)}, u32[]{:S(2)}, u32[]{:S(2)}) %collective-permute-start.15) | collective-permute-done | bytes 200736 | tf_op jit(solution)/shard_map/out_trail2/ppermute | solution.py:336
  37.0 1.4 %collective-permute-start.18 = (bf16[784,128]{1,0:T(8,128)(2,1)S(1)}, bf16[784,128]{1,0:T(8,128)(2,1)S(1)}, u32[]{:S(2)}, u32[]{:S(2)}) collective-permute-start(bf16[784,128]{1,0:T(8,128)(2,1)S(1)} %collective-permute-done.15.refs_1_), channel_id=1, source_target_pairs={{4,0},{8,4},{12,8},{14,12},{10,14},{6,10},{2,6},{0,2},{5,1},{9,5},... | collective-permute-start | bytes 602120 | tf_op jit(solution)/shard_map/out_trail3/ppermute | solution.py:336
  39.0 2.1 %experts.10 = (bf16[64,1536]{1,0:T(8,128)(2,1)S(1)}, bf16[64,1536]{1,0:T(8,128)(2,1)S(1)}) custom-call(s32[1]{0:T(128)} %bitcast.5.me_ref, bf16[784,128]{1,0:T(8,128)(2,1)S(1)} %collective-permute-done.8.refs_0_, bf16[784,128]{1,0:T(8,128)(2,1)S(1)} %collective-permute-done.9.refs_1_, bf16[1536,768]{1,0:T(8,128)(2,1)S(1)} %bitcast.12, ...), custom_call_target="tpu_custom_call" | custom-call | flops 1811939328 | bytes 1179648 | tf_op jit(solution)/shard_map/hop2/experts/pallas_call | solution.py:287
  41.3 1.6 %collective-permute-start.16 = (bf16[784,128]{1,0:T(8,128)(2,1)S(1)}, bf16[784,128]{1,0:T(8,128)(2,1)S(1)}, u32[]{:S(2)}, u32[]{:S(2)}) collective-permute-start(bf16[784,128]{1,0:T(8,128)(2,1)S(1)} %collective-permute-done.10.refs_0_), channel_id=1, source_target_pairs={{0,4},{4,8},{8,12},{12,14},{14,10},{10,6},{6,2},{2,0},{1,5},{5,9},... | collective-permute-start | bytes 602120 | tf_op jit(solution)/shard_map/out_lead4/ppermute | solution.py:336
  43.3 2.3 %collective-permute-done.18.refs_1_ = bf16[784,128]{1,0:T(8,128)(2,1)S(1)} collective-permute-done((bf16[784,128]{1,0:T(8,128)(2,1)S(1)}, bf16[784,128]{1,0:T(8,128)(2,1)S(1)}, u32[]{:S(2)}, u32[]{:S(2)}) %collective-permute-start.18) | collective-permute-done | bytes 200736 | tf_op jit(solution)/shard_map/out_trail3/ppermute | solution.py:336
  45.6 0.7 collective-permute-done.17.refs_0_
  46.3 2.1 %experts.11 = (bf16[64,1536]{1,0:T(8,128)(2,1)S(1)}, bf16[64,1536]{1,0:T(8,128)(2,1)S(1)}) custom-call(s32[1]{0:T(128)} %bitcast.5.me_ref, bf16[784,128]{1,0:T(8,128)(2,1)S(1)} %collective-permute-done.10.refs_0_, bf16[784,128]{1,0:T(8,128)(2,1)S(1)} %collective-permute-done.11.refs_1_, bf16[1536,768]{1,0:T(8,128)(2,1)S(1)} %bitcast.13, ...), custom_call_target="tpu_custom_call" | custom-call | flops 1811939328 | bytes 1179648 | tf_op jit(solution)/shard_map/hop3/experts/pallas_call | solution.py:287
  48.6 2.1 %experts.12 = (bf16[64,1536]{1,0:T(8,128)(2,1)S(1)}, bf16[64,1536]{1,0:T(8,128)(2,1)S(1)}) custom-call(s32[1]{0:T(128)} %bitcast.5.me_ref, bf16[784,128]{1,0:T(8,128)(2,1)S(1)} %collective-permute-done.16.refs_0_, bf16[784,128]{1,0:T(8,128)(2,1)S(1)} %collective-permute-done.19.refs_1_, bf16[1536,768]{1,0:T(8,128)(2,1)S(1)} %bitcast.14, ...), custom_call_target="tpu_custom_call" | custom-call | flops 1811939328 | bytes 1179648 | tf_op jit(solution)/shard_map/hop4/experts/pallas_call | solution.py:287
  50.7 1.5 %collective-permute-start.20 = (bf16[64,1536]{1,0:T(8,128)(2,1)S(1)}, bf16[64,1536]{1,0:T(8,128)(2,1)S(1)}, u32[]{:S(2)}, u32[]{:S(2)}) collective-permute-start(bf16[64,1536]{1,0:T(8,128)(2,1)S(1)} %get-tuple-element.132), channel_id=1, source_target_pairs={{0,4},{4,8},{8,12},{12,14},{14,10},{10,6},{6,2},{2,0},{1,5},{5,9},... | collective-permute-start | bytes 589832 | tf_op jit(solution)/shard_map/back_lead4/ppermute | solution.py:375
  52.8 1.6 %collective-permute-start.28 = (bf16[64,1536]{1,0:T(8,128)(2,1)S(1)}, bf16[64,1536]{1,0:T(8,128)(2,1)S(1)}, u32[]{:S(2)}, u32[]{:S(2)}) collective-permute-start(bf16[64,1536]{1,0:T(8,128)(2,1)S(1)} %get-tuple-element.149), channel_id=1, source_target_pairs={{4,0},{8,4},{12,8},{14,12},{10,14},{6,10},{2,6},{0,2},{5,1},{9,5},... | collective-permute-start | bytes 589832 | tf_op jit(solution)/shard_map/back_trail3/ppermute | solution.py:375
  54.8 2.1 %experts.13 = (bf16[64,1536]{1,0:T(8,128)(2,1)S(1)}, bf16[64,1536]{1,0:T(8,128)(2,1)S(1)}) custom-call(s32[1]{0:T(128)} %bitcast.5.me_ref, bf16[784,128]{1,0:T(8,128)(2,1)S(1)} %collective-permute-done.17.refs_0_, bf16[784,128]{1,0:T(8,128)(2,1)S(1)} %collective-permute-done.18.refs_1_, bf16[1536,768]{1,0:T(8,128)(2,1)S(1)} %bitcast.15, ...), custom_call_target="tpu_custom_call" | custom-call | flops 1811939328 | bytes 1179648 | tf_op jit(solution)/shard_map/hop3/experts/pallas_call | solution.py:287
  56.9 0.8 collective-permute-done.20
  57.8 1.2 %collective-permute-done.21 = bf16[64,1536]{1,0:T(8,128)(2,1)S(1)} collective-permute-done((bf16[64,1536]{1,0:T(8,128)(2,1)S(1)}, bf16[64,1536]{1,0:T(8,128)(2,1)S(1)}, u32[]{:S(2)}, u32[]{:S(2)}) %collective-permute-start.21) | collective-permute-done | bytes 196640 | tf_op jit(solution)/shard_map/back_lead4/ppermute | solution.py:375
  59.0 1.7 %collective-permute-start.23 = (bf16[64,1536]{1,0:T(8,128)(2,1)S(1)}, bf16[64,1536]{1,0:T(8,128)(2,1)S(1)}, u32[]{:S(2)}, u32[]{:S(2)}) collective-permute-start(bf16[64,1536]{1,0:T(8,128)(2,1)S(1)} %add_convert_fusion.8), channel_id=1, source_target_pairs={{4,0},{8,4},{12,8},{14,12},{10,14},{6,10},{2,6},{0,2},{5,1},{9,5},... | collective-permute-start | bytes 589832 | tf_op jit(solution)/shard_map/back_lead3/ppermute | solution.py:375
  60.8 0.6 collective-permute-start.22
  61.4 1.5 %collective-permute-done.28 = bf16[64,1536]{1,0:T(8,128)(2,1)S(1)} collective-permute-done((bf16[64,1536]{1,0:T(8,128)(2,1)S(1)}, bf16[64,1536]{1,0:T(8,128)(2,1)S(1)}, u32[]{:S(2)}, u32[]{:S(2)}) %collective-permute-start.28) | collective-permute-done | bytes 196640 | tf_op jit(solution)/shard_map/back_trail3/ppermute | solution.py:375
  63.0 2.0 %collective-permute-start.30 = (bf16[64,1536]{1,0:T(8,128)(2,1)S(1)}, bf16[64,1536]{1,0:T(8,128)(2,1)S(1)}, u32[]{:S(2)}, u32[]{:S(2)}) collective-permute-start(bf16[64,1536]{1,0:T(8,128)(2,1)S(1)} %add_convert_fusion.3), channel_id=1, source_target_pairs={{4,0},{8,4},{12,8},{14,12},{10,14},{6,10},{2,6},{0,2},{5,1},{9,5},... | collective-permute-start | bytes 589832 | tf_op jit(solution)/shard_map/back_trail2/ppermute | solution.py:375
  65.0 0.6 collective-permute-start.29
  65.6 2.1 %experts.14 = (bf16[64,1536]{1,0:T(8,128)(2,1)S(1)}, bf16[64,1536]{1,0:T(8,128)(2,1)S(1)}) custom-call(s32[1]{0:T(128)} %bitcast.5.me_ref, bf16[784,128]{1,0:T(8,128)(2,1)S(1)} %collective-permute-done.14.refs_0_, bf16[784,128]{1,0:T(8,128)(2,1)S(1)} %collective-permute-done.15.refs_1_, bf16[1536,768]{1,0:T(8,128)(2,1)S(1)} %bitcast.16, ...), custom_call_target="tpu_custom_call" | custom-call | flops 1811939328 | bytes 1179648 | tf_op jit(solution)/shard_map/hop2/experts/pallas_call | solution.py:287
  67.8 1.5 %collective-permute-start.25 = (bf16[64,1536]{1,0:T(8,128)(2,1)S(1)}, bf16[64,1536]{1,0:T(8,128)(2,1)S(1)}, u32[]{:S(2)}, u32[]{:S(2)}) collective-permute-start(bf16[64,1536]{1,0:T(8,128)(2,1)S(1)} %add_convert_fusion.6), channel_id=1, source_target_pairs={{4,0},{8,4},{12,8},{14,12},{10,14},{6,10},{2,6},{0,2},{5,1},{9,5},... | collective-permute-start | bytes 589832 | tf_op jit(solution)/shard_map/back_lead2/ppermute | solution.py:375
  69.4 0.6 collective-permute-start.24
  70.0 1.4 %collective-permute-done.30 = bf16[64,1536]{1,0:T(8,128)(2,1)S(1)} collective-permute-done((bf16[64,1536]{1,0:T(8,128)(2,1)S(1)}, bf16[64,1536]{1,0:T(8,128)(2,1)S(1)}, u32[]{:S(2)}, u32[]{:S(2)}) %collective-permute-start.30) | collective-permute-done | bytes 196640 | tf_op jit(solution)/shard_map/back_trail2/ppermute | solution.py:375
  71.6 1.8 %collective-permute-start.31 = (bf16[64,1536]{1,0:T(8,128)(2,1)S(1)}, bf16[64,1536]{1,0:T(8,128)(2,1)S(1)}, u32[]{:S(2)}, u32[]{:S(2)}) collective-permute-start(bf16[64,1536]{1,0:T(8,128)(2,1)S(1)} %add_convert_fusion.2), channel_id=1, source_target_pairs={{4,0},{8,4},{12,8},{14,12},{10,14},{6,10},{2,6},{0,2},{5,1},{9,5},... | collective-permute-start | bytes 589832 | tf_op jit(solution)/shard_map/back_trail1/ppermute | solution.py:375
  73.4 0.6 collective-permute-start.32
  74.1 2.1 %experts.15 = (bf16[64,1536]{1,0:T(8,128)(2,1)S(1)}, bf16[64,1536]{1,0:T(8,128)(2,1)S(1)}) custom-call(s32[1]{0:T(128)} %bitcast.5.me_ref, bf16[784,128]{1,0:T(8,128)(2,1)S(1)} %collective-permute-done.12.refs_0_, bf16[784,128]{1,0:T(8,128)(2,1)S(1)} %collective-permute-done.13.refs_1_, bf16[1536,768]{1,0:T(8,128)(2,1)S(1)} %bitcast.17, ...), custom_call_target="tpu_custom_call" | custom-call | flops 1811939328 | bytes 1179648 | tf_op jit(solution)/shard_map/hop1/experts/pallas_call | solution.py:287
  76.2 1.1 %collective-permute-done.24 = bf16[64,1536]{1,0:T(8,128)(2,1)S(1)} collective-permute-done((bf16[64,1536]{1,0:T(8,128)(2,1)S(1)}, bf16[64,1536]{1,0:T(8,128)(2,1)S(1)}, u32[]{:S(2)}, u32[]{:S(2)}) %collective-permute-start.24) | collective-permute-done | bytes 196640 | tf_op jit(solution)/shard_map/back_lead2/ppermute | solution.py:375
  77.3 1.0 %collective-permute-start.26 = (bf16[64,1536]{1,0:T(8,128)(2,1)S(1)}, bf16[64,1536]{1,0:T(8,128)(2,1)S(1)}, u32[]{:S(2)}, u32[]{:S(2)}) collective-permute-start(bf16[64,1536]{1,0:T(8,128)(2,1)S(1)} %add_convert_fusion.5), channel_id=1, source_target_pairs={{0,4},{4,8},{8,12},{12,14},{14,10},{10,6},{6,2},{2,0},{1,5},{5,9},... | collective-permute-start | bytes 589832 | tf_op jit(solution)/shard_map/back_lead1/ppermute | solution.py:375
  78.3 1.2 %collective-permute-start.33 = (bf16[64,1536]{1,0:T(8,128)(2,1)S(1)}, bf16[64,1536]{1,0:T(8,128)(2,1)S(1)}, u32[]{:S(2)}, u32[]{:S(2)}) collective-permute-start(bf16[64,1536]{1,0:T(8,128)(2,1)S(1)} %add_convert_fusion), channel_id=1, source_target_pairs={{4,0},{8,4},{12,8},{14,12},{10,14},{6,10},{2,6},{0,2},{5,1},{9,5},... | collective-permute-start | bytes 589832 | tf_op jit(solution)/shard_map/back_lead1/ppermute | solution.py:375
  79.6 3.5 %collective-permute-done.26 = bf16[64,1536]{1,0:T(8,128)(2,1)S(1)} collective-permute-done((bf16[64,1536]{1,0:T(8,128)(2,1)S(1)}, bf16[64,1536]{1,0:T(8,128)(2,1)S(1)}, u32[]{:S(2)}, u32[]{:S(2)}) %collective-permute-start.26) | collective-permute-done | bytes 196640 | tf_op jit(solution)/shard_map/back_lead1/ppermute | solution.py:375
  83.1 0.9 %collective-permute-done.33 = bf16[64,1536]{1,0:T(8,128)(2,1)S(1)} collective-permute-done((bf16[64,1536]{1,0:T(8,128)(2,1)S(1)}, bf16[64,1536]{1,0:T(8,128)(2,1)S(1)}, u32[]{:S(2)}, u32[]{:S(2)}) %collective-permute-start.33) | collective-permute-done | bytes 196640 | tf_op jit(solution)/shard_map/back_lead1/ppermute | solution.py:375
  84.1 0.8 fusion
  (61 shorter events, 5.6 us)
Async XLA Ops:
  0.0 15.5 %collective-permute-start.3 = (bf16[1536,768]{1,0:T(8,128)(2,1)}, bf16[1536,768]{1,0:T(8,128)(2,1)S(1)}, u32[]{:S(2)}, u32[]{:S(2)}) collective-permute-start(bf16[1536,768]{1,0:T(8,128)(2,1)} %bitcast.9), channel_id=1, source_target_pairs={{0,1},{1,0},{2,3},{3,2},{4,5},{5,4},{6,7},{7,6},{8,9},{9,8},{10,11... | collective-permute-start | bytes 7077896 | tf_op jit(solution)/shard_map/ppermute | solution.py:37
  0.5 15.1 %collective-permute-start.4 = (bf16[1536,768]{1,0:T(8,128)(2,1)}, bf16[1536,768]{1,0:T(8,128)(2,1)}, u32[]{:S(2)}, u32[]{:S(2)}) collective-permute-start(bf16[1536,768]{1,0:T(8,128)(2,1)} %bitcast.18), channel_id=1, source_target_pairs={{0,1},{1,0},{2,3},{3,2},{4,5},{5,4},{6,7},{7,6},{8,9},{9,8},{10,11... | collective-permute-start | bytes 7077896 | tf_op jit(solution)/shard_map/ppermute | solution.py:37
  0.5 15.1 %collective-permute-start.5 = (bf16[768,1536]{1,0:T(8,128)(2,1)}, bf16[768,1536]{1,0:T(8,128)(2,1)}, u32[]{:S(2)}, u32[]{:S(2)}) collective-permute-start(bf16[768,1536]{1,0:T(8,128)(2,1)} %bitcast.27), channel_id=1, source_target_pairs={{0,1},{1,0},{2,3},{3,2},{4,5},{5,4},{6,7},{7,6},{8,9},{9,8},{10,11... | collective-permute-start | bytes 7077896 | tf_op jit(solution)/shard_map/ppermute | solution.py:37
  1.0 8.7 %collective-permute-start = (bf16[256,128]{1,0:T(8,128)(2,1)}, bf16[256,128]{1,0:T(8,128)(2,1)S(1)}, u32[]{:S(2)}, u32[]{:S(2)}) collective-permute-start(bf16[256,128]{1,0:T(8,128)(2,1)} %refs_2_.1), channel_id=1, source_target_pairs={{0,2},{2,4},{4,6},{6,8},{8,10},{10,12},{12,14},{14,0},{1,3},{3,5},... | collective-permute-start | bytes 196616 | tf_op jit(solution)/shard_map/ppermute | solution.py:24
  3.5 7.4 %collective-permute-start.1 = (bf16[256,128]{1,0:T(8,128)(2,1)}, bf16[256,128]{1,0:T(8,128)(2,1)S(1)}, u32[]{:S(2)}, u32[]{:S(2)}) collective-permute-start(bf16[256,128]{1,0:T(8,128)(2,1)} %refs_3_.1), channel_id=1, source_target_pairs={{0,2},{2,4},{4,6},{6,8},{8,10},{10,12},{12,14},{14,0},{1,3},{3,5},... | collective-permute-start | bytes 196616 | tf_op jit(solution)/shard_map/ppermute | solution.py:24
  5.0 14.7 %copy-start.2 = (bf16[1,768,1536]{2,1,0:T(8,128)(2,1)S(1)}, bf16[1,768,1536]{2,1,0:T(8,128)(2,1)}, u32[]{:S(2)}) copy-start(bf16[1,768,1536]{2,1,0:T(8,128)(2,1)} %param.23) | copy-start | bytes 7077892
  8.0 5.5 %copy-start.7 = (f32[1536]{0:T(1024)S(1)}, f32[1536]{0:T(1024)}, u32[]{:S(2)}) copy-start(f32[1536]{0:T(1024)} %param.18) | copy-start | bytes 18436
  8.0 7.2 %copy-start.3 = (bf16[128,1536]{1,0:T(8,128)(2,1)S(1)}, bf16[128,1536]{1,0:T(8,128)(2,1)}, u32[]{:S(2)}) copy-start(bf16[128,1536]{1,0:T(8,128)(2,1)} %stream_ref.1) | copy-start | bytes 1179652
  8.0 7.2 %copy-start.4 = (s32[128,4]{0,1:T(4,128)S(1)}, s32[128,4]{0,1:T(4,128)}, u32[]{:S(2)}) copy-start(s32[128,4]{0,1:T(4,128)} %param.19) | copy-start | bytes 6148
  8.0 7.2 %copy-start.5 = (f32[128,4]{0,1:T(4,128)S(1)}, f32[128,4]{0,1:T(4,128)}, u32[]{:S(2)}) copy-start(f32[128,4]{0,1:T(4,128)} %param.20) | copy-start | bytes 6148
  10.9 8.8 %copy-start = (bf16[1,1536,768]{2,1,0:T(8,128)(2,1)S(1)}, bf16[1,1536,768]{2,1,0:T(8,128)(2,1)}, u32[]{:S(2)}) copy-start(bf16[1,1536,768]{2,1,0:T(8,128)(2,1)} %param.21) | copy-start | bytes 7077892
  10.9 8.8 %copy-start.1 = (bf16[1,1536,768]{2,1,0:T(8,128)(2,1)S(1)}, bf16[1,1536,768]{2,1,0:T(8,128)(2,1)}, u32[]{:S(2)}) copy-start(bf16[1,1536,768]{2,1,0:T(8,128)(2,1)} %param.22) | copy-start | bytes 7077892
  13.4 1.8 %collective-permute-start.2 = (bf16[128,1536]{1,0:T(8,128)(2,1)S(1)}, bf16[128,1536]{1,0:T(8,128)(2,1)S(1)}, u32[]{:S(2)}, u32[]{:S(2)}) collective-permute-start(bf16[128,1536]{1,0:T(8,128)(2,1)S(1)} %get-tuple-element.91), channel_id=1, source_target_pairs={{0,1},{1,0},{2,3},{3,2},{4,5},{5,4},{6,7},{7,6},{8,9},{9,8},{10,11... | collective-permute-start | bytes 1179656 | tf_op jit(solution)/shard_map/ppermute | solution.py:37
  15.5 4.1 %copy-start.6 = (bf16[1536,768]{1,0:T(8,128)(2,1)}, bf16[1536,768]{1,0:T(8,128)(2,1)S(1)}, u32[]{:S(2)}) copy-start(bf16[1536,768]{1,0:T(8,128)(2,1)S(1)} %collective-permute-done.3.refs_5_) | copy-start | bytes 7077892
  15.6 8.2 %collective-permute-start.6 = (bf16[784,128]{1,0:T(8,128)(2,1)S(1)}, bf16[784,128]{1,0:T(8,128)(2,1)S(1)}, u32[]{:S(2)}, u32[]{:S(2)}) collective-permute-start(bf16[784,128]{1,0:T(8,128)(2,1)S(1)} %get-tuple-element.98.refs_0_), channel_id=1, source_target_pairs={{0,4},{4,8},{8,12},{12,14},{14,10},{10,6},{6,2},{2,0},{1,5},{5,9},... | collective-permute-start | bytes 602120 | tf_op jit(solution)/shard_map/out_lead1/ppermute | solution.py:336
  15.6 8.2 %collective-permute-start.7 = (bf16[784,128]{1,0:T(8,128)(2,1)S(1)}, bf16[784,128]{1,0:T(8,128)(2,1)S(1)}, u32[]{:S(2)}, u32[]{:S(2)}) collective-permute-start(bf16[784,128]{1,0:T(8,128)(2,1)S(1)} %get-tuple-element.99.refs_1_), channel_id=1, source_target_pairs={{4,0},{8,4},{12,8},{14,12},{10,14},{6,10},{2,6},{0,2},{5,1},{9,5},... | collective-permute-start | bytes 602120 | tf_op jit(solution)/shard_map/out_lead1/ppermute | solution.py:336
  17.7 10.1 %collective-permute-start.12 = (bf16[784,128]{1,0:T(8,128)(2,1)S(1)}, bf16[784,128]{1,0:T(8,128)(2,1)S(1)}, u32[]{:S(2)}, u32[]{:S(2)}) collective-permute-start(bf16[784,128]{1,0:T(8,128)(2,1)S(1)} %get-tuple-element.99.refs_1_), channel_id=1, source_target_pairs={{0,4},{4,8},{8,12},{12,14},{14,10},{10,6},{6,2},{2,0},{1,5},{5,9},... | collective-permute-start | bytes 602120 | tf_op jit(solution)/shard_map/out_trail1/ppermute | solution.py:336
  17.7 10.1 %collective-permute-start.13 = (bf16[784,128]{1,0:T(8,128)(2,1)S(1)}, bf16[784,128]{1,0:T(8,128)(2,1)S(1)}, u32[]{:S(2)}, u32[]{:S(2)}) collective-permute-start(bf16[784,128]{1,0:T(8,128)(2,1)S(1)} %get-tuple-element.98.refs_0_), channel_id=1, source_target_pairs={{4,0},{8,4},{12,8},{14,12},{10,14},{6,10},{2,6},{0,2},{5,1},{9,5},... | collective-permute-start | bytes 602120 | tf_op jit(solution)/shard_map/out_trail1/ppermute | solution.py:336
  23.8 8.3 %collective-permute-start.8 = (bf16[784,128]{1,0:T(8,128)(2,1)S(1)}, bf16[784,128]{1,0:T(8,128)(2,1)S(1)}, u32[]{:S(2)}, u32[]{:S(2)}) collective-permute-start(bf16[784,128]{1,0:T(8,128)(2,1)S(1)} %collective-permute-done.6.refs_0_), channel_id=1, source_target_pairs={{0,4},{4,8},{8,12},{12,14},{14,10},{10,6},{6,2},{2,0},{1,5},{5,9},... | collective-permute-start | bytes 602120 | tf_op jit(solution)/shard_map/out_lead2/ppermute | solution.py:336
  24.8 7.9 %collective-permute-start.9 = (bf16[784,128]{1,0:T(8,128)(2,1)S(1)}, bf16[784,128]{1,0:T(8,128)(2,1)S(1)}, u32[]{:S(2)}, u32[]{:S(2)}) collective-permute-start(bf16[784,128]{1,0:T(8,128)(2,1)S(1)} %collective-permute-done.7.refs_1_), channel_id=1, source_target_pairs={{4,0},{8,4},{12,8},{14,12},{10,14},{6,10},{2,6},{0,2},{5,1},{9,5},... | collective-permute-start | bytes 602120 | tf_op jit(solution)/shard_map/out_lead2/ppermute | solution.py:336
  27.8 9.2 %collective-permute-start.15 = (bf16[784,128]{1,0:T(8,128)(2,1)S(1)}, bf16[784,128]{1,0:T(8,128)(2,1)S(1)}, u32[]{:S(2)}, u32[]{:S(2)}) collective-permute-start(bf16[784,128]{1,0:T(8,128)(2,1)S(1)} %collective-permute-done.13.refs_1_), channel_id=1, source_target_pairs={{4,0},{8,4},{12,8},{14,12},{10,14},{6,10},{2,6},{0,2},{5,1},{9,5},... | collective-permute-start | bytes 602120 | tf_op jit(solution)/shard_map/out_trail2/ppermute | solution.py:336
  29.8 7.2 %collective-permute-start.14 = (bf16[784,128]{1,0:T(8,128)(2,1)S(1)}, bf16[784,128]{1,0:T(8,128)(2,1)S(1)}, u32[]{:S(2)}, u32[]{:S(2)}) collective-permute-start(bf16[784,128]{1,0:T(8,128)(2,1)S(1)} %collective-permute-done.12.refs_0_), channel_id=1, source_target_pairs={{0,4},{4,8},{8,12},{12,14},{14,10},{10,6},{6,2},{2,0},{1,5},{5,9},... | collective-permute-start | bytes 602120 | tf_op jit(solution)/shard_map/out_trail2/ppermute | solution.py:336
  32.7 8.6 %collective-permute-start.11 = (bf16[784,128]{1,0:T(8,128)(2,1)S(1)}, bf16[784,128]{1,0:T(8,128)(2,1)S(1)}, u32[]{:S(2)}, u32[]{:S(2)}) collective-permute-start(bf16[784,128]{1,0:T(8,128)(2,1)S(1)} %collective-permute-done.9.refs_1_), channel_id=1, source_target_pairs={{4,0},{8,4},{12,8},{14,12},{10,14},{6,10},{2,6},{0,2},{5,1},{9,5},... | collective-permute-start | bytes 602120 | tf_op jit(solution)/shard_map/out_lead3/ppermute | solution.py:336
  34.1 7.2 %collective-permute-start.10 = (bf16[784,128]{1,0:T(8,128)(2,1)S(1)}, bf16[784,128]{1,0:T(8,128)(2,1)S(1)}, u32[]{:S(2)}, u32[]{:S(2)}) collective-permute-start(bf16[784,128]{1,0:T(8,128)(2,1)S(1)} %collective-permute-done.8.refs_0_), channel_id=1, source_target_pairs={{0,4},{4,8},{8,12},{12,14},{14,10},{10,6},{6,2},{2,0},{1,5},{5,9},... | collective-permute-start | bytes 602120 | tf_op jit(solution)/shard_map/out_lead3/ppermute | solution.py:336
  37.0 8.6 %collective-permute-start.18 = (bf16[784,128]{1,0:T(8,128)(2,1)S(1)}, bf16[784,128]{1,0:T(8,128)(2,1)S(1)}, u32[]{:S(2)}, u32[]{:S(2)}) collective-permute-start(bf16[784,128]{1,0:T(8,128)(2,1)S(1)} %collective-permute-done.15.refs_1_), channel_id=1, source_target_pairs={{4,0},{8,4},{12,8},{14,12},{10,14},{6,10},{2,6},{0,2},{5,1},{9,5},... | collective-permute-start | bytes 602120 | tf_op jit(solution)/shard_map/out_trail3/ppermute | solution.py:336
  38.4 7.9 %collective-permute-start.17 = (bf16[784,128]{1,0:T(8,128)(2,1)S(1)}, bf16[784,128]{1,0:T(8,128)(2,1)S(1)}, u32[]{:S(2)}, u32[]{:S(2)}) collective-permute-start(bf16[784,128]{1,0:T(8,128)(2,1)S(1)} %collective-permute-done.14.refs_0_), channel_id=1, source_target_pairs={{0,4},{4,8},{8,12},{12,14},{14,10},{10,6},{6,2},{2,0},{1,5},{5,9},... | collective-permute-start | bytes 602120 | tf_op jit(solution)/shard_map/out_trail3/ppermute | solution.py:336
  41.3 7.2 %collective-permute-start.16 = (bf16[784,128]{1,0:T(8,128)(2,1)S(1)}, bf16[784,128]{1,0:T(8,128)(2,1)S(1)}, u32[]{:S(2)}, u32[]{:S(2)}) collective-permute-start(bf16[784,128]{1,0:T(8,128)(2,1)S(1)} %collective-permute-done.10.refs_0_), channel_id=1, source_target_pairs={{0,4},{4,8},{8,12},{12,14},{14,10},{10,6},{6,2},{2,0},{1,5},{5,9},... | collective-permute-start | bytes 602120 | tf_op jit(solution)/shard_map/out_lead4/ppermute | solution.py:336
  42.9 5.7 %collective-permute-start.19 = (bf16[784,128]{1,0:T(8,128)(2,1)S(1)}, bf16[784,128]{1,0:T(8,128)(2,1)S(1)}, u32[]{:S(2)}, u32[]{:S(2)}) collective-permute-start(bf16[784,128]{1,0:T(8,128)(2,1)S(1)} %collective-permute-done.11.refs_1_), channel_id=1, source_target_pairs={{4,0},{8,4},{12,8},{14,12},{10,14},{6,10},{2,6},{0,2},{5,1},{9,5},... | collective-permute-start | bytes 602120 | tf_op jit(solution)/shard_map/out_lead4/ppermute | solution.py:336
  50.7 7.0 %collective-permute-start.20 = (bf16[64,1536]{1,0:T(8,128)(2,1)S(1)}, bf16[64,1536]{1,0:T(8,128)(2,1)S(1)}, u32[]{:S(2)}, u32[]{:S(2)}) collective-permute-start(bf16[64,1536]{1,0:T(8,128)(2,1)S(1)} %get-tuple-element.132), channel_id=1, source_target_pairs={{0,4},{4,8},{8,12},{12,14},{14,10},{10,6},{6,2},{2,0},{1,5},{5,9},... | collective-permute-start | bytes 589832 | tf_op jit(solution)/shard_map/back_lead4/ppermute | solution.py:375
  52.2 6.7 %collective-permute-start.21 = (bf16[64,1536]{1,0:T(8,128)(2,1)S(1)}, bf16[64,1536]{1,0:T(8,128)(2,1)S(1)}, u32[]{:S(2)}, u32[]{:S(2)}) collective-permute-start(bf16[64,1536]{1,0:T(8,128)(2,1)S(1)} %get-tuple-element.133), channel_id=1, source_target_pairs={{4,0},{8,4},{12,8},{14,12},{10,14},{6,10},{2,6},{0,2},{5,1},{9,5},... | collective-permute-start | bytes 589832 | tf_op jit(solution)/shard_map/back_lead4/ppermute | solution.py:375
  52.8 10.1 %collective-permute-start.28 = (bf16[64,1536]{1,0:T(8,128)(2,1)S(1)}, bf16[64,1536]{1,0:T(8,128)(2,1)S(1)}, u32[]{:S(2)}, u32[]{:S(2)}) collective-permute-start(bf16[64,1536]{1,0:T(8,128)(2,1)S(1)} %get-tuple-element.149), channel_id=1, source_target_pairs={{4,0},{8,4},{12,8},{14,12},{10,14},{6,10},{2,6},{0,2},{5,1},{9,5},... | collective-permute-start | bytes 589832 | tf_op jit(solution)/shard_map/back_trail3/ppermute | solution.py:375
  54.4 8.5 %collective-permute-start.27 = (bf16[64,1536]{1,0:T(8,128)(2,1)S(1)}, bf16[64,1536]{1,0:T(8,128)(2,1)S(1)}, u32[]{:S(2)}, u32[]{:S(2)}) collective-permute-start(bf16[64,1536]{1,0:T(8,128)(2,1)S(1)} %get-tuple-element.148), channel_id=1, source_target_pairs={{0,4},{4,8},{8,12},{12,14},{14,10},{10,6},{6,2},{2,0},{1,5},{5,9},... | collective-permute-start | bytes 589832 | tf_op jit(solution)/shard_map/back_trail3/ppermute | solution.py:375
  59.0 8.7 %collective-permute-start.23 = (bf16[64,1536]{1,0:T(8,128)(2,1)S(1)}, bf16[64,1536]{1,0:T(8,128)(2,1)S(1)}, u32[]{:S(2)}, u32[]{:S(2)}) collective-permute-start(bf16[64,1536]{1,0:T(8,128)(2,1)S(1)} %add_convert_fusion.8), channel_id=1, source_target_pairs={{4,0},{8,4},{12,8},{14,12},{10,14},{6,10},{2,6},{0,2},{5,1},{9,5},... | collective-permute-start | bytes 589832 | tf_op jit(solution)/shard_map/back_lead3/ppermute | solution.py:375
  60.8 7.0 %collective-permute-start.22 = (bf16[64,1536]{1,0:T(8,128)(2,1)S(1)}, bf16[64,1536]{1,0:T(8,128)(2,1)S(1)}, u32[]{:S(2)}, u32[]{:S(2)}) collective-permute-start(bf16[64,1536]{1,0:T(8,128)(2,1)S(1)} %add_convert_fusion.9), channel_id=1, source_target_pairs={{0,4},{4,8},{8,12},{12,14},{14,10},{10,6},{6,2},{2,0},{1,5},{5,9},... | collective-permute-start | bytes 589832 | tf_op jit(solution)/shard_map/back_lead3/ppermute | solution.py:375
  63.0 8.4 %collective-permute-start.30 = (bf16[64,1536]{1,0:T(8,128)(2,1)S(1)}, bf16[64,1536]{1,0:T(8,128)(2,1)S(1)}, u32[]{:S(2)}, u32[]{:S(2)}) collective-permute-start(bf16[64,1536]{1,0:T(8,128)(2,1)S(1)} %add_convert_fusion.3), channel_id=1, source_target_pairs={{4,0},{8,4},{12,8},{14,12},{10,14},{6,10},{2,6},{0,2},{5,1},{9,5},... | collective-permute-start | bytes 589832 | tf_op jit(solution)/shard_map/back_trail2/ppermute | solution.py:375
  65.0 6.6 %collective-permute-start.29 = (bf16[64,1536]{1,0:T(8,128)(2,1)S(1)}, bf16[64,1536]{1,0:T(8,128)(2,1)S(1)}, u32[]{:S(2)}, u32[]{:S(2)}) collective-permute-start(bf16[64,1536]{1,0:T(8,128)(2,1)S(1)} %add_convert_fusion.4), channel_id=1, source_target_pairs={{0,4},{4,8},{8,12},{12,14},{14,10},{10,6},{6,2},{2,0},{1,5},{5,9},... | collective-permute-start | bytes 589832 | tf_op jit(solution)/shard_map/back_trail2/ppermute | solution.py:375
  67.8 8.3 %collective-permute-start.25 = (bf16[64,1536]{1,0:T(8,128)(2,1)S(1)}, bf16[64,1536]{1,0:T(8,128)(2,1)S(1)}, u32[]{:S(2)}, u32[]{:S(2)}) collective-permute-start(bf16[64,1536]{1,0:T(8,128)(2,1)S(1)} %add_convert_fusion.6), channel_id=1, source_target_pairs={{4,0},{8,4},{12,8},{14,12},{10,14},{6,10},{2,6},{0,2},{5,1},{9,5},... | collective-permute-start | bytes 589832 | tf_op jit(solution)/shard_map/back_lead2/ppermute | solution.py:375
  69.4 7.9 %collective-permute-start.24 = (bf16[64,1536]{1,0:T(8,128)(2,1)S(1)}, bf16[64,1536]{1,0:T(8,128)(2,1)S(1)}, u32[]{:S(2)}, u32[]{:S(2)}) collective-permute-start(bf16[64,1536]{1,0:T(8,128)(2,1)S(1)} %add_convert_fusion.7), channel_id=1, source_target_pairs={{0,4},{4,8},{8,12},{12,14},{14,10},{10,6},{6,2},{2,0},{1,5},{5,9},... | collective-permute-start | bytes 589832 | tf_op jit(solution)/shard_map/back_lead2/ppermute | solution.py:375
  71.6 8.0 %collective-permute-start.31 = (bf16[64,1536]{1,0:T(8,128)(2,1)S(1)}, bf16[64,1536]{1,0:T(8,128)(2,1)S(1)}, u32[]{:S(2)}, u32[]{:S(2)}) collective-permute-start(bf16[64,1536]{1,0:T(8,128)(2,1)S(1)} %add_convert_fusion.2), channel_id=1, source_target_pairs={{4,0},{8,4},{12,8},{14,12},{10,14},{6,10},{2,6},{0,2},{5,1},{9,5},... | collective-permute-start | bytes 589832 | tf_op jit(solution)/shard_map/back_trail1/ppermute | solution.py:375
  73.4 9.7 %collective-permute-start.32 = (bf16[64,1536]{1,0:T(8,128)(2,1)S(1)}, bf16[64,1536]{1,0:T(8,128)(2,1)S(1)}, u32[]{:S(2)}, u32[]{:S(2)}) collective-permute-start(bf16[64,1536]{1,0:T(8,128)(2,1)S(1)} %add_convert_fusion.1), channel_id=1, source_target_pairs={{0,4},{4,8},{8,12},{12,14},{14,10},{10,6},{6,2},{2,0},{1,5},{5,9},... | collective-permute-start | bytes 589832 | tf_op jit(solution)/shard_map/back_trail1/ppermute | solution.py:375
  77.3 5.7 %collective-permute-start.26 = (bf16[64,1536]{1,0:T(8,128)(2,1)S(1)}, bf16[64,1536]{1,0:T(8,128)(2,1)S(1)}, u32[]{:S(2)}, u32[]{:S(2)}) collective-permute-start(bf16[64,1536]{1,0:T(8,128)(2,1)S(1)} %add_convert_fusion.5), channel_id=1, source_target_pairs={{0,4},{4,8},{8,12},{12,14},{14,10},{10,6},{6,2},{2,0},{1,5},{5,9},... | collective-permute-start | bytes 589832 | tf_op jit(solution)/shard_map/back_lead1/ppermute | solution.py:375
  78.3 5.7 %collective-permute-start.33 = (bf16[64,1536]{1,0:T(8,128)(2,1)S(1)}, bf16[64,1536]{1,0:T(8,128)(2,1)S(1)}, u32[]{:S(2)}, u32[]{:S(2)}) collective-permute-start(bf16[64,1536]{1,0:T(8,128)(2,1)S(1)} %add_convert_fusion), channel_id=1, source_target_pairs={{4,0},{8,4},{12,8},{14,12},{10,14},{6,10},{2,6},{0,2},{5,1},{9,5},... | collective-permute-start | bytes 589832 | tf_op jit(solution)/shard_map/back_lead1/ppermute | solution.py:375
